TPU v7x, 32 devices: a whole 2x2x4 slice. The times are simulated.
32 devices in a mesh: req: 8 (over z, y), head: 4 (over x, core).
Axes of the slice: x: 2, y: 2, z: 4, core: 2. Of those that a mesh axis runs over, the one named last changes fastest.
Arguments:
- tokens: bfloat16 [32, 64, 2048], P(('req', 'head')), may hold values from -3 to 3
- live: int32 [32, 64], P(('req', 'head')), may hold values from 0 to 1, as said below
- parents: int32 [32, 64], P('req'), may hold values from -1 to 62, as said below
- lengths: int32 [32], P('req'), may hold values from 1 to 2048, as said below
- accepted: int32 [32, 8], P('req'), may hold values from 0 to 31, as said below
- routes: int32 [32, 64, 6], P(('req', 'head')), may hold values from 0 to 15, all different within a row; in each aligned block of 64 rows (0 to 63, 64 to 127, ..., all dimensions but the last counted through in order) at most 32 rows name the same one
- cache: bfloat16 [32, 4, 2048, 256], P('req', 'head'), may hold values from -160 to 160, as said below
- attn_gain: float32 [2048], replicated, may hold values from 0.1 to 1.9
- w_qkv: bfloat16 [2048, 3072], P(None, 'head'), may hold values from -0.125 to 0.125
- w_out: bfloat16 [2048, 2048], P('head'), may hold values from -0.125 to 0.125
- ffn_gain: float32 [2048], replicated, may hold values from 0.1 to 1.9
- shared_gate: bfloat16 [2048, 1408], P(None, 'head'), may hold values from -0.125 to 0.125
- shared_up: bfloat16 [2048, 1408], P(None, 'head'), may hold values from -0.125 to 0.125
- shared_down: bfloat16 [1408, 2048], P('head'), may hold values from -0.15625 to 0.15625
- router: bfloat16 [2048, 16], replicated, may hold values from -0.125 to 0.125
- expert_in: bfloat16 [32, 2048, 1408], P(('req', 'head')), may hold values from -0.125 to 0.125
- expert_out: bfloat16 [32, 704, 2048], P(('req', 'head')), may hold values from -0.21875 to 0.21875
Outputs:
- hidden_out: bfloat16 [32, 64, 2048], P(('req', 'head'))
- accepted_kv: bfloat16 [32, 4, 8, 256], P('req', 'head')
Inputs may be any that keep to these rules, and one draw needn't show every extreme that they name: lengths run from 1 to 2048; every draw has a request with all 2048 slots filled. Each request's live entries are its first ones; at least 32 are live and some request has all 64 live. parents[r, 0] = -1 and parents[r, i] < i for i > 0. `accepted`: each request's entries are distinct, ascending, begin with 0 and name live nodes; some request names node 31. `routes`: within the 64 nodes of one request no expert is named more than 32 times, and in some request one expert is named exactly 32 times; the 6 experts of a node differ. `cache`: entries are finite.
All inputs are finite; a program needn't handle non-finite values.
Results may differ from a plain program's by a relative error of at most 0.012.
The roundings to bfloat16 on the way count: a program that leaves them out, or rounds other values in their place, can miss the bound.
Values may be sent and summed in bfloat16 or wider, within the bound.
No kernel may reach another device: no remote copies, remote signals or barrier semaphores. Data moves between devices by JAX's collectives and lax.ppermute only.
A program may use at most 128 MiB of HBM per device.

v0:
```python
import math

import jax
import jax.numpy as jnp
from jax import lax
from jax.sharding import PartitionSpec as P

EPSILON = 1e-06
ROPE_BASE = 10000.0


def rms_norm(values, gain):
    wide = values.astype(jnp.float32)
    power = jnp.mean(wide * wide, axis=-1, keepdims=True)
    return (wide * lax.rsqrt(power + EPSILON) * gain).astype(jnp.bfloat16)


def rotate(values, position):
    half = values.shape[-1] // 2
    frequency = ROPE_BASE ** (-jnp.arange(half, dtype=jnp.float32) / half)
    angle = position[..., None] * frequency
    cosine = jnp.cos(angle)
    sine = jnp.sin(angle)
    first = values[..., :half]
    second = values[..., half:]
    return jnp.concatenate(
        [first * cosine - second * sine, second * cosine + first * sine], axis=-1
    )


def ancestry(parents):
    nodes_count = parents.shape[-1]
    nodes = jnp.arange(nodes_count, dtype=jnp.int32)
    reach = (parents[..., :, None] == nodes).astype(jnp.float32) + jnp.eye(
        nodes_count, dtype=jnp.float32
    )
    for turn in range(nodes_count.bit_length()):
        reach = jnp.minimum(
            jnp.einsum("rij,rjk->rik", reach, reach, precision=lax.Precision.HIGHEST), 1.0
        )
    depth = jnp.sum(reach, axis=-1) - 1.0
    return (reach, depth)


def head_group(projected, position, length, reach, cache_rows):
    group = projected.shape[0] - 2
    tree = projected.shape[1]
    head_dim = projected.shape[2]
    query = rotate(projected[:group], position).astype(jnp.bfloat16).reshape(group * tree, head_dim)
    key_new = rotate(projected[group], position).astype(jnp.bfloat16)
    value_new = projected[group + 1].astype(jnp.bfloat16)
    scale = 1.0 / math.sqrt(head_dim)
    cache_keys = cache_rows[:, :head_dim]
    cache_values = cache_rows[:, head_dim:]
    old_scores = (
        jnp.einsum("qd,kd->qk", query, cache_keys, preferred_element_type=jnp.float32) * scale
    )
    new_scores = jnp.einsum("qd,kd->qk", query, key_new, preferred_element_type=jnp.float32) * scale
    visible = jnp.arange(cache_rows.shape[0], dtype=jnp.int32) < length
    old_scores = jnp.where(visible[None, :], old_scores, -1e30)
    new_scores = jnp.where(jnp.tile(reach, (group, 1)) > 0.5, new_scores, -1e30)
    peak = jnp.maximum(
        jnp.max(old_scores, axis=-1, keepdims=True), jnp.max(new_scores, axis=-1, keepdims=True)
    )
    old_weights = jnp.exp(old_scores - peak)
    new_weights = jnp.exp(new_scores - peak)
    denominator = jnp.sum(old_weights, axis=-1, keepdims=True) + jnp.sum(
        new_weights, axis=-1, keepdims=True
    )
    old_probs = (old_weights / denominator).astype(jnp.bfloat16)
    new_probs = (new_weights / denominator).astype(jnp.bfloat16)
    mixed = jnp.dot(old_probs, cache_values, preferred_element_type=jnp.float32) + jnp.dot(
        new_probs, value_new, preferred_element_type=jnp.float32
    )
    mixed = (
        mixed.astype(jnp.bfloat16)
        .reshape(group, tree, head_dim)
        .transpose(1, 0, 2)
        .reshape(tree, group * head_dim)
    )
    return (mixed, jnp.concatenate([key_new, value_new], axis=-1))


def expert_half(rows, inner, outer):
    both = jnp.dot(rows, inner, preferred_element_type=jnp.float32)
    half = inner.shape[1] // 2
    hidden = (jax.nn.silu(both[:, :half]) * both[:, half:]).astype(jnp.bfloat16)
    return jnp.dot(hidden, outer, preferred_element_type=jnp.float32).astype(jnp.bfloat16)


def body(
    tokens,
    live,
    parents,
    lengths,
    accepted,
    routes,
    cache,
    attn_gain,
    w_qkv,
    w_out,
    ffn_gain,
    shared_gate,
    shared_up,
    shared_down,
    router,
    expert_in,
    expert_out,
):
    tree = tokens.shape[1]
    width = tokens.shape[2]
    own_rows = tokens[0]
    group_count = lax.axis_size("head")
    local_heads = cache.shape[1]
    head_dim = cache.shape[3] // 2
    group = w_qkv.shape[1] // (local_heads * head_dim) - 2
    projected = jnp.dot(
        rms_norm(lax.all_gather(own_rows, "head", axis=0, tiled=True), attn_gain),
        w_qkv,
        preferred_element_type=jnp.float32,
    )
    projected = projected.reshape(group_count, tree, local_heads, group + 2, head_dim).transpose(
        0, 2, 3, 1, 4
    )
    reach, depth = ancestry(parents)
    positions = lengths[:, None].astype(jnp.float32) + depth
    inner_map = jax.vmap(head_group, in_axes=(0, None, None, None, 0))
    mixed, fresh = jax.vmap(inner_map)(projected, positions, lengths, reach, cache)
    mixed = mixed.transpose(0, 2, 1, 3).reshape(group_count * tree, local_heads * group * head_dim)
    accepted_kv = jnp.take_along_axis(fresh, accepted[:, None, :, None], axis=2)
    block = mixed
    attn_own = lax.psum_scatter(
        jnp.dot(block, w_out, preferred_element_type=jnp.float32),
        "head",
        scatter_dimension=0,
        tiled=True,
    )
    resid = (own_rows.astype(jnp.float32) + attn_own).astype(jnp.bfloat16)
    normed = rms_norm(resid, ffn_gain)
    normed_all = lax.all_gather(normed, "head", axis=0, tiled=True)
    block = normed_all
    gated = jax.nn.silu(jnp.dot(block, shared_gate, preferred_element_type=jnp.float32))
    hidden = (gated * jnp.dot(block, shared_up, preferred_element_type=jnp.float32)).astype(
        jnp.bfloat16
    )
    shared = lax.psum_scatter(
        jnp.dot(hidden, shared_down, preferred_element_type=jnp.float32).astype(jnp.bfloat16),
        "head",
        scatter_dimension=0,
        tiled=True,
    ).astype(jnp.float32)
    choose = routes[0]
    top_count = choose.shape[1]
    expert_count = router.shape[1]
    capacity = 4 * tree * top_count // (3 * expert_count)
    logits = jnp.dot(normed, router, preferred_element_type=jnp.float32)
    picked = jax.nn.sigmoid(jnp.take_along_axis(logits, choose, axis=1))
    gates = picked / jnp.sum(picked, axis=-1, keepdims=True)
    route_flat = choose.reshape(-1)
    onehot = (route_flat[:, None] == jnp.arange(expert_count, dtype=jnp.int32)).astype(jnp.int32)
    slots = jnp.sum((jnp.cumsum(onehot, axis=0) - onehot) * onehot, axis=-1)
    target = (route_flat * capacity + slots).reshape(tree, top_count)
    placing = jnp.any(
        target[:, :, None] == jnp.arange(expert_count * capacity, dtype=jnp.int32), axis=1
    ).astype(jnp.bfloat16)
    outgoing = jnp.einsum("ts,td->sd", placing, normed, preferred_element_type=jnp.float32).astype(
        jnp.bfloat16
    )
    outgoing = jnp.repeat(outgoing.reshape(expert_count, capacity, width), 2, axis=0)
    inner = expert_in[0]
    outer = expert_out[0]
    received = lax.all_to_all(outgoing, ("req", "head"), split_axis=0, concat_axis=0, tiled=True)
    partial_value = expert_half(received.reshape(-1, width), inner, outer).reshape(received.shape)
    returned = lax.all_to_all(
        partial_value, ("req", "head"), split_axis=0, concat_axis=0, tiled=True
    )
    halves = returned.reshape(expert_count, 2, capacity, width).astype(jnp.float32)
    expert_rows = (halves[:, 0] + halves[:, 1]).reshape(expert_count * capacity, width)
    routed = jnp.sum(gates[:, :, None] * expert_rows[target], axis=1)
    total_out = resid.astype(jnp.float32) + shared + routed
    hidden_out = jnp.where(live[0][:, None] == 1, total_out, 0.0).astype(jnp.bfloat16)
    return (hidden_out[None], accepted_kv)


def solution(mesh):
    in_specs = (
        P(("req", "head"), None, None),
        P(("req", "head"), None),
        P("req", None),
        P("req"),
        P("req", None),
        P(("req", "head"), None, None),
        P("req", "head", None, None),
        P(),
        P(None, "head"),
        P("head", None),
        P(),
        P(None, "head"),
        P(None, "head"),
        P("head", None),
        P(),
        P(("req", "head"), None, None),
        P(("req", "head"), None, None),
    )
    out_specs = (P(("req", "head"), None, None), P("req", "head", None, None))
    return jax.shard_map(body, mesh=mesh, in_specs=in_specs, out_specs=out_specs, check_vma=False)
```

profile of v0, /device:TPU:0, one launch (start us, length us, event | category | flops | bytes accessed | tf_op | source)
XLA Modules:
  0.0 320.8 jit_solution(872526104795171757)
XLA Ops:
  8.0 1.2 convolution_minimum_fusion.6
  11.8 0.9 gt.12
  13.3 0.7 iota_compare_fusion.4
  14.1 15.0 %all-gather.6.cloned.1.call-done = bf16[1,256,2048]{2,1,0:T(8,128)(2,1)} async-done(((bf16[1,64,2048]{2,1,0:T(8,128)(2,1)}), bf16[1,256,2048]{2,1,0:T(8,128)(2,1)}) %all-gather.6.cloned.1.call-update) | async-done | bytes 1048592 | tf_op jit(solution)/shard_map/all_gather | solution.py:118
  29.0 1.5 fusion.8
  30.6 3.2 fusion.17
  33.8 1.3 reshape.405
  36.1 1.1 copy-done.6
  37.2 1.7 fusion
  39.3 1.9 fusion.1
  41.2 2.9 fusion.5
  44.7 2.1 fusion.36
  47.2 0.9 reduce-window.6
  48.6 0.8 fusion.22
  49.4 28.9 %reduce-scatter.3.cloned.1.call-done = f32[64,2048]{1,0:T(8,128)} async-done(((f32[256,2048]{1,0:T(8,128)}), f32[64,2048]{1,0:T(8,128)}) %reduce-scatter.3.cloned.1.call-update) | async-done | bytes 524304 | tf_op jit(solution)/shard_map/reduce_scatter | solution.py:132
  78.4 1.3 fusion.23
  79.8 1.5 convolution_convert_fusion.1
  81.9 98.1 %all_to_all.10 = bf16[32,32,2048]{2,1,0:T(8,128)(2,1)S(1)} all-to-all(bf16[32,32,2048]{2,1,0:T(8,128)(2,1)S(1)} %bitcast.147), channel_id=1, replica_groups=mesh['req'=8,'head'=4] {'req','head'}, dimensions={0} | all-to-all | bytes 8388608 | tf_op jit(solution)/shard_map/all_to_all | solution.py:172
  180.0 6.7 %fusion.2 = f32[1024,1408]{1,0:T(8,128)S(1)} fusion(bf16[1024,2048]{1,0:T(8,128)(2,1)S(1)} %bitcast.154, bf16[1,2048,1408]{2,1,0:T(8,128)(2,1)S(1)} %bitcast.167), kind=kOutput, calls=%fused_computation.8 | convolution fusion | flops 5905580032 | bytes 15728640 | tf_op jit(solution)/shard_map/dot_general | solution.py:85
  186.7 5.3 %convolution_convert_fusion = bf16[1024,2048]{1,0:T(8,128)(2,1)} fusion(bf16[1,704,2048]{2,1,0:T(8,128)(2,1)S(1)} %copy-done.14, f32[1024,1408]{1,0:T(8,128)S(1)} %fusion.2), kind=kOutput, calls=%fused_computation.15 | convolution fusion | flops 2959212544 | bytes 13369344 | tf_op jit(solution)/shard_map/dot_general | solution.py:88
  191.9 3.8 %all-to-all-start.1 = ((bf16[32,32,2048]{2,1,0:T(8,128)(2,1)}), bf16[32,32,2048]{2,1,0:T(8,128)(2,1)}, u32[]{:S(2)}, u32[]{:S(2)}) async-start(bf16[32,32,2048]{2,1,0:T(8,128)(2,1)} %bitcast.153), calls=%async_computation.3 | async-start | bytes 8388608 | tf_op jit(solution)/shard_map/all_to_all | solution.py:174
  196.9 35.4 %all-gather.4.cloned.1.call-done = bf16[256,2048]{1,0:T(8,128)(2,1)} async-done(((bf16[64,2048]{1,0:T(8,128)(2,1)}), bf16[256,2048]{1,0:T(8,128)(2,1)}) %all-gather.4.cloned.1.call-update) | async-done | bytes 1048592 | tf_op jit(solution)/shard_map/all_gather | solution.py:140
  232.3 1.8 fusion.79
  234.1 5.3 %convolution_convert_fusion.2 = bf16[256,2048]{1,0:T(8,128)(2,1)} fusion(bf16[352,2048]{1,0:T(8,128)(2,1)} %param.30, bf16[256,2048]{1,0:T(8,128)(2,1)} %all-gather.4.cloned.1.call-done, bf16[2048,352]{0,1:T(8,128)(2,1)} %param.29, f32[256,352]{0,1:T(8,128)S(1)} %fusion.79), kind=kOutput, calls=%fused_computation.22 | convolution fusion | flops 739262464 | bytes 5341184 | tf_op jit(solution)/shard_map/dot_general | solution.py:147
  241.3 3.0 gather_fusion.1
  244.7 45.1 %all-to-all-done.1 = bf16[32,32,2048]{2,1,0:T(8,128)(2,1)} async-done(((bf16[32,32,2048]{2,1,0:T(8,128)(2,1)}), bf16[32,32,2048]{2,1,0:T(8,128)(2,1)}, u32[]{:S(2)}, u32[]{:S(2)}) %all-to-all-start.1) | async-done | bytes 4194336 | tf_op jit(solution)/shard_map/all_to_all | solution.py:174
  289.8 3.3 %convert.24 = f32[16,2,32,2048]{3,2,1,0:T(8,128)S(1)} convert(bf16[16,2,32,2048]{3,2,1,0:T(8,128)(2,1)} %bitcast.26) | non-fusion elementwise | flops 2097152 | bytes 12582912 | tf_op jit(solution)/shard_map/convert_element_type | solution.py:177
  293.0 2.7 fusion.4
  295.7 7.3 %gather_fusion = f32[384,2048]{1,0:T(8,128)} fusion(f32[512,2048]{1,0:T(8,128)} %bitcast.146, s32[1024]{0:T(1024)S(1)} %pad_clamp_fusion), kind=kCustom, calls=%fused_computation | custom fusion | bytes 6292992 | tf_op jit(solution)/shard_map/gather | solution.py:179
  303.0 4.8 %reshape.418 = f32[64,6,2048]{2,1,0:T(8,128)} reshape(f32[384,2048]{1,0:T(8,128)} %gather_fusion) | data formatting | bytes 6291456 | tf_op jit(solution)/shard_map/gather | solution.py:179
  307.9 4.5 %multiply_reduce_fusion = f32[64,2048]{1,0:T(8,128)} fusion(f32[64,6,2048]{2,1,0:T(8,128)} %reshape.418, f32[64,6]{1,0:T(8,128)S(1)} %copy.74), kind=kLoop, calls=%fused_computation.13 | loop fusion | flops 1441792 | bytes 3671552 | tf_op jit(solution)/shard_map/reduce_sum | solution.py:179
  312.4 1.9 fusion.35
  (106 shorter events, 10.9 us)
Async XLA Ops:
  7.2 23.4 %copy-start = (bf16[2048,768]{1,0:T(8,128)(2,1)S(1)}, bf16[2048,768]{1,0:T(8,128)(2,1)}, u32[]{:S(2)}) copy-start(bf16[2048,768]{1,0:T(8,128)(2,1)} %param.25) | copy-start | bytes 9437188
  7.2 23.4 %copy-start.15 = (f32[2048]{0:T(1024)S(1)}, f32[2048]{0:T(1024)}, u32[]{:S(2)}) copy-start(f32[2048]{0:T(1024)} %param.24) | copy-start | bytes 24580
  7.2 21.8 %all-gather.6.cloned.1.call-start = ((), (), s32[]{:S(2)}) async-start(), calls=%async_computation.7 | async-start | bytes 1310720 | tf_op jit(solution)/shard_map/all_gather | solution.py:118
  7.9 70.4 %reduce-scatter.3.cloned.1.call-start = ((), (), s32[]{:S(2)}) async-start(), calls=%async_computation.4 | async-start | bytes 2621440 | tf_op jit(solution)/shard_map/reduce_scatter | solution.py:132
  35.0 2.2 copy-start.6
  37.2 1.7 copy-start.9
  41.2 3.5 %copy-start.4 = (bf16[512,2048]{1,0:T(8,128)(2,1)S(1)}, bf16[512,2048]{1,0:T(8,128)(2,1)}, u32[]{:S(2)}) copy-start(bf16[512,2048]{1,0:T(8,128)(2,1)} %param.26) | copy-start | bytes 6291460
  44.1 2.6 copy-start.11
  44.5 35.2 %copy-start.12 = (f32[2048]{0:T(1024)S(1)}, f32[2048]{0:T(1024)}, u32[]{:S(2)}) copy-start(f32[2048]{0:T(1024)} %param.27) | copy-start | bytes 24580
  46.9 2.5 copy-start.7
  79.8 2.1 copy-start.2
  81.4 98.6 %slice-start = ((s8[5767168]{0:T(1024)(128)(4,1)}), s8[4194304]{0:T(1024)(128)(4,1)S(1)}, s32[]{:S(2)}) async-start(s8[5767168]{0:T(1024)(128)(4,1)} %bitcast.166), calls=%async_computation.8 | async-start | bytes 8388608
  81.9 98.1 %slice-start.1 = ((s8[5767168]{0:T(1024)(128)(4,1)}), s8[1572864]{0:T(1024)(128)(4,1)S(1)}, s32[]{:S(2)}) async-start(s8[5767168]{0:T(1024)(128)(4,1)} %bitcast.166), calls=%async_computation.9 | async-start | bytes 3145728
  180.0 6.7 %copy-start.14 = (bf16[1,704,2048]{2,1,0:T(8,128)(2,1)S(1)}, bf16[1,704,2048]{2,1,0:T(8,128)(2,1)}, u32[]{:S(2)}) copy-start(bf16[1,704,2048]{2,1,0:T(8,128)(2,1)} %param.33) | copy-start | bytes 8650756
  191.9 4.8 %copy-start.8 = (s32[1,64,6]{2,1,0:T(8,128)S(1)}, s32[1,64,6]{2,1,0:T(8,128)}, u32[]{:S(2)}) copy-start(s32[1,64,6]{2,1,0:T(8,128)} %copy-done.7) | copy-start | bytes 4612
  191.9 5.0 %copy-start.16 = (s32[1,64]{1,0:T(1,128)S(1)}, s32[1,64]{1,0:T(1,128)}, u32[]{:S(2)}) copy-start(s32[1,64]{1,0:T(1,128)} %param.18) | copy-start | bytes 772
  191.9 5.0 %copy-start.13 = (s32[4,8]{1,0:T(4,128)S(1)}, s32[4,8]{1,0:T(4,128)}, u32[]{:S(2)}) copy-start(s32[4,8]{1,0:T(4,128)} %param.21) | copy-start | bytes 388
  191.9 40.4 %copy-start.5 = (bf16[2048,352]{0,1:T(8,128)(2,1)S(1)}, bf16[2048,352]{0,1:T(8,128)(2,1)}, u32[]{:S(2)}) copy-start(bf16[2048,352]{0,1:T(8,128)(2,1)} %param.28) | copy-start | bytes 4325380
  191.9 97.8 %all-to-all-start.1 = ((bf16[32,32,2048]{2,1,0:T(8,128)(2,1)}), bf16[32,32,2048]{2,1,0:T(8,128)(2,1)}, u32[]{:S(2)}, u32[]{:S(2)}) async-start(bf16[32,32,2048]{2,1,0:T(8,128)(2,1)} %bitcast.153), calls=%async_computation.3 | async-start | bytes 8388608 | tf_op jit(solution)/shard_map/all_to_all | solution.py:174
  195.8 36.5 %all-gather.4.cloned.1.call-start = ((), (), s32[]{:S(2)}) async-start(), calls=%async_computation.5 | async-start | bytes 1310720 | tf_op jit(solution)/shard_map/all_gather | solution.py:140
  196.5 115.9 %reduce-scatter.5.cloned.1.call-start = ((), (), s32[]{:S(2)}) async-start(), calls=%async_computation.6 | async-start | bytes 1310720 | tf_op jit(solution)/shard_map/reduce_scatter | solution.py:146
  234.1 7.0 %copy-start.3 = (bf16[64,2048]{1,0:T(8,128)(2,1)S(1)}, bf16[64,2048]{1,0:T(8,128)(2,1)}, u32[]{:S(2)}) copy-start(bf16[64,2048]{1,0:T(8,128)(2,1)} %copy-done.2) | copy-start | bytes 786436
  234.1 7.0 %copy-start.10 = (bf16[2048,16]{0,1:T(8,128)(2,1)S(1)}, bf16[2048,16]{0,1:T(8,128)(2,1)}, u32[]{:S(2)}) copy-start(bf16[2048,16]{0,1:T(8,128)(2,1)} %param.31) | copy-start | bytes 196612
  303.0 11.3 %copy-start.1 = (bf16[2048,768]{1,0:T(8,128)(2,1)S(1)}, bf16[2048,768]{1,0:T(8,128)(2,1)}, u32[]{:S(2)}) copy-start(bf16[2048,768]{1,0:T(8,128)(2,1)} %param.25) | copy-start | bytes 9437188
Sparse Core Ops, SparseCore 0:
  9.6 19.4 all-gather.5
  46.9 31.4 reduce-scatter.2
  198.8 33.4 all-gather.3
  239.5 30.4 reduce-scatter.4
where the time goes:
time: 322 us; the launch traced here: 321 us
  waiting for transfers between devices  126 us (39%)
  blocking collectives  98.1 us (30%)
  matrix products  33.9 us (11%)
  other arithmetic  22.9 us (7%)
  local copies, waits for them, and re-layouts  21.9 us (7%)
  between operations  14.3 us (4%)
  starting transfers between devices  4 us (1%)
    all_to_all x1, blocking collectives, body(): lax.all_to_all(outgoing, ('req', 'head'), split_axis=0, concat_axis=0, ti...  98.1 us
    all_to_all x1, waiting for transfers between devices, body(): lax.all_to_all(partial_value, ('req', 'head'), split_axis=0, concat_axis=...  45.1 us
    all_gather x1, waiting for transfers between devices, body(): normed_all = lax.all_gather(normed, 'head', axis=0, tiled=True)  35.4 us
    reduce_scatter x1, waiting for transfers between devices, body(): lax.psum_scatter(jnp.dot(block, w_out, preferred_element_type=jnp.float32...  28.9 us
    all_gather x1, waiting for transfers between devices, body(): lax.all_gather(own_rows, 'head', axis=0, tiled=True)  15 us
    gather x2, local copies, waits for them, and re-layouts, body(): routed = jnp.sum(gates[:, :, None] * expert_rows[target], axis=1)  12.1 us
    dot_general x1, matrix products, expert_half(): both = jnp.dot(rows, inner, preferred_element_type=jnp.float32)  6.65 us
  transfers between devices with their start and end apart: 5, of which 4 were waited for; matrix products, arithmetic and copies ran while one was open for 14% of the time, Pallas kernels for 0%

commit v1 on v0

v1 whole, which is shorter than its diff:
```python
import math

import jax
import jax.numpy as jnp
from jax import lax
from jax.sharding import Mesh
from jax.sharding import PartitionSpec as P

EPSILON = 1e-06
ROPE_BASE = 10000.0
PARTS = 2
ALL = ("z", "y", "x", "c")
PLANE = ("y", "x")
HEAD = ("x", "c")


def partner(value, axes, offset):
    if offset == 0:
        return value
    size = lax.axis_size(axes)
    return lax.ppermute(value, axes, [(i, i ^ offset) for i in range(size)])


def rms_norm(values, gain):
    wide = values.astype(jnp.float32)
    power = jnp.mean(wide * wide, axis=-1, keepdims=True)
    return (wide * lax.rsqrt(power + EPSILON) * gain).astype(jnp.bfloat16)


def dot(left, right):
    return jnp.dot(left, right, preferred_element_type=jnp.float32)


def rotate(values, position):
    half = values.shape[-1] // 2
    frequency = ROPE_BASE ** (-jnp.arange(half, dtype=jnp.float32) / half)
    angle = position[..., None] * frequency
    cosine = jnp.cos(angle)
    sine = jnp.sin(angle)
    first = values[..., :half]
    second = values[..., half:]
    return jnp.concatenate(
        [first * cosine - second * sine, second * cosine + first * sine], axis=-1
    )


def ancestry(parents):
    nodes_count = parents.shape[-1]
    nodes = jnp.arange(nodes_count, dtype=jnp.int32)
    reach = (parents[..., :, None] == nodes).astype(jnp.float32) + jnp.eye(
        nodes_count, dtype=jnp.float32
    )
    for turn in range((nodes_count - 1).bit_length()):
        near = reach.astype(jnp.bfloat16)
        reach = jnp.minimum(
            jnp.einsum("rij,rjk->rik", near, near, preferred_element_type=jnp.float32), 1.0
        )
    depth = jnp.sum(reach, axis=-1) - 1.0
    return (reach, depth)


def head_group(projected, position, length, reach, cache_rows):
    group = projected.shape[0] - 2
    tree = projected.shape[1]
    head_dim = projected.shape[2]
    query = rotate(projected[:group], position).astype(jnp.bfloat16).reshape(group * tree, head_dim)
    key_new = rotate(projected[group], position).astype(jnp.bfloat16)
    value_new = projected[group + 1].astype(jnp.bfloat16)
    scale = 1.0 / math.sqrt(head_dim)
    cache_keys = cache_rows[:, :head_dim]
    cache_values = cache_rows[:, head_dim:]
    old_scores = (
        jnp.einsum("qd,kd->qk", query, cache_keys, preferred_element_type=jnp.float32) * scale
    )
    new_scores = jnp.einsum("qd,kd->qk", query, key_new, preferred_element_type=jnp.float32) * scale
    visible = jnp.arange(cache_rows.shape[0], dtype=jnp.int32) < length
    old_scores = jnp.where(visible[None, :], old_scores, -1e30)
    new_scores = jnp.where(jnp.tile(reach, (group, 1)) > 0.5, new_scores, -1e30)
    peak = jnp.maximum(
        jnp.max(old_scores, axis=-1, keepdims=True), jnp.max(new_scores, axis=-1, keepdims=True)
    )
    old_weights = jnp.exp(old_scores - peak)
    new_weights = jnp.exp(new_scores - peak)
    denominator = jnp.sum(old_weights, axis=-1, keepdims=True) + jnp.sum(
        new_weights, axis=-1, keepdims=True
    )
    old_probs = (old_weights / denominator).astype(jnp.bfloat16)
    new_probs = (new_weights / denominator).astype(jnp.bfloat16)
    mixed = dot(old_probs, cache_values) + dot(new_probs, value_new)
    mixed = (
        mixed.astype(jnp.bfloat16)
        .reshape(group, tree, head_dim)
        .transpose(1, 0, 2)
        .reshape(tree, group * head_dim)
    )
    return (mixed, jnp.concatenate([key_new, value_new], axis=-1))


def body(
    tokens,
    live,
    parents,
    lengths,
    accepted,
    routes,
    cache,
    attn_gain,
    w_qkv,
    w_out,
    ffn_gain,
    shared_gate,
    shared_up,
    shared_down,
    router,
    expert_in,
    expert_out,
):
    tree = tokens.shape[1]
    width = tokens.shape[2]
    own_rows = tokens[0]
    group_count = lax.axis_size(HEAD)
    local_heads = cache.shape[1]
    head_dim = cache.shape[3] // 2
    group = w_qkv.shape[1] // (local_heads * head_dim) - 2
    me = lax.axis_index(HEAD)

    core_rows = partner(own_rows, "c", 1)
    side = lax.axis_size("x")
    near = [own_rows] + [partner(own_rows, "x", o) for o in range(1, side)]
    rows_by = []
    for o in range(side):
        rows_by += [near[o], core_rows if o == 0 else partner(near[o], "c", 1)]

    line = lax.axis_size("z")
    chosen = [partner(routes[0], "z", k) for k in range(line)]
    inner = [expert_in[0], partner(expert_in[0], "c", 1)]
    outer = [expert_out[0], partner(expert_out[0], "c", 1)]
    out_pair = [w_out, partner(w_out, "c", 1)]
    gate_pair = [shared_gate, partner(shared_gate, "c", 1)]
    up_pair = [shared_up, partner(shared_up, "c", 1)]
    down_pair = [shared_down, partner(shared_down, "c", 1)]

    order = me ^ jnp.arange(group_count, dtype=jnp.int32)
    rows = jnp.stack(rows_by)[order].reshape(group_count * tree, width)
    projected = dot(rms_norm(rows, attn_gain), w_qkv)
    projected = projected.reshape(group_count, tree, local_heads, group + 2, head_dim).transpose(
        0, 2, 3, 1, 4
    )
    reach, depth = ancestry(parents)
    positions = lengths[:, None].astype(jnp.float32) + depth
    inner_map = jax.vmap(head_group, in_axes=(0, None, None, None, 0))
    mixed, fresh = jax.vmap(inner_map)(projected, positions, lengths, reach, cache)
    mixed = mixed.transpose(0, 2, 1, 3).reshape(group_count, tree, local_heads * group * head_dim)
    accepted_kv = jnp.take_along_axis(fresh, accepted[:, None, :, None], axis=2)

    mixed = mixed[order].reshape(side, 2, tree, -1)
    mine = mixed[:, 0].reshape(side * tree, -1)
    other = partner(mixed[:, 1].reshape(side * tree, -1), "c", 1)
    terms = (dot(mine, out_pair[0]) + dot(other, out_pair[1])).reshape(side, tree, width)
    attn = terms[0]
    for o in range(1, side):
        attn = attn + partner(terms[o].astype(jnp.bfloat16), "x", o).astype(jnp.float32)
    resid = (own_rows.astype(jnp.float32) + attn).astype(jnp.bfloat16)
    normed = rms_norm(resid, ffn_gain)

    expert_count = router.shape[1]
    top_count = routes.shape[2]
    capacity = 4 * tree * top_count // (3 * expert_count)
    plane = lax.axis_size(PLANE)
    spot = lax.axis_index(PLANE)
    first = lax.axis_index("z") * plane
    choose = jnp.stack(chosen)
    member = jnp.any(
        choose[..., None] == jnp.arange(expert_count, dtype=jnp.int32), axis=2
    )
    before = jnp.tril(jnp.ones((tree, tree), jnp.bfloat16), -1)
    ranks = jnp.einsum(
        "nm,kme->kne", before, member.astype(jnp.bfloat16), preferred_element_type=jnp.float32
    ).astype(jnp.int32)
    near_experts = first + (spot ^ jnp.arange(plane, dtype=jnp.int32))
    is_near = near_experts[:, None] == jnp.arange(expert_count, dtype=jnp.int32)
    slot = jnp.where(member, ranks, -1)
    slot_near = jnp.sum(
        jnp.where(is_near[:, None, None, :], slot[None] + 1, 0), axis=-1
    ) - 1
    places = jnp.arange(capacity, dtype=jnp.int32)
    pick = slot_near[:, :, None, :] == places[:, None]
    pick_bf = pick.astype(jnp.bfloat16)

    cols = width // PARTS
    line_rows = []
    received = []
    for p in range(PARTS):
        piece = normed[:, p * cols : (p + 1) * cols]
        line_piece = [partner(piece, "z", k) for k in range(line)]
        line_rows.append(line_piece)
        stack = jnp.stack(line_piece)
        got = []
        for o in range(plane):
            out = jnp.einsum(
                "ksn,knd->ksd", pick_bf[o], stack, preferred_element_type=jnp.float32
            ).astype(jnp.bfloat16)
            got.append(partner(out.reshape(line * capacity, cols), PLANE, o))
        received.append(jnp.concatenate(got, axis=0))

    near_normed = [normed] + [partner(normed, "x", o) for o in range(1, side)]
    block = jnp.concatenate(near_normed, axis=0)
    shared_terms = 0.0
    for i in range(2):
        hidden = (jax.nn.silu(dot(block, gate_pair[i])) * dot(block, up_pair[i])).astype(
            jnp.bfloat16
        )
        shared_terms = shared_terms + dot(hidden, down_pair[i])
    shared_terms = shared_terms.reshape(side, tree, width)
    shared = shared_terms[0]
    for o in range(1, side):
        shared = shared + partner(shared_terms[o].astype(jnp.bfloat16), "x", o).astype(jnp.float32)

    logits = sum(
        dot(jnp.concatenate(line_rows[p], axis=0), router[p * cols : (p + 1) * cols])
        for p in range(PARTS)
    ).reshape(line, tree, expert_count)
    picked = jnp.where(member, jax.nn.sigmoid(logits), 0.0)
    gates = picked / jnp.sum(picked, axis=-1, keepdims=True)
    gates_near = jnp.sum(jnp.where(is_near[:, None, None, :], gates[None], 0.0), axis=-1)
    spread = jnp.where(pick, gates_near[:, :, None, :], 0.0)
    spread = spread.astype(jnp.bfloat16)

    hidden = []
    for i in range(2):
        both = sum(dot(received[p], inner[i][p * cols : (p + 1) * cols]) for p in range(PARTS))
        half = both.shape[1] // 2
        hidden.append((jax.nn.silu(both[:, :half]) * both[:, half:]).astype(jnp.bfloat16))

    routed = []
    for p in range(PARTS):
        result = sum(
            dot(hidden[i], outer[i][:, p * cols : (p + 1) * cols])
            .astype(jnp.bfloat16)
            .astype(jnp.float32)
            for i in range(2)
        ).astype(jnp.bfloat16)
        result = result.reshape(plane, line, capacity, cols)
        back = jnp.stack([partner(result[o], PLANE, o) for o in range(plane)])
        partial = jnp.einsum(
            "oksn,oksd->knd", spread, back, preferred_element_type=jnp.float32
        )
        total = partial[0]
        for k in range(1, line):
            total = total + partner(partial[k].astype(jnp.bfloat16), "z", k).astype(jnp.float32)
        routed.append(total)
    routed = jnp.concatenate(routed, axis=1)

    total_out = resid.astype(jnp.float32) + shared + routed
    hidden_out = jnp.where(live[0][:, None] == 1, total_out, 0.0).astype(jnp.bfloat16)
    return (hidden_out[None], accepted_kv)


def solution(mesh):
    line = 4
    shape = (line, mesh.shape["req"] // line, mesh.shape["head"] // 2, 2)
    grid = Mesh(mesh.devices.reshape(shape), ALL)
    req = ("z", "y")
    in_specs = (
        P(ALL, None, None),
        P(ALL, None),
        P(req, None),
        P(req),
        P(req, None),
        P(ALL, None, None),
        P(req, HEAD, None, None),
        P(),
        P(None, HEAD),
        P(HEAD, None),
        P(),
        P(None, HEAD),
        P(None, HEAD),
        P(HEAD, None),
        P(),
        P(ALL, None, None),
        P(ALL, None, None),
    )
    out_specs = (P(ALL, None, None), P(req, HEAD, None, None))
    return jax.shard_map(body, mesh=grid, in_specs=in_specs, out_specs=out_specs, check_vma=False)
```

time: 322 us -> 182 us (0.57)
  blocking collectives: 98.1 us -> 0 us
  waiting for transfers between devices: 126 us -> 55.3 us
  starting transfers between devices: 4 us -> 48.8 us
  matrix products: 33.9 us -> 56.5 us
  local copies, waits for them, and re-layouts: 21.9 us -> 8.92 us
  between operations: 14.3 us -> 1.33 us
  other arithmetic: 22.9 us -> 10.9 us
    all_to_all x1 -> x0, blocking collectives: 98.1 us -> none  [body(): lax.all_to_all(outgoing, ('req', 'head'), split_axis=0, concat_axis=0, ti...]
    ppermute x0 -> x40, waiting for transfers between devices: none -> 55.3 us  [partner(): return lax.ppermute(value, axes, [(i, i ^ offset) for i in range(size)])]
    all_gather x2 -> x0, waiting for transfers between devices: 50.3 us -> none  [the longest x1 35.4 us: body(): normed_all = lax.all_gather(normed, 'head', axis=0, tiled=True)]
    ppermute x0 -> x40, starting transfers between devices: none -> 48.8 us  [partner(): return lax.ppermute(value, axes, [(i, i ^ offset) for i in range(size)])]
    all_to_all x1 -> x0, waiting for transfers between devices: 45.1 us -> none  [body(): lax.all_to_all(partial_value, ('req', 'head'), split_axis=0, concat_axis=...]
    reduce_scatter x2 -> x0, waiting for transfers between devices: 28.9 us -> none  [the longest x1 28.9 us: body(): lax.psum_scatter(jnp.dot(block, w_out, preferred_element_type=jnp.float32...]
    dot_general x17 -> x33, matrix products: 32 us -> 54.5 us  [the longest x19 44.8 us: dot(): return jnp.dot(left, right, preferred_element_type=jnp.float32)]
    gather x6 -> x2, local copies, waits for them, and re-layouts: 15.5 us -> 1.18 us  [the longest x1 0.61 us: body(): rows = jnp.stack(rows_by)[order].reshape(group_count * tree, width)]
  transfers between devices with their start and end apart: 5 -> 40, of which waited for: 4 -> 15; matrix products, arithmetic and copies ran while one was open for 14% -> 41% of each run, Pallas kernels for 0% -> 0%
where the time goes in v1:
time: 182 us
  matrix products  56.5 us (31%)
  waiting for transfers between devices  55.3 us (30%)
  starting transfers between devices  48.8 us (27%)
  other arithmetic  10.9 us (6%)
  local copies, waits for them, and re-layouts  8.92 us (5%)
    ppermute x40, waiting for transfers between devices, partner(): return lax.ppermute(value, axes, [(i, i ^ offset) for i in range(size)])  55.3 us
    ppermute x40, starting transfers between devices, partner(): return lax.ppermute(value, axes, [(i, i ^ offset) for i in range(size)])  48.8 us
    dot_general x19, matrix products, dot(): return jnp.dot(left, right, preferred_element_type=jnp.float32)  44.8 us
    dot_general x8, matrix products, body(): jnp.einsum('ksn,knd->ksd', pick_bf[o], stack, preferred_element_type=jnp....  6.79 us
    unnamed x20, local copies, waits for them, and re-layouts  5.54 us
  transfers between devices with their start and end apart: 40, of which 15 were waited for; matrix products, arithmetic and copies ran while one was open for 41% of the time, Pallas kernels for 0%

profile of v1, /device:TPU:0, one launch (start us, length us, event | category | flops | bytes accessed | tf_op | source)
XLA Modules:
  0.0 181.7 jit_solution(15753969138417317836)
XLA Ops:
  0.6 3.0 %collective-permute-start.1 = (bf16[64,2048]{1,0:T(8,128)(2,1)}, bf16[64,2048]{1,0:T(8,128)(2,1)S(1)}, u32[]{:S(2)}, u32[]{:S(2)}) collective-permute-start(bf16[64,2048]{1,0:T(8,128)(2,1)} %bitcast.207), channel_id=1, source_target_pairs={{0,2},{2,0},{1,3},{3,1},{4,6},{6,4},{5,7},{7,5},{8,10},{10,8},{9,1... | collective-permute-start | bytes 786440 | tf_op jit(solution)/shard_map/ppermute | solution.py:21
  5.9 2.6 %collective-permute-start.12 = (s32[64,6]{0,1:T(8,128)S(1)}, s32[64,6]{0,1:T(8,128)S(1)}, u32[]{:S(2)}, u32[]{:S(2)}) collective-permute-start(s32[64,6]{0,1:T(8,128)S(1)} %bitcast.226), channel_id=1, source_target_pairs={{0,16},{8,24},{16,0},{24,8},{1,17},{9,25},{17,1},{25,9},{2,18},{10... | collective-permute-start | bytes 4616 | tf_op jit(solution)/shard_map/ppermute | solution.py:21
  14.9 4.8 %copy.52 = bf16[2048,768]{0,1:T(8,128)(2,1)} copy(bf16[2048,768]{1,0:T(8,128)(2,1)} %param.25) | data formatting | bytes 6291456 | tf_op args[8]
  22.0 3.2 %collective-permute-done.2 = bf16[64,2048]{1,0:T(8,128)(2,1)S(1)} collective-permute-done((bf16[64,2048]{1,0:T(8,128)(2,1)S(1)}, bf16[64,2048]{1,0:T(8,128)(2,1)S(1)}, u32[]{:S(2)}, u32[]{:S(2)}) %collective-permute-start.2) | collective-permute-done | bytes 262176 | tf_op jit(solution)/shard_map/ppermute | solution.py:21
  26.4 3.1 %convolution_bitcast_fusion.2 = f32[4,1,6,64,128]{4,3,2,0,1:T(8,128)S(1)} fusion(bf16[6,128,2048,1]{2,1,0,3:T(8,128)(2,1)} %bitcast.198, bf16[4,64,2048]{2,1,0:T(8,128)(2,1)S(1)} %gather_fusion, f32[2048]{0:T(1024)S(1)} %copy-done.6, f32[4,64]{1,0:T(4,128)S(1)} %add_rsqrt_fusion), kind=kOutput, calls=%fused_computation.45 | convolution fusion | flops 807403520 | bytes 4989952 | tf_op jit(solution)/shard_map/dot_general | solution.py:31
  34.3 3.1 %fusion.2 = f32[4,256,128]{2,1,0:T(8,128)S(1)} fusion(f32[4,256,2048]{2,1,0:T(8,128)S(1)} %get-tuple-element.33, f32[4,256]{1,0:T(4,128)S(1)} %add.209, f32[4,256]{1,0:T(4,128)S(1)} %max.8, pred[4,2048]{1,0:T(4,128)(4,1)S(1)} %iota_compare_fusion.7, bf16[4,1,2048,256]{3,2,0,1:T(8,128)(2,1)S(1)} %bitcast.206), kind=kOutput, calls=%fused_computation.8 | convolution fusion | flops 547356672 | bytes 11026432 | tf_op jit(solution)/shard_map/vmap(vmap())/dot_general | solution.py:31
  38.8 2.0 %fusion.164 = f32[128,2048]{1,0:T(8,128)S(1)} fusion(bf16[128,512]{1,0:T(8,128)(2,1)S(1)} %bitcast.211, bf16[512,2048]{1,0:T(8,128)(2,1)} %param.26), kind=kOutput, calls=%fused_computation.270 | convolution fusion | flops 268435456 | bytes 3276800 | tf_op jit(solution)/shard_map/dot_general | solution.py:31
  40.9 2.0 %convolution_add_fusion.3 = f32[128,2048]{1,0:T(8,128)S(1)} fusion(f32[128,2048]{1,0:T(8,128)S(1)} %fusion.164, bf16[128,512]{1,0:T(8,128)(2,1)S(1)} %collective-permute-done.3, bf16[512,2048]{1,0:T(8,128)(2,1)} %collective-permute-done.4), kind=kOutput, calls=%fused_computation.22 | convolution fusion | flops 268697600 | bytes 4325376 | tf_op jit(solution)/shard_map/dot_general | solution.py:31
  44.2 7.4 %collective-permute-done.5 = bf16[64,2048]{1,0:T(8,128)(2,1)S(1)} collective-permute-done((bf16[64,2048]{1,0:T(8,128)(2,1)S(1)}, bf16[64,2048]{1,0:T(8,128)(2,1)S(1)}, u32[]{:S(2)}, u32[]{:S(2)}) %collective-permute-start.5) | collective-permute-done | bytes 262176 | tf_op jit(solution)/shard_map/ppermute | solution.py:21
  52.8 3.5 %collective-permute-start.18 = (bf16[64,1024]{1,0:T(8,128)(2,1)S(1)}, bf16[64,1024]{1,0:T(8,128)(2,1)S(1)}, u32[]{:S(2)}, u32[]{:S(2)}) collective-permute-start(bf16[64,1024]{1,0:T(8,128)(2,1)S(1)} %get-tuple-element.22), channel_id=1, source_target_pairs={{0,16},{8,24},{16,0},{24,8},{1,17},{9,25},{17,1},{25,9},{2,18},{10... | collective-permute-start | bytes 393224 | tf_op jit(solution)/shard_map/ppermute | solution.py:21
  58.7 7.6 %collective-permute-done.18 = bf16[64,1024]{1,0:T(8,128)(2,1)S(1)} collective-permute-done((bf16[64,1024]{1,0:T(8,128)(2,1)S(1)}, bf16[64,1024]{1,0:T(8,128)(2,1)S(1)}, u32[]{:S(2)}, u32[]{:S(2)}) %collective-permute-start.18) | collective-permute-done | bytes 131104 | tf_op jit(solution)/shard_map/ppermute | solution.py:21
  66.3 5.0 %collective-permute-start.16 = (bf16[64,1024]{1,0:T(8,128)(2,1)S(1)}, bf16[64,1024]{1,0:T(8,128)(2,1)S(1)}, u32[]{:S(2)}, u32[]{:S(2)}) collective-permute-start(bf16[64,1024]{1,0:T(8,128)(2,1)S(1)} %get-tuple-element.23), channel_id=1, source_target_pairs={{0,24},{8,16},{16,8},{24,0},{1,25},{9,17},{17,9},{25,1},{2,26},{10... | collective-permute-start | bytes 393224 | tf_op jit(solution)/shard_map/ppermute | solution.py:21
  71.6 5.9 %collective-permute-done.15 = bf16[64,1024]{1,0:T(8,128)(2,1)S(1)} collective-permute-done((bf16[64,1024]{1,0:T(8,128)(2,1)S(1)}, bf16[64,1024]{1,0:T(8,128)(2,1)S(1)}, u32[]{:S(2)}, u32[]{:S(2)}) %collective-permute-start.15) | collective-permute-done | bytes 131104 | tf_op jit(solution)/shard_map/ppermute | solution.py:21
  89.7 3.3 %fusion.105 = f32[128,2048]{1,0:T(8,128)S(1)} fusion(bf16[352,2048]{1,0:T(8,128)(2,1)} %param.30, f32[128,352]{0,1:T(8,128)S(1)} %fusion.154, bf16[2048,352]{0,1:T(8,128)(2,1)} %param.28, bf16[64,2048]{1,0:T(8,128)(2,1)S(1)} %collective-permute-done.6, bf16[64,2048]{1,0:T(8,128)(2,1)S(1)} %fusion.59), kind=kOutput, calls=%fused_computation.186 | convolution fusion | flops 370417664 | bytes 4636672 | tf_op jit(solution)/shard_map/dot_general | solution.py:31
  95.7 3.3 %convolution_add_fusion.2 = f32[128,2048]{1,0:T(8,128)S(1)} fusion(f32[128,2048]{1,0:T(8,128)S(1)} %fusion.105, bf16[352,2048]{1,0:T(8,128)(2,1)} %collective-permute-done.9, f32[128,352]{0,1:T(8,128)S(1)} %fusion.152, bf16[2048,352]{0,1:T(8,128)(2,1)} %collective-permute-done.7, bf16[64,2048]{1,0:T(8,128)(2,1)S(1)} %collective-permute-done.6, ...), kind=kOutput, calls=%fused_computation.21 | convolution fusion | flops 370679808 | bytes 5685248 | tf_op jit(solution)/shard_map/dot_general | solution.py:31
  100.0 7.2 %collective-permute-done.24 = bf16[128,1024]{1,0:T(8,128)(2,1)} collective-permute-done((bf16[128,1024]{1,0:T(8,128)(2,1)}, bf16[128,1024]{1,0:T(8,128)(2,1)}, u32[]{:S(2)}, u32[]{:S(2)}) %collective-permute-start.24) | collective-permute-done | bytes 262176 | tf_op jit(solution)/shard_map/ppermute | solution.py:21
  110.0 4.0 %fusion.6 = f32[512,1408]{1,0:T(8,128)S(1)} fusion(bf16[1,2048,1408]{2,1,0:T(8,128)(2,1)} %param.32, bf16[128,1024]{1,0:T(8,128)(2,1)} %collective-permute-done.25, bf16[128,1024]{1,0:T(8,128)(2,1)} %collective-permute-done.24, bf16[128,1024]{1,0:T(8,128)(2,1)} %collective-permute-done.23, bf16[128,1024]{1,0:T(8,128)(2,1)} %bitcast.264), kind=kOutput, calls=%fused_computation.14 | convolution fusion | flops 1480589312 | bytes 6815744 | tf_op jit(solution)/shard_map/dot_general | solution.py:31
  114.8 5.4 %collective-permute-done.21 = bf16[128,1024]{1,0:T(8,128)(2,1)S(1)} collective-permute-done((bf16[128,1024]{1,0:T(8,128)(2,1)S(1)}, bf16[128,1024]{1,0:T(8,128)(2,1)S(1)}, u32[]{:S(2)}, u32[]{:S(2)}) %collective-permute-start.21) | collective-permute-done | bytes 262176 | tf_op jit(solution)/shard_map/ppermute | solution.py:21
  120.2 3.6 %convolution_add_fusion.1 = f32[512,1408]{1,0:T(8,128)S(1)} fusion(f32[512,1408]{1,0:T(8,128)S(1)} %fusion.6, bf16[1,2048,1408]{2,1,0:T(8,128)(2,1)} %param.32, bf16[128,1024]{1,0:T(8,128)(2,1)S(1)} %collective-permute-done.22, bf16[128,1024]{1,0:T(8,128)(2,1)S(1)} %collective-permute-done.21, bf16[128,1024]{1,0:T(8,128)(2,1)S(1)} %collective-permute-done.20, ...), kind=kOutput, calls=%fused_computation.10 | convolution fusion | flops 1481310208 | bytes 9699328 | tf_op jit(solution)/shard_map/dot_general | solution.py:31
  124.3 2.3 %convolution_convert_fusion.3 = bf16[512,1024]{1,0:T(8,128)(2,1)S(1)} fusion(bf16[512,704]{1,0:T(8,128)(2,1)S(1)} %fusion.16, bf16[704,2048]{1,0:T(8,128)(2,1)} %bitcast.55), kind=kOutput, calls=%fused_computation.38 | convolution fusion | flops 738721792 | bytes 3211264 | tf_op jit(solution)/shard_map/dot_general | solution.py:31
  126.7 2.6 %convolution_convert_fusion.1 = bf16[512,1024]{1,0:T(8,128)(2,1)S(1)} fusion(bf16[512,704]{1,0:T(8,128)(2,1)S(1)} %fusion.16, bf16[704,2048]{1,0:T(8,128)(2,1)} %bitcast.55), kind=kOutput, calls=%fused_computation.36 | convolution fusion | flops 738721792 | bytes 3211264 | tf_op jit(solution)/shard_map/dot_general | solution.py:31
  129.3 3.9 %fusion.3 = f32[512,1408]{1,0:T(8,128)S(1)} fusion(bf16[2048,1408]{1,0:T(8,128)(2,1)} %collective-permute-done.26, bf16[128,1024]{1,0:T(8,128)(2,1)} %collective-permute-done.25, bf16[128,1024]{1,0:T(8,128)(2,1)} %collective-permute-done.24, bf16[128,1024]{1,0:T(8,128)(2,1)} %collective-permute-done.23, bf16[128,1024]{1,0:T(8,128)(2,1)S(1)} %bitcast.265), kind=kOutput, calls=%fused_computation.11 | convolution fusion | flops 1480589312 | bytes 6815744 | tf_op jit(solution)/shard_map/dot_general | solution.py:31
  133.2 3.6 %convolution_add_fusion = f32[512,1408]{1,0:T(8,128)S(1)} fusion(f32[512,1408]{1,0:T(8,128)S(1)} %fusion.3, bf16[2048,1408]{1,0:T(8,128)(2,1)} %collective-permute-done.26, bf16[128,1024]{1,0:T(8,128)(2,1)S(1)} %collective-permute-done.22, bf16[128,1024]{1,0:T(8,128)(2,1)S(1)} %collective-permute-done.21, bf16[128,1024]{1,0:T(8,128)(2,1)S(1)} %collective-permute-done.20, ...), kind=kOutput, calls=%fused_computation.9 | convolution fusion | flops 1481310208 | bytes 9699328 | tf_op jit(solution)/shard_map/dot_general | solution.py:31
  137.4 2.4 %add_convert_fusion.1 = bf16[512,1024]{1,0:T(8,128)(2,1)S(1)} fusion(bf16[512,1024]{1,0:T(8,128)(2,1)S(1)} %convolution_convert_fusion.3, bf16[512,704]{1,0:T(8,128)(2,1)S(1)} %fusion.15, bf16[704,2048]{1,0:T(8,128)(2,1)} %collective-permute-done.27), kind=kOutput, calls=%fused_computation.30 | convolution fusion | flops 740818944 | bytes 4259840 | tf_op jit(solution)/shard_map/dot_general | solution.py:31
  143.4 2.4 %add_convert_fusion = bf16[512,1024]{1,0:T(8,128)(2,1)S(1)} fusion(bf16[512,1024]{1,0:T(8,128)(2,1)S(1)} %convolution_convert_fusion.1, bf16[512,704]{1,0:T(8,128)(2,1)S(1)} %fusion.15, bf16[704,2048]{1,0:T(8,128)(2,1)} %collective-permute-done.27), kind=kOutput, calls=%fused_computation.29 | convolution fusion | flops 740818944 | bytes 4259840 | tf_op jit(solution)/shard_map/dot_general | solution.py:31
  150.6 4.3 %collective-permute-done.29 = bf16[4,32,1024]{2,1,0:T(8,128)(2,1)S(1)} collective-permute-done((bf16[4,32,1024]{2,1,0:T(8,128)(2,1)S(1)}, bf16[4,32,1024]{2,1,0:T(8,128)(2,1)S(1)}, u32[]{:S(2)}, u32[]{:S(2)}) %collective-permute-start.29) | collective-permute-done | bytes 262176 | tf_op jit(solution)/shard_map/ppermute | solution.py:21
  156.1 4.3 %collective-permute-start.31 = (bf16[64,1024]{1,0:T(8,128)(2,1)S(1)}, bf16[64,1024]{1,0:T(8,128)(2,1)S(1)}, u32[]{:S(2)}, u32[]{:S(2)}) collective-permute-start(bf16[64,1024]{1,0:T(8,128)(2,1)S(1)} %get-tuple-element.14), channel_id=1, source_target_pairs={{0,8},{8,0},{16,24},{24,16},{1,9},{9,1},{17,25},{25,17},{2,10},{10... | collective-permute-start | bytes 393224 | tf_op jit(solution)/shard_map/ppermute | solution.py:21
  160.4 3.1 %collective-permute-start.32 = (bf16[64,1024]{1,0:T(8,128)(2,1)S(1)}, bf16[64,1024]{1,0:T(8,128)(2,1)S(1)}, u32[]{:S(2)}, u32[]{:S(2)}) collective-permute-start(bf16[64,1024]{1,0:T(8,128)(2,1)S(1)} %get-tuple-element.16), channel_id=1, source_target_pairs={{0,16},{8,24},{16,0},{24,8},{1,17},{9,25},{17,1},{25,9},{2,18},{10... | collective-permute-start | bytes 393224 | tf_op jit(solution)/shard_map/ppermute | solution.py:21
  164.7 2.5 %collective-permute-start.33 = (bf16[64,1024]{1,0:T(8,128)(2,1)S(1)}, bf16[64,1024]{1,0:T(8,128)(2,1)S(1)}, u32[]{:S(2)}, u32[]{:S(2)}) collective-permute-start(bf16[64,1024]{1,0:T(8,128)(2,1)S(1)} %get-tuple-element.15), channel_id=1, source_target_pairs={{0,24},{8,16},{16,8},{24,0},{1,25},{9,17},{17,9},{25,1},{2,26},{10... | collective-permute-start | bytes 393224 | tf_op jit(solution)/shard_map/ppermute | solution.py:21
  169.6 2.5 %collective-permute-start.39 = (bf16[64,1024]{1,0:T(8,128)(2,1)S(1)}, bf16[64,1024]{1,0:T(8,128)(2,1)S(1)}, u32[]{:S(2)}, u32[]{:S(2)}) collective-permute-start(bf16[64,1024]{1,0:T(8,128)(2,1)S(1)} %get-tuple-element.18), channel_id=1, source_target_pairs={{0,24},{8,16},{16,8},{24,0},{1,25},{9,17},{17,9},{25,1},{2,26},{10... | collective-permute-start | bytes 393224 | tf_op jit(solution)/shard_map/ppermute | solution.py:21
  173.2 2.4 %collective-permute-done.37 = bf16[64,1024]{1,0:T(8,128)(2,1)S(1)} collective-permute-done((bf16[64,1024]{1,0:T(8,128)(2,1)S(1)}, bf16[64,1024]{1,0:T(8,128)(2,1)S(1)}, u32[]{:S(2)}, u32[]{:S(2)}) %collective-permute-start.37) | collective-permute-done | bytes 131104 | tf_op jit(solution)/shard_map/ppermute | solution.py:21
  175.6 5.1 %collective-permute-done.38 = bf16[64,1024]{1,0:T(8,128)(2,1)S(1)} collective-permute-done((bf16[64,1024]{1,0:T(8,128)(2,1)S(1)}, bf16[64,1024]{1,0:T(8,128)(2,1)S(1)}, u32[]{:S(2)}, u32[]{:S(2)}) %collective-permute-start.38) | collective-permute-done | bytes 131104 | tf_op jit(solution)/shard_map/ppermute | solution.py:21
  (171 shorter events, 58.9 us)
Async XLA Ops:
  0.6 20.8 %collective-permute-start.1 = (bf16[64,2048]{1,0:T(8,128)(2,1)}, bf16[64,2048]{1,0:T(8,128)(2,1)S(1)}, u32[]{:S(2)}, u32[]{:S(2)}) collective-permute-start(bf16[64,2048]{1,0:T(8,128)(2,1)} %bitcast.207), channel_id=1, source_target_pairs={{0,2},{2,0},{1,3},{3,1},{4,6},{6,4},{5,7},{7,5},{8,10},{10,8},{9,1... | collective-permute-start | bytes 786440 | tf_op jit(solution)/shard_map/ppermute | solution.py:21
  3.6 18.4 %collective-permute-start = (bf16[64,2048]{1,0:T(8,128)(2,1)}, bf16[64,2048]{1,0:T(8,128)(2,1)S(1)}, u32[]{:S(2)}, u32[]{:S(2)}) collective-permute-start(bf16[64,2048]{1,0:T(8,128)(2,1)} %bitcast.208), channel_id=1, source_target_pairs={{0,1},{1,0},{2,3},{3,2},{4,5},{5,4},{6,7},{7,6},{8,9},{9,8},{10,11... | collective-permute-start | bytes 786440 | tf_op jit(solution)/shard_map/ppermute | solution.py:21
  4.3 16.0 %collective-permute-start.11 = (s32[64,6]{0,1:T(8,128)S(1)}, s32[64,6]{0,1:T(8,128)S(1)}, u32[]{:S(2)}, u32[]{:S(2)}) collective-permute-start(s32[64,6]{0,1:T(8,128)S(1)} %bitcast.225), channel_id=1, source_target_pairs={{0,8},{8,0},{16,24},{24,16},{1,9},{9,1},{17,25},{25,17},{2,10},{10... | collective-permute-start | bytes 4616 | tf_op jit(solution)/shard_map/ppermute | solution.py:21
  5.9 14.5 %collective-permute-start.12 = (s32[64,6]{0,1:T(8,128)S(1)}, s32[64,6]{0,1:T(8,128)S(1)}, u32[]{:S(2)}, u32[]{:S(2)}) collective-permute-start(s32[64,6]{0,1:T(8,128)S(1)} %bitcast.226), channel_id=1, source_target_pairs={{0,16},{8,24},{16,0},{24,8},{1,17},{9,25},{17,1},{25,9},{2,18},{10... | collective-permute-start | bytes 4616 | tf_op jit(solution)/shard_map/ppermute | solution.py:21
  8.5 12.4 %collective-permute-start.13 = (s32[64,6]{0,1:T(8,128)S(1)}, s32[64,6]{0,1:T(8,128)S(1)}, u32[]{:S(2)}, u32[]{:S(2)}) collective-permute-start(s32[64,6]{0,1:T(8,128)S(1)} %bitcast.227), channel_id=1, source_target_pairs={{0,24},{8,16},{16,8},{24,0},{1,25},{9,17},{17,9},{25,1},{2,26},{10... | collective-permute-start | bytes 4616 | tf_op jit(solution)/shard_map/ppermute | solution.py:21
  20.4 20.5 %collective-permute-start.4 = (bf16[512,2048]{1,0:T(8,128)(2,1)}, bf16[512,2048]{1,0:T(8,128)(2,1)}, u32[]{:S(2)}, u32[]{:S(2)}) collective-permute-start(bf16[512,2048]{1,0:T(8,128)(2,1)} %param.26), channel_id=1, source_target_pairs={{0,1},{1,0},{2,3},{3,2},{4,5},{5,4},{6,7},{7,6},{8,9},{9,8},{10,11... | collective-permute-start | bytes 6291464 | tf_op jit(solution)/shard_map/ppermute | solution.py:21
  20.4 66.4 %collective-permute-start.8 = (bf16[2048,352]{0,1:T(8,128)(2,1)}, bf16[2048,352]{0,1:T(8,128)(2,1)}, u32[]{:S(2)}, u32[]{:S(2)}) collective-permute-start(bf16[2048,352]{0,1:T(8,128)(2,1)} %param.29), channel_id=1, source_target_pairs={{0,1},{1,0},{2,3},{3,2},{4,5},{5,4},{6,7},{7,6},{8,9},{9,8},{10,11... | collective-permute-start | bytes 4325384 | tf_op jit(solution)/shard_map/ppermute | solution.py:21
  20.9 108.4 %collective-permute-start.26 = (bf16[2048,1408]{1,0:T(8,128)(2,1)}, bf16[2048,1408]{1,0:T(8,128)(2,1)}, u32[]{:S(2)}, u32[]{:S(2)}) collective-permute-start(bf16[2048,1408]{1,0:T(8,128)(2,1)} %bitcast.230), channel_id=1, source_target_pairs={{0,1},{1,0},{2,3},{3,2},{4,5},{5,4},{6,7},{7,6},{8,9},{9,8},{10,11... | collective-permute-start | bytes 17301512 | tf_op jit(solution)/shard_map/ppermute | solution.py:21
  52.8 13.5 %collective-permute-start.18 = (bf16[64,1024]{1,0:T(8,128)(2,1)S(1)}, bf16[64,1024]{1,0:T(8,128)(2,1)S(1)}, u32[]{:S(2)}, u32[]{:S(2)}) collective-permute-start(bf16[64,1024]{1,0:T(8,128)(2,1)S(1)} %get-tuple-element.22), channel_id=1, source_target_pairs={{0,16},{8,24},{16,0},{24,8},{1,17},{9,25},{17,1},{25,9},{2,18},{10... | collective-permute-start | bytes 393224 | tf_op jit(solution)/shard_map/ppermute | solution.py:21
  56.3 10.0 %collective-permute-start.19 = (bf16[64,1024]{1,0:T(8,128)(2,1)S(1)}, bf16[64,1024]{1,0:T(8,128)(2,1)S(1)}, u32[]{:S(2)}, u32[]{:S(2)}) collective-permute-start(bf16[64,1024]{1,0:T(8,128)(2,1)S(1)} %get-tuple-element.22), channel_id=1, source_target_pairs={{0,24},{8,16},{16,8},{24,0},{1,25},{9,17},{17,9},{25,1},{2,26},{10... | collective-permute-start | bytes 393224 | tf_op jit(solution)/shard_map/ppermute | solution.py:21
  58.7 12.9 %collective-permute-start.14 = (bf16[64,1024]{1,0:T(8,128)(2,1)S(1)}, bf16[64,1024]{1,0:T(8,128)(2,1)S(1)}, u32[]{:S(2)}, u32[]{:S(2)}) collective-permute-start(bf16[64,1024]{1,0:T(8,128)(2,1)S(1)} %get-tuple-element.23), channel_id=1, source_target_pairs={{0,8},{8,0},{16,24},{24,16},{1,9},{9,1},{17,25},{25,17},{2,10},{10... | collective-permute-start | bytes 393224 | tf_op jit(solution)/shard_map/ppermute | solution.py:21
  66.3 11.2 %collective-permute-start.15 = (bf16[64,1024]{1,0:T(8,128)(2,1)S(1)}, bf16[64,1024]{1,0:T(8,128)(2,1)S(1)}, u32[]{:S(2)}, u32[]{:S(2)}) collective-permute-start(bf16[64,1024]{1,0:T(8,128)(2,1)S(1)} %get-tuple-element.23), channel_id=1, source_target_pairs={{0,16},{8,24},{16,0},{24,8},{1,17},{9,25},{17,1},{25,9},{2,18},{10... | collective-permute-start | bytes 393224 | tf_op jit(solution)/shard_map/ppermute | solution.py:21
  66.3 11.2 %collective-permute-start.16 = (bf16[64,1024]{1,0:T(8,128)(2,1)S(1)}, bf16[64,1024]{1,0:T(8,128)(2,1)S(1)}, u32[]{:S(2)}, u32[]{:S(2)}) collective-permute-start(bf16[64,1024]{1,0:T(8,128)(2,1)S(1)} %get-tuple-element.23), channel_id=1, source_target_pairs={{0,24},{8,16},{16,8},{24,0},{1,25},{9,17},{17,9},{25,1},{2,26},{10... | collective-permute-start | bytes 393224 | tf_op jit(solution)/shard_map/ppermute | solution.py:21
  71.6 21.4 %collective-permute-start.7 = (bf16[2048,352]{0,1:T(8,128)(2,1)}, bf16[2048,352]{0,1:T(8,128)(2,1)}, u32[]{:S(2)}, u32[]{:S(2)}) collective-permute-start(bf16[2048,352]{0,1:T(8,128)(2,1)} %param.28), channel_id=1, source_target_pairs={{0,1},{1,0},{2,3},{3,2},{4,5},{5,4},{6,7},{7,6},{8,9},{9,8},{10,11... | collective-permute-start | bytes 4325384 | tf_op jit(solution)/shard_map/ppermute | solution.py:21
  77.5 17.1 %collective-permute-start.9 = (bf16[352,2048]{1,0:T(8,128)(2,1)}, bf16[352,2048]{1,0:T(8,128)(2,1)}, u32[]{:S(2)}, u32[]{:S(2)}) collective-permute-start(bf16[352,2048]{1,0:T(8,128)(2,1)} %param.30), channel_id=1, source_target_pairs={{0,1},{1,0},{2,3},{3,2},{4,5},{5,4},{6,7},{7,6},{8,9},{9,8},{10,11... | collective-permute-start | bytes 4325384 | tf_op jit(solution)/shard_map/ppermute | solution.py:21
  86.3 51.1 %collective-permute-start.27 = (bf16[704,2048]{1,0:T(8,128)(2,1)}, bf16[704,2048]{1,0:T(8,128)(2,1)}, u32[]{:S(2)}, u32[]{:S(2)}) collective-permute-start(bf16[704,2048]{1,0:T(8,128)(2,1)} %bitcast.55), channel_id=1, source_target_pairs={{0,1},{1,0},{2,3},{3,2},{4,5},{5,4},{6,7},{7,6},{8,9},{9,8},{10,11... | collective-permute-start | bytes 8650760 | tf_op jit(solution)/shard_map/ppermute | solution.py:21
  86.8 12.2 %collective-permute-start.23 = (bf16[128,1024]{1,0:T(8,128)(2,1)}, bf16[128,1024]{1,0:T(8,128)(2,1)}, u32[]{:S(2)}, u32[]{:S(2)}) collective-permute-start(bf16[128,1024]{1,0:T(8,128)(2,1)} %bitcast.51), channel_id=1, source_target_pairs={{0,2},{2,0},{4,6},{6,4},{1,3},{3,1},{5,7},{7,5},{8,10},{10,8},{12,... | collective-permute-start | bytes 786440 | tf_op jit(solution)/shard_map/ppermute | solution.py:21
  93.0 14.2 %collective-permute-start.24 = (bf16[128,1024]{1,0:T(8,128)(2,1)}, bf16[128,1024]{1,0:T(8,128)(2,1)}, u32[]{:S(2)}, u32[]{:S(2)}) collective-permute-start(bf16[128,1024]{1,0:T(8,128)(2,1)} %bitcast.52), channel_id=1, source_target_pairs={{0,4},{2,6},{4,0},{6,2},{1,5},{3,7},{5,1},{7,3},{8,12},{10,14},{12... | collective-permute-start | bytes 786440 | tf_op jit(solution)/shard_map/ppermute | solution.py:21
  94.6 14.1 %collective-permute-start.25 = (bf16[128,1024]{1,0:T(8,128)(2,1)}, bf16[128,1024]{1,0:T(8,128)(2,1)}, u32[]{:S(2)}, u32[]{:S(2)}) collective-permute-start(bf16[128,1024]{1,0:T(8,128)(2,1)} %bitcast.53), channel_id=1, source_target_pairs={{0,6},{2,4},{4,2},{6,0},{1,7},{3,5},{5,3},{7,1},{8,14},{10,12},{12... | collective-permute-start | bytes 786440 | tf_op jit(solution)/shard_map/ppermute | solution.py:21
  99.0 15.0 %collective-permute-start.20 = (bf16[128,1024]{1,0:T(8,128)(2,1)}, bf16[128,1024]{1,0:T(8,128)(2,1)S(1)}, u32[]{:S(2)}, u32[]{:S(2)}) collective-permute-start(bf16[128,1024]{1,0:T(8,128)(2,1)} %bitcast.233), channel_id=1, source_target_pairs={{0,2},{2,0},{4,6},{6,4},{1,3},{3,1},{5,7},{7,5},{8,10},{10,8},{12,... | collective-permute-start | bytes 786440 | tf_op jit(solution)/shard_map/ppermute | solution.py:21
  107.2 13.0 %collective-permute-start.21 = (bf16[128,1024]{1,0:T(8,128)(2,1)S(1)}, bf16[128,1024]{1,0:T(8,128)(2,1)S(1)}, u32[]{:S(2)}, u32[]{:S(2)}) collective-permute-start(bf16[128,1024]{1,0:T(8,128)(2,1)S(1)} %bitcast.231), channel_id=1, source_target_pairs={{0,4},{2,6},{4,0},{6,2},{1,5},{3,7},{5,1},{7,3},{8,12},{10,14},{12... | collective-permute-start | bytes 786440 | tf_op jit(solution)/shard_map/ppermute | solution.py:21
  108.7 11.5 %collective-permute-start.22 = (bf16[128,1024]{1,0:T(8,128)(2,1)}, bf16[128,1024]{1,0:T(8,128)(2,1)S(1)}, u32[]{:S(2)}, u32[]{:S(2)}) collective-permute-start(bf16[128,1024]{1,0:T(8,128)(2,1)} %bitcast.232), channel_id=1, source_target_pairs={{0,6},{2,4},{4,2},{6,0},{1,7},{3,5},{5,3},{7,1},{8,14},{10,12},{12... | collective-permute-start | bytes 786440 | tf_op jit(solution)/shard_map/ppermute | solution.py:21
  114.0 66.8 %collective-permute-start.10 = (bf16[64,2048]{1,0:T(8,128)(2,1)S(1)}, bf16[64,2048]{1,0:T(8,128)(2,1)S(1)}, u32[]{:S(2)}, u32[]{:S(2)}) collective-permute-start(bf16[64,2048]{1,0:T(8,128)(2,1)S(1)} %slice.394), channel_id=1, source_target_pairs={{0,2},{2,0},{1,3},{3,1},{4,6},{6,4},{5,7},{7,5},{8,10},{10,8},{9,1... | collective-permute-start | bytes 786440 | tf_op jit(solution)/shard_map/ppermute | solution.py:21
  139.8 9.3 %collective-permute-start.28 = (bf16[4,32,1024]{2,1,0:T(8,128)(2,1)S(1)}, bf16[4,32,1024]{2,1,0:T(8,128)(2,1)S(1)}, u32[]{:S(2)}, u32[]{:S(2)}) collective-permute-start(bf16[4,32,1024]{2,1,0:T(8,128)(2,1)S(1)} %bitcast.222), channel_id=1, source_target_pairs={{0,2},{2,0},{4,6},{6,4},{1,3},{3,1},{5,7},{7,5},{8,10},{10,8},{12,... | collective-permute-start | bytes 786440 | tf_op jit(solution)/shard_map/ppermute | solution.py:21
  141.5 13.5 %collective-permute-start.29 = (bf16[4,32,1024]{2,1,0:T(8,128)(2,1)S(1)}, bf16[4,32,1024]{2,1,0:T(8,128)(2,1)S(1)}, u32[]{:S(2)}, u32[]{:S(2)}) collective-permute-start(bf16[4,32,1024]{2,1,0:T(8,128)(2,1)S(1)} %bitcast.221), channel_id=1, source_target_pairs={{0,4},{2,6},{4,0},{6,2},{1,5},{3,7},{5,1},{7,3},{8,12},{10,14},{12... | collective-permute-start | bytes 786440 | tf_op jit(solution)/shard_map/ppermute | solution.py:21
  143.0 12.7 %collective-permute-start.30 = (bf16[4,32,1024]{2,1,0:T(8,128)(2,1)S(1)}, bf16[4,32,1024]{2,1,0:T(8,128)(2,1)S(1)}, u32[]{:S(2)}, u32[]{:S(2)}) collective-permute-start(bf16[4,32,1024]{2,1,0:T(8,128)(2,1)S(1)} %bitcast.220), channel_id=1, source_target_pairs={{0,6},{2,4},{4,2},{6,0},{1,7},{3,5},{5,3},{7,1},{8,14},{10,12},{12... | collective-permute-start | bytes 786440 | tf_op jit(solution)/shard_map/ppermute | solution.py:21
  145.8 14.6 %collective-permute-start.34 = (bf16[4,32,1024]{2,1,0:T(8,128)(2,1)S(1)}, bf16[4,32,1024]{2,1,0:T(8,128)(2,1)S(1)}, u32[]{:S(2)}, u32[]{:S(2)}) collective-permute-start(bf16[4,32,1024]{2,1,0:T(8,128)(2,1)S(1)} %bitcast.219), channel_id=1, source_target_pairs={{0,2},{2,0},{4,6},{6,4},{1,3},{3,1},{5,7},{7,5},{8,10},{10,8},{12,... | collective-permute-start | bytes 786440 | tf_op jit(solution)/shard_map/ppermute | solution.py:21
  149.1 15.6 %collective-permute-start.35 = (bf16[4,32,1024]{2,1,0:T(8,128)(2,1)S(1)}, bf16[4,32,1024]{2,1,0:T(8,128)(2,1)S(1)}, u32[]{:S(2)}, u32[]{:S(2)}) collective-permute-start(bf16[4,32,1024]{2,1,0:T(8,128)(2,1)S(1)} %bitcast.217), channel_id=1, source_target_pairs={{0,4},{2,6},{4,0},{6,2},{1,5},{3,7},{5,1},{7,3},{8,12},{10,14},{12... | collective-permute-start | bytes 786440 | tf_op jit(solution)/shard_map/ppermute | solution.py:21
  154.9 12.2 %collective-permute-start.36 = (bf16[4,32,1024]{2,1,0:T(8,128)(2,1)S(1)}, bf16[4,32,1024]{2,1,0:T(8,128)(2,1)S(1)}, u32[]{:S(2)}, u32[]{:S(2)}) collective-permute-start(bf16[4,32,1024]{2,1,0:T(8,128)(2,1)S(1)} %bitcast.216), channel_id=1, source_target_pairs={{0,6},{2,4},{4,2},{6,0},{1,7},{3,5},{5,3},{7,1},{8,14},{10,12},{12... | collective-permute-start | bytes 786440 | tf_op jit(solution)/shard_map/ppermute | solution.py:21
  156.1 11.6 %collective-permute-start.31 = (bf16[64,1024]{1,0:T(8,128)(2,1)S(1)}, bf16[64,1024]{1,0:T(8,128)(2,1)S(1)}, u32[]{:S(2)}, u32[]{:S(2)}) collective-permute-start(bf16[64,1024]{1,0:T(8,128)(2,1)S(1)} %get-tuple-element.14), channel_id=1, source_target_pairs={{0,8},{8,0},{16,24},{24,16},{1,9},{9,1},{17,25},{25,17},{2,10},{10... | collective-permute-start | bytes 393224 | tf_op jit(solution)/shard_map/ppermute | solution.py:21
  167.7 13.1 %collective-permute-start.38 = (bf16[64,1024]{1,0:T(8,128)(2,1)S(1)}, bf16[64,1024]{1,0:T(8,128)(2,1)S(1)}, u32[]{:S(2)}, u32[]{:S(2)}) collective-permute-start(bf16[64,1024]{1,0:T(8,128)(2,1)S(1)} %get-tuple-element.19), channel_id=1, source_target_pairs={{0,16},{8,24},{16,0},{24,8},{1,17},{9,25},{17,1},{25,9},{2,18},{10... | collective-permute-start | bytes 393224 | tf_op jit(solution)/shard_map/ppermute | solution.py:21
  169.6 11.2 %collective-permute-start.39 = (bf16[64,1024]{1,0:T(8,128)(2,1)S(1)}, bf16[64,1024]{1,0:T(8,128)(2,1)S(1)}, u32[]{:S(2)}, u32[]{:S(2)}) collective-permute-start(bf16[64,1024]{1,0:T(8,128)(2,1)S(1)} %get-tuple-element.18), channel_id=1, source_target_pairs={{0,24},{8,16},{16,8},{24,0},{1,25},{9,17},{17,9},{25,1},{2,26},{10... | collective-permute-start | bytes 393224 | tf_op jit(solution)/shard_map/ppermute | solution.py:21
  (17 other events, 129.4 us)

commit v2 on v1

v2 whole, which is shorter than its diff:
```python
import math

import jax
import jax.numpy as jnp
from jax import lax
from jax.experimental import pallas as pl
from jax.experimental.pallas import tpu as pltpu
from jax.sharding import Mesh
from jax.sharding import PartitionSpec as P

EPSILON = 1e-06
ROPE_BASE = 10000.0
GROUPS = ((0, 1), (3,), (2,))
CHUNK = 512
ALL = ("z", "y", "x", "c")
PLANE = ("y", "x")
HEAD = ("x", "c")


def partner(value, axes, offset):
    if offset == 0:
        return value
    size = lax.axis_size(axes)
    return lax.ppermute(value, axes, [(i, i ^ offset) for i in range(size)])


def rms_norm(values, gain):
    wide = values.astype(jnp.float32)
    power = jnp.mean(wide * wide, axis=-1, keepdims=True)
    return (wide * lax.rsqrt(power + EPSILON) * gain).astype(jnp.bfloat16)


def dot(left, right):
    return jnp.dot(left, right, preferred_element_type=jnp.float32)


def ancestry(parents):
    nodes_count = parents.shape[-1]
    nodes = jnp.arange(nodes_count, dtype=jnp.int32)
    reach = (parents[..., :, None] == nodes).astype(jnp.float32) + jnp.eye(
        nodes_count, dtype=jnp.float32
    )
    for turn in range((nodes_count - 1).bit_length()):
        near = reach.astype(jnp.bfloat16)
        reach = jnp.minimum(
            jnp.einsum("rij,rjk->rik", near, near, preferred_element_type=jnp.float32), 1.0
        )
    depth = jnp.sum(reach, axis=-1) - 1.0
    return (reach, depth)


def attend_kernel(
    ids, lengths, first, second, gain, weight, cosine, sine, reach, cache, mixed, fresh, projected
):
    step = pl.program_id(0)
    tree = first.shape[0]
    head_dim = cosine.shape[2]
    group = weight.shape[1] // head_dim - 2

    @pl.when(step == 0)
    def _():
        wide = jnp.concatenate([first[...], second[...]], axis=0).astype(jnp.float32)
        power = jnp.mean(wide * wide, axis=-1, keepdims=True)
        normed = (wide * lax.rsqrt(power + EPSILON) * gain[...]).astype(jnp.bfloat16)
        projected[...] = dot(normed, weight[...])

    rows = pl.ds(pl.multiple_of(step * tree, tree), tree)
    length = lengths[ids[step]]

    def rope(values):
        return values * cosine[0] + pltpu.roll(values, head_dim // 2, 1) * sine[0]

    def column(i):
        return projected[rows, i * head_dim : (i + 1) * head_dim]

    query = jnp.concatenate([rope(column(h)).astype(jnp.bfloat16) for h in range(group)], axis=0)
    key_new = rope(column(group)).astype(jnp.bfloat16)
    value_new = column(group + 1).astype(jnp.bfloat16)
    fresh[0, :, :head_dim] = key_new
    fresh[0, :, head_dim:] = value_new
    scale = 1.0 / math.sqrt(head_dim)

    def against(keys):
        return (
            lax.dot_general(
                query, keys, (((1,), (1,)), ((), ())), preferred_element_type=jnp.float32
            )
            * scale
        )

    allowed = jnp.concatenate([reach[0]] * group, axis=0) > 0.5
    scores = jnp.where(allowed, against(key_new), -1e30)
    peak = jnp.max(scores, axis=-1, keepdims=True)
    weights = jnp.exp(scores - peak)
    total = jnp.sum(weights, axis=-1, keepdims=True)
    summed = dot(weights.astype(jnp.bfloat16), value_new)

    def chunk(j, carry):
        peak, total, summed = carry
        block = pl.ds(pl.multiple_of(j * CHUNK, CHUNK), CHUNK)
        scores = against(cache[0, block, :head_dim])
        place = j * CHUNK + lax.broadcasted_iota(jnp.int32, scores.shape, 1)
        scores = jnp.where(place < length, scores, -1e30)
        higher = jnp.maximum(peak, jnp.max(scores, axis=-1, keepdims=True))
        fade = jnp.exp(peak - higher)
        weights = jnp.exp(scores - higher)
        total = total * fade + jnp.sum(weights, axis=-1, keepdims=True)
        summed = summed * fade + dot(weights.astype(jnp.bfloat16), cache[0, block, head_dim:])
        return (higher, total, summed)

    peak, total, summed = lax.fori_loop(
        0, lax.div(length + CHUNK - 1, CHUNK), chunk, (peak, total, summed)
    )
    result = (summed / total).astype(jnp.bfloat16)
    for h in range(group):
        mixed[0, :, h * head_dim : (h + 1) * head_dim] = result[h * tree : (h + 1) * tree]


def attend(ids, lengths, first, second, gain, weight, cosine, sine, reach, cache):
    tree, width = first.shape
    slots, pair = cache.shape[1:]
    head_dim = pair // 2
    columns = weight.shape[1]
    whole = lambda i, ids, lengths: (0, 0)
    by_request = lambda i, ids, lengths: (ids[i], 0, 0)
    by_step = lambda i, ids, lengths: (i, 0, 0)
    group_columns = columns - pair
    return pl.pallas_call(
        attend_kernel,
        grid_spec=pltpu.PrefetchScalarGridSpec(
            num_scalar_prefetch=2,
            grid=(2,),
            in_specs=[
                pl.BlockSpec((tree, width), whole),
                pl.BlockSpec((tree, width), whole),
                pl.BlockSpec((1, width), whole),
                pl.BlockSpec((width, columns), whole),
                pl.BlockSpec((1, tree, head_dim), by_request),
                pl.BlockSpec((1, tree, head_dim), by_request),
                pl.BlockSpec((1, tree, tree), by_request),
                pl.BlockSpec((1, slots, pair), by_request),
            ],
            out_specs=[
                pl.BlockSpec((1, tree, group_columns), by_step),
                pl.BlockSpec((1, tree, pair), by_step),
            ],
            scratch_shapes=[pltpu.VMEM((2 * tree, columns), jnp.float32)],
        ),
        out_shape=[
            jax.ShapeDtypeStruct((2, tree, group_columns), jnp.bfloat16),
            jax.ShapeDtypeStruct((2, tree, pair), jnp.bfloat16),
        ],
        compiler_params=pltpu.CompilerParams(vmem_limit_bytes=24 * 2**20),
        cost_estimate=pl.CostEstimate(
            flops=4 * tree * (width * columns + group_columns * slots * 2),
            bytes_accessed=2 * (width * columns + 2 * slots * pair),
            transcendentals=2 * tree * slots * group_columns // head_dim,
        ),
    )(ids, lengths, first, second, gain, weight, cosine, sine, reach, cache)


def body(
    tokens,
    live,
    parents,
    lengths,
    accepted,
    routes,
    cache,
    attn_gain,
    w_qkv,
    w_out,
    ffn_gain,
    shared_gate,
    shared_up,
    shared_down,
    router,
    expert_in,
    expert_out,
):
    tree = tokens.shape[1]
    width = tokens.shape[2]
    own_rows = tokens[0]
    group_count = lax.axis_size(HEAD)
    head_dim = cache.shape[3] // 2
    me = lax.axis_index(HEAD)

    side = lax.axis_size("x")
    near = [own_rows] + [partner(own_rows, "x", o) for o in range(1, side)]
    near_core = [partner(rows, "c", 1) for rows in near]

    reach, depth = ancestry(parents)
    positions = lengths[:, None].astype(jnp.float32) + depth
    frequency = ROPE_BASE ** (-jnp.arange(head_dim // 2, dtype=jnp.float32) / (head_dim // 2))
    angle = positions[..., None] * frequency
    cosine = jnp.cos(angle)
    sine = jnp.sin(angle)
    cosine = jnp.concatenate([cosine, cosine], axis=-1)
    sine = jnp.concatenate([-sine, sine], axis=-1)

    line = lax.axis_size("z")
    own_routes, _ = lax.optimization_barrier((routes[0], sine))
    chosen = [partner(own_routes, "z", k) for k in range(line)]
    early, _ = lax.optimization_barrier(((w_out, shared_gate), near_core[0]))
    late, _ = lax.optimization_barrier(
        ((expert_in[0], expert_out[0], shared_up, shared_down), near_core[side - 1])
    )
    early = [partner(weight, "c", 1) for weight in early]
    late = [partner(weight, "c", 1) for weight in late]
    out_pair = [w_out, early[0]]

    terms = [None] * side
    fresh = [None] * side
    follow = None
    for o in reversed(range(side)):
        if follow is not None:
            near_core[o], _ = lax.optimization_barrier((near_core[o], follow))
        ids = me ^ jnp.arange(2 * o, 2 * o + 2, dtype=jnp.int32)
        mixed, fresh[o] = attend(
            ids,
            lengths,
            near[o],
            near_core[o],
            attn_gain[None],
            w_qkv,
            cosine,
            sine,
            reach,
            cache[:, 0],
        )
        follow = mixed
        other = partner(mixed[1], "c", 1)
        terms[o] = dot(mixed[0], out_pair[0]) + dot(other, out_pair[1])
    attn = terms[0]
    for o in range(1, side):
        attn = attn + partner(terms[o].astype(jnp.bfloat16), "x", o).astype(jnp.float32)
    resid = (own_rows.astype(jnp.float32) + attn).astype(jnp.bfloat16)
    normed = rms_norm(resid, ffn_gain)
    normed, gate_core, late = lax.optimization_barrier((normed, early[1], late))
    inner = [expert_in[0], late[0]]
    outer = [expert_out[0], late[1]]
    gate_pair = [shared_gate, gate_core]
    up_pair = [shared_up, late[2]]
    down_pair = [shared_down, late[3]]
    order = me ^ jnp.arange(group_count, dtype=jnp.int32)
    kept = accepted[order][:, :, None] == jnp.arange(tree, dtype=jnp.int32)
    accepted_kv = jnp.einsum(
        "ran,rnd->rad",
        kept.astype(jnp.bfloat16),
        jnp.concatenate(fresh, axis=0),
        preferred_element_type=jnp.float32,
    ).astype(jnp.bfloat16)[order][:, None]

    expert_count = router.shape[1]
    top_count = routes.shape[2]
    capacity = 4 * tree * top_count // (3 * expert_count)
    plane = lax.axis_size(PLANE)
    spot = lax.axis_index(PLANE)
    first = lax.axis_index("z") * plane
    choose = jnp.stack(chosen)
    member = jnp.any(
        choose[..., None] == jnp.arange(expert_count, dtype=jnp.int32), axis=2
    )
    before = jnp.tril(jnp.ones((tree, tree), jnp.bfloat16), -1)
    ranks = jnp.einsum(
        "nm,kme->kne", before, member.astype(jnp.bfloat16), preferred_element_type=jnp.float32
    ).astype(jnp.int32)
    near_experts = first + (spot ^ jnp.arange(plane, dtype=jnp.int32))
    is_near = near_experts[:, None] == jnp.arange(expert_count, dtype=jnp.int32)
    slot = jnp.where(member, ranks, -1)
    slot_near = jnp.sum(
        jnp.where(is_near[:, None, None, :], slot[None] + 1, 0), axis=-1
    ) - 1
    places = jnp.arange(capacity, dtype=jnp.int32)
    pick = slot_near[:, :, None, :] == places[:, None]
    pick_bf = pick.astype(jnp.bfloat16)

    line_rows = [partner(normed, "z", k) for k in range(line)]
    calm, _ = lax.optimization_barrier((normed, line_rows[1]))
    near_normed = [normed] + [partner(calm, "x", o) for o in range(1, side)]

    def dispatch(ks):
        out = [
            dot(pick_bf[:, k].reshape(plane * capacity, tree), line_rows[k])
            .astype(jnp.bfloat16)
            .reshape(plane, capacity, width)
            for k in ks
        ]
        return [
            partner(jnp.concatenate([piece[o] for piece in out], axis=0), PLANE, o)
            for o in range(plane)
        ]

    def experts(got):
        rows = jnp.concatenate(got, axis=0)
        result = 0.0
        for i in range(2):
            both = dot(rows, inner[i])
            half = both.shape[1] // 2
            hidden = (jax.nn.silu(both[:, :half]) * both[:, half:]).astype(jnp.bfloat16)
            result = result + dot(hidden, outer[i]).astype(jnp.bfloat16).astype(jnp.float32)
        return result.astype(jnp.bfloat16).reshape(plane, -1, capacity, width)

    results = {}
    for ks in GROUPS:
        made = experts(dispatch(ks))
        for i, k in enumerate(ks):
            results[k] = made[:, i]

    block = jnp.concatenate(near_normed, axis=0)
    shared_terms = 0.0
    for i in range(2):
        hidden = (jax.nn.silu(dot(block, gate_pair[i])) * dot(block, up_pair[i])).astype(
            jnp.bfloat16
        )
        shared_terms = shared_terms + dot(hidden, down_pair[i])
    shared_terms = shared_terms.reshape(side, tree, width)
    shared = shared_terms[0]
    for o in range(1, side):
        shared = shared + partner(shared_terms[o].astype(jnp.bfloat16), "x", o).astype(jnp.float32)

    logits = jnp.stack([dot(rows, router) for rows in line_rows])
    picked = jnp.where(member, jax.nn.sigmoid(logits), 0.0)
    gates = picked / jnp.sum(picked, axis=-1, keepdims=True)
    gates_near = jnp.sum(jnp.where(is_near[:, None, None, :], gates[None], 0.0), axis=-1)
    spread = jnp.where(pick, gates_near[:, :, None, :], 0.0)
    spread = spread.astype(jnp.bfloat16)

    routed = 0.0
    for k in reversed(range(line)):
        back = jnp.concatenate([partner(results[k][o], PLANE, o) for o in range(plane)], axis=0)
        weights = spread[:, k].reshape(plane * capacity, tree)
        partial = jnp.einsum("sn,sd->nd", weights, back, preferred_element_type=jnp.float32)
        if k:
            partial = partner(partial.astype(jnp.bfloat16), "z", k).astype(jnp.float32)
        routed = routed + partial

    total_out = resid.astype(jnp.float32) + shared + routed
    hidden_out = jnp.where(live[0][:, None] == 1, total_out, 0.0).astype(jnp.bfloat16)
    return (hidden_out[None], accepted_kv)


def solution(mesh):
    line = 4
    shape = (line, mesh.shape["req"] // line, mesh.shape["head"] // 2, 2)
    grid = Mesh(mesh.devices.reshape(shape), ALL)
    req = ("z", "y")
    in_specs = (
        P(ALL, None, None),
        P(ALL, None),
        P(req, None),
        P(req),
        P(req, None),
        P(ALL, None, None),
        P(req, HEAD, None, None),
        P(),
        P(None, HEAD),
        P(HEAD, None),
        P(),
        P(None, HEAD),
        P(None, HEAD),
        P(HEAD, None),
        P(),
        P(ALL, None, None),
        P(ALL, None, None),
    )
    out_specs = (P(ALL, None, None), P(req, HEAD, None, None))
    return jax.shard_map(body, mesh=grid, in_specs=in_specs, out_specs=out_specs, check_vma=False)
```

time: 182 us -> 160 us (0.88)
  waiting for transfers between devices: 55.3 us -> 39.4 us
  matrix products: 56.5 us -> 45.6 us
  Pallas kernels: 0 us -> 8.04 us
  other arithmetic: 10.9 us -> 4.07 us
  local copies, waits for them, and re-layouts: 8.92 us -> 12.3 us
    ppermute x40 -> x44, waiting for transfers between devices: 55.3 us -> 39.4 us  [partner(): return lax.ppermute(value, axes, [(i, i ^ offset) for i in range(size)])]
    dot_general x19 -> x28, matrix products: 44.8 us -> 36.2 us  [dot(): return jnp.dot(left, right, preferred_element_type=jnp.float32)]
    pallas_call x0 -> x2, Pallas kernels: none -> 8.04 us  [attend(): pl.pallas_call(attend_kernel, grid_spec=pltpu.PrefetchScalarGridSpec(num_...]
    unnamed x20 -> x62, local copies, waits for them, and re-layouts: 5.54 us -> 8.14 us
    reduce_sum x4 -> x0, other arithmetic: 2.48 us -> none  [the longest x1 1.92 us: head_group(): jnp.sum(old_weights, axis=-1, keepdims=True)]
    dot_general x12 -> x5, matrix products: 9.49 us -> 7.21 us  [the longest x4 7.02 us: body(): jnp.einsum('sn,sd->nd', weights, back, preferred_element_type=jnp.float32)]
    slice x4 -> x8, local copies, waits for them, and re-layouts: 0.19 us -> 2.28 us  [the longest x2 1.49 us: body(): results[k][o]]
    ppermute x40 -> x44, starting transfers between devices: 48.8 us -> 48.9 us  [partner(): return lax.ppermute(value, axes, [(i, i ^ offset) for i in range(size)])]
  transfers between devices with their start and end apart: 40 -> 44, of which waited for: 15 -> 13; matrix products, arithmetic and copies ran while one was open for 41% -> 33% of each run, Pallas kernels for 0% -> 5%
where the time goes in v2:
time: 160 us
  starting transfers between devices  48.9 us (31%)
  matrix products  45.6 us (28%)
  waiting for transfers between devices  39.4 us (25%)
  local copies, waits for them, and re-layouts  12.3 us (8%)
  Pallas kernels  8.04 us (5%)
  other arithmetic  4.07 us (3%)
    ppermute x44, starting transfers between devices, partner(): return lax.ppermute(value, axes, [(i, i ^ offset) for i in range(size)])  48.9 us
    ppermute x44, waiting for transfers between devices, partner(): return lax.ppermute(value, axes, [(i, i ^ offset) for i in range(size)])  39.4 us
    dot_general x28, matrix products, dot(): return jnp.dot(left, right, preferred_element_type=jnp.float32)  36.2 us
    unnamed x62, local copies, waits for them, and re-layouts  8.14 us
    pallas_call x2, Pallas kernels, attend(): pl.pallas_call(attend_kernel, grid_spec=pltpu.PrefetchScalarGridSpec(num_...  8.04 us
    dot_general x4, matrix products, body(): jnp.einsum('sn,sd->nd', weights, back, preferred_element_type=jnp.float32)  7.02 us
  transfers between devices with their start and end apart: 44, of which 13 were waited for; matrix products, arithmetic and copies ran while one was open for 33% of the time, Pallas kernels for 5%

profile of v2, /device:TPU:0, one launch (start us, length us, event | category | flops | bytes accessed | tf_op | source)
XLA Modules:
  0.0 159.8 jit_solution(5278993279416469142)
XLA Ops:
  0.6 3.0 %collective-permute-start.1 = (bf16[64,2048]{1,0:T(8,128)(2,1)}, bf16[64,2048]{1,0:T(8,128)(2,1)S(1)}, u32[]{:S(2)}, u32[]{:S(2)}) collective-permute-start(bf16[64,2048]{1,0:T(8,128)(2,1)} %bitcast.137), channel_id=1, source_target_pairs={{0,2},{2,0},{1,3},{3,1},{4,6},{6,4},{5,7},{7,5},{8,10},{10,8},{9,1... | collective-permute-start | bytes 786440 | tf_op jit(solution)/shard_map/ppermute | solution.py:24
  3.7 6.5 %collective-permute-done.1.first = bf16[64,2048]{1,0:T(8,128)(2,1)S(1)} collective-permute-done((bf16[64,2048]{1,0:T(8,128)(2,1)}, bf16[64,2048]{1,0:T(8,128)(2,1)S(1)}, u32[]{:S(2)}, u32[]{:S(2)}) %collective-permute-start.1) | collective-permute-done | bytes 262176 | tf_op jit(solution)/shard_map/ppermute | solution.py:24
  14.9 1.9 %collective-permute-start.15 = (s32[64,6]{0,1:T(8,128)S(1)}, s32[64,6]{0,1:T(8,128)S(1)}, u32[]{:S(2)}, u32[]{:S(2)}) collective-permute-start(s32[64,6]{0,1:T(8,128)S(1)} %bitcast.152), channel_id=1, source_target_pairs={{0,8},{8,0},{16,24},{24,16},{1,9},{9,1},{17,25},{25,17},{2,10},{10... | collective-permute-start | bytes 4616 | tf_op jit(solution)/shard_map/ppermute | solution.py:24
  16.7 2.6 %collective-permute-start.16 = (s32[64,6]{0,1:T(8,128)S(1)}, s32[64,6]{0,1:T(8,128)S(1)}, u32[]{:S(2)}, u32[]{:S(2)}) collective-permute-start(s32[64,6]{0,1:T(8,128)S(1)} %bitcast.153), channel_id=1, source_target_pairs={{0,16},{8,24},{16,0},{24,8},{1,17},{9,25},{17,1},{25,9},{2,18},{10... | collective-permute-start | bytes 4616 | tf_op jit(solution)/shard_map/ppermute | solution.py:24
  21.3 3.5 %collective-permute-done.17 = s32[64,6]{0,1:T(8,128)S(1)} collective-permute-done((s32[64,6]{0,1:T(8,128)S(1)}, s32[64,6]{0,1:T(8,128)S(1)}, u32[]{:S(2)}, u32[]{:S(2)}) %collective-permute-start.17) | collective-permute-done | bytes 1568 | tf_op jit(solution)/shard_map/ppermute | solution.py:24
  25.2 2.2 %copy-done.2 = bf16[4,1,2048,256]{3,2,1,0:T(8,128)(2,1)S(1)} copy-done((bf16[4,1,2048,256]{3,2,1,0:T(8,128)(2,1)S(1)}, bf16[4,1,2048,256]{3,2,1,0:T(8,128)(2,1)}, u32[]{:S(2)}) %copy-start.2) | copy-done | bytes 4194328
  27.4 1.9 %copy-done.4 = bf16[2048,768]{1,0:T(8,128)(2,1)S(1)} copy-done((bf16[2048,768]{1,0:T(8,128)(2,1)S(1)}, bf16[2048,768]{1,0:T(8,128)(2,1)}, u32[]{:S(2)}) %copy-start.4) | copy-done | bytes 3145752
  30.6 3.3 %shard_map.176 = (bf16[2,64,512]{2,1,0:T(8,128)(2,1)S(1)}, bf16[2,64,256]{2,1,0:T(8,128)(2,1)S(1)}) custom-call(s32[2]{0:T(128)S(1)} %add_xor_fusion.ids, s32[4]{0:T(128)S(1)} %copy-done.8, bf16[64,2048]{1,0:T(8,128)(2,1)S(1)} %collective-permute-done.1.first, bf16[64,2048]{1,0:T(8,128)(2,1)S(1)} %collective-permute-done.2.second, f32[1,2048]{1,0:T(1,128)S(1)} %bitcast.140, ...), custom_call_target="tpu_custom_call" | custom-call | flops 939524096 | bytes 5242880 | tf_op jit(solution)/shard_map/pallas_call | solution.py:128
  34.5 4.8 %shard_map.177 = (bf16[2,64,512]{2,1,0:T(8,128)(2,1)S(1)}, bf16[2,64,256]{2,1,0:T(8,128)(2,1)S(1)}) custom-call(s32[2]{0:T(128)S(1)} %iota_xor_fusion.ids, s32[4]{0:T(128)S(1)} %copy-done.8, bf16[64,2048]{1,0:T(8,128)(2,1)S(1)} %bitcast.139, bf16[64,2048]{1,0:T(8,128)(2,1)S(1)} %collective-permute-done.second, f32[1,2048]{1,0:T(1,128)S(1)} %bitcast.141, ...), custom_call_target="tpu_custom_call" | custom-call | flops 939524096 | bytes 5242880 | tf_op jit(solution)/shard_map/pallas_call | solution.py:128
  44.4 5.4 %collective-permute-done.6 = bf16[64,2048]{1,0:T(8,128)(2,1)S(1)} collective-permute-done((bf16[64,2048]{1,0:T(8,128)(2,1)S(1)}, bf16[64,2048]{1,0:T(8,128)(2,1)S(1)}, u32[]{:S(2)}, u32[]{:S(2)}) %collective-permute-start.6) | collective-permute-done | bytes 262176 | tf_op jit(solution)/shard_map/ppermute | solution.py:24
  51.1 1.8 %collective-permute-done.11 = bf16[352,2048]{1,0:T(8,128)(2,1)S(1)} collective-permute-done((bf16[352,2048]{1,0:T(8,128)(2,1)S(1)}, bf16[352,2048]{1,0:T(8,128)(2,1)S(1)}, u32[]{:S(2)}, u32[]{:S(2)}) %collective-permute-start.11) | collective-permute-done | bytes 1441824 | tf_op jit(solution)/shard_map/ppermute | solution.py:24
  53.1 3.4 %collective-permute-start.18 = (bf16[64,2048]{1,0:T(8,128)(2,1)S(1)}, bf16[64,2048]{1,0:T(8,128)(2,1)S(1)}, u32[]{:S(2)}, u32[]{:S(2)}) collective-permute-start(bf16[64,2048]{1,0:T(8,128)(2,1)S(1)} %multiply_convert_fusion), channel_id=1, source_target_pairs={{0,16},{8,24},{16,0},{24,8},{1,17},{9,25},{17,1},{25,9},{2,18},{10... | collective-permute-start | bytes 786440 | tf_op jit(solution)/shard_map/ppermute | solution.py:24
  57.1 9.9 %collective-permute-done.12 = bf16[64,2048]{1,0:T(8,128)(2,1)S(1)} collective-permute-done((bf16[64,2048]{1,0:T(8,128)(2,1)S(1)}, bf16[64,2048]{1,0:T(8,128)(2,1)S(1)}, u32[]{:S(2)}, u32[]{:S(2)}) %collective-permute-start.12) | collective-permute-done | bytes 262176 | tf_op jit(solution)/shard_map/ppermute | solution.py:24
  72.8 6.7 %collective-permute-done.18 = bf16[64,2048]{1,0:T(8,128)(2,1)S(1)} collective-permute-done((bf16[64,2048]{1,0:T(8,128)(2,1)S(1)}, bf16[64,2048]{1,0:T(8,128)(2,1)S(1)}, u32[]{:S(2)}, u32[]{:S(2)}) %collective-permute-start.18) | collective-permute-done | bytes 262176 | tf_op jit(solution)/shard_map/ppermute | solution.py:24
  80.4 1.5 collective-permute-start.27
  85.1 1.9 %collective-permute-start.36 = (bf16[64,2048]{1,0:T(8,128)(2,1)S(1)}, bf16[64,2048]{1,0:T(8,128)(2,1)S(1)}, u32[]{:S(2)}, u32[]{:S(2)}) collective-permute-start(bf16[64,2048]{1,0:T(8,128)(2,1)S(1)} %pad_maximum_fusion.4), channel_id=1, source_target_pairs={{0,6},{2,4},{4,2},{6,0},{1,7},{3,5},{5,3},{7,1},{8,14},{10,12},{12... | collective-permute-start | bytes 786440 | tf_op jit(solution)/shard_map/ppermute | solution.py:24
  89.5 3.6 %fusion.86 = f32[128,1408]{1,0:T(8,128)S(1)} fusion(bf16[2048,1408]{1,0:T(8,128)(2,1)} %collective-permute-done.8, bf16[32,2048]{1,0:T(8,128)(2,1)S(1)} %collective-permute-done.22, bf16[32,2048]{1,0:T(8,128)(2,1)S(1)} %collective-permute-done.21, bf16[32,2048]{1,0:T(8,128)(2,1)S(1)} %collective-permute-done.20, bf16[32,2048]{1,0:T(8,128)(2,1)S(1)} %get-tuple-element.56), kind=kOutput, calls=%fused_computation.148 | convolution fusion | flops 740294656 | bytes 7012352 | tf_op jit(solution)/shard_map/dot_general | solution.py:34
  100.3 3.6 %fusion.84 = f32[128,1408]{1,0:T(8,128)S(1)} fusion(bf16[2048,1408]{1,0:T(8,128)(2,1)} %collective-permute-done.8, bf16[32,2048]{1,0:T(8,128)(2,1)S(1)} %collective-permute-done.29, bf16[32,2048]{1,0:T(8,128)(2,1)S(1)} %collective-permute-done.28, bf16[32,2048]{1,0:T(8,128)(2,1)S(1)} %collective-permute-done.27, bf16[32,2048]{1,0:T(8,128)(2,1)S(1)} %get-tuple-element.64), kind=kOutput, calls=%fused_computation.146 | convolution fusion | flops 740294656 | bytes 7012352 | tf_op jit(solution)/shard_map/dot_general | solution.py:34
  109.0 5.6 %fusion.165 = f32[256,1408]{1,0:T(8,128)} fusion(bf16[256,2048]{1,0:T(8,128)(2,1)S(1)} %constant_dynamic-update-slice_fusion.2, bf16[2048,1408]{1,0:T(8,128)(2,1)} %collective-permute-done.8), kind=kOutput, calls=%fused_computation.244 | convolution fusion | flops 1476395008 | bytes 8257536 | tf_op jit(solution)/shard_map/dot_general | solution.py:34
  114.6 3.0 %fusion.130 = f32[256,1408]{1,0:T(8,128)} fusion(bf16[256,2048]{1,0:T(8,128)(2,1)S(1)} %constant_dynamic-update-slice_fusion.2, bf16[1,2048,1408]{2,1,0:T(8,128)(2,1)S(1)} %bitcast.160), kind=kOutput, calls=%fused_computation.212 | convolution fusion | flops 1476395008 | bytes 8257536 | tf_op jit(solution)/shard_map/dot_general | solution.py:34
  119.7 3.5 %fusion.81 = f32[128,2048]{1,0:T(8,128)S(1)} fusion(bf16[352,2048]{1,0:T(8,128)(2,1)} %param.30, f32[128,352]{0,1:T(8,128)S(1)} %fusion.163, bf16[128,2048]{1,0:T(8,128)(2,1)S(1)} %constant_dynamic-update-slice_fusion, bf16[2048,352]{0,1:T(8,128)(2,1)} %param.29), kind=kOutput, calls=%fused_computation.143 | convolution fusion | flops 369369088 | bytes 4636672 | tf_op jit(solution)/shard_map/dot_general | solution.py:34
  123.2 3.3 %convolution_add_fusion = f32[128,2048]{1,0:T(8,128)S(1)} fusion(f32[128,2048]{1,0:T(8,128)S(1)} %fusion.81, bf16[352,2048]{1,0:T(8,128)(2,1)} %copy-done.16, f32[128,352]{0,1:T(8,128)S(1)} %fusion.164, bf16[128,2048]{1,0:T(8,128)(2,1)S(1)} %constant_dynamic-update-slice_fusion, bf16[2048,352]{0,1:T(8,128)(2,1)} %copy-done.15), kind=kOutput, calls=%fused_computation.8 | convolution fusion | flops 369631232 | bytes 5685248 | tf_op jit(solution)/shard_map/dot_general | solution.py:34
  129.1 2.0 %convolution_convert_fusion.12 = bf16[64,2048]{1,0:T(8,128)(2,1)} fusion(bf16[128,64]{1,0:T(8,128)(2,1)S(1)} %bitcast.150, bf16[32,2048]{1,0:T(8,128)(2,1)} %collective-permute-done.25, bf16[32,2048]{1,0:T(8,128)(2,1)} %collective-permute-done.24, bf16[32,2048]{1,0:T(8,128)(2,1)} %collective-permute-done.23, bf16[32,2048]{1,0:T(8,128)(2,1)S(1)} %get-tuple-element.52), kind=kOutput, calls=%fused_computation.34 | convolution fusion | flops 35782656 | bytes 802816 | tf_op jit(solution)/shard_map/sn,sd->nd/dot_general | solution.py:333
  132.6 2.9 %fusion.3 = f32[256,2048]{1,0:T(8,128)S(1)} fusion(f32[256,1408]{1,0:T(8,128)S(1)} %copy-done.26, bf16[1,704,2048]{2,1,0:T(8,128)(2,1)} %param.33), kind=kOutput, calls=%fused_computation.7 | convolution fusion | flops 740327424 | bytes 6553600 | tf_op jit(solution)/shard_map/dot_general | solution.py:34
  137.3 2.0 %collective-permute-start.38 = (bf16[32,2048]{1,0:T(8,128)(2,1)S(1)}, bf16[32,2048]{1,0:T(8,128)(2,1)S(1)}, u32[]{:S(2)}, u32[]{:S(2)}) collective-permute-start(bf16[32,2048]{1,0:T(8,128)(2,1)S(1)} %get-tuple-element.49), channel_id=1, source_target_pairs={{0,4},{2,6},{4,0},{6,2},{1,5},{3,7},{5,1},{7,3},{8,12},{10,14},{12... | collective-permute-start | bytes 393224 | tf_op jit(solution)/shard_map/ppermute | solution.py:24
  140.3 1.9 %convolution_convert_fusion.11 = bf16[64,2048]{1,0:T(8,128)(2,1)} fusion(bf16[128,64]{1,0:T(8,128)(2,1)S(1)} %bitcast.149, bf16[32,2048]{1,0:T(8,128)(2,1)S(1)} %collective-permute-done.32, bf16[32,2048]{1,0:T(8,128)(2,1)} %collective-permute-done.31, bf16[32,2048]{1,0:T(8,128)(2,1)} %collective-permute-done.30, bf16[32,2048]{1,0:T(8,128)(2,1)S(1)} %get-tuple-element.60), kind=kOutput, calls=%fused_computation.33 | convolution fusion | flops 35782656 | bytes 802816 | tf_op jit(solution)/shard_map/sn,sd->nd/dot_general | solution.py:333
  144.0 1.6 %collective-permute-start.41 = (bf16[32,2048]{1,0:T(8,128)(2,1)S(1)}, bf16[32,2048]{1,0:T(8,128)(2,1)S(1)}, u32[]{:S(2)}, u32[]{:S(2)}) collective-permute-start(bf16[32,2048]{1,0:T(8,128)(2,1)S(1)} %get-tuple-element.47), channel_id=1, source_target_pairs={{0,2},{2,0},{4,6},{6,4},{1,3},{3,1},{5,7},{7,5},{8,10},{10,8},{12,... | collective-permute-start | bytes 393224 | tf_op jit(solution)/shard_map/ppermute | solution.py:24
  145.8 2.3 %collective-permute-start.42 = (bf16[32,2048]{1,0:T(8,128)(2,1)S(1)}, bf16[32,2048]{1,0:T(8,128)(2,1)}, u32[]{:S(2)}, u32[]{:S(2)}) collective-permute-start(bf16[32,2048]{1,0:T(8,128)(2,1)S(1)} %get-tuple-element.46), channel_id=1, source_target_pairs={{0,4},{2,6},{4,0},{6,2},{1,5},{3,7},{5,1},{7,3},{8,12},{10,14},{12... | collective-permute-start | bytes 393224 | tf_op jit(solution)/shard_map/ppermute | solution.py:24
  149.0 1.9 %collective-permute-start.40 = (bf16[64,2048]{1,0:T(8,128)(2,1)}, bf16[64,2048]{1,0:T(8,128)(2,1)}, u32[]{:S(2)}, u32[]{:S(2)}) collective-permute-start(bf16[64,2048]{1,0:T(8,128)(2,1)} %convolution_convert_fusion.10), channel_id=1, source_target_pairs={{0,8},{8,0},{16,24},{24,16},{1,9},{9,1},{17,25},{25,17},{2,10},{10... | collective-permute-start | bytes 786440 | tf_op jit(solution)/shard_map/ppermute | solution.py:24
  151.5 2.5 %collective-permute-start.43 = (bf16[32,2048]{1,0:T(8,128)(2,1)S(1)}, bf16[32,2048]{1,0:T(8,128)(2,1)}, u32[]{:S(2)}, u32[]{:S(2)}) collective-permute-start(bf16[32,2048]{1,0:T(8,128)(2,1)S(1)} %get-tuple-element.45), channel_id=1, source_target_pairs={{0,6},{2,4},{4,2},{6,0},{1,7},{3,5},{5,3},{7,1},{8,14},{10,12},{12... | collective-permute-start | bytes 393224 | tf_op jit(solution)/shard_map/ppermute | solution.py:24
  155.4 2.2 %collective-permute-done.43 = bf16[32,2048]{1,0:T(8,128)(2,1)} collective-permute-done((bf16[32,2048]{1,0:T(8,128)(2,1)S(1)}, bf16[32,2048]{1,0:T(8,128)(2,1)}, u32[]{:S(2)}, u32[]{:S(2)}) %collective-permute-start.43) | collective-permute-done | bytes 131104 | tf_op jit(solution)/shard_map/ppermute | solution.py:24
  157.6 2.1 %fusion.68 = bf16[1,64,2048]{2,1,0:T(8,128)(2,1)} fusion(bf16[64,2048]{1,0:T(8,128)(2,1)} %collective-permute-done.40, bf16[64,2048]{1,0:T(8,128)(2,1)S(1)} %collective-permute-done.33, bf16[64,2048]{1,0:T(8,128)(2,1)S(1)} %collective-permute-done.26, f32[64,2048]{1,0:T(8,128)S(1)} %copy-done.11, bf16[64,2048]{1,0:T(8,128)(2,1)S(1)} %collective-permute-done.14, ...), kind=kOutput, calls=%fused_computation.108 | convolution fusion | flops 37224448 | bytes 2900032 | tf_op jit(solution)/shard_map/sn,sd->nd/dot_general | solution.py:333
  (201 shorter events, 54.1 us)
Async XLA Ops:
  0.6 9.5 %collective-permute-start.1 = (bf16[64,2048]{1,0:T(8,128)(2,1)}, bf16[64,2048]{1,0:T(8,128)(2,1)S(1)}, u32[]{:S(2)}, u32[]{:S(2)}) collective-permute-start(bf16[64,2048]{1,0:T(8,128)(2,1)} %bitcast.137), channel_id=1, source_target_pairs={{0,2},{2,0},{1,3},{3,1},{4,6},{6,4},{5,7},{7,5},{8,10},{10,8},{9,1... | collective-permute-start | bytes 786440 | tf_op jit(solution)/shard_map/ppermute | solution.py:24
  3.6 15.7 %collective-permute-start = (bf16[64,2048]{1,0:T(8,128)(2,1)}, bf16[64,2048]{1,0:T(8,128)(2,1)S(1)}, u32[]{:S(2)}, u32[]{:S(2)}) collective-permute-start(bf16[64,2048]{1,0:T(8,128)(2,1)} %bitcast.138), channel_id=1, source_target_pairs={{0,1},{1,0},{2,3},{3,2},{4,5},{5,4},{6,7},{7,6},{8,9},{9,8},{10,11... | collective-permute-start | bytes 786440 | tf_op jit(solution)/shard_map/ppermute | solution.py:24
  12.8 40.1 %collective-permute-start.8 = (bf16[2048,1408]{1,0:T(8,128)(2,1)}, bf16[2048,1408]{1,0:T(8,128)(2,1)}, u32[]{:S(2)}, u32[]{:S(2)}) collective-permute-start(bf16[2048,1408]{1,0:T(8,128)(2,1)} %bitcast.158), channel_id=1, source_target_pairs={{0,1},{1,0},{2,3},{3,2},{4,5},{5,4},{6,7},{7,6},{8,9},{9,8},{10,11... | collective-permute-start | bytes 17301512 | tf_op jit(solution)/shard_map/ppermute | solution.py:24
  19.3 20.0 %collective-permute-start.4 = (bf16[512,2048]{1,0:T(8,128)(2,1)}, bf16[512,2048]{1,0:T(8,128)(2,1)S(1)}, u32[]{:S(2)}, u32[]{:S(2)}) collective-permute-start(bf16[512,2048]{1,0:T(8,128)(2,1)} %param.26), channel_id=1, source_target_pairs={{0,1},{1,0},{2,3},{3,2},{4,5},{5,4},{6,7},{7,6},{8,9},{9,8},{10,11... | collective-permute-start | bytes 6291464 | tf_op jit(solution)/shard_map/ppermute | solution.py:24
  25.1 27.8 %collective-permute-start.9 = (bf16[704,2048]{1,0:T(8,128)(2,1)}, bf16[704,2048]{1,0:T(8,128)(2,1)S(1)}, u32[]{:S(2)}, u32[]{:S(2)}) collective-permute-start(bf16[704,2048]{1,0:T(8,128)(2,1)} %bitcast.161), channel_id=1, source_target_pairs={{0,1},{1,0},{2,3},{3,2},{4,5},{5,4},{6,7},{7,6},{8,9},{9,8},{10,11... | collective-permute-start | bytes 8650760 | tf_op jit(solution)/shard_map/ppermute | solution.py:24
  41.4 8.3 %collective-permute-start.6 = (bf16[64,2048]{1,0:T(8,128)(2,1)S(1)}, bf16[64,2048]{1,0:T(8,128)(2,1)S(1)}, u32[]{:S(2)}, u32[]{:S(2)}) collective-permute-start(bf16[64,2048]{1,0:T(8,128)(2,1)S(1)} %fusion.16), channel_id=1, source_target_pairs={{0,2},{2,0},{1,3},{3,1},{4,6},{6,4},{5,7},{7,5},{8,10},{10,8},{9,1... | collective-permute-start | bytes 786440 | tf_op jit(solution)/shard_map/ppermute | solution.py:24
  43.0 8.1 %collective-permute-start.7 = (bf16[2048,352]{0,1:T(8,128)(2,1)S(1)}, bf16[2048,352]{0,1:T(8,128)(2,1)S(1)}, u32[]{:S(2)}, u32[]{:S(2)}) collective-permute-start(bf16[2048,352]{0,1:T(8,128)(2,1)S(1)} %copy-done.12), channel_id=1, source_target_pairs={{0,1},{1,0},{2,3},{3,2},{4,5},{5,4},{6,7},{7,6},{8,9},{9,8},{10,11... | collective-permute-start | bytes 4325384 | tf_op jit(solution)/shard_map/ppermute | solution.py:24
  44.2 6.9 %collective-permute-start.10 = (bf16[2048,352]{0,1:T(8,128)(2,1)S(1)}, bf16[2048,352]{0,1:T(8,128)(2,1)S(1)}, u32[]{:S(2)}, u32[]{:S(2)}) collective-permute-start(bf16[2048,352]{0,1:T(8,128)(2,1)S(1)} %copy-done.14), channel_id=1, source_target_pairs={{0,1},{1,0},{2,3},{3,2},{4,5},{5,4},{6,7},{7,6},{8,9},{9,8},{10,11... | collective-permute-start | bytes 4325384 | tf_op jit(solution)/shard_map/ppermute | solution.py:24
  53.0 14.0 %collective-permute-start.12 = (bf16[64,2048]{1,0:T(8,128)(2,1)S(1)}, bf16[64,2048]{1,0:T(8,128)(2,1)S(1)}, u32[]{:S(2)}, u32[]{:S(2)}) collective-permute-start(bf16[64,2048]{1,0:T(8,128)(2,1)S(1)} %multiply_convert_fusion), channel_id=1, source_target_pairs={{0,8},{8,0},{16,24},{24,16},{1,9},{9,1},{17,25},{25,17},{2,10},{10... | collective-permute-start | bytes 786440 | tf_op jit(solution)/shard_map/ppermute | solution.py:24
  53.0 15.4 %collective-permute-start.19 = (bf16[64,2048]{1,0:T(8,128)(2,1)S(1)}, bf16[64,2048]{1,0:T(8,128)(2,1)S(1)}, u32[]{:S(2)}, u32[]{:S(2)}) collective-permute-start(bf16[64,2048]{1,0:T(8,128)(2,1)S(1)} %multiply_convert_fusion), channel_id=1, source_target_pairs={{0,24},{8,16},{16,8},{24,0},{1,25},{9,17},{17,9},{25,1},{2,26},{10... | collective-permute-start | bytes 786440 | tf_op jit(solution)/shard_map/ppermute | solution.py:24
  53.1 26.3 %collective-permute-start.18 = (bf16[64,2048]{1,0:T(8,128)(2,1)S(1)}, bf16[64,2048]{1,0:T(8,128)(2,1)S(1)}, u32[]{:S(2)}, u32[]{:S(2)}) collective-permute-start(bf16[64,2048]{1,0:T(8,128)(2,1)S(1)} %multiply_convert_fusion), channel_id=1, source_target_pairs={{0,16},{8,24},{16,0},{24,8},{1,17},{9,25},{17,1},{25,9},{2,18},{10... | collective-permute-start | bytes 786440 | tf_op jit(solution)/shard_map/ppermute | solution.py:24
  67.0 50.6 %collective-permute-start.13 = (bf16[64,2048]{1,0:T(8,128)(2,1)S(1)}, bf16[64,2048]{1,0:T(8,128)(2,1)S(1)}, u32[]{:S(2)}, u32[]{:S(2)}) collective-permute-start(bf16[64,2048]{1,0:T(8,128)(2,1)S(1)} %multiply_convert_fusion), channel_id=1, source_target_pairs={{0,2},{2,0},{1,3},{3,1},{4,6},{6,4},{5,7},{7,5},{8,10},{10,8},{9,1... | collective-permute-start | bytes 786440 | tf_op jit(solution)/shard_map/ppermute | solution.py:24
  68.8 14.2 %collective-permute-start.20 = (bf16[32,2048]{1,0:T(8,128)(2,1)S(1)}, bf16[32,2048]{1,0:T(8,128)(2,1)S(1)}, u32[]{:S(2)}, u32[]{:S(2)}) collective-permute-start(bf16[32,2048]{1,0:T(8,128)(2,1)S(1)} %get-tuple-element.59), channel_id=1, source_target_pairs={{0,2},{2,0},{4,6},{6,4},{1,3},{3,1},{5,7},{7,5},{8,10},{10,8},{12,... | collective-permute-start | bytes 393224 | tf_op jit(solution)/shard_map/ppermute | solution.py:24
  69.5 14.6 %collective-permute-start.21 = (bf16[32,2048]{1,0:T(8,128)(2,1)S(1)}, bf16[32,2048]{1,0:T(8,128)(2,1)S(1)}, u32[]{:S(2)}, u32[]{:S(2)}) collective-permute-start(bf16[32,2048]{1,0:T(8,128)(2,1)S(1)} %get-tuple-element.58), channel_id=1, source_target_pairs={{0,4},{2,6},{4,0},{6,2},{1,5},{3,7},{5,1},{7,3},{8,12},{10,14},{12... | collective-permute-start | bytes 393224 | tf_op jit(solution)/shard_map/ppermute | solution.py:24
  70.9 14.1 %collective-permute-start.22 = (bf16[32,2048]{1,0:T(8,128)(2,1)S(1)}, bf16[32,2048]{1,0:T(8,128)(2,1)S(1)}, u32[]{:S(2)}, u32[]{:S(2)}) collective-permute-start(bf16[32,2048]{1,0:T(8,128)(2,1)S(1)} %get-tuple-element.57), channel_id=1, source_target_pairs={{0,6},{2,4},{4,2},{6,0},{1,7},{3,5},{5,3},{7,1},{8,14},{10,12},{12... | collective-permute-start | bytes 393224 | tf_op jit(solution)/shard_map/ppermute | solution.py:24
  80.4 14.1 %collective-permute-start.27 = (bf16[32,2048]{1,0:T(8,128)(2,1)S(1)}, bf16[32,2048]{1,0:T(8,128)(2,1)S(1)}, u32[]{:S(2)}, u32[]{:S(2)}) collective-permute-start(bf16[32,2048]{1,0:T(8,128)(2,1)S(1)} %get-tuple-element.67), channel_id=1, source_target_pairs={{0,2},{2,0},{4,6},{6,4},{1,3},{3,1},{5,7},{7,5},{8,10},{10,8},{12,... | collective-permute-start | bytes 393224 | tf_op jit(solution)/shard_map/ppermute | solution.py:24
  83.0 13.6 %collective-permute-start.28 = (bf16[32,2048]{1,0:T(8,128)(2,1)S(1)}, bf16[32,2048]{1,0:T(8,128)(2,1)S(1)}, u32[]{:S(2)}, u32[]{:S(2)}) collective-permute-start(bf16[32,2048]{1,0:T(8,128)(2,1)S(1)} %get-tuple-element.66), channel_id=1, source_target_pairs={{0,4},{2,6},{4,0},{6,2},{1,5},{3,7},{5,1},{7,3},{8,12},{10,14},{12... | collective-permute-start | bytes 393224 | tf_op jit(solution)/shard_map/ppermute | solution.py:24
  84.1 13.2 %collective-permute-start.29 = (bf16[32,2048]{1,0:T(8,128)(2,1)S(1)}, bf16[32,2048]{1,0:T(8,128)(2,1)S(1)}, u32[]{:S(2)}, u32[]{:S(2)}) collective-permute-start(bf16[32,2048]{1,0:T(8,128)(2,1)S(1)} %get-tuple-element.65), channel_id=1, source_target_pairs={{0,6},{2,4},{4,2},{6,0},{1,7},{3,5},{5,3},{7,1},{8,14},{10,12},{12... | collective-permute-start | bytes 393224 | tf_op jit(solution)/shard_map/ppermute | solution.py:24
  85.1 22.5 %collective-permute-start.36 = (bf16[64,2048]{1,0:T(8,128)(2,1)S(1)}, bf16[64,2048]{1,0:T(8,128)(2,1)S(1)}, u32[]{:S(2)}, u32[]{:S(2)}) collective-permute-start(bf16[64,2048]{1,0:T(8,128)(2,1)S(1)} %pad_maximum_fusion.4), channel_id=1, source_target_pairs={{0,6},{2,4},{4,2},{6,0},{1,7},{3,5},{5,3},{7,1},{8,14},{10,12},{12... | collective-permute-start | bytes 786440 | tf_op jit(solution)/shard_map/ppermute | solution.py:24
  94.5 11.8 %collective-permute-start.35 = (bf16[64,2048]{1,0:T(8,128)(2,1)S(1)}, bf16[64,2048]{1,0:T(8,128)(2,1)S(1)}, u32[]{:S(2)}, u32[]{:S(2)}) collective-permute-start(bf16[64,2048]{1,0:T(8,128)(2,1)S(1)} %pad_maximum_fusion.3), channel_id=1, source_target_pairs={{0,4},{2,6},{4,0},{6,2},{1,5},{3,7},{5,1},{7,3},{8,12},{10,14},{12... | collective-permute-start | bytes 786440 | tf_op jit(solution)/shard_map/ppermute | solution.py:24
  96.6 8.7 %collective-permute-start.34 = (bf16[64,2048]{1,0:T(8,128)(2,1)S(1)}, bf16[64,2048]{1,0:T(8,128)(2,1)S(1)}, u32[]{:S(2)}, u32[]{:S(2)}) collective-permute-start(bf16[64,2048]{1,0:T(8,128)(2,1)S(1)} %pad_maximum_fusion.2), channel_id=1, source_target_pairs={{0,2},{2,0},{4,6},{6,4},{1,3},{3,1},{5,7},{7,5},{8,10},{10,8},{12,... | collective-permute-start | bytes 786440 | tf_op jit(solution)/shard_map/ppermute | solution.py:24
  97.3 29.3 %collective-permute-start.23 = (bf16[32,2048]{1,0:T(8,128)(2,1)}, bf16[32,2048]{1,0:T(8,128)(2,1)}, u32[]{:S(2)}, u32[]{:S(2)}) collective-permute-start(bf16[32,2048]{1,0:T(8,128)(2,1)} %get-tuple-element.55), channel_id=1, source_target_pairs={{0,2},{2,0},{4,6},{6,4},{1,3},{3,1},{5,7},{7,5},{8,10},{10,8},{12,... | collective-permute-start | bytes 393224 | tf_op jit(solution)/shard_map/ppermute | solution.py:24
  105.3 22.4 %collective-permute-start.24 = (bf16[32,2048]{1,0:T(8,128)(2,1)}, bf16[32,2048]{1,0:T(8,128)(2,1)}, u32[]{:S(2)}, u32[]{:S(2)}) collective-permute-start(bf16[32,2048]{1,0:T(8,128)(2,1)} %get-tuple-element.54), channel_id=1, source_target_pairs={{0,4},{2,6},{4,0},{6,2},{1,5},{3,7},{5,1},{7,3},{8,12},{10,14},{12... | collective-permute-start | bytes 393224 | tf_op jit(solution)/shard_map/ppermute | solution.py:24
  106.4 22.8 %collective-permute-start.25 = (bf16[32,2048]{1,0:T(8,128)(2,1)S(1)}, bf16[32,2048]{1,0:T(8,128)(2,1)}, u32[]{:S(2)}, u32[]{:S(2)}) collective-permute-start(bf16[32,2048]{1,0:T(8,128)(2,1)S(1)} %get-tuple-element.53), channel_id=1, source_target_pairs={{0,6},{2,4},{4,2},{6,0},{1,7},{3,5},{5,3},{7,1},{8,14},{10,12},{12... | collective-permute-start | bytes 393224 | tf_op jit(solution)/shard_map/ppermute | solution.py:24
  107.6 29.1 %collective-permute-start.30 = (bf16[32,2048]{1,0:T(8,128)(2,1)}, bf16[32,2048]{1,0:T(8,128)(2,1)}, u32[]{:S(2)}, u32[]{:S(2)}) collective-permute-start(bf16[32,2048]{1,0:T(8,128)(2,1)} %get-tuple-element.63), channel_id=1, source_target_pairs={{0,2},{2,0},{4,6},{6,4},{1,3},{3,1},{5,7},{7,5},{8,10},{10,8},{12,... | collective-permute-start | bytes 393224 | tf_op jit(solution)/shard_map/ppermute | solution.py:24
  117.6 19.7 %collective-permute-start.31 = (bf16[32,2048]{1,0:T(8,128)(2,1)}, bf16[32,2048]{1,0:T(8,128)(2,1)}, u32[]{:S(2)}, u32[]{:S(2)}) collective-permute-start(bf16[32,2048]{1,0:T(8,128)(2,1)} %get-tuple-element.62), channel_id=1, source_target_pairs={{0,4},{2,6},{4,0},{6,2},{1,5},{3,7},{5,1},{7,3},{8,12},{10,14},{12... | collective-permute-start | bytes 393224 | tf_op jit(solution)/shard_map/ppermute | solution.py:24
  126.6 12.7 %collective-permute-start.32 = (bf16[32,2048]{1,0:T(8,128)(2,1)S(1)}, bf16[32,2048]{1,0:T(8,128)(2,1)S(1)}, u32[]{:S(2)}, u32[]{:S(2)}) collective-permute-start(bf16[32,2048]{1,0:T(8,128)(2,1)S(1)} %get-tuple-element.61), channel_id=1, source_target_pairs={{0,6},{2,4},{4,2},{6,0},{1,7},{3,5},{5,3},{7,1},{8,14},{10,12},{12... | collective-permute-start | bytes 393224 | tf_op jit(solution)/shard_map/ppermute | solution.py:24
  127.7 29.8 %collective-permute-start.14 = (bf16[64,2048]{1,0:T(8,128)(2,1)S(1)}, bf16[64,2048]{1,0:T(8,128)(2,1)S(1)}, u32[]{:S(2)}, u32[]{:S(2)}) collective-permute-start(bf16[64,2048]{1,0:T(8,128)(2,1)S(1)} %slice.403), channel_id=1, source_target_pairs={{0,2},{2,0},{1,3},{3,1},{4,6},{6,4},{5,7},{7,5},{8,10},{10,8},{9,1... | collective-permute-start | bytes 786440 | tf_op jit(solution)/shard_map/ppermute | solution.py:24
  131.1 26.5 %collective-permute-start.26 = (bf16[64,2048]{1,0:T(8,128)(2,1)}, bf16[64,2048]{1,0:T(8,128)(2,1)S(1)}, u32[]{:S(2)}, u32[]{:S(2)}) collective-permute-start(bf16[64,2048]{1,0:T(8,128)(2,1)} %convolution_convert_fusion.12), channel_id=1, source_target_pairs={{0,24},{8,16},{16,8},{24,0},{1,25},{9,17},{17,9},{25,1},{2,26},{10... | collective-permute-start | bytes 786440 | tf_op jit(solution)/shard_map/ppermute | solution.py:24
  137.3 6.7 %collective-permute-start.38 = (bf16[32,2048]{1,0:T(8,128)(2,1)S(1)}, bf16[32,2048]{1,0:T(8,128)(2,1)S(1)}, u32[]{:S(2)}, u32[]{:S(2)}) collective-permute-start(bf16[32,2048]{1,0:T(8,128)(2,1)S(1)} %get-tuple-element.49), channel_id=1, source_target_pairs={{0,4},{2,6},{4,0},{6,2},{1,5},{3,7},{5,1},{7,3},{8,12},{10,14},{12... | collective-permute-start | bytes 393224 | tf_op jit(solution)/shard_map/ppermute | solution.py:24
  142.3 15.2 %collective-permute-start.33 = (bf16[64,2048]{1,0:T(8,128)(2,1)}, bf16[64,2048]{1,0:T(8,128)(2,1)S(1)}, u32[]{:S(2)}, u32[]{:S(2)}) collective-permute-start(bf16[64,2048]{1,0:T(8,128)(2,1)} %convolution_convert_fusion.11), channel_id=1, source_target_pairs={{0,16},{8,24},{16,0},{24,8},{1,17},{9,25},{17,1},{25,9},{2,18},{10... | collective-permute-start | bytes 786440 | tf_op jit(solution)/shard_map/ppermute | solution.py:24
  149.0 8.6 %collective-permute-start.40 = (bf16[64,2048]{1,0:T(8,128)(2,1)}, bf16[64,2048]{1,0:T(8,128)(2,1)}, u32[]{:S(2)}, u32[]{:S(2)}) collective-permute-start(bf16[64,2048]{1,0:T(8,128)(2,1)} %convolution_convert_fusion.10), channel_id=1, source_target_pairs={{0,8},{8,0},{16,24},{24,16},{1,9},{9,1},{17,25},{25,17},{2,10},{10... | collective-permute-start | bytes 786440 | tf_op jit(solution)/shard_map/ppermute | solution.py:24
  (41 other events, 409.2 us)

commit v3 on v2

v3 whole, which is shorter than its diff:
```python
import functools
import math

import jax
import jax.numpy as jnp
from jax import lax
from jax.experimental import pallas as pl
from jax.experimental.pallas import tpu as pltpu
from jax.sharding import Mesh
from jax.sharding import PartitionSpec as P

EPSILON = 1e-06
ROPE_BASE = 10000.0
GROUPS = ((0, 1), (3,), (2,))
CHUNK = 512
ALL = ("z", "y", "x", "c")
PLANE = ("y", "x")
HEAD = ("x", "c")


def partner(value, axes, offset):
    if offset == 0:
        return value
    size = lax.axis_size(axes)
    return lax.ppermute(value, axes, [(i, i ^ offset) for i in range(size)])


def rms_norm(values, gain):
    wide = values.astype(jnp.float32)
    power = jnp.mean(wide * wide, axis=-1, keepdims=True)
    return (wide * lax.rsqrt(power + EPSILON) * gain).astype(jnp.bfloat16)


def dot(left, right):
    return jnp.dot(left, right, preferred_element_type=jnp.float32)


def ancestry(parents):
    nodes_count = parents.shape[-1]
    nodes = jnp.arange(nodes_count, dtype=jnp.int32)
    reach = (parents[..., :, None] == nodes).astype(jnp.float32) + jnp.eye(
        nodes_count, dtype=jnp.float32
    )
    for turn in range((nodes_count - 1).bit_length()):
        near = reach.astype(jnp.bfloat16)
        reach = jnp.minimum(
            jnp.einsum("rij,rjk->rik", near, near, preferred_element_type=jnp.float32), 1.0
        )
    depth = jnp.sum(reach, axis=-1) - 1.0
    return (reach, depth)


def arrive(copies):
    for copy in copies:
        copy.wait()


def attend_kernel(
    info, first, second, gain, weight, cosine, sine, reach, cache, *outs_and_scratch
):
    mixed = outs_and_scratch[0:2]
    fresh = outs_and_scratch[2:4]
    weight_here, cache_here, gain_here, sems = outs_and_scratch[4:]
    tree = first.shape[0]
    width, columns = weight.shape
    head_dim = cosine.shape[2]
    group = columns // head_dim - 2
    deep = width // 2

    gain_copy = pltpu.make_async_copy(gain, gain_here, sems.at[0])
    weight_copies = [
        pltpu.make_async_copy(
            weight.at[pl.ds(i * deep, deep)], weight_here.at[pl.ds(i * deep, deep)], sems.at[1 + i]
        )
        for i in range(2)
    ]
    cache_copies = [
        pltpu.make_async_copy(cache.at[info[i]], cache_here.at[i], sems.at[3 + i])
        for i in range(2)
    ]
    for copy in [gain_copy, *weight_copies, *cache_copies]:
        copy.start()

    wide = jnp.concatenate([first[...], second[...]], axis=0).astype(jnp.float32)
    power = jnp.mean(wide * wide, axis=-1, keepdims=True)
    gain_copy.wait()
    normed = (wide * lax.rsqrt(power + EPSILON) * gain_here[...]).astype(jnp.bfloat16)
    weight_copies[0].wait()
    projected = dot(normed[:, :deep], weight_here[:deep])
    weight_copies[1].wait()
    projected = projected + dot(normed[:, deep:], weight_here[deep:])
    scale = 1.0 / math.sqrt(head_dim)

    for i in range(2):
        own = projected[i * tree : (i + 1) * tree]
        request = info[i]
        length = info[2 + i]

        def rope(values):
            return values * cosine[request] + pltpu.roll(values, head_dim // 2, 1) * sine[request]

        def column(c):
            return own[:, c * head_dim : (c + 1) * head_dim]

        query = jnp.concatenate(
            [rope(column(h)).astype(jnp.bfloat16) for h in range(group)], axis=0
        )
        key_new = rope(column(group)).astype(jnp.bfloat16)
        value_new = column(group + 1).astype(jnp.bfloat16)
        fresh[i][:, :head_dim] = key_new
        fresh[i][:, head_dim:] = value_new

        def against(keys):
            return (
                lax.dot_general(
                    query, keys, (((1,), (1,)), ((), ())), preferred_element_type=jnp.float32
                )
                * scale
            )

        allowed = jnp.concatenate([reach[request]] * group, axis=0) > 0.5
        scores = jnp.where(allowed, against(key_new), -1e30)
        peak = jnp.max(scores, axis=-1, keepdims=True)
        weights = jnp.exp(scores - peak)
        total = jnp.sum(weights, axis=-1, keepdims=True)
        summed = dot(weights.astype(jnp.bfloat16), value_new)
        cache_copies[i].wait()

        def chunk(j, carry):
            peak, total, summed = carry
            block = pl.ds(pl.multiple_of(j * CHUNK, CHUNK), CHUNK)
            scores = against(cache_here[i, block, :head_dim])
            place = j * CHUNK + lax.broadcasted_iota(jnp.int32, scores.shape, 1)
            scores = jnp.where(place < length, scores, -1e30)
            higher = jnp.maximum(peak, jnp.max(scores, axis=-1, keepdims=True))
            fade = jnp.exp(peak - higher)
            weights = jnp.exp(scores - higher)
            total = total * fade + jnp.sum(weights, axis=-1, keepdims=True)
            values = cache_here[i, block, head_dim:]
            summed = summed * fade + dot(weights.astype(jnp.bfloat16), values)
            return (higher, total, summed)

        peak, total, summed = lax.fori_loop(
            0, lax.div(length + CHUNK - 1, CHUNK), chunk, (peak, total, summed)
        )
        result = (summed / total).astype(jnp.bfloat16)
        for h in range(group):
            mixed[i][:, h * head_dim : (h + 1) * head_dim] = result[h * tree : (h + 1) * tree]


def in_vmem():
    return pl.BlockSpec(memory_space=pltpu.VMEM)


def in_hbm():
    return pl.BlockSpec(memory_space=pltpu.HBM)


def attend(info, first, second, gain, weight, cosine, sine, reach, cache):
    tree, width = first.shape
    slots, pair = cache.shape[1:]
    head_dim = pair // 2
    columns = weight.shape[1]
    group_columns = columns - pair
    return pl.pallas_call(
        attend_kernel,
        in_specs=[
            pl.BlockSpec(memory_space=pltpu.SMEM),
            in_vmem(),
            in_vmem(),
            in_hbm(),
            in_hbm(),
            in_vmem(),
            in_vmem(),
            in_vmem(),
            in_hbm(),
        ],
        out_specs=[in_vmem()] * 4,
        out_shape=[jax.ShapeDtypeStruct((tree, group_columns), jnp.bfloat16)] * 2
        + [jax.ShapeDtypeStruct((tree, pair), jnp.bfloat16)] * 2,
        scratch_shapes=[
            pltpu.VMEM((width, columns), jnp.bfloat16),
            pltpu.VMEM((2, slots, pair), jnp.bfloat16),
            pltpu.VMEM((1, width), jnp.float32),
            pltpu.SemaphoreType.DMA((5,)),
        ],
        compiler_params=pltpu.CompilerParams(vmem_limit_bytes=24 * 2**20),
        name="attend",
    )(info, first, second, gain, weight, cosine, sine, reach, cache)


def silu(values):
    return values / (1.0 + jnp.exp(-values))


def expert_kernel(*refs, plane, deep):
    pieces = refs[:plane]
    weights = refs[plane : plane + 4]
    outs = refs[plane + 4 : 2 * plane + 4]
    rows, inner_a, outer_a, inner_b, outer_b, sems = refs[2 * plane + 4 :]
    each = pieces[0].shape[0]
    width = rows.shape[1]
    parts = width // deep
    copies = []
    for n, (inner, outer, inner_here, outer_here) in enumerate(
        ((weights[0], weights[1], inner_a, outer_a), (weights[2], weights[3], inner_b, outer_b))
    ):
        base = n * (parts + 1)
        for p in range(parts):
            block = pl.ds(p * deep, deep)
            copies.append(
                pltpu.make_async_copy(inner.at[block], inner_here.at[block], sems.at[base + p])
            )
        copies.append(pltpu.make_async_copy(outer, outer_here, sems.at[base + parts]))
    for copy in copies:
        copy.start()
    for i in range(plane):
        rows[i * each : (i + 1) * each] = pieces[i][...]
    result = None
    for n, (inner_here, outer_here) in enumerate(((inner_a, outer_a), (inner_b, outer_b))):
        base = n * (parts + 1)
        both = None
        for p in range(parts):
            copies[base + p].wait()
            term = dot(rows[:, p * deep : (p + 1) * deep], inner_here[p * deep : (p + 1) * deep])
            both = term if both is None else both + term
        half = both.shape[1] // 2
        hidden = (silu(both[:, :half]) * both[:, half:]).astype(jnp.bfloat16)
        copies[base + parts].wait()
        term = dot(hidden, outer_here[...]).astype(jnp.bfloat16).astype(jnp.float32)
        result = term if result is None else result + term
    for i in range(plane):
        outs[i][...] = result[i * each : (i + 1) * each].astype(jnp.bfloat16)


def experts(pieces, inner, outer):
    plane = len(pieces)
    each, width = pieces[0].shape
    hidden = inner[0].shape[1]
    deep = width // 2
    kernel = functools.partial(expert_kernel, plane=plane, deep=deep)
    weight_scratch = [
        pltpu.VMEM((width, hidden), jnp.bfloat16),
        pltpu.VMEM((hidden // 2, width), jnp.bfloat16),
    ]
    return pl.pallas_call(
        kernel,
        in_specs=[in_vmem()] * plane + [in_hbm()] * 4,
        out_specs=[in_vmem()] * plane,
        out_shape=[jax.ShapeDtypeStruct((each, width), jnp.bfloat16)] * plane,
        scratch_shapes=[pltpu.VMEM((plane * each, width), jnp.bfloat16)]
        + weight_scratch * 2
        + [pltpu.SemaphoreType.DMA((2 * (width // deep + 1),))],
        compiler_params=pltpu.CompilerParams(vmem_limit_bytes=40 * 2**20),
        name="expert",
    )(*pieces, inner[0], outer[0], inner[1], outer[1])


def shared_kernel(*refs, side):
    blocks = refs[:side]
    weights = refs[side : side + 6]
    outs = refs[side + 6 : 2 * side + 6]
    here, sems = refs[2 * side + 6 :]
    copies = [pltpu.make_async_copy(weights[i], here.at[i], sems.at[i]) for i in range(6)]
    for copy in copies:
        copy.start()
    tree = blocks[0].shape[0]
    rows = jnp.concatenate([block[...] for block in blocks], axis=0)

    def turned(i):
        copies[i].wait()
        return lax.dot_general(
            rows, here[i], (((1,), (1,)), ((), ())), preferred_element_type=jnp.float32
        )

    result = None
    for n in range(2):
        hidden = silu(turned(3 * n))
        hidden = (hidden * turned(3 * n + 1)).astype(jnp.bfloat16)
        copies[3 * n + 2].wait()
        term = dot(hidden, here[3 * n + 2])
        result = term if result is None else result + term
    for i in range(side):
        outs[i][...] = result[i * tree : (i + 1) * tree].astype(outs[i].dtype)


def shared_terms(own, beside, weights):
    tree, width = own.shape
    units = weights[0].shape[0]
    side = 1 + len(beside)
    outs = pl.pallas_call(
        functools.partial(shared_kernel, side=side),
        in_specs=[in_vmem()] * side + [in_hbm()] * 6,
        out_specs=[in_vmem()] * side,
        out_shape=[jax.ShapeDtypeStruct((tree, width), jnp.float32)]
        + [jax.ShapeDtypeStruct((tree, width), jnp.bfloat16)] * (side - 1),
        scratch_shapes=[
            pltpu.VMEM((6, units, width), jnp.bfloat16),
            pltpu.SemaphoreType.DMA((6,)),
        ],
        compiler_params=pltpu.CompilerParams(vmem_limit_bytes=24 * 2**20),
        name="shared",
    )(own, *beside, *weights)
    return outs[0], list(outs[1:])


def combine_kernel(spread, *refs, start):
    out = refs[-1]
    slots = spread.shape[0] // (len(refs) - 1)
    total = None
    for i, piece in enumerate(refs[:-1]):
        term = lax.dot_general(
            spread[i * slots : (i + 1) * slots],
            piece[start : start + slots],
            (((0,), (0,)), ((), ())),
            preferred_element_type=jnp.float32,
        )
        total = term if total is None else total + term
    out[...] = total.astype(out.dtype)


def combine(spread, pieces, start, dtype):
    tree = spread.shape[1]
    width = pieces[0].shape[1]
    return pl.pallas_call(
        functools.partial(combine_kernel, start=start),
        in_specs=[in_vmem()] * (1 + len(pieces)),
        out_specs=in_vmem(),
        out_shape=jax.ShapeDtypeStruct((tree, width), dtype),
        compiler_params=pltpu.CompilerParams(vmem_limit_bytes=16 * 2**20),
        name="combine",
    )(spread, *pieces)


def body(
    tokens,
    live,
    parents,
    lengths,
    accepted,
    routes,
    cache,
    attn_gain,
    w_qkv,
    w_out,
    ffn_gain,
    shared_gate,
    shared_up,
    shared_down,
    router,
    expert_in,
    expert_out,
):
    tree = tokens.shape[1]
    width = tokens.shape[2]
    own_rows = tokens[0]
    group_count = lax.axis_size(HEAD)
    head_dim = cache.shape[3] // 2
    me = lax.axis_index(HEAD)

    side = lax.axis_size("x")
    near = [own_rows] + [partner(own_rows, "x", o) for o in range(1, side)]
    near_core = [partner(own_rows, "c", 1)]

    reach, depth = ancestry(parents)
    positions = lengths[:, None].astype(jnp.float32) + depth
    frequency = ROPE_BASE ** (-jnp.arange(head_dim // 2, dtype=jnp.float32) / (head_dim // 2))
    angle = positions[..., None] * frequency
    cosine = jnp.cos(angle)
    sine = jnp.sin(angle)
    cosine = jnp.concatenate([cosine, cosine], axis=-1)
    sine = jnp.concatenate([-sine, sine], axis=-1)
    for o in range(1, side):
        near[o], cosine, sine, reach = lax.optimization_barrier((near[o], cosine, sine, reach))
        near_core.append(partner(near[o], "c", 1))

    gate_turned, up_turned = shared_gate.T, shared_up.T
    early, _ = lax.optimization_barrier(((w_out, gate_turned), near_core[0]))
    early = [partner(weight, "c", 1) for weight in early]
    late, _ = lax.optimization_barrier(
        ((up_turned, shared_down, expert_in[0], expert_out[0]), near_core[side - 1])
    )
    late = [partner(weight, "c", 1) for weight in late]

    terms = [None] * side
    fresh = [None] * side
    follow = None
    for o in reversed(range(side)):
        if follow is not None:
            near_core[o], _ = lax.optimization_barrier((near_core[o], follow))
        ids = me ^ jnp.arange(2 * o, 2 * o + 2, dtype=jnp.int32)
        here = ids[:, None] == jnp.arange(group_count, dtype=jnp.int32)
        info = jnp.concatenate([ids, jnp.sum(jnp.where(here, lengths, 0), axis=1)])
        mixed_own, mixed_other, fresh_own, fresh_other = attend(
            info,
            near[o],
            near_core[o],
            attn_gain[None],
            w_qkv,
            cosine,
            sine,
            reach,
            cache[:, 0],
        )
        follow = mixed_own
        fresh[o] = jnp.stack([fresh_own, fresh_other])
        other = partner(mixed_other, "c", 1)
        terms[o] = dot(mixed_own, w_out) + dot(other, early[0])
        if o:
            terms[o] = terms[o].astype(jnp.bfloat16)
            terms[o], early, late[0], late[1] = lax.optimization_barrier(
                (terms[o], early, late[0], late[1])
            )
    own_routes, _ = lax.optimization_barrier((routes[0], terms[side - 1]))
    attn = terms[0]
    for o in range(1, side):
        attn = attn + partner(terms[o], "x", o).astype(jnp.float32)
    resid = (own_rows.astype(jnp.float32) + attn).astype(jnp.bfloat16)
    normed = rms_norm(resid, ffn_gain)
    line = lax.axis_size("z")
    chosen = [partner(own_routes, "z", k) for k in range(line)]
    normed, chosen, late = lax.optimization_barrier((normed, chosen, late))
    inner = [expert_in[0], late[2]]
    outer = [expert_out[0], late[3]]
    shared_weights = [gate_turned, up_turned, shared_down, early[1], late[0], late[1]]
    order = me ^ jnp.arange(group_count, dtype=jnp.int32)
    kept = accepted[order][:, :, None] == jnp.arange(tree, dtype=jnp.int32)
    accepted_kv = jnp.einsum(
        "ran,rnd->rad",
        kept.astype(jnp.bfloat16),
        jnp.concatenate(fresh, axis=0),
        preferred_element_type=jnp.float32,
    ).astype(jnp.bfloat16)[order][:, None]

    expert_count = router.shape[1]
    top_count = routes.shape[2]
    capacity = 4 * tree * top_count // (3 * expert_count)
    plane = lax.axis_size(PLANE)
    spot = lax.axis_index(PLANE)
    first = lax.axis_index("z") * plane
    choose = jnp.stack(chosen)
    member = jnp.any(
        choose[..., None] == jnp.arange(expert_count, dtype=jnp.int32), axis=2
    )
    before = jnp.tril(jnp.ones((tree, tree), jnp.bfloat16), -1)
    ranks = jnp.einsum(
        "nm,kme->kne", before, member.astype(jnp.bfloat16), preferred_element_type=jnp.float32
    ).astype(jnp.int32)
    near_experts = first + (spot ^ jnp.arange(plane, dtype=jnp.int32))
    is_near = near_experts[:, None] == jnp.arange(expert_count, dtype=jnp.int32)
    slot = jnp.where(member, ranks, -1)
    slot_near = jnp.sum(
        jnp.where(is_near[:, None, None, :], slot[None] + 1, 0), axis=-1
    ) - 1
    places = jnp.arange(capacity, dtype=jnp.int32)
    pick = slot_near[:, :, None, :] == places[:, None]
    pick_bf = pick.astype(jnp.bfloat16)

    line_rows = [normed] + [partner(normed, "z", k) for k in range(1, line)]
    beside = [partner(normed, "x", o) for o in range(1, side)]

    own_part, beside_part = shared_terms(normed, beside, shared_weights)

    line_rows[1], beside_part = lax.optimization_barrier((line_rows[1], beside_part))

    logits = jnp.stack([dot(rows, router) for rows in line_rows])
    picked = jnp.where(member, jax.nn.sigmoid(logits), 0.0)
    gates = picked / jnp.sum(picked, axis=-1, keepdims=True)
    gates_near = jnp.sum(jnp.where(is_near[:, None, None, :], gates[None], 0.0), axis=-1)
    spread = jnp.where(pick, gates_near[:, :, None, :], 0.0)
    spread = spread.astype(jnp.bfloat16)

    def dispatch(ks):
        out = [
            dot(pick_bf[:, k].reshape(plane * capacity, tree), line_rows[k])
            .astype(jnp.bfloat16)
            .reshape(plane, capacity, width)
            for k in ks
        ]
        return [
            partner(jnp.concatenate([piece[o] for piece in out], axis=0), PLANE, o)
            for o in range(plane)
        ]

    sent = [dispatch(ks) for ks in GROUPS]
    made = []
    for pieces in sent:
        if made:
            pieces, made[-1] = lax.optimization_barrier((pieces, made[-1]))
        made.append(experts(pieces, inner, outer))

    shared = own_part
    for o in range(1, side):
        shared = shared + partner(beside_part[o - 1], "x", o).astype(jnp.float32)
    routed = 0.0
    for ks, pieces in reversed(list(zip(GROUPS, made))):
        back = [partner(pieces[o], PLANE, o) for o in range(plane)]
        for i, k in enumerate(ks):
            weights = spread[:, k].reshape(plane * capacity, tree)
            partial = combine(
                weights, back, i * capacity, jnp.bfloat16 if k else jnp.float32
            )
            routed = routed + partner(partial, "z", k).astype(jnp.float32)

    total_out = resid.astype(jnp.float32) + shared + routed
    hidden_out = jnp.where(live[0][:, None] == 1, total_out, 0.0).astype(jnp.bfloat16)
    return (hidden_out[None], accepted_kv)


def solution(mesh):
    line = 4
    shape = (line, mesh.shape["req"] // line, mesh.shape["head"] // 2, 2)
    grid = Mesh(mesh.devices.reshape(shape), ALL)
    req = ("z", "y")
    in_specs = (
        P(ALL, None, None),
        P(ALL, None),
        P(req, None),
        P(req),
        P(req, None),
        P(ALL, None, None),
        P(req, HEAD, None, None),
        P(),
        P(None, HEAD),
        P(HEAD, None),
        P(),
        P(None, HEAD),
        P(None, HEAD),
        P(HEAD, None),
        P(),
        P(ALL, None, None),
        P(ALL, None, None),
    )
    out_specs = (P(ALL, None, None), P(req, HEAD, None, None))
    return jax.shard_map(body, mesh=grid, in_specs=in_specs, out_specs=out_specs, check_vma=False)
```

time: 160 us -> 160 us (level)
  matrix products: 45.6 us -> 9.77 us
  Pallas kernels: 8.04 us -> 34.4 us
  waiting for transfers between devices: 39.4 us -> 44.7 us
  starting transfers between devices: 48.9 us -> 44.3 us
  local copies, waits for them, and re-layouts: 12.3 us -> 16.8 us
  other arithmetic: 4.07 us -> 7.17 us
    dot_general x28 -> x12, matrix products: 36.2 us -> 7.39 us  [dot(): return jnp.dot(left, right, preferred_element_type=jnp.float32)]
    pallas_call x2 -> x10, Pallas kernels: 8.04 us -> 34.4 us  [the longest x3 17.2 us: experts(): pl.pallas_call(kernel, in_specs=[in_vmem()] * plane + [in_hbm()] * 4, out...]
    dot_general x4 -> x0, matrix products: 7.02 us -> none  [body(): jnp.einsum('sn,sd->nd', weights, back, preferred_element_type=jnp.float32)]
    unnamed x62 -> x65, local copies, waits for them, and re-layouts: 8.14 us -> 14.9 us
    ppermute x44 -> x41, waiting for transfers between devices: 39.4 us -> 44.7 us  [partner(): return lax.ppermute(value, axes, [(i, i ^ offset) for i in range(size)])]
    ppermute x44 -> x41, starting transfers between devices: 48.9 us -> 44.3 us  [partner(): return lax.ppermute(value, axes, [(i, i ^ offset) for i in range(size)])]
    broadcast_in_dim x0 -> x1, other arithmetic: none -> 2.12 us  [body(): return (hidden_out[None], accepted_kv)]
  transfers between devices with their start and end apart: 44 -> 41, of which waited for: 13 -> 17; matrix products, arithmetic and copies ran while one was open for 33% -> 11% of each run, Pallas kernels for 5% -> 19%
where the time goes in v3:
time: 160 us; the launch traced here: 158 us
  waiting for transfers between devices  44.7 us (28%)
  starting transfers between devices  44.3 us (28%)
  Pallas kernels  34.4 us (22%)
  local copies, waits for them, and re-layouts  16.8 us (10%)
  matrix products  9.77 us (6%)
  other arithmetic  7.17 us (4%)
    ppermute x41, waiting for transfers between devices, partner(): return lax.ppermute(value, axes, [(i, i ^ offset) for i in range(size)])  44.7 us
    ppermute x41, starting transfers between devices, partner(): return lax.ppermute(value, axes, [(i, i ^ offset) for i in range(size)])  44.3 us
    pallas_call x3, Pallas kernels, experts(): pl.pallas_call(kernel, in_specs=[in_vmem()] * plane + [in_hbm()] * 4, out...  17.2 us
    unnamed x65, local copies, waits for them, and re-layouts  14.9 us
    pallas_call x2, Pallas kernels, attend(): pl.pallas_call(attend_kernel, in_specs=[pl.BlockSpec(memory_space=pltpu.S...  9.83 us
    dot_general x12, matrix products, dot(): return jnp.dot(left, right, preferred_element_type=jnp.float32)  7.39 us
    pallas_call x1, Pallas kernels, shared_terms(): pl.pallas_call(functools.partial(shared_kernel, side=side), in_specs=[in_...  5.54 us
  transfers between devices with their start and end apart: 41, of which 17 were waited for; matrix products, arithmetic and copies ran while one was open for 11% of the time, Pallas kernels for 19%

profile of v3, /device:TPU:0, one launch (start us, length us, event | category | flops | bytes accessed | tf_op | source)
XLA Modules:
  0.0 158.4 jit_solution(14562209431352096905)
XLA Ops:
  0.6 3.0 %collective-permute-start.1 = (bf16[64,2048]{1,0:T(8,128)(2,1)}, bf16[64,2048]{1,0:T(8,128)(2,1)S(1)}, u32[]{:S(2)}, u32[]{:S(2)}) collective-permute-start(bf16[64,2048]{1,0:T(8,128)(2,1)} %bitcast.98), channel_id=1, source_target_pairs={{0,2},{2,0},{1,3},{3,1},{4,6},{6,4},{5,7},{7,5},{8,10},{10,8},{9,1... | collective-permute-start | bytes 786440 | tf_op jit(solution)/shard_map/ppermute | solution.py:25
  7.1 3.1 %collective-permute-done.1.first = bf16[64,2048]{1,0:T(8,128)(2,1)S(1)} collective-permute-done((bf16[64,2048]{1,0:T(8,128)(2,1)}, bf16[64,2048]{1,0:T(8,128)(2,1)S(1)}, u32[]{:S(2)}, u32[]{:S(2)}) %collective-permute-start.1) | collective-permute-done | bytes 262176 | tf_op jit(solution)/shard_map/ppermute | solution.py:25
  12.9 5.1 %collective-permute-done.second = bf16[64,2048]{1,0:T(8,128)(2,1)S(1)} collective-permute-done((bf16[64,2048]{1,0:T(8,128)(2,1)}, bf16[64,2048]{1,0:T(8,128)(2,1)S(1)}, u32[]{:S(2)}, u32[]{:S(2)}) %collective-permute-start) | collective-permute-done | bytes 262176 | tf_op jit(solution)/shard_map/ppermute | solution.py:25
  20.7 2.2 %copy-done.2 = bf16[4,1,2048,256]{3,2,1,0:T(8,128)(2,1)S(1)} copy-done((bf16[4,1,2048,256]{3,2,1,0:T(8,128)(2,1)S(1)}, bf16[4,1,2048,256]{3,2,1,0:T(8,128)(2,1)}, u32[]{:S(2)}) %copy-start.2) | copy-done | bytes 4194328
  22.9 1.9 %copy-done.4 = bf16[2048,768]{1,0:T(8,128)(2,1)S(1)} copy-done((bf16[2048,768]{1,0:T(8,128)(2,1)S(1)}, bf16[2048,768]{1,0:T(8,128)(2,1)}, u32[]{:S(2)}) %copy-start.4) | copy-done | bytes 3145752
  27.4 5.4 %attend.2 = (bf16[64,512]{1,0:T(8,128)(2,1)S(1)}, bf16[64,512]{1,0:T(8,128)(2,1)S(1)}, bf16[64,256]{1,0:T(8,128)(2,1)S(1)}, bf16[64,256]{1,0:T(8,128)(2,1)S(1)}) custom-call(s32[4]{0:T(128)S(1)} %pad_add_fusion.2.info, bf16[64,2048]{1,0:T(8,128)(2,1)S(1)} %copy-done.15, bf16[64,2048]{1,0:T(8,128)(2,1)S(1)} %copy-done.17, f32[1,2048]{1,0:T(1,128)S(1)} %bitcast.105, ...), custom_call_target="tpu_custom_call" | custom-call | tf_op jit(solution)/shard_map/attend/pallas_call | solution.py:165
  36.3 2.2 %copy-done.3 = bf16[4,1,2048,256]{3,2,1,0:T(8,128)(2,1)S(1)} copy-done((bf16[4,1,2048,256]{3,2,1,0:T(8,128)(2,1)S(1)}, bf16[4,1,2048,256]{3,2,1,0:T(8,128)(2,1)}, u32[]{:S(2)}) %copy-start.3) | copy-done | bytes 4194328
  38.5 1.9 %copy-done.5 = bf16[2048,768]{1,0:T(8,128)(2,1)S(1)} copy-done((bf16[2048,768]{1,0:T(8,128)(2,1)S(1)}, bf16[2048,768]{1,0:T(8,128)(2,1)}, u32[]{:S(2)}) %copy-start.5) | copy-done | bytes 3145752
  42.3 4.4 %attend.3 = (bf16[64,512]{1,0:T(8,128)(2,1)S(1)}, bf16[64,512]{1,0:T(8,128)(2,1)S(1)}, bf16[64,256]{1,0:T(8,128)(2,1)S(1)}, bf16[64,256]{1,0:T(8,128)(2,1)S(1)}) custom-call(s32[4]{0:T(128)S(1)} %pad_add_fusion.1.info, bf16[64,2048]{1,0:T(8,128)(2,1)S(1)} %bitcast.100, bf16[64,2048]{1,0:T(8,128)(2,1)S(1)} %copy-done.13, f32[1,2048]{1,0:T(1,128)S(1)} %bitcast.106, ...), custom_call_target="tpu_custom_call" | custom-call | tf_op jit(solution)/shard_map/attend/pallas_call | solution.py:165
  46.7 2.3 %fusion.63 = f32[64,2048]{1,0:T(8,128)S(1)} fusion(bf16[64,512]{1,0:T(8,128)(2,1)} %collective-permute-done.4, bf16[512,2048]{1,0:T(8,128)(2,1)} %collective-permute-done.5), kind=kOutput, calls=%fused_computation.119 | convolution fusion | flops 134217728 | bytes 2686976 | tf_op jit(solution)/shard_map/dot_general | solution.py:35
  50.0 1.7 %collective-permute-start.9 = (bf16[64,2048]{1,0:T(8,128)(2,1)S(1)}, bf16[64,2048]{1,0:T(8,128)(2,1)S(1)}, u32[]{:S(2)}, u32[]{:S(2)}) collective-permute-start(bf16[64,2048]{1,0:T(8,128)(2,1)S(1)} %fusion.4), channel_id=1, source_target_pairs={{0,2},{2,0},{1,3},{3,1},{4,6},{6,4},{5,7},{7,5},{8,10},{10,8},{9,1... | collective-permute-start | bytes 786440 | tf_op jit(solution)/shard_map/ppermute | solution.py:25
  52.2 1.6 %collective-permute-start.10 = (s32[64,6]{0,1:T(8,128)S(1)}, s32[64,6]{0,1:T(8,128)S(1)}, u32[]{:S(2)}, u32[]{:S(2)}) collective-permute-start(s32[64,6]{0,1:T(8,128)S(1)} %bitcast.116), channel_id=1, source_target_pairs={{0,8},{8,0},{16,24},{24,16},{1,9},{9,1},{17,25},{25,17},{2,10},{10... | collective-permute-start | bytes 4616 | tf_op jit(solution)/shard_map/ppermute | solution.py:25
  53.8 2.1 %collective-permute-start.11 = (s32[64,6]{0,1:T(8,128)S(1)}, s32[64,6]{0,1:T(8,128)S(1)}, u32[]{:S(2)}, u32[]{:S(2)}) collective-permute-start(s32[64,6]{0,1:T(8,128)S(1)} %bitcast.117), channel_id=1, source_target_pairs={{0,16},{8,24},{16,0},{24,8},{1,17},{9,25},{17,1},{25,9},{2,18},{10... | collective-permute-start | bytes 4616 | tf_op jit(solution)/shard_map/ppermute | solution.py:25
  55.9 2.4 %collective-permute-done.9 = bf16[64,2048]{1,0:T(8,128)(2,1)S(1)} collective-permute-done((bf16[64,2048]{1,0:T(8,128)(2,1)S(1)}, bf16[64,2048]{1,0:T(8,128)(2,1)S(1)}, u32[]{:S(2)}, u32[]{:S(2)}) %collective-permute-start.9) | collective-permute-done | bytes 262176 | tf_op jit(solution)/shard_map/ppermute | solution.py:25
  58.3 2.9 %collective-permute-start.12 = (s32[64,6]{0,1:T(8,128)S(1)}, s32[64,6]{0,1:T(8,128)S(1)}, u32[]{:S(2)}, u32[]{:S(2)}) collective-permute-start(s32[64,6]{0,1:T(8,128)S(1)} %bitcast.118), channel_id=1, source_target_pairs={{0,24},{8,16},{16,8},{24,0},{1,25},{9,17},{17,9},{25,1},{2,26},{10... | collective-permute-start | bytes 4616 | tf_op jit(solution)/shard_map/ppermute | solution.py:25
  61.2 2.4 %multiply_reduce_fusion = (f32[64]{0:T(128)S(1)}, f32[64,2048]{1,0:T(8,128)S(1)}) fusion(bf16[64,2048]{1,0:T(8,128)(2,1)S(1)} %collective-permute-done.9, f32[64,2048]{1,0:T(8,128)S(1)} %fusion.62, bf16[64,512]{1,0:T(8,128)(2,1)S(1)} %collective-permute-done.3, bf16[512,2048]{1,0:T(8,128)(2,1)} %collective-permute-done.5, bf16[1,64,2048]{2,1,0:T(8,128)(2,1)S(1)} %copy-done.9), kind=kOutput, calls=%fused_computation.35 | convolution fusion | flops 135397312 | bytes 3735808 | tf_op jit(solution)/shard_map/dot_general | solution.py:35
  63.8 1.7 %collective-permute-start.15 = (bf16[64,2048]{1,0:T(8,128)(2,1)S(1)}, bf16[64,2048]{1,0:T(8,128)(2,1)S(1)}, u32[]{:S(2)}, u32[]{:S(2)}) collective-permute-start(bf16[64,2048]{1,0:T(8,128)(2,1)S(1)} %multiply_convert_fusion.refs_0_), channel_id=1, source_target_pairs={{0,2},{2,0},{1,3},{3,1},{4,6},{6,4},{5,7},{7,5},{8,10},{10,8},{9,1... | collective-permute-start | bytes 786440 | tf_op jit(solution)/shard_map/ppermute | solution.py:25
  66.8 1.9 %collective-permute-start.19 = (bf16[64,2048]{1,0:T(8,128)(2,1)S(1)}, bf16[64,2048]{1,0:T(8,128)(2,1)S(1)}, u32[]{:S(2)}, u32[]{:S(2)}) collective-permute-start(bf16[64,2048]{1,0:T(8,128)(2,1)S(1)} %multiply_convert_fusion.refs_0_), channel_id=1, source_target_pairs={{0,24},{8,16},{16,8},{24,0},{1,25},{9,17},{17,9},{25,1},{2,26},{10... | collective-permute-start | bytes 786440 | tf_op jit(solution)/shard_map/ppermute | solution.py:25
  71.1 5.5 %shared.1 = (f32[64,2048]{1,0:T(8,128)S(1)}, bf16[64,2048]{1,0:T(8,128)(2,1)S(1)}) custom-call(bf16[64,2048]{1,0:T(8,128)(2,1)S(1)} %multiply_convert_fusion.refs_0_, bf16[64,2048]{1,0:T(8,128)(2,1)S(1)} %collective-permute-done.15.refs_1_, bf16[352,2048]{1,0:T(8,128)(2,1)S(1)} %bitcast.95, bf16[352,2048]{1,0:T(8,128)(2,1)S(1)} %bitcast.97, ...), custom_call_target="tpu_custom_call" | custom-call | tf_op jit(solution)/shard_map/shared/pallas_call | solution.py:291
  82.7 7.6 %collective-permute-done.18 = bf16[64,2048]{1,0:T(8,128)(2,1)S(1)} collective-permute-done((bf16[64,2048]{1,0:T(8,128)(2,1)S(1)}, bf16[64,2048]{1,0:T(8,128)(2,1)S(1)}, u32[]{:S(2)}, u32[]{:S(2)}) %collective-permute-start.18) | collective-permute-done | bytes 262176 | tf_op jit(solution)/shard_map/ppermute | solution.py:25
  91.9 2.4 %collective-permute-start.25 = (bf16[32,2048]{1,0:T(8,128)(2,1)S(1)}, bf16[32,2048]{1,0:T(8,128)(2,1)S(1)}, u32[]{:S(2)}, u32[]{:S(2)}) collective-permute-start(bf16[32,2048]{1,0:T(8,128)(2,1)S(1)} %get-tuple-element.152), channel_id=1, source_target_pairs={{0,6},{2,4},{4,2},{6,0},{1,7},{3,5},{5,3},{7,1},{8,14},{10,12},{12... | collective-permute-start | bytes 393224 | tf_op jit(solution)/shard_map/ppermute | solution.py:25
  95.4 2.4 %collective-permute-start.22 = (bf16[32,2048]{1,0:T(8,128)(2,1)S(1)}, bf16[32,2048]{1,0:T(8,128)(2,1)S(1)}, u32[]{:S(2)}, u32[]{:S(2)}) collective-permute-start(bf16[32,2048]{1,0:T(8,128)(2,1)S(1)} %get-tuple-element.140), channel_id=1, source_target_pairs={{0,6},{2,4},{4,2},{6,0},{1,7},{3,5},{5,3},{7,1},{8,14},{10,12},{12... | collective-permute-start | bytes 393224 | tf_op jit(solution)/shard_map/ppermute | solution.py:25
  98.2 7.2 %expert.3 = (bf16[64,2048]{1,0:T(8,128)(2,1)S(1)}, bf16[64,2048]{1,0:T(8,128)(2,1)S(1)}, bf16[64,2048]{1,0:T(8,128)(2,1)S(1)}, bf16[64,2048]{1,0:T(8,128)(2,1)S(1)}) custom-call(bf16[64,2048]{1,0:T(8,128)(2,1)S(1)} %pad_maximum_fusion.refs_0_, bf16[64,2048]{1,0:T(8,128)(2,1)S(1)} %collective-permute-done.26.refs_1_, ...), custom_call_target="tpu_custom_call" | custom-call | tf_op jit(solution)/shard_map/expert/pallas_call | solution.py:246
  105.4 5.0 %expert.4 = (bf16[32,2048]{1,0:T(8,128)(2,1)S(1)}, bf16[32,2048]{1,0:T(8,128)(2,1)S(1)}, bf16[32,2048]{1,0:T(8,128)(2,1)S(1)}, bf16[32,2048]{1,0:T(8,128)(2,1)S(1)}) custom-call(bf16[32,2048]{1,0:T(8,128)(2,1)S(1)} %get-tuple-element.106.refs_0_, bf16[32,2048]{1,0:T(8,128)(2,1)S(1)} %collective-permute-done.23.refs_1_, ...), custom_call_target="tpu_custom_call" | custom-call | tf_op jit(solution)/shard_map/expert/pallas_call | solution.py:246
  110.5 5.0 %expert.5 = (bf16[32,2048]{1,0:T(8,128)(2,1)S(1)}, bf16[32,2048]{1,0:T(8,128)(2,1)S(1)}, bf16[32,2048]{1,0:T(8,128)(2,1)S(1)}, bf16[32,2048]{1,0:T(8,128)(2,1)S(1)}) custom-call(bf16[32,2048]{1,0:T(8,128)(2,1)S(1)} %get-tuple-element.114.refs_0_, bf16[32,2048]{1,0:T(8,128)(2,1)S(1)} %collective-permute-done.20.refs_1_, ...), custom_call_target="tpu_custom_call" | custom-call | tf_op jit(solution)/shard_map/expert/pallas_call | solution.py:246
  116.9 2.5 %collective-permute-start.31 = (bf16[32,2048]{1,0:T(8,128)(2,1)S(1)}, bf16[32,2048]{1,0:T(8,128)(2,1)S(1)}, u32[]{:S(2)}, u32[]{:S(2)}) collective-permute-start(bf16[32,2048]{1,0:T(8,128)(2,1)S(1)} %get-tuple-element.121), channel_id=1, source_target_pairs={{0,6},{2,4},{4,2},{6,0},{1,7},{3,5},{5,3},{7,1},{8,14},{10,12},{12... | collective-permute-start | bytes 393224 | tf_op jit(solution)/shard_map/ppermute | solution.py:25
  124.9 1.8 %collective-permute-start.34 = (bf16[32,2048]{1,0:T(8,128)(2,1)S(1)}, bf16[32,2048]{1,0:T(8,128)(2,1)S(1)}, u32[]{:S(2)}, u32[]{:S(2)}) collective-permute-start(bf16[32,2048]{1,0:T(8,128)(2,1)S(1)} %get-tuple-element.124), channel_id=1, source_target_pairs={{0,4},{2,6},{4,0},{6,2},{1,5},{3,7},{5,1},{7,3},{8,12},{10,14},{12... | collective-permute-start | bytes 393224 | tf_op jit(solution)/shard_map/ppermute | solution.py:25
  129.1 5.8 %collective-permute-done.34.refs_2_ = bf16[32,2048]{1,0:T(8,128)(2,1)S(1)} collective-permute-done((bf16[32,2048]{1,0:T(8,128)(2,1)S(1)}, bf16[32,2048]{1,0:T(8,128)(2,1)S(1)}, u32[]{:S(2)}, u32[]{:S(2)}) %collective-permute-start.34) | collective-permute-done | bytes 131104 | tf_op jit(solution)/shard_map/ppermute | solution.py:25
  135.3 4.6 %collective-permute-done.35.refs_3_ = bf16[32,2048]{1,0:T(8,128)(2,1)S(1)} collective-permute-done((bf16[32,2048]{1,0:T(8,128)(2,1)S(1)}, bf16[32,2048]{1,0:T(8,128)(2,1)S(1)}, u32[]{:S(2)}, u32[]{:S(2)}) %collective-permute-start.35) | collective-permute-done | bytes 131104 | tf_op jit(solution)/shard_map/ppermute | solution.py:25
  140.4 4.0 %collective-permute-start.36 = (bf16[64,2048]{1,0:T(8,128)(2,1)S(1)}, bf16[64,2048]{1,0:T(8,128)(2,1)}, u32[]{:S(2)}, u32[]{:S(2)}) collective-permute-start(bf16[64,2048]{1,0:T(8,128)(2,1)S(1)} %combine.5), channel_id=1, source_target_pairs={{0,24},{8,16},{16,8},{24,0},{1,25},{9,17},{17,9},{25,1},{2,26},{10... | collective-permute-start | bytes 786440 | tf_op jit(solution)/shard_map/ppermute | solution.py:25
  147.3 8.5 %collective-permute-done.32 = bf16[64,2048]{1,0:T(8,128)(2,1)} collective-permute-done((bf16[64,2048]{1,0:T(8,128)(2,1)S(1)}, bf16[64,2048]{1,0:T(8,128)(2,1)}, u32[]{:S(2)}, u32[]{:S(2)}) %collective-permute-start.32) | collective-permute-done | bytes 262176 | tf_op jit(solution)/shard_map/ppermute | solution.py:25
  156.3 2.1 %fusion.13 = bf16[1,64,2048]{2,1,0:T(8,128)(2,1)} fusion(bf16[64,2048]{1,0:T(8,128)(2,1)} %collective-permute-done.40, f32[64,2048]{1,0:T(8,128)S(1)} %combine.6, bf16[64,2048]{1,0:T(8,128)(2,1)} %collective-permute-done.36, bf16[64,2048]{1,0:T(8,128)(2,1)} %collective-permute-done.32, f32[64,2048]{1,0:T(8,128)S(1)} %copy-done.26, ...), kind=kLoop, calls=%fused_computation.36 | loop fusion | flops 1572864 | bytes 2883648 | tf_op jit(solution)/shard_map/broadcast_in_dim | solution.py:507
  (185 shorter events, 44.5 us)
Async XLA Ops:
  0.6 9.5 %collective-permute-start.1 = (bf16[64,2048]{1,0:T(8,128)(2,1)}, bf16[64,2048]{1,0:T(8,128)(2,1)S(1)}, u32[]{:S(2)}, u32[]{:S(2)}) collective-permute-start(bf16[64,2048]{1,0:T(8,128)(2,1)} %bitcast.98), channel_id=1, source_target_pairs={{0,2},{2,0},{1,3},{3,1},{4,6},{6,4},{5,7},{7,5},{8,10},{10,8},{9,1... | collective-permute-start | bytes 786440 | tf_op jit(solution)/shard_map/ppermute | solution.py:25
  12.4 51.4 %collective-permute-start.13 = (bf16[2048,1408]{1,0:T(8,128)(2,1)}, bf16[2048,1408]{1,0:T(8,128)(2,1)}, u32[]{:S(2)}, u32[]{:S(2)}) collective-permute-start(bf16[2048,1408]{1,0:T(8,128)(2,1)} %bitcast.82), channel_id=1, source_target_pairs={{0,1},{1,0},{2,3},{3,2},{4,5},{5,4},{6,7},{7,6},{8,9},{9,8},{10,11... | collective-permute-start | bytes 17301512 | tf_op jit(solution)/shard_map/ppermute | solution.py:25
  18.8 15.9 %collective-permute-start.5 = (bf16[512,2048]{1,0:T(8,128)(2,1)}, bf16[512,2048]{1,0:T(8,128)(2,1)}, u32[]{:S(2)}, u32[]{:S(2)}) collective-permute-start(bf16[512,2048]{1,0:T(8,128)(2,1)} %param.26), channel_id=1, source_target_pairs={{0,1},{1,0},{2,3},{3,2},{4,5},{5,4},{6,7},{7,6},{8,9},{9,8},{10,11... | collective-permute-start | bytes 6291464 | tf_op jit(solution)/shard_map/ppermute | solution.py:25
  20.5 43.3 %collective-permute-start.14 = (bf16[704,2048]{1,0:T(8,128)(2,1)}, bf16[704,2048]{1,0:T(8,128)(2,1)S(1)}, u32[]{:S(2)}, u32[]{:S(2)}) collective-permute-start(bf16[704,2048]{1,0:T(8,128)(2,1)} %bitcast.88), channel_id=1, source_target_pairs={{0,1},{1,0},{2,3},{3,2},{4,5},{5,4},{6,7},{7,6},{8,9},{9,8},{10,11... | collective-permute-start | bytes 8650760 | tf_op jit(solution)/shard_map/ppermute | solution.py:25
  33.3 16.3 %collective-permute-start.6 = (bf16[352,2048]{1,0:T(8,128)(2,1)}, bf16[352,2048]{1,0:T(8,128)(2,1)S(1)}, u32[]{:S(2)}, u32[]{:S(2)}) collective-permute-start(bf16[352,2048]{1,0:T(8,128)(2,1)} %bitcast.94), channel_id=1, source_target_pairs={{0,1},{1,0},{2,3},{3,2},{4,5},{5,4},{6,7},{7,6},{8,9},{9,8},{10,11... | collective-permute-start | bytes 4325384 | tf_op jit(solution)/shard_map/ppermute | solution.py:25
  34.3 15.7 %collective-permute-start.7 = (bf16[352,2048]{1,0:T(8,128)(2,1)}, bf16[352,2048]{1,0:T(8,128)(2,1)S(1)}, u32[]{:S(2)}, u32[]{:S(2)}) collective-permute-start(bf16[352,2048]{1,0:T(8,128)(2,1)} %bitcast.96), channel_id=1, source_target_pairs={{0,1},{1,0},{2,3},{3,2},{4,5},{5,4},{6,7},{7,6},{8,9},{9,8},{10,11... | collective-permute-start | bytes 4325384 | tf_op jit(solution)/shard_map/ppermute | solution.py:25
  34.7 15.3 %collective-permute-start.8 = (bf16[352,2048]{1,0:T(8,128)(2,1)}, bf16[352,2048]{1,0:T(8,128)(2,1)S(1)}, u32[]{:S(2)}, u32[]{:S(2)}) collective-permute-start(bf16[352,2048]{1,0:T(8,128)(2,1)} %refs_4_.1), channel_id=1, source_target_pairs={{0,1},{1,0},{2,3},{3,2},{4,5},{5,4},{6,7},{7,6},{8,9},{9,8},{10,11... | collective-permute-start | bytes 4325384 | tf_op jit(solution)/shard_map/ppermute | solution.py:25
  50.0 8.4 %collective-permute-start.9 = (bf16[64,2048]{1,0:T(8,128)(2,1)S(1)}, bf16[64,2048]{1,0:T(8,128)(2,1)S(1)}, u32[]{:S(2)}, u32[]{:S(2)}) collective-permute-start(bf16[64,2048]{1,0:T(8,128)(2,1)S(1)} %fusion.4), channel_id=1, source_target_pairs={{0,2},{2,0},{1,3},{3,1},{4,6},{6,4},{5,7},{7,5},{8,10},{10,8},{9,1... | collective-permute-start | bytes 786440 | tf_op jit(solution)/shard_map/ppermute | solution.py:25
  52.2 11.6 %collective-permute-start.10 = (s32[64,6]{0,1:T(8,128)S(1)}, s32[64,6]{0,1:T(8,128)S(1)}, u32[]{:S(2)}, u32[]{:S(2)}) collective-permute-start(s32[64,6]{0,1:T(8,128)S(1)} %bitcast.116), channel_id=1, source_target_pairs={{0,8},{8,0},{16,24},{24,16},{1,9},{9,1},{17,25},{25,17},{2,10},{10... | collective-permute-start | bytes 4616 | tf_op jit(solution)/shard_map/ppermute | solution.py:25
  53.8 9.9 %collective-permute-start.11 = (s32[64,6]{0,1:T(8,128)S(1)}, s32[64,6]{0,1:T(8,128)S(1)}, u32[]{:S(2)}, u32[]{:S(2)}) collective-permute-start(s32[64,6]{0,1:T(8,128)S(1)} %bitcast.117), channel_id=1, source_target_pairs={{0,16},{8,24},{16,0},{24,8},{1,17},{9,25},{17,1},{25,9},{2,18},{10... | collective-permute-start | bytes 4616 | tf_op jit(solution)/shard_map/ppermute | solution.py:25
  65.5 11.2 %collective-permute-start.16 = (bf16[64,2048]{1,0:T(8,128)(2,1)S(1)}, bf16[64,2048]{1,0:T(8,128)(2,1)S(1)}, u32[]{:S(2)}, u32[]{:S(2)}) collective-permute-start(bf16[64,2048]{1,0:T(8,128)(2,1)S(1)} %multiply_convert_fusion.refs_0_), channel_id=1, source_target_pairs={{0,8},{8,0},{16,24},{24,16},{1,9},{9,1},{17,25},{25,17},{2,10},{10... | collective-permute-start | bytes 786440 | tf_op jit(solution)/shard_map/ppermute | solution.py:25
  66.8 14.6 %collective-permute-start.19 = (bf16[64,2048]{1,0:T(8,128)(2,1)S(1)}, bf16[64,2048]{1,0:T(8,128)(2,1)S(1)}, u32[]{:S(2)}, u32[]{:S(2)}) collective-permute-start(bf16[64,2048]{1,0:T(8,128)(2,1)S(1)} %multiply_convert_fusion.refs_0_), channel_id=1, source_target_pairs={{0,24},{8,16},{16,8},{24,0},{1,25},{9,17},{17,9},{25,1},{2,26},{10... | collective-permute-start | bytes 786440 | tf_op jit(solution)/shard_map/ppermute | solution.py:25
  68.7 21.7 %collective-permute-start.18 = (bf16[64,2048]{1,0:T(8,128)(2,1)S(1)}, bf16[64,2048]{1,0:T(8,128)(2,1)S(1)}, u32[]{:S(2)}, u32[]{:S(2)}) collective-permute-start(bf16[64,2048]{1,0:T(8,128)(2,1)S(1)} %multiply_convert_fusion.refs_0_), channel_id=1, source_target_pairs={{0,16},{8,24},{16,0},{24,8},{1,17},{9,25},{17,1},{25,9},{2,18},{10... | collective-permute-start | bytes 786440 | tf_op jit(solution)/shard_map/ppermute | solution.py:25
  77.1 17.3 %collective-permute-start.28 = (bf16[64,2048]{1,0:T(8,128)(2,1)S(1)}, bf16[64,2048]{1,0:T(8,128)(2,1)S(1)}, u32[]{:S(2)}, u32[]{:S(2)}) collective-permute-start(bf16[64,2048]{1,0:T(8,128)(2,1)S(1)} %pad_maximum_fusion.3), channel_id=1, source_target_pairs={{0,6},{2,4},{4,2},{6,0},{1,7},{3,5},{5,3},{7,1},{8,14},{10,12},{12... | collective-permute-start | bytes 786440 | tf_op jit(solution)/shard_map/ppermute | solution.py:25
  78.6 16.4 %collective-permute-start.27 = (bf16[64,2048]{1,0:T(8,128)(2,1)S(1)}, bf16[64,2048]{1,0:T(8,128)(2,1)S(1)}, u32[]{:S(2)}, u32[]{:S(2)}) collective-permute-start(bf16[64,2048]{1,0:T(8,128)(2,1)S(1)} %pad_maximum_fusion.2), channel_id=1, source_target_pairs={{0,4},{2,6},{4,0},{6,2},{1,5},{3,7},{5,1},{7,3},{8,12},{10,14},{12... | collective-permute-start | bytes 786440 | tf_op jit(solution)/shard_map/ppermute | solution.py:25
  80.2 15.2 %collective-permute-start.26 = (bf16[64,2048]{1,0:T(8,128)(2,1)S(1)}, bf16[64,2048]{1,0:T(8,128)(2,1)S(1)}, u32[]{:S(2)}, u32[]{:S(2)}) collective-permute-start(bf16[64,2048]{1,0:T(8,128)(2,1)S(1)} %pad_maximum_fusion.1), channel_id=1, source_target_pairs={{0,2},{2,0},{4,6},{6,4},{1,3},{3,1},{5,7},{7,5},{8,10},{10,8},{12,... | collective-permute-start | bytes 786440 | tf_op jit(solution)/shard_map/ppermute | solution.py:25
  81.8 10.1 %collective-permute-start.23 = (bf16[32,2048]{1,0:T(8,128)(2,1)S(1)}, bf16[32,2048]{1,0:T(8,128)(2,1)S(1)}, u32[]{:S(2)}, u32[]{:S(2)}) collective-permute-start(bf16[32,2048]{1,0:T(8,128)(2,1)S(1)} %get-tuple-element.154), channel_id=1, source_target_pairs={{0,2},{2,0},{4,6},{6,4},{1,3},{3,1},{5,7},{7,5},{8,10},{10,8},{12,... | collective-permute-start | bytes 393224 | tf_op jit(solution)/shard_map/ppermute | solution.py:25
  90.4 15.0 %collective-permute-start.24 = (bf16[32,2048]{1,0:T(8,128)(2,1)S(1)}, bf16[32,2048]{1,0:T(8,128)(2,1)S(1)}, u32[]{:S(2)}, u32[]{:S(2)}) collective-permute-start(bf16[32,2048]{1,0:T(8,128)(2,1)S(1)} %get-tuple-element.153), channel_id=1, source_target_pairs={{0,4},{2,6},{4,0},{6,2},{1,5},{3,7},{5,1},{7,3},{8,12},{10,14},{12... | collective-permute-start | bytes 393224 | tf_op jit(solution)/shard_map/ppermute | solution.py:25
  91.9 13.5 %collective-permute-start.25 = (bf16[32,2048]{1,0:T(8,128)(2,1)S(1)}, bf16[32,2048]{1,0:T(8,128)(2,1)S(1)}, u32[]{:S(2)}, u32[]{:S(2)}) collective-permute-start(bf16[32,2048]{1,0:T(8,128)(2,1)S(1)} %get-tuple-element.152), channel_id=1, source_target_pairs={{0,6},{2,4},{4,2},{6,0},{1,7},{3,5},{5,3},{7,1},{8,14},{10,12},{12... | collective-permute-start | bytes 393224 | tf_op jit(solution)/shard_map/ppermute | solution.py:25
  94.3 16.1 %collective-permute-start.20 = (bf16[32,2048]{1,0:T(8,128)(2,1)S(1)}, bf16[32,2048]{1,0:T(8,128)(2,1)S(1)}, u32[]{:S(2)}, u32[]{:S(2)}) collective-permute-start(bf16[32,2048]{1,0:T(8,128)(2,1)S(1)} %get-tuple-element.142), channel_id=1, source_target_pairs={{0,2},{2,0},{4,6},{6,4},{1,3},{3,1},{5,7},{7,5},{8,10},{10,8},{12,... | collective-permute-start | bytes 393224 | tf_op jit(solution)/shard_map/ppermute | solution.py:25
  95.0 15.4 %collective-permute-start.21 = (bf16[32,2048]{1,0:T(8,128)(2,1)S(1)}, bf16[32,2048]{1,0:T(8,128)(2,1)S(1)}, u32[]{:S(2)}, u32[]{:S(2)}) collective-permute-start(bf16[32,2048]{1,0:T(8,128)(2,1)S(1)} %get-tuple-element.141), channel_id=1, source_target_pairs={{0,4},{2,6},{4,0},{6,2},{1,5},{3,7},{5,1},{7,3},{8,12},{10,14},{12... | collective-permute-start | bytes 393224 | tf_op jit(solution)/shard_map/ppermute | solution.py:25
  95.4 15.1 %collective-permute-start.22 = (bf16[32,2048]{1,0:T(8,128)(2,1)S(1)}, bf16[32,2048]{1,0:T(8,128)(2,1)S(1)}, u32[]{:S(2)}, u32[]{:S(2)}) collective-permute-start(bf16[32,2048]{1,0:T(8,128)(2,1)S(1)} %get-tuple-element.140), channel_id=1, source_target_pairs={{0,6},{2,4},{4,2},{6,0},{1,7},{3,5},{5,3},{7,1},{8,14},{10,12},{12... | collective-permute-start | bytes 393224 | tf_op jit(solution)/shard_map/ppermute | solution.py:25
  119.5 8.2 %collective-permute-start.33 = (bf16[32,2048]{1,0:T(8,128)(2,1)S(1)}, bf16[32,2048]{1,0:T(8,128)(2,1)S(1)}, u32[]{:S(2)}, u32[]{:S(2)}) collective-permute-start(bf16[32,2048]{1,0:T(8,128)(2,1)S(1)} %get-tuple-element.123), channel_id=1, source_target_pairs={{0,2},{2,0},{4,6},{6,4},{1,3},{3,1},{5,7},{7,5},{8,10},{10,8},{12,... | collective-permute-start | bytes 393224 | tf_op jit(solution)/shard_map/ppermute | solution.py:25
  120.2 20.2 %collective-permute-start.37 = (bf16[64,2048]{1,0:T(8,128)(2,1)S(1)}, bf16[64,2048]{1,0:T(8,128)(2,1)S(1)}, u32[]{:S(2)}, u32[]{:S(2)}) collective-permute-start(bf16[64,2048]{1,0:T(8,128)(2,1)S(1)} %get-tuple-element.127), channel_id=1, source_target_pairs={{0,2},{2,0},{4,6},{6,4},{1,3},{3,1},{5,7},{7,5},{8,10},{10,8},{12,... | collective-permute-start | bytes 786440 | tf_op jit(solution)/shard_map/ppermute | solution.py:25
  122.0 22.3 %collective-permute-start.38 = (bf16[64,2048]{1,0:T(8,128)(2,1)S(1)}, bf16[64,2048]{1,0:T(8,128)(2,1)S(1)}, u32[]{:S(2)}, u32[]{:S(2)}) collective-permute-start(bf16[64,2048]{1,0:T(8,128)(2,1)S(1)} %get-tuple-element.128), channel_id=1, source_target_pairs={{0,4},{2,6},{4,0},{6,2},{1,5},{3,7},{5,1},{7,3},{8,12},{10,14},{12... | collective-permute-start | bytes 786440 | tf_op jit(solution)/shard_map/ppermute | solution.py:25
  123.4 20.9 %collective-permute-start.39 = (bf16[64,2048]{1,0:T(8,128)(2,1)S(1)}, bf16[64,2048]{1,0:T(8,128)(2,1)S(1)}, u32[]{:S(2)}, u32[]{:S(2)}) collective-permute-start(bf16[64,2048]{1,0:T(8,128)(2,1)S(1)} %get-tuple-element.129), channel_id=1, source_target_pairs={{0,6},{2,4},{4,2},{6,0},{1,7},{3,5},{5,3},{7,1},{8,14},{10,12},{12... | collective-permute-start | bytes 786440 | tf_op jit(solution)/shard_map/ppermute | solution.py:25
  124.9 10.0 %collective-permute-start.34 = (bf16[32,2048]{1,0:T(8,128)(2,1)S(1)}, bf16[32,2048]{1,0:T(8,128)(2,1)S(1)}, u32[]{:S(2)}, u32[]{:S(2)}) collective-permute-start(bf16[32,2048]{1,0:T(8,128)(2,1)S(1)} %get-tuple-element.124), channel_id=1, source_target_pairs={{0,4},{2,6},{4,0},{6,2},{1,5},{3,7},{5,1},{7,3},{8,12},{10,14},{12... | collective-permute-start | bytes 393224 | tf_op jit(solution)/shard_map/ppermute | solution.py:25
  127.6 12.3 %collective-permute-start.35 = (bf16[32,2048]{1,0:T(8,128)(2,1)S(1)}, bf16[32,2048]{1,0:T(8,128)(2,1)S(1)}, u32[]{:S(2)}, u32[]{:S(2)}) collective-permute-start(bf16[32,2048]{1,0:T(8,128)(2,1)S(1)} %get-tuple-element.125), channel_id=1, source_target_pairs={{0,6},{2,4},{4,2},{6,0},{1,7},{3,5},{5,3},{7,1},{8,14},{10,12},{12... | collective-permute-start | bytes 393224 | tf_op jit(solution)/shard_map/ppermute | solution.py:25
  134.9 12.5 %collective-permute-start.17 = (bf16[64,2048]{1,0:T(8,128)(2,1)S(1)}, bf16[64,2048]{1,0:T(8,128)(2,1)}, u32[]{:S(2)}, u32[]{:S(2)}) collective-permute-start(bf16[64,2048]{1,0:T(8,128)(2,1)S(1)} %get-tuple-element.94), channel_id=1, source_target_pairs={{0,2},{2,0},{1,3},{3,1},{4,6},{6,4},{5,7},{7,5},{8,10},{10,8},{9,1... | collective-permute-start | bytes 786440 | tf_op jit(solution)/shard_map/ppermute | solution.py:25
  139.9 15.9 %collective-permute-start.32 = (bf16[64,2048]{1,0:T(8,128)(2,1)S(1)}, bf16[64,2048]{1,0:T(8,128)(2,1)}, u32[]{:S(2)}, u32[]{:S(2)}) collective-permute-start(bf16[64,2048]{1,0:T(8,128)(2,1)S(1)} %combine.4), channel_id=1, source_target_pairs={{0,16},{8,24},{16,0},{24,8},{1,17},{9,25},{17,1},{25,9},{2,18},{10... | collective-permute-start | bytes 786440 | tf_op jit(solution)/shard_map/ppermute | solution.py:25
  140.4 15.4 %collective-permute-start.36 = (bf16[64,2048]{1,0:T(8,128)(2,1)S(1)}, bf16[64,2048]{1,0:T(8,128)(2,1)}, u32[]{:S(2)}, u32[]{:S(2)}) collective-permute-start(bf16[64,2048]{1,0:T(8,128)(2,1)S(1)} %combine.5), channel_id=1, source_target_pairs={{0,24},{8,16},{16,8},{24,0},{1,25},{9,17},{17,9},{25,1},{2,26},{10... | collective-permute-start | bytes 786440 | tf_op jit(solution)/shard_map/ppermute | solution.py:25
  144.8 11.5 %collective-permute-start.40 = (bf16[64,2048]{1,0:T(8,128)(2,1)S(1)}, bf16[64,2048]{1,0:T(8,128)(2,1)}, u32[]{:S(2)}, u32[]{:S(2)}) collective-permute-start(bf16[64,2048]{1,0:T(8,128)(2,1)S(1)} %combine.7), channel_id=1, source_target_pairs={{0,8},{8,0},{16,24},{24,16},{1,9},{9,1},{17,25},{25,17},{2,10},{10... | collective-permute-start | bytes 786440 | tf_op jit(solution)/shard_map/ppermute | solution.py:25
  (41 other events, 396.9 us)

commit v4 on v3

--- a/solution.py
+++ b/solution.py
@@ -13,6 +13,7 @@
 ROPE_BASE = 10000.0
 GROUPS = ((0, 1), (3,), (2,))
 CHUNK = 512
+EXTRA = 128
 ALL = ("z", "y", "x", "c")
 PLANE = ("y", "x")
 HEAD = ("x", "c")
@@ -23,12 +24,6 @@
         return value
     size = lax.axis_size(axes)
     return lax.ppermute(value, axes, [(i, i ^ offset) for i in range(size)])
-
-
-def rms_norm(values, gain):
-    wide = values.astype(jnp.float32)
-    power = jnp.mean(wide * wide, axis=-1, keepdims=True)
-    return (wide * lax.rsqrt(power + EPSILON) * gain).astype(jnp.bfloat16)
 
 
 def dot(left, right):
@@ -184,7 +179,7 @@
             pltpu.VMEM((1, width), jnp.float32),
             pltpu.SemaphoreType.DMA((5,)),
         ],
-        compiler_params=pltpu.CompilerParams(vmem_limit_bytes=24 * 2**20),
+        compiler_params=pltpu.CompilerParams(vmem_limit_bytes=60 * 2**20),
         name="attend",
     )(info, first, second, gain, weight, cosine, sine, reach, cache)
 
@@ -304,23 +299,118 @@
     return outs[0], list(outs[1:])
 
 
+def finish_kernel(tokens, term, gain, routes, *refs):
+    others = refs[:-3]
+    resid, normed, payload = refs[-3:]
+    width = tokens.shape[1]
+    attn = term[...]
+    for other in others:
+        attn = attn + other[...].astype(jnp.float32)
+    rounded = (tokens[...].astype(jnp.float32) + attn).astype(jnp.bfloat16)
+    resid[...] = rounded
+    wide = rounded.astype(jnp.float32)
+    power = jnp.mean(wide * wide, axis=-1, keepdims=True)
+    rows = (wide * lax.rsqrt(power + EPSILON) * gain[...]).astype(jnp.bfloat16)
+    normed[...] = rows
+    payload[:, :width] = rows
+    extra = payload.shape[1] - width
+    lane = lax.broadcasted_iota(jnp.int32, (tokens.shape[0], extra), 1)
+    numbers = jnp.zeros(lane.shape, jnp.float32)
+    for t in range(routes.shape[1]):
+        numbers = jnp.where(lane == t, routes[:, t : t + 1].astype(jnp.float32), numbers)
+    payload[:, width:] = numbers.astype(jnp.bfloat16)
+
+
+def finish(tokens, term, others, gain, routes):
+    tree, width = tokens.shape
+    return pl.pallas_call(
+        finish_kernel,
+        in_specs=[in_vmem()] * (4 + len(others)),
+        out_specs=[in_vmem()] * 3,
+        out_shape=[
+            jax.ShapeDtypeStruct((tree, width), jnp.bfloat16),
+            jax.ShapeDtypeStruct((tree, width), jnp.bfloat16),
+            jax.ShapeDtypeStruct((tree, width + EXTRA), jnp.bfloat16),
+        ],
+        compiler_params=pltpu.CompilerParams(vmem_limit_bytes=16 * 2**20),
+        name="finish",
+    )(tokens, term, gain, routes, *others)
+
+
+def select_kernel(*refs, count, plane, capacity, top_count):
+    near = refs[0]
+    router = refs[1]
+    sources = refs[2 : 2 + count]
+    outs = refs[2 + count : 2 + count + plane]
+    spreads = refs[2 + count + plane :]
+    width, expert_count = router.shape
+    tree = sources[0].shape[0]
+    lane = lax.broadcasted_iota(jnp.int32, (tree, plane * capacity), 1)
+    place = lax.rem(lane, capacity).astype(jnp.float32)
+    owner = lax.div(lane, capacity)
+    expert = lax.broadcasted_iota(jnp.int32, (tree, expert_count), 1)
+    row = lax.broadcasted_iota(jnp.int32, (tree, tree), 0)
+    column = lax.broadcasted_iota(jnp.int32, (tree, tree), 1)
+    before = jnp.where(column < row, 1.0, 0.0).astype(jnp.bfloat16)
+    for i in range(count):
+        rows = sources[i][:, :width]
+        routes = sources[i][:, width:].astype(jnp.float32)
+        member = jnp.zeros((tree, expert_count), jnp.float32)
+        for t in range(top_count):
+            named = routes[:, t : t + 1] == expert.astype(jnp.float32)
+            member = jnp.where(named, 1.0, member)
+        ranks = dot(before, member.astype(jnp.bfloat16))
+        slots = jnp.where(member > 0.5, ranks, -1.0)
+        logits = dot(rows, router[...])
+        picked = member / (1.0 + jnp.exp(-logits))
+        gates = picked / jnp.sum(picked, axis=-1, keepdims=True)
+        slot = jnp.zeros(lane.shape, jnp.float32)
+        gate = jnp.zeros(lane.shape, jnp.float32)
+        for o in range(plane):
+            mine = expert == near[o]
+            slot_o = jnp.sum(jnp.where(mine, slots, 0.0), axis=-1, keepdims=True)
+            gate_o = jnp.sum(jnp.where(mine, gates, 0.0), axis=-1, keepdims=True)
+            slot = jnp.where(owner == o, slot_o, slot)
+            gate = jnp.where(owner == o, gate_o, gate)
+        pick = slot == place
+        spreads[i][...] = jnp.where(pick, gate, 0.0).astype(jnp.bfloat16)
+        chosen = lax.dot_general(
+            jnp.where(pick, 1.0, 0.0).astype(jnp.bfloat16),
+            rows,
+            (((0,), (0,)), ((), ())),
+            preferred_element_type=jnp.float32,
+        ).astype(jnp.bfloat16)
+        for o in range(plane):
+            outs[o][i * capacity : (i + 1) * capacity] = chosen[o * capacity : (o + 1) * capacity]
+
+
+def select(near, router, sources, plane, capacity, top_count):
+    tree = sources[0].shape[0]
+    width = router.shape[0]
+    count = len(sources)
+    made = pl.pallas_call(
+        functools.partial(
+            select_kernel, count=count, plane=plane, capacity=capacity, top_count=top_count
+        ),
+        in_specs=[pl.BlockSpec(memory_space=pltpu.SMEM)] + [in_vmem()] * (1 + count),
+        out_specs=[in_vmem()] * (plane + count),
+        out_shape=[jax.ShapeDtypeStruct((count * capacity, width), jnp.bfloat16)] * plane
+        + [jax.ShapeDtypeStruct((tree, plane * capacity), jnp.bfloat16)] * count,
+        compiler_params=pltpu.CompilerParams(vmem_limit_bytes=16 * 2**20),
+        name="select",
+    )(near, router, *sources)
+    return list(made[:plane]), list(made[plane:])
+
+
 def combine_kernel(spread, *refs, start):
     out = refs[-1]
-    slots = spread.shape[0] // (len(refs) - 1)
-    total = None
-    for i, piece in enumerate(refs[:-1]):
-        term = lax.dot_general(
-            spread[i * slots : (i + 1) * slots],
-            piece[start : start + slots],
-            (((0,), (0,)), ((), ())),
-            preferred_element_type=jnp.float32,
-        )
-        total = term if total is None else total + term
-    out[...] = total.astype(out.dtype)
+    slots = spread.shape[1] // (len(refs) - 1)
+    back = jnp.concatenate([piece[start : start + slots] for piece in refs[:-1]], axis=0)
+    out[...] = dot(spread[...], back).astype(out.dtype)
 
 
 def combine(spread, pieces, start, dtype):
-    tree = spread.shape[1]
+    tree = spread.shape[0]
     width = pieces[0].shape[1]
     return pl.pallas_call(
         functools.partial(combine_kernel, start=start),
@@ -330,6 +420,24 @@
         compiler_params=pltpu.CompilerParams(vmem_limit_bytes=16 * 2**20),
         name="combine",
     )(spread, *pieces)
+
+
+def final_kernel(live, resid, shared, routed, *refs):
+    total = resid[...].astype(jnp.float32) + shared[...] + routed[...]
+    for part in refs[:-1]:
+        total = total + part[...].astype(jnp.float32)
+    refs[-1][...] = jnp.where(live[...] == 1, total, 0.0).astype(jnp.bfloat16)
+
+
+def final(live, resid, shared, routed, parts):
+    return pl.pallas_call(
+        final_kernel,
+        in_specs=[in_vmem()] * (4 + len(parts)),
+        out_specs=in_vmem(),
+        out_shape=jax.ShapeDtypeStruct(resid.shape, jnp.bfloat16),
+        compiler_params=pltpu.CompilerParams(vmem_limit_bytes=16 * 2**20),
+        name="final",
+    )(live, resid, shared, routed, *parts)
 
 
 def body(
@@ -377,8 +485,8 @@
     gate_turned, up_turned = shared_gate.T, shared_up.T
     early, _ = lax.optimization_barrier(((w_out, gate_turned), near_core[0]))
     early = [partner(weight, "c", 1) for weight in early]
-    late, _ = lax.optimization_barrier(
-        ((up_turned, shared_down, expert_in[0], expert_out[0]), near_core[side - 1])
+    late, near_core = lax.optimization_barrier(
+        ((up_turned, shared_down, expert_in[0], expert_out[0]), near_core)
     )
     late = [partner(weight, "c", 1) for weight in late]
 
@@ -402,24 +510,15 @@
             reach,
             cache[:, 0],
         )
-        follow = mixed_own
         fresh[o] = jnp.stack([fresh_own, fresh_other])
         other = partner(mixed_other, "c", 1)
         terms[o] = dot(mixed_own, w_out) + dot(other, early[0])
         if o:
             terms[o] = terms[o].astype(jnp.bfloat16)
-            terms[o], early, late[0], late[1] = lax.optimization_barrier(
-                (terms[o], early, late[0], late[1])
-            )
-    own_routes, _ = lax.optimization_barrier((routes[0], terms[side - 1]))
-    attn = terms[0]
-    for o in range(1, side):
-        attn = attn + partner(terms[o], "x", o).astype(jnp.float32)
-    resid = (own_rows.astype(jnp.float32) + attn).astype(jnp.bfloat16)
-    normed = rms_norm(resid, ffn_gain)
-    line = lax.axis_size("z")
-    chosen = [partner(own_routes, "z", k) for k in range(line)]
-    normed, chosen, late = lax.optimization_barrier((normed, chosen, late))
+        follow = terms[o]
+    others = [partner(terms[o], "x", o) for o in range(1, side)]
+    own_term, late, early = lax.optimization_barrier((terms[0], late, early))
+    resid, normed, payload = finish(own_rows, own_term, others, ffn_gain[None], routes[0])
     inner = [expert_in[0], late[2]]
     outer = [expert_out[0], late[3]]
     shared_weights = [gate_turned, up_turned, shared_down, early[1], late[0], late[1]]
@@ -436,74 +535,44 @@
     top_count = routes.shape[2]
     capacity = 4 * tree * top_count // (3 * expert_count)
     plane = lax.axis_size(PLANE)
-    spot = lax.axis_index(PLANE)
-    first = lax.axis_index("z") * plane
-    choose = jnp.stack(chosen)
-    member = jnp.any(
-        choose[..., None] == jnp.arange(expert_count, dtype=jnp.int32), axis=2
+    line = lax.axis_size("z")
+    near_experts = lax.axis_index("z") * plane + (
+        lax.axis_index(PLANE) ^ jnp.arange(plane, dtype=jnp.int32)
     )
-    before = jnp.tril(jnp.ones((tree, tree), jnp.bfloat16), -1)
-    ranks = jnp.einsum(
-        "nm,kme->kne", before, member.astype(jnp.bfloat16), preferred_element_type=jnp.float32
-    ).astype(jnp.int32)
-    near_experts = first + (spot ^ jnp.arange(plane, dtype=jnp.int32))
-    is_near = near_experts[:, None] == jnp.arange(expert_count, dtype=jnp.int32)
-    slot = jnp.where(member, ranks, -1)
-    slot_near = jnp.sum(
-        jnp.where(is_near[:, None, None, :], slot[None] + 1, 0), axis=-1
-    ) - 1
-    places = jnp.arange(capacity, dtype=jnp.int32)
-    pick = slot_near[:, :, None, :] == places[:, None]
-    pick_bf = pick.astype(jnp.bfloat16)
-
-    line_rows = [normed] + [partner(normed, "z", k) for k in range(1, line)]
+    line_rows = [payload] + [partner(payload, "z", k) for k in range(1, line)]
     beside = [partner(normed, "x", o) for o in range(1, side)]
 
-    own_part, beside_part = shared_terms(normed, beside, shared_weights)
-
-    line_rows[1], beside_part = lax.optimization_barrier((line_rows[1], beside_part))
-
-    logits = jnp.stack([dot(rows, router) for rows in line_rows])
-    picked = jnp.where(member, jax.nn.sigmoid(logits), 0.0)
-    gates = picked / jnp.sum(picked, axis=-1, keepdims=True)
-    gates_near = jnp.sum(jnp.where(is_near[:, None, None, :], gates[None], 0.0), axis=-1)
-    spread = jnp.where(pick, gates_near[:, :, None, :], 0.0)
-    spread = spread.astype(jnp.bfloat16)
-
-    def dispatch(ks):
-        out = [
-            dot(pick_bf[:, k].reshape(plane * capacity, tree), line_rows[k])
-            .astype(jnp.bfloat16)
-            .reshape(plane, capacity, width)
-            for k in ks
-        ]
-        return [
-            partner(jnp.concatenate([piece[o] for piece in out], axis=0), PLANE, o)
-            for o in range(plane)
-        ]
-
-    sent = [dispatch(ks) for ks in GROUPS]
+    shared, beside = shared_terms(normed, beside, shared_weights)
+    line_rows[1], beside = lax.optimization_barrier((line_rows[1], beside))
+
+    sent = []
+    spread = {}
+    for ks in GROUPS:
+        pieces, spreads = select(
+            near_experts, router, [line_rows[k] for k in ks], plane, capacity, top_count
+        )
+        spread.update(zip(ks, spreads))
+        sent.append([partner(pieces[o], PLANE, o) for o in range(plane)])
     made = []
     for pieces in sent:
         if made:
             pieces, made[-1] = lax.optimization_barrier((pieces, made[-1]))
         made.append(experts(pieces, inner, outer))
 
-    shared = own_part
-    for o in range(1, side):
-        shared = shared + partner(beside_part[o - 1], "x", o).astype(jnp.float32)
-    routed = 0.0
+    parts = [partner(beside[o - 1], "x", o) for o in range(1, side)]
+    routed = None
+    follow = None
     for ks, pieces in reversed(list(zip(GROUPS, made))):
+        if len(ks) > 1:
+            pieces, follow = lax.optimization_barrier((pieces, follow))
         back = [partner(pieces[o], PLANE, o) for o in range(plane)]
-        for i, k in enumerate(ks):
-            weights = spread[:, k].reshape(plane * capacity, tree)
-            partial = combine(
-                weights, back, i * capacity, jnp.bfloat16 if k else jnp.float32
-            )
-            routed = routed + partner(partial, "z", k).astype(jnp.float32)
-
-    total_out = resid.astype(jnp.float32) + shared + routed
-    hidden_out = jnp.where(live[0][:, None] == 1, total_out, 0.0).astype(jnp.bfloat16)
+        for i, k in reversed(list(enumerate(ks))):
+            if k:
+                follow = combine(spread[k], back, i * capacity, jnp.bfloat16)
+                parts.append(partner(follow, "z", k))
+            else:
+                routed = combine(spread[k], back, i * capacity, jnp.float32)
+    hidden_out = final(live[0][:, None], resid, shared, routed, parts)
     return (hidden_out[None], accepted_kv)
 
 

time: 160 us -> 161 us (level)
  Pallas kernels: 34.4 us -> 44.5 us
  starting transfers between devices: 44.3 us -> 38.1 us
  local copies, waits for them, and re-layouts: 16.8 us -> 11.9 us
  waiting for transfers between devices: 44.7 us -> 48.7 us
  other arithmetic: 7.17 us -> 3.62 us
  matrix products: 9.77 us -> 11.9 us
    pallas_call x0 -> x5, Pallas kernels: none -> 6.76 us  [the longest x3 4.49 us: select(): pl.pallas_call(functools.partial(select_kernel, count=count, plane=plane,...]
    ppermute x41 -> x38, starting transfers between devices: 44.3 us -> 38.1 us  [partner(): return lax.ppermute(value, axes, [(i, i ^ offset) for i in range(size)])]
    unnamed x65 -> x52, local copies, waits for them, and re-layouts: 14.9 us -> 10 us
    pallas_call x2, Pallas kernels: 9.83 us -> 14.3 us  [attend(): pl.pallas_call(attend_kernel, in_specs=[pl.BlockSpec(memory_space=pltpu.S...]
    ppermute x41 -> x38, waiting for transfers between devices: 44.7 us -> 48.7 us  [partner(): return lax.ppermute(value, axes, [(i, i ^ offset) for i in range(size)])]
    broadcast_in_dim x1 -> x0, other arithmetic: 2.12 us -> none  [body(): return (hidden_out[None], accepted_kv)]
    dot_general x12 -> x4, matrix products: 7.39 us -> 8.4 us  [dot(): return jnp.dot(left, right, preferred_element_type=jnp.float32)]
  transfers between devices with their start and end apart: 41 -> 38, of which waited for: 17 -> 11; matrix products, arithmetic and copies ran while one was open for 11% -> 11% of each run, Pallas kernels for 19% -> 26%
where the time goes in v4:
time: 161 us; the launch traced here: 160 us
  waiting for transfers between devices  48.7 us (30%)
  Pallas kernels  44.5 us (28%)
  starting transfers between devices  38.1 us (24%)
  local copies, waits for them, and re-layouts  11.9 us (7%)
  matrix products  11.9 us (7%)
  other arithmetic  3.62 us (2%)
    ppermute x38, waiting for transfers between devices, partner(): return lax.ppermute(value, axes, [(i, i ^ offset) for i in range(size)])  48.7 us
    ppermute x38, starting transfers between devices, partner(): return lax.ppermute(value, axes, [(i, i ^ offset) for i in range(size)])  38.1 us
    pallas_call x3, Pallas kernels, experts(): pl.pallas_call(kernel, in_specs=[in_vmem()] * plane + [in_hbm()] * 4, out...  17.2 us
    pallas_call x2, Pallas kernels, attend(): pl.pallas_call(attend_kernel, in_specs=[pl.BlockSpec(memory_space=pltpu.S...  14.3 us
    unnamed x52, local copies, waits for them, and re-layouts  10 us
    dot_general x4, matrix products, dot(): return jnp.dot(left, right, preferred_element_type=jnp.float32)  8.4 us
    pallas_call x1, Pallas kernels, shared_terms(): pl.pallas_call(functools.partial(shared_kernel, side=side), in_specs=[in_...  5.43 us
    pallas_call x3, Pallas kernels, select(): pl.pallas_call(functools.partial(select_kernel, count=count, plane=plane,...  4.49 us
  transfers between devices with their start and end apart: 38, of which 11 were waited for; matrix products, arithmetic and copies ran while one was open for 11% of the time, Pallas kernels for 26%

profile of v4, /device:TPU:0, one launch (start us, length us, event | category | flops | bytes accessed | tf_op | source)
XLA Modules:
  0.0 159.8 jit_solution(16850457708578751716)
XLA Ops:
  0.6 3.0 %collective-permute-start.1 = (bf16[64,2048]{1,0:T(8,128)(2,1)}, bf16[64,2048]{1,0:T(8,128)(2,1)S(1)}, u32[]{:S(2)}, u32[]{:S(2)}) collective-permute-start(bf16[64,2048]{1,0:T(8,128)(2,1)} %bitcast.46), channel_id=1, source_target_pairs={{0,2},{2,0},{1,3},{3,1},{4,6},{6,4},{5,7},{7,5},{8,10},{10,8},{9,1... | collective-permute-start | bytes 786440 | tf_op jit(solution)/shard_map/ppermute | solution.py:26
  8.3 1.8 %collective-permute-done.1.first = bf16[64,2048]{1,0:T(8,128)(2,1)S(1)} collective-permute-done((bf16[64,2048]{1,0:T(8,128)(2,1)}, bf16[64,2048]{1,0:T(8,128)(2,1)S(1)}, u32[]{:S(2)}, u32[]{:S(2)}) %collective-permute-start.1) | collective-permute-done | bytes 262176 | tf_op jit(solution)/shard_map/ppermute | solution.py:26
  10.2 1.5 collective-permute-done.2.second
  14.6 6.3 %attend.2 = (bf16[64,512]{1,0:T(8,128)(2,1)}, bf16[64,512]{1,0:T(8,128)(2,1)}, bf16[64,256]{1,0:T(8,128)(2,1)}, bf16[64,256]{1,0:T(8,128)(2,1)}) custom-call(s32[4]{0:T(128)} %get-tuple-element.178.info, bf16[64,2048]{1,0:T(8,128)(2,1)} %copy-done.16, bf16[64,2048]{1,0:T(8,128)(2,1)} %copy-done.17, f32[1,2048]{1,0:T(1,128)} %bitcast.55, ...), custom_call_target="tpu_custom_call" | custom-call | tf_op jit(solution)/shard_map/attend/pallas_call | solution.py:160
  21.3 8.4 %collective-permute-done.3 = bf16[64,512]{1,0:T(8,128)(2,1)S(1)} collective-permute-done((bf16[64,512]{1,0:T(8,128)(2,1)}, bf16[64,512]{1,0:T(8,128)(2,1)S(1)}, u32[]{:S(2)}, u32[]{:S(2)}) %collective-permute-start.3) | collective-permute-done | bytes 65568 | tf_op jit(solution)/shard_map/ppermute | solution.py:26
  30.4 2.1 %fusion.31 = f32[64,2048]{1,0:T(8,128)S(1)} fusion(bf16[64,512]{1,0:T(8,128)(2,1)} %get-tuple-element.90, bf16[512,2048]{1,0:T(8,128)(2,1)} %param.26), kind=kOutput, calls=%fused_computation.59 | convolution fusion | flops 134217728 | bytes 2686976 | tf_op jit(solution)/shard_map/dot_general | solution.py:30
  32.5 2.1 %fusion = bf16[64,2048]{1,0:T(8,128)(2,1)S(1)} fusion(f32[64,2048]{1,0:T(8,128)S(1)} %fusion.31, bf16[64,512]{1,0:T(8,128)(2,1)S(1)} %collective-permute-done.3, bf16[512,2048]{1,0:T(8,128)(2,1)} %collective-permute-done.4), kind=kOutput, calls=%fused_computation.4 | convolution fusion | flops 134479872 | bytes 2949120 | tf_op jit(solution)/shard_map/dot_general | solution.py:30
  34.6 8.0 %attend.3 = (bf16[64,512]{1,0:T(8,128)(2,1)}, bf16[64,512]{1,0:T(8,128)(2,1)}, bf16[64,256]{1,0:T(8,128)(2,1)}, bf16[64,256]{1,0:T(8,128)(2,1)}) custom-call(s32[4]{0:T(128)} %get-tuple-element.177.info, bf16[64,2048]{1,0:T(8,128)(2,1)} %bitcast.48, bf16[64,2048]{1,0:T(8,128)(2,1)} %copy-done.15, f32[1,2048]{1,0:T(1,128)} %bitcast.56, ...), custom_call_target="tpu_custom_call" | custom-call | tf_op jit(solution)/shard_map/attend/pallas_call | solution.py:160
  42.8 2.1 %fusion.32 = f32[64,2048]{1,0:T(8,128)S(1)} fusion(bf16[64,512]{1,0:T(8,128)(2,1)} %get-tuple-element.94, bf16[512,2048]{1,0:T(8,128)(2,1)} %param.26), kind=kOutput, calls=%fused_computation.60 | convolution fusion | flops 134217728 | bytes 2686976 | tf_op jit(solution)/shard_map/dot_general | solution.py:30
  45.3 2.1 %convolution_add_fusion.term = f32[64,2048]{1,0:T(8,128)S(1)} fusion(f32[64,2048]{1,0:T(8,128)S(1)} %fusion.32, bf16[64,512]{1,0:T(8,128)(2,1)S(1)} %collective-permute-done.5, bf16[512,2048]{1,0:T(8,128)(2,1)} %collective-permute-done.4), kind=kOutput, calls=%fused_computation.2 | convolution fusion | flops 134348800 | bytes 3211264 | tf_op jit(solution)/shard_map/dot_general | solution.py:30
  47.5 1.6 %copy-done.2 = bf16[704,2048]{1,0:T(8,128)(2,1)} copy-done((bf16[704,2048]{1,0:T(8,128)(2,1)}, bf16[704,2048]{1,0:T(8,128)(2,1)S(1)}, u32[]{:S(2)}) %copy-start.2) | copy-done | bytes 2883608
  49.1 4.5 %collective-permute-done.11.refs_0_ = bf16[64,2048]{1,0:T(8,128)(2,1)S(1)} collective-permute-done((bf16[64,2048]{1,0:T(8,128)(2,1)S(1)}, bf16[64,2048]{1,0:T(8,128)(2,1)S(1)}, u32[]{:S(2)}, u32[]{:S(2)}) %collective-permute-start.11) | collective-permute-done | bytes 262176 | tf_op jit(solution)/shard_map/ppermute | solution.py:26
  55.1 1.7 %collective-permute-start.12 = (bf16[64,2048]{1,0:T(8,128)(2,1)S(1)}, bf16[64,2048]{1,0:T(8,128)(2,1)S(1)}, u32[]{:S(2)}, u32[]{:S(2)}) collective-permute-start(bf16[64,2048]{1,0:T(8,128)(2,1)S(1)} %get-tuple-element.103.refs_0_), channel_id=1, source_target_pairs={{0,2},{2,0},{1,3},{3,1},{4,6},{6,4},{5,7},{7,5},{8,10},{10,8},{9,1... | collective-permute-start | bytes 786440 | tf_op jit(solution)/shard_map/ppermute | solution.py:26
  56.9 3.0 %collective-permute-start.14 = (bf16[64,2176]{1,0:T(8,128)(2,1)S(1)}, bf16[64,2176]{1,0:T(8,128)(2,1)S(1)}, u32[]{:S(2)}, u32[]{:S(2)}) collective-permute-start(bf16[64,2176]{1,0:T(8,128)(2,1)S(1)} %get-tuple-element.108.refs_2_), channel_id=1, source_target_pairs={{0,24},{8,16},{16,8},{24,0},{1,25},{9,17},{17,9},{25,1},{2,26},{10... | collective-permute-start | bytes 835592 | tf_op jit(solution)/shard_map/ppermute | solution.py:26
  60.8 2.1 %collective-permute-done.12.refs_1_ = bf16[64,2048]{1,0:T(8,128)(2,1)S(1)} collective-permute-done((bf16[64,2048]{1,0:T(8,128)(2,1)S(1)}, bf16[64,2048]{1,0:T(8,128)(2,1)S(1)}, u32[]{:S(2)}, u32[]{:S(2)}) %collective-permute-start.12) | collective-permute-done | bytes 262176 | tf_op jit(solution)/shard_map/ppermute | solution.py:26
  69.6 5.4 %shared.1 = (f32[64,2048]{1,0:T(8,128)S(1)}, bf16[64,2048]{1,0:T(8,128)(2,1)}) custom-call(bf16[64,2048]{1,0:T(8,128)(2,1)S(1)} %copy-done.9, bf16[64,2048]{1,0:T(8,128)(2,1)S(1)} %copy-done.11, bf16[352,2048]{1,0:T(8,128)(2,1)S(1)} %bitcast.43, bf16[352,2048]{1,0:T(8,128)(2,1)S(1)} %bitcast.45, bf16[352,2048]{1,0:T(8,128)(2,1)S(1)} %copy-done.6, ...), custom_call_target="tpu_custom_call" | custom-call | tf_op jit(solution)/shard_map/shared/pallas_call | solution.py:286
  75.1 2.1 %select.3 = (bf16[64,2048]{1,0:T(8,128)(2,1)S(1)}, bf16[64,2048]{1,0:T(8,128)(2,1)S(1)}, bf16[64,2048]{1,0:T(8,128)(2,1)S(1)}, bf16[64,2048]{1,0:T(8,128)(2,1)S(...) custom-call(s32[4]{0:T(128)S(1)} %xor_add_fusion.refs_0_, bf16[2048,16]{1,0:T(8,128)(2,1)S(1)} %copy.30.refs_1_, ...), custom_call_target="tpu_custom_call" | custom-call | tf_op jit(solution)/shard_map/select/pallas_call | solution.py:391
  77.2 1.5 collective-permute-start.18
  81.9 1.5 collective-permute-start.15
  85.0 7.7 %collective-permute-done.15.refs_1_ = bf16[32,2048]{1,0:T(8,128)(2,1)S(1)} collective-permute-done((bf16[32,2048]{1,0:T(8,128)(2,1)S(1)}, bf16[32,2048]{1,0:T(8,128)(2,1)S(1)}, u32[]{:S(2)}, u32[]{:S(2)}) %collective-permute-start.15) | collective-permute-done | bytes 131104 | tf_op jit(solution)/shard_map/ppermute | solution.py:26
  92.6 2.1 %collective-permute-start.17 = (bf16[32,2048]{1,0:T(8,128)(2,1)S(1)}, bf16[32,2048]{1,0:T(8,128)(2,1)S(1)}, u32[]{:S(2)}, u32[]{:S(2)}) collective-permute-start(bf16[32,2048]{1,0:T(8,128)(2,1)S(1)} %get-tuple-element.115), channel_id=1, source_target_pairs={{0,6},{2,4},{4,2},{6,0},{1,7},{3,5},{5,3},{7,1},{8,14},{10,12},{12... | collective-permute-start | bytes 393224 | tf_op jit(solution)/shard_map/ppermute | solution.py:26
  97.4 2.1 %collective-permute-start.24 = (bf16[32,2048]{1,0:T(8,128)(2,1)S(1)}, bf16[32,2048]{1,0:T(8,128)(2,1)S(1)}, u32[]{:S(2)}, u32[]{:S(2)}) collective-permute-start(bf16[32,2048]{1,0:T(8,128)(2,1)S(1)} %get-tuple-element.134), channel_id=1, source_target_pairs={{0,6},{2,4},{4,2},{6,0},{1,7},{3,5},{5,3},{7,1},{8,14},{10,12},{12... | collective-permute-start | bytes 393224 | tf_op jit(solution)/shard_map/ppermute | solution.py:26
  99.5 7.2 %expert.3 = (bf16[64,2048]{1,0:T(8,128)(2,1)S(1)}, bf16[64,2048]{1,0:T(8,128)(2,1)S(1)}, bf16[64,2048]{1,0:T(8,128)(2,1)S(1)}, bf16[64,2048]{1,0:T(8,128)(2,1)S(1)}) custom-call(bf16[64,2048]{1,0:T(8,128)(2,1)S(1)} %get-tuple-element.116.refs_0_, bf16[64,2048]{1,0:T(8,128)(2,1)S(1)} %collective-permute-done.18.refs_1_, ...), custom_call_target="tpu_custom_call" | custom-call | tf_op jit(solution)/shard_map/expert/pallas_call | solution.py:241
  106.7 5.0 %expert.4 = (bf16[32,2048]{1,0:T(8,128)(2,1)S(1)}, bf16[32,2048]{1,0:T(8,128)(2,1)S(1)}, bf16[32,2048]{1,0:T(8,128)(2,1)S(1)}, bf16[32,2048]{1,0:T(8,128)(2,1)S(1)}) custom-call(bf16[32,2048]{1,0:T(8,128)(2,1)S(1)} %get-tuple-element.135.refs_0_, bf16[32,2048]{1,0:T(8,128)(2,1)S(1)} %collective-permute-done.15.refs_1_, ...), custom_call_target="tpu_custom_call" | custom-call | tf_op jit(solution)/shard_map/expert/pallas_call | solution.py:241
  113.2 2.1 %collective-permute-start.27 = (bf16[32,2048]{1,0:T(8,128)(2,1)S(1)}, bf16[32,2048]{1,0:T(8,128)(2,1)S(1)}, u32[]{:S(2)}, u32[]{:S(2)}) collective-permute-start(bf16[32,2048]{1,0:T(8,128)(2,1)S(1)} %get-tuple-element.146), channel_id=1, source_target_pairs={{0,6},{2,4},{4,2},{6,0},{1,7},{3,5},{5,3},{7,1},{8,14},{10,12},{12... | collective-permute-start | bytes 393224 | tf_op jit(solution)/shard_map/ppermute | solution.py:26
  115.3 5.0 %expert.5 = (bf16[32,2048]{1,0:T(8,128)(2,1)S(1)}, bf16[32,2048]{1,0:T(8,128)(2,1)S(1)}, bf16[32,2048]{1,0:T(8,128)(2,1)S(1)}, bf16[32,2048]{1,0:T(8,128)(2,1)S(1)}) custom-call(bf16[32,2048]{1,0:T(8,128)(2,1)S(1)} %get-tuple-element.153.refs_0_, bf16[32,2048]{1,0:T(8,128)(2,1)S(1)} %collective-permute-done.22.refs_1_, ...), custom_call_target="tpu_custom_call" | custom-call | tf_op jit(solution)/shard_map/expert/pallas_call | solution.py:241
  123.3 1.8 %collective-permute-start.30 = (bf16[64,2048]{1,0:T(8,128)(2,1)S(1)}, bf16[64,2048]{1,0:T(8,128)(2,1)S(1)}, u32[]{:S(2)}, u32[]{:S(2)}) collective-permute-start(bf16[64,2048]{1,0:T(8,128)(2,1)S(1)} %get-tuple-element.150), channel_id=1, source_target_pairs={{0,6},{2,4},{4,2},{6,0},{1,7},{3,5},{5,3},{7,1},{8,14},{10,12},{12... | collective-permute-start | bytes 786440 | tf_op jit(solution)/shard_map/ppermute | solution.py:26
  127.7 5.8 %collective-permute-done.33.refs_2_ = bf16[32,2048]{1,0:T(8,128)(2,1)S(1)} collective-permute-done((bf16[32,2048]{1,0:T(8,128)(2,1)S(1)}, bf16[32,2048]{1,0:T(8,128)(2,1)S(1)}, u32[]{:S(2)}, u32[]{:S(2)}) %collective-permute-start.33) | collective-permute-done | bytes 131104 | tf_op jit(solution)/shard_map/ppermute | solution.py:26
  135.0 3.8 %collective-permute-done.34.refs_3_ = bf16[32,2048]{1,0:T(8,128)(2,1)S(1)} collective-permute-done((bf16[32,2048]{1,0:T(8,128)(2,1)S(1)}, bf16[32,2048]{1,0:T(8,128)(2,1)S(1)}, u32[]{:S(2)}, u32[]{:S(2)}) %collective-permute-start.34) | collective-permute-done | bytes 131104 | tf_op jit(solution)/shard_map/ppermute | solution.py:26
  138.8 3.4 %collective-permute-start.36 = (bf16[64,2048]{1,0:T(8,128)(2,1)S(1)}, bf16[64,2048]{1,0:T(8,128)(2,1)S(1)}, u32[]{:S(2)}, u32[]{:S(2)}) collective-permute-start(bf16[64,2048]{1,0:T(8,128)(2,1)S(1)} %combine.4), channel_id=1, source_target_pairs={{0,24},{8,16},{16,8},{24,0},{1,25},{9,17},{17,9},{25,1},{2,26},{10... | collective-permute-start | bytes 786440 | tf_op jit(solution)/shard_map/ppermute | solution.py:26
  146.8 10.9 %collective-permute-done.35.refs_1_ = bf16[64,2048]{1,0:T(8,128)(2,1)S(1)} collective-permute-done((bf16[64,2048]{1,0:T(8,128)(2,1)S(1)}, bf16[64,2048]{1,0:T(8,128)(2,1)S(1)}, u32[]{:S(2)}, u32[]{:S(2)}) %collective-permute-start.35) | collective-permute-done | bytes 262176 | tf_op jit(solution)/shard_map/ppermute | solution.py:26
  157.8 2.0 %final.1 = bf16[64,2048]{1,0:T(8,128)(2,1)} custom-call(s32[64,1]{1,0:T(8,128)S(1)} %copy.33.live, bf16[64,2048]{1,0:T(8,128)(2,1)S(1)} %copy-done.13, f32[64,2048]{1,0:T(8,128)S(1)} %get-tuple-element.107.shared, f32[64,2048]{1,0:T(8,128)S(1)} %combine.5.routed, bf16[64,2048]{1,0:T(8,128)(2,1)S(1)} %collective-permute-done.31.refs_0_, ...), custom_call_target="tpu_custom_call" | custom-call | tf_op jit(solution)/shard_map/final/pallas_call | solution.py:433
  (136 shorter events, 38.7 us)
Async XLA Ops:
  0.6 9.5 %collective-permute-start.1 = (bf16[64,2048]{1,0:T(8,128)(2,1)}, bf16[64,2048]{1,0:T(8,128)(2,1)S(1)}, u32[]{:S(2)}, u32[]{:S(2)}) collective-permute-start(bf16[64,2048]{1,0:T(8,128)(2,1)} %bitcast.46), channel_id=1, source_target_pairs={{0,2},{2,0},{1,3},{3,1},{4,6},{6,4},{5,7},{7,5},{8,10},{10,8},{9,1... | collective-permute-start | bytes 786440 | tf_op jit(solution)/shard_map/ppermute | solution.py:26
  11.7 37.4 %collective-permute-start.8 = (bf16[2048,1408]{1,0:T(8,128)(2,1)}, bf16[2048,1408]{1,0:T(8,128)(2,1)}, u32[]{:S(2)}, u32[]{:S(2)}) collective-permute-start(bf16[2048,1408]{1,0:T(8,128)(2,1)} %bitcast.32), channel_id=1, source_target_pairs={{0,1},{1,0},{2,3},{3,2},{4,5},{5,4},{6,7},{7,6},{8,9},{9,8},{10,11... | collective-permute-start | bytes 17301512 | tf_op jit(solution)/shard_map/ppermute | solution.py:26
  12.4 17.5 %collective-permute-start.4 = (bf16[512,2048]{1,0:T(8,128)(2,1)}, bf16[512,2048]{1,0:T(8,128)(2,1)}, u32[]{:S(2)}, u32[]{:S(2)}) collective-permute-start(bf16[512,2048]{1,0:T(8,128)(2,1)} %param.26), channel_id=1, source_target_pairs={{0,1},{1,0},{2,3},{3,2},{4,5},{5,4},{6,7},{7,6},{8,9},{9,8},{10,11... | collective-permute-start | bytes 6291464 | tf_op jit(solution)/shard_map/ppermute | solution.py:26
  12.6 34.9 %collective-permute-start.9 = (bf16[704,2048]{1,0:T(8,128)(2,1)}, bf16[704,2048]{1,0:T(8,128)(2,1)S(1)}, u32[]{:S(2)}, u32[]{:S(2)}) collective-permute-start(bf16[704,2048]{1,0:T(8,128)(2,1)} %bitcast.38), channel_id=1, source_target_pairs={{0,1},{1,0},{2,3},{3,2},{4,5},{5,4},{6,7},{7,6},{8,9},{9,8},{10,11... | collective-permute-start | bytes 8650760 | tf_op jit(solution)/shard_map/ppermute | solution.py:26
  12.9 29.6 %collective-permute-start.10 = (bf16[352,2048]{1,0:T(8,128)(2,1)}, bf16[352,2048]{1,0:T(8,128)(2,1)}, u32[]{:S(2)}, u32[]{:S(2)}) collective-permute-start(bf16[352,2048]{1,0:T(8,128)(2,1)} %bitcast.42), channel_id=1, source_target_pairs={{0,1},{1,0},{2,3},{3,2},{4,5},{5,4},{6,7},{7,6},{8,9},{9,8},{10,11... | collective-permute-start | bytes 4325384 | tf_op jit(solution)/shard_map/ppermute | solution.py:26
  20.9 8.9 %collective-permute-start.3 = (bf16[64,512]{1,0:T(8,128)(2,1)}, bf16[64,512]{1,0:T(8,128)(2,1)S(1)}, u32[]{:S(2)}, u32[]{:S(2)}) collective-permute-start(bf16[64,512]{1,0:T(8,128)(2,1)} %get-tuple-element.91), channel_id=1, source_target_pairs={{0,1},{1,0},{2,3},{3,2},{4,5},{5,4},{6,7},{7,6},{8,9},{9,8},{10,11... | collective-permute-start | bytes 196616 | tf_op jit(solution)/shard_map/ppermute | solution.py:26
  29.8 17.7 %collective-permute-start.6 = (bf16[352,2048]{1,0:T(8,128)(2,1)}, bf16[352,2048]{1,0:T(8,128)(2,1)}, u32[]{:S(2)}, u32[]{:S(2)}) collective-permute-start(bf16[352,2048]{1,0:T(8,128)(2,1)} %bitcast.44), channel_id=1, source_target_pairs={{0,1},{1,0},{2,3},{3,2},{4,5},{5,4},{6,7},{7,6},{8,9},{9,8},{10,11... | collective-permute-start | bytes 4325384 | tf_op jit(solution)/shard_map/ppermute | solution.py:26
  29.9 17.5 %collective-permute-start.7 = (bf16[352,2048]{1,0:T(8,128)(2,1)}, bf16[352,2048]{1,0:T(8,128)(2,1)}, u32[]{:S(2)}, u32[]{:S(2)}) collective-permute-start(bf16[352,2048]{1,0:T(8,128)(2,1)} %refs_4_.1), channel_id=1, source_target_pairs={{0,1},{1,0},{2,3},{3,2},{4,5},{5,4},{6,7},{7,6},{8,9},{9,8},{10,11... | collective-permute-start | bytes 4325384 | tf_op jit(solution)/shard_map/ppermute | solution.py:26
  44.9 8.6 %collective-permute-start.11 = (bf16[64,2048]{1,0:T(8,128)(2,1)S(1)}, bf16[64,2048]{1,0:T(8,128)(2,1)S(1)}, u32[]{:S(2)}, u32[]{:S(2)}) collective-permute-start(bf16[64,2048]{1,0:T(8,128)(2,1)S(1)} %fusion), channel_id=1, source_target_pairs={{0,2},{2,0},{1,3},{3,1},{4,6},{6,4},{5,7},{7,5},{8,10},{10,8},{9,1... | collective-permute-start | bytes 786440 | tf_op jit(solution)/shard_map/ppermute | solution.py:26
  54.5 20.5 %collective-permute-start.13 = (bf16[64,2176]{1,0:T(8,128)(2,1)S(1)}, bf16[64,2176]{1,0:T(8,128)(2,1)}, u32[]{:S(2)}, u32[]{:S(2)}) collective-permute-start(bf16[64,2176]{1,0:T(8,128)(2,1)S(1)} %get-tuple-element.108.refs_2_), channel_id=1, source_target_pairs={{0,8},{8,0},{16,24},{24,16},{1,9},{9,1},{17,25},{25,17},{2,10},{10... | collective-permute-start | bytes 835592 | tf_op jit(solution)/shard_map/ppermute | solution.py:26
  56.9 23.8 %collective-permute-start.14 = (bf16[64,2176]{1,0:T(8,128)(2,1)S(1)}, bf16[64,2176]{1,0:T(8,128)(2,1)S(1)}, u32[]{:S(2)}, u32[]{:S(2)}) collective-permute-start(bf16[64,2176]{1,0:T(8,128)(2,1)S(1)} %get-tuple-element.108.refs_2_), channel_id=1, source_target_pairs={{0,24},{8,16},{16,8},{24,0},{1,25},{9,17},{17,9},{25,1},{2,26},{10... | collective-permute-start | bytes 835592 | tf_op jit(solution)/shard_map/ppermute | solution.py:26
  59.9 24.3 %collective-permute-start.21 = (bf16[64,2176]{1,0:T(8,128)(2,1)S(1)}, bf16[64,2176]{1,0:T(8,128)(2,1)S(1)}, u32[]{:S(2)}, u32[]{:S(2)}) collective-permute-start(bf16[64,2176]{1,0:T(8,128)(2,1)S(1)} %get-tuple-element.108.refs_2_), channel_id=1, source_target_pairs={{0,16},{8,24},{16,0},{24,8},{1,17},{9,25},{17,1},{25,9},{2,18},{10... | collective-permute-start | bytes 835592 | tf_op jit(solution)/shard_map/ppermute | solution.py:26
  77.2 18.8 %collective-permute-start.18 = (bf16[64,2048]{1,0:T(8,128)(2,1)S(1)}, bf16[64,2048]{1,0:T(8,128)(2,1)S(1)}, u32[]{:S(2)}, u32[]{:S(2)}) collective-permute-start(bf16[64,2048]{1,0:T(8,128)(2,1)S(1)} %get-tuple-element.117), channel_id=1, source_target_pairs={{0,2},{2,0},{4,6},{6,4},{1,3},{3,1},{5,7},{7,5},{8,10},{10,8},{12,... | collective-permute-start | bytes 786440 | tf_op jit(solution)/shard_map/ppermute | solution.py:26
  78.7 18.2 %collective-permute-start.19 = (bf16[64,2048]{1,0:T(8,128)(2,1)S(1)}, bf16[64,2048]{1,0:T(8,128)(2,1)S(1)}, u32[]{:S(2)}, u32[]{:S(2)}) collective-permute-start(bf16[64,2048]{1,0:T(8,128)(2,1)S(1)} %get-tuple-element.118), channel_id=1, source_target_pairs={{0,4},{2,6},{4,0},{6,2},{1,5},{3,7},{5,1},{7,3},{8,12},{10,14},{12... | collective-permute-start | bytes 786440 | tf_op jit(solution)/shard_map/ppermute | solution.py:26
  80.2 17.2 %collective-permute-start.20 = (bf16[64,2048]{1,0:T(8,128)(2,1)S(1)}, bf16[64,2048]{1,0:T(8,128)(2,1)S(1)}, u32[]{:S(2)}, u32[]{:S(2)}) collective-permute-start(bf16[64,2048]{1,0:T(8,128)(2,1)S(1)} %get-tuple-element.119), channel_id=1, source_target_pairs={{0,6},{2,4},{4,2},{6,0},{1,7},{3,5},{5,3},{7,1},{8,14},{10,12},{12... | collective-permute-start | bytes 786440 | tf_op jit(solution)/shard_map/ppermute | solution.py:26
  81.9 10.7 %collective-permute-start.15 = (bf16[32,2048]{1,0:T(8,128)(2,1)S(1)}, bf16[32,2048]{1,0:T(8,128)(2,1)S(1)}, u32[]{:S(2)}, u32[]{:S(2)}) collective-permute-start(bf16[32,2048]{1,0:T(8,128)(2,1)S(1)} %get-tuple-element.113), channel_id=1, source_target_pairs={{0,2},{2,0},{4,6},{6,4},{1,3},{3,1},{5,7},{7,5},{8,10},{10,8},{12,... | collective-permute-start | bytes 393224 | tf_op jit(solution)/shard_map/ppermute | solution.py:26
  84.2 22.5 %collective-permute-start.16 = (bf16[32,2048]{1,0:T(8,128)(2,1)S(1)}, bf16[32,2048]{1,0:T(8,128)(2,1)S(1)}, u32[]{:S(2)}, u32[]{:S(2)}) collective-permute-start(bf16[32,2048]{1,0:T(8,128)(2,1)S(1)} %get-tuple-element.114), channel_id=1, source_target_pairs={{0,4},{2,6},{4,0},{6,2},{1,5},{3,7},{5,1},{7,3},{8,12},{10,14},{12... | collective-permute-start | bytes 393224 | tf_op jit(solution)/shard_map/ppermute | solution.py:26
  92.6 14.1 %collective-permute-start.17 = (bf16[32,2048]{1,0:T(8,128)(2,1)S(1)}, bf16[32,2048]{1,0:T(8,128)(2,1)S(1)}, u32[]{:S(2)}, u32[]{:S(2)}) collective-permute-start(bf16[32,2048]{1,0:T(8,128)(2,1)S(1)} %get-tuple-element.115), channel_id=1, source_target_pairs={{0,6},{2,4},{4,2},{6,0},{1,7},{3,5},{5,3},{7,1},{8,14},{10,12},{12... | collective-permute-start | bytes 393224 | tf_op jit(solution)/shard_map/ppermute | solution.py:26
  95.9 15.8 %collective-permute-start.22 = (bf16[32,2048]{1,0:T(8,128)(2,1)S(1)}, bf16[32,2048]{1,0:T(8,128)(2,1)S(1)}, u32[]{:S(2)}, u32[]{:S(2)}) collective-permute-start(bf16[32,2048]{1,0:T(8,128)(2,1)S(1)} %get-tuple-element.132), channel_id=1, source_target_pairs={{0,2},{2,0},{4,6},{6,4},{1,3},{3,1},{5,7},{7,5},{8,10},{10,8},{12,... | collective-permute-start | bytes 393224 | tf_op jit(solution)/shard_map/ppermute | solution.py:26
  96.9 14.9 %collective-permute-start.23 = (bf16[32,2048]{1,0:T(8,128)(2,1)S(1)}, bf16[32,2048]{1,0:T(8,128)(2,1)S(1)}, u32[]{:S(2)}, u32[]{:S(2)}) collective-permute-start(bf16[32,2048]{1,0:T(8,128)(2,1)S(1)} %get-tuple-element.133), channel_id=1, source_target_pairs={{0,4},{2,6},{4,0},{6,2},{1,5},{3,7},{5,1},{7,3},{8,12},{10,14},{12... | collective-permute-start | bytes 393224 | tf_op jit(solution)/shard_map/ppermute | solution.py:26
  97.4 14.3 %collective-permute-start.24 = (bf16[32,2048]{1,0:T(8,128)(2,1)S(1)}, bf16[32,2048]{1,0:T(8,128)(2,1)S(1)}, u32[]{:S(2)}, u32[]{:S(2)}) collective-permute-start(bf16[32,2048]{1,0:T(8,128)(2,1)S(1)} %get-tuple-element.134), channel_id=1, source_target_pairs={{0,6},{2,4},{4,2},{6,0},{1,7},{3,5},{5,3},{7,1},{8,14},{10,12},{12... | collective-permute-start | bytes 393224 | tf_op jit(solution)/shard_map/ppermute | solution.py:26
  111.8 9.6 %collective-permute-start.25 = (bf16[32,2048]{1,0:T(8,128)(2,1)S(1)}, bf16[32,2048]{1,0:T(8,128)(2,1)S(1)}, u32[]{:S(2)}, u32[]{:S(2)}) collective-permute-start(bf16[32,2048]{1,0:T(8,128)(2,1)S(1)} %get-tuple-element.144), channel_id=1, source_target_pairs={{0,2},{2,0},{4,6},{6,4},{1,3},{3,1},{5,7},{7,5},{8,10},{10,8},{12,... | collective-permute-start | bytes 393224 | tf_op jit(solution)/shard_map/ppermute | solution.py:26
  112.7 8.6 %collective-permute-start.26 = (bf16[32,2048]{1,0:T(8,128)(2,1)S(1)}, bf16[32,2048]{1,0:T(8,128)(2,1)S(1)}, u32[]{:S(2)}, u32[]{:S(2)}) collective-permute-start(bf16[32,2048]{1,0:T(8,128)(2,1)S(1)} %get-tuple-element.145), channel_id=1, source_target_pairs={{0,4},{2,6},{4,0},{6,2},{1,5},{3,7},{5,1},{7,3},{8,12},{10,14},{12... | collective-permute-start | bytes 393224 | tf_op jit(solution)/shard_map/ppermute | solution.py:26
  121.6 20.8 %collective-permute-start.28 = (bf16[64,2048]{1,0:T(8,128)(2,1)S(1)}, bf16[64,2048]{1,0:T(8,128)(2,1)S(1)}, u32[]{:S(2)}, u32[]{:S(2)}) collective-permute-start(bf16[64,2048]{1,0:T(8,128)(2,1)S(1)} %get-tuple-element.148), channel_id=1, source_target_pairs={{0,2},{2,0},{4,6},{6,4},{1,3},{3,1},{5,7},{7,5},{8,10},{10,8},{12,... | collective-permute-start | bytes 786440 | tf_op jit(solution)/shard_map/ppermute | solution.py:26
  122.8 19.9 %collective-permute-start.29 = (bf16[64,2048]{1,0:T(8,128)(2,1)S(1)}, bf16[64,2048]{1,0:T(8,128)(2,1)S(1)}, u32[]{:S(2)}, u32[]{:S(2)}) collective-permute-start(bf16[64,2048]{1,0:T(8,128)(2,1)S(1)} %get-tuple-element.149), channel_id=1, source_target_pairs={{0,4},{2,6},{4,0},{6,2},{1,5},{3,7},{5,1},{7,3},{8,12},{10,14},{12... | collective-permute-start | bytes 786440 | tf_op jit(solution)/shard_map/ppermute | solution.py:26
  123.3 19.4 %collective-permute-start.30 = (bf16[64,2048]{1,0:T(8,128)(2,1)S(1)}, bf16[64,2048]{1,0:T(8,128)(2,1)S(1)}, u32[]{:S(2)}, u32[]{:S(2)}) collective-permute-start(bf16[64,2048]{1,0:T(8,128)(2,1)S(1)} %get-tuple-element.150), channel_id=1, source_target_pairs={{0,6},{2,4},{4,2},{6,0},{1,7},{3,5},{5,3},{7,1},{8,14},{10,12},{12... | collective-permute-start | bytes 786440 | tf_op jit(solution)/shard_map/ppermute | solution.py:26
  125.1 8.4 %collective-permute-start.33 = (bf16[32,2048]{1,0:T(8,128)(2,1)S(1)}, bf16[32,2048]{1,0:T(8,128)(2,1)S(1)}, u32[]{:S(2)}, u32[]{:S(2)}) collective-permute-start(bf16[32,2048]{1,0:T(8,128)(2,1)S(1)} %get-tuple-element.159), channel_id=1, source_target_pairs={{0,4},{2,6},{4,0},{6,2},{1,5},{3,7},{5,1},{7,3},{8,12},{10,14},{12... | collective-permute-start | bytes 393224 | tf_op jit(solution)/shard_map/ppermute | solution.py:26
  126.9 11.9 %collective-permute-start.34 = (bf16[32,2048]{1,0:T(8,128)(2,1)S(1)}, bf16[32,2048]{1,0:T(8,128)(2,1)S(1)}, u32[]{:S(2)}, u32[]{:S(2)}) collective-permute-start(bf16[32,2048]{1,0:T(8,128)(2,1)S(1)} %get-tuple-element.160), channel_id=1, source_target_pairs={{0,6},{2,4},{4,2},{6,0},{1,7},{3,5},{5,3},{7,1},{8,14},{10,12},{12... | collective-permute-start | bytes 393224 | tf_op jit(solution)/shard_map/ppermute | solution.py:26
  133.6 13.2 %collective-permute-start.31 = (bf16[64,2048]{1,0:T(8,128)(2,1)}, bf16[64,2048]{1,0:T(8,128)(2,1)S(1)}, u32[]{:S(2)}, u32[]{:S(2)}) collective-permute-start(bf16[64,2048]{1,0:T(8,128)(2,1)} %get-tuple-element.151), channel_id=1, source_target_pairs={{0,2},{2,0},{1,3},{3,1},{4,6},{6,4},{5,7},{7,5},{8,10},{10,8},{9,1... | collective-permute-start | bytes 786440 | tf_op jit(solution)/shard_map/ppermute | solution.py:26
  138.8 19.0 %collective-permute-start.36 = (bf16[64,2048]{1,0:T(8,128)(2,1)S(1)}, bf16[64,2048]{1,0:T(8,128)(2,1)S(1)}, u32[]{:S(2)}, u32[]{:S(2)}) collective-permute-start(bf16[64,2048]{1,0:T(8,128)(2,1)S(1)} %combine.4), channel_id=1, source_target_pairs={{0,24},{8,16},{16,8},{24,0},{1,25},{9,17},{17,9},{25,1},{2,26},{10... | collective-permute-start | bytes 786440 | tf_op jit(solution)/shard_map/ppermute | solution.py:26
  142.4 15.3 %collective-permute-start.35 = (bf16[64,2048]{1,0:T(8,128)(2,1)S(1)}, bf16[64,2048]{1,0:T(8,128)(2,1)S(1)}, u32[]{:S(2)}, u32[]{:S(2)}) collective-permute-start(bf16[64,2048]{1,0:T(8,128)(2,1)S(1)} %combine.6), channel_id=1, source_target_pairs={{0,16},{8,24},{16,0},{24,8},{1,17},{9,25},{17,1},{25,9},{2,18},{10... | collective-permute-start | bytes 786440 | tf_op jit(solution)/shard_map/ppermute | solution.py:26
  142.9 14.9 %collective-permute-start.37 = (bf16[64,2048]{1,0:T(8,128)(2,1)S(1)}, bf16[64,2048]{1,0:T(8,128)(2,1)}, u32[]{:S(2)}, u32[]{:S(2)}) collective-permute-start(bf16[64,2048]{1,0:T(8,128)(2,1)S(1)} %combine.7), channel_id=1, source_target_pairs={{0,8},{8,0},{16,24},{24,16},{1,9},{9,1},{17,25},{25,17},{2,10},{10... | collective-permute-start | bytes 786440 | tf_op jit(solution)/shard_map/ppermute | solution.py:26
  (31 other events, 480.5 us)

commit v5 on v4

--- a/solution.py
+++ b/solution.py
@@ -11,9 +11,11 @@
 
 EPSILON = 1e-06
 ROPE_BASE = 10000.0
-GROUPS = ((0, 1), (3,), (2,))
+GROUPS = ((0, 1), (3, 2))
+BACK = ((1, None), (3, None), (2, 3), (0, 2))
 CHUNK = 512
 EXTRA = 128
+SMALL = pl.CostEstimate(flops=1024, bytes_accessed=1024, transcendentals=0)
 ALL = ("z", "y", "x", "c")
 PLANE = ("y", "x")
 HEAD = ("x", "c")
@@ -51,11 +53,11 @@
 
 
 def attend_kernel(
-    info, first, second, gain, weight, cosine, sine, reach, cache, *outs_and_scratch
+    info, first, second, gain, weight, cosine, sine, reach, cache, outward, *outs_and_scratch
 ):
-    mixed = outs_and_scratch[0:2]
+    term, mixed = outs_and_scratch[0:2]
     fresh = outs_and_scratch[2:4]
-    weight_here, cache_here, gain_here, sems = outs_and_scratch[4:]
+    weight_here, cache_here, gain_here, outward_here, sems = outs_and_scratch[4:]
     tree = first.shape[0]
     width, columns = weight.shape
     head_dim = cosine.shape[2]
@@ -73,7 +75,8 @@
         pltpu.make_async_copy(cache.at[info[i]], cache_here.at[i], sems.at[3 + i])
         for i in range(2)
     ]
-    for copy in [gain_copy, *weight_copies, *cache_copies]:
+    outward_copy = pltpu.make_async_copy(outward, outward_here, sems.at[5])
+    for copy in [gain_copy, *weight_copies, *cache_copies, outward_copy]:
         copy.start()
 
     wide = jnp.concatenate([first[...], second[...]], axis=0).astype(jnp.float32)
@@ -139,8 +142,15 @@
             0, lax.div(length + CHUNK - 1, CHUNK), chunk, (peak, total, summed)
         )
         result = (summed / total).astype(jnp.bfloat16)
-        for h in range(group):
-            mixed[i][:, h * head_dim : (h + 1) * head_dim] = result[h * tree : (h + 1) * tree]
+        result = jnp.concatenate(
+            [result[h * tree : (h + 1) * tree] for h in range(group)], axis=1
+        )
+        if i:
+            mixed[...] = result
+        else:
+            kept = result
+    outward_copy.wait()
+    term[...] = dot(kept, outward_here[...])
 
 
 def in_vmem():
@@ -151,7 +161,7 @@
     return pl.BlockSpec(memory_space=pltpu.HBM)
 
 
-def attend(info, first, second, gain, weight, cosine, sine, reach, cache):
+def attend(info, first, second, gain, weight, cosine, sine, reach, cache, outward):
     tree, width = first.shape
     slots, pair = cache.shape[1:]
     head_dim = pair // 2
@@ -169,30 +179,67 @@
             in_vmem(),
             in_vmem(),
             in_hbm(),
+            in_hbm(),
         ],
         out_specs=[in_vmem()] * 4,
-        out_shape=[jax.ShapeDtypeStruct((tree, group_columns), jnp.bfloat16)] * 2
+        out_shape=[
+            jax.ShapeDtypeStruct((tree, width), jnp.float32),
+            jax.ShapeDtypeStruct((tree, group_columns), jnp.bfloat16),
+        ]
         + [jax.ShapeDtypeStruct((tree, pair), jnp.bfloat16)] * 2,
         scratch_shapes=[
             pltpu.VMEM((width, columns), jnp.bfloat16),
             pltpu.VMEM((2, slots, pair), jnp.bfloat16),
             pltpu.VMEM((1, width), jnp.float32),
-            pltpu.SemaphoreType.DMA((5,)),
+            pltpu.VMEM((group_columns, width), jnp.bfloat16),
+            pltpu.SemaphoreType.DMA((6,)),
         ],
         compiler_params=pltpu.CompilerParams(vmem_limit_bytes=60 * 2**20),
+        cost_estimate=SMALL,
         name="attend",
-    )(info, first, second, gain, weight, cosine, sine, reach, cache)
+    )(info, first, second, gain, weight, cosine, sine, reach, cache, outward)
+
+
+def project_kernel(term, mixed, outward, out, here, sems):
+    half = here.shape[0] // 2
+    copies = [
+        pltpu.make_async_copy(
+            outward.at[pl.ds(i * half, half)], here.at[pl.ds(i * half, half)], sems.at[i]
+        )
+        for i in range(2)
+    ]
+    for copy in copies:
+        copy.start()
+    total = term[...]
+    for i, copy in enumerate(copies):
+        copy.wait()
+        block = slice(i * half, (i + 1) * half)
+        total = total + dot(mixed[:, block], here[block])
+    out[...] = total.astype(out.dtype)
+
+
+def project(term, mixed, outward, dtype):
+    return pl.pallas_call(
+        project_kernel,
+        in_specs=[in_vmem(), in_vmem(), in_hbm()],
+        out_specs=in_vmem(),
+        out_shape=jax.ShapeDtypeStruct(term.shape, dtype),
+        scratch_shapes=[pltpu.VMEM(outward.shape, jnp.bfloat16), pltpu.SemaphoreType.DMA((2,))],
+        compiler_params=pltpu.CompilerParams(vmem_limit_bytes=60 * 2**20),
+        cost_estimate=SMALL,
+        name="project",
+    )(term, mixed, outward)
 
 
 def silu(values):
     return values / (1.0 + jnp.exp(-values))
 
 
-def expert_kernel(*refs, plane, deep):
+def expert_kernel(*refs, plane, count, deep):
     pieces = refs[:plane]
     weights = refs[plane : plane + 4]
-    outs = refs[plane + 4 : 2 * plane + 4]
-    rows, inner_a, outer_a, inner_b, outer_b, sems = refs[2 * plane + 4 :]
+    outs = refs[plane + 4 : plane + 4 + count * plane]
+    rows, inner_a, outer_a, inner_b, outer_b, sems = refs[plane + 4 + count * plane :]
     each = pieces[0].shape[0]
     width = rows.shape[1]
     parts = width // deep
@@ -224,31 +271,35 @@
         copies[base + parts].wait()
         term = dot(hidden, outer_here[...]).astype(jnp.bfloat16).astype(jnp.float32)
         result = term if result is None else result + term
-    for i in range(plane):
-        outs[i][...] = result[i * each : (i + 1) * each].astype(jnp.bfloat16)
-
-
-def experts(pieces, inner, outer):
+    step = each // count
+    for n in range(count * plane):
+        base = (n % plane) * each + (n // plane) * step
+        outs[n][...] = result[base : base + step].astype(jnp.bfloat16)
+
+
+def experts(pieces, count, inner, outer):
     plane = len(pieces)
     each, width = pieces[0].shape
     hidden = inner[0].shape[1]
     deep = width // 2
-    kernel = functools.partial(expert_kernel, plane=plane, deep=deep)
+    kernel = functools.partial(expert_kernel, plane=plane, count=count, deep=deep)
     weight_scratch = [
         pltpu.VMEM((width, hidden), jnp.bfloat16),
         pltpu.VMEM((hidden // 2, width), jnp.bfloat16),
     ]
-    return pl.pallas_call(
+    made = pl.pallas_call(
         kernel,
         in_specs=[in_vmem()] * plane + [in_hbm()] * 4,
-        out_specs=[in_vmem()] * plane,
-        out_shape=[jax.ShapeDtypeStruct((each, width), jnp.bfloat16)] * plane,
+        out_specs=[in_vmem()] * (count * plane),
+        out_shape=[jax.ShapeDtypeStruct((each // count, width), jnp.bfloat16)] * (count * plane),
         scratch_shapes=[pltpu.VMEM((plane * each, width), jnp.bfloat16)]
         + weight_scratch * 2
         + [pltpu.SemaphoreType.DMA((2 * (width // deep + 1),))],
-        compiler_params=pltpu.CompilerParams(vmem_limit_bytes=40 * 2**20),
+        compiler_params=pltpu.CompilerParams(vmem_limit_bytes=60 * 2**20),
+        cost_estimate=SMALL,
         name="expert",
     )(*pieces, inner[0], outer[0], inner[1], outer[1])
+    return [list(made[i * plane : (i + 1) * plane]) for i in range(count)]
 
 
 def shared_kernel(*refs, side):
@@ -293,7 +344,8 @@
             pltpu.VMEM((6, units, width), jnp.bfloat16),
             pltpu.SemaphoreType.DMA((6,)),
         ],
-        compiler_params=pltpu.CompilerParams(vmem_limit_bytes=24 * 2**20),
+        compiler_params=pltpu.CompilerParams(vmem_limit_bytes=60 * 2**20),
+        cost_estimate=SMALL,
         name="shared",
     )(own, *beside, *weights)
     return outs[0], list(outs[1:])
@@ -333,6 +385,7 @@
             jax.ShapeDtypeStruct((tree, width + EXTRA), jnp.bfloat16),
         ],
         compiler_params=pltpu.CompilerParams(vmem_limit_bytes=16 * 2**20),
+        cost_estimate=SMALL,
         name="finish",
     )(tokens, term, gain, routes, *others)
 
@@ -397,27 +450,28 @@
         out_shape=[jax.ShapeDtypeStruct((count * capacity, width), jnp.bfloat16)] * plane
         + [jax.ShapeDtypeStruct((tree, plane * capacity), jnp.bfloat16)] * count,
         compiler_params=pltpu.CompilerParams(vmem_limit_bytes=16 * 2**20),
+        cost_estimate=SMALL,
         name="select",
     )(near, router, *sources)
     return list(made[:plane]), list(made[plane:])
 
 
-def combine_kernel(spread, *refs, start):
+def combine_kernel(spread, *refs):
     out = refs[-1]
-    slots = spread.shape[1] // (len(refs) - 1)
-    back = jnp.concatenate([piece[start : start + slots] for piece in refs[:-1]], axis=0)
+    back = jnp.concatenate([piece[...] for piece in refs[:-1]], axis=0)
     out[...] = dot(spread[...], back).astype(out.dtype)
 
 
-def combine(spread, pieces, start, dtype):
+def combine(spread, pieces, dtype):
     tree = spread.shape[0]
     width = pieces[0].shape[1]
     return pl.pallas_call(
-        functools.partial(combine_kernel, start=start),
+        combine_kernel,
         in_specs=[in_vmem()] * (1 + len(pieces)),
         out_specs=in_vmem(),
         out_shape=jax.ShapeDtypeStruct((tree, width), dtype),
         compiler_params=pltpu.CompilerParams(vmem_limit_bytes=16 * 2**20),
+        cost_estimate=SMALL,
         name="combine",
     )(spread, *pieces)
 
@@ -436,6 +490,7 @@
         out_specs=in_vmem(),
         out_shape=jax.ShapeDtypeStruct(resid.shape, jnp.bfloat16),
         compiler_params=pltpu.CompilerParams(vmem_limit_bytes=16 * 2**20),
+        cost_estimate=SMALL,
         name="final",
     )(live, resid, shared, routed, *parts)
 
@@ -478,29 +533,35 @@
     sine = jnp.sin(angle)
     cosine = jnp.concatenate([cosine, cosine], axis=-1)
     sine = jnp.concatenate([-sine, sine], axis=-1)
+    info = []
+    for o in range(side):
+        ids = me ^ jnp.arange(2 * o, 2 * o + 2, dtype=jnp.int32)
+        here = ids[:, None] == jnp.arange(group_count, dtype=jnp.int32)
+        info.append(jnp.concatenate([ids, jnp.sum(jnp.where(here, lengths, 0), axis=1)]))
     for o in range(1, side):
-        near[o], cosine, sine, reach = lax.optimization_barrier((near[o], cosine, sine, reach))
+        near[o], cosine, sine, reach, info = lax.optimization_barrier(
+            (near[o], cosine, sine, reach, info)
+        )
         near_core.append(partner(near[o], "c", 1))
 
     gate_turned, up_turned = shared_gate.T, shared_up.T
-    early, _ = lax.optimization_barrier(((w_out, gate_turned), near_core[0]))
+    early, near_core[0] = lax.optimization_barrier(((w_out, expert_out[0]), near_core[0]))
     early = [partner(weight, "c", 1) for weight in early]
-    late, near_core = lax.optimization_barrier(
-        ((up_turned, shared_down, expert_in[0], expert_out[0]), near_core)
+    middle, near_core = lax.optimization_barrier(
+        ((gate_turned, up_turned, shared_down), near_core)
     )
-    late = [partner(weight, "c", 1) for weight in late]
+    middle = [partner(weight, "c", 1) for weight in middle]
+    near_core, early = lax.optimization_barrier((near_core, early))
 
     terms = [None] * side
     fresh = [None] * side
     follow = None
+    late = expert_in[0]
     for o in reversed(range(side)):
         if follow is not None:
-            near_core[o], _ = lax.optimization_barrier((near_core[o], follow))
-        ids = me ^ jnp.arange(2 * o, 2 * o + 2, dtype=jnp.int32)
-        here = ids[:, None] == jnp.arange(group_count, dtype=jnp.int32)
-        info = jnp.concatenate([ids, jnp.sum(jnp.where(here, lengths, 0), axis=1)])
-        mixed_own, mixed_other, fresh_own, fresh_other = attend(
-            info,
+            near_core[o], follow = lax.optimization_barrier((near_core[o], follow))
+        own_part, mixed, fresh_own, fresh_other = attend(
+            info[o],
             near[o],
             near_core[o],
             attn_gain[None],
@@ -509,19 +570,21 @@
             sine,
             reach,
             cache[:, 0],
+            w_out,
         )
         fresh[o] = jnp.stack([fresh_own, fresh_other])
-        other = partner(mixed_other, "c", 1)
-        terms[o] = dot(mixed_own, w_out) + dot(other, early[0])
-        if o:
-            terms[o] = terms[o].astype(jnp.bfloat16)
+        other = partner(mixed, "c", 1)
+        if o == side - 1:
+            other, middle, late = lax.optimization_barrier((other, middle, late))
+            late = partner(late, "c", 1)
+        terms[o] = project(own_part, other, early[0], jnp.bfloat16 if o else jnp.float32)
         follow = terms[o]
     others = [partner(terms[o], "x", o) for o in range(1, side)]
-    own_term, late, early = lax.optimization_barrier((terms[0], late, early))
+    own_term, late = lax.optimization_barrier((terms[0], late))
     resid, normed, payload = finish(own_rows, own_term, others, ffn_gain[None], routes[0])
-    inner = [expert_in[0], late[2]]
-    outer = [expert_out[0], late[3]]
-    shared_weights = [gate_turned, up_turned, shared_down, early[1], late[0], late[1]]
+    inner = [expert_in[0], late]
+    outer = [expert_out[0], early[1]]
+    shared_weights = [gate_turned, up_turned, shared_down, *middle]
     order = me ^ jnp.arange(group_count, dtype=jnp.int32)
     kept = accepted[order][:, :, None] == jnp.arange(tree, dtype=jnp.int32)
     accepted_kv = jnp.einsum(
@@ -553,25 +616,23 @@
         )
         spread.update(zip(ks, spreads))
         sent.append([partner(pieces[o], PLANE, o) for o in range(plane)])
-    made = []
-    for pieces in sent:
-        if made:
-            pieces, made[-1] = lax.optimization_barrier((pieces, made[-1]))
-        made.append(experts(pieces, inner, outer))
-
     parts = [partner(beside[o - 1], "x", o) for o in range(1, side)]
-    routed = None
-    follow = None
-    for ks, pieces in reversed(list(zip(GROUPS, made))):
-        if len(ks) > 1:
-            pieces, follow = lax.optimization_barrier((pieces, follow))
+    made = None
+    results = {}
+    for ks, pieces in zip(GROUPS, sent):
+        if made is not None:
+            pieces, made = lax.optimization_barrier((pieces, made))
+        made = experts(pieces, len(ks), inner, outer)
+        results.update(zip(ks, made))
+    totals = {}
+    for k, after in BACK:
+        pieces = results[k]
+        if after is not None:
+            pieces, totals[after] = lax.optimization_barrier((pieces, totals[after]))
         back = [partner(pieces[o], PLANE, o) for o in range(plane)]
-        for i, k in reversed(list(enumerate(ks))):
-            if k:
-                follow = combine(spread[k], back, i * capacity, jnp.bfloat16)
-                parts.append(partner(follow, "z", k))
-            else:
-                routed = combine(spread[k], back, i * capacity, jnp.float32)
+        totals[k] = combine(spread[k], back, jnp.bfloat16 if k else jnp.float32)
+    parts += [partner(totals[k], "z", k) for k, after in BACK if k]
+    routed = totals[0]
     hidden_out = final(live[0][:, None], resid, shared, routed, parts)
     return (hidden_out[None], accepted_kv)
 

time: 161 us -> 158 us (0.981)
  waiting for transfers between devices: 48.7 us -> 34.8 us
  Pallas kernels: 44.5 us -> 58.4 us
  matrix products: 11.9 us -> 3.5 us
  starting transfers between devices: 38.1 us -> 44.5 us
    ppermute x38, waiting for transfers between devices: 48.7 us -> 34.8 us  [partner(): return lax.ppermute(value, axes, [(i, i ^ offset) for i in range(size)])]
    dot_general x4 -> x0, matrix products: 8.4 us -> none  [dot(): return jnp.dot(left, right, preferred_element_type=jnp.float32)]
    pallas_call x4 -> x6, Pallas kernels: 0.85 us -> 8.17 us  [the longest x2 7.33 us: project(): pl.pallas_call(project_kernel, in_specs=[in_vmem(), in_vmem(), in_hbm()],...]
    ppermute x38, starting transfers between devices: 38.1 us -> 44.5 us  [partner(): return lax.ppermute(value, axes, [(i, i ^ offset) for i in range(size)])]
    pallas_call x3 -> x2, Pallas kernels: 17.2 us -> 22.3 us  [experts(): pl.pallas_call(kernel, in_specs=[in_vmem()] * plane + [in_hbm()] * 4, out...]
    pallas_call x2, Pallas kernels: 14.3 us -> 16.3 us  [attend(): pl.pallas_call(attend_kernel, in_specs=[pl.BlockSpec(memory_space=pltpu.S...]
    unnamed x52 -> x74, local copies, waits for them, and re-layouts: 10 us -> 8.8 us
    pallas_call x3 -> x2, Pallas kernels: 4.49 us -> 3.33 us  [select(): pl.pallas_call(functools.partial(select_kernel, count=count, plane=plane,...]
  transfers between devices with their start and end apart: 38 -> 38, of which waited for: 11 -> 14; matrix products, arithmetic and copies ran while one was open for 11% -> 6% of each run, Pallas kernels for 26% -> 29%
where the time goes in v5:
time: 158 us; the launch traced here: 157 us
  Pallas kernels  58.4 us (37%)
  starting transfers between devices  44.5 us (28%)
  waiting for transfers between devices  34.8 us (22%)
  local copies, waits for them, and re-layouts  10.6 us (7%)
  other arithmetic  4.23 us (3%)
  matrix products  3.5 us (2%)
    ppermute x38, starting transfers between devices, partner(): return lax.ppermute(value, axes, [(i, i ^ offset) for i in range(size)])  44.5 us
    ppermute x38, waiting for transfers between devices, partner(): return lax.ppermute(value, axes, [(i, i ^ offset) for i in range(size)])  34.8 us
    pallas_call x2, Pallas kernels, experts(): pl.pallas_call(kernel, in_specs=[in_vmem()] * plane + [in_hbm()] * 4, out...  22.3 us
    pallas_call x2, Pallas kernels, attend(): pl.pallas_call(attend_kernel, in_specs=[pl.BlockSpec(memory_space=pltpu.S...  16.3 us
    unnamed x74, local copies, waits for them, and re-layouts  8.8 us
    pallas_call x2, Pallas kernels, project(): pl.pallas_call(project_kernel, in_specs=[in_vmem(), in_vmem(), in_hbm()],...  7.33 us
    pallas_call x1, Pallas kernels, shared_terms(): pl.pallas_call(functools.partial(shared_kernel, side=side), in_specs=[in_...  7.01 us
    pallas_call x2, Pallas kernels, select(): pl.pallas_call(functools.partial(select_kernel, count=count, plane=plane,...  3.33 us
  transfers between devices with their start and end apart: 38, of which 14 were waited for; matrix products, arithmetic and copies ran while one was open for 6% of the time, Pallas kernels for 29%

profile of v5, /device:TPU:0, one launch (start us, length us, event | category | flops | bytes accessed | tf_op | source)
XLA Modules:
  0.0 157.2 jit_solution(14614213336599219957)
XLA Ops:
  0.6 3.0 %collective-permute-start = (bf16[64,2048]{1,0:T(8,128)(2,1)}, bf16[64,2048]{1,0:T(8,128)(2,1)}, u32[]{:S(2)}, u32[]{:S(2)}) collective-permute-start(bf16[64,2048]{1,0:T(8,128)(2,1)} %bitcast.24), channel_id=1, source_target_pairs={{0,2},{2,0},{1,3},{3,1},{4,6},{6,4},{5,7},{7,5},{8,10},{10,8},{9,1... | collective-permute-start | bytes 786440 | tf_op jit(solution)/shard_map/ppermute | solution.py:28
  11.6 3.4 %collective-permute-done.2.second = bf16[64,2048]{1,0:T(8,128)(2,1)S(1)} collective-permute-done((bf16[64,2048]{1,0:T(8,128)(2,1)}, bf16[64,2048]{1,0:T(8,128)(2,1)S(1)}, u32[]{:S(2)}, u32[]{:S(2)}) %collective-permute-start.2) | collective-permute-done | bytes 262176 | tf_op jit(solution)/shard_map/ppermute | solution.py:28
  17.2 7.7 %attend.2 = (f32[64,2048]{1,0:T(8,128)}, bf16[64,512]{1,0:T(8,128)(2,1)}, bf16[64,256]{1,0:T(8,128)(2,1)}, bf16[64,256]{1,0:T(8,128)(2,1)}) custom-call(s32[4]{0:T(128)} %pad_add_fusion.1.info, bf16[64,2048]{1,0:T(8,128)(2,1)} %collective-permute-done.first, bf16[64,2048]{1,0:T(8,128)(2,1)} %copy-done.22, f32[1,2048]{1,0:T(1,128)} %bitcast.43, ...), custom_call_target="tpu_custom_call" | custom-call | flops 1024 | bytes 1024 | tf_op jit(solution)/shard_map/attend/pallas_call | solution.py:170
  25.2 1.3 collective-permute-done.5.mixed
  27.1 3.6 %project.2 = bf16[64,2048]{1,0:T(8,128)(2,1)} custom-call(f32[64,2048]{1,0:T(8,128)} %get-tuple-element.98.term, bf16[64,512]{1,0:T(8,128)(2,1)} %copy-done.24, bf16[512,2048]{1,0:T(8,128)(2,1)} %copy-done.13), custom_call_target="tpu_custom_call" | custom-call | flops 1024 | bytes 1024 | tf_op jit(solution)/shard_map/project/pallas_call | solution.py:222
  30.7 1.6 %collective-permute-start.11 = (bf16[64,2048]{1,0:T(8,128)(2,1)}, bf16[64,2048]{1,0:T(8,128)(2,1)S(1)}, u32[]{:S(2)}, u32[]{:S(2)}) collective-permute-start(bf16[64,2048]{1,0:T(8,128)(2,1)} %project.2), channel_id=1, source_target_pairs={{0,2},{2,0},{1,3},{3,1},{4,6},{6,4},{5,7},{7,5},{8,10},{10,8},{9,1... | collective-permute-start | bytes 786440 | tf_op jit(solution)/shard_map/ppermute | solution.py:28
  32.3 8.6 %attend.3 = (f32[64,2048]{1,0:T(8,128)}, bf16[64,512]{1,0:T(8,128)(2,1)}, bf16[64,256]{1,0:T(8,128)(2,1)}, bf16[64,256]{1,0:T(8,128)(2,1)}) custom-call(s32[4]{0:T(128)} %pad_add_fusion.info, bf16[64,2048]{1,0:T(8,128)(2,1)} %bitcast.26, bf16[64,2048]{1,0:T(8,128)(2,1)} %copy-done.20, f32[1,2048]{1,0:T(1,128)} %bitcast.44, bf16[2048,768]{1,0:T(8,128)(2,1)} %weight.3, ...), custom_call_target="tpu_custom_call" | custom-call | flops 1024 | bytes 1024 | tf_op jit(solution)/shard_map/attend/pallas_call | solution.py:170
  41.2 1.3 collective-permute-done.9.mixed
  43.1 3.7 %project.3.term = f32[64,2048]{1,0:T(8,128)} custom-call(f32[64,2048]{1,0:T(8,128)} %get-tuple-element.106.term, bf16[64,512]{1,0:T(8,128)(2,1)} %copy-done.25, bf16[512,2048]{1,0:T(8,128)(2,1)} %copy-done.13), custom_call_target="tpu_custom_call" | custom-call | flops 1024 | bytes 1024 | tf_op jit(solution)/shard_map/project/pallas_call | solution.py:222
  49.3 3.5 %collective-permute-start.12 = (bf16[64,2048]{1,0:T(8,128)(2,1)S(1)}, bf16[64,2048]{1,0:T(8,128)(2,1)S(1)}, u32[]{:S(2)}, u32[]{:S(2)}) collective-permute-start(bf16[64,2048]{1,0:T(8,128)(2,1)S(1)} %get-tuple-element.111.refs_0_), channel_id=1, source_target_pairs={{0,2},{2,0},{1,3},{3,1},{4,6},{6,4},{5,7},{7,5},{8,10},{10,8},{9,1... | collective-permute-start | bytes 786440 | tf_op jit(solution)/shard_map/ppermute | solution.py:28
  52.8 1.5 collective-permute-start.18
  54.6 4.5 %collective-permute-done.12.refs_1_ = bf16[64,2048]{1,0:T(8,128)(2,1)S(1)} collective-permute-done((bf16[64,2048]{1,0:T(8,128)(2,1)S(1)}, bf16[64,2048]{1,0:T(8,128)(2,1)S(1)}, u32[]{:S(2)}, u32[]{:S(2)}) %collective-permute-start.12) | collective-permute-done | bytes 262176 | tf_op jit(solution)/shard_map/ppermute | solution.py:28
  59.8 7.0 %shared.1 = (f32[64,2048]{1,0:T(8,128)}, bf16[64,2048]{1,0:T(8,128)(2,1)}) custom-call(bf16[64,2048]{1,0:T(8,128)(2,1)} %copy-done.6, bf16[64,2048]{1,0:T(8,128)(2,1)} %copy-done.21, bf16[352,2048]{1,0:T(8,128)(2,1)} %bitcast.39, bf16[352,2048]{1,0:T(8,128)(2,1)} %bitcast.41, bf16[352,2048]{1,0:T(8,128)(2,1)} %refs_4_.1, ...), custom_call_target="tpu_custom_call" | custom-call | flops 1024 | bytes 1024 | tf_op jit(solution)/shard_map/shared/pallas_call | solution.py:337
  66.9 1.7 %select.2 = (bf16[64,2048]{1,0:T(8,128)(2,1)S(1)}, bf16[64,2048]{1,0:T(8,128)(2,1)S(1)}, bf16[64,2048]{1,0:T(8,128)(2,1)S(1)}, bf16[64,2048]{1,0:T(8,128)(2,1)S(...) custom-call(s32[4]{0:T(128)S(1)} %xor_add_fusion.refs_0_, bf16[2048,16]{1,0:T(8,128)(2,1)S(1)} %copy.29.refs_1_, ...), custom_call_target="tpu_custom_call" | custom-call | flops 1024 | bytes 1024 | tf_op jit(solution)/shard_map/select/pallas_call | solution.py:444
  69.2 1.7 %collective-permute-start.14 = (bf16[64,2048]{1,0:T(8,128)(2,1)S(1)}, bf16[64,2048]{1,0:T(8,128)(2,1)S(1)}, u32[]{:S(2)}, u32[]{:S(2)}) collective-permute-start(bf16[64,2048]{1,0:T(8,128)(2,1)S(1)} %get-tuple-element.121), channel_id=1, source_target_pairs={{0,2},{2,0},{4,6},{6,4},{1,3},{3,1},{5,7},{7,5},{8,10},{10,8},{12,... | collective-permute-start | bytes 786440 | tf_op jit(solution)/shard_map/ppermute | solution.py:28
  71.0 1.7 %collective-permute-start.16 = (bf16[64,2048]{1,0:T(8,128)(2,1)S(1)}, bf16[64,2048]{1,0:T(8,128)(2,1)S(1)}, u32[]{:S(2)}, u32[]{:S(2)}) collective-permute-start(bf16[64,2048]{1,0:T(8,128)(2,1)S(1)} %get-tuple-element.123), channel_id=1, source_target_pairs={{0,6},{2,4},{4,2},{6,0},{1,7},{3,5},{5,3},{7,1},{8,14},{10,12},{12... | collective-permute-start | bytes 786440 | tf_op jit(solution)/shard_map/ppermute | solution.py:28
  72.7 5.9 %collective-permute-done.18.refs_3_ = bf16[64,2176]{1,0:T(8,128)(2,1)S(1)} collective-permute-done((bf16[64,2176]{1,0:T(8,128)(2,1)S(1)}, bf16[64,2176]{1,0:T(8,128)(2,1)S(1)}, u32[]{:S(2)}, u32[]{:S(2)}) %collective-permute-start.18) | collective-permute-done | bytes 278560 | tf_op jit(solution)/shard_map/ppermute | solution.py:28
  78.6 1.7 %select.3 = (bf16[64,2048]{1,0:T(8,128)(2,1)S(1)}, bf16[64,2048]{1,0:T(8,128)(2,1)S(1)}, bf16[64,2048]{1,0:T(8,128)(2,1)S(1)}, bf16[64,2048]{1,0:T(8,128)(2,1)S(...) custom-call(s32[4]{0:T(128)S(1)} %xor_add_fusion.refs_0_, bf16[2048,16]{1,0:T(8,128)(2,1)S(1)} %copy.29.refs_1_, ...), custom_call_target="tpu_custom_call" | custom-call | flops 1024 | bytes 1024 | tf_op jit(solution)/shard_map/select/pallas_call | solution.py:444
  81.0 3.2 %collective-permute-start.20 = (bf16[64,2048]{1,0:T(8,128)(2,1)S(1)}, bf16[64,2048]{1,0:T(8,128)(2,1)S(1)}, u32[]{:S(2)}, u32[]{:S(2)}) collective-permute-start(bf16[64,2048]{1,0:T(8,128)(2,1)S(1)} %get-tuple-element.133), channel_id=1, source_target_pairs={{0,4},{2,6},{4,0},{6,2},{1,5},{3,7},{5,1},{7,3},{8,12},{10,14},{12... | collective-permute-start | bytes 786440 | tf_op jit(solution)/shard_map/ppermute | solution.py:28
  86.2 10.9 %expert.2 = (bf16[32,2048]{1,0:T(8,128)(2,1)}, bf16[32,2048]{1,0:T(8,128)(2,1)}, bf16[32,2048]{1,0:T(8,128)(2,1)}, bf16[32,2048]{1,0:T(8,128)(2,1)}, bf16[32,204...) custom-call(bf16[64,2048]{1,0:T(8,128)(2,1)} %copy-done.5, ...), custom_call_target="tpu_custom_call" | custom-call | flops 1024 | bytes 1024 | tf_op jit(solution)/shard_map/expert/pallas_call | solution.py:290
  98.2 11.3 %expert.3 = (bf16[32,2048]{1,0:T(8,128)(2,1)}, bf16[32,2048]{1,0:T(8,128)(2,1)}, bf16[32,2048]{1,0:T(8,128)(2,1)}, bf16[32,2048]{1,0:T(8,128)(2,1)}, bf16[32,204...) custom-call(bf16[64,2048]{1,0:T(8,128)(2,1)} %copy-done.4, ...), custom_call_target="tpu_custom_call" | custom-call | flops 1024 | bytes 1024 | tf_op jit(solution)/shard_map/expert/pallas_call | solution.py:290
  110.2 1.6 %collective-permute-start.23 = (bf16[32,2048]{1,0:T(8,128)(2,1)}, bf16[32,2048]{1,0:T(8,128)(2,1)S(1)}, u32[]{:S(2)}, u32[]{:S(2)}) collective-permute-start(bf16[32,2048]{1,0:T(8,128)(2,1)} %get-tuple-element.150), channel_id=1, source_target_pairs={{0,4},{2,6},{4,0},{6,2},{1,5},{3,7},{5,1},{7,3},{8,12},{10,14},{12... | collective-permute-start | bytes 393224 | tf_op jit(solution)/shard_map/ppermute | solution.py:28
  113.1 2.2 %collective-permute-done.22.refs_1_ = bf16[32,2048]{1,0:T(8,128)(2,1)S(1)} collective-permute-done((bf16[32,2048]{1,0:T(8,128)(2,1)}, bf16[32,2048]{1,0:T(8,128)(2,1)S(1)}, u32[]{:S(2)}, u32[]{:S(2)}) %collective-permute-start.22) | collective-permute-done | bytes 131104 | tf_op jit(solution)/shard_map/ppermute | solution.py:28
  116.3 1.6 %collective-permute-done.24.refs_3_ = bf16[32,2048]{1,0:T(8,128)(2,1)S(1)} collective-permute-done((bf16[32,2048]{1,0:T(8,128)(2,1)}, bf16[32,2048]{1,0:T(8,128)(2,1)S(1)}, u32[]{:S(2)}, u32[]{:S(2)}) %collective-permute-start.24) | collective-permute-done | bytes 131104 | tf_op jit(solution)/shard_map/ppermute | solution.py:28
  119.0 1.8 %collective-permute-start.25 = (bf16[32,2048]{1,0:T(8,128)(2,1)}, bf16[32,2048]{1,0:T(8,128)(2,1)S(1)}, u32[]{:S(2)}, u32[]{:S(2)}) collective-permute-start(bf16[32,2048]{1,0:T(8,128)(2,1)} %get-tuple-element.153), channel_id=1, source_target_pairs={{0,2},{2,0},{4,6},{6,4},{1,3},{3,1},{5,7},{7,5},{8,10},{10,8},{12,... | collective-permute-start | bytes 393224 | tf_op jit(solution)/shard_map/ppermute | solution.py:28
  122.6 1.7 %collective-permute-start.32 = (bf16[32,2048]{1,0:T(8,128)(2,1)S(1)}, bf16[32,2048]{1,0:T(8,128)(2,1)S(1)}, u32[]{:S(2)}, u32[]{:S(2)}) collective-permute-start(bf16[32,2048]{1,0:T(8,128)(2,1)S(1)} %copy-done.33), channel_id=1, source_target_pairs={{0,2},{2,0},{4,6},{6,4},{1,3},{3,1},{5,7},{7,5},{8,10},{10,8},{12,... | collective-permute-start | bytes 393224 | tf_op jit(solution)/shard_map/ppermute | solution.py:28
  125.6 1.9 %collective-permute-start.34 = (bf16[32,2048]{1,0:T(8,128)(2,1)S(1)}, bf16[32,2048]{1,0:T(8,128)(2,1)S(1)}, u32[]{:S(2)}, u32[]{:S(2)}) collective-permute-start(bf16[32,2048]{1,0:T(8,128)(2,1)S(1)} %copy-done.31), channel_id=1, source_target_pairs={{0,6},{2,4},{4,2},{6,0},{1,7},{3,5},{5,3},{7,1},{8,14},{10,12},{12... | collective-permute-start | bytes 393224 | tf_op jit(solution)/shard_map/ppermute | solution.py:28
  127.6 2.3 %collective-permute-done.26.refs_2_ = bf16[32,2048]{1,0:T(8,128)(2,1)S(1)} collective-permute-done((bf16[32,2048]{1,0:T(8,128)(2,1)}, bf16[32,2048]{1,0:T(8,128)(2,1)S(1)}, u32[]{:S(2)}, u32[]{:S(2)}) %collective-permute-start.26) | collective-permute-done | bytes 131104 | tf_op jit(solution)/shard_map/ppermute | solution.py:28
  131.2 1.8 %collective-permute-start.29 = (bf16[32,2048]{1,0:T(8,128)(2,1)S(1)}, bf16[32,2048]{1,0:T(8,128)(2,1)S(1)}, u32[]{:S(2)}, u32[]{:S(2)}) collective-permute-start(bf16[32,2048]{1,0:T(8,128)(2,1)S(1)} %copy-done.29), channel_id=1, source_target_pairs={{0,4},{2,6},{4,0},{6,2},{1,5},{3,7},{5,1},{7,3},{8,12},{10,14},{12... | collective-permute-start | bytes 393224 | tf_op jit(solution)/shard_map/ppermute | solution.py:28
  135.0 5.4 %collective-permute-start.36 = (bf16[64,2048]{1,0:T(8,128)(2,1)S(1)}, bf16[64,2048]{1,0:T(8,128)(2,1)S(1)}, u32[]{:S(2)}, u32[]{:S(2)}) collective-permute-start(bf16[64,2048]{1,0:T(8,128)(2,1)S(1)} %combine.4), channel_id=1, source_target_pairs={{0,24},{8,16},{16,8},{24,0},{1,25},{9,17},{17,9},{25,1},{2,26},{10... | collective-permute-start | bytes 786440 | tf_op jit(solution)/shard_map/ppermute | solution.py:28
  141.1 2.9 %collective-permute-start.30 = (bf16[32,2048]{1,0:T(8,128)(2,1)}, bf16[32,2048]{1,0:T(8,128)(2,1)S(1)}, u32[]{:S(2)}, u32[]{:S(2)}) collective-permute-start(bf16[32,2048]{1,0:T(8,128)(2,1)} %get-tuple-element.159), channel_id=1, source_target_pairs={{0,6},{2,4},{4,2},{6,0},{1,7},{3,5},{5,3},{7,1},{8,14},{10,12},{12... | collective-permute-start | bytes 393224 | tf_op jit(solution)/shard_map/ppermute | solution.py:28
  147.6 8.5 %collective-permute-done.37.refs_3_ = bf16[64,2048]{1,0:T(8,128)(2,1)S(1)} collective-permute-done((bf16[64,2048]{1,0:T(8,128)(2,1)S(1)}, bf16[64,2048]{1,0:T(8,128)(2,1)S(1)}, u32[]{:S(2)}, u32[]{:S(2)}) %collective-permute-start.37) | collective-permute-done | bytes 262176 | tf_op jit(solution)/shard_map/ppermute | solution.py:28
  (153 shorter events, 35.2 us)
Async XLA Ops:
  0.6 10.5 %collective-permute-start = (bf16[64,2048]{1,0:T(8,128)(2,1)}, bf16[64,2048]{1,0:T(8,128)(2,1)}, u32[]{:S(2)}, u32[]{:S(2)}) collective-permute-start(bf16[64,2048]{1,0:T(8,128)(2,1)} %bitcast.24), channel_id=1, source_target_pairs={{0,2},{2,0},{1,3},{3,1},{4,6},{6,4},{5,7},{7,5},{8,10},{10,8},{9,1... | collective-permute-start | bytes 786440 | tf_op jit(solution)/shard_map/ppermute | solution.py:28
  6.0 10.0 %collective-permute-start.4 = (bf16[704,2048]{1,0:T(8,128)(2,1)}, bf16[704,2048]{1,0:T(8,128)(2,1)S(1)}, u32[]{:S(2)}, u32[]{:S(2)}) collective-permute-start(bf16[704,2048]{1,0:T(8,128)(2,1)} %bitcast.35), channel_id=1, source_target_pairs={{0,1},{1,0},{2,3},{3,2},{4,5},{5,4},{6,7},{7,6},{8,9},{9,8},{10,11... | collective-permute-start | bytes 8650760 | tf_op jit(solution)/shard_map/ppermute | solution.py:28
  8.1 7.8 %collective-permute-start.3 = (bf16[512,2048]{1,0:T(8,128)(2,1)}, bf16[512,2048]{1,0:T(8,128)(2,1)S(1)}, u32[]{:S(2)}, u32[]{:S(2)}) collective-permute-start(bf16[512,2048]{1,0:T(8,128)(2,1)} %outward.3), channel_id=1, source_target_pairs={{0,1},{1,0},{2,3},{3,2},{4,5},{5,4},{6,7},{7,6},{8,9},{9,8},{10,11... | collective-permute-start | bytes 6291464 | tf_op jit(solution)/shard_map/ppermute | solution.py:28
  15.0 10.1 %collective-permute-start.6 = (bf16[352,2048]{1,0:T(8,128)(2,1)}, bf16[352,2048]{1,0:T(8,128)(2,1)}, u32[]{:S(2)}, u32[]{:S(2)}) collective-permute-start(bf16[352,2048]{1,0:T(8,128)(2,1)} %bitcast.38), channel_id=1, source_target_pairs={{0,1},{1,0},{2,3},{3,2},{4,5},{5,4},{6,7},{7,6},{8,9},{9,8},{10,11... | collective-permute-start | bytes 4325384 | tf_op jit(solution)/shard_map/ppermute | solution.py:28
  15.4 9.8 %collective-permute-start.7 = (bf16[352,2048]{1,0:T(8,128)(2,1)}, bf16[352,2048]{1,0:T(8,128)(2,1)}, u32[]{:S(2)}, u32[]{:S(2)}) collective-permute-start(bf16[352,2048]{1,0:T(8,128)(2,1)} %bitcast.40), channel_id=1, source_target_pairs={{0,1},{1,0},{2,3},{3,2},{4,5},{5,4},{6,7},{7,6},{8,9},{9,8},{10,11... | collective-permute-start | bytes 4325384 | tf_op jit(solution)/shard_map/ppermute | solution.py:28
  15.5 9.6 %collective-permute-start.8 = (bf16[352,2048]{1,0:T(8,128)(2,1)}, bf16[352,2048]{1,0:T(8,128)(2,1)}, u32[]{:S(2)}, u32[]{:S(2)}) collective-permute-start(bf16[352,2048]{1,0:T(8,128)(2,1)} %refs_4_.1), channel_id=1, source_target_pairs={{0,1},{1,0},{2,3},{3,2},{4,5},{5,4},{6,7},{7,6},{8,9},{9,8},{10,11... | collective-permute-start | bytes 4325384 | tf_op jit(solution)/shard_map/ppermute | solution.py:28
  26.5 20.4 %collective-permute-start.10 = (bf16[2048,1408]{1,0:T(8,128)(2,1)}, bf16[2048,1408]{1,0:T(8,128)(2,1)}, u32[]{:S(2)}, u32[]{:S(2)}) collective-permute-start(bf16[2048,1408]{1,0:T(8,128)(2,1)} %bitcast.30), channel_id=1, source_target_pairs={{0,1},{1,0},{2,3},{3,2},{4,5},{5,4},{6,7},{7,6},{8,9},{9,8},{10,11... | collective-permute-start | bytes 17301512 | tf_op jit(solution)/shard_map/ppermute | solution.py:28
  30.7 16.2 %collective-permute-start.11 = (bf16[64,2048]{1,0:T(8,128)(2,1)}, bf16[64,2048]{1,0:T(8,128)(2,1)S(1)}, u32[]{:S(2)}, u32[]{:S(2)}) collective-permute-start(bf16[64,2048]{1,0:T(8,128)(2,1)} %project.2), channel_id=1, source_target_pairs={{0,2},{2,0},{1,3},{3,1},{4,6},{6,4},{5,7},{7,5},{8,10},{10,8},{9,1... | collective-permute-start | bytes 786440 | tf_op jit(solution)/shard_map/ppermute | solution.py:28
  48.2 18.7 %collective-permute-start.13 = (bf16[64,2176]{1,0:T(8,128)(2,1)S(1)}, bf16[64,2176]{1,0:T(8,128)(2,1)S(1)}, u32[]{:S(2)}, u32[]{:S(2)}) collective-permute-start(bf16[64,2176]{1,0:T(8,128)(2,1)S(1)} %get-tuple-element.116.refs_2_), channel_id=1, source_target_pairs={{0,8},{8,0},{16,24},{24,16},{1,9},{9,1},{17,25},{25,17},{2,10},{10... | collective-permute-start | bytes 835592 | tf_op jit(solution)/shard_map/ppermute | solution.py:28
  49.3 9.8 %collective-permute-start.12 = (bf16[64,2048]{1,0:T(8,128)(2,1)S(1)}, bf16[64,2048]{1,0:T(8,128)(2,1)S(1)}, u32[]{:S(2)}, u32[]{:S(2)}) collective-permute-start(bf16[64,2048]{1,0:T(8,128)(2,1)S(1)} %get-tuple-element.111.refs_0_), channel_id=1, source_target_pairs={{0,2},{2,0},{1,3},{3,1},{4,6},{6,4},{5,7},{7,5},{8,10},{10,8},{9,1... | collective-permute-start | bytes 786440 | tf_op jit(solution)/shard_map/ppermute | solution.py:28
  52.8 20.0 %collective-permute-start.17 = (bf16[64,2176]{1,0:T(8,128)(2,1)S(1)}, bf16[64,2176]{1,0:T(8,128)(2,1)S(1)}, u32[]{:S(2)}, u32[]{:S(2)}) collective-permute-start(bf16[64,2176]{1,0:T(8,128)(2,1)S(1)} %get-tuple-element.116.refs_2_), channel_id=1, source_target_pairs={{0,24},{8,16},{16,8},{24,0},{1,25},{9,17},{17,9},{25,1},{2,26},{10... | collective-permute-start | bytes 835592 | tf_op jit(solution)/shard_map/ppermute | solution.py:28
  52.8 25.9 %collective-permute-start.18 = (bf16[64,2176]{1,0:T(8,128)(2,1)S(1)}, bf16[64,2176]{1,0:T(8,128)(2,1)S(1)}, u32[]{:S(2)}, u32[]{:S(2)}) collective-permute-start(bf16[64,2176]{1,0:T(8,128)(2,1)S(1)} %get-tuple-element.116.refs_2_), channel_id=1, source_target_pairs={{0,16},{8,24},{16,0},{24,8},{1,17},{9,25},{17,1},{25,9},{2,18},{10... | collective-permute-start | bytes 835592 | tf_op jit(solution)/shard_map/ppermute | solution.py:28
  69.2 15.0 %collective-permute-start.14 = (bf16[64,2048]{1,0:T(8,128)(2,1)S(1)}, bf16[64,2048]{1,0:T(8,128)(2,1)S(1)}, u32[]{:S(2)}, u32[]{:S(2)}) collective-permute-start(bf16[64,2048]{1,0:T(8,128)(2,1)S(1)} %get-tuple-element.121), channel_id=1, source_target_pairs={{0,2},{2,0},{4,6},{6,4},{1,3},{3,1},{5,7},{7,5},{8,10},{10,8},{12,... | collective-permute-start | bytes 786440 | tf_op jit(solution)/shard_map/ppermute | solution.py:28
  71.0 14.5 %collective-permute-start.15 = (bf16[64,2048]{1,0:T(8,128)(2,1)S(1)}, bf16[64,2048]{1,0:T(8,128)(2,1)S(1)}, u32[]{:S(2)}, u32[]{:S(2)}) collective-permute-start(bf16[64,2048]{1,0:T(8,128)(2,1)S(1)} %get-tuple-element.122), channel_id=1, source_target_pairs={{0,4},{2,6},{4,0},{6,2},{1,5},{3,7},{5,1},{7,3},{8,12},{10,14},{12... | collective-permute-start | bytes 786440 | tf_op jit(solution)/shard_map/ppermute | solution.py:28
  71.0 14.5 %collective-permute-start.16 = (bf16[64,2048]{1,0:T(8,128)(2,1)S(1)}, bf16[64,2048]{1,0:T(8,128)(2,1)S(1)}, u32[]{:S(2)}, u32[]{:S(2)}) collective-permute-start(bf16[64,2048]{1,0:T(8,128)(2,1)S(1)} %get-tuple-element.123), channel_id=1, source_target_pairs={{0,6},{2,4},{4,2},{6,0},{1,7},{3,5},{5,3},{7,1},{8,14},{10,12},{12... | collective-permute-start | bytes 786440 | tf_op jit(solution)/shard_map/ppermute | solution.py:28
  80.3 16.9 %collective-permute-start.19 = (bf16[64,2048]{1,0:T(8,128)(2,1)S(1)}, bf16[64,2048]{1,0:T(8,128)(2,1)S(1)}, u32[]{:S(2)}, u32[]{:S(2)}) collective-permute-start(bf16[64,2048]{1,0:T(8,128)(2,1)S(1)} %get-tuple-element.132), channel_id=1, source_target_pairs={{0,2},{2,0},{4,6},{6,4},{1,3},{3,1},{5,7},{7,5},{8,10},{10,8},{12,... | collective-permute-start | bytes 786440 | tf_op jit(solution)/shard_map/ppermute | solution.py:28
  81.0 16.2 %collective-permute-start.20 = (bf16[64,2048]{1,0:T(8,128)(2,1)S(1)}, bf16[64,2048]{1,0:T(8,128)(2,1)S(1)}, u32[]{:S(2)}, u32[]{:S(2)}) collective-permute-start(bf16[64,2048]{1,0:T(8,128)(2,1)S(1)} %get-tuple-element.133), channel_id=1, source_target_pairs={{0,4},{2,6},{4,0},{6,2},{1,5},{3,7},{5,1},{7,3},{8,12},{10,14},{12... | collective-permute-start | bytes 786440 | tf_op jit(solution)/shard_map/ppermute | solution.py:28
  84.2 13.0 %collective-permute-start.21 = (bf16[64,2048]{1,0:T(8,128)(2,1)S(1)}, bf16[64,2048]{1,0:T(8,128)(2,1)S(1)}, u32[]{:S(2)}, u32[]{:S(2)}) collective-permute-start(bf16[64,2048]{1,0:T(8,128)(2,1)S(1)} %get-tuple-element.134), channel_id=1, source_target_pairs={{0,6},{2,4},{4,2},{6,0},{1,7},{3,5},{5,3},{7,1},{8,14},{10,12},{12... | collective-permute-start | bytes 786440 | tf_op jit(solution)/shard_map/ppermute | solution.py:28
  111.8 6.1 %collective-permute-start.24 = (bf16[32,2048]{1,0:T(8,128)(2,1)}, bf16[32,2048]{1,0:T(8,128)(2,1)S(1)}, u32[]{:S(2)}, u32[]{:S(2)}) collective-permute-start(bf16[32,2048]{1,0:T(8,128)(2,1)} %get-tuple-element.151), channel_id=1, source_target_pairs={{0,6},{2,4},{4,2},{6,0},{1,7},{3,5},{5,3},{7,1},{8,14},{10,12},{12... | collective-permute-start | bytes 393224 | tf_op jit(solution)/shard_map/ppermute | solution.py:28
  119.0 6.6 %collective-permute-start.25 = (bf16[32,2048]{1,0:T(8,128)(2,1)}, bf16[32,2048]{1,0:T(8,128)(2,1)S(1)}, u32[]{:S(2)}, u32[]{:S(2)}) collective-permute-start(bf16[32,2048]{1,0:T(8,128)(2,1)} %get-tuple-element.153), channel_id=1, source_target_pairs={{0,2},{2,0},{4,6},{6,4},{1,3},{3,1},{5,7},{7,5},{8,10},{10,8},{12,... | collective-permute-start | bytes 393224 | tf_op jit(solution)/shard_map/ppermute | solution.py:28
  120.8 9.0 %collective-permute-start.26 = (bf16[32,2048]{1,0:T(8,128)(2,1)}, bf16[32,2048]{1,0:T(8,128)(2,1)S(1)}, u32[]{:S(2)}, u32[]{:S(2)}) collective-permute-start(bf16[32,2048]{1,0:T(8,128)(2,1)} %get-tuple-element.154), channel_id=1, source_target_pairs={{0,4},{2,6},{4,0},{6,2},{1,5},{3,7},{5,1},{7,3},{8,12},{10,14},{12... | collective-permute-start | bytes 393224 | tf_op jit(solution)/shard_map/ppermute | solution.py:28
  121.6 8.2 %collective-permute-start.27 = (bf16[32,2048]{1,0:T(8,128)(2,1)}, bf16[32,2048]{1,0:T(8,128)(2,1)S(1)}, u32[]{:S(2)}, u32[]{:S(2)}) collective-permute-start(bf16[32,2048]{1,0:T(8,128)(2,1)} %get-tuple-element.155), channel_id=1, source_target_pairs={{0,6},{2,4},{4,2},{6,0},{1,7},{3,5},{5,3},{7,1},{8,14},{10,12},{12... | collective-permute-start | bytes 393224 | tf_op jit(solution)/shard_map/ppermute | solution.py:28
  122.6 10.4 %collective-permute-start.32 = (bf16[32,2048]{1,0:T(8,128)(2,1)S(1)}, bf16[32,2048]{1,0:T(8,128)(2,1)S(1)}, u32[]{:S(2)}, u32[]{:S(2)}) collective-permute-start(bf16[32,2048]{1,0:T(8,128)(2,1)S(1)} %copy-done.33), channel_id=1, source_target_pairs={{0,2},{2,0},{4,6},{6,4},{1,3},{3,1},{5,7},{7,5},{8,10},{10,8},{12,... | collective-permute-start | bytes 393224 | tf_op jit(solution)/shard_map/ppermute | solution.py:28
  124.3 9.5 %collective-permute-start.33 = (bf16[32,2048]{1,0:T(8,128)(2,1)S(1)}, bf16[32,2048]{1,0:T(8,128)(2,1)S(1)}, u32[]{:S(2)}, u32[]{:S(2)}) collective-permute-start(bf16[32,2048]{1,0:T(8,128)(2,1)S(1)} %copy-done.32), channel_id=1, source_target_pairs={{0,4},{2,6},{4,0},{6,2},{1,5},{3,7},{5,1},{7,3},{8,12},{10,14},{12... | collective-permute-start | bytes 393224 | tf_op jit(solution)/shard_map/ppermute | solution.py:28
  125.6 9.1 %collective-permute-start.34 = (bf16[32,2048]{1,0:T(8,128)(2,1)S(1)}, bf16[32,2048]{1,0:T(8,128)(2,1)S(1)}, u32[]{:S(2)}, u32[]{:S(2)}) collective-permute-start(bf16[32,2048]{1,0:T(8,128)(2,1)S(1)} %copy-done.31), channel_id=1, source_target_pairs={{0,6},{2,4},{4,2},{6,0},{1,7},{3,5},{5,3},{7,1},{8,14},{10,12},{12... | collective-permute-start | bytes 393224 | tf_op jit(solution)/shard_map/ppermute | solution.py:28
  131.0 9.4 %collective-permute-start.28 = (bf16[32,2048]{1,0:T(8,128)(2,1)S(1)}, bf16[32,2048]{1,0:T(8,128)(2,1)S(1)}, u32[]{:S(2)}, u32[]{:S(2)}) collective-permute-start(bf16[32,2048]{1,0:T(8,128)(2,1)S(1)} %copy-done.30), channel_id=1, source_target_pairs={{0,2},{2,0},{4,6},{6,4},{1,3},{3,1},{5,7},{7,5},{8,10},{10,8},{12,... | collective-permute-start | bytes 393224 | tf_op jit(solution)/shard_map/ppermute | solution.py:28
  131.2 9.9 %collective-permute-start.29 = (bf16[32,2048]{1,0:T(8,128)(2,1)S(1)}, bf16[32,2048]{1,0:T(8,128)(2,1)S(1)}, u32[]{:S(2)}, u32[]{:S(2)}) collective-permute-start(bf16[32,2048]{1,0:T(8,128)(2,1)S(1)} %copy-done.29), channel_id=1, source_target_pairs={{0,4},{2,6},{4,0},{6,2},{1,5},{3,7},{5,1},{7,3},{8,12},{10,14},{12... | collective-permute-start | bytes 393224 | tf_op jit(solution)/shard_map/ppermute | solution.py:28
  133.0 14.4 %collective-permute-start.31 = (bf16[64,2048]{1,0:T(8,128)(2,1)S(1)}, bf16[64,2048]{1,0:T(8,128)(2,1)S(1)}, u32[]{:S(2)}, u32[]{:S(2)}) collective-permute-start(bf16[64,2048]{1,0:T(8,128)(2,1)S(1)} %copy-done.28), channel_id=1, source_target_pairs={{0,2},{2,0},{1,3},{3,1},{4,6},{6,4},{5,7},{7,5},{8,10},{10,8},{9,1... | collective-permute-start | bytes 786440 | tf_op jit(solution)/shard_map/ppermute | solution.py:28
  134.9 12.5 %collective-permute-start.35 = (bf16[64,2048]{1,0:T(8,128)(2,1)S(1)}, bf16[64,2048]{1,0:T(8,128)(2,1)S(1)}, u32[]{:S(2)}, u32[]{:S(2)}) collective-permute-start(bf16[64,2048]{1,0:T(8,128)(2,1)S(1)} %combine.7), channel_id=1, source_target_pairs={{0,8},{8,0},{16,24},{24,16},{1,9},{9,1},{17,25},{25,17},{2,10},{10... | collective-permute-start | bytes 786440 | tf_op jit(solution)/shard_map/ppermute | solution.py:28
  135.0 12.6 %collective-permute-start.36 = (bf16[64,2048]{1,0:T(8,128)(2,1)S(1)}, bf16[64,2048]{1,0:T(8,128)(2,1)S(1)}, u32[]{:S(2)}, u32[]{:S(2)}) collective-permute-start(bf16[64,2048]{1,0:T(8,128)(2,1)S(1)} %combine.4), channel_id=1, source_target_pairs={{0,24},{8,16},{16,8},{24,0},{1,25},{9,17},{17,9},{25,1},{2,26},{10... | collective-permute-start | bytes 786440 | tf_op jit(solution)/shard_map/ppermute | solution.py:28
  140.4 15.7 %collective-permute-start.37 = (bf16[64,2048]{1,0:T(8,128)(2,1)S(1)}, bf16[64,2048]{1,0:T(8,128)(2,1)S(1)}, u32[]{:S(2)}, u32[]{:S(2)}) collective-permute-start(bf16[64,2048]{1,0:T(8,128)(2,1)S(1)} %combine.5), channel_id=1, source_target_pairs={{0,16},{8,24},{16,0},{24,8},{1,17},{9,25},{17,1},{25,9},{2,18},{10... | collective-permute-start | bytes 786440 | tf_op jit(solution)/shard_map/ppermute | solution.py:28
  141.1 6.1 %collective-permute-start.30 = (bf16[32,2048]{1,0:T(8,128)(2,1)}, bf16[32,2048]{1,0:T(8,128)(2,1)S(1)}, u32[]{:S(2)}, u32[]{:S(2)}) collective-permute-start(bf16[32,2048]{1,0:T(8,128)(2,1)} %get-tuple-element.159), channel_id=1, source_target_pairs={{0,6},{2,4},{4,2},{6,0},{1,7},{3,5},{5,3},{7,1},{8,14},{10,12},{12... | collective-permute-start | bytes 393224 | tf_op jit(solution)/shard_map/ppermute | solution.py:28
  (42 other events, 708.2 us)

commit v6 on v5

--- a/solution.py
+++ b/solution.py
@@ -3,6 +3,7 @@
 
 import jax
 import jax.numpy as jnp
+import numpy as np
 from jax import lax
 from jax.experimental import pallas as pl
 from jax.experimental.pallas import tpu as pltpu
@@ -32,67 +33,118 @@
     return jnp.dot(left, right, preferred_element_type=jnp.float32)
 
 
-def ancestry(parents):
-    nodes_count = parents.shape[-1]
-    nodes = jnp.arange(nodes_count, dtype=jnp.int32)
-    reach = (parents[..., :, None] == nodes).astype(jnp.float32) + jnp.eye(
-        nodes_count, dtype=jnp.float32
-    )
-    for turn in range((nodes_count - 1).bit_length()):
-        near = reach.astype(jnp.bfloat16)
-        reach = jnp.minimum(
-            jnp.einsum("rij,rjk->rik", near, near, preferred_element_type=jnp.float32), 1.0
-        )
-    depth = jnp.sum(reach, axis=-1) - 1.0
-    return (reach, depth)
-
-
-def arrive(copies):
+def in_vmem():
+    return pl.BlockSpec(memory_space=pltpu.VMEM)
+
+
+def in_hbm():
+    return pl.BlockSpec(memory_space=pltpu.HBM)
+
+
+def in_smem():
+    return pl.BlockSpec(memory_space=pltpu.SMEM)
+
+
+def vmem(mib):
+    return pltpu.CompilerParams(vmem_limit_bytes=mib * 2**20)
+
+
+def load_kernel(*refs):
+    count = len(refs) // 2
+    sems = refs[2 * count]
+    copies = [pltpu.make_async_copy(refs[i], refs[count + i], sems.at[i]) for i in range(count)]
+    for copy in copies:
+        copy.start()
     for copy in copies:
         copy.wait()
 
 
+def load(arrays):
+    return pl.pallas_call(
+        load_kernel,
+        in_specs=[in_hbm()] * len(arrays),
+        out_specs=[in_vmem()] * len(arrays),
+        out_shape=[jax.ShapeDtypeStruct(array.shape, array.dtype) for array in arrays],
+        scratch_shapes=[pltpu.SemaphoreType.DMA((len(arrays),))],
+        compiler_params=vmem(20),
+        cost_estimate=SMALL,
+        name="load",
+    )(*arrays)
+
+
+def prepare_kernel(lengths, parents, frequency, *refs):
+    count = (len(refs) - 4) // 2
+    sources = refs[:count]
+    reach, cosine, sine = refs[count : count + 3]
+    targets = refs[count + 3 : 2 * count + 3]
+    sems = refs[-1]
+    copies = [
+        pltpu.make_async_copy(sources[i], targets[i], sems.at[i]) for i in range(count)
+    ]
+    for copy in copies:
+        copy.start()
+    requests, tree = parents.shape[:2]
+    row = lax.broadcasted_iota(jnp.int32, (tree, tree), 0)
+    column = lax.broadcasted_iota(jnp.int32, (tree, tree), 1)
+    near = [
+        jnp.where((parents[r] == column) | (row == column), 1.0, 0.0) for r in range(requests)
+    ]
+    for turn in range((tree - 1).bit_length()):
+        for r in range(requests):
+            step = near[r].astype(jnp.bfloat16)
+            near[r] = jnp.minimum(dot(step, step), 1.0)
+    half = cosine.shape[2] // 2
+    lane = lax.broadcasted_iota(jnp.int32, cosine.shape[1:], 1)
+    for r in range(requests):
+        reach[r] = near[r]
+        depth = jnp.sum(near[r], axis=-1, keepdims=True) - 1.0
+        angle = (lengths[r].astype(jnp.float32) + depth) * frequency[...]
+        cosine[r] = jnp.cos(angle)
+        sines = jnp.sin(angle)
+        sine[r] = jnp.where(lane < half, -sines, sines)
+    for copy in copies:
+        copy.wait()
+
+
+def prepare(lengths, parents, head_dim, arrays):
+    requests, tree = parents.shape
+    half = head_dim // 2
+    frequency = ROPE_BASE ** (-np.arange(half, dtype=np.float64) / half)
+    frequency = np.concatenate([frequency, frequency])[None].astype(np.float32)
+    table = jax.ShapeDtypeStruct((requests, tree, head_dim), jnp.float32)
+    made = pl.pallas_call(
+        prepare_kernel,
+        in_specs=[in_smem(), in_vmem(), in_vmem()] + [in_hbm()] * len(arrays),
+        out_specs=[in_vmem()] * (3 + len(arrays)),
+        out_shape=[jax.ShapeDtypeStruct((requests, tree, tree), jnp.float32), table, table]
+        + [jax.ShapeDtypeStruct(array.shape, array.dtype) for array in arrays],
+        scratch_shapes=[pltpu.SemaphoreType.DMA((len(arrays),))],
+        compiler_params=vmem(20),
+        cost_estimate=SMALL,
+        name="prepare",
+    )(lengths, parents[..., None], frequency, *arrays)
+    return made[:3], made[3:]
+
+
 def attend_kernel(
-    info, first, second, gain, weight, cosine, sine, reach, cache, outward, *outs_and_scratch
+    place, lengths, first, second, gain, weight, cosine, sine, reach, cache, outward, *outs, offset
 ):
-    term, mixed = outs_and_scratch[0:2]
-    fresh = outs_and_scratch[2:4]
-    weight_here, cache_here, gain_here, outward_here, sems = outs_and_scratch[4:]
+    term, mixed = outs[0:2]
+    fresh = outs[2:4]
     tree = first.shape[0]
-    width, columns = weight.shape
+    columns = weight.shape[1]
     head_dim = cosine.shape[2]
     group = columns // head_dim - 2
-    deep = width // 2
-
-    gain_copy = pltpu.make_async_copy(gain, gain_here, sems.at[0])
-    weight_copies = [
-        pltpu.make_async_copy(
-            weight.at[pl.ds(i * deep, deep)], weight_here.at[pl.ds(i * deep, deep)], sems.at[1 + i]
-        )
-        for i in range(2)
-    ]
-    cache_copies = [
-        pltpu.make_async_copy(cache.at[info[i]], cache_here.at[i], sems.at[3 + i])
-        for i in range(2)
-    ]
-    outward_copy = pltpu.make_async_copy(outward, outward_here, sems.at[5])
-    for copy in [gain_copy, *weight_copies, *cache_copies, outward_copy]:
-        copy.start()
-
     wide = jnp.concatenate([first[...], second[...]], axis=0).astype(jnp.float32)
     power = jnp.mean(wide * wide, axis=-1, keepdims=True)
-    gain_copy.wait()
-    normed = (wide * lax.rsqrt(power + EPSILON) * gain_here[...]).astype(jnp.bfloat16)
-    weight_copies[0].wait()
-    projected = dot(normed[:, :deep], weight_here[:deep])
-    weight_copies[1].wait()
-    projected = projected + dot(normed[:, deep:], weight_here[deep:])
+    normed = (wide * lax.rsqrt(power + EPSILON) * gain[...]).astype(jnp.bfloat16)
+    projected = dot(normed, weight[...])
     scale = 1.0 / math.sqrt(head_dim)
 
     for i in range(2):
         own = projected[i * tree : (i + 1) * tree]
-        request = info[i]
-        length = info[2 + i]
+        request = place[0] ^ (offset + i)
+        length = lengths[request]
 
         def rope(values):
             return values * cosine[request] + pltpu.roll(values, head_dim // 2, 1) * sine[request]
@@ -122,19 +174,18 @@
         weights = jnp.exp(scores - peak)
         total = jnp.sum(weights, axis=-1, keepdims=True)
         summed = dot(weights.astype(jnp.bfloat16), value_new)
-        cache_copies[i].wait()
 
         def chunk(j, carry):
             peak, total, summed = carry
             block = pl.ds(pl.multiple_of(j * CHUNK, CHUNK), CHUNK)
-            scores = against(cache_here[i, block, :head_dim])
+            scores = against(cache[request, block, :head_dim])
             place = j * CHUNK + lax.broadcasted_iota(jnp.int32, scores.shape, 1)
             scores = jnp.where(place < length, scores, -1e30)
             higher = jnp.maximum(peak, jnp.max(scores, axis=-1, keepdims=True))
             fade = jnp.exp(peak - higher)
             weights = jnp.exp(scores - higher)
             total = total * fade + jnp.sum(weights, axis=-1, keepdims=True)
-            values = cache_here[i, block, head_dim:]
+            values = cache[request, block, head_dim:]
             summed = summed * fade + dot(weights.astype(jnp.bfloat16), values)
             return (higher, total, summed)
 
@@ -149,83 +200,41 @@
             mixed[...] = result
         else:
             kept = result
-    outward_copy.wait()
-    term[...] = dot(kept, outward_here[...])
-
-
-def in_vmem():
-    return pl.BlockSpec(memory_space=pltpu.VMEM)
-
-
-def in_hbm():
-    return pl.BlockSpec(memory_space=pltpu.HBM)
-
-
-def attend(info, first, second, gain, weight, cosine, sine, reach, cache, outward):
+    term[...] = dot(kept, outward[...])
+
+
+def attend(offset, place, lengths, first, second, gain, weight, tables, cache, outward):
     tree, width = first.shape
     slots, pair = cache.shape[1:]
-    head_dim = pair // 2
     columns = weight.shape[1]
     group_columns = columns - pair
+    reach, cosine, sine = tables
     return pl.pallas_call(
-        attend_kernel,
-        in_specs=[
-            pl.BlockSpec(memory_space=pltpu.SMEM),
-            in_vmem(),
-            in_vmem(),
-            in_hbm(),
-            in_hbm(),
-            in_vmem(),
-            in_vmem(),
-            in_vmem(),
-            in_hbm(),
-            in_hbm(),
-        ],
+        functools.partial(attend_kernel, offset=offset),
+        in_specs=[in_smem()] * 2 + [in_vmem()] * 9,
         out_specs=[in_vmem()] * 4,
         out_shape=[
             jax.ShapeDtypeStruct((tree, width), jnp.float32),
             jax.ShapeDtypeStruct((tree, group_columns), jnp.bfloat16),
         ]
         + [jax.ShapeDtypeStruct((tree, pair), jnp.bfloat16)] * 2,
-        scratch_shapes=[
-            pltpu.VMEM((width, columns), jnp.bfloat16),
-            pltpu.VMEM((2, slots, pair), jnp.bfloat16),
-            pltpu.VMEM((1, width), jnp.float32),
-            pltpu.VMEM((group_columns, width), jnp.bfloat16),
-            pltpu.SemaphoreType.DMA((6,)),
-        ],
-        compiler_params=pltpu.CompilerParams(vmem_limit_bytes=60 * 2**20),
+        compiler_params=vmem(24),
         cost_estimate=SMALL,
         name="attend",
-    )(info, first, second, gain, weight, cosine, sine, reach, cache, outward)
-
-
-def project_kernel(term, mixed, outward, out, here, sems):
-    half = here.shape[0] // 2
-    copies = [
-        pltpu.make_async_copy(
-            outward.at[pl.ds(i * half, half)], here.at[pl.ds(i * half, half)], sems.at[i]
-        )
-        for i in range(2)
-    ]
-    for copy in copies:
-        copy.start()
-    total = term[...]
-    for i, copy in enumerate(copies):
-        copy.wait()
-        block = slice(i * half, (i + 1) * half)
-        total = total + dot(mixed[:, block], here[block])
-    out[...] = total.astype(out.dtype)
+    )(place, lengths, first, second, gain, weight, cosine, sine, reach, cache, outward)
+
+
+def project_kernel(term, mixed, outward, out):
+    out[...] = (term[...] + dot(mixed[...], outward[...])).astype(out.dtype)
 
 
 def project(term, mixed, outward, dtype):
     return pl.pallas_call(
         project_kernel,
-        in_specs=[in_vmem(), in_vmem(), in_hbm()],
+        in_specs=[in_vmem()] * 3,
         out_specs=in_vmem(),
         out_shape=jax.ShapeDtypeStruct(term.shape, dtype),
-        scratch_shapes=[pltpu.VMEM(outward.shape, jnp.bfloat16), pltpu.SemaphoreType.DMA((2,))],
-        compiler_params=pltpu.CompilerParams(vmem_limit_bytes=60 * 2**20),
+        compiler_params=vmem(16),
         cost_estimate=SMALL,
         name="project",
     )(term, mixed, outward)
@@ -235,41 +244,18 @@
     return values / (1.0 + jnp.exp(-values))
 
 
-def expert_kernel(*refs, plane, count, deep):
+def expert_kernel(*refs, plane, count):
     pieces = refs[:plane]
     weights = refs[plane : plane + 4]
-    outs = refs[plane + 4 : plane + 4 + count * plane]
-    rows, inner_a, outer_a, inner_b, outer_b, sems = refs[plane + 4 + count * plane :]
+    outs = refs[plane + 4 :]
     each = pieces[0].shape[0]
-    width = rows.shape[1]
-    parts = width // deep
-    copies = []
-    for n, (inner, outer, inner_here, outer_here) in enumerate(
-        ((weights[0], weights[1], inner_a, outer_a), (weights[2], weights[3], inner_b, outer_b))
-    ):
-        base = n * (parts + 1)
-        for p in range(parts):
-            block = pl.ds(p * deep, deep)
-            copies.append(
-                pltpu.make_async_copy(inner.at[block], inner_here.at[block], sems.at[base + p])
-            )
-        copies.append(pltpu.make_async_copy(outer, outer_here, sems.at[base + parts]))
-    for copy in copies:
-        copy.start()
-    for i in range(plane):
-        rows[i * each : (i + 1) * each] = pieces[i][...]
+    rows = jnp.concatenate([piece[...] for piece in pieces], axis=0)
     result = None
-    for n, (inner_here, outer_here) in enumerate(((inner_a, outer_a), (inner_b, outer_b))):
-        base = n * (parts + 1)
-        both = None
-        for p in range(parts):
-            copies[base + p].wait()
-            term = dot(rows[:, p * deep : (p + 1) * deep], inner_here[p * deep : (p + 1) * deep])
-            both = term if both is None else both + term
+    for n in range(2):
+        both = dot(rows, weights[2 * n][...])
         half = both.shape[1] // 2
         hidden = (silu(both[:, :half]) * both[:, half:]).astype(jnp.bfloat16)
-        copies[base + parts].wait()
-        term = dot(hidden, outer_here[...]).astype(jnp.bfloat16).astype(jnp.float32)
+        term = dot(hidden, weights[2 * n + 1][...]).astype(jnp.bfloat16).astype(jnp.float32)
         result = term if result is None else result + term
     step = each // count
     for n in range(count * plane):
@@ -277,77 +263,67 @@
         outs[n][...] = result[base : base + step].astype(jnp.bfloat16)
 
 
-def experts(pieces, count, inner, outer):
+def experts(pieces, count, weights):
     plane = len(pieces)
     each, width = pieces[0].shape
-    hidden = inner[0].shape[1]
-    deep = width // 2
-    kernel = functools.partial(expert_kernel, plane=plane, count=count, deep=deep)
-    weight_scratch = [
-        pltpu.VMEM((width, hidden), jnp.bfloat16),
-        pltpu.VMEM((hidden // 2, width), jnp.bfloat16),
-    ]
     made = pl.pallas_call(
-        kernel,
-        in_specs=[in_vmem()] * plane + [in_hbm()] * 4,
+        functools.partial(expert_kernel, plane=plane, count=count),
+        in_specs=[in_vmem()] * (plane + 4),
         out_specs=[in_vmem()] * (count * plane),
         out_shape=[jax.ShapeDtypeStruct((each // count, width), jnp.bfloat16)] * (count * plane),
-        scratch_shapes=[pltpu.VMEM((plane * each, width), jnp.bfloat16)]
-        + weight_scratch * 2
-        + [pltpu.SemaphoreType.DMA((2 * (width // deep + 1),))],
-        compiler_params=pltpu.CompilerParams(vmem_limit_bytes=60 * 2**20),
+        compiler_params=vmem(36),
         cost_estimate=SMALL,
         name="expert",
-    )(*pieces, inner[0], outer[0], inner[1], outer[1])
+    )(*pieces, *weights)
     return [list(made[i * plane : (i + 1) * plane]) for i in range(count)]
 
 
 def shared_kernel(*refs, side):
     blocks = refs[:side]
-    weights = refs[side : side + 6]
+    near = refs[side : side + 3]
+    weights = refs[side + 3 : side + 6]
     outs = refs[side + 6 : 2 * side + 6]
     here, sems = refs[2 * side + 6 :]
-    copies = [pltpu.make_async_copy(weights[i], here.at[i], sems.at[i]) for i in range(6)]
+    copies = [pltpu.make_async_copy(weights[i], here.at[i], sems.at[i]) for i in range(3)]
     for copy in copies:
         copy.start()
     tree = blocks[0].shape[0]
     rows = jnp.concatenate([block[...] for block in blocks], axis=0)
 
-    def turned(i):
-        copies[i].wait()
+    def turned(weight):
         return lax.dot_general(
-            rows, here[i], (((1,), (1,)), ((), ())), preferred_element_type=jnp.float32
+            rows, weight, (((1,), (1,)), ((), ())), preferred_element_type=jnp.float32
         )
 
-    result = None
-    for n in range(2):
-        hidden = silu(turned(3 * n))
-        hidden = (hidden * turned(3 * n + 1)).astype(jnp.bfloat16)
-        copies[3 * n + 2].wait()
-        term = dot(hidden, here[3 * n + 2])
-        result = term if result is None else result + term
+    hidden = (silu(turned(near[0][...])) * turned(near[1][...])).astype(jnp.bfloat16)
+    result = dot(hidden, near[2][...])
+    copies[0].wait()
+    gated = silu(turned(here[0]))
+    copies[1].wait()
+    hidden = (gated * turned(here[1])).astype(jnp.bfloat16)
+    copies[2].wait()
+    result = result + dot(hidden, here[2])
     for i in range(side):
         outs[i][...] = result[i * tree : (i + 1) * tree].astype(outs[i].dtype)
 
 
-def shared_terms(own, beside, weights):
+def shared_terms(own, beside, near, weights):
     tree, width = own.shape
-    units = weights[0].shape[0]
     side = 1 + len(beside)
     outs = pl.pallas_call(
         functools.partial(shared_kernel, side=side),
-        in_specs=[in_vmem()] * side + [in_hbm()] * 6,
+        in_specs=[in_vmem()] * (side + 3) + [in_hbm()] * 3,
         out_specs=[in_vmem()] * side,
         out_shape=[jax.ShapeDtypeStruct((tree, width), jnp.float32)]
         + [jax.ShapeDtypeStruct((tree, width), jnp.bfloat16)] * (side - 1),
         scratch_shapes=[
-            pltpu.VMEM((6, units, width), jnp.bfloat16),
-            pltpu.SemaphoreType.DMA((6,)),
+            pltpu.VMEM((3, *weights[0].shape), jnp.bfloat16),
+            pltpu.SemaphoreType.DMA((3,)),
         ],
-        compiler_params=pltpu.CompilerParams(vmem_limit_bytes=60 * 2**20),
+        compiler_params=vmem(20),
         cost_estimate=SMALL,
         name="shared",
-    )(own, *beside, *weights)
+    )(own, *beside, *near, *weights)
     return outs[0], list(outs[1:])
 
 
@@ -384,7 +360,7 @@
             jax.ShapeDtypeStruct((tree, width), jnp.bfloat16),
             jax.ShapeDtypeStruct((tree, width + EXTRA), jnp.bfloat16),
         ],
-        compiler_params=pltpu.CompilerParams(vmem_limit_bytes=16 * 2**20),
+        compiler_params=vmem(16),
         cost_estimate=SMALL,
         name="finish",
     )(tokens, term, gain, routes, *others)
@@ -445,11 +421,11 @@
         functools.partial(
             select_kernel, count=count, plane=plane, capacity=capacity, top_count=top_count
         ),
-        in_specs=[pl.BlockSpec(memory_space=pltpu.SMEM)] + [in_vmem()] * (1 + count),
+        in_specs=[in_smem()] + [in_vmem()] * (1 + count),
         out_specs=[in_vmem()] * (plane + count),
         out_shape=[jax.ShapeDtypeStruct((count * capacity, width), jnp.bfloat16)] * plane
         + [jax.ShapeDtypeStruct((tree, plane * capacity), jnp.bfloat16)] * count,
-        compiler_params=pltpu.CompilerParams(vmem_limit_bytes=16 * 2**20),
+        compiler_params=vmem(16),
         cost_estimate=SMALL,
         name="select",
     )(near, router, *sources)
@@ -470,7 +446,7 @@
         in_specs=[in_vmem()] * (1 + len(pieces)),
         out_specs=in_vmem(),
         out_shape=jax.ShapeDtypeStruct((tree, width), dtype),
-        compiler_params=pltpu.CompilerParams(vmem_limit_bytes=16 * 2**20),
+        compiler_params=vmem(16),
         cost_estimate=SMALL,
         name="combine",
     )(spread, *pieces)
@@ -489,7 +465,7 @@
         in_specs=[in_vmem()] * (4 + len(parts)),
         out_specs=in_vmem(),
         out_shape=jax.ShapeDtypeStruct(resid.shape, jnp.bfloat16),
-        compiler_params=pltpu.CompilerParams(vmem_limit_bytes=16 * 2**20),
+        compiler_params=vmem(16),
         cost_estimate=SMALL,
         name="final",
     )(live, resid, shared, routed, *parts)
@@ -525,23 +501,12 @@
     near = [own_rows] + [partner(own_rows, "x", o) for o in range(1, side)]
     near_core = [partner(own_rows, "c", 1)]
 
-    reach, depth = ancestry(parents)
-    positions = lengths[:, None].astype(jnp.float32) + depth
-    frequency = ROPE_BASE ** (-jnp.arange(head_dim // 2, dtype=jnp.float32) / (head_dim // 2))
-    angle = positions[..., None] * frequency
-    cosine = jnp.cos(angle)
-    sine = jnp.sin(angle)
-    cosine = jnp.concatenate([cosine, cosine], axis=-1)
-    sine = jnp.concatenate([-sine, sine], axis=-1)
-    info = []
-    for o in range(side):
-        ids = me ^ jnp.arange(2 * o, 2 * o + 2, dtype=jnp.int32)
-        here = ids[:, None] == jnp.arange(group_count, dtype=jnp.int32)
-        info.append(jnp.concatenate([ids, jnp.sum(jnp.where(here, lengths, 0), axis=1)]))
+    tables, (qkv_here, cache_here, out_here) = prepare(
+        lengths, parents, head_dim, [w_qkv, cache[:, 0], w_out]
+    )
+    place = me.astype(jnp.int32)[None]
     for o in range(1, side):
-        near[o], cosine, sine, reach, info = lax.optimization_barrier(
-            (near[o], cosine, sine, reach, info)
-        )
+        near[o], tables, place = lax.optimization_barrier((near[o], tables, place))
         near_core.append(partner(near[o], "c", 1))
 
     gate_turned, up_turned = shared_gate.T, shared_up.T
@@ -561,16 +526,16 @@
         if follow is not None:
             near_core[o], follow = lax.optimization_barrier((near_core[o], follow))
         own_part, mixed, fresh_own, fresh_other = attend(
-            info[o],
+            2 * o,
+            place,
+            lengths,
             near[o],
             near_core[o],
             attn_gain[None],
-            w_qkv,
-            cosine,
-            sine,
-            reach,
-            cache[:, 0],
-            w_out,
+            qkv_here,
+            tables,
+            cache_here,
+            out_here,
         )
         fresh[o] = jnp.stack([fresh_own, fresh_other])
         other = partner(mixed, "c", 1)
@@ -580,11 +545,13 @@
         terms[o] = project(own_part, other, early[0], jnp.bfloat16 if o else jnp.float32)
         follow = terms[o]
     others = [partner(terms[o], "x", o) for o in range(1, side)]
-    own_term, late = lax.optimization_barrier((terms[0], late))
+    expert_in_own, expert_out_own, _ = lax.optimization_barrier(
+        (expert_in[0], expert_out[0], terms[0])
+    )
+    inner_here, outer_here = load([expert_in_own, expert_out_own])
+    own_term, late, inner_here = lax.optimization_barrier((terms[0], late, inner_here))
     resid, normed, payload = finish(own_rows, own_term, others, ffn_gain[None], routes[0])
-    inner = [expert_in[0], late]
-    outer = [expert_out[0], early[1]]
-    shared_weights = [gate_turned, up_turned, shared_down, *middle]
+    expert_weights = [inner_here, outer_here, late, early[1]]
     order = me ^ jnp.arange(group_count, dtype=jnp.int32)
     kept = accepted[order][:, :, None] == jnp.arange(tree, dtype=jnp.int32)
     accepted_kv = jnp.einsum(
@@ -605,7 +572,9 @@
     line_rows = [payload] + [partner(payload, "z", k) for k in range(1, line)]
     beside = [partner(normed, "x", o) for o in range(1, side)]
 
-    shared, beside = shared_terms(normed, beside, shared_weights)
+    shared, beside = shared_terms(
+        normed, beside, middle, [gate_turned, up_turned, shared_down]
+    )
     line_rows[1], beside = lax.optimization_barrier((line_rows[1], beside))
 
     sent = []
@@ -622,7 +591,7 @@
     for ks, pieces in zip(GROUPS, sent):
         if made is not None:
             pieces, made = lax.optimization_barrier((pieces, made))
-        made = experts(pieces, len(ks), inner, outer)
+        made = experts(pieces, len(ks), expert_weights)
         results.update(zip(ks, made))
     totals = {}
     for k, after in BACK:

time: 158 us -> 169 us (1.070)
  local copies, waits for them, and re-layouts: 10.6 us -> 40.2 us
  starting transfers between devices: 44.5 us -> 37.5 us
  Pallas kernels: 58.4 us -> 52.8 us
  other arithmetic: 4.23 us -> 0.02 us
  matrix products: 3.5 us -> 0.19 us
  waiting for transfers between devices: 34.8 us -> 37 us
    unnamed x74 -> x104, local copies, waits for them, and re-layouts: 8.8 us -> 36.9 us
    pallas_call x6 -> x8, Pallas kernels: 45.9 us -> 38.2 us  [the longest x2 18 us: experts(): pl.pallas_call(functools.partial(expert_kernel, plane=plane, count=count)...]
    ppermute x38, starting transfers between devices: 44.5 us -> 37.5 us  [partner(): return lax.ppermute(value, axes, [(i, i ^ offset) for i in range(size)])]
    dot_general x3 -> x0, matrix products: 2.54 us -> none  [ancestry(): jnp.einsum('rij,rjk->rik', near, near, preferred_element_type=jnp.float32)]
    ppermute x38, waiting for transfers between devices: 34.8 us -> 37 us  [partner(): return lax.ppermute(value, axes, [(i, i ^ offset) for i in range(size)])]
    concatenate x3 -> x0, other arithmetic: 2.05 us -> none  [the longest x2 1.2 us: body(): jnp.concatenate([ids, jnp.sum(jnp.where(here, lengths, 0), axis=1)])]
    pallas_call x1, Pallas kernels: 0.22 us -> 2.01 us  [finish(): pl.pallas_call(finish_kernel, in_specs=[in_vmem()] * (4 + len(others)), o...]
  transfers between devices with their start and end apart: 38 -> 38, of which waited for: 14 -> 16; matrix products, arithmetic and copies ran while one was open for 6% -> 3% of each run, Pallas kernels for 29% -> 24%
where the time goes in v6:
time: 169 us
  Pallas kernels  52.8 us (31%)
  local copies, waits for them, and re-layouts  40.2 us (24%)
  starting transfers between devices  37.5 us (22%)
  waiting for transfers between devices  37 us (22%)
    ppermute x38, starting transfers between devices, partner(): return lax.ppermute(value, axes, [(i, i ^ offset) for i in range(size)])  37.5 us
    ppermute x38, waiting for transfers between devices, partner(): return lax.ppermute(value, axes, [(i, i ^ offset) for i in range(size)])  37 us
    unnamed x104, local copies, waits for them, and re-layouts  36.9 us
    pallas_call x2, Pallas kernels, experts(): pl.pallas_call(functools.partial(expert_kernel, plane=plane, count=count)...  18 us
    pallas_call x2, Pallas kernels, attend(): pl.pallas_call(functools.partial(attend_kernel, offset=offset), in_specs=...  9.76 us
    pallas_call x1, Pallas kernels, shared_terms(): pl.pallas_call(functools.partial(shared_kernel, side=side), in_specs=[in_...  6.12 us
    pallas_call x2, Pallas kernels, project(): pl.pallas_call(project_kernel, in_specs=[in_vmem()] * 3, out_specs=in_vme...  5.1 us
    pallas_call x2, Pallas kernels, select(): pl.pallas_call(functools.partial(select_kernel, count=count, plane=plane,...  4.51 us
  transfers between devices with their start and end apart: 38, of which 16 were waited for; matrix products, arithmetic and copies ran while one was open for 3% of the time, Pallas kernels for 24%

profile of v6, /device:TPU:0, one launch (start us, length us, event | category | flops | bytes accessed | tf_op | source)
XLA Modules:
  0.0 168.8 jit_solution(14781325563136860168)
XLA Ops:
  3.8 2.9 %collective-permute-start = (bf16[64,2048]{1,0:T(8,128)(2,1)}, bf16[64,2048]{1,0:T(8,128)(2,1)}, u32[]{:S(2)}, u32[]{:S(2)}) collective-permute-start(bf16[64,2048]{1,0:T(8,128)(2,1)} %bitcast.32), channel_id=1, source_target_pairs={{0,2},{2,0},{1,3},{3,1},{4,6},{6,4},{5,7},{7,5},{8,10},{10,8},{9,1... | collective-permute-start | bytes 786440 | tf_op jit(solution)/shard_map/ppermute | solution.py:29
  8.1 2.2 %copy-done.7 = bf16[4,1,2048,256]{3,2,1,0:T(8,128)(2,1)S(1)} copy-done((bf16[4,1,2048,256]{3,2,1,0:T(8,128)(2,1)S(1)}, bf16[4,1,2048,256]{3,2,1,0:T(8,128)(2,1)}, u32[]{:S(2)}) %copy-start.7) | copy-done | bytes 4194328
  10.3 1.9 %copy-done.8 = bf16[2048,768]{1,0:T(8,128)(2,1)S(1)} copy-done((bf16[2048,768]{1,0:T(8,128)(2,1)S(1)}, bf16[2048,768]{1,0:T(8,128)(2,1)}, u32[]{:S(2)}) %copy-start.8) | copy-done | bytes 3145752
  16.0 2.6 %prepare.1 = (f32[4,64,64]{2,1,0:T(8,128)S(1)}, f32[4,64,128]{2,1,0:T(8,128)S(1)}, f32[4,64,128]{2,1,0:T(8,128)S(1)}, bf16[2048,768]{1,0:T(8,128)(2,1)S(1)}, bf1...) custom-call(s32[4]{0:T(128)S(1)} %copy-done.36, s32[4,64,1]{2,1,0:T(8,128)S(1)} %copy-done.25, ...), custom_call_target="tpu_custom_call" | custom-call | flops 1024 | bytes 1024 | tf_op jit(solution)/shard_map/prepare/pallas_call | solution.py:115
  18.6 2.0 %copy-done.3 = bf16[4,2048,256]{2,1,0:T(8,128)(2,1)} copy-done((bf16[4,2048,256]{2,1,0:T(8,128)(2,1)}, bf16[4,2048,256]{2,1,0:T(8,128)(2,1)S(1)}, u32[]{:S(2)}) %copy-start.3) | copy-done | bytes 4194328
  24.3 2.2 %copy-done.4 = bf16[4,2048,256]{2,1,0:T(8,128)(2,1)S(1)} copy-done((bf16[4,2048,256]{2,1,0:T(8,128)(2,1)S(1)}, bf16[4,2048,256]{2,1,0:T(8,128)(2,1)}, u32[]{:S(2)}) %copy-start.4) | copy-done | bytes 4194328
  28.1 5.5 %attend.2 = (f32[64,2048]{1,0:T(8,128)S(1)}, bf16[64,512]{1,0:T(8,128)(2,1)S(1)}, bf16[64,256]{1,0:T(8,128)(2,1)S(1)}, bf16[64,256]{1,0:T(8,128)(2,1)S(1)}) custom-call(s32[1]{0:T(128)} %bitcast.4.place, s32[4]{0:T(128)S(1)} %copy-done.37, bf16[64,2048]{1,0:T(8,128)(2,1)} %collective-permute-done.first, bf16[64,2048]{1,0:T(8,128)(2,1)S(1)} %collective-permute-done.2.second, ...), custom_call_target="tpu_custom_call" | custom-call | flops 1024 | bytes 1024 | tf_op jit(solution)/shard_map/attend/pallas_call | solution.py:212
  36.7 3.0 %project.2 = bf16[64,2048]{1,0:T(8,128)(2,1)} custom-call(f32[64,2048]{1,0:T(8,128)S(1)} %get-tuple-element.113.term, bf16[64,512]{1,0:T(8,128)(2,1)S(1)} %collective-permute-done.5.mixed, bf16[512,2048]{1,0:T(8,128)(2,1)} %collective-permute-done.3.outward), custom_call_target="tpu_custom_call" | custom-call | flops 1024 | bytes 1024 | tf_op jit(solution)/shard_map/project/pallas_call | solution.py:232
  39.8 4.2 %attend.3 = (f32[64,2048]{1,0:T(8,128)S(1)}, bf16[64,512]{1,0:T(8,128)(2,1)}, bf16[64,256]{1,0:T(8,128)(2,1)S(1)}, bf16[64,256]{1,0:T(8,128)(2,1)S(1)}) custom-call(s32[1]{0:T(128)} %bitcast.4.place, s32[4]{0:T(128)S(1)} %copy-done.37, bf16[64,2048]{1,0:T(8,128)(2,1)S(1)} %bitcast.33, bf16[64,2048]{1,0:T(8,128)(2,1)S(1)} %copy-done.31, ...), custom_call_target="tpu_custom_call" | custom-call | flops 1024 | bytes 1024 | tf_op jit(solution)/shard_map/attend/pallas_call | solution.py:212
  48.5 2.1 %project.3.term = f32[64,2048]{1,0:T(8,128)S(1)} custom-call(f32[64,2048]{1,0:T(8,128)S(1)} %copy-done.27, bf16[64,512]{1,0:T(8,128)(2,1)S(1)} %collective-permute-done.9.mixed, bf16[512,2048]{1,0:T(8,128)(2,1)} %collective-permute-done.3.outward), custom_call_target="tpu_custom_call" | custom-call | flops 1024 | bytes 1024 | tf_op jit(solution)/shard_map/project/pallas_call | solution.py:232
  50.6 1.8 %copy-done.9 = bf16[1,704,2048]{2,1,0:T(8,128)(2,1)S(1)} copy-done((bf16[1,704,2048]{2,1,0:T(8,128)(2,1)S(1)}, bf16[1,704,2048]{2,1,0:T(8,128)(2,1)}, u32[]{:S(2)}) %copy-start.9) | copy-done | bytes 2883608
  52.4 2.7 %load.1 = (bf16[2048,1408]{1,0:T(8,128)(2,1)S(1)}, bf16[704,2048]{1,0:T(8,128)(2,1)S(1)}) custom-call(bf16[2048,1408]{1,0:T(8,128)(2,1)} %bitcast.9.refs_0_, bf16[704,2048]{1,0:T(8,128)(2,1)S(1)} %bitcast.26), custom_call_target="tpu_custom_call" | custom-call | flops 1024 | bytes 1024 | tf_op jit(solution)/shard_map/load/pallas_call | solution.py:63
  55.1 2.5 %copy-done.1 = bf16[2048,1408]{1,0:T(8,128)(2,1)} copy-done((bf16[2048,1408]{1,0:T(8,128)(2,1)}, bf16[2048,1408]{1,0:T(8,128)(2,1)S(1)}, u32[]{:S(2)}) %copy-start.1) | copy-done | bytes 5767192
  57.6 2.0 %finish.1 = (bf16[64,2048]{1,0:T(8,128)(2,1)S(1)}, bf16[64,2048]{1,0:T(8,128)(2,1)}, bf16[64,2176]{1,0:T(8,128)(2,1)}) custom-call(bf16[64,2048]{1,0:T(8,128)(2,1)S(1)} %bitcast.34, f32[64,2048]{1,0:T(8,128)S(1)} %project.3.term, f32[1,2048]{1,0:T(1,128)S(1)} %bitcast.38, s32[64,6]{1,0:T(8,128)S(1)} %bitcast.35, bf16[64,2048]{1,0:T(8,128)(2,1)} %collective-permute-done.11.refs_0_), custom_call_target="tpu_custom_call" | custom-call | flops 1024 | bytes 1024 | tf_op jit(solution)/shard_map/finish/pallas_call | solution.py:354
  60.3 3.0 %collective-permute-start.13 = (bf16[64,2176]{1,0:T(8,128)(2,1)}, bf16[64,2176]{1,0:T(8,128)(2,1)}, u32[]{:S(2)}, u32[]{:S(2)}) collective-permute-start(bf16[64,2176]{1,0:T(8,128)(2,1)} %get-tuple-element.134.refs_2_), channel_id=1, source_target_pairs={{0,8},{8,0},{16,24},{24,16},{1,9},{9,1},{17,25},{25,17},{2,10},{10... | collective-permute-start | bytes 835592 | tf_op jit(solution)/shard_map/ppermute | solution.py:29
  63.4 3.0 %collective-permute-start.12 = (bf16[64,2048]{1,0:T(8,128)(2,1)}, bf16[64,2048]{1,0:T(8,128)(2,1)}, u32[]{:S(2)}, u32[]{:S(2)}) collective-permute-start(bf16[64,2048]{1,0:T(8,128)(2,1)} %get-tuple-element.129.refs_0_), channel_id=1, source_target_pairs={{0,2},{2,0},{1,3},{3,1},{4,6},{6,4},{5,7},{7,5},{8,10},{10,8},{9,1... | collective-permute-start | bytes 786440 | tf_op jit(solution)/shard_map/ppermute | solution.py:29
  68.2 4.8 %collective-permute-done.12.refs_1_ = bf16[64,2048]{1,0:T(8,128)(2,1)} collective-permute-done((bf16[64,2048]{1,0:T(8,128)(2,1)}, bf16[64,2048]{1,0:T(8,128)(2,1)}, u32[]{:S(2)}, u32[]{:S(2)}) %collective-permute-start.12) | collective-permute-done | bytes 262176 | tf_op jit(solution)/shard_map/ppermute | solution.py:29
  81.2 6.1 %shared.1 = (f32[64,2048]{1,0:T(8,128)S(1)}, bf16[64,2048]{1,0:T(8,128)(2,1)}) custom-call(bf16[64,2048]{1,0:T(8,128)(2,1)} %get-tuple-element.129.refs_0_, bf16[64,2048]{1,0:T(8,128)(2,1)} %collective-permute-done.12.refs_1_, bf16[352,2048]{1,0:T(8,128)(2,1)S(1)} %copy-done.15, bf16[352,2048]{1,0:T(8,128)(2,1)S(1)} %copy-done.17, ...), custom_call_target="tpu_custom_call" | custom-call | flops 1024 | bytes 1024 | tf_op jit(solution)/shard_map/shared/pallas_call | solution.py:313
  87.3 2.3 %select.2 = (bf16[64,2048]{1,0:T(8,128)(2,1)S(1)}, bf16[64,2048]{1,0:T(8,128)(2,1)S(1)}, bf16[64,2048]{1,0:T(8,128)(2,1)S(1)}, bf16[64,2048]{1,0:T(8,128)(2,1)S(...) custom-call(s32[4]{0:T(128)S(1)} %xor_add_fusion.refs_0_, bf16[2048,16]{1,0:T(8,128)(2,1)S(1)} %copy.27.refs_1_, ...), custom_call_target="tpu_custom_call" | custom-call | flops 1024 | bytes 1024 | tf_op jit(solution)/shard_map/select/pallas_call | solution.py:420
  89.7 1.8 %collective-permute-start.14 = (bf16[64,2048]{1,0:T(8,128)(2,1)S(1)}, bf16[64,2048]{1,0:T(8,128)(2,1)S(1)}, u32[]{:S(2)}, u32[]{:S(2)}) collective-permute-start(bf16[64,2048]{1,0:T(8,128)(2,1)S(1)} %get-tuple-element.139), channel_id=1, source_target_pairs={{0,2},{2,0},{4,6},{6,4},{1,3},{3,1},{5,7},{7,5},{8,10},{10,8},{12,... | collective-permute-start | bytes 786440 | tf_op jit(solution)/shard_map/ppermute | solution.py:29
  93.3 2.2 %select.3 = (bf16[64,2048]{1,0:T(8,128)(2,1)S(1)}, bf16[64,2048]{1,0:T(8,128)(2,1)S(1)}, bf16[64,2048]{1,0:T(8,128)(2,1)S(1)}, bf16[64,2048]{1,0:T(8,128)(2,1)S(...) custom-call(s32[4]{0:T(128)S(1)} %xor_add_fusion.refs_0_, bf16[2048,16]{1,0:T(8,128)(2,1)S(1)} %copy.27.refs_1_, ...), custom_call_target="tpu_custom_call" | custom-call | flops 1024 | bytes 1024 | tf_op jit(solution)/shard_map/select/pallas_call | solution.py:420
  95.4 1.8 %collective-permute-start.19 = (bf16[64,2048]{1,0:T(8,128)(2,1)S(1)}, bf16[64,2048]{1,0:T(8,128)(2,1)S(1)}, u32[]{:S(2)}, u32[]{:S(2)}) collective-permute-start(bf16[64,2048]{1,0:T(8,128)(2,1)S(1)} %get-tuple-element.152), channel_id=1, source_target_pairs={{0,2},{2,0},{4,6},{6,4},{1,3},{3,1},{5,7},{7,5},{8,10},{10,8},{12,... | collective-permute-start | bytes 786440 | tf_op jit(solution)/shard_map/ppermute | solution.py:29
  97.2 1.8 %collective-permute-done.14.refs_1_ = bf16[64,2048]{1,0:T(8,128)(2,1)S(1)} collective-permute-done((bf16[64,2048]{1,0:T(8,128)(2,1)S(1)}, bf16[64,2048]{1,0:T(8,128)(2,1)S(1)}, u32[]{:S(2)}, u32[]{:S(2)}) %collective-permute-start.14) | collective-permute-done | bytes 262176 | tf_op jit(solution)/shard_map/ppermute | solution.py:29
  99.5 6.5 %collective-permute-done.15.refs_2_ = bf16[64,2048]{1,0:T(8,128)(2,1)S(1)} collective-permute-done((bf16[64,2048]{1,0:T(8,128)(2,1)S(1)}, bf16[64,2048]{1,0:T(8,128)(2,1)S(1)}, u32[]{:S(2)}, u32[]{:S(2)}) %collective-permute-start.15) | collective-permute-done | bytes 262176 | tf_op jit(solution)/shard_map/ppermute | solution.py:29
  106.0 2.6 %copy-done.2 = bf16[2048,1408]{1,0:T(8,128)(2,1)S(1)} copy-done((bf16[2048,1408]{1,0:T(8,128)(2,1)S(1)}, bf16[2048,1408]{1,0:T(8,128)(2,1)}, u32[]{:S(2)}) %copy-start.2) | copy-done | bytes 5767192
  108.6 8.9 %expert.2 = (bf16[32,2048]{1,0:T(8,128)(2,1)S(1)}, bf16[32,2048]{1,0:T(8,128)(2,1)S(1)}, bf16[32,2048]{1,0:T(8,128)(2,1)S(1)}, bf16[32,2048]{1,0:T(8,128)(2,1)S(...) custom-call(bf16[64,2048]{1,0:T(8,128)(2,1)S(1)} %get-tuple-element., ...), custom_call_target="tpu_custom_call" | custom-call | flops 1024 | bytes 1024 | tf_op jit(solution)/shard_map/expert/pallas_call | solution.py:269
  117.7 9.1 %expert.3 = (bf16[32,2048]{1,0:T(8,128)(2,1)S(1)}, bf16[32,2048]{1,0:T(8,128)(2,1)S(1)}, bf16[32,2048]{1,0:T(8,128)(2,1)S(1)}, bf16[32,2048]{1,0:T(8,128)(2,1)S(...) custom-call(bf16[64,2048]{1,0:T(8,128)(2,1)S(1)} %get-tuple-element., ...), custom_call_target="tpu_custom_call" | custom-call | flops 1024 | bytes 1024 | tf_op jit(solution)/shard_map/expert/pallas_call | solution.py:269
  132.3 3.7 %collective-permute-done.24.refs_3_ = bf16[32,2048]{1,0:T(8,128)(2,1)S(1)} collective-permute-done((bf16[32,2048]{1,0:T(8,128)(2,1)S(1)}, bf16[32,2048]{1,0:T(8,128)(2,1)S(1)}, u32[]{:S(2)}, u32[]{:S(2)}) %collective-permute-start.24) | collective-permute-done | bytes 131104 | tf_op jit(solution)/shard_map/ppermute | solution.py:29
  149.2 1.9 %collective-permute-done.34.refs_3_ = bf16[32,2048]{1,0:T(8,128)(2,1)S(1)} collective-permute-done((bf16[32,2048]{1,0:T(8,128)(2,1)S(1)}, bf16[32,2048]{1,0:T(8,128)(2,1)S(1)}, u32[]{:S(2)}, u32[]{:S(2)}) %collective-permute-start.34) | collective-permute-done | bytes 131104 | tf_op jit(solution)/shard_map/ppermute | solution.py:29
  152.1 2.4 %collective-permute-start.36 = (bf16[64,2048]{1,0:T(8,128)(2,1)S(1)}, bf16[64,2048]{1,0:T(8,128)(2,1)S(1)}, u32[]{:S(2)}, u32[]{:S(2)}) collective-permute-start(bf16[64,2048]{1,0:T(8,128)(2,1)S(1)} %combine.4), channel_id=1, source_target_pairs={{0,24},{8,16},{16,8},{24,0},{1,25},{9,17},{17,9},{25,1},{2,26},{10... | collective-permute-start | bytes 786440 | tf_op jit(solution)/shard_map/ppermute | solution.py:29
  158.3 3.3 %collective-permute-done.30.refs_3_ = bf16[32,2048]{1,0:T(8,128)(2,1)S(1)} collective-permute-done((bf16[32,2048]{1,0:T(8,128)(2,1)S(1)}, bf16[32,2048]{1,0:T(8,128)(2,1)S(1)}, u32[]{:S(2)}, u32[]{:S(2)}) %collective-permute-start.30) | collective-permute-done | bytes 131104 | tf_op jit(solution)/shard_map/ppermute | solution.py:29
  161.8 5.9 %collective-permute-done.37.refs_3_ = bf16[64,2048]{1,0:T(8,128)(2,1)S(1)} collective-permute-done((bf16[64,2048]{1,0:T(8,128)(2,1)S(1)}, bf16[64,2048]{1,0:T(8,128)(2,1)S(1)}, u32[]{:S(2)}, u32[]{:S(2)}) %collective-permute-start.37) | collective-permute-done | bytes 262176 | tf_op jit(solution)/shard_map/ppermute | solution.py:29
  (174 shorter events, 59.0 us)
Async XLA Ops:
  3.2 21.1 %collective-permute-start.4 = (bf16[704,2048]{1,0:T(8,128)(2,1)}, bf16[704,2048]{1,0:T(8,128)(2,1)}, u32[]{:S(2)}, u32[]{:S(2)}) collective-permute-start(bf16[704,2048]{1,0:T(8,128)(2,1)} %bitcast.25), channel_id=1, source_target_pairs={{0,1},{1,0},{2,3},{3,2},{4,5},{5,4},{6,7},{7,6},{8,9},{9,8},{10,11... | collective-permute-start | bytes 8650760 | tf_op jit(solution)/shard_map/ppermute | solution.py:29
  3.6 20.7 %collective-permute-start.3 = (bf16[512,2048]{1,0:T(8,128)(2,1)}, bf16[512,2048]{1,0:T(8,128)(2,1)}, u32[]{:S(2)}, u32[]{:S(2)}) collective-permute-start(bf16[512,2048]{1,0:T(8,128)(2,1)} %refs_2_.1), channel_id=1, source_target_pairs={{0,1},{1,0},{2,3},{3,2},{4,5},{5,4},{6,7},{7,6},{8,9},{9,8},{10,11... | collective-permute-start | bytes 6291464 | tf_op jit(solution)/shard_map/ppermute | solution.py:29
  3.8 18.2 %collective-permute-start = (bf16[64,2048]{1,0:T(8,128)(2,1)}, bf16[64,2048]{1,0:T(8,128)(2,1)}, u32[]{:S(2)}, u32[]{:S(2)}) collective-permute-start(bf16[64,2048]{1,0:T(8,128)(2,1)} %bitcast.32), channel_id=1, source_target_pairs={{0,2},{2,0},{1,3},{3,1},{4,6},{6,4},{5,7},{7,5},{8,10},{10,8},{9,1... | collective-permute-start | bytes 786440 | tf_op jit(solution)/shard_map/ppermute | solution.py:29
  23.7 11.8 %collective-permute-start.6 = (bf16[352,2048]{1,0:T(8,128)(2,1)}, bf16[352,2048]{1,0:T(8,128)(2,1)S(1)}, u32[]{:S(2)}, u32[]{:S(2)}) collective-permute-start(bf16[352,2048]{1,0:T(8,128)(2,1)} %bitcast.27), channel_id=1, source_target_pairs={{0,1},{1,0},{2,3},{3,2},{4,5},{5,4},{6,7},{7,6},{8,9},{9,8},{10,11... | collective-permute-start | bytes 4325384 | tf_op jit(solution)/shard_map/ppermute | solution.py:29
  23.8 11.7 %collective-permute-start.7 = (bf16[352,2048]{1,0:T(8,128)(2,1)}, bf16[352,2048]{1,0:T(8,128)(2,1)S(1)}, u32[]{:S(2)}, u32[]{:S(2)}) collective-permute-start(bf16[352,2048]{1,0:T(8,128)(2,1)} %bitcast.29), channel_id=1, source_target_pairs={{0,1},{1,0},{2,3},{3,2},{4,5},{5,4},{6,7},{7,6},{8,9},{9,8},{10,11... | collective-permute-start | bytes 4325384 | tf_op jit(solution)/shard_map/ppermute | solution.py:29
  24.2 11.3 %collective-permute-start.8 = (bf16[352,2048]{1,0:T(8,128)(2,1)}, bf16[352,2048]{1,0:T(8,128)(2,1)S(1)}, u32[]{:S(2)}, u32[]{:S(2)}) collective-permute-start(bf16[352,2048]{1,0:T(8,128)(2,1)} %refs_7_.1), channel_id=1, source_target_pairs={{0,1},{1,0},{2,3},{3,2},{4,5},{5,4},{6,7},{7,6},{8,9},{9,8},{10,11... | collective-permute-start | bytes 4325384 | tf_op jit(solution)/shard_map/ppermute | solution.py:29
  36.3 21.2 %collective-permute-start.10 = (bf16[2048,1408]{1,0:T(8,128)(2,1)}, bf16[2048,1408]{1,0:T(8,128)(2,1)}, u32[]{:S(2)}, u32[]{:S(2)}) collective-permute-start(bf16[2048,1408]{1,0:T(8,128)(2,1)} %bitcast.9.refs_0_), channel_id=1, source_target_pairs={{0,1},{1,0},{2,3},{3,2},{4,5},{5,4},{6,7},{7,6},{8,9},{9,8},{10,11... | collective-permute-start | bytes 17301512 | tf_op jit(solution)/shard_map/ppermute | solution.py:29
  39.7 17.9 %collective-permute-start.11 = (bf16[64,2048]{1,0:T(8,128)(2,1)}, bf16[64,2048]{1,0:T(8,128)(2,1)}, u32[]{:S(2)}, u32[]{:S(2)}) collective-permute-start(bf16[64,2048]{1,0:T(8,128)(2,1)} %project.2), channel_id=1, source_target_pairs={{0,2},{2,0},{1,3},{3,1},{4,6},{6,4},{5,7},{7,5},{8,10},{10,8},{9,1... | collective-permute-start | bytes 786440 | tf_op jit(solution)/shard_map/ppermute | solution.py:29
  60.3 27.0 %collective-permute-start.13 = (bf16[64,2176]{1,0:T(8,128)(2,1)}, bf16[64,2176]{1,0:T(8,128)(2,1)}, u32[]{:S(2)}, u32[]{:S(2)}) collective-permute-start(bf16[64,2176]{1,0:T(8,128)(2,1)} %get-tuple-element.134.refs_2_), channel_id=1, source_target_pairs={{0,8},{8,0},{16,24},{24,16},{1,9},{9,1},{17,25},{25,17},{2,10},{10... | collective-permute-start | bytes 835592 | tf_op jit(solution)/shard_map/ppermute | solution.py:29
  63.4 9.6 %collective-permute-start.12 = (bf16[64,2048]{1,0:T(8,128)(2,1)}, bf16[64,2048]{1,0:T(8,128)(2,1)}, u32[]{:S(2)}, u32[]{:S(2)}) collective-permute-start(bf16[64,2048]{1,0:T(8,128)(2,1)} %get-tuple-element.129.refs_0_), channel_id=1, source_target_pairs={{0,2},{2,0},{1,3},{3,1},{4,6},{6,4},{5,7},{7,5},{8,10},{10,8},{9,1... | collective-permute-start | bytes 786440 | tf_op jit(solution)/shard_map/ppermute | solution.py:29
  66.3 26.9 %collective-permute-start.17 = (bf16[64,2176]{1,0:T(8,128)(2,1)}, bf16[64,2176]{1,0:T(8,128)(2,1)}, u32[]{:S(2)}, u32[]{:S(2)}) collective-permute-start(bf16[64,2176]{1,0:T(8,128)(2,1)} %get-tuple-element.134.refs_2_), channel_id=1, source_target_pairs={{0,24},{8,16},{16,8},{24,0},{1,25},{9,17},{17,9},{25,1},{2,26},{10... | collective-permute-start | bytes 835592 | tf_op jit(solution)/shard_map/ppermute | solution.py:29
  67.4 25.9 %collective-permute-start.18 = (bf16[64,2176]{1,0:T(8,128)(2,1)}, bf16[64,2176]{1,0:T(8,128)(2,1)}, u32[]{:S(2)}, u32[]{:S(2)}) collective-permute-start(bf16[64,2176]{1,0:T(8,128)(2,1)} %get-tuple-element.134.refs_2_), channel_id=1, source_target_pairs={{0,16},{8,24},{16,0},{24,8},{1,17},{9,25},{17,1},{25,9},{2,18},{10... | collective-permute-start | bytes 835592 | tf_op jit(solution)/shard_map/ppermute | solution.py:29
  89.7 9.3 %collective-permute-start.14 = (bf16[64,2048]{1,0:T(8,128)(2,1)S(1)}, bf16[64,2048]{1,0:T(8,128)(2,1)S(1)}, u32[]{:S(2)}, u32[]{:S(2)}) collective-permute-start(bf16[64,2048]{1,0:T(8,128)(2,1)S(1)} %get-tuple-element.139), channel_id=1, source_target_pairs={{0,2},{2,0},{4,6},{6,4},{1,3},{3,1},{5,7},{7,5},{8,10},{10,8},{12,... | collective-permute-start | bytes 786440 | tf_op jit(solution)/shard_map/ppermute | solution.py:29
  91.5 14.5 %collective-permute-start.15 = (bf16[64,2048]{1,0:T(8,128)(2,1)S(1)}, bf16[64,2048]{1,0:T(8,128)(2,1)S(1)}, u32[]{:S(2)}, u32[]{:S(2)}) collective-permute-start(bf16[64,2048]{1,0:T(8,128)(2,1)S(1)} %get-tuple-element.140), channel_id=1, source_target_pairs={{0,4},{2,6},{4,0},{6,2},{1,5},{3,7},{5,1},{7,3},{8,12},{10,14},{12... | collective-permute-start | bytes 786440 | tf_op jit(solution)/shard_map/ppermute | solution.py:29
  91.5 14.5 %collective-permute-start.16 = (bf16[64,2048]{1,0:T(8,128)(2,1)S(1)}, bf16[64,2048]{1,0:T(8,128)(2,1)S(1)}, u32[]{:S(2)}, u32[]{:S(2)}) collective-permute-start(bf16[64,2048]{1,0:T(8,128)(2,1)S(1)} %get-tuple-element.141), channel_id=1, source_target_pairs={{0,6},{2,4},{4,2},{6,0},{1,7},{3,5},{5,3},{7,1},{8,14},{10,12},{12... | collective-permute-start | bytes 786440 | tf_op jit(solution)/shard_map/ppermute | solution.py:29
  95.4 22.2 %collective-permute-start.19 = (bf16[64,2048]{1,0:T(8,128)(2,1)S(1)}, bf16[64,2048]{1,0:T(8,128)(2,1)S(1)}, u32[]{:S(2)}, u32[]{:S(2)}) collective-permute-start(bf16[64,2048]{1,0:T(8,128)(2,1)S(1)} %get-tuple-element.152), channel_id=1, source_target_pairs={{0,2},{2,0},{4,6},{6,4},{1,3},{3,1},{5,7},{7,5},{8,10},{10,8},{12,... | collective-permute-start | bytes 786440 | tf_op jit(solution)/shard_map/ppermute | solution.py:29
  97.2 20.4 %collective-permute-start.20 = (bf16[64,2048]{1,0:T(8,128)(2,1)S(1)}, bf16[64,2048]{1,0:T(8,128)(2,1)S(1)}, u32[]{:S(2)}, u32[]{:S(2)}) collective-permute-start(bf16[64,2048]{1,0:T(8,128)(2,1)S(1)} %get-tuple-element.153), channel_id=1, source_target_pairs={{0,4},{2,6},{4,0},{6,2},{1,5},{3,7},{5,1},{7,3},{8,12},{10,14},{12... | collective-permute-start | bytes 786440 | tf_op jit(solution)/shard_map/ppermute | solution.py:29
  99.0 18.6 %collective-permute-start.21 = (bf16[64,2048]{1,0:T(8,128)(2,1)S(1)}, bf16[64,2048]{1,0:T(8,128)(2,1)S(1)}, u32[]{:S(2)}, u32[]{:S(2)}) collective-permute-start(bf16[64,2048]{1,0:T(8,128)(2,1)S(1)} %get-tuple-element.154), channel_id=1, source_target_pairs={{0,6},{2,4},{4,2},{6,0},{1,7},{3,5},{5,3},{7,1},{8,14},{10,12},{12... | collective-permute-start | bytes 786440 | tf_op jit(solution)/shard_map/ppermute | solution.py:29
  128.7 7.2 %collective-permute-start.24 = (bf16[32,2048]{1,0:T(8,128)(2,1)S(1)}, bf16[32,2048]{1,0:T(8,128)(2,1)S(1)}, u32[]{:S(2)}, u32[]{:S(2)}) collective-permute-start(bf16[32,2048]{1,0:T(8,128)(2,1)S(1)} %get-tuple-element.171), channel_id=1, source_target_pairs={{0,6},{2,4},{4,2},{6,0},{1,7},{3,5},{5,3},{7,1},{8,14},{10,12},{12... | collective-permute-start | bytes 393224 | tf_op jit(solution)/shard_map/ppermute | solution.py:29
  136.2 6.4 %collective-permute-start.25 = (bf16[32,2048]{1,0:T(8,128)(2,1)S(1)}, bf16[32,2048]{1,0:T(8,128)(2,1)S(1)}, u32[]{:S(2)}, u32[]{:S(2)}) collective-permute-start(bf16[32,2048]{1,0:T(8,128)(2,1)S(1)} %get-tuple-element.173), channel_id=1, source_target_pairs={{0,2},{2,0},{4,6},{6,4},{1,3},{3,1},{5,7},{7,5},{8,10},{10,8},{12,... | collective-permute-start | bytes 393224 | tf_op jit(solution)/shard_map/ppermute | solution.py:29
  136.7 7.3 %collective-permute-start.26 = (bf16[32,2048]{1,0:T(8,128)(2,1)S(1)}, bf16[32,2048]{1,0:T(8,128)(2,1)S(1)}, u32[]{:S(2)}, u32[]{:S(2)}) collective-permute-start(bf16[32,2048]{1,0:T(8,128)(2,1)S(1)} %get-tuple-element.174), channel_id=1, source_target_pairs={{0,4},{2,6},{4,0},{6,2},{1,5},{3,7},{5,1},{7,3},{8,12},{10,14},{12... | collective-permute-start | bytes 393224 | tf_op jit(solution)/shard_map/ppermute | solution.py:29
  138.2 7.3 %collective-permute-start.27 = (bf16[32,2048]{1,0:T(8,128)(2,1)S(1)}, bf16[32,2048]{1,0:T(8,128)(2,1)S(1)}, u32[]{:S(2)}, u32[]{:S(2)}) collective-permute-start(bf16[32,2048]{1,0:T(8,128)(2,1)S(1)} %get-tuple-element.175), channel_id=1, source_target_pairs={{0,6},{2,4},{4,2},{6,0},{1,7},{3,5},{5,3},{7,1},{8,14},{10,12},{12... | collective-permute-start | bytes 393224 | tf_op jit(solution)/shard_map/ppermute | solution.py:29
  139.7 8.4 %collective-permute-start.32 = (bf16[32,2048]{1,0:T(8,128)(2,1)S(1)}, bf16[32,2048]{1,0:T(8,128)(2,1)S(1)}, u32[]{:S(2)}, u32[]{:S(2)}) collective-permute-start(bf16[32,2048]{1,0:T(8,128)(2,1)S(1)} %get-tuple-element.156), channel_id=1, source_target_pairs={{0,2},{2,0},{4,6},{6,4},{1,3},{3,1},{5,7},{7,5},{8,10},{10,8},{12,... | collective-permute-start | bytes 393224 | tf_op jit(solution)/shard_map/ppermute | solution.py:29
  140.1 9.1 %collective-permute-start.33 = (bf16[32,2048]{1,0:T(8,128)(2,1)S(1)}, bf16[32,2048]{1,0:T(8,128)(2,1)S(1)}, u32[]{:S(2)}, u32[]{:S(2)}) collective-permute-start(bf16[32,2048]{1,0:T(8,128)(2,1)S(1)} %get-tuple-element.157), channel_id=1, source_target_pairs={{0,4},{2,6},{4,0},{6,2},{1,5},{3,7},{5,1},{7,3},{8,12},{10,14},{12... | collective-permute-start | bytes 393224 | tf_op jit(solution)/shard_map/ppermute | solution.py:29
  142.5 8.6 %collective-permute-start.34 = (bf16[32,2048]{1,0:T(8,128)(2,1)S(1)}, bf16[32,2048]{1,0:T(8,128)(2,1)S(1)}, u32[]{:S(2)}, u32[]{:S(2)}) collective-permute-start(bf16[32,2048]{1,0:T(8,128)(2,1)S(1)} %get-tuple-element.158), channel_id=1, source_target_pairs={{0,6},{2,4},{4,2},{6,0},{1,7},{3,5},{5,3},{7,1},{8,14},{10,12},{12... | collective-permute-start | bytes 393224 | tf_op jit(solution)/shard_map/ppermute | solution.py:29
  145.8 8.6 %collective-permute-start.28 = (bf16[32,2048]{1,0:T(8,128)(2,1)S(1)}, bf16[32,2048]{1,0:T(8,128)(2,1)S(1)}, u32[]{:S(2)}, u32[]{:S(2)}) collective-permute-start(bf16[32,2048]{1,0:T(8,128)(2,1)S(1)} %get-tuple-element.177), channel_id=1, source_target_pairs={{0,2},{2,0},{4,6},{6,4},{1,3},{3,1},{5,7},{7,5},{8,10},{10,8},{12,... | collective-permute-start | bytes 393224 | tf_op jit(solution)/shard_map/ppermute | solution.py:29
  147.1 8.5 %collective-permute-start.29 = (bf16[32,2048]{1,0:T(8,128)(2,1)S(1)}, bf16[32,2048]{1,0:T(8,128)(2,1)S(1)}, u32[]{:S(2)}, u32[]{:S(2)}) collective-permute-start(bf16[32,2048]{1,0:T(8,128)(2,1)S(1)} %get-tuple-element.178), channel_id=1, source_target_pairs={{0,4},{2,6},{4,0},{6,2},{1,5},{3,7},{5,1},{7,3},{8,12},{10,14},{12... | collective-permute-start | bytes 393224 | tf_op jit(solution)/shard_map/ppermute | solution.py:29
  148.2 13.6 %collective-permute-start.31 = (bf16[64,2048]{1,0:T(8,128)(2,1)}, bf16[64,2048]{1,0:T(8,128)(2,1)S(1)}, u32[]{:S(2)}, u32[]{:S(2)}) collective-permute-start(bf16[64,2048]{1,0:T(8,128)(2,1)} %get-tuple-element.180), channel_id=1, source_target_pairs={{0,2},{2,0},{1,3},{3,1},{4,6},{6,4},{5,7},{7,5},{8,10},{10,8},{9,1... | collective-permute-start | bytes 786440 | tf_op jit(solution)/shard_map/ppermute | solution.py:29
  151.4 10.4 %collective-permute-start.35 = (bf16[64,2048]{1,0:T(8,128)(2,1)S(1)}, bf16[64,2048]{1,0:T(8,128)(2,1)S(1)}, u32[]{:S(2)}, u32[]{:S(2)}) collective-permute-start(bf16[64,2048]{1,0:T(8,128)(2,1)S(1)} %combine.7), channel_id=1, source_target_pairs={{0,8},{8,0},{16,24},{24,16},{1,9},{9,1},{17,25},{25,17},{2,10},{10... | collective-permute-start | bytes 786440 | tf_op jit(solution)/shard_map/ppermute | solution.py:29
  152.1 9.7 %collective-permute-start.36 = (bf16[64,2048]{1,0:T(8,128)(2,1)S(1)}, bf16[64,2048]{1,0:T(8,128)(2,1)S(1)}, u32[]{:S(2)}, u32[]{:S(2)}) collective-permute-start(bf16[64,2048]{1,0:T(8,128)(2,1)S(1)} %combine.4), channel_id=1, source_target_pairs={{0,24},{8,16},{16,8},{24,0},{1,25},{9,17},{17,9},{25,1},{2,26},{10... | collective-permute-start | bytes 786440 | tf_op jit(solution)/shard_map/ppermute | solution.py:29
  154.4 13.3 %collective-permute-start.37 = (bf16[64,2048]{1,0:T(8,128)(2,1)S(1)}, bf16[64,2048]{1,0:T(8,128)(2,1)S(1)}, u32[]{:S(2)}, u32[]{:S(2)}) collective-permute-start(bf16[64,2048]{1,0:T(8,128)(2,1)S(1)} %combine.5), channel_id=1, source_target_pairs={{0,16},{8,24},{16,0},{24,8},{1,17},{9,25},{17,1},{25,9},{2,18},{10... | collective-permute-start | bytes 786440 | tf_op jit(solution)/shard_map/ppermute | solution.py:29
  155.6 5.9 %collective-permute-start.30 = (bf16[32,2048]{1,0:T(8,128)(2,1)S(1)}, bf16[32,2048]{1,0:T(8,128)(2,1)S(1)}, u32[]{:S(2)}, u32[]{:S(2)}) collective-permute-start(bf16[32,2048]{1,0:T(8,128)(2,1)S(1)} %get-tuple-element.179), channel_id=1, source_target_pairs={{0,6},{2,4},{4,2},{6,0},{1,7},{3,5},{5,3},{7,1},{8,14},{10,12},{12... | collective-permute-start | bytes 393224 | tf_op jit(solution)/shard_map/ppermute | solution.py:29
  (57 other events, 646.9 us)

commit v7 on v5

--- a/solution.py
+++ b/solution.py
@@ -12,7 +12,7 @@
 EPSILON = 1e-06
 ROPE_BASE = 10000.0
 GROUPS = ((0, 1), (3, 2))
-BACK = ((1, None), (3, None), (2, 3), (0, 2))
+BACK = ((3, None, None), (2, 3, None), (1, 3, None), (0, 2, 3))
 CHUNK = 512
 EXTRA = 128
 SMALL = pl.CostEstimate(flops=1024, bytes_accessed=1024, transcendentals=0)
@@ -55,7 +55,7 @@
 def attend_kernel(
     info, first, second, gain, weight, cosine, sine, reach, cache, outward, *outs_and_scratch
 ):
-    term, mixed = outs_and_scratch[0:2]
+    term, term_other = outs_and_scratch[0:2]
     fresh = outs_and_scratch[2:4]
     weight_here, cache_here, gain_here, outward_here, sems = outs_and_scratch[4:]
     tree = first.shape[0]
@@ -76,7 +76,7 @@
         for i in range(2)
     ]
     outward_copy = pltpu.make_async_copy(outward, outward_here, sems.at[5])
-    for copy in [gain_copy, *weight_copies, *cache_copies, outward_copy]:
+    for copy in [gain_copy, *weight_copies]:
         copy.start()
 
     wide = jnp.concatenate([first[...], second[...]], axis=0).astype(jnp.float32)
@@ -84,10 +84,13 @@
     gain_copy.wait()
     normed = (wide * lax.rsqrt(power + EPSILON) * gain_here[...]).astype(jnp.bfloat16)
     weight_copies[0].wait()
+    cache_copies[0].start()
     projected = dot(normed[:, :deep], weight_here[:deep])
     weight_copies[1].wait()
+    cache_copies[1].start()
     projected = projected + dot(normed[:, deep:], weight_here[deep:])
     scale = 1.0 / math.sqrt(head_dim)
+    results = []
 
     for i in range(2):
         own = projected[i * tree : (i + 1) * tree]
@@ -123,6 +126,8 @@
         total = jnp.sum(weights, axis=-1, keepdims=True)
         summed = dot(weights.astype(jnp.bfloat16), value_new)
         cache_copies[i].wait()
+        if i == 0:
+            outward_copy.start()
 
         def chunk(j, carry):
             peak, total, summed = carry
@@ -145,12 +150,11 @@
         result = jnp.concatenate(
             [result[h * tree : (h + 1) * tree] for h in range(group)], axis=1
         )
-        if i:
-            mixed[...] = result
-        else:
-            kept = result
+        results.append(result)
     outward_copy.wait()
-    term[...] = dot(kept, outward_here[...])
+    terms = dot(jnp.concatenate(results, axis=0), outward_here[...])
+    term[...] = terms[:tree]
+    term_other[...] = terms[tree:].astype(jnp.bfloat16)
 
 
 def in_vmem():
@@ -184,7 +188,7 @@
         out_specs=[in_vmem()] * 4,
         out_shape=[
             jax.ShapeDtypeStruct((tree, width), jnp.float32),
-            jax.ShapeDtypeStruct((tree, group_columns), jnp.bfloat16),
+            jax.ShapeDtypeStruct((tree, width), jnp.bfloat16),
         ]
         + [jax.ShapeDtypeStruct((tree, pair), jnp.bfloat16)] * 2,
         scratch_shapes=[
@@ -198,37 +202,6 @@
         cost_estimate=SMALL,
         name="attend",
     )(info, first, second, gain, weight, cosine, sine, reach, cache, outward)
-
-
-def project_kernel(term, mixed, outward, out, here, sems):
-    half = here.shape[0] // 2
-    copies = [
-        pltpu.make_async_copy(
-            outward.at[pl.ds(i * half, half)], here.at[pl.ds(i * half, half)], sems.at[i]
-        )
-        for i in range(2)
-    ]
-    for copy in copies:
-        copy.start()
-    total = term[...]
-    for i, copy in enumerate(copies):
-        copy.wait()
-        block = slice(i * half, (i + 1) * half)
-        total = total + dot(mixed[:, block], here[block])
-    out[...] = total.astype(out.dtype)
-
-
-def project(term, mixed, outward, dtype):
-    return pl.pallas_call(
-        project_kernel,
-        in_specs=[in_vmem(), in_vmem(), in_hbm()],
-        out_specs=in_vmem(),
-        out_shape=jax.ShapeDtypeStruct(term.shape, dtype),
-        scratch_shapes=[pltpu.VMEM(outward.shape, jnp.bfloat16), pltpu.SemaphoreType.DMA((2,))],
-        compiler_params=pltpu.CompilerParams(vmem_limit_bytes=60 * 2**20),
-        cost_estimate=SMALL,
-        name="project",
-    )(term, mixed, outward)
 
 
 def silu(values):
@@ -254,8 +227,14 @@
                 pltpu.make_async_copy(inner.at[block], inner_here.at[block], sems.at[base + p])
             )
         copies.append(pltpu.make_async_copy(outer, outer_here, sems.at[base + parts]))
-    for copy in copies:
+    for copy in copies[:2]:
         copy.start()
+
+    def take(number):
+        copies[number].wait()
+        if number + 2 < len(copies):
+            copies[number + 2].start()
+
     for i in range(plane):
         rows[i * each : (i + 1) * each] = pieces[i][...]
     result = None
@@ -263,12 +242,12 @@
         base = n * (parts + 1)
         both = None
         for p in range(parts):
-            copies[base + p].wait()
+            take(base + p)
             term = dot(rows[:, p * deep : (p + 1) * deep], inner_here[p * deep : (p + 1) * deep])
             both = term if both is None else both + term
         half = both.shape[1] // 2
         hidden = (silu(both[:, :half]) * both[:, half:]).astype(jnp.bfloat16)
-        copies[base + parts].wait()
+        take(base + parts)
         term = dot(hidden, outer_here[...]).astype(jnp.bfloat16).astype(jnp.float32)
         result = term if result is None else result + term
     step = each // count
@@ -308,13 +287,19 @@
     outs = refs[side + 6 : 2 * side + 6]
     here, sems = refs[2 * side + 6 :]
     copies = [pltpu.make_async_copy(weights[i], here.at[i], sems.at[i]) for i in range(6)]
-    for copy in copies:
+    for copy in copies[:2]:
         copy.start()
+
+    def take(number):
+        copies[number].wait()
+        if number + 2 < len(copies):
+            copies[number + 2].start()
+
     tree = blocks[0].shape[0]
     rows = jnp.concatenate([block[...] for block in blocks], axis=0)
 
     def turned(i):
-        copies[i].wait()
+        take(i)
         return lax.dot_general(
             rows, here[i], (((1,), (1,)), ((), ())), preferred_element_type=jnp.float32
         )
@@ -323,7 +308,7 @@
     for n in range(2):
         hidden = silu(turned(3 * n))
         hidden = (hidden * turned(3 * n + 1)).astype(jnp.bfloat16)
-        copies[3 * n + 2].wait()
+        take(3 * n + 2)
         term = dot(hidden, here[3 * n + 2])
         result = term if result is None else result + term
     for i in range(side):
@@ -545,10 +530,10 @@
         near_core.append(partner(near[o], "c", 1))
 
     gate_turned, up_turned = shared_gate.T, shared_up.T
-    early, near_core[0] = lax.optimization_barrier(((w_out, expert_out[0]), near_core[0]))
+    early, near_core[0] = lax.optimization_barrier(((gate_turned, expert_out[0]), near_core[0]))
     early = [partner(weight, "c", 1) for weight in early]
     middle, near_core = lax.optimization_barrier(
-        ((gate_turned, up_turned, shared_down), near_core)
+        ((up_turned, shared_down), near_core)
     )
     middle = [partner(weight, "c", 1) for weight in middle]
     near_core, early = lax.optimization_barrier((near_core, early))
@@ -560,7 +545,7 @@
     for o in reversed(range(side)):
         if follow is not None:
             near_core[o], follow = lax.optimization_barrier((near_core[o], follow))
-        own_part, mixed, fresh_own, fresh_other = attend(
+        own_part, other_part, fresh_own, fresh_other = attend(
             info[o],
             near[o],
             near_core[o],
@@ -573,18 +558,20 @@
             w_out,
         )
         fresh[o] = jnp.stack([fresh_own, fresh_other])
-        other = partner(mixed, "c", 1)
+        other = partner(other_part, "c", 1)
         if o == side - 1:
             other, middle, late = lax.optimization_barrier((other, middle, late))
             late = partner(late, "c", 1)
-        terms[o] = project(own_part, other, early[0], jnp.bfloat16 if o else jnp.float32)
+        terms[o] = own_part + other.astype(jnp.float32)
+        if o:
+            terms[o] = terms[o].astype(jnp.bfloat16)
         follow = terms[o]
     others = [partner(terms[o], "x", o) for o in range(1, side)]
     own_term, late = lax.optimization_barrier((terms[0], late))
     resid, normed, payload = finish(own_rows, own_term, others, ffn_gain[None], routes[0])
     inner = [expert_in[0], late]
     outer = [expert_out[0], early[1]]
-    shared_weights = [gate_turned, up_turned, shared_down, *middle]
+    shared_weights = [gate_turned, up_turned, shared_down, early[0], *middle]
     order = me ^ jnp.arange(group_count, dtype=jnp.int32)
     kept = accepted[order][:, :, None] == jnp.arange(tree, dtype=jnp.int32)
     accepted_kv = jnp.einsum(
@@ -625,13 +612,18 @@
         made = experts(pieces, len(ks), inner, outer)
         results.update(zip(ks, made))
     totals = {}
-    for k, after in BACK:
+    landed = {}
+    for k, after, arrived in BACK:
         pieces = results[k]
         if after is not None:
             pieces, totals[after] = lax.optimization_barrier((pieces, totals[after]))
+        if arrived is not None:
+            pieces, landed[arrived] = lax.optimization_barrier((pieces, landed[arrived]))
         back = [partner(pieces[o], PLANE, o) for o in range(plane)]
         totals[k] = combine(spread[k], back, jnp.bfloat16 if k else jnp.float32)
-    parts += [partner(totals[k], "z", k) for k, after in BACK if k]
+        if k:
+            landed[k] = partner(totals[k], "z", k)
+    parts += list(landed.values())
     routed = totals[0]
     hidden_out = final(live[0][:, None], resid, shared, routed, parts)
     return (hidden_out[None], accepted_kv)

time: 158 us -> 149 us (0.943)
  starting transfers between devices: 44.5 us -> 33.9 us
  waiting for transfers between devices: 34.8 us -> 40.5 us
  Pallas kernels: 58.4 us -> 54.1 us
  local copies, waits for them, and re-layouts: 10.6 us -> 8.29 us
  other arithmetic: 4.23 us -> 6.46 us
    ppermute x38 -> x37, starting transfers between devices: 44.5 us -> 33.9 us  [partner(): return lax.ppermute(value, axes, [(i, i ^ offset) for i in range(size)])]
    pallas_call x2 -> x0, Pallas kernels: 7.33 us -> none  [project(): pl.pallas_call(project_kernel, in_specs=[in_vmem(), in_vmem(), in_hbm()],...]
    ppermute x38 -> x37, waiting for transfers between devices: 34.8 us -> 40.5 us  [partner(): return lax.ppermute(value, axes, [(i, i ^ offset) for i in range(size)])]
    unnamed x74 -> x70, local copies, waits for them, and re-layouts: 8.8 us -> 6.48 us
  transfers between devices with their start and end apart: 38 -> 37, of which waited for: 14 -> 15; matrix products, arithmetic and copies ran while one was open for 6% -> 8% of each run, Pallas kernels for 29% -> 27%
where the time goes in v7:
time: 149 us; the launch traced here: 148 us
  Pallas kernels  54.1 us (36%)
  waiting for transfers between devices  40.5 us (27%)
  starting transfers between devices  33.9 us (23%)
  local copies, waits for them, and re-layouts  8.29 us (6%)
  other arithmetic  6.46 us (4%)
  matrix products  3.49 us (2%)
    ppermute x37, waiting for transfers between devices, partner(): return lax.ppermute(value, axes, [(i, i ^ offset) for i in range(size)])  40.5 us
    ppermute x37, starting transfers between devices, partner(): return lax.ppermute(value, axes, [(i, i ^ offset) for i in range(size)])  33.9 us
    pallas_call x2, Pallas kernels, experts(): pl.pallas_call(kernel, in_specs=[in_vmem()] * plane + [in_hbm()] * 4, out...  23.5 us
    pallas_call x2, Pallas kernels, attend(): pl.pallas_call(attend_kernel, in_specs=[pl.BlockSpec(memory_space=pltpu.S...  17.4 us
    pallas_call x1, Pallas kernels, shared_terms(): pl.pallas_call(functools.partial(shared_kernel, side=side), in_specs=[in_...  7.69 us
    unnamed x70, local copies, waits for them, and re-layouts  6.48 us
    pallas_call x2, Pallas kernels, select(): pl.pallas_call(functools.partial(select_kernel, count=count, plane=plane,...  3.3 us
  transfers between devices with their start and end apart: 37, of which 15 were waited for; matrix products, arithmetic and copies ran while one was open for 8% of the time, Pallas kernels for 27%

profile of v7, /device:TPU:0, one launch (start us, length us, event | category | flops | bytes accessed | tf_op | source)
XLA Modules:
  0.0 147.9 jit_solution(10113805453871796893)
XLA Ops:
  0.6 3.0 %collective-permute-start = (bf16[64,2048]{1,0:T(8,128)(2,1)}, bf16[64,2048]{1,0:T(8,128)(2,1)}, u32[]{:S(2)}, u32[]{:S(2)}) collective-permute-start(bf16[64,2048]{1,0:T(8,128)(2,1)} %bitcast.24), channel_id=1, source_target_pairs={{0,2},{2,0},{1,3},{3,1},{4,6},{6,4},{5,7},{7,5},{8,10},{10,8},{9,1... | collective-permute-start | bytes 786440 | tf_op jit(solution)/shard_map/ppermute | solution.py:28
  5.8 1.3 fusion.1
  11.6 3.3 %collective-permute-done.2.second = bf16[64,2048]{1,0:T(8,128)(2,1)S(1)} collective-permute-done((bf16[64,2048]{1,0:T(8,128)(2,1)}, bf16[64,2048]{1,0:T(8,128)(2,1)S(1)}, u32[]{:S(2)}, u32[]{:S(2)}) %collective-permute-start.2) | collective-permute-done | bytes 262176 | tf_op jit(solution)/shard_map/ppermute | solution.py:28
  16.5 8.7 %attend.2 = (f32[64,2048]{1,0:T(8,128)}, bf16[64,2048]{1,0:T(8,128)(2,1)}, bf16[64,256]{1,0:T(8,128)(2,1)}, bf16[64,256]{1,0:T(8,128)(2,1)}) custom-call(s32[4]{0:T(128)} %pad_add_fusion.1.info, bf16[64,2048]{1,0:T(8,128)(2,1)} %collective-permute-done.first, bf16[64,2048]{1,0:T(8,128)(2,1)} %copy-done.21, f32[1,2048]{1,0:T(1,128)} %bitcast.43, ...), custom_call_target="tpu_custom_call" | custom-call | flops 1024 | bytes 1024 | tf_op jit(solution)/shard_map/attend/pallas_call | solution.py:174
  25.4 1.6 %collective-permute-done.5 = bf16[64,2048]{1,0:T(8,128)(2,1)S(1)} collective-permute-done((bf16[64,2048]{1,0:T(8,128)(2,1)}, bf16[64,2048]{1,0:T(8,128)(2,1)S(1)}, u32[]{:S(2)}, u32[]{:S(2)}) %collective-permute-start.5) | collective-permute-done | bytes 262176 | tf_op jit(solution)/shard_map/ppermute | solution.py:28
  28.3 8.7 %attend.3 = (f32[64,2048]{1,0:T(8,128)}, bf16[64,2048]{1,0:T(8,128)(2,1)}, bf16[64,256]{1,0:T(8,128)(2,1)}, bf16[64,256]{1,0:T(8,128)(2,1)}) custom-call(s32[4]{0:T(128)} %pad_add_fusion.info, bf16[64,2048]{1,0:T(8,128)(2,1)} %bitcast.26, bf16[64,2048]{1,0:T(8,128)(2,1)} %copy-done.19, f32[1,2048]{1,0:T(1,128)} %bitcast.44, bf16[2048,768]{1,0:T(8,128)(2,1)} %weight.3, ...), custom_call_target="tpu_custom_call" | custom-call | flops 1024 | bytes 1024 | tf_op jit(solution)/shard_map/attend/pallas_call | solution.py:174
  39.9 6.0 %collective-permute-done.10.refs_0_ = bf16[64,2048]{1,0:T(8,128)(2,1)S(1)} collective-permute-done((bf16[64,2048]{1,0:T(8,128)(2,1)S(1)}, bf16[64,2048]{1,0:T(8,128)(2,1)S(1)}, u32[]{:S(2)}, u32[]{:S(2)}) %collective-permute-start.10) | collective-permute-done | bytes 262176 | tf_op jit(solution)/shard_map/ppermute | solution.py:28
  46.6 4.2 %collective-permute-start.16 = (bf16[64,2176]{1,0:T(8,128)(2,1)S(1)}, bf16[64,2176]{1,0:T(8,128)(2,1)S(1)}, u32[]{:S(2)}, u32[]{:S(2)}) collective-permute-start(bf16[64,2176]{1,0:T(8,128)(2,1)S(1)} %get-tuple-element.119.refs_2_), channel_id=1, source_target_pairs={{0,24},{8,16},{16,8},{24,0},{1,25},{9,17},{17,9},{25,1},{2,26},{10... | collective-permute-start | bytes 835592 | tf_op jit(solution)/shard_map/ppermute | solution.py:28
  51.1 2.7 %collective-permute-done.11.refs_1_ = bf16[64,2048]{1,0:T(8,128)(2,1)S(1)} collective-permute-done((bf16[64,2048]{1,0:T(8,128)(2,1)S(1)}, bf16[64,2048]{1,0:T(8,128)(2,1)S(1)}, u32[]{:S(2)}, u32[]{:S(2)}) %collective-permute-start.11) | collective-permute-done | bytes 262176 | tf_op jit(solution)/shard_map/ppermute | solution.py:28
  54.5 7.7 %shared.1 = (f32[64,2048]{1,0:T(8,128)}, bf16[64,2048]{1,0:T(8,128)(2,1)}) custom-call(bf16[64,2048]{1,0:T(8,128)(2,1)} %copy-done.5, bf16[64,2048]{1,0:T(8,128)(2,1)} %copy-done.20, bf16[352,2048]{1,0:T(8,128)(2,1)} %bitcast.39, bf16[352,2048]{1,0:T(8,128)(2,1)} %bitcast.41, bf16[352,2048]{1,0:T(8,128)(2,1)} %refs_4_.1, bf16[352,2048]{1,0:T(8,128)(2,1)} %copy-done.12, ...), custom_call_target="tpu_custom_call" | custom-call | flops 1024 | bytes 1024 | tf_op jit(solution)/shard_map/shared/pallas_call | solution.py:322
  62.2 1.7 %select.2 = (bf16[64,2048]{1,0:T(8,128)(2,1)S(1)}, bf16[64,2048]{1,0:T(8,128)(2,1)S(1)}, bf16[64,2048]{1,0:T(8,128)(2,1)S(1)}, bf16[64,2048]{1,0:T(8,128)(2,1)S(...) custom-call(s32[4]{0:T(128)S(1)} %xor_add_fusion.refs_0_, bf16[2048,16]{1,0:T(8,128)(2,1)S(1)} %copy.29.refs_1_, ...), custom_call_target="tpu_custom_call" | custom-call | flops 1024 | bytes 1024 | tf_op jit(solution)/shard_map/select/pallas_call | solution.py:429
  65.6 2.5 %collective-permute-start.15 = (bf16[64,2048]{1,0:T(8,128)(2,1)S(1)}, bf16[64,2048]{1,0:T(8,128)(2,1)S(1)}, u32[]{:S(2)}, u32[]{:S(2)}) collective-permute-start(bf16[64,2048]{1,0:T(8,128)(2,1)S(1)} %get-tuple-element.126), channel_id=1, source_target_pairs={{0,6},{2,4},{4,2},{6,0},{1,7},{3,5},{5,3},{7,1},{8,14},{10,12},{12... | collective-permute-start | bytes 786440 | tf_op jit(solution)/shard_map/ppermute | solution.py:28
  68.1 5.3 %collective-permute-done.17.refs_3_ = bf16[64,2176]{1,0:T(8,128)(2,1)S(1)} collective-permute-done((bf16[64,2176]{1,0:T(8,128)(2,1)S(1)}, bf16[64,2176]{1,0:T(8,128)(2,1)S(1)}, u32[]{:S(2)}, u32[]{:S(2)}) %collective-permute-start.17) | collective-permute-done | bytes 278560 | tf_op jit(solution)/shard_map/ppermute | solution.py:28
  73.4 1.6 %select.3 = (bf16[64,2048]{1,0:T(8,128)(2,1)S(1)}, bf16[64,2048]{1,0:T(8,128)(2,1)S(1)}, bf16[64,2048]{1,0:T(8,128)(2,1)S(1)}, bf16[64,2048]{1,0:T(8,128)(2,1)S(...) custom-call(s32[4]{0:T(128)S(1)} %xor_add_fusion.refs_0_, bf16[2048,16]{1,0:T(8,128)(2,1)S(1)} %copy.29.refs_1_, ...), custom_call_target="tpu_custom_call" | custom-call | flops 1024 | bytes 1024 | tf_op jit(solution)/shard_map/select/pallas_call | solution.py:429
  75.1 1.6 %collective-permute-start.18 = (bf16[64,2048]{1,0:T(8,128)(2,1)S(1)}, bf16[64,2048]{1,0:T(8,128)(2,1)S(1)}, u32[]{:S(2)}, u32[]{:S(2)}) collective-permute-start(bf16[64,2048]{1,0:T(8,128)(2,1)S(1)} %get-tuple-element.135), channel_id=1, source_target_pairs={{0,2},{2,0},{4,6},{6,4},{1,3},{3,1},{5,7},{7,5},{8,10},{10,8},{12,... | collective-permute-start | bytes 786440 | tf_op jit(solution)/shard_map/ppermute | solution.py:28
  76.7 2.5 %collective-permute-start.19 = (bf16[64,2048]{1,0:T(8,128)(2,1)S(1)}, bf16[64,2048]{1,0:T(8,128)(2,1)S(1)}, u32[]{:S(2)}, u32[]{:S(2)}) collective-permute-start(bf16[64,2048]{1,0:T(8,128)(2,1)S(1)} %get-tuple-element.136), channel_id=1, source_target_pairs={{0,4},{2,6},{4,0},{6,2},{1,5},{3,7},{5,1},{7,3},{8,12},{10,14},{12... | collective-permute-start | bytes 786440 | tf_op jit(solution)/shard_map/ppermute | solution.py:28
  80.0 11.6 %expert.2 = (bf16[32,2048]{1,0:T(8,128)(2,1)}, bf16[32,2048]{1,0:T(8,128)(2,1)}, bf16[32,2048]{1,0:T(8,128)(2,1)}, bf16[32,2048]{1,0:T(8,128)(2,1)}, bf16[32,204...) custom-call(bf16[64,2048]{1,0:T(8,128)(2,1)} %copy-done.4, ...), custom_call_target="tpu_custom_call" | custom-call | flops 1024 | bytes 1024 | tf_op jit(solution)/shard_map/expert/pallas_call | solution.py:269
  92.6 11.9 %expert.3 = (bf16[32,2048]{1,0:T(8,128)(2,1)}, bf16[32,2048]{1,0:T(8,128)(2,1)}, bf16[32,2048]{1,0:T(8,128)(2,1)}, bf16[32,2048]{1,0:T(8,128)(2,1)}, bf16[32,204...) custom-call(bf16[64,2048]{1,0:T(8,128)(2,1)} %copy-done.3, ...), custom_call_target="tpu_custom_call" | custom-call | flops 1024 | bytes 1024 | tf_op jit(solution)/shard_map/expert/pallas_call | solution.py:269
  104.5 1.5 %collective-permute-start.21 = (bf16[32,2048]{1,0:T(8,128)(2,1)}, bf16[32,2048]{1,0:T(8,128)(2,1)S(1)}, u32[]{:S(2)}, u32[]{:S(2)}) collective-permute-start(bf16[32,2048]{1,0:T(8,128)(2,1)} %get-tuple-element.152), channel_id=1, source_target_pairs={{0,2},{2,0},{4,6},{6,4},{1,3},{3,1},{5,7},{7,5},{8,10},{10,8},{12,... | collective-permute-start | bytes 393224 | tf_op jit(solution)/shard_map/ppermute | solution.py:28
  106.1 2.0 %collective-permute-start.22 = (bf16[32,2048]{1,0:T(8,128)(2,1)}, bf16[32,2048]{1,0:T(8,128)(2,1)S(1)}, u32[]{:S(2)}, u32[]{:S(2)}) collective-permute-start(bf16[32,2048]{1,0:T(8,128)(2,1)} %get-tuple-element.153), channel_id=1, source_target_pairs={{0,4},{2,6},{4,0},{6,2},{1,5},{3,7},{5,1},{7,3},{8,12},{10,14},{12... | collective-permute-start | bytes 393224 | tf_op jit(solution)/shard_map/ppermute | solution.py:28
  108.1 2.1 %collective-permute-done.21.refs_1_ = bf16[32,2048]{1,0:T(8,128)(2,1)S(1)} collective-permute-done((bf16[32,2048]{1,0:T(8,128)(2,1)}, bf16[32,2048]{1,0:T(8,128)(2,1)S(1)}, u32[]{:S(2)}, u32[]{:S(2)}) %collective-permute-start.21) | collective-permute-done | bytes 131104 | tf_op jit(solution)/shard_map/ppermute | solution.py:28
  110.2 2.1 %collective-permute-done.22.refs_2_ = bf16[32,2048]{1,0:T(8,128)(2,1)S(1)} collective-permute-done((bf16[32,2048]{1,0:T(8,128)(2,1)}, bf16[32,2048]{1,0:T(8,128)(2,1)S(1)}, u32[]{:S(2)}, u32[]{:S(2)}) %collective-permute-start.22) | collective-permute-done | bytes 131104 | tf_op jit(solution)/shard_map/ppermute | solution.py:28
  112.2 1.8 %collective-permute-done.23.refs_3_ = bf16[32,2048]{1,0:T(8,128)(2,1)S(1)} collective-permute-done((bf16[32,2048]{1,0:T(8,128)(2,1)}, bf16[32,2048]{1,0:T(8,128)(2,1)S(1)}, u32[]{:S(2)}, u32[]{:S(2)}) %collective-permute-start.23) | collective-permute-done | bytes 131104 | tf_op jit(solution)/shard_map/ppermute | solution.py:28
  115.2 2.7 %collective-permute-start.27 = (bf16[64,2048]{1,0:T(8,128)(2,1)S(1)}, bf16[64,2048]{1,0:T(8,128)(2,1)S(1)}, u32[]{:S(2)}, u32[]{:S(2)}) collective-permute-start(bf16[64,2048]{1,0:T(8,128)(2,1)S(1)} %combine.4), channel_id=1, source_target_pairs={{0,24},{8,16},{16,8},{24,0},{1,25},{9,17},{17,9},{25,1},{2,26},{10... | collective-permute-start | bytes 786440 | tf_op jit(solution)/shard_map/ppermute | solution.py:28
  119.2 2.2 %collective-permute-start.26 = (bf16[32,2048]{1,0:T(8,128)(2,1)}, bf16[32,2048]{1,0:T(8,128)(2,1)S(1)}, u32[]{:S(2)}, u32[]{:S(2)}) collective-permute-start(bf16[32,2048]{1,0:T(8,128)(2,1)} %get-tuple-element.158), channel_id=1, source_target_pairs={{0,6},{2,4},{4,2},{6,0},{1,7},{3,5},{5,3},{7,1},{8,14},{10,12},{12... | collective-permute-start | bytes 393224 | tf_op jit(solution)/shard_map/ppermute | solution.py:28
  122.0 1.5 %collective-permute-done.24.refs_1_ = bf16[32,2048]{1,0:T(8,128)(2,1)S(1)} collective-permute-done((bf16[32,2048]{1,0:T(8,128)(2,1)}, bf16[32,2048]{1,0:T(8,128)(2,1)S(1)}, u32[]{:S(2)}, u32[]{:S(2)}) %collective-permute-start.24) | collective-permute-done | bytes 131104 | tf_op jit(solution)/shard_map/ppermute | solution.py:28
  123.6 3.0 %collective-permute-done.25.refs_2_ = bf16[32,2048]{1,0:T(8,128)(2,1)S(1)} collective-permute-done((bf16[32,2048]{1,0:T(8,128)(2,1)}, bf16[32,2048]{1,0:T(8,128)(2,1)S(1)}, u32[]{:S(2)}, u32[]{:S(2)}) %collective-permute-start.25) | collective-permute-done | bytes 131104 | tf_op jit(solution)/shard_map/ppermute | solution.py:28
  127.8 1.2 collective-permute-start.28
  129.9 4.1 %collective-permute-done.35.refs_3_ = bf16[32,2048]{1,0:T(8,128)(2,1)S(1)} collective-permute-done((bf16[32,2048]{1,0:T(8,128)(2,1)S(1)}, bf16[32,2048]{1,0:T(8,128)(2,1)S(1)}, u32[]{:S(2)}, u32[]{:S(2)}) %collective-permute-start.35) | collective-permute-done | bytes 131104 | tf_op jit(solution)/shard_map/ppermute | solution.py:28
  134.2 2.5 %collective-permute-start.36 = (bf16[64,2048]{1,0:T(8,128)(2,1)S(1)}, bf16[64,2048]{1,0:T(8,128)(2,1)S(1)}, u32[]{:S(2)}, u32[]{:S(2)}) collective-permute-start(bf16[64,2048]{1,0:T(8,128)(2,1)S(1)} %combine.7), channel_id=1, source_target_pairs={{0,8},{8,0},{16,24},{24,16},{1,9},{9,1},{17,25},{25,17},{2,10},{10... | collective-permute-start | bytes 786440 | tf_op jit(solution)/shard_map/ppermute | solution.py:28
  140.9 2.9 %collective-permute-done.29.refs_2_ = bf16[32,2048]{1,0:T(8,128)(2,1)S(1)} collective-permute-done((bf16[32,2048]{1,0:T(8,128)(2,1)S(1)}, bf16[32,2048]{1,0:T(8,128)(2,1)S(1)}, u32[]{:S(2)}, u32[]{:S(2)}) %collective-permute-start.29) | collective-permute-done | bytes 131104 | tf_op jit(solution)/shard_map/ppermute | solution.py:28
  144.1 2.7 %collective-permute-done.32.refs_2_ = bf16[64,2048]{1,0:T(8,128)(2,1)S(1)} collective-permute-done((bf16[64,2048]{1,0:T(8,128)(2,1)S(1)}, bf16[64,2048]{1,0:T(8,128)(2,1)S(1)}, u32[]{:S(2)}, u32[]{:S(2)}) %collective-permute-start.32) | collective-permute-done | bytes 262176 | tf_op jit(solution)/shard_map/ppermute | solution.py:28
  (147 shorter events, 28.6 us)
Async XLA Ops:
  0.6 10.5 %collective-permute-start = (bf16[64,2048]{1,0:T(8,128)(2,1)}, bf16[64,2048]{1,0:T(8,128)(2,1)}, u32[]{:S(2)}, u32[]{:S(2)}) collective-permute-start(bf16[64,2048]{1,0:T(8,128)(2,1)} %bitcast.24), channel_id=1, source_target_pairs={{0,2},{2,0},{1,3},{3,1},{4,6},{6,4},{5,7},{7,5},{8,10},{10,8},{9,1... | collective-permute-start | bytes 786440 | tf_op jit(solution)/shard_map/ppermute | solution.py:28
  5.4 10.0 %collective-permute-start.4 = (bf16[704,2048]{1,0:T(8,128)(2,1)}, bf16[704,2048]{1,0:T(8,128)(2,1)S(1)}, u32[]{:S(2)}, u32[]{:S(2)}) collective-permute-start(bf16[704,2048]{1,0:T(8,128)(2,1)} %bitcast.35), channel_id=1, source_target_pairs={{0,1},{1,0},{2,3},{3,2},{4,5},{5,4},{6,7},{7,6},{8,9},{9,8},{10,11... | collective-permute-start | bytes 8650760 | tf_op jit(solution)/shard_map/ppermute | solution.py:28
  14.9 10.5 %collective-permute-start.6 = (bf16[352,2048]{1,0:T(8,128)(2,1)}, bf16[352,2048]{1,0:T(8,128)(2,1)}, u32[]{:S(2)}, u32[]{:S(2)}) collective-permute-start(bf16[352,2048]{1,0:T(8,128)(2,1)} %bitcast.40), channel_id=1, source_target_pairs={{0,1},{1,0},{2,3},{3,2},{4,5},{5,4},{6,7},{7,6},{8,9},{9,8},{10,11... | collective-permute-start | bytes 4325384 | tf_op jit(solution)/shard_map/ppermute | solution.py:28
  15.0 10.4 %collective-permute-start.7 = (bf16[352,2048]{1,0:T(8,128)(2,1)}, bf16[352,2048]{1,0:T(8,128)(2,1)}, u32[]{:S(2)}, u32[]{:S(2)}) collective-permute-start(bf16[352,2048]{1,0:T(8,128)(2,1)} %refs_4_.1), channel_id=1, source_target_pairs={{0,1},{1,0},{2,3},{3,2},{4,5},{5,4},{6,7},{7,6},{8,9},{9,8},{10,11... | collective-permute-start | bytes 4325384 | tf_op jit(solution)/shard_map/ppermute | solution.py:28
  27.0 12.9 %collective-permute-start.9 = (bf16[2048,1408]{1,0:T(8,128)(2,1)}, bf16[2048,1408]{1,0:T(8,128)(2,1)}, u32[]{:S(2)}, u32[]{:S(2)}) collective-permute-start(bf16[2048,1408]{1,0:T(8,128)(2,1)} %bitcast.30), channel_id=1, source_target_pairs={{0,1},{1,0},{2,3},{3,2},{4,5},{5,4},{6,7},{7,6},{8,9},{9,8},{10,11... | collective-permute-start | bytes 17301512 | tf_op jit(solution)/shard_map/ppermute | solution.py:28
  37.5 8.4 %collective-permute-start.10 = (bf16[64,2048]{1,0:T(8,128)(2,1)S(1)}, bf16[64,2048]{1,0:T(8,128)(2,1)S(1)}, u32[]{:S(2)}, u32[]{:S(2)}) collective-permute-start(bf16[64,2048]{1,0:T(8,128)(2,1)S(1)} %add_convert_fusion), channel_id=1, source_target_pairs={{0,2},{2,0},{1,3},{3,1},{4,6},{6,4},{5,7},{7,5},{8,10},{10,8},{9,1... | collective-permute-start | bytes 786440 | tf_op jit(solution)/shard_map/ppermute | solution.py:28
  46.1 16.1 %collective-permute-start.12 = (bf16[64,2176]{1,0:T(8,128)(2,1)S(1)}, bf16[64,2176]{1,0:T(8,128)(2,1)S(1)}, u32[]{:S(2)}, u32[]{:S(2)}) collective-permute-start(bf16[64,2176]{1,0:T(8,128)(2,1)S(1)} %get-tuple-element.119.refs_2_), channel_id=1, source_target_pairs={{0,8},{8,0},{16,24},{24,16},{1,9},{9,1},{17,25},{25,17},{2,10},{10... | collective-permute-start | bytes 835592 | tf_op jit(solution)/shard_map/ppermute | solution.py:28
  46.2 7.6 %collective-permute-start.11 = (bf16[64,2048]{1,0:T(8,128)(2,1)S(1)}, bf16[64,2048]{1,0:T(8,128)(2,1)S(1)}, u32[]{:S(2)}, u32[]{:S(2)}) collective-permute-start(bf16[64,2048]{1,0:T(8,128)(2,1)S(1)} %get-tuple-element.114.refs_0_), channel_id=1, source_target_pairs={{0,2},{2,0},{1,3},{3,1},{4,6},{6,4},{5,7},{7,5},{8,10},{10,8},{9,1... | collective-permute-start | bytes 786440 | tf_op jit(solution)/shard_map/ppermute | solution.py:28
  46.6 21.5 %collective-permute-start.16 = (bf16[64,2176]{1,0:T(8,128)(2,1)S(1)}, bf16[64,2176]{1,0:T(8,128)(2,1)S(1)}, u32[]{:S(2)}, u32[]{:S(2)}) collective-permute-start(bf16[64,2176]{1,0:T(8,128)(2,1)S(1)} %get-tuple-element.119.refs_2_), channel_id=1, source_target_pairs={{0,24},{8,16},{16,8},{24,0},{1,25},{9,17},{17,9},{25,1},{2,26},{10... | collective-permute-start | bytes 835592 | tf_op jit(solution)/shard_map/ppermute | solution.py:28
  50.8 22.6 %collective-permute-start.17 = (bf16[64,2176]{1,0:T(8,128)(2,1)S(1)}, bf16[64,2176]{1,0:T(8,128)(2,1)S(1)}, u32[]{:S(2)}, u32[]{:S(2)}) collective-permute-start(bf16[64,2176]{1,0:T(8,128)(2,1)S(1)} %get-tuple-element.119.refs_2_), channel_id=1, source_target_pairs={{0,16},{8,24},{16,0},{24,8},{1,17},{9,25},{17,1},{25,9},{2,18},{10... | collective-permute-start | bytes 835592 | tf_op jit(solution)/shard_map/ppermute | solution.py:28
  64.6 14.5 %collective-permute-start.13 = (bf16[64,2048]{1,0:T(8,128)(2,1)S(1)}, bf16[64,2048]{1,0:T(8,128)(2,1)S(1)}, u32[]{:S(2)}, u32[]{:S(2)}) collective-permute-start(bf16[64,2048]{1,0:T(8,128)(2,1)S(1)} %get-tuple-element.124), channel_id=1, source_target_pairs={{0,2},{2,0},{4,6},{6,4},{1,3},{3,1},{5,7},{7,5},{8,10},{10,8},{12,... | collective-permute-start | bytes 786440 | tf_op jit(solution)/shard_map/ppermute | solution.py:28
  65.1 14.1 %collective-permute-start.14 = (bf16[64,2048]{1,0:T(8,128)(2,1)S(1)}, bf16[64,2048]{1,0:T(8,128)(2,1)S(1)}, u32[]{:S(2)}, u32[]{:S(2)}) collective-permute-start(bf16[64,2048]{1,0:T(8,128)(2,1)S(1)} %get-tuple-element.125), channel_id=1, source_target_pairs={{0,4},{2,6},{4,0},{6,2},{1,5},{3,7},{5,1},{7,3},{8,12},{10,14},{12... | collective-permute-start | bytes 786440 | tf_op jit(solution)/shard_map/ppermute | solution.py:28
  65.6 13.6 %collective-permute-start.15 = (bf16[64,2048]{1,0:T(8,128)(2,1)S(1)}, bf16[64,2048]{1,0:T(8,128)(2,1)S(1)}, u32[]{:S(2)}, u32[]{:S(2)}) collective-permute-start(bf16[64,2048]{1,0:T(8,128)(2,1)S(1)} %get-tuple-element.126), channel_id=1, source_target_pairs={{0,6},{2,4},{4,2},{6,0},{1,7},{3,5},{5,3},{7,1},{8,14},{10,12},{12... | collective-permute-start | bytes 786440 | tf_op jit(solution)/shard_map/ppermute | solution.py:28
  75.1 16.5 %collective-permute-start.18 = (bf16[64,2048]{1,0:T(8,128)(2,1)S(1)}, bf16[64,2048]{1,0:T(8,128)(2,1)S(1)}, u32[]{:S(2)}, u32[]{:S(2)}) collective-permute-start(bf16[64,2048]{1,0:T(8,128)(2,1)S(1)} %get-tuple-element.135), channel_id=1, source_target_pairs={{0,2},{2,0},{4,6},{6,4},{1,3},{3,1},{5,7},{7,5},{8,10},{10,8},{12,... | collective-permute-start | bytes 786440 | tf_op jit(solution)/shard_map/ppermute | solution.py:28
  76.7 15.0 %collective-permute-start.19 = (bf16[64,2048]{1,0:T(8,128)(2,1)S(1)}, bf16[64,2048]{1,0:T(8,128)(2,1)S(1)}, u32[]{:S(2)}, u32[]{:S(2)}) collective-permute-start(bf16[64,2048]{1,0:T(8,128)(2,1)S(1)} %get-tuple-element.136), channel_id=1, source_target_pairs={{0,4},{2,6},{4,0},{6,2},{1,5},{3,7},{5,1},{7,3},{8,12},{10,14},{12... | collective-permute-start | bytes 786440 | tf_op jit(solution)/shard_map/ppermute | solution.py:28
  79.1 12.5 %collective-permute-start.20 = (bf16[64,2048]{1,0:T(8,128)(2,1)S(1)}, bf16[64,2048]{1,0:T(8,128)(2,1)S(1)}, u32[]{:S(2)}, u32[]{:S(2)}) collective-permute-start(bf16[64,2048]{1,0:T(8,128)(2,1)S(1)} %get-tuple-element.137), channel_id=1, source_target_pairs={{0,6},{2,4},{4,2},{6,0},{1,7},{3,5},{5,3},{7,1},{8,14},{10,12},{12... | collective-permute-start | bytes 786440 | tf_op jit(solution)/shard_map/ppermute | solution.py:28
  104.5 5.6 %collective-permute-start.21 = (bf16[32,2048]{1,0:T(8,128)(2,1)}, bf16[32,2048]{1,0:T(8,128)(2,1)S(1)}, u32[]{:S(2)}, u32[]{:S(2)}) collective-permute-start(bf16[32,2048]{1,0:T(8,128)(2,1)} %get-tuple-element.152), channel_id=1, source_target_pairs={{0,2},{2,0},{4,6},{6,4},{1,3},{3,1},{5,7},{7,5},{8,10},{10,8},{12,... | collective-permute-start | bytes 393224 | tf_op jit(solution)/shard_map/ppermute | solution.py:28
  106.1 6.2 %collective-permute-start.22 = (bf16[32,2048]{1,0:T(8,128)(2,1)}, bf16[32,2048]{1,0:T(8,128)(2,1)S(1)}, u32[]{:S(2)}, u32[]{:S(2)}) collective-permute-start(bf16[32,2048]{1,0:T(8,128)(2,1)} %get-tuple-element.153), channel_id=1, source_target_pairs={{0,4},{2,6},{4,0},{6,2},{1,5},{3,7},{5,1},{7,3},{8,12},{10,14},{12... | collective-permute-start | bytes 393224 | tf_op jit(solution)/shard_map/ppermute | solution.py:28
  108.0 6.1 %collective-permute-start.23 = (bf16[32,2048]{1,0:T(8,128)(2,1)}, bf16[32,2048]{1,0:T(8,128)(2,1)S(1)}, u32[]{:S(2)}, u32[]{:S(2)}) collective-permute-start(bf16[32,2048]{1,0:T(8,128)(2,1)} %get-tuple-element.154), channel_id=1, source_target_pairs={{0,6},{2,4},{4,2},{6,0},{1,7},{3,5},{5,3},{7,1},{8,14},{10,12},{12... | collective-permute-start | bytes 393224 | tf_op jit(solution)/shard_map/ppermute | solution.py:28
  115.2 12.6 %collective-permute-start.27 = (bf16[64,2048]{1,0:T(8,128)(2,1)S(1)}, bf16[64,2048]{1,0:T(8,128)(2,1)S(1)}, u32[]{:S(2)}, u32[]{:S(2)}) collective-permute-start(bf16[64,2048]{1,0:T(8,128)(2,1)S(1)} %combine.4), channel_id=1, source_target_pairs={{0,24},{8,16},{16,8},{24,0},{1,25},{9,17},{17,9},{25,1},{2,26},{10... | collective-permute-start | bytes 786440 | tf_op jit(solution)/shard_map/ppermute | solution.py:28
  117.9 5.5 %collective-permute-start.24 = (bf16[32,2048]{1,0:T(8,128)(2,1)}, bf16[32,2048]{1,0:T(8,128)(2,1)S(1)}, u32[]{:S(2)}, u32[]{:S(2)}) collective-permute-start(bf16[32,2048]{1,0:T(8,128)(2,1)} %get-tuple-element.156), channel_id=1, source_target_pairs={{0,2},{2,0},{4,6},{6,4},{1,3},{3,1},{5,7},{7,5},{8,10},{10,8},{12,... | collective-permute-start | bytes 393224 | tf_op jit(solution)/shard_map/ppermute | solution.py:28
  118.5 8.2 %collective-permute-start.25 = (bf16[32,2048]{1,0:T(8,128)(2,1)}, bf16[32,2048]{1,0:T(8,128)(2,1)S(1)}, u32[]{:S(2)}, u32[]{:S(2)}) collective-permute-start(bf16[32,2048]{1,0:T(8,128)(2,1)} %get-tuple-element.157), channel_id=1, source_target_pairs={{0,4},{2,6},{4,0},{6,2},{1,5},{3,7},{5,1},{7,3},{8,12},{10,14},{12... | collective-permute-start | bytes 393224 | tf_op jit(solution)/shard_map/ppermute | solution.py:28
  119.2 7.5 %collective-permute-start.26 = (bf16[32,2048]{1,0:T(8,128)(2,1)}, bf16[32,2048]{1,0:T(8,128)(2,1)S(1)}, u32[]{:S(2)}, u32[]{:S(2)}) collective-permute-start(bf16[32,2048]{1,0:T(8,128)(2,1)} %get-tuple-element.158), channel_id=1, source_target_pairs={{0,6},{2,4},{4,2},{6,0},{1,7},{3,5},{5,3},{7,1},{8,14},{10,12},{12... | collective-permute-start | bytes 393224 | tf_op jit(solution)/shard_map/ppermute | solution.py:28
  121.4 8.5 %collective-permute-start.33 = (bf16[32,2048]{1,0:T(8,128)(2,1)S(1)}, bf16[32,2048]{1,0:T(8,128)(2,1)S(1)}, u32[]{:S(2)}, u32[]{:S(2)}) collective-permute-start(bf16[32,2048]{1,0:T(8,128)(2,1)S(1)} %copy-done.31), channel_id=1, source_target_pairs={{0,2},{2,0},{4,6},{6,4},{1,3},{3,1},{5,7},{7,5},{8,10},{10,8},{12,... | collective-permute-start | bytes 393224 | tf_op jit(solution)/shard_map/ppermute | solution.py:28
  123.5 6.5 %collective-permute-start.34 = (bf16[32,2048]{1,0:T(8,128)(2,1)S(1)}, bf16[32,2048]{1,0:T(8,128)(2,1)S(1)}, u32[]{:S(2)}, u32[]{:S(2)}) collective-permute-start(bf16[32,2048]{1,0:T(8,128)(2,1)S(1)} %copy-done.30), channel_id=1, source_target_pairs={{0,4},{2,6},{4,0},{6,2},{1,5},{3,7},{5,1},{7,3},{8,12},{10,14},{12... | collective-permute-start | bytes 393224 | tf_op jit(solution)/shard_map/ppermute | solution.py:28
  126.7 7.3 %collective-permute-start.35 = (bf16[32,2048]{1,0:T(8,128)(2,1)S(1)}, bf16[32,2048]{1,0:T(8,128)(2,1)S(1)}, u32[]{:S(2)}, u32[]{:S(2)}) collective-permute-start(bf16[32,2048]{1,0:T(8,128)(2,1)S(1)} %copy-done.29), channel_id=1, source_target_pairs={{0,6},{2,4},{4,2},{6,0},{1,7},{3,5},{5,3},{7,1},{8,14},{10,12},{12... | collective-permute-start | bytes 393224 | tf_op jit(solution)/shard_map/ppermute | solution.py:28
  127.8 10.0 %collective-permute-start.28 = (bf16[32,2048]{1,0:T(8,128)(2,1)S(1)}, bf16[32,2048]{1,0:T(8,128)(2,1)S(1)}, u32[]{:S(2)}, u32[]{:S(2)}) collective-permute-start(bf16[32,2048]{1,0:T(8,128)(2,1)S(1)} %copy-done.28), channel_id=1, source_target_pairs={{0,2},{2,0},{4,6},{6,4},{1,3},{3,1},{5,7},{7,5},{8,10},{10,8},{12,... | collective-permute-start | bytes 393224 | tf_op jit(solution)/shard_map/ppermute | solution.py:28
  129.0 15.0 %collective-permute-start.31 = (bf16[64,2048]{1,0:T(8,128)(2,1)S(1)}, bf16[64,2048]{1,0:T(8,128)(2,1)S(1)}, u32[]{:S(2)}, u32[]{:S(2)}) collective-permute-start(bf16[64,2048]{1,0:T(8,128)(2,1)S(1)} %copy-done.25), channel_id=1, source_target_pairs={{0,2},{2,0},{1,3},{3,1},{4,6},{6,4},{5,7},{7,5},{8,10},{10,8},{9,1... | collective-permute-start | bytes 786440 | tf_op jit(solution)/shard_map/ppermute | solution.py:28
  134.2 9.8 %collective-permute-start.36 = (bf16[64,2048]{1,0:T(8,128)(2,1)S(1)}, bf16[64,2048]{1,0:T(8,128)(2,1)S(1)}, u32[]{:S(2)}, u32[]{:S(2)}) collective-permute-start(bf16[64,2048]{1,0:T(8,128)(2,1)S(1)} %combine.7), channel_id=1, source_target_pairs={{0,8},{8,0},{16,24},{24,16},{1,9},{9,1},{17,25},{25,17},{2,10},{10... | collective-permute-start | bytes 786440 | tf_op jit(solution)/shard_map/ppermute | solution.py:28
  136.7 10.1 %collective-permute-start.32 = (bf16[64,2048]{1,0:T(8,128)(2,1)S(1)}, bf16[64,2048]{1,0:T(8,128)(2,1)S(1)}, u32[]{:S(2)}, u32[]{:S(2)}) collective-permute-start(bf16[64,2048]{1,0:T(8,128)(2,1)S(1)} %combine.5), channel_id=1, source_target_pairs={{0,16},{8,24},{16,0},{24,8},{1,17},{9,25},{17,1},{25,9},{2,18},{10... | collective-permute-start | bytes 786440 | tf_op jit(solution)/shard_map/ppermute | solution.py:28
  137.4 6.4 %collective-permute-start.29 = (bf16[32,2048]{1,0:T(8,128)(2,1)S(1)}, bf16[32,2048]{1,0:T(8,128)(2,1)S(1)}, u32[]{:S(2)}, u32[]{:S(2)}) collective-permute-start(bf16[32,2048]{1,0:T(8,128)(2,1)S(1)} %copy-done.27), channel_id=1, source_target_pairs={{0,4},{2,6},{4,0},{6,2},{1,5},{3,7},{5,1},{7,3},{8,12},{10,14},{12... | collective-permute-start | bytes 393224 | tf_op jit(solution)/shard_map/ppermute | solution.py:28
  137.9 6.0 %collective-permute-start.30 = (bf16[32,2048]{1,0:T(8,128)(2,1)S(1)}, bf16[32,2048]{1,0:T(8,128)(2,1)S(1)}, u32[]{:S(2)}, u32[]{:S(2)}) collective-permute-start(bf16[32,2048]{1,0:T(8,128)(2,1)S(1)} %copy-done.26), channel_id=1, source_target_pairs={{0,6},{2,4},{4,2},{6,0},{1,7},{3,5},{5,3},{7,1},{8,14},{10,12},{12... | collective-permute-start | bytes 393224 | tf_op jit(solution)/shard_map/ppermute | solution.py:28
  (39 other events, 798.8 us)

commit v8 on v7

--- a/solution.py
+++ b/solution.py
@@ -274,7 +274,7 @@
         scratch_shapes=[pltpu.VMEM((plane * each, width), jnp.bfloat16)]
         + weight_scratch * 2
         + [pltpu.SemaphoreType.DMA((2 * (width // deep + 1),))],
-        compiler_params=pltpu.CompilerParams(vmem_limit_bytes=60 * 2**20),
+        compiler_params=pltpu.CompilerParams(vmem_limit_bytes=40 * 2**20),
         cost_estimate=SMALL,
         name="expert",
     )(*pieces, inner[0], outer[0], inner[1], outer[1])
@@ -296,20 +296,20 @@
             copies[number + 2].start()
 
     tree = blocks[0].shape[0]
-    rows = jnp.concatenate([block[...] for block in blocks], axis=0)
+    rows = jnp.concatenate([block[...] for block in blocks], axis=0).T
 
     def turned(i):
         take(i)
-        return lax.dot_general(
-            rows, here[i], (((1,), (1,)), ((), ())), preferred_element_type=jnp.float32
-        )
+        return dot(here[i], rows)
 
     result = None
     for n in range(2):
         hidden = silu(turned(3 * n))
         hidden = (hidden * turned(3 * n + 1)).astype(jnp.bfloat16)
         take(3 * n + 2)
-        term = dot(hidden, here[3 * n + 2])
+        term = lax.dot_general(
+            hidden, here[3 * n + 2], (((0,), (0,)), ((), ())), preferred_element_type=jnp.float32
+        )
         result = term if result is None else result + term
     for i in range(side):
         outs[i][...] = result[i * tree : (i + 1) * tree].astype(outs[i].dtype)
@@ -562,12 +562,13 @@
         if o == side - 1:
             other, middle, late = lax.optimization_barrier((other, middle, late))
             late = partner(late, "c", 1)
-        terms[o] = own_part + other.astype(jnp.float32)
         if o:
-            terms[o] = terms[o].astype(jnp.bfloat16)
-        follow = terms[o]
-    others = [partner(terms[o], "x", o) for o in range(1, side)]
-    own_term, late = lax.optimization_barrier((terms[0], late))
+            follow = (own_part + other.astype(jnp.float32)).astype(jnp.bfloat16)
+            crossed = partner(follow, "x", o).astype(jnp.float32)
+            terms[o] = crossed if o == side - 1 else crossed + terms[o + 1]
+    own_term = own_part + terms[1] if side > 1 else own_part
+    own_term, late = lax.optimization_barrier((own_term, late))
+    others = [other]
     resid, normed, payload = finish(own_rows, own_term, others, ffn_gain[None], routes[0])
     inner = [expert_in[0], late]
     outer = [expert_out[0], early[1]]
@@ -608,7 +609,7 @@
     results = {}
     for ks, pieces in zip(GROUPS, sent):
         if made is not None:
-            pieces, made = lax.optimization_barrier((pieces, made))
+            pieces, made, parts = lax.optimization_barrier((pieces, made, parts))
         made = experts(pieces, len(ks), inner, outer)
         results.update(zip(ks, made))
     totals = {}

time: 149 us -> 134 us (0.90)
  waiting for transfers between devices: 40.5 us -> 27.7 us
  Pallas kernels: 54.1 us -> 47.1 us
  starting transfers between devices: 33.9 us -> 37.4 us
  matrix products: 3.49 us -> 5.12 us
    ppermute x37, waiting for transfers between devices: 40.5 us -> 27.7 us  [partner(): return lax.ppermute(value, axes, [(i, i ^ offset) for i in range(size)])]
    pallas_call x2, Pallas kernels: 23.5 us -> 15.3 us  [experts(): pl.pallas_call(kernel, in_specs=[in_vmem()] * plane + [in_hbm()] * 4, out...]
    ppermute x37, starting transfers between devices: 33.9 us -> 37.4 us  [partner(): return lax.ppermute(value, axes, [(i, i ^ offset) for i in range(size)])]
    dot_general x3, matrix products: 2.53 us -> 4.14 us  [ancestry(): jnp.einsum('rij,rjk->rik', near, near, preferred_element_type=jnp.float32)]
    unnamed x70 -> x46, local copies, waits for them, and re-layouts: 6.48 us -> 6.71 us
  transfers between devices with their start and end apart: 37 -> 37, of which waited for: 15 -> 15; matrix products, arithmetic and copies ran while one was open for 8% -> 10% of each run, Pallas kernels for 27% -> 29%
where the time goes in v8:
time: 134 us; the launch traced here: 133 us
  Pallas kernels  47.1 us (35%)
  starting transfers between devices  37.4 us (28%)
  waiting for transfers between devices  27.7 us (21%)
  local copies, waits for them, and re-layouts  8.52 us (6%)
  other arithmetic  6.42 us (5%)
  matrix products  5.12 us (4%)
    ppermute x37, starting transfers between devices, partner(): return lax.ppermute(value, axes, [(i, i ^ offset) for i in range(size)])  37.4 us
    ppermute x37, waiting for transfers between devices, partner(): return lax.ppermute(value, axes, [(i, i ^ offset) for i in range(size)])  27.7 us
    pallas_call x2, Pallas kernels, attend(): pl.pallas_call(attend_kernel, in_specs=[pl.BlockSpec(memory_space=pltpu.S...  17.5 us
    pallas_call x2, Pallas kernels, experts(): pl.pallas_call(kernel, in_specs=[in_vmem()] * plane + [in_hbm()] * 4, out...  15.3 us
    pallas_call x1, Pallas kernels, shared_terms(): pl.pallas_call(functools.partial(shared_kernel, side=side), in_specs=[in_...  8.35 us
    unnamed x46, local copies, waits for them, and re-layouts  6.71 us
    dot_general x3, matrix products, ancestry(): jnp.einsum('rij,rjk->rik', near, near, preferred_element_type=jnp.float32)  4.14 us
    pallas_call x2, Pallas kernels, select(): pl.pallas_call(functools.partial(select_kernel, count=count, plane=plane,...  3.8 us
  transfers between devices with their start and end apart: 37, of which 15 were waited for; matrix products, arithmetic and copies ran while one was open for 10% of the time, Pallas kernels for 29%

profile of v8, /device:TPU:0, one launch (start us, length us, event | category | flops | bytes accessed | tf_op | source)
XLA Modules:
  0.0 133.3 jit_solution(5190864748574510399)
XLA Ops:
  0.6 3.0 %collective-permute-start = (bf16[64,2048]{1,0:T(8,128)(2,1)}, bf16[64,2048]{1,0:T(8,128)(2,1)S(1)}, u32[]{:S(2)}, u32[]{:S(2)}) collective-permute-start(bf16[64,2048]{1,0:T(8,128)(2,1)} %bitcast.30), channel_id=1, source_target_pairs={{0,2},{2,0},{1,3},{3,1},{4,6},{6,4},{5,7},{7,5},{8,10},{10,8},{9,1... | collective-permute-start | bytes 786440 | tf_op jit(solution)/shard_map/ppermute | solution.py:28
  5.8 1.9 %fusion.1 = bf16[4,64,64]{2,1,0:T(8,128)(2,1)} fusion(f32[64,64]{1,0:T(8,128)S(1)} %fusion.20, s32[4,64]{1,0:T(4,128)} %param.19), kind=kOutput, calls=%fused_computation.9 | convolution fusion | flops 4325376 | bytes 50176 | tf_op jit(solution)/shard_map/rij,rjk->rik/dot_general | solution.py:44
  13.1 2.8 %collective-permute-done.2.second = bf16[64,2048]{1,0:T(8,128)(2,1)S(1)} collective-permute-done((bf16[64,2048]{1,0:T(8,128)(2,1)S(1)}, bf16[64,2048]{1,0:T(8,128)(2,1)S(1)}, u32[]{:S(2)}, u32[]{:S(2)}) %collective-permute-start.2) | collective-permute-done | bytes 262176 | tf_op jit(solution)/shard_map/ppermute | solution.py:28
  17.6 10.2 %attend.2 = (f32[64,2048]{1,0:T(8,128)}, bf16[64,2048]{1,0:T(8,128)(2,1)}, bf16[64,256]{1,0:T(8,128)(2,1)}, bf16[64,256]{1,0:T(8,128)(2,1)}) custom-call(s32[4]{0:T(128)} %pad_add_fusion.1.info, bf16[64,2048]{1,0:T(8,128)(2,1)} %copy-done.15, bf16[64,2048]{1,0:T(8,128)(2,1)} %copy-done.16, f32[1,2048]{1,0:T(1,128)} %bitcast.43, bf16[2048,768]{1,0:T(8,128)(2,1)} %weight.3, ...), custom_call_target="tpu_custom_call" | custom-call | flops 1024 | bytes 1024 | tf_op jit(solution)/shard_map/attend/pallas_call | solution.py:174
  31.3 7.2 %attend.3 = (f32[64,2048]{1,0:T(8,128)}, bf16[64,2048]{1,0:T(8,128)(2,1)}, bf16[64,256]{1,0:T(8,128)(2,1)}, bf16[64,256]{1,0:T(8,128)(2,1)}) custom-call(s32[4]{0:T(128)} %pad_add_fusion.info, bf16[64,2048]{1,0:T(8,128)(2,1)} %bitcast.32, bf16[64,2048]{1,0:T(8,128)(2,1)} %copy-done.14, f32[1,2048]{1,0:T(1,128)} %bitcast.44, bf16[2048,768]{1,0:T(8,128)(2,1)} %weight.3, ...), custom_call_target="tpu_custom_call" | custom-call | flops 1024 | bytes 1024 | tf_op jit(solution)/shard_map/attend/pallas_call | solution.py:174
  41.6 2.3 %collective-permute-start.12 = (bf16[64,2176]{1,0:T(8,128)(2,1)S(1)}, bf16[64,2176]{1,0:T(8,128)(2,1)S(1)}, u32[]{:S(2)}, u32[]{:S(2)}) collective-permute-start(bf16[64,2176]{1,0:T(8,128)(2,1)S(1)} %get-tuple-element.120.refs_2_), channel_id=1, source_target_pairs={{0,8},{8,0},{16,24},{24,16},{1,9},{9,1},{17,25},{25,17},{2,10},{10... | collective-permute-start | bytes 835592 | tf_op jit(solution)/shard_map/ppermute | solution.py:28
  43.9 1.9 %collective-permute-start.11 = (bf16[64,2048]{1,0:T(8,128)(2,1)S(1)}, bf16[64,2048]{1,0:T(8,128)(2,1)}, u32[]{:S(2)}, u32[]{:S(2)}) collective-permute-start(bf16[64,2048]{1,0:T(8,128)(2,1)S(1)} %get-tuple-element.115.refs_0_), channel_id=1, source_target_pairs={{0,2},{2,0},{1,3},{3,1},{4,6},{6,4},{5,7},{7,5},{8,10},{10,8},{9,1... | collective-permute-start | bytes 786440 | tf_op jit(solution)/shard_map/ppermute | solution.py:28
  45.8 1.6 %collective-permute-start.16 = (bf16[64,2176]{1,0:T(8,128)(2,1)S(1)}, bf16[64,2176]{1,0:T(8,128)(2,1)}, u32[]{:S(2)}, u32[]{:S(2)}) collective-permute-start(bf16[64,2176]{1,0:T(8,128)(2,1)S(1)} %get-tuple-element.120.refs_2_), channel_id=1, source_target_pairs={{0,24},{8,16},{16,8},{24,0},{1,25},{9,17},{17,9},{25,1},{2,26},{10... | collective-permute-start | bytes 835592 | tf_op jit(solution)/shard_map/ppermute | solution.py:28
  47.4 1.8 %collective-permute-start.17 = (bf16[64,2176]{1,0:T(8,128)(2,1)S(1)}, bf16[64,2176]{1,0:T(8,128)(2,1)}, u32[]{:S(2)}, u32[]{:S(2)}) collective-permute-start(bf16[64,2176]{1,0:T(8,128)(2,1)S(1)} %get-tuple-element.120.refs_2_), channel_id=1, source_target_pairs={{0,16},{8,24},{16,0},{24,8},{1,17},{9,25},{17,1},{25,9},{2,18},{10... | collective-permute-start | bytes 835592 | tf_op jit(solution)/shard_map/ppermute | solution.py:28
  49.6 2.9 %collective-permute-done.11.refs_1_ = bf16[64,2048]{1,0:T(8,128)(2,1)} collective-permute-done((bf16[64,2048]{1,0:T(8,128)(2,1)S(1)}, bf16[64,2048]{1,0:T(8,128)(2,1)}, u32[]{:S(2)}, u32[]{:S(2)}) %collective-permute-start.11) | collective-permute-done | bytes 262176 | tf_op jit(solution)/shard_map/ppermute | solution.py:28
  52.5 8.4 %shared.1 = (f32[64,2048]{1,0:T(8,128)}, bf16[64,2048]{1,0:T(8,128)(2,1)}) custom-call(bf16[64,2048]{1,0:T(8,128)(2,1)} %copy-done.7, bf16[64,2048]{1,0:T(8,128)(2,1)} %collective-permute-done.11.refs_1_, bf16[352,2048]{1,0:T(8,128)(2,1)} %bitcast.39, bf16[352,2048]{1,0:T(8,128)(2,1)} %bitcast.41, bf16[352,2048]{1,0:T(8,128)(2,1)} %refs_4_.1, ...), custom_call_target="tpu_custom_call" | custom-call | flops 1024 | bytes 1024 | tf_op jit(solution)/shard_map/shared/pallas_call | solution.py:322
  60.9 1.6 %select.2 = (bf16[64,2048]{1,0:T(8,128)(2,1)S(1)}, bf16[64,2048]{1,0:T(8,128)(2,1)S(1)}, bf16[64,2048]{1,0:T(8,128)(2,1)S(1)}, bf16[64,2048]{1,0:T(8,128)(2,1)S(...) custom-call(s32[4]{0:T(128)S(1)} %xor_add_fusion.refs_0_, bf16[2048,16]{1,0:T(8,128)(2,1)S(1)} %copy.29.refs_1_, ...), custom_call_target="tpu_custom_call" | custom-call | flops 1024 | bytes 1024 | tf_op jit(solution)/shard_map/select/pallas_call | solution.py:429
  62.5 1.8 %collective-permute-start.13 = (bf16[64,2048]{1,0:T(8,128)(2,1)S(1)}, bf16[64,2048]{1,0:T(8,128)(2,1)S(1)}, u32[]{:S(2)}, u32[]{:S(2)}) collective-permute-start(bf16[64,2048]{1,0:T(8,128)(2,1)S(1)} %get-tuple-element.125), channel_id=1, source_target_pairs={{0,2},{2,0},{4,6},{6,4},{1,3},{3,1},{5,7},{7,5},{8,10},{10,8},{12,... | collective-permute-start | bytes 786440 | tf_op jit(solution)/shard_map/ppermute | solution.py:28
  64.4 1.7 %collective-permute-start.15 = (bf16[64,2048]{1,0:T(8,128)(2,1)S(1)}, bf16[64,2048]{1,0:T(8,128)(2,1)S(1)}, u32[]{:S(2)}, u32[]{:S(2)}) collective-permute-start(bf16[64,2048]{1,0:T(8,128)(2,1)S(1)} %get-tuple-element.127), channel_id=1, source_target_pairs={{0,6},{2,4},{4,2},{6,0},{1,7},{3,5},{5,3},{7,1},{8,14},{10,12},{12... | collective-permute-start | bytes 786440 | tf_op jit(solution)/shard_map/ppermute | solution.py:28
  66.1 7.3 %collective-permute-done.17.refs_3_ = bf16[64,2176]{1,0:T(8,128)(2,1)} collective-permute-done((bf16[64,2176]{1,0:T(8,128)(2,1)S(1)}, bf16[64,2176]{1,0:T(8,128)(2,1)}, u32[]{:S(2)}, u32[]{:S(2)}) %collective-permute-start.17) | collective-permute-done | bytes 278560 | tf_op jit(solution)/shard_map/ppermute | solution.py:28
  73.4 2.2 %select.3 = (bf16[64,2048]{1,0:T(8,128)(2,1)S(1)}, bf16[64,2048]{1,0:T(8,128)(2,1)S(1)}, bf16[64,2048]{1,0:T(8,128)(2,1)S(1)}, bf16[64,2048]{1,0:T(8,128)(2,1)S(...) custom-call(s32[4]{0:T(128)S(1)} %xor_add_fusion.refs_0_, bf16[2048,16]{1,0:T(8,128)(2,1)S(1)} %copy.29.refs_1_, ...), custom_call_target="tpu_custom_call" | custom-call | flops 1024 | bytes 1024 | tf_op jit(solution)/shard_map/select/pallas_call | solution.py:429
  75.9 3.2 %collective-permute-start.20 = (bf16[64,2048]{1,0:T(8,128)(2,1)S(1)}, bf16[64,2048]{1,0:T(8,128)(2,1)S(1)}, u32[]{:S(2)}, u32[]{:S(2)}) collective-permute-start(bf16[64,2048]{1,0:T(8,128)(2,1)S(1)} %get-tuple-element.138), channel_id=1, source_target_pairs={{0,6},{2,4},{4,2},{6,0},{1,7},{3,5},{5,3},{7,1},{8,14},{10,12},{12... | collective-permute-start | bytes 786440 | tf_op jit(solution)/shard_map/ppermute | solution.py:28
  79.4 2.6 %copy-done.1 = bf16[1,2048,1408]{2,1,0:T(8,128)(2,1)S(1)} copy-done((bf16[1,2048,1408]{2,1,0:T(8,128)(2,1)S(1)}, bf16[1,2048,1408]{2,1,0:T(8,128)(2,1)}, u32[]{:S(2)}) %copy-start.1) | copy-done | bytes 5767192
  82.1 1.8 %copy-done.4 = bf16[704,2048]{1,0:T(8,128)(2,1)S(1)} copy-done((bf16[704,2048]{1,0:T(8,128)(2,1)S(1)}, bf16[704,2048]{1,0:T(8,128)(2,1)}, u32[]{:S(2)}) %copy-start.4) | copy-done | bytes 2883608
  83.9 7.6 %expert.2 = (bf16[32,2048]{1,0:T(8,128)(2,1)S(1)}, bf16[32,2048]{1,0:T(8,128)(2,1)S(1)}, bf16[32,2048]{1,0:T(8,128)(2,1)S(1)}, bf16[32,2048]{1,0:T(8,128)(2,1)S(...) custom-call(bf16[64,2048]{1,0:T(8,128)(2,1)S(1)} %get-tuple-element., ...), custom_call_target="tpu_custom_call" | custom-call | flops 1024 | bytes 1024 | tf_op jit(solution)/shard_map/expert/pallas_call | solution.py:269
  91.6 2.5 %collective-permute-done.21.refs_0_ = bf16[64,2048]{1,0:T(8,128)(2,1)S(1)} collective-permute-done((bf16[64,2048]{1,0:T(8,128)(2,1)S(1)}, bf16[64,2048]{1,0:T(8,128)(2,1)S(1)}, u32[]{:S(2)}, u32[]{:S(2)}) %collective-permute-start.21) | collective-permute-done | bytes 262176 | tf_op jit(solution)/shard_map/ppermute | solution.py:28
  94.1 7.6 %expert.3 = (bf16[32,2048]{1,0:T(8,128)(2,1)S(1)}, bf16[32,2048]{1,0:T(8,128)(2,1)S(1)}, bf16[32,2048]{1,0:T(8,128)(2,1)S(1)}, bf16[32,2048]{1,0:T(8,128)(2,1)S(...) custom-call(bf16[64,2048]{1,0:T(8,128)(2,1)S(1)} %get-tuple-element., ...), custom_call_target="tpu_custom_call" | custom-call | flops 1024 | bytes 1024 | tf_op jit(solution)/shard_map/expert/pallas_call | solution.py:269
  102.2 3.2 %collective-permute-start.24 = (bf16[32,2048]{1,0:T(8,128)(2,1)S(1)}, bf16[32,2048]{1,0:T(8,128)(2,1)S(1)}, u32[]{:S(2)}, u32[]{:S(2)}) collective-permute-start(bf16[32,2048]{1,0:T(8,128)(2,1)S(1)} %get-tuple-element.156), channel_id=1, source_target_pairs={{0,6},{2,4},{4,2},{6,0},{1,7},{3,5},{5,3},{7,1},{8,14},{10,12},{12... | collective-permute-start | bytes 393224 | tf_op jit(solution)/shard_map/ppermute | solution.py:28
  105.9 2.3 %collective-permute-done.22.refs_1_ = bf16[32,2048]{1,0:T(8,128)(2,1)S(1)} collective-permute-done((bf16[32,2048]{1,0:T(8,128)(2,1)S(1)}, bf16[32,2048]{1,0:T(8,128)(2,1)S(1)}, u32[]{:S(2)}, u32[]{:S(2)}) %collective-permute-start.22) | collective-permute-done | bytes 131104 | tf_op jit(solution)/shard_map/ppermute | solution.py:28
  108.2 1.7 %collective-permute-done.23.refs_2_ = bf16[32,2048]{1,0:T(8,128)(2,1)S(1)} collective-permute-done((bf16[32,2048]{1,0:T(8,128)(2,1)S(1)}, bf16[32,2048]{1,0:T(8,128)(2,1)S(1)}, u32[]{:S(2)}, u32[]{:S(2)}) %collective-permute-start.23) | collective-permute-done | bytes 131104 | tf_op jit(solution)/shard_map/ppermute | solution.py:28
  110.1 1.4 %collective-permute-start.28 = (bf16[64,2048]{1,0:T(8,128)(2,1)S(1)}, bf16[64,2048]{1,0:T(8,128)(2,1)S(1)}, u32[]{:S(2)}, u32[]{:S(2)}) collective-permute-start(bf16[64,2048]{1,0:T(8,128)(2,1)S(1)} %combine.4), channel_id=1, source_target_pairs={{0,24},{8,16},{16,8},{24,0},{1,25},{9,17},{17,9},{25,1},{2,26},{10... | collective-permute-start | bytes 786440 | tf_op jit(solution)/shard_map/ppermute | solution.py:28
  111.6 1.8 %collective-permute-start.35 = (bf16[32,2048]{1,0:T(8,128)(2,1)S(1)}, bf16[32,2048]{1,0:T(8,128)(2,1)S(1)}, u32[]{:S(2)}, u32[]{:S(2)}) collective-permute-start(bf16[32,2048]{1,0:T(8,128)(2,1)S(1)} %get-tuple-element.175), channel_id=1, source_target_pairs={{0,6},{2,4},{4,2},{6,0},{1,7},{3,5},{5,3},{7,1},{8,14},{10,12},{12... | collective-permute-start | bytes 393224 | tf_op jit(solution)/shard_map/ppermute | solution.py:28
  115.0 1.8 %collective-permute-start.27 = (bf16[32,2048]{1,0:T(8,128)(2,1)S(1)}, bf16[32,2048]{1,0:T(8,128)(2,1)S(1)}, u32[]{:S(2)}, u32[]{:S(2)}) collective-permute-start(bf16[32,2048]{1,0:T(8,128)(2,1)S(1)} %get-tuple-element.160), channel_id=1, source_target_pairs={{0,6},{2,4},{4,2},{6,0},{1,7},{3,5},{5,3},{7,1},{8,14},{10,12},{12... | collective-permute-start | bytes 393224 | tf_op jit(solution)/shard_map/ppermute | solution.py:28
  119.3 1.6 %collective-permute-done.27.refs_3_ = bf16[32,2048]{1,0:T(8,128)(2,1)S(1)} collective-permute-done((bf16[32,2048]{1,0:T(8,128)(2,1)S(1)}, bf16[32,2048]{1,0:T(8,128)(2,1)S(1)}, u32[]{:S(2)}, u32[]{:S(2)}) %collective-permute-start.27) | collective-permute-done | bytes 131104 | tf_op jit(solution)/shard_map/ppermute | solution.py:28
  121.1 1.5 %collective-permute-start.32 = (bf16[64,2048]{1,0:T(8,128)(2,1)S(1)}, bf16[64,2048]{1,0:T(8,128)(2,1)S(1)}, u32[]{:S(2)}, u32[]{:S(2)}) collective-permute-start(bf16[64,2048]{1,0:T(8,128)(2,1)S(1)} %combine.5), channel_id=1, source_target_pairs={{0,16},{8,24},{16,0},{24,8},{1,17},{9,25},{17,1},{25,9},{2,18},{10... | collective-permute-start | bytes 786440 | tf_op jit(solution)/shard_map/ppermute | solution.py:28
  125.4 1.6 %collective-permute-start.31 = (bf16[32,2048]{1,0:T(8,128)(2,1)S(1)}, bf16[32,2048]{1,0:T(8,128)(2,1)S(1)}, u32[]{:S(2)}, u32[]{:S(2)}) collective-permute-start(bf16[32,2048]{1,0:T(8,128)(2,1)S(1)} %get-tuple-element.168), channel_id=1, source_target_pairs={{0,6},{2,4},{4,2},{6,0},{1,7},{3,5},{5,3},{7,1},{8,14},{10,12},{12... | collective-permute-start | bytes 393224 | tf_op jit(solution)/shard_map/ppermute | solution.py:28
  129.2 2.0 %collective-permute-done.31.refs_3_ = bf16[32,2048]{1,0:T(8,128)(2,1)S(1)} collective-permute-done((bf16[32,2048]{1,0:T(8,128)(2,1)S(1)}, bf16[32,2048]{1,0:T(8,128)(2,1)S(1)}, u32[]{:S(2)}, u32[]{:S(2)}) %collective-permute-start.31) | collective-permute-done | bytes 131104 | tf_op jit(solution)/shard_map/ppermute | solution.py:28
  (123 shorter events, 29.1 us)
Async XLA Ops:
  0.6 12.1 %collective-permute-start = (bf16[64,2048]{1,0:T(8,128)(2,1)}, bf16[64,2048]{1,0:T(8,128)(2,1)S(1)}, u32[]{:S(2)}, u32[]{:S(2)}) collective-permute-start(bf16[64,2048]{1,0:T(8,128)(2,1)} %bitcast.30), channel_id=1, source_target_pairs={{0,2},{2,0},{1,3},{3,1},{4,6},{6,4},{5,7},{7,5},{8,10},{10,8},{9,1... | collective-permute-start | bytes 786440 | tf_op jit(solution)/shard_map/ppermute | solution.py:28
  5.4 11.1 %collective-permute-start.4 = (bf16[704,2048]{1,0:T(8,128)(2,1)}, bf16[704,2048]{1,0:T(8,128)(2,1)S(1)}, u32[]{:S(2)}, u32[]{:S(2)}) collective-permute-start(bf16[704,2048]{1,0:T(8,128)(2,1)} %bitcast.27), channel_id=1, source_target_pairs={{0,1},{1,0},{2,3},{3,2},{4,5},{5,4},{6,7},{7,6},{8,9},{9,8},{10,11... | collective-permute-start | bytes 8650760 | tf_op jit(solution)/shard_map/ppermute | solution.py:28
  15.9 12.4 %collective-permute-start.6 = (bf16[352,2048]{1,0:T(8,128)(2,1)}, bf16[352,2048]{1,0:T(8,128)(2,1)}, u32[]{:S(2)}, u32[]{:S(2)}) collective-permute-start(bf16[352,2048]{1,0:T(8,128)(2,1)} %bitcast.40), channel_id=1, source_target_pairs={{0,1},{1,0},{2,3},{3,2},{4,5},{5,4},{6,7},{7,6},{8,9},{9,8},{10,11... | collective-permute-start | bytes 4325384 | tf_op jit(solution)/shard_map/ppermute | solution.py:28
  16.3 12.0 %collective-permute-start.7 = (bf16[352,2048]{1,0:T(8,128)(2,1)}, bf16[352,2048]{1,0:T(8,128)(2,1)}, u32[]{:S(2)}, u32[]{:S(2)}) collective-permute-start(bf16[352,2048]{1,0:T(8,128)(2,1)} %refs_4_.1), channel_id=1, source_target_pairs={{0,1},{1,0},{2,3},{3,2},{4,5},{5,4},{6,7},{7,6},{8,9},{9,8},{10,11... | collective-permute-start | bytes 4325384 | tf_op jit(solution)/shard_map/ppermute | solution.py:28
  29.7 11.0 %collective-permute-start.9 = (bf16[2048,1408]{1,0:T(8,128)(2,1)}, bf16[2048,1408]{1,0:T(8,128)(2,1)}, u32[]{:S(2)}, u32[]{:S(2)}) collective-permute-start(bf16[2048,1408]{1,0:T(8,128)(2,1)} %bitcast.24), channel_id=1, source_target_pairs={{0,1},{1,0},{2,3},{3,2},{4,5},{5,4},{6,7},{7,6},{8,9},{9,8},{10,11... | collective-permute-start | bytes 17301512 | tf_op jit(solution)/shard_map/ppermute | solution.py:28
  31.1 8.4 %collective-permute-start.8 = (bf16[64,2048]{1,0:T(8,128)(2,1)S(1)}, bf16[64,2048]{1,0:T(8,128)(2,1)S(1)}, u32[]{:S(2)}, u32[]{:S(2)}) collective-permute-start(bf16[64,2048]{1,0:T(8,128)(2,1)S(1)} %add_convert_fusion), channel_id=1, source_target_pairs={{0,2},{2,0},{1,3},{3,1},{4,6},{6,4},{5,7},{7,5},{8,10},{10,8},{9,1... | collective-permute-start | bytes 786440 | tf_op jit(solution)/shard_map/ppermute | solution.py:28
  41.6 19.2 %collective-permute-start.12 = (bf16[64,2176]{1,0:T(8,128)(2,1)S(1)}, bf16[64,2176]{1,0:T(8,128)(2,1)S(1)}, u32[]{:S(2)}, u32[]{:S(2)}) collective-permute-start(bf16[64,2176]{1,0:T(8,128)(2,1)S(1)} %get-tuple-element.120.refs_2_), channel_id=1, source_target_pairs={{0,8},{8,0},{16,24},{24,16},{1,9},{9,1},{17,25},{25,17},{2,10},{10... | collective-permute-start | bytes 835592 | tf_op jit(solution)/shard_map/ppermute | solution.py:28
  43.9 8.6 %collective-permute-start.11 = (bf16[64,2048]{1,0:T(8,128)(2,1)S(1)}, bf16[64,2048]{1,0:T(8,128)(2,1)}, u32[]{:S(2)}, u32[]{:S(2)}) collective-permute-start(bf16[64,2048]{1,0:T(8,128)(2,1)S(1)} %get-tuple-element.115.refs_0_), channel_id=1, source_target_pairs={{0,2},{2,0},{1,3},{3,1},{4,6},{6,4},{5,7},{7,5},{8,10},{10,8},{9,1... | collective-permute-start | bytes 786440 | tf_op jit(solution)/shard_map/ppermute | solution.py:28
  45.8 20.3 %collective-permute-start.16 = (bf16[64,2176]{1,0:T(8,128)(2,1)S(1)}, bf16[64,2176]{1,0:T(8,128)(2,1)}, u32[]{:S(2)}, u32[]{:S(2)}) collective-permute-start(bf16[64,2176]{1,0:T(8,128)(2,1)S(1)} %get-tuple-element.120.refs_2_), channel_id=1, source_target_pairs={{0,24},{8,16},{16,8},{24,0},{1,25},{9,17},{17,9},{25,1},{2,26},{10... | collective-permute-start | bytes 835592 | tf_op jit(solution)/shard_map/ppermute | solution.py:28
  47.4 26.0 %collective-permute-start.17 = (bf16[64,2176]{1,0:T(8,128)(2,1)S(1)}, bf16[64,2176]{1,0:T(8,128)(2,1)}, u32[]{:S(2)}, u32[]{:S(2)}) collective-permute-start(bf16[64,2176]{1,0:T(8,128)(2,1)S(1)} %get-tuple-element.120.refs_2_), channel_id=1, source_target_pairs={{0,16},{8,24},{16,0},{24,8},{1,17},{9,25},{17,1},{25,9},{2,18},{10... | collective-permute-start | bytes 835592 | tf_op jit(solution)/shard_map/ppermute | solution.py:28
  62.5 13.4 %collective-permute-start.13 = (bf16[64,2048]{1,0:T(8,128)(2,1)S(1)}, bf16[64,2048]{1,0:T(8,128)(2,1)S(1)}, u32[]{:S(2)}, u32[]{:S(2)}) collective-permute-start(bf16[64,2048]{1,0:T(8,128)(2,1)S(1)} %get-tuple-element.125), channel_id=1, source_target_pairs={{0,2},{2,0},{4,6},{6,4},{1,3},{3,1},{5,7},{7,5},{8,10},{10,8},{12,... | collective-permute-start | bytes 786440 | tf_op jit(solution)/shard_map/ppermute | solution.py:28
  64.3 14.8 %collective-permute-start.14 = (bf16[64,2048]{1,0:T(8,128)(2,1)S(1)}, bf16[64,2048]{1,0:T(8,128)(2,1)S(1)}, u32[]{:S(2)}, u32[]{:S(2)}) collective-permute-start(bf16[64,2048]{1,0:T(8,128)(2,1)S(1)} %get-tuple-element.126), channel_id=1, source_target_pairs={{0,4},{2,6},{4,0},{6,2},{1,5},{3,7},{5,1},{7,3},{8,12},{10,14},{12... | collective-permute-start | bytes 786440 | tf_op jit(solution)/shard_map/ppermute | solution.py:28
  64.4 15.1 %collective-permute-start.15 = (bf16[64,2048]{1,0:T(8,128)(2,1)S(1)}, bf16[64,2048]{1,0:T(8,128)(2,1)S(1)}, u32[]{:S(2)}, u32[]{:S(2)}) collective-permute-start(bf16[64,2048]{1,0:T(8,128)(2,1)S(1)} %get-tuple-element.127), channel_id=1, source_target_pairs={{0,6},{2,4},{4,2},{6,0},{1,7},{3,5},{5,3},{7,1},{8,14},{10,12},{12... | collective-permute-start | bytes 786440 | tf_op jit(solution)/shard_map/ppermute | solution.py:28
  75.6 16.0 %collective-permute-start.18 = (bf16[64,2048]{1,0:T(8,128)(2,1)S(1)}, bf16[64,2048]{1,0:T(8,128)(2,1)S(1)}, u32[]{:S(2)}, u32[]{:S(2)}) collective-permute-start(bf16[64,2048]{1,0:T(8,128)(2,1)S(1)} %get-tuple-element.136), channel_id=1, source_target_pairs={{0,2},{2,0},{4,6},{6,4},{1,3},{3,1},{5,7},{7,5},{8,10},{10,8},{12,... | collective-permute-start | bytes 786440 | tf_op jit(solution)/shard_map/ppermute | solution.py:28
  75.9 15.6 %collective-permute-start.19 = (bf16[64,2048]{1,0:T(8,128)(2,1)S(1)}, bf16[64,2048]{1,0:T(8,128)(2,1)S(1)}, u32[]{:S(2)}, u32[]{:S(2)}) collective-permute-start(bf16[64,2048]{1,0:T(8,128)(2,1)S(1)} %get-tuple-element.137), channel_id=1, source_target_pairs={{0,4},{2,6},{4,0},{6,2},{1,5},{3,7},{5,1},{7,3},{8,12},{10,14},{12... | collective-permute-start | bytes 786440 | tf_op jit(solution)/shard_map/ppermute | solution.py:28
  75.9 15.6 %collective-permute-start.20 = (bf16[64,2048]{1,0:T(8,128)(2,1)S(1)}, bf16[64,2048]{1,0:T(8,128)(2,1)S(1)}, u32[]{:S(2)}, u32[]{:S(2)}) collective-permute-start(bf16[64,2048]{1,0:T(8,128)(2,1)S(1)} %get-tuple-element.138), channel_id=1, source_target_pairs={{0,6},{2,4},{4,2},{6,0},{1,7},{3,5},{5,3},{7,1},{8,14},{10,12},{12... | collective-permute-start | bytes 786440 | tf_op jit(solution)/shard_map/ppermute | solution.py:28
  79.1 15.0 %collective-permute-start.21 = (bf16[64,2048]{1,0:T(8,128)(2,1)S(1)}, bf16[64,2048]{1,0:T(8,128)(2,1)S(1)}, u32[]{:S(2)}, u32[]{:S(2)}) collective-permute-start(bf16[64,2048]{1,0:T(8,128)(2,1)S(1)} %copy-done.20), channel_id=1, source_target_pairs={{0,2},{2,0},{1,3},{3,1},{4,6},{6,4},{5,7},{7,5},{8,10},{10,8},{9,1... | collective-permute-start | bytes 786440 | tf_op jit(solution)/shard_map/ppermute | solution.py:28
  101.8 6.4 %collective-permute-start.22 = (bf16[32,2048]{1,0:T(8,128)(2,1)S(1)}, bf16[32,2048]{1,0:T(8,128)(2,1)S(1)}, u32[]{:S(2)}, u32[]{:S(2)}) collective-permute-start(bf16[32,2048]{1,0:T(8,128)(2,1)S(1)} %get-tuple-element.154), channel_id=1, source_target_pairs={{0,2},{2,0},{4,6},{6,4},{1,3},{3,1},{5,7},{7,5},{8,10},{10,8},{12,... | collective-permute-start | bytes 393224 | tf_op jit(solution)/shard_map/ppermute | solution.py:28
  102.2 7.7 %collective-permute-start.23 = (bf16[32,2048]{1,0:T(8,128)(2,1)S(1)}, bf16[32,2048]{1,0:T(8,128)(2,1)S(1)}, u32[]{:S(2)}, u32[]{:S(2)}) collective-permute-start(bf16[32,2048]{1,0:T(8,128)(2,1)S(1)} %get-tuple-element.155), channel_id=1, source_target_pairs={{0,4},{2,6},{4,0},{6,2},{1,5},{3,7},{5,1},{7,3},{8,12},{10,14},{12... | collective-permute-start | bytes 393224 | tf_op jit(solution)/shard_map/ppermute | solution.py:28
  102.2 7.7 %collective-permute-start.24 = (bf16[32,2048]{1,0:T(8,128)(2,1)S(1)}, bf16[32,2048]{1,0:T(8,128)(2,1)S(1)}, u32[]{:S(2)}, u32[]{:S(2)}) collective-permute-start(bf16[32,2048]{1,0:T(8,128)(2,1)S(1)} %get-tuple-element.156), channel_id=1, source_target_pairs={{0,6},{2,4},{4,2},{6,0},{1,7},{3,5},{5,3},{7,1},{8,14},{10,12},{12... | collective-permute-start | bytes 393224 | tf_op jit(solution)/shard_map/ppermute | solution.py:28
  105.4 8.9 %collective-permute-start.33 = (bf16[32,2048]{1,0:T(8,128)(2,1)S(1)}, bf16[32,2048]{1,0:T(8,128)(2,1)S(1)}, u32[]{:S(2)}, u32[]{:S(2)}) collective-permute-start(bf16[32,2048]{1,0:T(8,128)(2,1)S(1)} %get-tuple-element.173), channel_id=1, source_target_pairs={{0,2},{2,0},{4,6},{6,4},{1,3},{3,1},{5,7},{7,5},{8,10},{10,8},{12,... | collective-permute-start | bytes 393224 | tf_op jit(solution)/shard_map/ppermute | solution.py:28
  105.7 9.4 %collective-permute-start.34 = (bf16[32,2048]{1,0:T(8,128)(2,1)S(1)}, bf16[32,2048]{1,0:T(8,128)(2,1)S(1)}, u32[]{:S(2)}, u32[]{:S(2)}) collective-permute-start(bf16[32,2048]{1,0:T(8,128)(2,1)S(1)} %get-tuple-element.174), channel_id=1, source_target_pairs={{0,4},{2,6},{4,0},{6,2},{1,5},{3,7},{5,1},{7,3},{8,12},{10,14},{12... | collective-permute-start | bytes 393224 | tf_op jit(solution)/shard_map/ppermute | solution.py:28
  110.1 13.2 %collective-permute-start.28 = (bf16[64,2048]{1,0:T(8,128)(2,1)S(1)}, bf16[64,2048]{1,0:T(8,128)(2,1)S(1)}, u32[]{:S(2)}, u32[]{:S(2)}) collective-permute-start(bf16[64,2048]{1,0:T(8,128)(2,1)S(1)} %combine.4), channel_id=1, source_target_pairs={{0,24},{8,16},{16,8},{24,0},{1,25},{9,17},{17,9},{25,1},{2,26},{10... | collective-permute-start | bytes 786440 | tf_op jit(solution)/shard_map/ppermute | solution.py:28
  111.6 5.9 %collective-permute-start.35 = (bf16[32,2048]{1,0:T(8,128)(2,1)S(1)}, bf16[32,2048]{1,0:T(8,128)(2,1)S(1)}, u32[]{:S(2)}, u32[]{:S(2)}) collective-permute-start(bf16[32,2048]{1,0:T(8,128)(2,1)S(1)} %get-tuple-element.175), channel_id=1, source_target_pairs={{0,6},{2,4},{4,2},{6,0},{1,7},{3,5},{5,3},{7,1},{8,14},{10,12},{12... | collective-permute-start | bytes 393224 | tf_op jit(solution)/shard_map/ppermute | solution.py:28
  113.4 5.3 %collective-permute-start.25 = (bf16[32,2048]{1,0:T(8,128)(2,1)S(1)}, bf16[32,2048]{1,0:T(8,128)(2,1)S(1)}, u32[]{:S(2)}, u32[]{:S(2)}) collective-permute-start(bf16[32,2048]{1,0:T(8,128)(2,1)S(1)} %get-tuple-element.158), channel_id=1, source_target_pairs={{0,2},{2,0},{4,6},{6,4},{1,3},{3,1},{5,7},{7,5},{8,10},{10,8},{12,... | collective-permute-start | bytes 393224 | tf_op jit(solution)/shard_map/ppermute | solution.py:28
  114.3 5.0 %collective-permute-start.26 = (bf16[32,2048]{1,0:T(8,128)(2,1)S(1)}, bf16[32,2048]{1,0:T(8,128)(2,1)S(1)}, u32[]{:S(2)}, u32[]{:S(2)}) collective-permute-start(bf16[32,2048]{1,0:T(8,128)(2,1)S(1)} %get-tuple-element.159), channel_id=1, source_target_pairs={{0,4},{2,6},{4,0},{6,2},{1,5},{3,7},{5,1},{7,3},{8,12},{10,14},{12... | collective-permute-start | bytes 393224 | tf_op jit(solution)/shard_map/ppermute | solution.py:28
  115.0 5.9 %collective-permute-start.27 = (bf16[32,2048]{1,0:T(8,128)(2,1)S(1)}, bf16[32,2048]{1,0:T(8,128)(2,1)S(1)}, u32[]{:S(2)}, u32[]{:S(2)}) collective-permute-start(bf16[32,2048]{1,0:T(8,128)(2,1)S(1)} %get-tuple-element.160), channel_id=1, source_target_pairs={{0,6},{2,4},{4,2},{6,0},{1,7},{3,5},{5,3},{7,1},{8,14},{10,12},{12... | collective-permute-start | bytes 393224 | tf_op jit(solution)/shard_map/ppermute | solution.py:28
  117.6 13.8 %collective-permute-start.36 = (bf16[64,2048]{1,0:T(8,128)(2,1)S(1)}, bf16[64,2048]{1,0:T(8,128)(2,1)S(1)}, u32[]{:S(2)}, u32[]{:S(2)}) collective-permute-start(bf16[64,2048]{1,0:T(8,128)(2,1)S(1)} %combine.7), channel_id=1, source_target_pairs={{0,8},{8,0},{16,24},{24,16},{1,9},{9,1},{17,25},{25,17},{2,10},{10... | collective-permute-start | bytes 786440 | tf_op jit(solution)/shard_map/ppermute | solution.py:28
  121.1 11.0 %collective-permute-start.32 = (bf16[64,2048]{1,0:T(8,128)(2,1)S(1)}, bf16[64,2048]{1,0:T(8,128)(2,1)S(1)}, u32[]{:S(2)}, u32[]{:S(2)}) collective-permute-start(bf16[64,2048]{1,0:T(8,128)(2,1)S(1)} %combine.5), channel_id=1, source_target_pairs={{0,16},{8,24},{16,0},{24,8},{1,17},{9,25},{17,1},{25,9},{2,18},{10... | collective-permute-start | bytes 786440 | tf_op jit(solution)/shard_map/ppermute | solution.py:28
  123.4 5.7 %collective-permute-start.29 = (bf16[32,2048]{1,0:T(8,128)(2,1)S(1)}, bf16[32,2048]{1,0:T(8,128)(2,1)S(1)}, u32[]{:S(2)}, u32[]{:S(2)}) collective-permute-start(bf16[32,2048]{1,0:T(8,128)(2,1)S(1)} %copy-done.12), channel_id=1, source_target_pairs={{0,2},{2,0},{4,6},{6,4},{1,3},{3,1},{5,7},{7,5},{8,10},{10,8},{12,... | collective-permute-start | bytes 393224 | tf_op jit(solution)/shard_map/ppermute | solution.py:28
  124.2 5.0 %collective-permute-start.30 = (bf16[32,2048]{1,0:T(8,128)(2,1)S(1)}, bf16[32,2048]{1,0:T(8,128)(2,1)S(1)}, u32[]{:S(2)}, u32[]{:S(2)}) collective-permute-start(bf16[32,2048]{1,0:T(8,128)(2,1)S(1)} %get-tuple-element.167), channel_id=1, source_target_pairs={{0,4},{2,6},{4,0},{6,2},{1,5},{3,7},{5,1},{7,3},{8,12},{10,14},{12... | collective-permute-start | bytes 393224 | tf_op jit(solution)/shard_map/ppermute | solution.py:28
  125.4 5.9 %collective-permute-start.31 = (bf16[32,2048]{1,0:T(8,128)(2,1)S(1)}, bf16[32,2048]{1,0:T(8,128)(2,1)S(1)}, u32[]{:S(2)}, u32[]{:S(2)}) collective-permute-start(bf16[32,2048]{1,0:T(8,128)(2,1)S(1)} %get-tuple-element.168), channel_id=1, source_target_pairs={{0,6},{2,4},{4,2},{6,0},{1,7},{3,5},{5,3},{7,1},{8,14},{10,12},{12... | collective-permute-start | bytes 393224 | tf_op jit(solution)/shard_map/ppermute | solution.py:28
  (27 other events, 415.3 us)

commit v9 on v8

--- a/solution.py
+++ b/solution.py
@@ -3,6 +3,7 @@
 
 import jax
 import jax.numpy as jnp
+import numpy as np
 from jax import lax
 from jax.experimental import pallas as pl
 from jax.experimental.pallas import tpu as pltpu
@@ -11,8 +12,8 @@
 
 EPSILON = 1e-06
 ROPE_BASE = 10000.0
-GROUPS = ((0, 1), (3, 2))
-BACK = ((3, None, None), (2, 3, None), (1, 3, None), (0, 2, 3))
+GROUPS = ((0, 3), (2, 1))
+BACK = ((3, None, None), (2, None, None), (1, 3, None), (0, 2, 3))
 CHUNK = 512
 EXTRA = 128
 SMALL = pl.CostEstimate(flops=1024, bytes_accessed=1024, transcendentals=0)
@@ -32,32 +33,55 @@
     return jnp.dot(left, right, preferred_element_type=jnp.float32)
 
 
-def ancestry(parents):
-    nodes_count = parents.shape[-1]
-    nodes = jnp.arange(nodes_count, dtype=jnp.int32)
-    reach = (parents[..., :, None] == nodes).astype(jnp.float32) + jnp.eye(
-        nodes_count, dtype=jnp.float32
-    )
-    for turn in range((nodes_count - 1).bit_length()):
-        near = reach.astype(jnp.bfloat16)
-        reach = jnp.minimum(
-            jnp.einsum("rij,rjk->rik", near, near, preferred_element_type=jnp.float32), 1.0
-        )
-    depth = jnp.sum(reach, axis=-1) - 1.0
-    return (reach, depth)
-
-
-def arrive(copies):
-    for copy in copies:
-        copy.wait()
+def prepare_kernel(lengths, parents, frequency, reach, cosine, sine):
+    requests, tree = parents.shape
+    row = lax.broadcasted_iota(jnp.int32, (tree, tree), 0)
+    column = lax.broadcasted_iota(jnp.int32, (tree, tree), 1)
+    places = column.astype(jnp.float32)
+    known = parents[...].astype(jnp.float32)
+    near = []
+    for r in range(requests):
+        spread = jnp.where(row == column, known[r : r + 1], 0.0)
+        parent = jnp.sum(spread, axis=-1, keepdims=True)
+        near.append(jnp.where((parent == places) | (row == column), 1.0, 0.0))
+    for turn in range((tree - 1).bit_length()):
+        for r in range(requests):
+            step = near[r].astype(jnp.bfloat16)
+            near[r] = jnp.minimum(dot(step, step), 1.0)
+    half = cosine.shape[2] // 2
+    lane = lax.broadcasted_iota(jnp.int32, cosine.shape[1:], 1)
+    for r in range(requests):
+        reach[r] = near[r]
+        depth = jnp.sum(near[r], axis=-1, keepdims=True) - 1.0
+        angle = (lengths[r].astype(jnp.float32) + depth) * frequency[...]
+        cosine[r] = jnp.cos(angle)
+        sines = jnp.sin(angle)
+        sine[r] = jnp.where(lane < half, -sines, sines)
+
+
+def prepare(lengths, parents, head_dim):
+    requests, tree = parents.shape
+    half = head_dim // 2
+    frequency = ROPE_BASE ** (-np.arange(half, dtype=np.float64) / half)
+    frequency = np.concatenate([frequency, frequency])[None].astype(np.float32)
+    table = jax.ShapeDtypeStruct((requests, tree, head_dim), jnp.float32)
+    return pl.pallas_call(
+        prepare_kernel,
+        in_specs=[in_smem(), in_vmem(), in_vmem()],
+        out_specs=[in_vmem()] * 3,
+        out_shape=[jax.ShapeDtypeStruct((requests, tree, tree), jnp.float32), table, table],
+        compiler_params=pltpu.CompilerParams(vmem_limit_bytes=16 * 2**20),
+        cost_estimate=SMALL,
+        name="prepare",
+    )(lengths, parents, frequency)
 
 
 def attend_kernel(
-    info, first, second, gain, weight, cosine, sine, reach, cache, outward, *outs_and_scratch
+    place, lengths, first, second, gain, weight, cosine, sine, reach, cache, outward, *rest, offset
 ):
-    term, term_other = outs_and_scratch[0:2]
-    fresh = outs_and_scratch[2:4]
-    weight_here, cache_here, gain_here, outward_here, sems = outs_and_scratch[4:]
+    term, term_other = rest[0:2]
+    fresh = rest[2:4]
+    weight_here, cache_here, gain_here, outward_here, sems = rest[4:]
     tree = first.shape[0]
     width, columns = weight.shape
     head_dim = cosine.shape[2]
@@ -72,7 +96,9 @@
         for i in range(2)
     ]
     cache_copies = [
-        pltpu.make_async_copy(cache.at[info[i]], cache_here.at[i], sems.at[3 + i])
+        pltpu.make_async_copy(
+            cache.at[place[0] ^ (offset + i)], cache_here.at[i], sems.at[3 + i]
+        )
         for i in range(2)
     ]
     outward_copy = pltpu.make_async_copy(outward, outward_here, sems.at[5])
@@ -94,8 +120,8 @@
 
     for i in range(2):
         own = projected[i * tree : (i + 1) * tree]
-        request = info[i]
-        length = info[2 + i]
+        request = place[0] ^ (offset + i)
+        length = lengths[request]
 
         def rope(values):
             return values * cosine[request] + pltpu.roll(values, head_dim // 2, 1) * sine[request]
@@ -161,20 +187,25 @@
     return pl.BlockSpec(memory_space=pltpu.VMEM)
 
 
+def in_smem():
+    return pl.BlockSpec(memory_space=pltpu.SMEM)
+
+
 def in_hbm():
     return pl.BlockSpec(memory_space=pltpu.HBM)
 
 
-def attend(info, first, second, gain, weight, cosine, sine, reach, cache, outward):
+def attend(offset, place, lengths, first, second, gain, weight, cosine, sine, reach, cache, outward):
     tree, width = first.shape
     slots, pair = cache.shape[1:]
     head_dim = pair // 2
     columns = weight.shape[1]
     group_columns = columns - pair
     return pl.pallas_call(
-        attend_kernel,
+        functools.partial(attend_kernel, offset=offset),
         in_specs=[
-            pl.BlockSpec(memory_space=pltpu.SMEM),
+            in_smem(),
+            in_smem(),
             in_vmem(),
             in_vmem(),
             in_hbm(),
@@ -201,7 +232,7 @@
         compiler_params=pltpu.CompilerParams(vmem_limit_bytes=60 * 2**20),
         cost_estimate=SMALL,
         name="attend",
-    )(info, first, second, gain, weight, cosine, sine, reach, cache, outward)
+    )(place, lengths, first, second, gain, weight, cosine, sine, reach, cache, outward)
 
 
 def silu(values):
@@ -430,7 +461,7 @@
         functools.partial(
             select_kernel, count=count, plane=plane, capacity=capacity, top_count=top_count
         ),
-        in_specs=[pl.BlockSpec(memory_space=pltpu.SMEM)] + [in_vmem()] * (1 + count),
+        in_specs=[in_smem()] + [in_vmem()] * (1 + count),
         out_specs=[in_vmem()] * (plane + count),
         out_shape=[jax.ShapeDtypeStruct((count * capacity, width), jnp.bfloat16)] * plane
         + [jax.ShapeDtypeStruct((tree, plane * capacity), jnp.bfloat16)] * count,
@@ -510,22 +541,11 @@
     near = [own_rows] + [partner(own_rows, "x", o) for o in range(1, side)]
     near_core = [partner(own_rows, "c", 1)]
 
-    reach, depth = ancestry(parents)
-    positions = lengths[:, None].astype(jnp.float32) + depth
-    frequency = ROPE_BASE ** (-jnp.arange(head_dim // 2, dtype=jnp.float32) / (head_dim // 2))
-    angle = positions[..., None] * frequency
-    cosine = jnp.cos(angle)
-    sine = jnp.sin(angle)
-    cosine = jnp.concatenate([cosine, cosine], axis=-1)
-    sine = jnp.concatenate([-sine, sine], axis=-1)
-    info = []
-    for o in range(side):
-        ids = me ^ jnp.arange(2 * o, 2 * o + 2, dtype=jnp.int32)
-        here = ids[:, None] == jnp.arange(group_count, dtype=jnp.int32)
-        info.append(jnp.concatenate([ids, jnp.sum(jnp.where(here, lengths, 0), axis=1)]))
+    reach, cosine, sine = prepare(lengths, parents, head_dim)
+    place = me.astype(jnp.int32)[None]
     for o in range(1, side):
-        near[o], cosine, sine, reach, info = lax.optimization_barrier(
-            (near[o], cosine, sine, reach, info)
+        near[o], cosine, sine, reach, place = lax.optimization_barrier(
+            (near[o], cosine, sine, reach, place)
         )
         near_core.append(partner(near[o], "c", 1))
 
@@ -546,7 +566,9 @@
         if follow is not None:
             near_core[o], follow = lax.optimization_barrier((near_core[o], follow))
         own_part, other_part, fresh_own, fresh_other = attend(
-            info[o],
+            2 * o,
+            place,
+            lengths,
             near[o],
             near_core[o],
             attn_gain[None],
@@ -594,7 +616,7 @@
     beside = [partner(normed, "x", o) for o in range(1, side)]
 
     shared, beside = shared_terms(normed, beside, shared_weights)
-    line_rows[1], beside = lax.optimization_barrier((line_rows[1], beside))
+    line_rows[3], beside = lax.optimization_barrier((line_rows[3], beside))
 
     sent = []
     spread = {}

time: 134 us -> 135 us (level)
  starting transfers between devices: 37.4 us -> 43.4 us
  other arithmetic: 6.42 us -> 2.22 us
  matrix products: 5.12 us -> 0.98 us
  local copies, waits for them, and re-layouts: 8.52 us -> 12.4 us
    ppermute x37, starting transfers between devices: 37.4 us -> 43.4 us  [partner(): return lax.ppermute(value, axes, [(i, i ^ offset) for i in range(size)])]
    dot_general x3 -> x0, matrix products: 4.14 us -> none  [ancestry(): jnp.einsum('rij,rjk->rik', near, near, preferred_element_type=jnp.float32)]
    unnamed x46 -> x58, local copies, waits for them, and re-layouts: 6.71 us -> 10.6 us
    concatenate x3 -> x0, other arithmetic: 2.04 us -> none  [the longest x2 1.19 us: body(): jnp.concatenate([ids, jnp.sum(jnp.where(here, lengths, 0), axis=1)])]
    pallas_call x2 -> x3, Pallas kernels: 17.5 us -> 17.9 us  [the longest x2 15.9 us: attend(): pl.pallas_call(functools.partial(attend_kernel, offset=offset), in_specs=...]
  transfers between devices with their start and end apart: 37 -> 37, of which waited for: 15 -> 12; matrix products, arithmetic and copies ran while one was open for 10% -> 4% of each run, Pallas kernels for 29% -> 34%
where the time goes in v9:
time: 135 us; the launch traced here: 134 us
  Pallas kernels  47.5 us (35%)
  starting transfers between devices  43.4 us (32%)
  waiting for transfers between devices  26.5 us (20%)
  local copies, waits for them, and re-layouts  12.4 us (9%)
  other arithmetic  2.22 us (2%)
    ppermute x37, starting transfers between devices, partner(): return lax.ppermute(value, axes, [(i, i ^ offset) for i in range(size)])  43.4 us
    ppermute x37, waiting for transfers between devices, partner(): return lax.ppermute(value, axes, [(i, i ^ offset) for i in range(size)])  26.5 us
    pallas_call x2, Pallas kernels, attend(): pl.pallas_call(functools.partial(attend_kernel, offset=offset), in_specs=...  15.9 us
    pallas_call x2, Pallas kernels, experts(): pl.pallas_call(kernel, in_specs=[in_vmem()] * plane + [in_hbm()] * 4, out...  15.3 us
    unnamed x58, local copies, waits for them, and re-layouts  10.6 us
    pallas_call x1, Pallas kernels, shared_terms(): pl.pallas_call(functools.partial(shared_kernel, side=side), in_specs=[in_...  8.35 us
    pallas_call x2, Pallas kernels, select(): pl.pallas_call(functools.partial(select_kernel, count=count, plane=plane,...  3.8 us
  transfers between devices with their start and end apart: 37, of which 12 were waited for; matrix products, arithmetic and copies ran while one was open for 4% of the time, Pallas kernels for 34%

profile of v9, /device:TPU:0, one launch (start us, length us, event | category | flops | bytes accessed | tf_op | source)
XLA Modules:
  0.0 134.1 jit_solution(7281186063895825132)
XLA Ops:
  1.2 1.4 %collective-permute-done.1.second = bf16[64,2048]{1,0:T(8,128)(2,1)S(1)} collective-permute-done((bf16[64,2048]{1,0:T(8,128)(2,1)}, bf16[64,2048]{1,0:T(8,128)(2,1)S(1)}, u32[]{:S(2)}, u32[]{:S(2)}) %collective-permute-start.1) | collective-permute-done | bytes 262176 | tf_op jit(solution)/shard_map/ppermute | solution.py:29
  2.9 2.6 %collective-permute-start = (bf16[64,2048]{1,0:T(8,128)(2,1)}, bf16[64,2048]{1,0:T(8,128)(2,1)S(1)}, u32[]{:S(2)}, u32[]{:S(2)}) collective-permute-start(bf16[64,2048]{1,0:T(8,128)(2,1)} %bitcast.28), channel_id=1, source_target_pairs={{0,2},{2,0},{1,3},{3,1},{4,6},{6,4},{5,7},{7,5},{8,10},{10,8},{9,1... | collective-permute-start | bytes 786440 | tf_op jit(solution)/shard_map/ppermute | solution.py:29
  7.5 2.0 %prepare.1 = (f32[4,64,64]{2,1,0:T(8,128)S(1)}, f32[4,64,128]{2,1,0:T(8,128)S(1)}, f32[4,64,128]{2,1,0:T(8,128)S(1)}) custom-call(s32[4]{0:T(128)S(1)} %copy-done.14, s32[4,64]{1,0:T(4,128)S(1)} %copy-done.15, f32[1,128]{1,0:T(1,128)S(1)} %copy-done.16), custom_call_target="tpu_custom_call" | custom-call | flops 1024 | bytes 1024 | tf_op jit(solution)/shard_map/prepare/pallas_call | solution.py:68
  12.6 2.5 %collective-permute-done.2.second = bf16[64,2048]{1,0:T(8,128)(2,1)S(1)} collective-permute-done((bf16[64,2048]{1,0:T(8,128)(2,1)S(1)}, bf16[64,2048]{1,0:T(8,128)(2,1)S(1)}, u32[]{:S(2)}, u32[]{:S(2)}) %collective-permute-start.2) | collective-permute-done | bytes 262176 | tf_op jit(solution)/shard_map/ppermute | solution.py:29
  16.7 8.2 %attend.2 = (f32[64,2048]{1,0:T(8,128)}, bf16[64,2048]{1,0:T(8,128)(2,1)}, bf16[64,256]{1,0:T(8,128)(2,1)}, bf16[64,256]{1,0:T(8,128)(2,1)}) custom-call(s32[1]{0:T(128)} %bitcast.2.place, s32[4]{0:T(128)} %lengths.5, bf16[64,2048]{1,0:T(8,128)(2,1)} %copy-done.21, bf16[64,2048]{1,0:T(8,128)(2,1)} %copy-done.22, f32[1,2048]{1,0:T(1,128)} %bitcast.40, ...), custom_call_target="tpu_custom_call" | custom-call | flops 1024 | bytes 1024 | tf_op jit(solution)/shard_map/attend/pallas_call | solution.py:204
  25.2 1.6 %collective-permute-done.5 = bf16[64,2048]{1,0:T(8,128)(2,1)S(1)} collective-permute-done((bf16[64,2048]{1,0:T(8,128)(2,1)}, bf16[64,2048]{1,0:T(8,128)(2,1)S(1)}, u32[]{:S(2)}, u32[]{:S(2)}) %collective-permute-start.5) | collective-permute-done | bytes 262176 | tf_op jit(solution)/shard_map/ppermute | solution.py:29
  26.9 1.1 add_convert_fusion
  29.0 7.7 %attend.3 = (f32[64,2048]{1,0:T(8,128)}, bf16[64,2048]{1,0:T(8,128)(2,1)}, bf16[64,256]{1,0:T(8,128)(2,1)}, bf16[64,256]{1,0:T(8,128)(2,1)}) custom-call(s32[1]{0:T(128)} %bitcast.2.place, s32[4]{0:T(128)} %lengths.5, bf16[64,2048]{1,0:T(8,128)(2,1)} %bitcast.29, bf16[64,2048]{1,0:T(8,128)(2,1)} %copy-done.20, f32[1,2048]{1,0:T(1,128)} %bitcast.41, ...), custom_call_target="tpu_custom_call" | custom-call | flops 1024 | bytes 1024 | tf_op jit(solution)/shard_map/attend/pallas_call | solution.py:204
  36.9 1.1 convert_add_fusion.term
  39.5 7.5 %collective-permute-start.12 = (bf16[64,2176]{1,0:T(8,128)(2,1)S(1)}, bf16[64,2176]{1,0:T(8,128)(2,1)S(1)}, u32[]{:S(2)}, u32[]{:S(2)}) collective-permute-start(bf16[64,2176]{1,0:T(8,128)(2,1)S(1)} %get-tuple-element.120.refs_2_), channel_id=1, source_target_pairs={{0,24},{8,16},{16,8},{24,0},{1,25},{9,17},{17,9},{25,1},{2,26},{10... | collective-permute-start | bytes 835592 | tf_op jit(solution)/shard_map/ppermute | solution.py:29
  47.9 7.2 %collective-permute-done.11.refs_1_ = bf16[64,2048]{1,0:T(8,128)(2,1)} collective-permute-done((bf16[64,2048]{1,0:T(8,128)(2,1)S(1)}, bf16[64,2048]{1,0:T(8,128)(2,1)}, u32[]{:S(2)}, u32[]{:S(2)}) %collective-permute-start.11) | collective-permute-done | bytes 262176 | tf_op jit(solution)/shard_map/ppermute | solution.py:29
  55.1 8.3 %shared.1 = (f32[64,2048]{1,0:T(8,128)}, bf16[64,2048]{1,0:T(8,128)(2,1)}) custom-call(bf16[64,2048]{1,0:T(8,128)(2,1)} %copy-done.10, bf16[64,2048]{1,0:T(8,128)(2,1)} %collective-permute-done.11.refs_1_, bf16[352,2048]{1,0:T(8,128)(2,1)} %bitcast.36, bf16[352,2048]{1,0:T(8,128)(2,1)} %bitcast.38, bf16[352,2048]{1,0:T(8,128)(2,1)} %refs_4_.1, ...), custom_call_target="tpu_custom_call" | custom-call | flops 1024 | bytes 1024 | tf_op jit(solution)/shard_map/shared/pallas_call | solution.py:353
  63.5 1.6 %select.2 = (bf16[64,2048]{1,0:T(8,128)(2,1)S(1)}, bf16[64,2048]{1,0:T(8,128)(2,1)S(1)}, bf16[64,2048]{1,0:T(8,128)(2,1)S(1)}, bf16[64,2048]{1,0:T(8,128)(2,1)S(...) custom-call(s32[4]{0:T(128)S(1)} %xor_add_fusion.refs_0_, bf16[2048,16]{1,0:T(8,128)(2,1)S(1)} %copy.21.refs_1_, ...), custom_call_target="tpu_custom_call" | custom-call | flops 1024 | bytes 1024 | tf_op jit(solution)/shard_map/select/pallas_call | solution.py:460
  65.5 3.2 %collective-permute-start.15 = (bf16[64,2048]{1,0:T(8,128)(2,1)S(1)}, bf16[64,2048]{1,0:T(8,128)(2,1)S(1)}, u32[]{:S(2)}, u32[]{:S(2)}) collective-permute-start(bf16[64,2048]{1,0:T(8,128)(2,1)S(1)} %get-tuple-element.127), channel_id=1, source_target_pairs={{0,6},{2,4},{4,2},{6,0},{1,7},{3,5},{5,3},{7,1},{8,14},{10,12},{12... | collective-permute-start | bytes 786440 | tf_op jit(solution)/shard_map/ppermute | solution.py:29
  68.7 3.2 %collective-permute-done.16.refs_2_ = bf16[64,2176]{1,0:T(8,128)(2,1)} collective-permute-done((bf16[64,2176]{1,0:T(8,128)(2,1)S(1)}, bf16[64,2176]{1,0:T(8,128)(2,1)}, u32[]{:S(2)}, u32[]{:S(2)}) %collective-permute-start.16) | collective-permute-done | bytes 278560 | tf_op jit(solution)/shard_map/ppermute | solution.py:29
  71.9 2.2 %select.3 = (bf16[64,2048]{1,0:T(8,128)(2,1)S(1)}, bf16[64,2048]{1,0:T(8,128)(2,1)S(1)}, bf16[64,2048]{1,0:T(8,128)(2,1)S(1)}, bf16[64,2048]{1,0:T(8,128)(2,1)S(...) custom-call(s32[4]{0:T(128)S(1)} %xor_add_fusion.refs_0_, bf16[2048,16]{1,0:T(8,128)(2,1)S(1)} %copy.21.refs_1_, ...), custom_call_target="tpu_custom_call" | custom-call | flops 1024 | bytes 1024 | tf_op jit(solution)/shard_map/select/pallas_call | solution.py:460
  74.5 3.2 %collective-permute-start.20 = (bf16[64,2048]{1,0:T(8,128)(2,1)S(1)}, bf16[64,2048]{1,0:T(8,128)(2,1)S(1)}, u32[]{:S(2)}, u32[]{:S(2)}) collective-permute-start(bf16[64,2048]{1,0:T(8,128)(2,1)S(1)} %get-tuple-element.138), channel_id=1, source_target_pairs={{0,6},{2,4},{4,2},{6,0},{1,7},{3,5},{5,3},{7,1},{8,14},{10,12},{12... | collective-permute-start | bytes 786440 | tf_op jit(solution)/shard_map/ppermute | solution.py:29
  77.6 1.7 %collective-permute-done.14.refs_2_ = bf16[64,2048]{1,0:T(8,128)(2,1)S(1)} collective-permute-done((bf16[64,2048]{1,0:T(8,128)(2,1)S(1)}, bf16[64,2048]{1,0:T(8,128)(2,1)S(1)}, u32[]{:S(2)}, u32[]{:S(2)}) %collective-permute-start.14) | collective-permute-done | bytes 262176 | tf_op jit(solution)/shard_map/ppermute | solution.py:29
  79.4 1.1 collective-permute-start.21
  80.5 2.6 %copy-done.1 = bf16[1,2048,1408]{2,1,0:T(8,128)(2,1)S(1)} copy-done((bf16[1,2048,1408]{2,1,0:T(8,128)(2,1)S(1)}, bf16[1,2048,1408]{2,1,0:T(8,128)(2,1)}, u32[]{:S(2)}) %copy-start.1) | copy-done | bytes 5767192
  83.2 1.8 %copy-done.4 = bf16[704,2048]{1,0:T(8,128)(2,1)S(1)} copy-done((bf16[704,2048]{1,0:T(8,128)(2,1)S(1)}, bf16[704,2048]{1,0:T(8,128)(2,1)}, u32[]{:S(2)}) %copy-start.4) | copy-done | bytes 2883608
  85.0 7.6 %expert.2 = (bf16[32,2048]{1,0:T(8,128)(2,1)S(1)}, bf16[32,2048]{1,0:T(8,128)(2,1)S(1)}, bf16[32,2048]{1,0:T(8,128)(2,1)S(1)}, bf16[32,2048]{1,0:T(8,128)(2,1)S(...) custom-call(bf16[64,2048]{1,0:T(8,128)(2,1)S(1)} %get-tuple-element., ...), custom_call_target="tpu_custom_call" | custom-call | flops 1024 | bytes 1024 | tf_op jit(solution)/shard_map/expert/pallas_call | solution.py:300
  93.8 2.4 %collective-permute-start.27 = (bf16[32,2048]{1,0:T(8,128)(2,1)S(1)}, bf16[32,2048]{1,0:T(8,128)(2,1)S(1)}, u32[]{:S(2)}, u32[]{:S(2)}) collective-permute-start(bf16[32,2048]{1,0:T(8,128)(2,1)S(1)} %get-tuple-element.142), channel_id=1, source_target_pairs={{0,6},{2,4},{4,2},{6,0},{1,7},{3,5},{5,3},{7,1},{8,14},{10,12},{12... | collective-permute-start | bytes 393224 | tf_op jit(solution)/shard_map/ppermute | solution.py:29
  96.2 7.6 %expert.3 = (bf16[32,2048]{1,0:T(8,128)(2,1)S(1)}, bf16[32,2048]{1,0:T(8,128)(2,1)S(1)}, bf16[32,2048]{1,0:T(8,128)(2,1)S(1)}, bf16[32,2048]{1,0:T(8,128)(2,1)S(...) custom-call(bf16[64,2048]{1,0:T(8,128)(2,1)S(1)} %get-tuple-element., ...), custom_call_target="tpu_custom_call" | custom-call | flops 1024 | bytes 1024 | tf_op jit(solution)/shard_map/expert/pallas_call | solution.py:300
  105.9 2.6 %collective-permute-start.24 = (bf16[32,2048]{1,0:T(8,128)(2,1)S(1)}, bf16[32,2048]{1,0:T(8,128)(2,1)S(1)}, u32[]{:S(2)}, u32[]{:S(2)}) collective-permute-start(bf16[32,2048]{1,0:T(8,128)(2,1)S(1)} %get-tuple-element.151), channel_id=1, source_target_pairs={{0,6},{2,4},{4,2},{6,0},{1,7},{3,5},{5,3},{7,1},{8,14},{10,12},{12... | collective-permute-start | bytes 393224 | tf_op jit(solution)/shard_map/ppermute | solution.py:29
  110.5 3.3 %collective-permute-done.23.refs_2_ = bf16[32,2048]{1,0:T(8,128)(2,1)S(1)} collective-permute-done((bf16[32,2048]{1,0:T(8,128)(2,1)S(1)}, bf16[32,2048]{1,0:T(8,128)(2,1)S(1)}, u32[]{:S(2)}, u32[]{:S(2)}) %collective-permute-start.23) | collective-permute-done | bytes 131104 | tf_op jit(solution)/shard_map/ppermute | solution.py:29
  114.8 6.3 %collective-permute-start.32 = (bf16[64,2048]{1,0:T(8,128)(2,1)S(1)}, bf16[64,2048]{1,0:T(8,128)(2,1)S(1)}, u32[]{:S(2)}, u32[]{:S(2)}) collective-permute-start(bf16[64,2048]{1,0:T(8,128)(2,1)S(1)} %combine.4), channel_id=1, source_target_pairs={{0,16},{8,24},{16,0},{24,8},{1,17},{9,25},{17,1},{25,9},{2,18},{10... | collective-permute-start | bytes 786440 | tf_op jit(solution)/shard_map/ppermute | solution.py:29
  122.2 4.1 %collective-permute-start.29 = (bf16[32,2048]{1,0:T(8,128)(2,1)S(1)}, bf16[32,2048]{1,0:T(8,128)(2,1)S(1)}, u32[]{:S(2)}, u32[]{:S(2)}) collective-permute-start(bf16[32,2048]{1,0:T(8,128)(2,1)S(1)} %copy-done.18), channel_id=1, source_target_pairs={{0,2},{2,0},{4,6},{6,4},{1,3},{3,1},{5,7},{7,5},{8,10},{10,8},{12,... | collective-permute-start | bytes 393224 | tf_op jit(solution)/shard_map/ppermute | solution.py:29
  126.3 1.5 %collective-permute-start.31 = (bf16[32,2048]{1,0:T(8,128)(2,1)S(1)}, bf16[32,2048]{1,0:T(8,128)(2,1)S(1)}, u32[]{:S(2)}, u32[]{:S(2)}) collective-permute-start(bf16[32,2048]{1,0:T(8,128)(2,1)S(1)} %get-tuple-element.160), channel_id=1, source_target_pairs={{0,6},{2,4},{4,2},{6,0},{1,7},{3,5},{5,3},{7,1},{8,14},{10,12},{12... | collective-permute-start | bytes 393224 | tf_op jit(solution)/shard_map/ppermute | solution.py:29
  128.8 1.2 gather_fusion.1
  130.0 2.7 %collective-permute-done.30.refs_2_ = bf16[32,2048]{1,0:T(8,128)(2,1)S(1)} collective-permute-done((bf16[32,2048]{1,0:T(8,128)(2,1)S(1)}, bf16[32,2048]{1,0:T(8,128)(2,1)S(1)}, u32[]{:S(2)}, u32[]{:S(2)}) %collective-permute-start.30) | collective-permute-done | bytes 131104 | tf_op jit(solution)/shard_map/ppermute | solution.py:29
  133.0 1.1 final.1
  (123 shorter events, 20.6 us)
Async XLA Ops:
  2.5 13.1 %collective-permute-start.4 = (bf16[704,2048]{1,0:T(8,128)(2,1)}, bf16[704,2048]{1,0:T(8,128)(2,1)S(1)}, u32[]{:S(2)}, u32[]{:S(2)}) collective-permute-start(bf16[704,2048]{1,0:T(8,128)(2,1)} %bitcast.24), channel_id=1, source_target_pairs={{0,1},{1,0},{2,3},{3,2},{4,5},{5,4},{6,7},{7,6},{8,9},{9,8},{10,11... | collective-permute-start | bytes 8650760 | tf_op jit(solution)/shard_map/ppermute | solution.py:29
  2.9 9.7 %collective-permute-start = (bf16[64,2048]{1,0:T(8,128)(2,1)}, bf16[64,2048]{1,0:T(8,128)(2,1)S(1)}, u32[]{:S(2)}, u32[]{:S(2)}) collective-permute-start(bf16[64,2048]{1,0:T(8,128)(2,1)} %bitcast.28), channel_id=1, source_target_pairs={{0,2},{2,0},{1,3},{3,1},{4,6},{6,4},{5,7},{7,5},{8,10},{10,8},{9,1... | collective-permute-start | bytes 786440 | tf_op jit(solution)/shard_map/ppermute | solution.py:29
  15.1 10.1 %collective-permute-start.6 = (bf16[352,2048]{1,0:T(8,128)(2,1)}, bf16[352,2048]{1,0:T(8,128)(2,1)}, u32[]{:S(2)}, u32[]{:S(2)}) collective-permute-start(bf16[352,2048]{1,0:T(8,128)(2,1)} %bitcast.37), channel_id=1, source_target_pairs={{0,1},{1,0},{2,3},{3,2},{4,5},{5,4},{6,7},{7,6},{8,9},{9,8},{10,11... | collective-permute-start | bytes 4325384 | tf_op jit(solution)/shard_map/ppermute | solution.py:29
  15.2 9.9 %collective-permute-start.7 = (bf16[352,2048]{1,0:T(8,128)(2,1)}, bf16[352,2048]{1,0:T(8,128)(2,1)}, u32[]{:S(2)}, u32[]{:S(2)}) collective-permute-start(bf16[352,2048]{1,0:T(8,128)(2,1)} %refs_4_.1), channel_id=1, source_target_pairs={{0,1},{1,0},{2,3},{3,2},{4,5},{5,4},{6,7},{7,6},{8,9},{9,8},{10,11... | collective-permute-start | bytes 4325384 | tf_op jit(solution)/shard_map/ppermute | solution.py:29
  26.8 11.2 %collective-permute-start.9 = (bf16[2048,1408]{1,0:T(8,128)(2,1)}, bf16[2048,1408]{1,0:T(8,128)(2,1)}, u32[]{:S(2)}, u32[]{:S(2)}) collective-permute-start(bf16[2048,1408]{1,0:T(8,128)(2,1)} %bitcast.21), channel_id=1, source_target_pairs={{0,1},{1,0},{2,3},{3,2},{4,5},{5,4},{6,7},{7,6},{8,9},{9,8},{10,11... | collective-permute-start | bytes 17301512 | tf_op jit(solution)/shard_map/ppermute | solution.py:29
  28.0 8.9 %collective-permute-start.8 = (bf16[64,2048]{1,0:T(8,128)(2,1)S(1)}, bf16[64,2048]{1,0:T(8,128)(2,1)S(1)}, u32[]{:S(2)}, u32[]{:S(2)}) collective-permute-start(bf16[64,2048]{1,0:T(8,128)(2,1)S(1)} %add_convert_fusion), channel_id=1, source_target_pairs={{0,2},{2,0},{1,3},{3,1},{4,6},{6,4},{5,7},{7,5},{8,10},{10,8},{9,1... | collective-permute-start | bytes 786440 | tf_op jit(solution)/shard_map/ppermute | solution.py:29
  39.5 24.0 %collective-permute-start.12 = (bf16[64,2176]{1,0:T(8,128)(2,1)S(1)}, bf16[64,2176]{1,0:T(8,128)(2,1)S(1)}, u32[]{:S(2)}, u32[]{:S(2)}) collective-permute-start(bf16[64,2176]{1,0:T(8,128)(2,1)S(1)} %get-tuple-element.120.refs_2_), channel_id=1, source_target_pairs={{0,24},{8,16},{16,8},{24,0},{1,25},{9,17},{17,9},{25,1},{2,26},{10... | collective-permute-start | bytes 835592 | tf_op jit(solution)/shard_map/ppermute | solution.py:29
  47.0 8.2 %collective-permute-start.11 = (bf16[64,2048]{1,0:T(8,128)(2,1)S(1)}, bf16[64,2048]{1,0:T(8,128)(2,1)}, u32[]{:S(2)}, u32[]{:S(2)}) collective-permute-start(bf16[64,2048]{1,0:T(8,128)(2,1)S(1)} %get-tuple-element.115.refs_0_), channel_id=1, source_target_pairs={{0,2},{2,0},{1,3},{3,1},{4,6},{6,4},{5,7},{7,5},{8,10},{10,8},{9,1... | collective-permute-start | bytes 786440 | tf_op jit(solution)/shard_map/ppermute | solution.py:29
  47.0 25.0 %collective-permute-start.16 = (bf16[64,2176]{1,0:T(8,128)(2,1)S(1)}, bf16[64,2176]{1,0:T(8,128)(2,1)}, u32[]{:S(2)}, u32[]{:S(2)}) collective-permute-start(bf16[64,2176]{1,0:T(8,128)(2,1)S(1)} %get-tuple-element.120.refs_2_), channel_id=1, source_target_pairs={{0,16},{8,24},{16,0},{24,8},{1,17},{9,25},{17,1},{25,9},{2,18},{10... | collective-permute-start | bytes 835592 | tf_op jit(solution)/shard_map/ppermute | solution.py:29
  47.4 24.5 %collective-permute-start.17 = (bf16[64,2176]{1,0:T(8,128)(2,1)S(1)}, bf16[64,2176]{1,0:T(8,128)(2,1)}, u32[]{:S(2)}, u32[]{:S(2)}) collective-permute-start(bf16[64,2176]{1,0:T(8,128)(2,1)S(1)} %get-tuple-element.120.refs_2_), channel_id=1, source_target_pairs={{0,8},{8,0},{16,24},{24,16},{1,9},{9,1},{17,25},{25,17},{2,10},{10... | collective-permute-start | bytes 835592 | tf_op jit(solution)/shard_map/ppermute | solution.py:29
  65.2 9.3 %collective-permute-start.13 = (bf16[64,2048]{1,0:T(8,128)(2,1)S(1)}, bf16[64,2048]{1,0:T(8,128)(2,1)S(1)}, u32[]{:S(2)}, u32[]{:S(2)}) collective-permute-start(bf16[64,2048]{1,0:T(8,128)(2,1)S(1)} %get-tuple-element.125), channel_id=1, source_target_pairs={{0,2},{2,0},{4,6},{6,4},{1,3},{3,1},{5,7},{7,5},{8,10},{10,8},{12,... | collective-permute-start | bytes 786440 | tf_op jit(solution)/shard_map/ppermute | solution.py:29
  65.5 13.9 %collective-permute-start.14 = (bf16[64,2048]{1,0:T(8,128)(2,1)S(1)}, bf16[64,2048]{1,0:T(8,128)(2,1)S(1)}, u32[]{:S(2)}, u32[]{:S(2)}) collective-permute-start(bf16[64,2048]{1,0:T(8,128)(2,1)S(1)} %get-tuple-element.126), channel_id=1, source_target_pairs={{0,4},{2,6},{4,0},{6,2},{1,5},{3,7},{5,1},{7,3},{8,12},{10,14},{12... | collective-permute-start | bytes 786440 | tf_op jit(solution)/shard_map/ppermute | solution.py:29
  65.5 15.0 %collective-permute-start.15 = (bf16[64,2048]{1,0:T(8,128)(2,1)S(1)}, bf16[64,2048]{1,0:T(8,128)(2,1)S(1)}, u32[]{:S(2)}, u32[]{:S(2)}) collective-permute-start(bf16[64,2048]{1,0:T(8,128)(2,1)S(1)} %get-tuple-element.127), channel_id=1, source_target_pairs={{0,6},{2,4},{4,2},{6,0},{1,7},{3,5},{5,3},{7,1},{8,14},{10,12},{12... | collective-permute-start | bytes 786440 | tf_op jit(solution)/shard_map/ppermute | solution.py:29
  74.1 19.5 %collective-permute-start.18 = (bf16[64,2048]{1,0:T(8,128)(2,1)S(1)}, bf16[64,2048]{1,0:T(8,128)(2,1)S(1)}, u32[]{:S(2)}, u32[]{:S(2)}) collective-permute-start(bf16[64,2048]{1,0:T(8,128)(2,1)S(1)} %get-tuple-element.136), channel_id=1, source_target_pairs={{0,2},{2,0},{4,6},{6,4},{1,3},{3,1},{5,7},{7,5},{8,10},{10,8},{12,... | collective-permute-start | bytes 786440 | tf_op jit(solution)/shard_map/ppermute | solution.py:29
  74.2 19.6 %collective-permute-start.19 = (bf16[64,2048]{1,0:T(8,128)(2,1)S(1)}, bf16[64,2048]{1,0:T(8,128)(2,1)S(1)}, u32[]{:S(2)}, u32[]{:S(2)}) collective-permute-start(bf16[64,2048]{1,0:T(8,128)(2,1)S(1)} %get-tuple-element.137), channel_id=1, source_target_pairs={{0,4},{2,6},{4,0},{6,2},{1,5},{3,7},{5,1},{7,3},{8,12},{10,14},{12... | collective-permute-start | bytes 786440 | tf_op jit(solution)/shard_map/ppermute | solution.py:29
  74.5 21.7 %collective-permute-start.20 = (bf16[64,2048]{1,0:T(8,128)(2,1)S(1)}, bf16[64,2048]{1,0:T(8,128)(2,1)S(1)}, u32[]{:S(2)}, u32[]{:S(2)}) collective-permute-start(bf16[64,2048]{1,0:T(8,128)(2,1)S(1)} %get-tuple-element.138), channel_id=1, source_target_pairs={{0,6},{2,4},{4,2},{6,0},{1,7},{3,5},{5,3},{7,1},{8,14},{10,12},{12... | collective-permute-start | bytes 786440 | tf_op jit(solution)/shard_map/ppermute | solution.py:29
  79.4 16.8 %collective-permute-start.21 = (bf16[64,2048]{1,0:T(8,128)(2,1)S(1)}, bf16[64,2048]{1,0:T(8,128)(2,1)S(1)}, u32[]{:S(2)}, u32[]{:S(2)}) collective-permute-start(bf16[64,2048]{1,0:T(8,128)(2,1)S(1)} %copy-done.26), channel_id=1, source_target_pairs={{0,2},{2,0},{1,3},{3,1},{4,6},{6,4},{5,7},{7,5},{8,10},{10,8},{9,1... | collective-permute-start | bytes 786440 | tf_op jit(solution)/shard_map/ppermute | solution.py:29
  92.6 12.4 %collective-permute-start.25 = (bf16[32,2048]{1,0:T(8,128)(2,1)S(1)}, bf16[32,2048]{1,0:T(8,128)(2,1)S(1)}, u32[]{:S(2)}, u32[]{:S(2)}) collective-permute-start(bf16[32,2048]{1,0:T(8,128)(2,1)S(1)} %get-tuple-element.140), channel_id=1, source_target_pairs={{0,2},{2,0},{4,6},{6,4},{1,3},{3,1},{5,7},{7,5},{8,10},{10,8},{12,... | collective-permute-start | bytes 393224 | tf_op jit(solution)/shard_map/ppermute | solution.py:29
  93.6 11.5 %collective-permute-start.26 = (bf16[32,2048]{1,0:T(8,128)(2,1)S(1)}, bf16[32,2048]{1,0:T(8,128)(2,1)S(1)}, u32[]{:S(2)}, u32[]{:S(2)}) collective-permute-start(bf16[32,2048]{1,0:T(8,128)(2,1)S(1)} %get-tuple-element.141), channel_id=1, source_target_pairs={{0,4},{2,6},{4,0},{6,2},{1,5},{3,7},{5,1},{7,3},{8,12},{10,14},{12... | collective-permute-start | bytes 393224 | tf_op jit(solution)/shard_map/ppermute | solution.py:29
  93.8 11.3 %collective-permute-start.27 = (bf16[32,2048]{1,0:T(8,128)(2,1)S(1)}, bf16[32,2048]{1,0:T(8,128)(2,1)S(1)}, u32[]{:S(2)}, u32[]{:S(2)}) collective-permute-start(bf16[32,2048]{1,0:T(8,128)(2,1)S(1)} %get-tuple-element.142), channel_id=1, source_target_pairs={{0,6},{2,4},{4,2},{6,0},{1,7},{3,5},{5,3},{7,1},{8,14},{10,12},{12... | collective-permute-start | bytes 393224 | tf_op jit(solution)/shard_map/ppermute | solution.py:29
  103.9 6.5 %collective-permute-start.22 = (bf16[32,2048]{1,0:T(8,128)(2,1)S(1)}, bf16[32,2048]{1,0:T(8,128)(2,1)S(1)}, u32[]{:S(2)}, u32[]{:S(2)}) collective-permute-start(bf16[32,2048]{1,0:T(8,128)(2,1)S(1)} %get-tuple-element.149), channel_id=1, source_target_pairs={{0,2},{2,0},{4,6},{6,4},{1,3},{3,1},{5,7},{7,5},{8,10},{10,8},{12,... | collective-permute-start | bytes 393224 | tf_op jit(solution)/shard_map/ppermute | solution.py:29
  104.9 8.9 %collective-permute-start.23 = (bf16[32,2048]{1,0:T(8,128)(2,1)S(1)}, bf16[32,2048]{1,0:T(8,128)(2,1)S(1)}, u32[]{:S(2)}, u32[]{:S(2)}) collective-permute-start(bf16[32,2048]{1,0:T(8,128)(2,1)S(1)} %get-tuple-element.150), channel_id=1, source_target_pairs={{0,4},{2,6},{4,0},{6,2},{1,5},{3,7},{5,1},{7,3},{8,12},{10,14},{12... | collective-permute-start | bytes 393224 | tf_op jit(solution)/shard_map/ppermute | solution.py:29
  105.3 17.0 %collective-permute-start.28 = (bf16[64,2048]{1,0:T(8,128)(2,1)S(1)}, bf16[64,2048]{1,0:T(8,128)(2,1)S(1)}, u32[]{:S(2)}, u32[]{:S(2)}) collective-permute-start(bf16[64,2048]{1,0:T(8,128)(2,1)S(1)} %combine.5), channel_id=1, source_target_pairs={{0,24},{8,16},{16,8},{24,0},{1,25},{9,17},{17,9},{25,1},{2,26},{10... | collective-permute-start | bytes 786440 | tf_op jit(solution)/shard_map/ppermute | solution.py:29
  105.9 8.6 %collective-permute-start.24 = (bf16[32,2048]{1,0:T(8,128)(2,1)S(1)}, bf16[32,2048]{1,0:T(8,128)(2,1)S(1)}, u32[]{:S(2)}, u32[]{:S(2)}) collective-permute-start(bf16[32,2048]{1,0:T(8,128)(2,1)S(1)} %get-tuple-element.151), channel_id=1, source_target_pairs={{0,6},{2,4},{4,2},{6,0},{1,7},{3,5},{5,3},{7,1},{8,14},{10,12},{12... | collective-permute-start | bytes 393224 | tf_op jit(solution)/shard_map/ppermute | solution.py:29
  108.5 12.6 %collective-permute-start.33 = (bf16[32,2048]{1,0:T(8,128)(2,1)S(1)}, bf16[32,2048]{1,0:T(8,128)(2,1)S(1)}, u32[]{:S(2)}, u32[]{:S(2)}) collective-permute-start(bf16[32,2048]{1,0:T(8,128)(2,1)S(1)} %get-tuple-element.169), channel_id=1, source_target_pairs={{0,2},{2,0},{4,6},{6,4},{1,3},{3,1},{5,7},{7,5},{8,10},{10,8},{12,... | collective-permute-start | bytes 393224 | tf_op jit(solution)/shard_map/ppermute | solution.py:29
  110.4 10.7 %collective-permute-start.34 = (bf16[32,2048]{1,0:T(8,128)(2,1)S(1)}, bf16[32,2048]{1,0:T(8,128)(2,1)S(1)}, u32[]{:S(2)}, u32[]{:S(2)}) collective-permute-start(bf16[32,2048]{1,0:T(8,128)(2,1)S(1)} %get-tuple-element.170), channel_id=1, source_target_pairs={{0,4},{2,6},{4,0},{6,2},{1,5},{3,7},{5,1},{7,3},{8,12},{10,14},{12... | collective-permute-start | bytes 393224 | tf_op jit(solution)/shard_map/ppermute | solution.py:29
  113.8 7.3 %collective-permute-start.35 = (bf16[32,2048]{1,0:T(8,128)(2,1)S(1)}, bf16[32,2048]{1,0:T(8,128)(2,1)S(1)}, u32[]{:S(2)}, u32[]{:S(2)}) collective-permute-start(bf16[32,2048]{1,0:T(8,128)(2,1)S(1)} %get-tuple-element.171), channel_id=1, source_target_pairs={{0,6},{2,4},{4,2},{6,0},{1,7},{3,5},{5,3},{7,1},{8,14},{10,12},{12... | collective-permute-start | bytes 393224 | tf_op jit(solution)/shard_map/ppermute | solution.py:29
  114.8 18.2 %collective-permute-start.32 = (bf16[64,2048]{1,0:T(8,128)(2,1)S(1)}, bf16[64,2048]{1,0:T(8,128)(2,1)S(1)}, u32[]{:S(2)}, u32[]{:S(2)}) collective-permute-start(bf16[64,2048]{1,0:T(8,128)(2,1)S(1)} %combine.4), channel_id=1, source_target_pairs={{0,16},{8,24},{16,0},{24,8},{1,17},{9,25},{17,1},{25,9},{2,18},{10... | collective-permute-start | bytes 786440 | tf_op jit(solution)/shard_map/ppermute | solution.py:29
  121.3 11.6 %collective-permute-start.36 = (bf16[64,2048]{1,0:T(8,128)(2,1)S(1)}, bf16[64,2048]{1,0:T(8,128)(2,1)S(1)}, u32[]{:S(2)}, u32[]{:S(2)}) collective-permute-start(bf16[64,2048]{1,0:T(8,128)(2,1)S(1)} %combine.7), channel_id=1, source_target_pairs={{0,8},{8,0},{16,24},{24,16},{1,9},{9,1},{17,25},{25,17},{2,10},{10... | collective-permute-start | bytes 786440 | tf_op jit(solution)/shard_map/ppermute | solution.py:29
  122.2 7.8 %collective-permute-start.29 = (bf16[32,2048]{1,0:T(8,128)(2,1)S(1)}, bf16[32,2048]{1,0:T(8,128)(2,1)S(1)}, u32[]{:S(2)}, u32[]{:S(2)}) collective-permute-start(bf16[32,2048]{1,0:T(8,128)(2,1)S(1)} %copy-done.18), channel_id=1, source_target_pairs={{0,2},{2,0},{4,6},{6,4},{1,3},{3,1},{5,7},{7,5},{8,10},{10,8},{12,... | collective-permute-start | bytes 393224 | tf_op jit(solution)/shard_map/ppermute | solution.py:29
  126.3 6.4 %collective-permute-start.30 = (bf16[32,2048]{1,0:T(8,128)(2,1)S(1)}, bf16[32,2048]{1,0:T(8,128)(2,1)S(1)}, u32[]{:S(2)}, u32[]{:S(2)}) collective-permute-start(bf16[32,2048]{1,0:T(8,128)(2,1)S(1)} %get-tuple-element.159), channel_id=1, source_target_pairs={{0,4},{2,6},{4,0},{6,2},{1,5},{3,7},{5,1},{7,3},{8,12},{10,14},{12... | collective-permute-start | bytes 393224 | tf_op jit(solution)/shard_map/ppermute | solution.py:29
  126.3 6.4 %collective-permute-start.31 = (bf16[32,2048]{1,0:T(8,128)(2,1)S(1)}, bf16[32,2048]{1,0:T(8,128)(2,1)S(1)}, u32[]{:S(2)}, u32[]{:S(2)}) collective-permute-start(bf16[32,2048]{1,0:T(8,128)(2,1)S(1)} %get-tuple-element.160), channel_id=1, source_target_pairs={{0,6},{2,4},{4,2},{6,0},{1,7},{3,5},{5,3},{7,1},{8,14},{10,12},{12... | collective-permute-start | bytes 393224 | tf_op jit(solution)/shard_map/ppermute | solution.py:29
  (33 other events, 405.1 us)

commit v10 on v9

--- a/solution.py
+++ b/solution.py
@@ -235,6 +235,23 @@
     )(place, lengths, first, second, gain, weight, cosine, sine, reach, cache, outward)
 
 
+def add_kernel(left, right, out):
+    total = left[...].astype(jnp.float32) + right[...].astype(jnp.float32)
+    out[...] = total.astype(out.dtype)
+
+
+def add(left, right, dtype):
+    return pl.pallas_call(
+        add_kernel,
+        in_specs=[in_vmem()] * 2,
+        out_specs=in_vmem(),
+        out_shape=jax.ShapeDtypeStruct(left.shape, dtype),
+        compiler_params=pltpu.CompilerParams(vmem_limit_bytes=16 * 2**20),
+        cost_estimate=SMALL,
+        name="add",
+    )(left, right)
+
+
 def silu(values):
     return values / (1.0 + jnp.exp(-values))
 
@@ -310,6 +327,22 @@
         name="expert",
     )(*pieces, inner[0], outer[0], inner[1], outer[1])
     return [list(made[i * plane : (i + 1) * plane]) for i in range(count)]
+
+
+def hold_kernel(*refs):
+    refs[-1][...] = refs[0][...]
+
+
+def hold(token, weights):
+    return pl.pallas_call(
+        hold_kernel,
+        in_specs=[in_vmem()] + [in_hbm()] * len(weights),
+        out_specs=in_vmem(),
+        out_shape=jax.ShapeDtypeStruct(token.shape, token.dtype),
+        compiler_params=pltpu.CompilerParams(vmem_limit_bytes=16 * 2**20),
+        cost_estimate=SMALL,
+        name="hold",
+    )(token, *weights)
 
 
 def shared_kernel(*refs, side):
@@ -585,10 +618,11 @@
             other, middle, late = lax.optimization_barrier((other, middle, late))
             late = partner(late, "c", 1)
         if o:
-            follow = (own_part + other.astype(jnp.float32)).astype(jnp.bfloat16)
-            crossed = partner(follow, "x", o).astype(jnp.float32)
-            terms[o] = crossed if o == side - 1 else crossed + terms[o + 1]
-    own_term = own_part + terms[1] if side > 1 else own_part
+            follow = add(own_part, other, jnp.bfloat16)
+            terms[o] = partner(follow, "x", o)
+    own_term = own_part
+    for o in range(1, side):
+        own_term = add(own_term, terms[o], jnp.float32)
     own_term, late = lax.optimization_barrier((own_term, late))
     others = [other]
     resid, normed, payload = finish(own_rows, own_term, others, ffn_gain[None], routes[0])
@@ -625,6 +659,9 @@
             near_experts, router, [line_rows[k] for k in ks], plane, capacity, top_count
         )
         spread.update(zip(ks, spreads))
+        if len(sent) == 1:
+            token = hold(spreads[0], [inner[0], outer[0], inner[1], outer[1]])
+            sent[0], spread[ks[0]] = lax.optimization_barrier((sent[0], token))
         sent.append([partner(pieces[o], PLANE, o) for o in range(plane)])
     parts = [partner(beside[o - 1], "x", o) for o in range(1, side)]
     made = None

time: 135 us -> 137 us (1.015)
  local copies, waits for them, and re-layouts: 12.4 us -> 20.2 us
  waiting for transfers between devices: 26.5 us -> 23.4 us
  other arithmetic: 2.22 us -> 0.02 us
    unnamed x58 -> x70, local copies, waits for them, and re-layouts: 10.6 us -> 18.4 us
    ppermute x37, waiting for transfers between devices: 26.5 us -> 23.4 us  [partner(): return lax.ppermute(value, axes, [(i, i ^ offset) for i in range(size)])]
  transfers between devices with their start and end apart: 37 -> 37, of which waited for: 12 -> 16; matrix products, arithmetic and copies ran while one was open for 4% -> 2% of each run, Pallas kernels for 34% -> 34%
where the time goes in v10:
time: 137 us; the launch traced here: 135 us
  Pallas kernels  47.5 us (35%)
  starting transfers between devices  43 us (31%)
  waiting for transfers between devices  23.4 us (17%)
  local copies, waits for them, and re-layouts  20.2 us (15%)
    ppermute x37, starting transfers between devices, partner(): return lax.ppermute(value, axes, [(i, i ^ offset) for i in range(size)])  43 us
    ppermute x37, waiting for transfers between devices, partner(): return lax.ppermute(value, axes, [(i, i ^ offset) for i in range(size)])  23.4 us
    unnamed x70, local copies, waits for them, and re-layouts  18.4 us
    pallas_call x2, Pallas kernels, attend(): pl.pallas_call(functools.partial(attend_kernel, offset=offset), in_specs=...  16.4 us
    pallas_call x2, Pallas kernels, experts(): pl.pallas_call(kernel, in_specs=[in_vmem()] * plane + [in_hbm()] * 4, out...  15.3 us
    pallas_call x1, Pallas kernels, shared_terms(): pl.pallas_call(functools.partial(shared_kernel, side=side), in_specs=[in_...  8.29 us
    pallas_call x2, Pallas kernels, select(): pl.pallas_call(functools.partial(select_kernel, count=count, plane=plane,...  3.28 us
  transfers between devices with their start and end apart: 37, of which 16 were waited for; matrix products, arithmetic and copies ran while one was open for 2% of the time, Pallas kernels for 34%

profile of v10, /device:TPU:0, one launch (start us, length us, event | category | flops | bytes accessed | tf_op | source)
XLA Modules:
  0.0 135.5 jit_solution(13417144141123082201)
XLA Ops:
  1.2 1.4 %collective-permute-done.1.second = bf16[64,2048]{1,0:T(8,128)(2,1)S(1)} collective-permute-done((bf16[64,2048]{1,0:T(8,128)(2,1)}, bf16[64,2048]{1,0:T(8,128)(2,1)S(1)}, u32[]{:S(2)}, u32[]{:S(2)}) %collective-permute-start.1) | collective-permute-done | bytes 262176 | tf_op jit(solution)/shard_map/ppermute | solution.py:29
  2.9 2.6 %collective-permute-start = (bf16[64,2048]{1,0:T(8,128)(2,1)}, bf16[64,2048]{1,0:T(8,128)(2,1)S(1)}, u32[]{:S(2)}, u32[]{:S(2)}) collective-permute-start(bf16[64,2048]{1,0:T(8,128)(2,1)} %bitcast.32), channel_id=1, source_target_pairs={{0,2},{2,0},{1,3},{3,1},{4,6},{6,4},{5,7},{7,5},{8,10},{10,8},{9,1... | collective-permute-start | bytes 786440 | tf_op jit(solution)/shard_map/ppermute | solution.py:29
  7.5 2.0 %prepare.1 = (f32[4,64,64]{2,1,0:T(8,128)S(1)}, f32[4,64,128]{2,1,0:T(8,128)S(1)}, f32[4,64,128]{2,1,0:T(8,128)S(1)}) custom-call(s32[4]{0:T(128)S(1)} %copy-done.16, s32[4,64]{1,0:T(4,128)S(1)} %copy-done.17, f32[1,128]{1,0:T(1,128)S(1)} %copy-done.18), custom_call_target="tpu_custom_call" | custom-call | flops 1024 | bytes 1024 | tf_op jit(solution)/shard_map/prepare/pallas_call | solution.py:68
  12.6 2.5 %collective-permute-done.2.second = bf16[64,2048]{1,0:T(8,128)(2,1)S(1)} collective-permute-done((bf16[64,2048]{1,0:T(8,128)(2,1)S(1)}, bf16[64,2048]{1,0:T(8,128)(2,1)S(1)}, u32[]{:S(2)}, u32[]{:S(2)}) %collective-permute-start.2) | collective-permute-done | bytes 262176 | tf_op jit(solution)/shard_map/ppermute | solution.py:29
  16.7 9.2 %attend.2 = (f32[64,2048]{1,0:T(8,128)}, bf16[64,2048]{1,0:T(8,128)(2,1)}, bf16[64,256]{1,0:T(8,128)(2,1)}, bf16[64,256]{1,0:T(8,128)(2,1)}) custom-call(s32[1]{0:T(128)} %bitcast.2.place, s32[4]{0:T(128)} %lengths.5, bf16[64,2048]{1,0:T(8,128)(2,1)} %copy-done.21, bf16[64,2048]{1,0:T(8,128)(2,1)} %copy-done.23, f32[1,2048]{1,0:T(1,128)} %bitcast.44, ...), custom_call_target="tpu_custom_call" | custom-call | flops 1024 | bytes 1024 | tf_op jit(solution)/shard_map/attend/pallas_call | solution.py:204
  26.1 1.6 %collective-permute-done.5.right = bf16[64,2048]{1,0:T(8,128)(2,1)S(1)} collective-permute-done((bf16[64,2048]{1,0:T(8,128)(2,1)}, bf16[64,2048]{1,0:T(8,128)(2,1)S(1)}, u32[]{:S(2)}, u32[]{:S(2)}) %collective-permute-start.5) | collective-permute-done | bytes 262176 | tf_op jit(solution)/shard_map/ppermute | solution.py:29
  29.1 7.2 %attend.3 = (f32[64,2048]{1,0:T(8,128)}, bf16[64,2048]{1,0:T(8,128)(2,1)}, bf16[64,256]{1,0:T(8,128)(2,1)}, bf16[64,256]{1,0:T(8,128)(2,1)}) custom-call(s32[1]{0:T(128)} %bitcast.2.place, s32[4]{0:T(128)} %lengths.5, bf16[64,2048]{1,0:T(8,128)(2,1)} %bitcast.33, bf16[64,2048]{1,0:T(8,128)(2,1)} %copy-done.20, f32[1,2048]{1,0:T(1,128)} %bitcast.45, ...), custom_call_target="tpu_custom_call" | custom-call | flops 1024 | bytes 1024 | tf_op jit(solution)/shard_map/attend/pallas_call | solution.py:204
  39.0 4.3 %collective-permute-start.12 = (bf16[64,2176]{1,0:T(8,128)(2,1)S(1)}, bf16[64,2176]{1,0:T(8,128)(2,1)S(1)}, u32[]{:S(2)}, u32[]{:S(2)}) collective-permute-start(bf16[64,2176]{1,0:T(8,128)(2,1)S(1)} %get-tuple-element.125.refs_2_), channel_id=1, source_target_pairs={{0,24},{8,16},{16,8},{24,0},{1,25},{9,17},{17,9},{25,1},{2,26},{10... | collective-permute-start | bytes 835592 | tf_op jit(solution)/shard_map/ppermute | solution.py:29
  43.3 3.0 %collective-permute-start.17 = (bf16[64,2176]{1,0:T(8,128)(2,1)S(1)}, bf16[64,2176]{1,0:T(8,128)(2,1)S(1)}, u32[]{:S(2)}, u32[]{:S(2)}) collective-permute-start(bf16[64,2176]{1,0:T(8,128)(2,1)S(1)} %get-tuple-element.125.refs_2_), channel_id=1, source_target_pairs={{0,8},{8,0},{16,24},{24,16},{1,9},{9,1},{17,25},{25,17},{2,10},{10... | collective-permute-start | bytes 835592 | tf_op jit(solution)/shard_map/ppermute | solution.py:29
  46.6 4.8 %collective-permute-done.11.refs_1_ = bf16[64,2048]{1,0:T(8,128)(2,1)S(1)} collective-permute-done((bf16[64,2048]{1,0:T(8,128)(2,1)S(1)}, bf16[64,2048]{1,0:T(8,128)(2,1)S(1)}, u32[]{:S(2)}, u32[]{:S(2)}) %collective-permute-start.11) | collective-permute-done | bytes 262176 | tf_op jit(solution)/shard_map/ppermute | solution.py:29
  52.1 8.3 %shared.1 = (f32[64,2048]{1,0:T(8,128)}, bf16[64,2048]{1,0:T(8,128)(2,1)}) custom-call(bf16[64,2048]{1,0:T(8,128)(2,1)} %copy-done.14, bf16[64,2048]{1,0:T(8,128)(2,1)} %copy-done.22, bf16[352,2048]{1,0:T(8,128)(2,1)} %bitcast.40, bf16[352,2048]{1,0:T(8,128)(2,1)} %bitcast.42, bf16[352,2048]{1,0:T(8,128)(2,1)} %refs_4_.1, bf16[352,2048]{1,0:T(8,128)(2,1)} %copy-done.19, ...), custom_call_target="tpu_custom_call" | custom-call | flops 1024 | bytes 1024 | tf_op jit(solution)/shard_map/shared/pallas_call | solution.py:386
  60.4 1.6 %select.2 = (bf16[64,2048]{1,0:T(8,128)(2,1)S(1)}, bf16[64,2048]{1,0:T(8,128)(2,1)S(1)}, bf16[64,2048]{1,0:T(8,128)(2,1)S(1)}, bf16[64,2048]{1,0:T(8,128)(2,1)S(...) custom-call(s32[4]{0:T(128)S(1)} %xor_add_fusion.refs_0_, bf16[2048,16]{1,0:T(8,128)(2,1)S(1)} %copy.21.refs_1_, ...), custom_call_target="tpu_custom_call" | custom-call | flops 1024 | bytes 1024 | tf_op jit(solution)/shard_map/select/pallas_call | solution.py:493
  62.4 1.5 %collective-permute-start.14 = (bf16[64,2048]{1,0:T(8,128)(2,1)S(1)}, bf16[64,2048]{1,0:T(8,128)(2,1)S(1)}, u32[]{:S(2)}, u32[]{:S(2)}) collective-permute-start(bf16[64,2048]{1,0:T(8,128)(2,1)S(1)} %get-tuple-element.131), channel_id=1, source_target_pairs={{0,4},{2,6},{4,0},{6,2},{1,5},{3,7},{5,1},{7,3},{8,12},{10,14},{12... | collective-permute-start | bytes 786440 | tf_op jit(solution)/shard_map/ppermute | solution.py:29
  63.9 1.7 %collective-permute-start.15 = (bf16[64,2048]{1,0:T(8,128)(2,1)S(1)}, bf16[64,2048]{1,0:T(8,128)(2,1)S(1)}, u32[]{:S(2)}, u32[]{:S(2)}) collective-permute-start(bf16[64,2048]{1,0:T(8,128)(2,1)S(1)} %get-tuple-element.132), channel_id=1, source_target_pairs={{0,6},{2,4},{4,2},{6,0},{1,7},{3,5},{5,3},{7,1},{8,14},{10,12},{12... | collective-permute-start | bytes 786440 | tf_op jit(solution)/shard_map/ppermute | solution.py:29
  65.6 1.5 %collective-permute-done.16.refs_2_ = bf16[64,2176]{1,0:T(8,128)(2,1)S(1)} collective-permute-done((bf16[64,2176]{1,0:T(8,128)(2,1)S(1)}, bf16[64,2176]{1,0:T(8,128)(2,1)S(1)}, u32[]{:S(2)}, u32[]{:S(2)}) %collective-permute-start.16) | collective-permute-done | bytes 278560 | tf_op jit(solution)/shard_map/ppermute | solution.py:29
  67.2 1.6 %select.3 = (bf16[64,2048]{1,0:T(8,128)(2,1)S(1)}, bf16[64,2048]{1,0:T(8,128)(2,1)S(1)}, bf16[64,2048]{1,0:T(8,128)(2,1)S(1)}, bf16[64,2048]{1,0:T(8,128)(2,1)S(...) custom-call(s32[4]{0:T(128)S(1)} %xor_add_fusion.refs_0_, bf16[2048,16]{1,0:T(8,128)(2,1)S(1)} %copy.21.refs_1_, ...), custom_call_target="tpu_custom_call" | custom-call | flops 1024 | bytes 1024 | tf_op jit(solution)/shard_map/select/pallas_call | solution.py:493
  68.9 1.8 %collective-permute-start.19 = (bf16[64,2048]{1,0:T(8,128)(2,1)S(1)}, bf16[64,2048]{1,0:T(8,128)(2,1)S(1)}, u32[]{:S(2)}, u32[]{:S(2)}) collective-permute-start(bf16[64,2048]{1,0:T(8,128)(2,1)S(1)} %get-tuple-element.147), channel_id=1, source_target_pairs={{0,4},{2,6},{4,0},{6,2},{1,5},{3,7},{5,1},{7,3},{8,12},{10,14},{12... | collective-permute-start | bytes 786440 | tf_op jit(solution)/shard_map/ppermute | solution.py:29
  72.6 2.6 %collective-permute-done.14.refs_2_ = bf16[64,2048]{1,0:T(8,128)(2,1)S(1)} collective-permute-done((bf16[64,2048]{1,0:T(8,128)(2,1)S(1)}, bf16[64,2048]{1,0:T(8,128)(2,1)S(1)}, u32[]{:S(2)}, u32[]{:S(2)}) %collective-permute-start.14) | collective-permute-done | bytes 262176 | tf_op jit(solution)/shard_map/ppermute | solution.py:29
  76.0 2.6 %copy-done.1 = bf16[1,2048,1408]{2,1,0:T(8,128)(2,1)S(1)} copy-done((bf16[1,2048,1408]{2,1,0:T(8,128)(2,1)S(1)}, bf16[1,2048,1408]{2,1,0:T(8,128)(2,1)}, u32[]{:S(2)}) %copy-start.1) | copy-done | bytes 5767192
  78.6 1.8 %copy-done.2 = bf16[1,704,2048]{2,1,0:T(8,128)(2,1)S(1)} copy-done((bf16[1,704,2048]{2,1,0:T(8,128)(2,1)S(1)}, bf16[1,704,2048]{2,1,0:T(8,128)(2,1)}, u32[]{:S(2)}) %copy-start.2) | copy-done | bytes 2883608
  80.4 1.8 %copy-done.5 = bf16[704,2048]{1,0:T(8,128)(2,1)S(1)} copy-done((bf16[704,2048]{1,0:T(8,128)(2,1)S(1)}, bf16[704,2048]{1,0:T(8,128)(2,1)}, u32[]{:S(2)}) %copy-start.5) | copy-done | bytes 2883608
  82.3 3.9 %slice-done.1 = s8[4194304]{0:T(1024)(128)(4,1)S(1)} async-done(((s8[5767168]{0:T(1024)(128)(4,1)}), s8[4194304]{0:T(1024)(128)(4,1)S(1)}, s32[]{:S(2)}) %slice-start.1) | async-done | bytes 4194328
  86.1 7.6 %expert.2 = (bf16[32,2048]{1,0:T(8,128)(2,1)S(1)}, bf16[32,2048]{1,0:T(8,128)(2,1)S(1)}, bf16[32,2048]{1,0:T(8,128)(2,1)S(1)}, bf16[32,2048]{1,0:T(8,128)(2,1)S(...) custom-call(bf16[64,2048]{1,0:T(8,128)(2,1)S(1)} %get-tuple-element., ...), custom_call_target="tpu_custom_call" | custom-call | flops 1024 | bytes 1024 | tf_op jit(solution)/shard_map/expert/pallas_call | solution.py:317
  95.1 2.2 %collective-permute-start.27 = (bf16[32,2048]{1,0:T(8,128)(2,1)S(1)}, bf16[32,2048]{1,0:T(8,128)(2,1)S(1)}, u32[]{:S(2)}, u32[]{:S(2)}) collective-permute-start(bf16[32,2048]{1,0:T(8,128)(2,1)S(1)} %get-tuple-element.152), channel_id=1, source_target_pairs={{0,6},{2,4},{4,2},{6,0},{1,7},{3,5},{5,3},{7,1},{8,14},{10,12},{12... | collective-permute-start | bytes 393224 | tf_op jit(solution)/shard_map/ppermute | solution.py:29
  97.3 7.6 %expert.3 = (bf16[32,2048]{1,0:T(8,128)(2,1)S(1)}, bf16[32,2048]{1,0:T(8,128)(2,1)S(1)}, bf16[32,2048]{1,0:T(8,128)(2,1)S(1)}, bf16[32,2048]{1,0:T(8,128)(2,1)S(...) custom-call(bf16[64,2048]{1,0:T(8,128)(2,1)S(1)} %get-tuple-element., ...), custom_call_target="tpu_custom_call" | custom-call | flops 1024 | bytes 1024 | tf_op jit(solution)/shard_map/expert/pallas_call | solution.py:317
  105.0 1.4 collective-permute-start.22
  106.7 2.4 %collective-permute-start.28 = (bf16[64,2048]{1,0:T(8,128)(2,1)S(1)}, bf16[64,2048]{1,0:T(8,128)(2,1)S(1)}, u32[]{:S(2)}, u32[]{:S(2)}) collective-permute-start(bf16[64,2048]{1,0:T(8,128)(2,1)S(1)} %combine.5), channel_id=1, source_target_pairs={{0,24},{8,16},{16,8},{24,0},{1,25},{9,17},{17,9},{25,1},{2,26},{10... | collective-permute-start | bytes 786440 | tf_op jit(solution)/shard_map/ppermute | solution.py:29
  112.8 1.5 %collective-permute-start.35 = (bf16[32,2048]{1,0:T(8,128)(2,1)S(1)}, bf16[32,2048]{1,0:T(8,128)(2,1)S(1)}, u32[]{:S(2)}, u32[]{:S(2)}) collective-permute-start(bf16[32,2048]{1,0:T(8,128)(2,1)S(1)} %get-tuple-element.181), channel_id=1, source_target_pairs={{0,6},{2,4},{4,2},{6,0},{1,7},{3,5},{5,3},{7,1},{8,14},{10,12},{12... | collective-permute-start | bytes 393224 | tf_op jit(solution)/shard_map/ppermute | solution.py:29
  115.2 3.2 %collective-permute-start.32 = (bf16[64,2048]{1,0:T(8,128)(2,1)S(1)}, bf16[64,2048]{1,0:T(8,128)(2,1)S(1)}, u32[]{:S(2)}, u32[]{:S(2)}) collective-permute-start(bf16[64,2048]{1,0:T(8,128)(2,1)S(1)} %combine.4), channel_id=1, source_target_pairs={{0,16},{8,24},{16,0},{24,8},{1,17},{9,25},{17,1},{25,9},{2,18},{10... | collective-permute-start | bytes 786440 | tf_op jit(solution)/shard_map/ppermute | solution.py:29
  119.8 5.1 %collective-permute-start.36 = (bf16[64,2048]{1,0:T(8,128)(2,1)S(1)}, bf16[64,2048]{1,0:T(8,128)(2,1)S(1)}, u32[]{:S(2)}, u32[]{:S(2)}) collective-permute-start(bf16[64,2048]{1,0:T(8,128)(2,1)S(1)} %combine.7), channel_id=1, source_target_pairs={{0,8},{8,0},{16,24},{24,16},{1,9},{9,1},{17,25},{25,17},{2,10},{10... | collective-permute-start | bytes 786440 | tf_op jit(solution)/shard_map/ppermute | solution.py:29
  126.7 1.5 %collective-permute-start.30 = (bf16[32,2048]{1,0:T(8,128)(2,1)S(1)}, bf16[32,2048]{1,0:T(8,128)(2,1)S(1)}, u32[]{:S(2)}, u32[]{:S(2)}) collective-permute-start(bf16[32,2048]{1,0:T(8,128)(2,1)S(1)} %get-tuple-element.169), channel_id=1, source_target_pairs={{0,4},{2,6},{4,0},{6,2},{1,5},{3,7},{5,1},{7,3},{8,12},{10,14},{12... | collective-permute-start | bytes 393224 | tf_op jit(solution)/shard_map/ppermute | solution.py:29
  131.7 2.4 %collective-permute-done.31.refs_3_ = bf16[32,2048]{1,0:T(8,128)(2,1)S(1)} collective-permute-done((bf16[32,2048]{1,0:T(8,128)(2,1)S(1)}, bf16[32,2048]{1,0:T(8,128)(2,1)S(1)}, u32[]{:S(2)}, u32[]{:S(2)}) %collective-permute-start.31) | collective-permute-done | bytes 131104 | tf_op jit(solution)/shard_map/ppermute | solution.py:29
  (137 shorter events, 30.0 us)
Async XLA Ops:
  2.5 13.0 %collective-permute-start.4 = (bf16[704,2048]{1,0:T(8,128)(2,1)}, bf16[704,2048]{1,0:T(8,128)(2,1)S(1)}, u32[]{:S(2)}, u32[]{:S(2)}) collective-permute-start(bf16[704,2048]{1,0:T(8,128)(2,1)} %bitcast.27), channel_id=1, source_target_pairs={{0,1},{1,0},{2,3},{3,2},{4,5},{5,4},{6,7},{7,6},{8,9},{9,8},{10,11... | collective-permute-start | bytes 8650760 | tf_op jit(solution)/shard_map/ppermute | solution.py:29
  2.9 9.7 %collective-permute-start = (bf16[64,2048]{1,0:T(8,128)(2,1)}, bf16[64,2048]{1,0:T(8,128)(2,1)S(1)}, u32[]{:S(2)}, u32[]{:S(2)}) collective-permute-start(bf16[64,2048]{1,0:T(8,128)(2,1)} %bitcast.32), channel_id=1, source_target_pairs={{0,2},{2,0},{1,3},{3,1},{4,6},{6,4},{5,7},{7,5},{8,10},{10,8},{9,1... | collective-permute-start | bytes 786440 | tf_op jit(solution)/shard_map/ppermute | solution.py:29
  15.1 11.0 %collective-permute-start.6 = (bf16[352,2048]{1,0:T(8,128)(2,1)}, bf16[352,2048]{1,0:T(8,128)(2,1)}, u32[]{:S(2)}, u32[]{:S(2)}) collective-permute-start(bf16[352,2048]{1,0:T(8,128)(2,1)} %bitcast.41), channel_id=1, source_target_pairs={{0,1},{1,0},{2,3},{3,2},{4,5},{5,4},{6,7},{7,6},{8,9},{9,8},{10,11... | collective-permute-start | bytes 4325384 | tf_op jit(solution)/shard_map/ppermute | solution.py:29
  15.2 10.9 %collective-permute-start.7 = (bf16[352,2048]{1,0:T(8,128)(2,1)}, bf16[352,2048]{1,0:T(8,128)(2,1)}, u32[]{:S(2)}, u32[]{:S(2)}) collective-permute-start(bf16[352,2048]{1,0:T(8,128)(2,1)} %refs_4_.1), channel_id=1, source_target_pairs={{0,1},{1,0},{2,3},{3,2},{4,5},{5,4},{6,7},{7,6},{8,9},{9,8},{10,11... | collective-permute-start | bytes 4325384 | tf_op jit(solution)/shard_map/ppermute | solution.py:29
  27.7 11.0 %collective-permute-start.9 = (bf16[2048,1408]{1,0:T(8,128)(2,1)}, bf16[2048,1408]{1,0:T(8,128)(2,1)}, u32[]{:S(2)}, u32[]{:S(2)}) collective-permute-start(bf16[2048,1408]{1,0:T(8,128)(2,1)} %bitcast.21), channel_id=1, source_target_pairs={{0,1},{1,0},{2,3},{3,2},{4,5},{5,4},{6,7},{7,6},{8,9},{9,8},{10,11... | collective-permute-start | bytes 17301512 | tf_op jit(solution)/shard_map/ppermute | solution.py:29
  29.0 8.6 %collective-permute-start.8 = (bf16[64,2048]{1,0:T(8,128)(2,1)S(1)}, bf16[64,2048]{1,0:T(8,128)(2,1)S(1)}, u32[]{:S(2)}, u32[]{:S(2)}) collective-permute-start(bf16[64,2048]{1,0:T(8,128)(2,1)S(1)} %add.35), channel_id=1, source_target_pairs={{0,2},{2,0},{1,3},{3,1},{4,6},{6,4},{5,7},{7,5},{8,10},{10,8},{9,1... | collective-permute-start | bytes 786440 | tf_op jit(solution)/shard_map/ppermute | solution.py:29
  39.0 21.4 %collective-permute-start.12 = (bf16[64,2176]{1,0:T(8,128)(2,1)S(1)}, bf16[64,2176]{1,0:T(8,128)(2,1)S(1)}, u32[]{:S(2)}, u32[]{:S(2)}) collective-permute-start(bf16[64,2176]{1,0:T(8,128)(2,1)S(1)} %get-tuple-element.125.refs_2_), channel_id=1, source_target_pairs={{0,24},{8,16},{16,8},{24,0},{1,25},{9,17},{17,9},{25,1},{2,26},{10... | collective-permute-start | bytes 835592 | tf_op jit(solution)/shard_map/ppermute | solution.py:29
  43.3 8.1 %collective-permute-start.11 = (bf16[64,2048]{1,0:T(8,128)(2,1)S(1)}, bf16[64,2048]{1,0:T(8,128)(2,1)S(1)}, u32[]{:S(2)}, u32[]{:S(2)}) collective-permute-start(bf16[64,2048]{1,0:T(8,128)(2,1)S(1)} %get-tuple-element.120.refs_0_), channel_id=1, source_target_pairs={{0,2},{2,0},{1,3},{3,1},{4,6},{6,4},{5,7},{7,5},{8,10},{10,8},{9,1... | collective-permute-start | bytes 786440 | tf_op jit(solution)/shard_map/ppermute | solution.py:29
  43.3 23.8 %collective-permute-start.16 = (bf16[64,2176]{1,0:T(8,128)(2,1)S(1)}, bf16[64,2176]{1,0:T(8,128)(2,1)S(1)}, u32[]{:S(2)}, u32[]{:S(2)}) collective-permute-start(bf16[64,2176]{1,0:T(8,128)(2,1)S(1)} %get-tuple-element.125.refs_2_), channel_id=1, source_target_pairs={{0,16},{8,24},{16,0},{24,8},{1,17},{9,25},{17,1},{25,9},{2,18},{10... | collective-permute-start | bytes 835592 | tf_op jit(solution)/shard_map/ppermute | solution.py:29
  43.3 23.8 %collective-permute-start.17 = (bf16[64,2176]{1,0:T(8,128)(2,1)S(1)}, bf16[64,2176]{1,0:T(8,128)(2,1)S(1)}, u32[]{:S(2)}, u32[]{:S(2)}) collective-permute-start(bf16[64,2176]{1,0:T(8,128)(2,1)S(1)} %get-tuple-element.125.refs_2_), channel_id=1, source_target_pairs={{0,8},{8,0},{16,24},{24,16},{1,9},{9,1},{17,25},{25,17},{2,10},{10... | collective-permute-start | bytes 835592 | tf_op jit(solution)/shard_map/ppermute | solution.py:29
  62.1 9.3 %collective-permute-start.13 = (bf16[64,2048]{1,0:T(8,128)(2,1)S(1)}, bf16[64,2048]{1,0:T(8,128)(2,1)S(1)}, u32[]{:S(2)}, u32[]{:S(2)}) collective-permute-start(bf16[64,2048]{1,0:T(8,128)(2,1)S(1)} %get-tuple-element.130), channel_id=1, source_target_pairs={{0,2},{2,0},{4,6},{6,4},{1,3},{3,1},{5,7},{7,5},{8,10},{10,8},{12,... | collective-permute-start | bytes 786440 | tf_op jit(solution)/shard_map/ppermute | solution.py:29
  62.4 12.8 %collective-permute-start.14 = (bf16[64,2048]{1,0:T(8,128)(2,1)S(1)}, bf16[64,2048]{1,0:T(8,128)(2,1)S(1)}, u32[]{:S(2)}, u32[]{:S(2)}) collective-permute-start(bf16[64,2048]{1,0:T(8,128)(2,1)S(1)} %get-tuple-element.131), channel_id=1, source_target_pairs={{0,4},{2,6},{4,0},{6,2},{1,5},{3,7},{5,1},{7,3},{8,12},{10,14},{12... | collective-permute-start | bytes 786440 | tf_op jit(solution)/shard_map/ppermute | solution.py:29
  63.9 18.3 %collective-permute-start.15 = (bf16[64,2048]{1,0:T(8,128)(2,1)S(1)}, bf16[64,2048]{1,0:T(8,128)(2,1)S(1)}, u32[]{:S(2)}, u32[]{:S(2)}) collective-permute-start(bf16[64,2048]{1,0:T(8,128)(2,1)S(1)} %get-tuple-element.132), channel_id=1, source_target_pairs={{0,6},{2,4},{4,2},{6,0},{1,7},{3,5},{5,3},{7,1},{8,14},{10,12},{12... | collective-permute-start | bytes 786440 | tf_op jit(solution)/shard_map/ppermute | solution.py:29
  68.8 26.3 %collective-permute-start.18 = (bf16[64,2048]{1,0:T(8,128)(2,1)S(1)}, bf16[64,2048]{1,0:T(8,128)(2,1)S(1)}, u32[]{:S(2)}, u32[]{:S(2)}) collective-permute-start(bf16[64,2048]{1,0:T(8,128)(2,1)S(1)} %get-tuple-element.146), channel_id=1, source_target_pairs={{0,2},{2,0},{4,6},{6,4},{1,3},{3,1},{5,7},{7,5},{8,10},{10,8},{12,... | collective-permute-start | bytes 786440 | tf_op jit(solution)/shard_map/ppermute | solution.py:29
  68.9 26.2 %collective-permute-start.19 = (bf16[64,2048]{1,0:T(8,128)(2,1)S(1)}, bf16[64,2048]{1,0:T(8,128)(2,1)S(1)}, u32[]{:S(2)}, u32[]{:S(2)}) collective-permute-start(bf16[64,2048]{1,0:T(8,128)(2,1)S(1)} %get-tuple-element.147), channel_id=1, source_target_pairs={{0,4},{2,6},{4,0},{6,2},{1,5},{3,7},{5,1},{7,3},{8,12},{10,14},{12... | collective-permute-start | bytes 786440 | tf_op jit(solution)/shard_map/ppermute | solution.py:29
  71.4 25.9 %collective-permute-start.20 = (bf16[64,2048]{1,0:T(8,128)(2,1)S(1)}, bf16[64,2048]{1,0:T(8,128)(2,1)S(1)}, u32[]{:S(2)}, u32[]{:S(2)}) collective-permute-start(bf16[64,2048]{1,0:T(8,128)(2,1)S(1)} %get-tuple-element.148), channel_id=1, source_target_pairs={{0,6},{2,4},{4,2},{6,0},{1,7},{3,5},{5,3},{7,1},{8,14},{10,12},{12... | collective-permute-start | bytes 786440 | tf_op jit(solution)/shard_map/ppermute | solution.py:29
  75.2 22.1 %collective-permute-start.21 = (bf16[64,2048]{1,0:T(8,128)(2,1)S(1)}, bf16[64,2048]{1,0:T(8,128)(2,1)S(1)}, u32[]{:S(2)}, u32[]{:S(2)}) collective-permute-start(bf16[64,2048]{1,0:T(8,128)(2,1)S(1)} %copy-done.27), channel_id=1, source_target_pairs={{0,2},{2,0},{1,3},{3,1},{4,6},{6,4},{5,7},{7,5},{8,10},{10,8},{9,1... | collective-permute-start | bytes 786440 | tf_op jit(solution)/shard_map/ppermute | solution.py:29
  93.8 12.7 %collective-permute-start.25 = (bf16[32,2048]{1,0:T(8,128)(2,1)S(1)}, bf16[32,2048]{1,0:T(8,128)(2,1)S(1)}, u32[]{:S(2)}, u32[]{:S(2)}) collective-permute-start(bf16[32,2048]{1,0:T(8,128)(2,1)S(1)} %get-tuple-element.150), channel_id=1, source_target_pairs={{0,2},{2,0},{4,6},{6,4},{1,3},{3,1},{5,7},{7,5},{8,10},{10,8},{12,... | collective-permute-start | bytes 393224 | tf_op jit(solution)/shard_map/ppermute | solution.py:29
  95.1 11.3 %collective-permute-start.26 = (bf16[32,2048]{1,0:T(8,128)(2,1)S(1)}, bf16[32,2048]{1,0:T(8,128)(2,1)S(1)}, u32[]{:S(2)}, u32[]{:S(2)}) collective-permute-start(bf16[32,2048]{1,0:T(8,128)(2,1)S(1)} %get-tuple-element.151), channel_id=1, source_target_pairs={{0,4},{2,6},{4,0},{6,2},{1,5},{3,7},{5,1},{7,3},{8,12},{10,14},{12... | collective-permute-start | bytes 393224 | tf_op jit(solution)/shard_map/ppermute | solution.py:29
  95.1 11.3 %collective-permute-start.27 = (bf16[32,2048]{1,0:T(8,128)(2,1)S(1)}, bf16[32,2048]{1,0:T(8,128)(2,1)S(1)}, u32[]{:S(2)}, u32[]{:S(2)}) collective-permute-start(bf16[32,2048]{1,0:T(8,128)(2,1)S(1)} %get-tuple-element.152), channel_id=1, source_target_pairs={{0,6},{2,4},{4,2},{6,0},{1,7},{3,5},{5,3},{7,1},{8,14},{10,12},{12... | collective-permute-start | bytes 393224 | tf_op jit(solution)/shard_map/ppermute | solution.py:29
  105.0 6.5 %collective-permute-start.22 = (bf16[32,2048]{1,0:T(8,128)(2,1)S(1)}, bf16[32,2048]{1,0:T(8,128)(2,1)S(1)}, u32[]{:S(2)}, u32[]{:S(2)}) collective-permute-start(bf16[32,2048]{1,0:T(8,128)(2,1)S(1)} %get-tuple-element.159), channel_id=1, source_target_pairs={{0,2},{2,0},{4,6},{6,4},{1,3},{3,1},{5,7},{7,5},{8,10},{10,8},{12,... | collective-permute-start | bytes 393224 | tf_op jit(solution)/shard_map/ppermute | solution.py:29
  106.4 6.4 %collective-permute-start.23 = (bf16[32,2048]{1,0:T(8,128)(2,1)S(1)}, bf16[32,2048]{1,0:T(8,128)(2,1)S(1)}, u32[]{:S(2)}, u32[]{:S(2)}) collective-permute-start(bf16[32,2048]{1,0:T(8,128)(2,1)S(1)} %get-tuple-element.160), channel_id=1, source_target_pairs={{0,4},{2,6},{4,0},{6,2},{1,5},{3,7},{5,1},{7,3},{8,12},{10,14},{12... | collective-permute-start | bytes 393224 | tf_op jit(solution)/shard_map/ppermute | solution.py:29
  106.7 18.9 %collective-permute-start.28 = (bf16[64,2048]{1,0:T(8,128)(2,1)S(1)}, bf16[64,2048]{1,0:T(8,128)(2,1)S(1)}, u32[]{:S(2)}, u32[]{:S(2)}) collective-permute-start(bf16[64,2048]{1,0:T(8,128)(2,1)S(1)} %combine.5), channel_id=1, source_target_pairs={{0,24},{8,16},{16,8},{24,0},{1,25},{9,17},{17,9},{25,1},{2,26},{10... | collective-permute-start | bytes 786440 | tf_op jit(solution)/shard_map/ppermute | solution.py:29
  109.1 5.9 %collective-permute-start.24 = (bf16[32,2048]{1,0:T(8,128)(2,1)S(1)}, bf16[32,2048]{1,0:T(8,128)(2,1)S(1)}, u32[]{:S(2)}, u32[]{:S(2)}) collective-permute-start(bf16[32,2048]{1,0:T(8,128)(2,1)S(1)} %get-tuple-element.161), channel_id=1, source_target_pairs={{0,6},{2,4},{4,2},{6,0},{1,7},{3,5},{5,3},{7,1},{8,14},{10,12},{12... | collective-permute-start | bytes 393224 | tf_op jit(solution)/shard_map/ppermute | solution.py:29
  109.7 8.7 %collective-permute-start.33 = (bf16[32,2048]{1,0:T(8,128)(2,1)S(1)}, bf16[32,2048]{1,0:T(8,128)(2,1)S(1)}, u32[]{:S(2)}, u32[]{:S(2)}) collective-permute-start(bf16[32,2048]{1,0:T(8,128)(2,1)S(1)} %get-tuple-element.179), channel_id=1, source_target_pairs={{0,2},{2,0},{4,6},{6,4},{1,3},{3,1},{5,7},{7,5},{8,10},{10,8},{12,... | collective-permute-start | bytes 393224 | tf_op jit(solution)/shard_map/ppermute | solution.py:29
  111.5 6.9 %collective-permute-start.34 = (bf16[32,2048]{1,0:T(8,128)(2,1)S(1)}, bf16[32,2048]{1,0:T(8,128)(2,1)S(1)}, u32[]{:S(2)}, u32[]{:S(2)}) collective-permute-start(bf16[32,2048]{1,0:T(8,128)(2,1)S(1)} %get-tuple-element.180), channel_id=1, source_target_pairs={{0,4},{2,6},{4,0},{6,2},{1,5},{3,7},{5,1},{7,3},{8,12},{10,14},{12... | collective-permute-start | bytes 393224 | tf_op jit(solution)/shard_map/ppermute | solution.py:29
  112.8 6.8 %collective-permute-start.35 = (bf16[32,2048]{1,0:T(8,128)(2,1)S(1)}, bf16[32,2048]{1,0:T(8,128)(2,1)S(1)}, u32[]{:S(2)}, u32[]{:S(2)}) collective-permute-start(bf16[32,2048]{1,0:T(8,128)(2,1)S(1)} %get-tuple-element.181), channel_id=1, source_target_pairs={{0,6},{2,4},{4,2},{6,0},{1,7},{3,5},{5,3},{7,1},{8,14},{10,12},{12... | collective-permute-start | bytes 393224 | tf_op jit(solution)/shard_map/ppermute | solution.py:29
  115.2 19.1 %collective-permute-start.32 = (bf16[64,2048]{1,0:T(8,128)(2,1)S(1)}, bf16[64,2048]{1,0:T(8,128)(2,1)S(1)}, u32[]{:S(2)}, u32[]{:S(2)}) collective-permute-start(bf16[64,2048]{1,0:T(8,128)(2,1)S(1)} %combine.4), channel_id=1, source_target_pairs={{0,16},{8,24},{16,0},{24,8},{1,17},{9,25},{17,1},{25,9},{2,18},{10... | collective-permute-start | bytes 786440 | tf_op jit(solution)/shard_map/ppermute | solution.py:29
  119.8 14.5 %collective-permute-start.36 = (bf16[64,2048]{1,0:T(8,128)(2,1)S(1)}, bf16[64,2048]{1,0:T(8,128)(2,1)S(1)}, u32[]{:S(2)}, u32[]{:S(2)}) collective-permute-start(bf16[64,2048]{1,0:T(8,128)(2,1)S(1)} %combine.7), channel_id=1, source_target_pairs={{0,8},{8,0},{16,24},{24,16},{1,9},{9,1},{17,25},{25,17},{2,10},{10... | collective-permute-start | bytes 786440 | tf_op jit(solution)/shard_map/ppermute | solution.py:29
  125.6 5.0 %collective-permute-start.29 = (bf16[32,2048]{1,0:T(8,128)(2,1)S(1)}, bf16[32,2048]{1,0:T(8,128)(2,1)S(1)}, u32[]{:S(2)}, u32[]{:S(2)}) collective-permute-start(bf16[32,2048]{1,0:T(8,128)(2,1)S(1)} %get-tuple-element.168), channel_id=1, source_target_pairs={{0,2},{2,0},{4,6},{6,4},{1,3},{3,1},{5,7},{7,5},{8,10},{10,8},{12,... | collective-permute-start | bytes 393224 | tf_op jit(solution)/shard_map/ppermute | solution.py:29
  126.7 5.0 %collective-permute-start.30 = (bf16[32,2048]{1,0:T(8,128)(2,1)S(1)}, bf16[32,2048]{1,0:T(8,128)(2,1)S(1)}, u32[]{:S(2)}, u32[]{:S(2)}) collective-permute-start(bf16[32,2048]{1,0:T(8,128)(2,1)S(1)} %get-tuple-element.169), channel_id=1, source_target_pairs={{0,4},{2,6},{4,0},{6,2},{1,5},{3,7},{5,1},{7,3},{8,12},{10,14},{12... | collective-permute-start | bytes 393224 | tf_op jit(solution)/shard_map/ppermute | solution.py:29
  128.2 5.9 %collective-permute-start.31 = (bf16[32,2048]{1,0:T(8,128)(2,1)S(1)}, bf16[32,2048]{1,0:T(8,128)(2,1)S(1)}, u32[]{:S(2)}, u32[]{:S(2)}) collective-permute-start(bf16[32,2048]{1,0:T(8,128)(2,1)S(1)} %get-tuple-element.170), channel_id=1, source_target_pairs={{0,6},{2,4},{4,2},{6,0},{1,7},{3,5},{5,3},{7,1},{8,14},{10,12},{12... | collective-permute-start | bytes 393224 | tf_op jit(solution)/shard_map/ppermute | solution.py:29
  (39 other events, 452.1 us)

commit v11 on v10

--- a/solution.py
+++ b/solution.py
@@ -256,25 +256,27 @@
     return values / (1.0 + jnp.exp(-values))
 
 
-def expert_kernel(*refs, plane, count, deep):
+def expert_kernel(*refs, plane, count, tiles):
     pieces = refs[:plane]
     weights = refs[plane : plane + 4]
     outs = refs[plane + 4 : plane + 4 + count * plane]
-    rows, inner_a, outer_a, inner_b, outer_b, sems = refs[plane + 4 + count * plane :]
+    rows, inner_a, outer_a, inner_b, outer_b, both, hidden, first, sems = refs[
+        plane + 4 + count * plane :
+    ]
     each = pieces[0].shape[0]
-    width = rows.shape[1]
-    parts = width // deep
+    parts = len(tiles)
     copies = []
-    for n, (inner, outer, inner_here, outer_here) in enumerate(
-        ((weights[0], weights[1], inner_a, outer_a), (weights[2], weights[3], inner_b, outer_b))
+    for inner, outer, inner_here, outer_here in (
+        (weights[0], weights[1], inner_a, outer_a),
+        (weights[2], weights[3], inner_b, outer_b),
     ):
-        base = n * (parts + 1)
-        for p in range(parts):
-            block = pl.ds(p * deep, deep)
+        for start, size in tiles:
+            block = pl.ds(start, size)
+            number = len(copies)
             copies.append(
-                pltpu.make_async_copy(inner.at[block], inner_here.at[block], sems.at[base + p])
+                pltpu.make_async_copy(inner.at[block], inner_here.at[block], sems.at[number])
             )
-        copies.append(pltpu.make_async_copy(outer, outer_here, sems.at[base + parts]))
+        copies.append(pltpu.make_async_copy(outer, outer_here, sems.at[len(copies)]))
     for copy in copies[:2]:
         copy.start()
 
@@ -285,64 +287,53 @@
 
     for i in range(plane):
         rows[i * each : (i + 1) * each] = pieces[i][...]
-    result = None
     for n, (inner_here, outer_here) in enumerate(((inner_a, outer_a), (inner_b, outer_b))):
         base = n * (parts + 1)
-        both = None
-        for p in range(parts):
+        for p, (start, size) in enumerate(tiles):
             take(base + p)
-            term = dot(rows[:, p * deep : (p + 1) * deep], inner_here[p * deep : (p + 1) * deep])
-            both = term if both is None else both + term
+            term = dot(rows[:, start : start + size], inner_here[start : start + size])
+            both[...] = term if p == 0 else both[...] + term
         half = both.shape[1] // 2
-        hidden = (silu(both[:, :half]) * both[:, half:]).astype(jnp.bfloat16)
+        hidden[...] = (silu(both[:, :half]) * both[:, half:]).astype(jnp.bfloat16)
         take(base + parts)
-        term = dot(hidden, outer_here[...]).astype(jnp.bfloat16).astype(jnp.float32)
-        result = term if result is None else result + term
+        term = dot(hidden[...], outer_here[...]).astype(jnp.bfloat16)
+        if n == 0:
+            first[...] = term
+    result = (first[...].astype(jnp.float32) + term.astype(jnp.float32)).astype(jnp.bfloat16)
     step = each // count
     for n in range(count * plane):
         base = (n % plane) * each + (n // plane) * step
-        outs[n][...] = result[base : base + step].astype(jnp.bfloat16)
+        outs[n][...] = result[base : base + step]
 
 
 def experts(pieces, count, inner, outer):
     plane = len(pieces)
     each, width = pieces[0].shape
     hidden = inner[0].shape[1]
-    deep = width // 2
-    kernel = functools.partial(expert_kernel, plane=plane, count=count, deep=deep)
+    tiles = ((0, width // 2), (width // 2, width - width // 2))
+    rows = plane * each
     weight_scratch = [
         pltpu.VMEM((width, hidden), jnp.bfloat16),
         pltpu.VMEM((hidden // 2, width), jnp.bfloat16),
     ]
     made = pl.pallas_call(
-        kernel,
+        functools.partial(expert_kernel, plane=plane, count=count, tiles=tiles),
         in_specs=[in_vmem()] * plane + [in_hbm()] * 4,
         out_specs=[in_vmem()] * (count * plane),
         out_shape=[jax.ShapeDtypeStruct((each // count, width), jnp.bfloat16)] * (count * plane),
-        scratch_shapes=[pltpu.VMEM((plane * each, width), jnp.bfloat16)]
+        scratch_shapes=[pltpu.VMEM((rows, width), jnp.bfloat16)]
         + weight_scratch * 2
-        + [pltpu.SemaphoreType.DMA((2 * (width // deep + 1),))],
-        compiler_params=pltpu.CompilerParams(vmem_limit_bytes=40 * 2**20),
+        + [
+            pltpu.VMEM((rows, hidden), jnp.float32),
+            pltpu.VMEM((rows, hidden // 2), jnp.bfloat16),
+            pltpu.VMEM((rows, width), jnp.bfloat16),
+            pltpu.SemaphoreType.DMA((2 * (len(tiles) + 1),)),
+        ],
+        compiler_params=pltpu.CompilerParams(vmem_limit_bytes=60 * 2**20),
         cost_estimate=SMALL,
         name="expert",
     )(*pieces, inner[0], outer[0], inner[1], outer[1])
     return [list(made[i * plane : (i + 1) * plane]) for i in range(count)]
-
-
-def hold_kernel(*refs):
-    refs[-1][...] = refs[0][...]
-
-
-def hold(token, weights):
-    return pl.pallas_call(
-        hold_kernel,
-        in_specs=[in_vmem()] + [in_hbm()] * len(weights),
-        out_specs=in_vmem(),
-        out_shape=jax.ShapeDtypeStruct(token.shape, token.dtype),
-        compiler_params=pltpu.CompilerParams(vmem_limit_bytes=16 * 2**20),
-        cost_estimate=SMALL,
-        name="hold",
-    )(token, *weights)
 
 
 def shared_kernel(*refs, side):
@@ -646,11 +637,11 @@
     near_experts = lax.axis_index("z") * plane + (
         lax.axis_index(PLANE) ^ jnp.arange(plane, dtype=jnp.int32)
     )
-    line_rows = [payload] + [partner(payload, "z", k) for k in range(1, line)]
     beside = [partner(normed, "x", o) for o in range(1, side)]
-
-    shared, beside = shared_terms(normed, beside, shared_weights)
-    line_rows[3], beside = lax.optimization_barrier((line_rows[3], beside))
+    calm, beside = lax.optimization_barrier((payload, beside))
+    line_rows = [payload] + [
+        partner(payload if k in GROUPS[0] else calm, "z", k) for k in range(1, line)
+    ]
 
     sent = []
     spread = {}
@@ -659,10 +650,12 @@
             near_experts, router, [line_rows[k] for k in ks], plane, capacity, top_count
         )
         spread.update(zip(ks, spreads))
+        sent.append([partner(pieces[o], PLANE, o) for o in range(plane)])
         if len(sent) == 1:
-            token = hold(spreads[0], [inner[0], outer[0], inner[1], outer[1]])
-            sent[0], spread[ks[0]] = lax.optimization_barrier((sent[0], token))
-        sent.append([partner(pieces[o], PLANE, o) for o in range(plane)])
+            normed, spread[ks[0]] = lax.optimization_barrier((normed, spread[ks[0]]))
+            shared, beside = shared_terms(
+                normed, beside, [gate_turned, up_turned, shared_down, early[0], *middle]
+            )
     parts = [partner(beside[o - 1], "x", o) for o in range(1, side)]
     made = None
     results = {}

time: 137 us -> 138 us (level)
  local copies, waits for them, and re-layouts: 20.2 us -> 12.9 us
  Pallas kernels: 47.5 us -> 52.1 us
  starting transfers between devices: 43 us -> 46.7 us
    unnamed x70 -> x80, local copies, waits for them, and re-layouts: 18.4 us -> 11.1 us
    pallas_call x3 -> x2, Pallas kernels: 15.3 us -> 20.7 us  [experts(): pl.pallas_call(functools.partial(expert_kernel, plane=plane, count=count,...]
    ppermute x37, starting transfers between devices: 43 us -> 46.7 us  [partner(): return lax.ppermute(value, axes, [(i, i ^ offset) for i in range(size)])]
  transfers between devices with their start and end apart: 37 -> 37, of which waited for: 16 -> 12; matrix products, arithmetic and copies ran while one was open for 2% -> 2% of each run, Pallas kernels for 34% -> 37%
where the time goes in v11:
time: 138 us; the launch traced here: 135 us
  Pallas kernels  52.1 us (38%)
  starting transfers between devices  46.7 us (34%)
  waiting for transfers between devices  22.3 us (16%)
  local copies, waits for them, and re-layouts  12.9 us (9%)
    ppermute x37, starting transfers between devices, partner(): return lax.ppermute(value, axes, [(i, i ^ offset) for i in range(size)])  46.7 us
    ppermute x37, waiting for transfers between devices, partner(): return lax.ppermute(value, axes, [(i, i ^ offset) for i in range(size)])  22.3 us
    pallas_call x2, Pallas kernels, experts(): pl.pallas_call(functools.partial(expert_kernel, plane=plane, count=count,...  20.7 us
    pallas_call x2, Pallas kernels, attend(): pl.pallas_call(functools.partial(attend_kernel, offset=offset), in_specs=...  15.5 us
    unnamed x80, local copies, waits for them, and re-layouts  11.1 us
    pallas_call x1, Pallas kernels, shared_terms(): pl.pallas_call(functools.partial(shared_kernel, side=side), in_specs=[in_...  8.21 us
    pallas_call x2, Pallas kernels, select(): pl.pallas_call(functools.partial(select_kernel, count=count, plane=plane,...  3.3 us
  transfers between devices with their start and end apart: 37, of which 12 were waited for; matrix products, arithmetic and copies ran while one was open for 2% of the time, Pallas kernels for 37%

profile of v11, /device:TPU:0, one launch (start us, length us, event | category | flops | bytes accessed | tf_op | source)
XLA Modules:
  0.0 135.3 jit_solution(8296211181778812704)
XLA Ops:
  1.2 1.4 %collective-permute-done.1.second = bf16[64,2048]{1,0:T(8,128)(2,1)S(1)} collective-permute-done((bf16[64,2048]{1,0:T(8,128)(2,1)}, bf16[64,2048]{1,0:T(8,128)(2,1)S(1)}, u32[]{:S(2)}, u32[]{:S(2)}) %collective-permute-start.1) | collective-permute-done | bytes 262176 | tf_op jit(solution)/shard_map/ppermute | solution.py:29
  2.9 2.6 %collective-permute-start = (bf16[64,2048]{1,0:T(8,128)(2,1)}, bf16[64,2048]{1,0:T(8,128)(2,1)}, u32[]{:S(2)}, u32[]{:S(2)}) collective-permute-start(bf16[64,2048]{1,0:T(8,128)(2,1)} %bitcast.22), channel_id=1, source_target_pairs={{0,2},{2,0},{1,3},{3,1},{4,6},{6,4},{5,7},{7,5},{8,10},{10,8},{9,1... | collective-permute-start | bytes 786440 | tf_op jit(solution)/shard_map/ppermute | solution.py:29
  7.5 2.0 %prepare.1 = (f32[4,64,64]{2,1,0:T(8,128)S(1)}, f32[4,64,128]{2,1,0:T(8,128)S(1)}, f32[4,64,128]{2,1,0:T(8,128)S(1)}) custom-call(s32[4]{0:T(128)S(1)} %copy-done.16, s32[4,64]{1,0:T(4,128)S(1)} %copy-done.17, f32[1,128]{1,0:T(1,128)S(1)} %copy-done.18), custom_call_target="tpu_custom_call" | custom-call | flops 1024 | bytes 1024 | tf_op jit(solution)/shard_map/prepare/pallas_call | solution.py:68
  11.5 1.2 collective-permute-done.first
  12.7 2.6 %collective-permute-done.2.second = bf16[64,2048]{1,0:T(8,128)(2,1)S(1)} collective-permute-done((bf16[64,2048]{1,0:T(8,128)(2,1)}, bf16[64,2048]{1,0:T(8,128)(2,1)S(1)}, u32[]{:S(2)}, u32[]{:S(2)}) %collective-permute-start.2) | collective-permute-done | bytes 262176 | tf_op jit(solution)/shard_map/ppermute | solution.py:29
  16.9 7.8 %attend.2 = (f32[64,2048]{1,0:T(8,128)}, bf16[64,2048]{1,0:T(8,128)(2,1)}, bf16[64,256]{1,0:T(8,128)(2,1)}, bf16[64,256]{1,0:T(8,128)(2,1)}) custom-call(s32[1]{0:T(128)} %bitcast.2.place, s32[4]{0:T(128)} %lengths.5, bf16[64,2048]{1,0:T(8,128)(2,1)} %collective-permute-done.first, bf16[64,2048]{1,0:T(8,128)(2,1)} %copy-done.28, f32[1,2048]{1,0:T(1,128)} %bitcast.40, ...), custom_call_target="tpu_custom_call" | custom-call | flops 1024 | bytes 1024 | tf_op jit(solution)/shard_map/attend/pallas_call | solution.py:204
  25.0 1.6 %collective-permute-done.5.right = bf16[64,2048]{1,0:T(8,128)(2,1)S(1)} collective-permute-done((bf16[64,2048]{1,0:T(8,128)(2,1)}, bf16[64,2048]{1,0:T(8,128)(2,1)S(1)}, u32[]{:S(2)}, u32[]{:S(2)}) %collective-permute-start.5) | collective-permute-done | bytes 262176 | tf_op jit(solution)/shard_map/ppermute | solution.py:29
  27.8 1.3 collective-permute-start.8
  29.2 7.7 %attend.3 = (f32[64,2048]{1,0:T(8,128)}, bf16[64,2048]{1,0:T(8,128)(2,1)}, bf16[64,256]{1,0:T(8,128)(2,1)}, bf16[64,256]{1,0:T(8,128)(2,1)}) custom-call(s32[1]{0:T(128)} %bitcast.2.place, s32[4]{0:T(128)} %lengths.5, bf16[64,2048]{1,0:T(8,128)(2,1)} %bitcast.23, bf16[64,2048]{1,0:T(8,128)(2,1)} %copy-done.26, f32[1,2048]{1,0:T(1,128)} %bitcast.41, ...), custom_call_target="tpu_custom_call" | custom-call | flops 1024 | bytes 1024 | tf_op jit(solution)/shard_map/attend/pallas_call | solution.py:204
  39.3 3.6 %collective-permute-start.11 = (bf16[64,2176]{1,0:T(8,128)(2,1)S(1)}, bf16[64,2176]{1,0:T(8,128)(2,1)S(1)}, u32[]{:S(2)}, u32[]{:S(2)}) collective-permute-start(bf16[64,2176]{1,0:T(8,128)(2,1)S(1)} %get-tuple-element.137.refs_2_), channel_id=1, source_target_pairs={{0,24},{8,16},{16,8},{24,0},{1,25},{9,17},{17,9},{25,1},{2,26},{10... | collective-permute-start | bytes 835592 | tf_op jit(solution)/shard_map/ppermute | solution.py:29
  42.9 4.5 %collective-permute-done.12.refs_1_ = bf16[64,2048]{1,0:T(8,128)(2,1)S(1)} collective-permute-done((bf16[64,2048]{1,0:T(8,128)(2,1)S(1)}, bf16[64,2048]{1,0:T(8,128)(2,1)S(1)}, u32[]{:S(2)}, u32[]{:S(2)}) %collective-permute-start.12) | collective-permute-done | bytes 262176 | tf_op jit(solution)/shard_map/ppermute | solution.py:29
  47.4 2.0 %collective-permute-start.16 = (bf16[64,2176]{1,0:T(8,128)(2,1)S(1)}, bf16[64,2176]{1,0:T(8,128)(2,1)S(1)}, u32[]{:S(2)}, u32[]{:S(2)}) collective-permute-start(bf16[64,2176]{1,0:T(8,128)(2,1)S(1)} %get-tuple-element.137.refs_2_), channel_id=1, source_target_pairs={{0,16},{8,24},{16,0},{24,8},{1,17},{9,25},{17,1},{25,9},{2,18},{10... | collective-permute-start | bytes 835592 | tf_op jit(solution)/shard_map/ppermute | solution.py:29
  49.3 2.2 %collective-permute-start.17 = (bf16[64,2176]{1,0:T(8,128)(2,1)S(1)}, bf16[64,2176]{1,0:T(8,128)(2,1)S(1)}, u32[]{:S(2)}, u32[]{:S(2)}) collective-permute-start(bf16[64,2176]{1,0:T(8,128)(2,1)S(1)} %get-tuple-element.137.refs_2_), channel_id=1, source_target_pairs={{0,8},{8,0},{16,24},{24,16},{1,9},{9,1},{17,25},{25,17},{2,10},{10... | collective-permute-start | bytes 835592 | tf_op jit(solution)/shard_map/ppermute | solution.py:29
  51.9 1.7 %select.2 = (bf16[64,2048]{1,0:T(8,128)(2,1)S(1)}, bf16[64,2048]{1,0:T(8,128)(2,1)S(1)}, bf16[64,2048]{1,0:T(8,128)(2,1)S(1)}, bf16[64,2048]{1,0:T(8,128)(2,1)S(...) custom-call(s32[4]{0:T(128)S(1)} %xor_add_fusion.refs_0_, bf16[2048,16]{1,0:T(8,128)(2,1)S(1)} %copy.21.refs_1_, ...), custom_call_target="tpu_custom_call" | custom-call | flops 1024 | bytes 1024 | tf_op jit(solution)/shard_map/select/pallas_call | solution.py:484
  54.5 2.3 %collective-permute-start.14 = (bf16[64,2048]{1,0:T(8,128)(2,1)S(1)}, bf16[64,2048]{1,0:T(8,128)(2,1)S(1)}, u32[]{:S(2)}, u32[]{:S(2)}) collective-permute-start(bf16[64,2048]{1,0:T(8,128)(2,1)S(1)} %get-tuple-element.129), channel_id=1, source_target_pairs={{0,4},{2,6},{4,0},{6,2},{1,5},{3,7},{5,1},{7,3},{8,12},{10,14},{12... | collective-permute-start | bytes 786440 | tf_op jit(solution)/shard_map/ppermute | solution.py:29
  57.7 8.2 %shared.1 = (f32[64,2048]{1,0:T(8,128)}, bf16[64,2048]{1,0:T(8,128)(2,1)}) custom-call(bf16[64,2048]{1,0:T(8,128)(2,1)} %copy-done.10, bf16[64,2048]{1,0:T(8,128)(2,1)} %copy-done.27, bf16[352,2048]{1,0:T(8,128)(2,1)} %bitcast.36, bf16[352,2048]{1,0:T(8,128)(2,1)} %bitcast.38, bf16[352,2048]{1,0:T(8,128)(2,1)} %refs_4_.1, bf16[352,2048]{1,0:T(8,128)(2,1)} %copy-done.20, ...), custom_call_target="tpu_custom_call" | custom-call | flops 1024 | bytes 1024 | tf_op jit(solution)/shard_map/shared/pallas_call | solution.py:377
  66.0 1.5 %collective-permute-done.16.refs_2_ = bf16[64,2176]{1,0:T(8,128)(2,1)S(1)} collective-permute-done((bf16[64,2176]{1,0:T(8,128)(2,1)S(1)}, bf16[64,2176]{1,0:T(8,128)(2,1)S(1)}, u32[]{:S(2)}, u32[]{:S(2)}) %collective-permute-start.16) | collective-permute-done | bytes 278560 | tf_op jit(solution)/shard_map/ppermute | solution.py:29
  68.4 1.6 %select.3 = (bf16[64,2048]{1,0:T(8,128)(2,1)S(1)}, bf16[64,2048]{1,0:T(8,128)(2,1)S(1)}, bf16[64,2048]{1,0:T(8,128)(2,1)S(1)}, bf16[64,2048]{1,0:T(8,128)(2,1)S(...) custom-call(s32[4]{0:T(128)S(1)} %xor_add_fusion.refs_0_, bf16[2048,16]{1,0:T(8,128)(2,1)S(1)} %copy.21.refs_1_, ...), custom_call_target="tpu_custom_call" | custom-call | flops 1024 | bytes 1024 | tf_op jit(solution)/shard_map/select/pallas_call | solution.py:484
  70.0 1.2 collective-permute-start.18
  71.2 2.4 %collective-permute-start.19 = (bf16[64,2048]{1,0:T(8,128)(2,1)S(1)}, bf16[64,2048]{1,0:T(8,128)(2,1)S(1)}, u32[]{:S(2)}, u32[]{:S(2)}) collective-permute-start(bf16[64,2048]{1,0:T(8,128)(2,1)S(1)} %get-tuple-element.141), channel_id=1, source_target_pairs={{0,4},{2,6},{4,0},{6,2},{1,5},{3,7},{5,1},{7,3},{8,12},{10,14},{12... | collective-permute-start | bytes 786440 | tf_op jit(solution)/shard_map/ppermute | solution.py:29
  74.3 10.2 %expert.2 = (bf16[32,2048]{1,0:T(8,128)(2,1)}, bf16[32,2048]{1,0:T(8,128)(2,1)}, bf16[32,2048]{1,0:T(8,128)(2,1)}, bf16[32,2048]{1,0:T(8,128)(2,1)}, bf16[32,204...) custom-call(bf16[64,2048]{1,0:T(8,128)(2,1)} %copy-done.9, ...), custom_call_target="tpu_custom_call" | custom-call | flops 1024 | bytes 1024 | tf_op jit(solution)/shard_map/expert/pallas_call | solution.py:319
  85.5 1.9 %collective-permute-start.26 = (bf16[32,2048]{1,0:T(8,128)(2,1)}, bf16[32,2048]{1,0:T(8,128)(2,1)S(1)}, u32[]{:S(2)}, u32[]{:S(2)}) collective-permute-start(bf16[32,2048]{1,0:T(8,128)(2,1)} %get-tuple-element.145), channel_id=1, source_target_pairs={{0,4},{2,6},{4,0},{6,2},{1,5},{3,7},{5,1},{7,3},{8,12},{10,14},{12... | collective-permute-start | bytes 393224 | tf_op jit(solution)/shard_map/ppermute | solution.py:29
  88.1 1.8 %collective-permute-done.20.refs_3_ = bf16[64,2048]{1,0:T(8,128)(2,1)S(1)} collective-permute-done((bf16[64,2048]{1,0:T(8,128)(2,1)S(1)}, bf16[64,2048]{1,0:T(8,128)(2,1)S(1)}, u32[]{:S(2)}, u32[]{:S(2)}) %collective-permute-start.20) | collective-permute-done | bytes 262176 | tf_op jit(solution)/shard_map/ppermute | solution.py:29
  90.6 10.5 %expert.3 = (bf16[32,2048]{1,0:T(8,128)(2,1)}, bf16[32,2048]{1,0:T(8,128)(2,1)}, bf16[32,2048]{1,0:T(8,128)(2,1)}, bf16[32,2048]{1,0:T(8,128)(2,1)}, bf16[32,204...) custom-call(bf16[64,2048]{1,0:T(8,128)(2,1)} %copy-done.8, ...), custom_call_target="tpu_custom_call" | custom-call | flops 1024 | bytes 1024 | tf_op jit(solution)/shard_map/expert/pallas_call | solution.py:319
  102.6 2.4 %collective-permute-start.28 = (bf16[64,2048]{1,0:T(8,128)(2,1)S(1)}, bf16[64,2048]{1,0:T(8,128)(2,1)S(1)}, u32[]{:S(2)}, u32[]{:S(2)}) collective-permute-start(bf16[64,2048]{1,0:T(8,128)(2,1)S(1)} %combine.5), channel_id=1, source_target_pairs={{0,24},{8,16},{16,8},{24,0},{1,25},{9,17},{17,9},{25,1},{2,26},{10... | collective-permute-start | bytes 786440 | tf_op jit(solution)/shard_map/ppermute | solution.py:29
  105.0 2.1 %collective-permute-start.24 = (bf16[32,2048]{1,0:T(8,128)(2,1)}, bf16[32,2048]{1,0:T(8,128)(2,1)S(1)}, u32[]{:S(2)}, u32[]{:S(2)}) collective-permute-start(bf16[32,2048]{1,0:T(8,128)(2,1)} %get-tuple-element.155), channel_id=1, source_target_pairs={{0,6},{2,4},{4,2},{6,0},{1,7},{3,5},{5,3},{7,1},{8,14},{10,12},{12... | collective-permute-start | bytes 393224 | tf_op jit(solution)/shard_map/ppermute | solution.py:29
  108.5 3.8 %collective-permute-done.23.refs_2_ = bf16[32,2048]{1,0:T(8,128)(2,1)S(1)} collective-permute-done((bf16[32,2048]{1,0:T(8,128)(2,1)}, bf16[32,2048]{1,0:T(8,128)(2,1)S(1)}, u32[]{:S(2)}, u32[]{:S(2)}) %collective-permute-start.23) | collective-permute-done | bytes 131104 | tf_op jit(solution)/shard_map/ppermute | solution.py:29
  113.5 7.7 %collective-permute-start.32 = (bf16[64,2048]{1,0:T(8,128)(2,1)S(1)}, bf16[64,2048]{1,0:T(8,128)(2,1)S(1)}, u32[]{:S(2)}, u32[]{:S(2)}) collective-permute-start(bf16[64,2048]{1,0:T(8,128)(2,1)S(1)} %combine.4), channel_id=1, source_target_pairs={{0,16},{8,24},{16,0},{24,8},{1,17},{9,25},{17,1},{25,9},{2,18},{10... | collective-permute-start | bytes 786440 | tf_op jit(solution)/shard_map/ppermute | solution.py:29
  122.3 2.4 %collective-permute-start.36 = (bf16[64,2048]{1,0:T(8,128)(2,1)S(1)}, bf16[64,2048]{1,0:T(8,128)(2,1)S(1)}, u32[]{:S(2)}, u32[]{:S(2)}) collective-permute-start(bf16[64,2048]{1,0:T(8,128)(2,1)S(1)} %combine.7), channel_id=1, source_target_pairs={{0,8},{8,0},{16,24},{24,16},{1,9},{9,1},{17,25},{25,17},{2,10},{10... | collective-permute-start | bytes 786440 | tf_op jit(solution)/shard_map/ppermute | solution.py:29
  126.2 1.8 %collective-permute-start.30 = (bf16[32,2048]{1,0:T(8,128)(2,1)S(1)}, bf16[32,2048]{1,0:T(8,128)(2,1)S(1)}, u32[]{:S(2)}, u32[]{:S(2)}) collective-permute-start(bf16[32,2048]{1,0:T(8,128)(2,1)S(1)} %copy-done.33), channel_id=1, source_target_pairs={{0,4},{2,6},{4,0},{6,2},{1,5},{3,7},{5,1},{7,3},{8,12},{10,14},{12... | collective-permute-start | bytes 393224 | tf_op jit(solution)/shard_map/ppermute | solution.py:29
  129.2 1.2 gather_fusion.1
  131.2 2.7 %collective-permute-done.31.refs_3_ = bf16[32,2048]{1,0:T(8,128)(2,1)S(1)} collective-permute-done((bf16[32,2048]{1,0:T(8,128)(2,1)S(1)}, bf16[32,2048]{1,0:T(8,128)(2,1)S(1)}, u32[]{:S(2)}, u32[]{:S(2)}) %collective-permute-start.31) | collective-permute-done | bytes 131104 | tf_op jit(solution)/shard_map/ppermute | solution.py:29
  (145 shorter events, 26.4 us)
Async XLA Ops:
  2.5 13.2 %collective-permute-start.4 = (bf16[704,2048]{1,0:T(8,128)(2,1)}, bf16[704,2048]{1,0:T(8,128)(2,1)S(1)}, u32[]{:S(2)}, u32[]{:S(2)}) collective-permute-start(bf16[704,2048]{1,0:T(8,128)(2,1)} %bitcast.32), channel_id=1, source_target_pairs={{0,1},{1,0},{2,3},{3,2},{4,5},{5,4},{6,7},{7,6},{8,9},{9,8},{10,11... | collective-permute-start | bytes 8650760 | tf_op jit(solution)/shard_map/ppermute | solution.py:29
  2.9 9.8 %collective-permute-start = (bf16[64,2048]{1,0:T(8,128)(2,1)}, bf16[64,2048]{1,0:T(8,128)(2,1)}, u32[]{:S(2)}, u32[]{:S(2)}) collective-permute-start(bf16[64,2048]{1,0:T(8,128)(2,1)} %bitcast.22), channel_id=1, source_target_pairs={{0,2},{2,0},{1,3},{3,1},{4,6},{6,4},{5,7},{7,5},{8,10},{10,8},{9,1... | collective-permute-start | bytes 786440 | tf_op jit(solution)/shard_map/ppermute | solution.py:29
  15.3 9.7 %collective-permute-start.6 = (bf16[352,2048]{1,0:T(8,128)(2,1)}, bf16[352,2048]{1,0:T(8,128)(2,1)}, u32[]{:S(2)}, u32[]{:S(2)}) collective-permute-start(bf16[352,2048]{1,0:T(8,128)(2,1)} %bitcast.37), channel_id=1, source_target_pairs={{0,1},{1,0},{2,3},{3,2},{4,5},{5,4},{6,7},{7,6},{8,9},{9,8},{10,11... | collective-permute-start | bytes 4325384 | tf_op jit(solution)/shard_map/ppermute | solution.py:29
  15.4 9.6 %collective-permute-start.7 = (bf16[352,2048]{1,0:T(8,128)(2,1)}, bf16[352,2048]{1,0:T(8,128)(2,1)}, u32[]{:S(2)}, u32[]{:S(2)}) collective-permute-start(bf16[352,2048]{1,0:T(8,128)(2,1)} %refs_4_.1), channel_id=1, source_target_pairs={{0,1},{1,0},{2,3},{3,2},{4,5},{5,4},{6,7},{7,6},{8,9},{9,8},{10,11... | collective-permute-start | bytes 4325384 | tf_op jit(solution)/shard_map/ppermute | solution.py:29
  26.6 11.7 %collective-permute-start.9 = (bf16[2048,1408]{1,0:T(8,128)(2,1)}, bf16[2048,1408]{1,0:T(8,128)(2,1)}, u32[]{:S(2)}, u32[]{:S(2)}) collective-permute-start(bf16[2048,1408]{1,0:T(8,128)(2,1)} %bitcast.27), channel_id=1, source_target_pairs={{0,1},{1,0},{2,3},{3,2},{4,5},{5,4},{6,7},{7,6},{8,9},{9,8},{10,11... | collective-permute-start | bytes 17301512 | tf_op jit(solution)/shard_map/ppermute | solution.py:29
  27.8 9.3 %collective-permute-start.8 = (bf16[64,2048]{1,0:T(8,128)(2,1)S(1)}, bf16[64,2048]{1,0:T(8,128)(2,1)S(1)}, u32[]{:S(2)}, u32[]{:S(2)}) collective-permute-start(bf16[64,2048]{1,0:T(8,128)(2,1)S(1)} %add.35), channel_id=1, source_target_pairs={{0,2},{2,0},{1,3},{3,1},{4,6},{6,4},{5,7},{7,5},{8,10},{10,8},{9,1... | collective-permute-start | bytes 786440 | tf_op jit(solution)/shard_map/ppermute | solution.py:29
  39.0 8.4 %collective-permute-start.12 = (bf16[64,2048]{1,0:T(8,128)(2,1)S(1)}, bf16[64,2048]{1,0:T(8,128)(2,1)S(1)}, u32[]{:S(2)}, u32[]{:S(2)}) collective-permute-start(bf16[64,2048]{1,0:T(8,128)(2,1)S(1)} %get-tuple-element.120.refs_0_), channel_id=1, source_target_pairs={{0,2},{2,0},{1,3},{3,1},{4,6},{6,4},{5,7},{7,5},{8,10},{10,8},{9,1... | collective-permute-start | bytes 786440 | tf_op jit(solution)/shard_map/ppermute | solution.py:29
  39.3 12.6 %collective-permute-start.11 = (bf16[64,2176]{1,0:T(8,128)(2,1)S(1)}, bf16[64,2176]{1,0:T(8,128)(2,1)S(1)}, u32[]{:S(2)}, u32[]{:S(2)}) collective-permute-start(bf16[64,2176]{1,0:T(8,128)(2,1)S(1)} %get-tuple-element.137.refs_2_), channel_id=1, source_target_pairs={{0,24},{8,16},{16,8},{24,0},{1,25},{9,17},{17,9},{25,1},{2,26},{10... | collective-permute-start | bytes 835592 | tf_op jit(solution)/shard_map/ppermute | solution.py:29
  47.4 20.1 %collective-permute-start.16 = (bf16[64,2176]{1,0:T(8,128)(2,1)S(1)}, bf16[64,2176]{1,0:T(8,128)(2,1)S(1)}, u32[]{:S(2)}, u32[]{:S(2)}) collective-permute-start(bf16[64,2176]{1,0:T(8,128)(2,1)S(1)} %get-tuple-element.137.refs_2_), channel_id=1, source_target_pairs={{0,16},{8,24},{16,0},{24,8},{1,17},{9,25},{17,1},{25,9},{2,18},{10... | collective-permute-start | bytes 835592 | tf_op jit(solution)/shard_map/ppermute | solution.py:29
  49.3 19.1 %collective-permute-start.17 = (bf16[64,2176]{1,0:T(8,128)(2,1)S(1)}, bf16[64,2176]{1,0:T(8,128)(2,1)S(1)}, u32[]{:S(2)}, u32[]{:S(2)}) collective-permute-start(bf16[64,2176]{1,0:T(8,128)(2,1)S(1)} %get-tuple-element.137.refs_2_), channel_id=1, source_target_pairs={{0,8},{8,0},{16,24},{24,16},{1,9},{9,1},{17,25},{25,17},{2,10},{10... | collective-permute-start | bytes 835592 | tf_op jit(solution)/shard_map/ppermute | solution.py:29
  54.2 17.0 %collective-permute-start.13 = (bf16[64,2048]{1,0:T(8,128)(2,1)S(1)}, bf16[64,2048]{1,0:T(8,128)(2,1)S(1)}, u32[]{:S(2)}, u32[]{:S(2)}) collective-permute-start(bf16[64,2048]{1,0:T(8,128)(2,1)S(1)} %get-tuple-element.128), channel_id=1, source_target_pairs={{0,2},{2,0},{4,6},{6,4},{1,3},{3,1},{5,7},{7,5},{8,10},{10,8},{12,... | collective-permute-start | bytes 786440 | tf_op jit(solution)/shard_map/ppermute | solution.py:29
  54.5 19.1 %collective-permute-start.14 = (bf16[64,2048]{1,0:T(8,128)(2,1)S(1)}, bf16[64,2048]{1,0:T(8,128)(2,1)S(1)}, u32[]{:S(2)}, u32[]{:S(2)}) collective-permute-start(bf16[64,2048]{1,0:T(8,128)(2,1)S(1)} %get-tuple-element.129), channel_id=1, source_target_pairs={{0,4},{2,6},{4,0},{6,2},{1,5},{3,7},{5,1},{7,3},{8,12},{10,14},{12... | collective-permute-start | bytes 786440 | tf_op jit(solution)/shard_map/ppermute | solution.py:29
  56.9 17.2 %collective-permute-start.15 = (bf16[64,2048]{1,0:T(8,128)(2,1)S(1)}, bf16[64,2048]{1,0:T(8,128)(2,1)}, u32[]{:S(2)}, u32[]{:S(2)}) collective-permute-start(bf16[64,2048]{1,0:T(8,128)(2,1)S(1)} %get-tuple-element.130), channel_id=1, source_target_pairs={{0,6},{2,4},{4,2},{6,0},{1,7},{3,5},{5,3},{7,1},{8,14},{10,12},{12... | collective-permute-start | bytes 786440 | tf_op jit(solution)/shard_map/ppermute | solution.py:29
  67.5 18.1 %collective-permute-start.21 = (bf16[64,2048]{1,0:T(8,128)(2,1)}, bf16[64,2048]{1,0:T(8,128)(2,1)S(1)}, u32[]{:S(2)}, u32[]{:S(2)}) collective-permute-start(bf16[64,2048]{1,0:T(8,128)(2,1)} %get-tuple-element.147), channel_id=1, source_target_pairs={{0,2},{2,0},{1,3},{3,1},{4,6},{6,4},{5,7},{7,5},{8,10},{10,8},{9,1... | collective-permute-start | bytes 786440 | tf_op jit(solution)/shard_map/ppermute | solution.py:29
  70.0 17.4 %collective-permute-start.18 = (bf16[64,2048]{1,0:T(8,128)(2,1)S(1)}, bf16[64,2048]{1,0:T(8,128)(2,1)S(1)}, u32[]{:S(2)}, u32[]{:S(2)}) collective-permute-start(bf16[64,2048]{1,0:T(8,128)(2,1)S(1)} %get-tuple-element.140), channel_id=1, source_target_pairs={{0,2},{2,0},{4,6},{6,4},{1,3},{3,1},{5,7},{7,5},{8,10},{10,8},{12,... | collective-permute-start | bytes 786440 | tf_op jit(solution)/shard_map/ppermute | solution.py:29
  71.2 16.9 %collective-permute-start.19 = (bf16[64,2048]{1,0:T(8,128)(2,1)S(1)}, bf16[64,2048]{1,0:T(8,128)(2,1)S(1)}, u32[]{:S(2)}, u32[]{:S(2)}) collective-permute-start(bf16[64,2048]{1,0:T(8,128)(2,1)S(1)} %get-tuple-element.141), channel_id=1, source_target_pairs={{0,4},{2,6},{4,0},{6,2},{1,5},{3,7},{5,1},{7,3},{8,12},{10,14},{12... | collective-permute-start | bytes 786440 | tf_op jit(solution)/shard_map/ppermute | solution.py:29
  73.6 16.3 %collective-permute-start.20 = (bf16[64,2048]{1,0:T(8,128)(2,1)S(1)}, bf16[64,2048]{1,0:T(8,128)(2,1)S(1)}, u32[]{:S(2)}, u32[]{:S(2)}) collective-permute-start(bf16[64,2048]{1,0:T(8,128)(2,1)S(1)} %get-tuple-element.142), channel_id=1, source_target_pairs={{0,6},{2,4},{4,2},{6,0},{1,7},{3,5},{5,3},{7,1},{8,14},{10,12},{12... | collective-permute-start | bytes 786440 | tf_op jit(solution)/shard_map/ppermute | solution.py:29
  84.5 17.8 %collective-permute-start.25 = (bf16[32,2048]{1,0:T(8,128)(2,1)}, bf16[32,2048]{1,0:T(8,128)(2,1)S(1)}, u32[]{:S(2)}, u32[]{:S(2)}) collective-permute-start(bf16[32,2048]{1,0:T(8,128)(2,1)} %get-tuple-element.144), channel_id=1, source_target_pairs={{0,2},{2,0},{4,6},{6,4},{1,3},{3,1},{5,7},{7,5},{8,10},{10,8},{12,... | collective-permute-start | bytes 393224 | tf_op jit(solution)/shard_map/ppermute | solution.py:29
  85.5 16.9 %collective-permute-start.26 = (bf16[32,2048]{1,0:T(8,128)(2,1)}, bf16[32,2048]{1,0:T(8,128)(2,1)S(1)}, u32[]{:S(2)}, u32[]{:S(2)}) collective-permute-start(bf16[32,2048]{1,0:T(8,128)(2,1)} %get-tuple-element.145), channel_id=1, source_target_pairs={{0,4},{2,6},{4,0},{6,2},{1,5},{3,7},{5,1},{7,3},{8,12},{10,14},{12... | collective-permute-start | bytes 393224 | tf_op jit(solution)/shard_map/ppermute | solution.py:29
  87.4 15.0 %collective-permute-start.27 = (bf16[32,2048]{1,0:T(8,128)(2,1)}, bf16[32,2048]{1,0:T(8,128)(2,1)S(1)}, u32[]{:S(2)}, u32[]{:S(2)}) collective-permute-start(bf16[32,2048]{1,0:T(8,128)(2,1)} %get-tuple-element.146), channel_id=1, source_target_pairs={{0,6},{2,4},{4,2},{6,0},{1,7},{3,5},{5,3},{7,1},{8,14},{10,12},{12... | collective-permute-start | bytes 393224 | tf_op jit(solution)/shard_map/ppermute | solution.py:29
  101.2 6.7 %collective-permute-start.22 = (bf16[32,2048]{1,0:T(8,128)(2,1)}, bf16[32,2048]{1,0:T(8,128)(2,1)S(1)}, u32[]{:S(2)}, u32[]{:S(2)}) collective-permute-start(bf16[32,2048]{1,0:T(8,128)(2,1)} %get-tuple-element.153), channel_id=1, source_target_pairs={{0,2},{2,0},{4,6},{6,4},{1,3},{3,1},{5,7},{7,5},{8,10},{10,8},{12,... | collective-permute-start | bytes 393224 | tf_op jit(solution)/shard_map/ppermute | solution.py:29
  102.1 10.2 %collective-permute-start.23 = (bf16[32,2048]{1,0:T(8,128)(2,1)}, bf16[32,2048]{1,0:T(8,128)(2,1)S(1)}, u32[]{:S(2)}, u32[]{:S(2)}) collective-permute-start(bf16[32,2048]{1,0:T(8,128)(2,1)} %get-tuple-element.154), channel_id=1, source_target_pairs={{0,4},{2,6},{4,0},{6,2},{1,5},{3,7},{5,1},{7,3},{8,12},{10,14},{12... | collective-permute-start | bytes 393224 | tf_op jit(solution)/shard_map/ppermute | solution.py:29
  102.6 22.8 %collective-permute-start.28 = (bf16[64,2048]{1,0:T(8,128)(2,1)S(1)}, bf16[64,2048]{1,0:T(8,128)(2,1)S(1)}, u32[]{:S(2)}, u32[]{:S(2)}) collective-permute-start(bf16[64,2048]{1,0:T(8,128)(2,1)S(1)} %combine.5), channel_id=1, source_target_pairs={{0,24},{8,16},{16,8},{24,0},{1,25},{9,17},{17,9},{25,1},{2,26},{10... | collective-permute-start | bytes 786440 | tf_op jit(solution)/shard_map/ppermute | solution.py:29
  105.0 7.4 %collective-permute-start.24 = (bf16[32,2048]{1,0:T(8,128)(2,1)}, bf16[32,2048]{1,0:T(8,128)(2,1)S(1)}, u32[]{:S(2)}, u32[]{:S(2)}) collective-permute-start(bf16[32,2048]{1,0:T(8,128)(2,1)} %get-tuple-element.155), channel_id=1, source_target_pairs={{0,6},{2,4},{4,2},{6,0},{1,7},{3,5},{5,3},{7,1},{8,14},{10,12},{12... | collective-permute-start | bytes 393224 | tf_op jit(solution)/shard_map/ppermute | solution.py:29
  107.1 14.1 %collective-permute-start.33 = (bf16[32,2048]{1,0:T(8,128)(2,1)}, bf16[32,2048]{1,0:T(8,128)(2,1)S(1)}, u32[]{:S(2)}, u32[]{:S(2)}) collective-permute-start(bf16[32,2048]{1,0:T(8,128)(2,1)} %get-tuple-element.173), channel_id=1, source_target_pairs={{0,2},{2,0},{4,6},{6,4},{1,3},{3,1},{5,7},{7,5},{8,10},{10,8},{12,... | collective-permute-start | bytes 393224 | tf_op jit(solution)/shard_map/ppermute | solution.py:29
  107.8 13.4 %collective-permute-start.34 = (bf16[32,2048]{1,0:T(8,128)(2,1)}, bf16[32,2048]{1,0:T(8,128)(2,1)S(1)}, u32[]{:S(2)}, u32[]{:S(2)}) collective-permute-start(bf16[32,2048]{1,0:T(8,128)(2,1)} %get-tuple-element.174), channel_id=1, source_target_pairs={{0,4},{2,6},{4,0},{6,2},{1,5},{3,7},{5,1},{7,3},{8,12},{10,14},{12... | collective-permute-start | bytes 393224 | tf_op jit(solution)/shard_map/ppermute | solution.py:29
  112.3 8.9 %collective-permute-start.35 = (bf16[32,2048]{1,0:T(8,128)(2,1)}, bf16[32,2048]{1,0:T(8,128)(2,1)S(1)}, u32[]{:S(2)}, u32[]{:S(2)}) collective-permute-start(bf16[32,2048]{1,0:T(8,128)(2,1)} %get-tuple-element.175), channel_id=1, source_target_pairs={{0,6},{2,4},{4,2},{6,0},{1,7},{3,5},{5,3},{7,1},{8,14},{10,12},{12... | collective-permute-start | bytes 393224 | tf_op jit(solution)/shard_map/ppermute | solution.py:29
  113.5 20.6 %collective-permute-start.32 = (bf16[64,2048]{1,0:T(8,128)(2,1)S(1)}, bf16[64,2048]{1,0:T(8,128)(2,1)S(1)}, u32[]{:S(2)}, u32[]{:S(2)}) collective-permute-start(bf16[64,2048]{1,0:T(8,128)(2,1)S(1)} %combine.4), channel_id=1, source_target_pairs={{0,16},{8,24},{16,0},{24,8},{1,17},{9,25},{17,1},{25,9},{2,18},{10... | collective-permute-start | bytes 786440 | tf_op jit(solution)/shard_map/ppermute | solution.py:29
  122.3 11.8 %collective-permute-start.36 = (bf16[64,2048]{1,0:T(8,128)(2,1)S(1)}, bf16[64,2048]{1,0:T(8,128)(2,1)S(1)}, u32[]{:S(2)}, u32[]{:S(2)}) collective-permute-start(bf16[64,2048]{1,0:T(8,128)(2,1)S(1)} %combine.7), channel_id=1, source_target_pairs={{0,8},{8,0},{16,24},{24,16},{1,9},{9,1},{17,25},{25,17},{2,10},{10... | collective-permute-start | bytes 786440 | tf_op jit(solution)/shard_map/ppermute | solution.py:29
  125.4 5.0 %collective-permute-start.29 = (bf16[32,2048]{1,0:T(8,128)(2,1)S(1)}, bf16[32,2048]{1,0:T(8,128)(2,1)S(1)}, u32[]{:S(2)}, u32[]{:S(2)}) collective-permute-start(bf16[32,2048]{1,0:T(8,128)(2,1)S(1)} %copy-done.34), channel_id=1, source_target_pairs={{0,2},{2,0},{4,6},{6,4},{1,3},{3,1},{5,7},{7,5},{8,10},{10,8},{12,... | collective-permute-start | bytes 393224 | tf_op jit(solution)/shard_map/ppermute | solution.py:29
  126.2 5.0 %collective-permute-start.30 = (bf16[32,2048]{1,0:T(8,128)(2,1)S(1)}, bf16[32,2048]{1,0:T(8,128)(2,1)S(1)}, u32[]{:S(2)}, u32[]{:S(2)}) collective-permute-start(bf16[32,2048]{1,0:T(8,128)(2,1)S(1)} %copy-done.33), channel_id=1, source_target_pairs={{0,4},{2,6},{4,0},{6,2},{1,5},{3,7},{5,1},{7,3},{8,12},{10,14},{12... | collective-permute-start | bytes 393224 | tf_op jit(solution)/shard_map/ppermute | solution.py:29
  128.0 5.9 %collective-permute-start.31 = (bf16[32,2048]{1,0:T(8,128)(2,1)S(1)}, bf16[32,2048]{1,0:T(8,128)(2,1)S(1)}, u32[]{:S(2)}, u32[]{:S(2)}) collective-permute-start(bf16[32,2048]{1,0:T(8,128)(2,1)S(1)} %copy-done.32), channel_id=1, source_target_pairs={{0,6},{2,4},{4,2},{6,0},{1,7},{3,5},{5,3},{7,1},{8,14},{10,12},{12... | collective-permute-start | bytes 393224 | tf_op jit(solution)/shard_map/ppermute | solution.py:29
  (44 other events, 629.4 us)

commit v12 on v10

--- a/solution.py
+++ b/solution.py
@@ -12,7 +12,7 @@
 
 EPSILON = 1e-06
 ROPE_BASE = 10000.0
-GROUPS = ((0, 3), (2, 1))
+GROUPS = ((3,), (2, 1))
 BACK = ((3, None, None), (2, None, None), (1, 3, None), (0, 2, 3))
 CHUNK = 512
 EXTRA = 128
@@ -256,12 +256,11 @@
     return values / (1.0 + jnp.exp(-values))
 
 
-def expert_kernel(*refs, plane, count, deep):
-    pieces = refs[:plane]
-    weights = refs[plane : plane + 4]
-    outs = refs[plane + 4 : plane + 4 + count * plane]
-    rows, inner_a, outer_a, inner_b, outer_b, sems = refs[plane + 4 + count * plane :]
-    each = pieces[0].shape[0]
+def expert_kernel(*refs, layout, count, deep):
+    pieces = refs[:count]
+    weights = refs[count : count + 4]
+    outs = refs[count + 4 : count + 4 + len(layout)]
+    rows, inner_a, outer_a, inner_b, outer_b, sems = refs[count + 4 + len(layout) :]
     width = rows.shape[1]
     parts = width // deep
     copies = []
@@ -283,8 +282,10 @@
         if number + 2 < len(copies):
             copies[number + 2].start()
 
-    for i in range(plane):
-        rows[i * each : (i + 1) * each] = pieces[i][...]
+    base = 0
+    for piece in pieces:
+        rows[base : base + piece.shape[0]] = piece[...]
+        base += piece.shape[0]
     result = None
     for n, (inner_here, outer_here) in enumerate(((inner_a, outer_a), (inner_b, outer_b))):
         base = n * (parts + 1)
@@ -298,51 +299,35 @@
         take(base + parts)
         term = dot(hidden, outer_here[...]).astype(jnp.bfloat16).astype(jnp.float32)
         result = term if result is None else result + term
-    step = each // count
-    for n in range(count * plane):
-        base = (n % plane) * each + (n // plane) * step
-        outs[n][...] = result[base : base + step].astype(jnp.bfloat16)
-
-
-def experts(pieces, count, inner, outer):
-    plane = len(pieces)
-    each, width = pieces[0].shape
+    step = rows.shape[0] // len(layout)
+    for n, place in enumerate(layout):
+        outs[place][...] = result[n * step : (n + 1) * step].astype(jnp.bfloat16)
+
+
+def experts(pieces, layout, plane, inner, outer):
+    count = len(pieces)
+    rows = sum(piece.shape[0] for piece in pieces)
+    width = pieces[0].shape[1]
     hidden = inner[0].shape[1]
     deep = width // 2
-    kernel = functools.partial(expert_kernel, plane=plane, count=count, deep=deep)
+    step = rows // len(layout)
     weight_scratch = [
         pltpu.VMEM((width, hidden), jnp.bfloat16),
         pltpu.VMEM((hidden // 2, width), jnp.bfloat16),
     ]
     made = pl.pallas_call(
-        kernel,
-        in_specs=[in_vmem()] * plane + [in_hbm()] * 4,
-        out_specs=[in_vmem()] * (count * plane),
-        out_shape=[jax.ShapeDtypeStruct((each // count, width), jnp.bfloat16)] * (count * plane),
-        scratch_shapes=[pltpu.VMEM((plane * each, width), jnp.bfloat16)]
+        functools.partial(expert_kernel, layout=layout, count=count, deep=deep),
+        in_specs=[in_vmem()] * count + [in_hbm()] * 4,
+        out_specs=[in_vmem()] * len(layout),
+        out_shape=[jax.ShapeDtypeStruct((step, width), jnp.bfloat16)] * len(layout),
+        scratch_shapes=[pltpu.VMEM((rows, width), jnp.bfloat16)]
         + weight_scratch * 2
         + [pltpu.SemaphoreType.DMA((2 * (width // deep + 1),))],
         compiler_params=pltpu.CompilerParams(vmem_limit_bytes=40 * 2**20),
         cost_estimate=SMALL,
         name="expert",
     )(*pieces, inner[0], outer[0], inner[1], outer[1])
-    return [list(made[i * plane : (i + 1) * plane]) for i in range(count)]
-
-
-def hold_kernel(*refs):
-    refs[-1][...] = refs[0][...]
-
-
-def hold(token, weights):
-    return pl.pallas_call(
-        hold_kernel,
-        in_specs=[in_vmem()] + [in_hbm()] * len(weights),
-        out_specs=in_vmem(),
-        out_shape=jax.ShapeDtypeStruct(token.shape, token.dtype),
-        compiler_params=pltpu.CompilerParams(vmem_limit_bytes=16 * 2**20),
-        cost_estimate=SMALL,
-        name="hold",
-    )(token, *weights)
+    return [list(made[i : i + plane]) for i in range(0, len(layout), plane)]
 
 
 def shared_kernel(*refs, side):
@@ -360,7 +345,8 @@
             copies[number + 2].start()
 
     tree = blocks[0].shape[0]
-    rows = jnp.concatenate([block[...] for block in blocks], axis=0).T
+    width = here.shape[2]
+    rows = jnp.concatenate([block[:, :width] for block in blocks], axis=0).T
 
     def turned(i):
         take(i)
@@ -380,8 +366,8 @@
 
 
 def shared_terms(own, beside, weights):
-    tree, width = own.shape
-    units = weights[0].shape[0]
+    tree = own.shape[0]
+    units, width = weights[0].shape
     side = 1 + len(beside)
     outs = pl.pallas_call(
         functools.partial(shared_kernel, side=side),
@@ -647,30 +633,50 @@
         lax.axis_index(PLANE) ^ jnp.arange(plane, dtype=jnp.int32)
     )
     line_rows = [payload] + [partner(payload, "z", k) for k in range(1, line)]
-    beside = [partner(normed, "x", o) for o in range(1, side)]
-
-    shared, beside = shared_terms(normed, beside, shared_weights)
-    line_rows[3], beside = lax.optimization_barrier((line_rows[3], beside))
+    beside = [partner(payload, "x", o) for o in range(1, side)]
+
+    spread = {}
+
+    def choose(ks, sources, experts_near, count):
+        return select(experts_near, router, sources, count, capacity, top_count)
+
+    first_pieces, spreads = choose((0,), [payload], near_experts, plane)
+    spread[0] = spreads[0]
+    first_pieces, beside = lax.optimization_barrier((first_pieces, beside))
+    local, unused = choose((0,), [payload, *beside], near_experts[:1], 1)
+    first = local + [partner(first_pieces[o], PLANE, o) for o in range(side, plane)]
+
+    shared, beside = shared_terms(
+        normed, beside, [gate_turned, up_turned, shared_down, early[0], *middle]
+    )
+    line_rows[3], beside, first = lax.optimization_barrier((line_rows[3], beside, first))
 
     sent = []
-    spread = {}
+    layouts = []
     for ks in GROUPS:
-        pieces, spreads = select(
-            near_experts, router, [line_rows[k] for k in ks], plane, capacity, top_count
-        )
+        pieces, spreads = choose(ks, [line_rows[k] for k in ks], near_experts, plane)
         spread.update(zip(ks, spreads))
-        if len(sent) == 1:
-            token = hold(spreads[0], [inner[0], outer[0], inner[1], outer[1]])
-            sent[0], spread[ks[0]] = lax.optimization_barrier((sent[0], token))
-        sent.append([partner(pieces[o], PLANE, o) for o in range(plane)])
+        if sent:
+            pieces[-1], sent[0][-plane + 1] = lax.optimization_barrier(
+                (pieces[-1], sent[0][-plane + 1])
+            )
+        moved = [partner(pieces[o], PLANE, o) for o in range(plane)]
+        layout = [i * plane + o for o in range(plane) for i in range(len(ks))]
+        if not sent:
+            moved = first + moved
+            layout = list(range(plane)) + [plane + place for place in layout]
+        sent.append(moved)
+        layouts.append(layout)
+
+    beside, sent[0] = lax.optimization_barrier((beside, sent[0]))
     parts = [partner(beside[o - 1], "x", o) for o in range(1, side)]
     made = None
     results = {}
-    for ks, pieces in zip(GROUPS, sent):
+    for ks, pieces, layout in zip(GROUPS, sent, layouts):
         if made is not None:
             pieces, made, parts = lax.optimization_barrier((pieces, made, parts))
-        made = experts(pieces, len(ks), inner, outer)
-        results.update(zip(ks, made))
+        made = experts(pieces, layout, plane, inner, outer)
+        results.update(zip(ks if results else (0, *ks), made))
     totals = {}
     landed = {}
     for k, after, arrived in BACK:

time: 137 us -> 136 us (level); the launches traced: 135 us -> 136 us
  waiting for transfers between devices: 23.4 us -> 16.8 us
  Pallas kernels: 47.5 us -> 52.4 us
  starting transfers between devices: 43 us -> 46.6 us
  local copies, waits for them, and re-layouts: 20.2 us -> 18.8 us
    ppermute x37 -> x39, waiting for transfers between devices: 23.4 us -> 16.8 us  [partner(): return lax.ppermute(value, axes, [(i, i ^ offset) for i in range(size)])]
    pallas_call x2 -> x4, Pallas kernels: 3.28 us -> 8.6 us  [select(): pl.pallas_call(functools.partial(select_kernel, count=count, plane=plane,...]
    ppermute x37 -> x39, starting transfers between devices: 43 us -> 46.6 us  [partner(): return lax.ppermute(value, axes, [(i, i ^ offset) for i in range(size)])]
    unnamed x70 -> x92, local copies, waits for them, and re-layouts: 18.4 us -> 17 us
    pallas_call x3 -> x2, Pallas kernels: 15.3 us -> 15.3 us  [experts(): pl.pallas_call(functools.partial(expert_kernel, layout=layout, count=coun...]
  transfers between devices with their start and end apart: 37 -> 39, of which waited for: 16 -> 14; matrix products, arithmetic and copies ran while one was open for 2% -> 2% of each run, Pallas kernels for 34% -> 37%
where the time goes in v12:
time: 136 us
  Pallas kernels  52.4 us (39%)
  starting transfers between devices  46.6 us (34%)
  local copies, waits for them, and re-layouts  18.8 us (14%)
  waiting for transfers between devices  16.8 us (12%)
    ppermute x39, starting transfers between devices, partner(): return lax.ppermute(value, axes, [(i, i ^ offset) for i in range(size)])  46.6 us
    unnamed x92, local copies, waits for them, and re-layouts  17 us
    ppermute x39, waiting for transfers between devices, partner(): return lax.ppermute(value, axes, [(i, i ^ offset) for i in range(size)])  16.8 us
    pallas_call x2, Pallas kernels, experts(): pl.pallas_call(functools.partial(expert_kernel, layout=layout, count=coun...  15.3 us
    pallas_call x2, Pallas kernels, attend(): pl.pallas_call(functools.partial(attend_kernel, offset=offset), in_specs=...  15.2 us
    pallas_call x4, Pallas kernels, select(): pl.pallas_call(functools.partial(select_kernel, count=count, plane=plane,...  8.6 us
    pallas_call x1, Pallas kernels, shared_terms(): pl.pallas_call(functools.partial(shared_kernel, side=side), in_specs=[in_...  8.39 us
  transfers between devices with their start and end apart: 39, of which 14 were waited for; matrix products, arithmetic and copies ran while one was open for 2% of the time, Pallas kernels for 37%

profile of v12, /device:TPU:0, one launch (start us, length us, event | category | flops | bytes accessed | tf_op | source)
XLA Modules:
  0.0 135.9 jit_solution(7399296918458815468)
XLA Ops:
  1.2 1.4 %collective-permute-done.1.second = bf16[64,2048]{1,0:T(8,128)(2,1)S(1)} collective-permute-done((bf16[64,2048]{1,0:T(8,128)(2,1)}, bf16[64,2048]{1,0:T(8,128)(2,1)S(1)}, u32[]{:S(2)}, u32[]{:S(2)}) %collective-permute-start.1) | collective-permute-done | bytes 262176 | tf_op jit(solution)/shard_map/ppermute | solution.py:29
  2.9 2.6 %collective-permute-start = (bf16[64,2048]{1,0:T(8,128)(2,1)}, bf16[64,2048]{1,0:T(8,128)(2,1)S(1)}, u32[]{:S(2)}, u32[]{:S(2)}) collective-permute-start(bf16[64,2048]{1,0:T(8,128)(2,1)} %bitcast.29), channel_id=1, source_target_pairs={{0,2},{2,0},{1,3},{3,1},{4,6},{6,4},{5,7},{7,5},{8,10},{10,8},{9,1... | collective-permute-start | bytes 786440 | tf_op jit(solution)/shard_map/ppermute | solution.py:29
  7.5 2.0 %prepare.1 = (f32[4,64,64]{2,1,0:T(8,128)S(1)}, f32[4,64,128]{2,1,0:T(8,128)S(1)}, f32[4,64,128]{2,1,0:T(8,128)S(1)}) custom-call(s32[4]{0:T(128)S(1)} %copy-done.25, s32[4,64]{1,0:T(4,128)S(1)} %copy-done.26, f32[1,128]{1,0:T(1,128)S(1)} %copy-done.27), custom_call_target="tpu_custom_call" | custom-call | flops 1024 | bytes 1024 | tf_op jit(solution)/shard_map/prepare/pallas_call | solution.py:68
  12.6 2.5 %collective-permute-done.2.second = bf16[64,2048]{1,0:T(8,128)(2,1)S(1)} collective-permute-done((bf16[64,2048]{1,0:T(8,128)(2,1)S(1)}, bf16[64,2048]{1,0:T(8,128)(2,1)S(1)}, u32[]{:S(2)}, u32[]{:S(2)}) %collective-permute-start.2) | collective-permute-done | bytes 262176 | tf_op jit(solution)/shard_map/ppermute | solution.py:29
  16.7 7.9 %attend.2 = (f32[64,2048]{1,0:T(8,128)}, bf16[64,2048]{1,0:T(8,128)(2,1)}, bf16[64,256]{1,0:T(8,128)(2,1)}, bf16[64,256]{1,0:T(8,128)(2,1)}) custom-call(s32[1]{0:T(128)} %bitcast.2.place, s32[4]{0:T(128)} %lengths.5, bf16[64,2048]{1,0:T(8,128)(2,1)} %copy-done.36, bf16[64,2048]{1,0:T(8,128)(2,1)} %copy-done.37, f32[1,2048]{1,0:T(1,128)} %bitcast.42, ...), custom_call_target="tpu_custom_call" | custom-call | flops 1024 | bytes 1024 | tf_op jit(solution)/shard_map/attend/pallas_call | solution.py:204
  24.9 1.6 %collective-permute-done.5.right = bf16[64,2048]{1,0:T(8,128)(2,1)S(1)} collective-permute-done((bf16[64,2048]{1,0:T(8,128)(2,1)}, bf16[64,2048]{1,0:T(8,128)(2,1)S(1)}, u32[]{:S(2)}, u32[]{:S(2)}) %collective-permute-start.5) | collective-permute-done | bytes 262176 | tf_op jit(solution)/shard_map/ppermute | solution.py:29
  28.6 7.2 %attend.3 = (f32[64,2048]{1,0:T(8,128)}, bf16[64,2048]{1,0:T(8,128)(2,1)}, bf16[64,256]{1,0:T(8,128)(2,1)}, bf16[64,256]{1,0:T(8,128)(2,1)}) custom-call(s32[1]{0:T(128)} %bitcast.2.place, s32[4]{0:T(128)} %lengths.5, bf16[64,2048]{1,0:T(8,128)(2,1)} %bitcast.30, bf16[64,2048]{1,0:T(8,128)(2,1)} %copy-done.35, f32[1,2048]{1,0:T(1,128)} %bitcast.43, ...), custom_call_target="tpu_custom_call" | custom-call | flops 1024 | bytes 1024 | tf_op jit(solution)/shard_map/attend/pallas_call | solution.py:204
  41.2 4.4 %collective-permute-start.12 = (bf16[64,2176]{1,0:T(8,128)(2,1)}, bf16[64,2176]{1,0:T(8,128)(2,1)}, u32[]{:S(2)}, u32[]{:S(2)}) collective-permute-start(bf16[64,2176]{1,0:T(8,128)(2,1)} %get-tuple-element.135.refs_2_), channel_id=1, source_target_pairs={{0,24},{8,16},{16,8},{24,0},{1,25},{9,17},{17,9},{25,1},{2,26},{10... | collective-permute-start | bytes 835592 | tf_op jit(solution)/shard_map/ppermute | solution.py:29
  45.7 3.1 %collective-permute-start.15 = (bf16[64,2176]{1,0:T(8,128)(2,1)}, bf16[64,2176]{1,0:T(8,128)(2,1)}, u32[]{:S(2)}, u32[]{:S(2)}) collective-permute-start(bf16[64,2176]{1,0:T(8,128)(2,1)} %get-tuple-element.135.refs_2_), channel_id=1, source_target_pairs={{0,16},{8,24},{16,0},{24,8},{1,17},{9,25},{17,1},{25,9},{2,18},{10... | collective-permute-start | bytes 835592 | tf_op jit(solution)/shard_map/ppermute | solution.py:29
  49.0 2.3 %select.4 = (bf16[32,2048]{1,0:T(8,128)(2,1)}, bf16[32,2048]{1,0:T(8,128)(2,1)}, bf16[32,2048]{1,0:T(8,128)(2,1)}, bf16[32,2048]{1,0:T(8,128)(2,1)S(1)}, bf16[64,128]{1,0:T(8,128)(2,1)S(1)}) custom-call(s32[4]{0:T(128)S(1)} %xor_add_fusion.refs_0_, bf16[2048,16]{1,0:T(8,128)(2,1)S(1)} %copy.21.refs_1_, bf16[64,2176]{1,0:T(8,128)(2,1)} %get-tuple-element.135.refs_2_), custom_call_target="tpu_custom_call" | custom-call | flops 1024 | bytes 1024 | tf_op jit(solution)/shard_map/select/pallas_call | solution.py:479
  51.4 4.8 %collective-permute-start.13 = (bf16[32,2048]{1,0:T(8,128)(2,1)}, bf16[32,2048]{1,0:T(8,128)(2,1)S(1)}, u32[]{:S(2)}, u32[]{:S(2)}) collective-permute-start(bf16[32,2048]{1,0:T(8,128)(2,1)} %get-tuple-element.146), channel_id=1, source_target_pairs={{0,4},{2,6},{4,0},{6,2},{1,5},{3,7},{5,1},{7,3},{8,12},{10,14},{12... | collective-permute-start | bytes 393224 | tf_op jit(solution)/shard_map/ppermute | solution.py:29
  56.1 2.4 %select.5 = (bf16[64,2048]{1,0:T(8,128)(2,1)S(1)}, bf16[64,32]{1,0:T(8,128)(2,1)}, bf16[64,32]{1,0:T(8,128)(2,1)}) custom-call(s32[1]{0:T(128)S(1)} %bitcast.34, bf16[2048,16]{1,0:T(8,128)(2,1)S(1)} %copy.21.refs_1_, bf16[64,2176]{1,0:T(8,128)(2,1)} %get-tuple-element.135.refs_2_, bf16[64,2176]{1,0:T(8,128)(2,1)S(1)} %collective-permute-done.11.refs_1_.refs_3_), custom_call_target="tpu_custom_call" | custom-call | flops 1024 | bytes 1024 | tf_op jit(solution)/shard_map/select/pallas_call | solution.py:479
  58.6 8.4 %shared.1 = (f32[64,2048]{1,0:T(8,128)}, bf16[64,2048]{1,0:T(8,128)(2,1)}) custom-call(bf16[64,2048]{1,0:T(8,128)(2,1)} %copy-done.13, bf16[64,2176]{1,0:T(8,128)(2,1)} %copy-done.5, bf16[352,2048]{1,0:T(8,128)(2,1)} %bitcast.38, bf16[352,2048]{1,0:T(8,128)(2,1)} %bitcast.40, bf16[352,2048]{1,0:T(8,128)(2,1)} %refs_4_.1, bf16[352,2048]{1,0:T(8,128)(2,1)} %copy-done.34, ...), custom_call_target="tpu_custom_call" | custom-call | flops 1024 | bytes 1024 | tf_op jit(solution)/shard_map/shared/pallas_call | solution.py:372
  67.0 1.7 %select.6 = (bf16[32,2048]{1,0:T(8,128)(2,1)S(1)}, bf16[32,2048]{1,0:T(8,128)(2,1)S(1)}, bf16[32,2048]{1,0:T(8,128)(2,1)S(1)}, bf16[32,2048]{1,0:T(8,128)(2,1)S(1)}, bf16[64,128]{1,0:T(8,128)(2,1)S(1)}) custom-call(s32[4]{0:T(128)S(1)} %xor_add_fusion.refs_0_, bf16[2048,16]{1,0:T(8,128)(2,1)S(1)} %copy.21.refs_1_, ...), custom_call_target="tpu_custom_call" | custom-call | flops 1024 | bytes 1024 | tf_op jit(solution)/shard_map/select/pallas_call | solution.py:479
  68.7 1.5 %collective-permute-start.17 = (bf16[32,2048]{1,0:T(8,128)(2,1)S(1)}, bf16[32,2048]{1,0:T(8,128)(2,1)S(1)}, u32[]{:S(2)}, u32[]{:S(2)}) collective-permute-start(bf16[32,2048]{1,0:T(8,128)(2,1)S(1)} %get-tuple-element.155), channel_id=1, source_target_pairs={{0,2},{2,0},{4,6},{6,4},{1,3},{3,1},{5,7},{7,5},{8,10},{10,8},{12,... | collective-permute-start | bytes 393224 | tf_op jit(solution)/shard_map/ppermute | solution.py:29
  70.2 2.0 %collective-permute-start.18 = (bf16[32,2048]{1,0:T(8,128)(2,1)S(1)}, bf16[32,2048]{1,0:T(8,128)(2,1)S(1)}, u32[]{:S(2)}, u32[]{:S(2)}) collective-permute-start(bf16[32,2048]{1,0:T(8,128)(2,1)S(1)} %get-tuple-element.157), channel_id=1, source_target_pairs={{0,4},{2,6},{4,0},{6,2},{1,5},{3,7},{5,1},{7,3},{8,12},{10,14},{12... | collective-permute-start | bytes 393224 | tf_op jit(solution)/shard_map/ppermute | solution.py:29
  72.3 2.2 %select.7 = (bf16[64,2048]{1,0:T(8,128)(2,1)S(1)}, bf16[64,2048]{1,0:T(8,128)(2,1)S(1)}, bf16[64,2048]{1,0:T(8,128)(2,1)S(1)}, bf16[64,2048]{1,0:T(8,128)(2,1)S(...) custom-call(s32[4]{0:T(128)S(1)} %xor_add_fusion.refs_0_, bf16[2048,16]{1,0:T(8,128)(2,1)S(1)} %copy.21.refs_1_, ...), custom_call_target="tpu_custom_call" | custom-call | flops 1024 | bytes 1024 | tf_op jit(solution)/shard_map/select/pallas_call | solution.py:479
  74.4 1.5 %collective-permute-start.20 = (bf16[64,2048]{1,0:T(8,128)(2,1)S(1)}, bf16[64,2048]{1,0:T(8,128)(2,1)S(1)}, u32[]{:S(2)}, u32[]{:S(2)}) collective-permute-start(bf16[64,2048]{1,0:T(8,128)(2,1)S(1)} %get-tuple-element.174), channel_id=1, source_target_pairs={{0,2},{2,0},{4,6},{6,4},{1,3},{3,1},{5,7},{7,5},{8,10},{10,8},{12,... | collective-permute-start | bytes 786440 | tf_op jit(solution)/shard_map/ppermute | solution.py:29
  76.0 2.0 %collective-permute-start.21 = (bf16[64,2048]{1,0:T(8,128)(2,1)S(1)}, bf16[64,2048]{1,0:T(8,128)(2,1)S(1)}, u32[]{:S(2)}, u32[]{:S(2)}) collective-permute-start(bf16[64,2048]{1,0:T(8,128)(2,1)S(1)} %get-tuple-element.175), channel_id=1, source_target_pairs={{0,4},{2,6},{4,0},{6,2},{1,5},{3,7},{5,1},{7,3},{8,12},{10,14},{12... | collective-permute-start | bytes 786440 | tf_op jit(solution)/shard_map/ppermute | solution.py:29
  79.3 1.5 %collective-permute-start.23 = (bf16[64,2048]{1,0:T(8,128)(2,1)}, bf16[64,2048]{1,0:T(8,128)(2,1)S(1)}, u32[]{:S(2)}, u32[]{:S(2)}) collective-permute-start(bf16[64,2048]{1,0:T(8,128)(2,1)} %get-tuple-element.181), channel_id=1, source_target_pairs={{0,2},{2,0},{1,3},{3,1},{4,6},{6,4},{5,7},{7,5},{8,10},{10,8},{9,1... | collective-permute-start | bytes 786440 | tf_op jit(solution)/shard_map/ppermute | solution.py:29
  80.8 2.6 %copy-done.1 = bf16[1,2048,1408]{2,1,0:T(8,128)(2,1)S(1)} copy-done((bf16[1,2048,1408]{2,1,0:T(8,128)(2,1)S(1)}, bf16[1,2048,1408]{2,1,0:T(8,128)(2,1)}, u32[]{:S(2)}) %copy-start.1) | copy-done | bytes 5767192
  83.4 1.8 %copy-done.4 = bf16[704,2048]{1,0:T(8,128)(2,1)S(1)} copy-done((bf16[704,2048]{1,0:T(8,128)(2,1)S(1)}, bf16[704,2048]{1,0:T(8,128)(2,1)}, u32[]{:S(2)}) %copy-start.4) | copy-done | bytes 2883608
  86.1 7.6 %expert.2 = (bf16[32,2048]{1,0:T(8,128)(2,1)S(1)}, bf16[32,2048]{1,0:T(8,128)(2,1)S(1)}, bf16[32,2048]{1,0:T(8,128)(2,1)S(1)}, bf16[32,2048]{1,0:T(8,128)(2,1)S(...) custom-call(bf16[64,2048]{1,0:T(8,128)(2,1)S(1)} %get-tuple-element., ...), custom_call_target="tpu_custom_call" | custom-call | flops 1024 | bytes 1024 | tf_op jit(solution)/shard_map/expert/pallas_call | solution.py:318
  97.0 1.5 %collective-permute-start.28 = (bf16[32,2048]{1,0:T(8,128)(2,1)S(1)}, bf16[32,2048]{1,0:T(8,128)(2,1)S(1)}, u32[]{:S(2)}, u32[]{:S(2)}) collective-permute-start(bf16[32,2048]{1,0:T(8,128)(2,1)S(1)} %get-tuple-element.179), channel_id=1, source_target_pairs={{0,4},{2,6},{4,0},{6,2},{1,5},{3,7},{5,1},{7,3},{8,12},{10,14},{12... | collective-permute-start | bytes 393224 | tf_op jit(solution)/shard_map/ppermute | solution.py:29
  98.5 1.4 %collective-permute-start.29 = (bf16[32,2048]{1,0:T(8,128)(2,1)S(1)}, bf16[32,2048]{1,0:T(8,128)(2,1)S(1)}, u32[]{:S(2)}, u32[]{:S(2)}) collective-permute-start(bf16[32,2048]{1,0:T(8,128)(2,1)S(1)} %get-tuple-element.180), channel_id=1, source_target_pairs={{0,6},{2,4},{4,2},{6,0},{1,7},{3,5},{5,3},{7,1},{8,14},{10,12},{12... | collective-permute-start | bytes 393224 | tf_op jit(solution)/shard_map/ppermute | solution.py:29
  99.9 7.6 %expert.3 = (bf16[32,2048]{1,0:T(8,128)(2,1)S(1)}, bf16[32,2048]{1,0:T(8,128)(2,1)S(1)}, bf16[32,2048]{1,0:T(8,128)(2,1)S(1)}, bf16[32,2048]{1,0:T(8,128)(2,1)S(...) custom-call(bf16[64,2048]{1,0:T(8,128)(2,1)S(1)} %get-tuple-element., ...), custom_call_target="tpu_custom_call" | custom-call | flops 1024 | bytes 1024 | tf_op jit(solution)/shard_map/expert/pallas_call | solution.py:318
  108.3 1.5 %collective-permute-start.25 = (bf16[32,2048]{1,0:T(8,128)(2,1)S(1)}, bf16[32,2048]{1,0:T(8,128)(2,1)S(1)}, u32[]{:S(2)}, u32[]{:S(2)}) collective-permute-start(bf16[32,2048]{1,0:T(8,128)(2,1)S(1)} %get-tuple-element.188), channel_id=1, source_target_pairs={{0,4},{2,6},{4,0},{6,2},{1,5},{3,7},{5,1},{7,3},{8,12},{10,14},{12... | collective-permute-start | bytes 393224 | tf_op jit(solution)/shard_map/ppermute | solution.py:29
  116.9 1.8 %collective-permute-done.26.refs_3_ = bf16[32,2048]{1,0:T(8,128)(2,1)S(1)} collective-permute-done((bf16[32,2048]{1,0:T(8,128)(2,1)S(1)}, bf16[32,2048]{1,0:T(8,128)(2,1)S(1)}, u32[]{:S(2)}, u32[]{:S(2)}) %collective-permute-start.26) | collective-permute-done | bytes 131104 | tf_op jit(solution)/shard_map/ppermute | solution.py:29
  120.3 1.4 %collective-permute-done.37.refs_3_ = bf16[32,2048]{1,0:T(8,128)(2,1)S(1)} collective-permute-done((bf16[32,2048]{1,0:T(8,128)(2,1)S(1)}, bf16[32,2048]{1,0:T(8,128)(2,1)S(1)}, u32[]{:S(2)}, u32[]{:S(2)}) %collective-permute-start.37) | collective-permute-done | bytes 131104 | tf_op jit(solution)/shard_map/ppermute | solution.py:29
  124.0 4.1 %collective-permute-start.31 = (bf16[32,2048]{1,0:T(8,128)(2,1)S(1)}, bf16[32,2048]{1,0:T(8,128)(2,1)S(1)}, u32[]{:S(2)}, u32[]{:S(2)}) collective-permute-start(bf16[32,2048]{1,0:T(8,128)(2,1)S(1)} %copy-done.33), channel_id=1, source_target_pairs={{0,2},{2,0},{4,6},{6,4},{1,3},{3,1},{5,7},{7,5},{8,10},{10,8},{12,... | collective-permute-start | bytes 393224 | tf_op jit(solution)/shard_map/ppermute | solution.py:29
  128.1 1.5 %collective-permute-start.33 = (bf16[32,2048]{1,0:T(8,128)(2,1)S(1)}, bf16[32,2048]{1,0:T(8,128)(2,1)S(1)}, u32[]{:S(2)}, u32[]{:S(2)}) collective-permute-start(bf16[32,2048]{1,0:T(8,128)(2,1)S(1)} %copy-done.29), channel_id=1, source_target_pairs={{0,6},{2,4},{4,2},{6,0},{1,7},{3,5},{5,3},{7,1},{8,14},{10,12},{12... | collective-permute-start | bytes 393224 | tf_op jit(solution)/shard_map/ppermute | solution.py:29
  131.0 3.4 %collective-permute-done.32.refs_2_ = bf16[32,2048]{1,0:T(8,128)(2,1)S(1)} collective-permute-done((bf16[32,2048]{1,0:T(8,128)(2,1)S(1)}, bf16[32,2048]{1,0:T(8,128)(2,1)S(1)}, u32[]{:S(2)}, u32[]{:S(2)}) %collective-permute-start.32) | collective-permute-done | bytes 131104 | tf_op jit(solution)/shard_map/ppermute | solution.py:29
  (163 shorter events, 35.3 us)
Async XLA Ops:
  2.5 13.1 %collective-permute-start.4 = (bf16[704,2048]{1,0:T(8,128)(2,1)}, bf16[704,2048]{1,0:T(8,128)(2,1)S(1)}, u32[]{:S(2)}, u32[]{:S(2)}) collective-permute-start(bf16[704,2048]{1,0:T(8,128)(2,1)} %bitcast.25), channel_id=1, source_target_pairs={{0,1},{1,0},{2,3},{3,2},{4,5},{5,4},{6,7},{7,6},{8,9},{9,8},{10,11... | collective-permute-start | bytes 8650760 | tf_op jit(solution)/shard_map/ppermute | solution.py:29
  2.9 9.7 %collective-permute-start = (bf16[64,2048]{1,0:T(8,128)(2,1)}, bf16[64,2048]{1,0:T(8,128)(2,1)S(1)}, u32[]{:S(2)}, u32[]{:S(2)}) collective-permute-start(bf16[64,2048]{1,0:T(8,128)(2,1)} %bitcast.29), channel_id=1, source_target_pairs={{0,2},{2,0},{1,3},{3,1},{4,6},{6,4},{5,7},{7,5},{8,10},{10,8},{9,1... | collective-permute-start | bytes 786440 | tf_op jit(solution)/shard_map/ppermute | solution.py:29
  15.1 9.8 %collective-permute-start.6 = (bf16[352,2048]{1,0:T(8,128)(2,1)}, bf16[352,2048]{1,0:T(8,128)(2,1)}, u32[]{:S(2)}, u32[]{:S(2)}) collective-permute-start(bf16[352,2048]{1,0:T(8,128)(2,1)} %bitcast.39), channel_id=1, source_target_pairs={{0,1},{1,0},{2,3},{3,2},{4,5},{5,4},{6,7},{7,6},{8,9},{9,8},{10,11... | collective-permute-start | bytes 4325384 | tf_op jit(solution)/shard_map/ppermute | solution.py:29
  15.2 9.6 %collective-permute-start.7 = (bf16[352,2048]{1,0:T(8,128)(2,1)}, bf16[352,2048]{1,0:T(8,128)(2,1)}, u32[]{:S(2)}, u32[]{:S(2)}) collective-permute-start(bf16[352,2048]{1,0:T(8,128)(2,1)} %refs_4_.1), channel_id=1, source_target_pairs={{0,1},{1,0},{2,3},{3,2},{4,5},{5,4},{6,7},{7,6},{8,9},{9,8},{10,11... | collective-permute-start | bytes 4325384 | tf_op jit(solution)/shard_map/ppermute | solution.py:29
  26.5 11.0 %collective-permute-start.9 = (bf16[2048,1408]{1,0:T(8,128)(2,1)}, bf16[2048,1408]{1,0:T(8,128)(2,1)}, u32[]{:S(2)}, u32[]{:S(2)}) collective-permute-start(bf16[2048,1408]{1,0:T(8,128)(2,1)} %bitcast.22), channel_id=1, source_target_pairs={{0,1},{1,0},{2,3},{3,2},{4,5},{5,4},{6,7},{7,6},{8,9},{9,8},{10,11... | collective-permute-start | bytes 17301512 | tf_op jit(solution)/shard_map/ppermute | solution.py:29
  27.7 8.6 %collective-permute-start.8 = (bf16[64,2048]{1,0:T(8,128)(2,1)S(1)}, bf16[64,2048]{1,0:T(8,128)(2,1)S(1)}, u32[]{:S(2)}, u32[]{:S(2)}) collective-permute-start(bf16[64,2048]{1,0:T(8,128)(2,1)S(1)} %add.35), channel_id=1, source_target_pairs={{0,2},{2,0},{1,3},{3,1},{4,6},{6,4},{5,7},{7,5},{8,10},{10,8},{9,1... | collective-permute-start | bytes 786440 | tf_op jit(solution)/shard_map/ppermute | solution.py:29
  40.0 11.4 %collective-permute-start.11 = (bf16[64,2176]{1,0:T(8,128)(2,1)}, bf16[64,2176]{1,0:T(8,128)(2,1)S(1)}, u32[]{:S(2)}, u32[]{:S(2)}) collective-permute-start(bf16[64,2176]{1,0:T(8,128)(2,1)} %get-tuple-element.135.refs_2_), channel_id=1, source_target_pairs={{0,2},{2,0},{1,3},{3,1},{4,6},{6,4},{5,7},{7,5},{8,10},{10,8},{9,1... | collective-permute-start | bytes 835592 | tf_op jit(solution)/shard_map/ppermute | solution.py:29
  41.2 25.7 %collective-permute-start.12 = (bf16[64,2176]{1,0:T(8,128)(2,1)}, bf16[64,2176]{1,0:T(8,128)(2,1)}, u32[]{:S(2)}, u32[]{:S(2)}) collective-permute-start(bf16[64,2176]{1,0:T(8,128)(2,1)} %get-tuple-element.135.refs_2_), channel_id=1, source_target_pairs={{0,24},{8,16},{16,8},{24,0},{1,25},{9,17},{17,9},{25,1},{2,26},{10... | collective-permute-start | bytes 835592 | tf_op jit(solution)/shard_map/ppermute | solution.py:29
  45.7 26.6 %collective-permute-start.15 = (bf16[64,2176]{1,0:T(8,128)(2,1)}, bf16[64,2176]{1,0:T(8,128)(2,1)}, u32[]{:S(2)}, u32[]{:S(2)}) collective-permute-start(bf16[64,2176]{1,0:T(8,128)(2,1)} %get-tuple-element.135.refs_2_), channel_id=1, source_target_pairs={{0,16},{8,24},{16,0},{24,8},{1,17},{9,25},{17,1},{25,9},{2,18},{10... | collective-permute-start | bytes 835592 | tf_op jit(solution)/shard_map/ppermute | solution.py:29
  48.7 23.5 %collective-permute-start.16 = (bf16[64,2176]{1,0:T(8,128)(2,1)}, bf16[64,2176]{1,0:T(8,128)(2,1)}, u32[]{:S(2)}, u32[]{:S(2)}) collective-permute-start(bf16[64,2176]{1,0:T(8,128)(2,1)} %get-tuple-element.135.refs_2_), channel_id=1, source_target_pairs={{0,8},{8,0},{16,24},{24,16},{1,9},{9,1},{17,25},{25,17},{2,10},{10... | collective-permute-start | bytes 835592 | tf_op jit(solution)/shard_map/ppermute | solution.py:29
  51.4 15.6 %collective-permute-start.13 = (bf16[32,2048]{1,0:T(8,128)(2,1)}, bf16[32,2048]{1,0:T(8,128)(2,1)S(1)}, u32[]{:S(2)}, u32[]{:S(2)}) collective-permute-start(bf16[32,2048]{1,0:T(8,128)(2,1)} %get-tuple-element.146), channel_id=1, source_target_pairs={{0,4},{2,6},{4,0},{6,2},{1,5},{3,7},{5,1},{7,3},{8,12},{10,14},{12... | collective-permute-start | bytes 393224 | tf_op jit(solution)/shard_map/ppermute | solution.py:29
  56.1 10.9 %collective-permute-start.14 = (bf16[32,2048]{1,0:T(8,128)(2,1)S(1)}, bf16[32,2048]{1,0:T(8,128)(2,1)S(1)}, u32[]{:S(2)}, u32[]{:S(2)}) collective-permute-start(bf16[32,2048]{1,0:T(8,128)(2,1)S(1)} %get-tuple-element.147), channel_id=1, source_target_pairs={{0,6},{2,4},{4,2},{6,0},{1,7},{3,5},{5,3},{7,1},{8,14},{10,12},{12... | collective-permute-start | bytes 393224 | tf_op jit(solution)/shard_map/ppermute | solution.py:29
  68.7 9.3 %collective-permute-start.17 = (bf16[32,2048]{1,0:T(8,128)(2,1)S(1)}, bf16[32,2048]{1,0:T(8,128)(2,1)S(1)}, u32[]{:S(2)}, u32[]{:S(2)}) collective-permute-start(bf16[32,2048]{1,0:T(8,128)(2,1)S(1)} %get-tuple-element.155), channel_id=1, source_target_pairs={{0,2},{2,0},{4,6},{6,4},{1,3},{3,1},{5,7},{7,5},{8,10},{10,8},{12,... | collective-permute-start | bytes 393224 | tf_op jit(solution)/shard_map/ppermute | solution.py:29
  70.2 7.8 %collective-permute-start.18 = (bf16[32,2048]{1,0:T(8,128)(2,1)S(1)}, bf16[32,2048]{1,0:T(8,128)(2,1)S(1)}, u32[]{:S(2)}, u32[]{:S(2)}) collective-permute-start(bf16[32,2048]{1,0:T(8,128)(2,1)S(1)} %get-tuple-element.157), channel_id=1, source_target_pairs={{0,4},{2,6},{4,0},{6,2},{1,5},{3,7},{5,1},{7,3},{8,12},{10,14},{12... | collective-permute-start | bytes 393224 | tf_op jit(solution)/shard_map/ppermute | solution.py:29
  74.4 22.5 %collective-permute-start.20 = (bf16[64,2048]{1,0:T(8,128)(2,1)S(1)}, bf16[64,2048]{1,0:T(8,128)(2,1)S(1)}, u32[]{:S(2)}, u32[]{:S(2)}) collective-permute-start(bf16[64,2048]{1,0:T(8,128)(2,1)S(1)} %get-tuple-element.174), channel_id=1, source_target_pairs={{0,2},{2,0},{4,6},{6,4},{1,3},{3,1},{5,7},{7,5},{8,10},{10,8},{12,... | collective-permute-start | bytes 786440 | tf_op jit(solution)/shard_map/ppermute | solution.py:29
  76.0 22.5 %collective-permute-start.21 = (bf16[64,2048]{1,0:T(8,128)(2,1)S(1)}, bf16[64,2048]{1,0:T(8,128)(2,1)S(1)}, u32[]{:S(2)}, u32[]{:S(2)}) collective-permute-start(bf16[64,2048]{1,0:T(8,128)(2,1)S(1)} %get-tuple-element.175), channel_id=1, source_target_pairs={{0,4},{2,6},{4,0},{6,2},{1,5},{3,7},{5,1},{7,3},{8,12},{10,14},{12... | collective-permute-start | bytes 786440 | tf_op jit(solution)/shard_map/ppermute | solution.py:29
  78.2 21.7 %collective-permute-start.22 = (bf16[64,2048]{1,0:T(8,128)(2,1)S(1)}, bf16[64,2048]{1,0:T(8,128)(2,1)S(1)}, u32[]{:S(2)}, u32[]{:S(2)}) collective-permute-start(bf16[64,2048]{1,0:T(8,128)(2,1)S(1)} %get-tuple-element.176), channel_id=1, source_target_pairs={{0,6},{2,4},{4,2},{6,0},{1,7},{3,5},{5,3},{7,1},{8,14},{10,12},{12... | collective-permute-start | bytes 786440 | tf_op jit(solution)/shard_map/ppermute | solution.py:29
  79.3 20.6 %collective-permute-start.23 = (bf16[64,2048]{1,0:T(8,128)(2,1)}, bf16[64,2048]{1,0:T(8,128)(2,1)S(1)}, u32[]{:S(2)}, u32[]{:S(2)}) collective-permute-start(bf16[64,2048]{1,0:T(8,128)(2,1)} %get-tuple-element.181), channel_id=1, source_target_pairs={{0,2},{2,0},{1,3},{3,1},{4,6},{6,4},{5,7},{7,5},{8,10},{10,8},{9,1... | collective-permute-start | bytes 786440 | tf_op jit(solution)/shard_map/ppermute | solution.py:29
  96.4 13.4 %collective-permute-start.27 = (bf16[32,2048]{1,0:T(8,128)(2,1)S(1)}, bf16[32,2048]{1,0:T(8,128)(2,1)S(1)}, u32[]{:S(2)}, u32[]{:S(2)}) collective-permute-start(bf16[32,2048]{1,0:T(8,128)(2,1)S(1)} %get-tuple-element.178), channel_id=1, source_target_pairs={{0,2},{2,0},{4,6},{6,4},{1,3},{3,1},{5,7},{7,5},{8,10},{10,8},{12,... | collective-permute-start | bytes 393224 | tf_op jit(solution)/shard_map/ppermute | solution.py:29
  97.0 12.9 %collective-permute-start.28 = (bf16[32,2048]{1,0:T(8,128)(2,1)S(1)}, bf16[32,2048]{1,0:T(8,128)(2,1)S(1)}, u32[]{:S(2)}, u32[]{:S(2)}) collective-permute-start(bf16[32,2048]{1,0:T(8,128)(2,1)S(1)} %get-tuple-element.179), channel_id=1, source_target_pairs={{0,4},{2,6},{4,0},{6,2},{1,5},{3,7},{5,1},{7,3},{8,12},{10,14},{12... | collective-permute-start | bytes 393224 | tf_op jit(solution)/shard_map/ppermute | solution.py:29
  98.5 11.4 %collective-permute-start.29 = (bf16[32,2048]{1,0:T(8,128)(2,1)S(1)}, bf16[32,2048]{1,0:T(8,128)(2,1)S(1)}, u32[]{:S(2)}, u32[]{:S(2)}) collective-permute-start(bf16[32,2048]{1,0:T(8,128)(2,1)S(1)} %get-tuple-element.180), channel_id=1, source_target_pairs={{0,6},{2,4},{4,2},{6,0},{1,7},{3,5},{5,3},{7,1},{8,14},{10,12},{12... | collective-permute-start | bytes 393224 | tf_op jit(solution)/shard_map/ppermute | solution.py:29
  107.7 6.4 %collective-permute-start.24 = (bf16[32,2048]{1,0:T(8,128)(2,1)S(1)}, bf16[32,2048]{1,0:T(8,128)(2,1)S(1)}, u32[]{:S(2)}, u32[]{:S(2)}) collective-permute-start(bf16[32,2048]{1,0:T(8,128)(2,1)S(1)} %get-tuple-element.187), channel_id=1, source_target_pairs={{0,2},{2,0},{4,6},{6,4},{1,3},{3,1},{5,7},{7,5},{8,10},{10,8},{12,... | collective-permute-start | bytes 393224 | tf_op jit(solution)/shard_map/ppermute | solution.py:29
  108.3 7.5 %collective-permute-start.25 = (bf16[32,2048]{1,0:T(8,128)(2,1)S(1)}, bf16[32,2048]{1,0:T(8,128)(2,1)S(1)}, u32[]{:S(2)}, u32[]{:S(2)}) collective-permute-start(bf16[32,2048]{1,0:T(8,128)(2,1)S(1)} %get-tuple-element.188), channel_id=1, source_target_pairs={{0,4},{2,6},{4,0},{6,2},{1,5},{3,7},{5,1},{7,3},{8,12},{10,14},{12... | collective-permute-start | bytes 393224 | tf_op jit(solution)/shard_map/ppermute | solution.py:29
  110.1 13.9 %collective-permute-start.30 = (bf16[64,2048]{1,0:T(8,128)(2,1)S(1)}, bf16[64,2048]{1,0:T(8,128)(2,1)S(1)}, u32[]{:S(2)}, u32[]{:S(2)}) collective-permute-start(bf16[64,2048]{1,0:T(8,128)(2,1)S(1)} %combine.5), channel_id=1, source_target_pairs={{0,24},{8,16},{16,8},{24,0},{1,25},{9,17},{17,9},{25,1},{2,26},{10... | collective-permute-start | bytes 786440 | tf_op jit(solution)/shard_map/ppermute | solution.py:29
  111.4 7.4 %collective-permute-start.26 = (bf16[32,2048]{1,0:T(8,128)(2,1)S(1)}, bf16[32,2048]{1,0:T(8,128)(2,1)S(1)}, u32[]{:S(2)}, u32[]{:S(2)}) collective-permute-start(bf16[32,2048]{1,0:T(8,128)(2,1)S(1)} %get-tuple-element.189), channel_id=1, source_target_pairs={{0,6},{2,4},{4,2},{6,0},{1,7},{3,5},{5,3},{7,1},{8,14},{10,12},{12... | collective-permute-start | bytes 393224 | tf_op jit(solution)/shard_map/ppermute | solution.py:29
  112.5 7.0 %collective-permute-start.35 = (bf16[32,2048]{1,0:T(8,128)(2,1)S(1)}, bf16[32,2048]{1,0:T(8,128)(2,1)S(1)}, u32[]{:S(2)}, u32[]{:S(2)}) collective-permute-start(bf16[32,2048]{1,0:T(8,128)(2,1)S(1)} %get-tuple-element.207), channel_id=1, source_target_pairs={{0,2},{2,0},{4,6},{6,4},{1,3},{3,1},{5,7},{7,5},{8,10},{10,8},{12,... | collective-permute-start | bytes 393224 | tf_op jit(solution)/shard_map/ppermute | solution.py:29
  114.1 6.2 %collective-permute-start.36 = (bf16[32,2048]{1,0:T(8,128)(2,1)S(1)}, bf16[32,2048]{1,0:T(8,128)(2,1)S(1)}, u32[]{:S(2)}, u32[]{:S(2)}) collective-permute-start(bf16[32,2048]{1,0:T(8,128)(2,1)S(1)} %get-tuple-element.208), channel_id=1, source_target_pairs={{0,4},{2,6},{4,0},{6,2},{1,5},{3,7},{5,1},{7,3},{8,12},{10,14},{12... | collective-permute-start | bytes 393224 | tf_op jit(solution)/shard_map/ppermute | solution.py:29
  119.0 15.7 %collective-permute-start.34 = (bf16[64,2048]{1,0:T(8,128)(2,1)S(1)}, bf16[64,2048]{1,0:T(8,128)(2,1)S(1)}, u32[]{:S(2)}, u32[]{:S(2)}) collective-permute-start(bf16[64,2048]{1,0:T(8,128)(2,1)S(1)} %combine.4), channel_id=1, source_target_pairs={{0,16},{8,24},{16,0},{24,8},{1,17},{9,25},{17,1},{25,9},{2,18},{10... | collective-permute-start | bytes 786440 | tf_op jit(solution)/shard_map/ppermute | solution.py:29
  122.0 12.7 %collective-permute-start.38 = (bf16[64,2048]{1,0:T(8,128)(2,1)S(1)}, bf16[64,2048]{1,0:T(8,128)(2,1)S(1)}, u32[]{:S(2)}, u32[]{:S(2)}) collective-permute-start(bf16[64,2048]{1,0:T(8,128)(2,1)S(1)} %combine.7), channel_id=1, source_target_pairs={{0,8},{8,0},{16,24},{24,16},{1,9},{9,1},{17,25},{25,17},{2,10},{10... | collective-permute-start | bytes 786440 | tf_op jit(solution)/shard_map/ppermute | solution.py:29
  124.0 7.0 %collective-permute-start.31 = (bf16[32,2048]{1,0:T(8,128)(2,1)S(1)}, bf16[32,2048]{1,0:T(8,128)(2,1)S(1)}, u32[]{:S(2)}, u32[]{:S(2)}) collective-permute-start(bf16[32,2048]{1,0:T(8,128)(2,1)S(1)} %copy-done.33), channel_id=1, source_target_pairs={{0,2},{2,0},{4,6},{6,4},{1,3},{3,1},{5,7},{7,5},{8,10},{10,8},{12,... | collective-permute-start | bytes 393224 | tf_op jit(solution)/shard_map/ppermute | solution.py:29
  128.1 6.4 %collective-permute-start.32 = (bf16[32,2048]{1,0:T(8,128)(2,1)S(1)}, bf16[32,2048]{1,0:T(8,128)(2,1)S(1)}, u32[]{:S(2)}, u32[]{:S(2)}) collective-permute-start(bf16[32,2048]{1,0:T(8,128)(2,1)S(1)} %copy-done.31), channel_id=1, source_target_pairs={{0,4},{2,6},{4,0},{6,2},{1,5},{3,7},{5,1},{7,3},{8,12},{10,14},{12... | collective-permute-start | bytes 393224 | tf_op jit(solution)/shard_map/ppermute | solution.py:29
  128.1 6.4 %collective-permute-start.33 = (bf16[32,2048]{1,0:T(8,128)(2,1)S(1)}, bf16[32,2048]{1,0:T(8,128)(2,1)S(1)}, u32[]{:S(2)}, u32[]{:S(2)}) collective-permute-start(bf16[32,2048]{1,0:T(8,128)(2,1)S(1)} %copy-done.29), channel_id=1, source_target_pairs={{0,6},{2,4},{4,2},{6,0},{1,7},{3,5},{5,3},{7,1},{8,14},{10,12},{12... | collective-permute-start | bytes 393224 | tf_op jit(solution)/shard_map/ppermute | solution.py:29
  (52 other events, 596.8 us)

commit v13 on v11

--- a/solution.py
+++ b/solution.py
@@ -116,67 +116,68 @@
     cache_copies[1].start()
     projected = projected + dot(normed[:, deep:], weight_here[deep:])
     scale = 1.0 / math.sqrt(head_dim)
-    results = []
-
-    for i in range(2):
+    outward_copy.start()
+
+    def rope(values, request):
+        return values * cosine[request] + pltpu.roll(values, head_dim // 2, 1) * sine[request]
+
+    def against(query, keys):
+        return (
+            lax.dot_general(
+                query, keys, (((1,), (1,)), ((), ())), preferred_element_type=jnp.float32
+            )
+            * scale
+        )
+
+    requests = [place[0] ^ (offset + i) for i in range(2)]
+    bounds = [lengths[request] for request in requests]
+    queries = []
+    states = []
+    for i, request in enumerate(requests):
         own = projected[i * tree : (i + 1) * tree]
-        request = place[0] ^ (offset + i)
-        length = lengths[request]
-
-        def rope(values):
-            return values * cosine[request] + pltpu.roll(values, head_dim // 2, 1) * sine[request]
-
-        def column(c):
-            return own[:, c * head_dim : (c + 1) * head_dim]
-
+        columns_of = [own[:, c * head_dim : (c + 1) * head_dim] for c in range(group + 2)]
         query = jnp.concatenate(
-            [rope(column(h)).astype(jnp.bfloat16) for h in range(group)], axis=0
-        )
-        key_new = rope(column(group)).astype(jnp.bfloat16)
-        value_new = column(group + 1).astype(jnp.bfloat16)
+            [rope(columns_of[h], request).astype(jnp.bfloat16) for h in range(group)], axis=0
+        )
+        key_new = rope(columns_of[group], request).astype(jnp.bfloat16)
+        value_new = columns_of[group + 1].astype(jnp.bfloat16)
         fresh[i][:, :head_dim] = key_new
         fresh[i][:, head_dim:] = value_new
-
-        def against(keys):
-            return (
-                lax.dot_general(
-                    query, keys, (((1,), (1,)), ((), ())), preferred_element_type=jnp.float32
-                )
-                * scale
-            )
-
         allowed = jnp.concatenate([reach[request]] * group, axis=0) > 0.5
-        scores = jnp.where(allowed, against(key_new), -1e30)
+        scores = jnp.where(allowed, against(query, key_new), -1e30)
         peak = jnp.max(scores, axis=-1, keepdims=True)
         weights = jnp.exp(scores - peak)
         total = jnp.sum(weights, axis=-1, keepdims=True)
         summed = dot(weights.astype(jnp.bfloat16), value_new)
-        cache_copies[i].wait()
-        if i == 0:
-            outward_copy.start()
-
-        def chunk(j, carry):
-            peak, total, summed = carry
-            block = pl.ds(pl.multiple_of(j * CHUNK, CHUNK), CHUNK)
-            scores = against(cache_here[i, block, :head_dim])
-            place = j * CHUNK + lax.broadcasted_iota(jnp.int32, scores.shape, 1)
-            scores = jnp.where(place < length, scores, -1e30)
+        queries.append(query)
+        states.append((peak, total, summed))
+    for copy in cache_copies:
+        copy.wait()
+
+    def chunk(j, states):
+        block = pl.ds(pl.multiple_of(j * CHUNK, CHUNK), CHUNK)
+        later = []
+        for i, (peak, total, summed) in enumerate(states):
+            scores = against(queries[i], cache_here[i, block, :head_dim])
+            slot = j * CHUNK + lax.broadcasted_iota(jnp.int32, scores.shape, 1)
+            scores = jnp.where(slot < bounds[i], scores, -1e30)
             higher = jnp.maximum(peak, jnp.max(scores, axis=-1, keepdims=True))
             fade = jnp.exp(peak - higher)
             weights = jnp.exp(scores - higher)
             total = total * fade + jnp.sum(weights, axis=-1, keepdims=True)
             values = cache_here[i, block, head_dim:]
             summed = summed * fade + dot(weights.astype(jnp.bfloat16), values)
-            return (higher, total, summed)
-
-        peak, total, summed = lax.fori_loop(
-            0, lax.div(length + CHUNK - 1, CHUNK), chunk, (peak, total, summed)
-        )
+            later.append((higher, total, summed))
+        return tuple(later)
+
+    longest = jnp.maximum(bounds[0], bounds[1])
+    states = lax.fori_loop(0, lax.div(longest + CHUNK - 1, CHUNK), chunk, tuple(states))
+    results = []
+    for peak, total, summed in states:
         result = (summed / total).astype(jnp.bfloat16)
-        result = jnp.concatenate(
-            [result[h * tree : (h + 1) * tree] for h in range(group)], axis=1
-        )
-        results.append(result)
+        results.append(
+            jnp.concatenate([result[h * tree : (h + 1) * tree] for h in range(group)], axis=1)
+        )
     outward_copy.wait()
     terms = dot(jnp.concatenate(results, axis=0), outward_here[...])
     term[...] = terms[:tree]
@@ -235,23 +236,6 @@
     )(place, lengths, first, second, gain, weight, cosine, sine, reach, cache, outward)
 
 
-def add_kernel(left, right, out):
-    total = left[...].astype(jnp.float32) + right[...].astype(jnp.float32)
-    out[...] = total.astype(out.dtype)
-
-
-def add(left, right, dtype):
-    return pl.pallas_call(
-        add_kernel,
-        in_specs=[in_vmem()] * 2,
-        out_specs=in_vmem(),
-        out_shape=jax.ShapeDtypeStruct(left.shape, dtype),
-        compiler_params=pltpu.CompilerParams(vmem_limit_bytes=16 * 2**20),
-        cost_estimate=SMALL,
-        name="add",
-    )(left, right)
-
-
 def silu(values):
     return values / (1.0 + jnp.exp(-values))
 
@@ -306,7 +290,7 @@
         outs[n][...] = result[base : base + step]
 
 
-def experts(pieces, count, inner, outer):
+def experts(pieces, count, inner, outer, room):
     plane = len(pieces)
     each, width = pieces[0].shape
     hidden = inner[0].shape[1]
@@ -329,7 +313,7 @@
             pltpu.VMEM((rows, width), jnp.bfloat16),
             pltpu.SemaphoreType.DMA((2 * (len(tiles) + 1),)),
         ],
-        compiler_params=pltpu.CompilerParams(vmem_limit_bytes=60 * 2**20),
+        compiler_params=pltpu.CompilerParams(vmem_limit_bytes=room * 2**20),
         cost_estimate=SMALL,
         name="expert",
     )(*pieces, inner[0], outer[0], inner[1], outer[1])
@@ -609,11 +593,10 @@
             other, middle, late = lax.optimization_barrier((other, middle, late))
             late = partner(late, "c", 1)
         if o:
-            follow = add(own_part, other, jnp.bfloat16)
-            terms[o] = partner(follow, "x", o)
-    own_term = own_part
-    for o in range(1, side):
-        own_term = add(own_term, terms[o], jnp.float32)
+            follow = (own_part + other.astype(jnp.float32)).astype(jnp.bfloat16)
+            crossed = partner(follow, "x", o).astype(jnp.float32)
+            terms[o] = crossed if o == side - 1 else crossed + terms[o + 1]
+    own_term = own_part + terms[1] if side > 1 else own_part
     own_term, late = lax.optimization_barrier((own_term, late))
     others = [other]
     resid, normed, payload = finish(own_rows, own_term, others, ffn_gain[None], routes[0])
@@ -637,11 +620,11 @@
     near_experts = lax.axis_index("z") * plane + (
         lax.axis_index(PLANE) ^ jnp.arange(plane, dtype=jnp.int32)
     )
+    line_rows = [payload] + [partner(payload, "z", k) for k in range(1, line)]
     beside = [partner(normed, "x", o) for o in range(1, side)]
-    calm, beside = lax.optimization_barrier((payload, beside))
-    line_rows = [payload] + [
-        partner(payload if k in GROUPS[0] else calm, "z", k) for k in range(1, line)
-    ]
+
+    shared, beside = shared_terms(normed, beside, shared_weights)
+    line_rows[3], beside = lax.optimization_barrier((line_rows[3], beside))
 
     sent = []
     spread = {}
@@ -651,18 +634,13 @@
         )
         spread.update(zip(ks, spreads))
         sent.append([partner(pieces[o], PLANE, o) for o in range(plane)])
-        if len(sent) == 1:
-            normed, spread[ks[0]] = lax.optimization_barrier((normed, spread[ks[0]]))
-            shared, beside = shared_terms(
-                normed, beside, [gate_turned, up_turned, shared_down, early[0], *middle]
-            )
     parts = [partner(beside[o - 1], "x", o) for o in range(1, side)]
     made = None
     results = {}
     for ks, pieces in zip(GROUPS, sent):
         if made is not None:
             pieces, made, parts = lax.optimization_barrier((pieces, made, parts))
-        made = experts(pieces, len(ks), inner, outer)
+        made = experts(pieces, len(ks), inner, outer, 40 if results else 60)
         results.update(zip(ks, made))
     totals = {}
     landed = {}

time: 138 us -> 139 us (level); the launches traced: 135 us -> 139 us
  starting transfers between devices: 46.7 us -> 51.8 us
  Pallas kernels: 52.1 us -> 49.4 us
  other arithmetic: 0.02 us -> 2.22 us
  waiting for transfers between devices: 22.3 us -> 20.2 us
    ppermute x37, starting transfers between devices: 46.7 us -> 51.8 us  [partner(): return lax.ppermute(value, axes, [(i, i ^ offset) for i in range(size)])]
    pallas_call x2, Pallas kernels: 20.7 us -> 17.5 us  [experts(): pl.pallas_call(functools.partial(expert_kernel, plane=plane, count=count,...]
    ppermute x37, waiting for transfers between devices: 22.3 us -> 20.2 us  [partner(): return lax.ppermute(value, axes, [(i, i ^ offset) for i in range(size)])]
    unnamed x80 -> x78, local copies, waits for them, and re-layouts: 11.1 us -> 12 us
  transfers between devices with their start and end apart: 37 -> 37, of which waited for: 12 -> 15; matrix products, arithmetic and copies ran while one was open for 2% -> 3% of each run, Pallas kernels for 37% -> 34%
where the time goes in v13:
time: 139 us
  starting transfers between devices  51.8 us (37%)
  Pallas kernels  49.4 us (36%)
  waiting for transfers between devices  20.2 us (15%)
  local copies, waits for them, and re-layouts  13.9 us (10%)
  other arithmetic  2.22 us (2%)
    ppermute x37, starting transfers between devices, partner(): return lax.ppermute(value, axes, [(i, i ^ offset) for i in range(size)])  51.8 us
    ppermute x37, waiting for transfers between devices, partner(): return lax.ppermute(value, axes, [(i, i ^ offset) for i in range(size)])  20.2 us
    pallas_call x2, Pallas kernels, experts(): pl.pallas_call(functools.partial(expert_kernel, plane=plane, count=count,...  17.5 us
    pallas_call x2, Pallas kernels, attend(): pl.pallas_call(functools.partial(attend_kernel, offset=offset), in_specs=...  14.5 us
    unnamed x78, local copies, waits for them, and re-layouts  12 us
    pallas_call x1, Pallas kernels, shared_terms(): pl.pallas_call(functools.partial(shared_kernel, side=side), in_specs=[in_...  8.2 us
    pallas_call x2, Pallas kernels, select(): pl.pallas_call(functools.partial(select_kernel, count=count, plane=plane,...  4.17 us
  transfers between devices with their start and end apart: 37, of which 15 were waited for; matrix products, arithmetic and copies ran while one was open for 3% of the time, Pallas kernels for 34%

profile of v13, /device:TPU:0, one launch (start us, length us, event | category | flops | bytes accessed | tf_op | source)
XLA Modules:
  0.0 138.8 jit_solution(4987360860814929657)
XLA Ops:
  1.2 1.4 collective-permute-done.1.second
  2.9 2.6 %collective-permute-start = (bf16[64,2048]{1,0:T(8,128)(2,1)}, bf16[64,2048]{1,0:T(8,128)(2,1)S(1)}, u32[]{:S(2)}, u32[]{:S(2)}) collective-permute-start(bf16[64,2048]{1,0:T(8,128)(2,1)} %bitcast.28), channel_id=1, source_target_pairs={{0,2},{2,0},{1,3},{3,1},{4,6},{6,4},{5,7},{7,5},{8,10},{10,8},{9,1... | collective-permute-start | bytes 786440 | tf_op jit(solution)/shard_map/ppermute | solution.py:29
  7.5 2.0 %prepare.1 = (f32[4,64,64]{2,1,0:T(8,128)S(1)}, f32[4,64,128]{2,1,0:T(8,128)S(1)}, f32[4,64,128]{2,1,0:T(8,128)S(1)}) custom-call(s32[4]{0:T(128)S(1)} %copy-done.17, s32[4,64]{1,0:T(4,128)S(1)} %copy-done.18, f32[1,128]{1,0:T(1,128)S(1)} %copy-done.19), custom_call_target="tpu_custom_call" | custom-call | flops 1024 | bytes 1024 | tf_op jit(solution)/shard_map/prepare/pallas_call | solution.py:68
  12.6 2.5 %collective-permute-done.2.second = bf16[64,2048]{1,0:T(8,128)(2,1)S(1)} collective-permute-done((bf16[64,2048]{1,0:T(8,128)(2,1)S(1)}, bf16[64,2048]{1,0:T(8,128)(2,1)S(1)}, u32[]{:S(2)}, u32[]{:S(2)}) %collective-permute-start.2) | collective-permute-done | bytes 262176 | tf_op jit(solution)/shard_map/ppermute | solution.py:29
  16.7 7.5 %attend.2 = (f32[64,2048]{1,0:T(8,128)}, bf16[64,2048]{1,0:T(8,128)(2,1)}, bf16[64,256]{1,0:T(8,128)(2,1)}, bf16[64,256]{1,0:T(8,128)(2,1)}) custom-call(s32[1]{0:T(128)} %bitcast.2.place, s32[4]{0:T(128)} %lengths.5, bf16[64,2048]{1,0:T(8,128)(2,1)} %copy-done.25, bf16[64,2048]{1,0:T(8,128)(2,1)} %copy-done.27, f32[1,2048]{1,0:T(1,128)} %bitcast.40, ...), custom_call_target="tpu_custom_call" | custom-call | flops 1024 | bytes 1024 | tf_op jit(solution)/shard_map/attend/pallas_call | solution.py:205
  24.4 1.6 %collective-permute-done.5 = bf16[64,2048]{1,0:T(8,128)(2,1)S(1)} collective-permute-done((bf16[64,2048]{1,0:T(8,128)(2,1)}, bf16[64,2048]{1,0:T(8,128)(2,1)S(1)}, u32[]{:S(2)}, u32[]{:S(2)}) %collective-permute-start.5) | collective-permute-done | bytes 262176 | tf_op jit(solution)/shard_map/ppermute | solution.py:29
  28.3 7.0 %attend.3 = (f32[64,2048]{1,0:T(8,128)}, bf16[64,2048]{1,0:T(8,128)(2,1)}, bf16[64,256]{1,0:T(8,128)(2,1)}, bf16[64,256]{1,0:T(8,128)(2,1)}) custom-call(s32[1]{0:T(128)} %bitcast.2.place, s32[4]{0:T(128)} %lengths.5, bf16[64,2048]{1,0:T(8,128)(2,1)} %bitcast.29, bf16[64,2048]{1,0:T(8,128)(2,1)} %copy-done.24, f32[1,2048]{1,0:T(1,128)} %bitcast.41, ...), custom_call_target="tpu_custom_call" | custom-call | flops 1024 | bytes 1024 | tf_op jit(solution)/shard_map/attend/pallas_call | solution.py:205
  38.1 5.2 %collective-permute-start.12 = (bf16[64,2176]{1,0:T(8,128)(2,1)S(1)}, bf16[64,2176]{1,0:T(8,128)(2,1)S(1)}, u32[]{:S(2)}, u32[]{:S(2)}) collective-permute-start(bf16[64,2176]{1,0:T(8,128)(2,1)S(1)} %get-tuple-element.120.refs_2_), channel_id=1, source_target_pairs={{0,24},{8,16},{16,8},{24,0},{1,25},{9,17},{17,9},{25,1},{2,26},{10... | collective-permute-start | bytes 835592 | tf_op jit(solution)/shard_map/ppermute | solution.py:29
  43.3 3.0 %collective-permute-start.11 = (bf16[64,2048]{1,0:T(8,128)(2,1)S(1)}, bf16[64,2048]{1,0:T(8,128)(2,1)S(1)}, u32[]{:S(2)}, u32[]{:S(2)}) collective-permute-start(bf16[64,2048]{1,0:T(8,128)(2,1)S(1)} %get-tuple-element.115.refs_0_), channel_id=1, source_target_pairs={{0,2},{2,0},{1,3},{3,1},{4,6},{6,4},{5,7},{7,5},{8,10},{10,8},{9,1... | collective-permute-start | bytes 786440 | tf_op jit(solution)/shard_map/ppermute | solution.py:29
  47.7 4.9 %collective-permute-done.11.refs_1_ = bf16[64,2048]{1,0:T(8,128)(2,1)S(1)} collective-permute-done((bf16[64,2048]{1,0:T(8,128)(2,1)S(1)}, bf16[64,2048]{1,0:T(8,128)(2,1)S(1)}, u32[]{:S(2)}, u32[]{:S(2)}) %collective-permute-start.11) | collective-permute-done | bytes 262176 | tf_op jit(solution)/shard_map/ppermute | solution.py:29
  53.3 8.2 %shared.1 = (f32[64,2048]{1,0:T(8,128)}, bf16[64,2048]{1,0:T(8,128)(2,1)}) custom-call(bf16[64,2048]{1,0:T(8,128)(2,1)} %copy-done.11, bf16[64,2048]{1,0:T(8,128)(2,1)} %copy-done.26, bf16[352,2048]{1,0:T(8,128)(2,1)} %bitcast.36, bf16[352,2048]{1,0:T(8,128)(2,1)} %bitcast.38, bf16[352,2048]{1,0:T(8,128)(2,1)} %refs_4_.1, bf16[352,2048]{1,0:T(8,128)(2,1)} %copy-done.20, ...), custom_call_target="tpu_custom_call" | custom-call | flops 1024 | bytes 1024 | tf_op jit(solution)/shard_map/shared/pallas_call | solution.py:361
  61.5 1.6 %select.2 = (bf16[64,2048]{1,0:T(8,128)(2,1)S(1)}, bf16[64,2048]{1,0:T(8,128)(2,1)S(1)}, bf16[64,2048]{1,0:T(8,128)(2,1)S(1)}, bf16[64,2048]{1,0:T(8,128)(2,1)S(...) custom-call(s32[4]{0:T(128)S(1)} %xor_add_fusion.refs_0_, bf16[2048,16]{1,0:T(8,128)(2,1)S(1)} %copy.21.refs_1_, ...), custom_call_target="tpu_custom_call" | custom-call | flops 1024 | bytes 1024 | tf_op jit(solution)/shard_map/select/pallas_call | solution.py:468
  63.2 1.8 %collective-permute-start.13 = (bf16[64,2048]{1,0:T(8,128)(2,1)S(1)}, bf16[64,2048]{1,0:T(8,128)(2,1)S(1)}, u32[]{:S(2)}, u32[]{:S(2)}) collective-permute-start(bf16[64,2048]{1,0:T(8,128)(2,1)S(1)} %get-tuple-element.125), channel_id=1, source_target_pairs={{0,2},{2,0},{4,6},{6,4},{1,3},{3,1},{5,7},{7,5},{8,10},{10,8},{12,... | collective-permute-start | bytes 786440 | tf_op jit(solution)/shard_map/ppermute | solution.py:29
  65.0 2.3 %collective-permute-start.14 = (bf16[64,2048]{1,0:T(8,128)(2,1)S(1)}, bf16[64,2048]{1,0:T(8,128)(2,1)S(1)}, u32[]{:S(2)}, u32[]{:S(2)}) collective-permute-start(bf16[64,2048]{1,0:T(8,128)(2,1)S(1)} %get-tuple-element.126), channel_id=1, source_target_pairs={{0,4},{2,6},{4,0},{6,2},{1,5},{3,7},{5,1},{7,3},{8,12},{10,14},{12... | collective-permute-start | bytes 786440 | tf_op jit(solution)/shard_map/ppermute | solution.py:29
  68.5 2.5 %select.3 = (bf16[64,2048]{1,0:T(8,128)(2,1)S(1)}, bf16[64,2048]{1,0:T(8,128)(2,1)}, bf16[64,2048]{1,0:T(8,128)(2,1)}, bf16[64,2048]{1,0:T(8,128)(2,1)}, bf16[64...) custom-call(s32[4]{0:T(128)S(1)} %xor_add_fusion.refs_0_, bf16[2048,16]{1,0:T(8,128)(2,1)S(1)} %copy.21.refs_1_, ...), custom_call_target="tpu_custom_call" | custom-call | flops 1024 | bytes 1024 | tf_op jit(solution)/shard_map/select/pallas_call | solution.py:468
  71.0 2.6 %collective-permute-start.18 = (bf16[64,2048]{1,0:T(8,128)(2,1)}, bf16[64,2048]{1,0:T(8,128)(2,1)S(1)}, u32[]{:S(2)}, u32[]{:S(2)}) collective-permute-start(bf16[64,2048]{1,0:T(8,128)(2,1)} %get-tuple-element.136), channel_id=1, source_target_pairs={{0,2},{2,0},{4,6},{6,4},{1,3},{3,1},{5,7},{7,5},{8,10},{10,8},{12,... | collective-permute-start | bytes 786440 | tf_op jit(solution)/shard_map/ppermute | solution.py:29
  73.7 2.3 %collective-permute-start.20 = (bf16[64,2048]{1,0:T(8,128)(2,1)}, bf16[64,2048]{1,0:T(8,128)(2,1)S(1)}, u32[]{:S(2)}, u32[]{:S(2)}) collective-permute-start(bf16[64,2048]{1,0:T(8,128)(2,1)} %get-tuple-element.138), channel_id=1, source_target_pairs={{0,6},{2,4},{4,2},{6,0},{1,7},{3,5},{5,3},{7,1},{8,14},{10,12},{12... | collective-permute-start | bytes 786440 | tf_op jit(solution)/shard_map/ppermute | solution.py:29
  76.0 3.7 %collective-permute-done.14.refs_2_ = bf16[64,2048]{1,0:T(8,128)(2,1)S(1)} collective-permute-done((bf16[64,2048]{1,0:T(8,128)(2,1)S(1)}, bf16[64,2048]{1,0:T(8,128)(2,1)S(1)}, u32[]{:S(2)}, u32[]{:S(2)}) %collective-permute-start.14) | collective-permute-done | bytes 262176 | tf_op jit(solution)/shard_map/ppermute | solution.py:29
  82.0 10.4 %expert.2 = (bf16[32,2048]{1,0:T(8,128)(2,1)}, bf16[32,2048]{1,0:T(8,128)(2,1)}, bf16[32,2048]{1,0:T(8,128)(2,1)}, bf16[32,2048]{1,0:T(8,128)(2,1)}, bf16[32,204...) custom-call(bf16[64,2048]{1,0:T(8,128)(2,1)} %copy-done.10, ...), custom_call_target="tpu_custom_call" | custom-call | flops 1024 | bytes 1024 | tf_op jit(solution)/shard_map/expert/pallas_call | solution.py:303
  92.9 2.4 %collective-permute-start.26 = (bf16[32,2048]{1,0:T(8,128)(2,1)}, bf16[32,2048]{1,0:T(8,128)(2,1)S(1)}, u32[]{:S(2)}, u32[]{:S(2)}) collective-permute-start(bf16[32,2048]{1,0:T(8,128)(2,1)} %get-tuple-element.141), channel_id=1, source_target_pairs={{0,4},{2,6},{4,0},{6,2},{1,5},{3,7},{5,1},{7,3},{8,12},{10,14},{12... | collective-permute-start | bytes 393224 | tf_op jit(solution)/shard_map/ppermute | solution.py:29
  96.2 2.6 %copy-done.1 = bf16[1,2048,1408]{2,1,0:T(8,128)(2,1)S(1)} copy-done((bf16[1,2048,1408]{2,1,0:T(8,128)(2,1)S(1)}, bf16[1,2048,1408]{2,1,0:T(8,128)(2,1)}, u32[]{:S(2)}) %copy-start.1) | copy-done | bytes 5767192
  98.8 1.8 %copy-done.4 = bf16[704,2048]{1,0:T(8,128)(2,1)S(1)} copy-done((bf16[704,2048]{1,0:T(8,128)(2,1)S(1)}, bf16[704,2048]{1,0:T(8,128)(2,1)}, u32[]{:S(2)}) %copy-start.4) | copy-done | bytes 2883608
  100.6 7.1 %expert.3 = (bf16[32,2048]{1,0:T(8,128)(2,1)S(1)}, bf16[32,2048]{1,0:T(8,128)(2,1)S(1)}, bf16[32,2048]{1,0:T(8,128)(2,1)S(1)}, bf16[32,2048]{1,0:T(8,128)(2,1)S(...) custom-call(bf16[64,2048]{1,0:T(8,128)(2,1)S(1)} %get-tuple-element., ...), custom_call_target="tpu_custom_call" | custom-call | flops 1024 | bytes 1024 | tf_op jit(solution)/shard_map/expert/pallas_call | solution.py:303
  108.5 2.3 %collective-permute-start.23 = (bf16[32,2048]{1,0:T(8,128)(2,1)S(1)}, bf16[32,2048]{1,0:T(8,128)(2,1)S(1)}, u32[]{:S(2)}, u32[]{:S(2)}) collective-permute-start(bf16[32,2048]{1,0:T(8,128)(2,1)S(1)} %get-tuple-element.150), channel_id=1, source_target_pairs={{0,4},{2,6},{4,0},{6,2},{1,5},{3,7},{5,1},{7,3},{8,12},{10,14},{12... | collective-permute-start | bytes 393224 | tf_op jit(solution)/shard_map/ppermute | solution.py:29
  114.2 2.8 %collective-permute-start.34 = (bf16[32,2048]{1,0:T(8,128)(2,1)S(1)}, bf16[32,2048]{1,0:T(8,128)(2,1)S(1)}, u32[]{:S(2)}, u32[]{:S(2)}) collective-permute-start(bf16[32,2048]{1,0:T(8,128)(2,1)S(1)} %get-tuple-element.170), channel_id=1, source_target_pairs={{0,4},{2,6},{4,0},{6,2},{1,5},{3,7},{5,1},{7,3},{8,12},{10,14},{12... | collective-permute-start | bytes 393224 | tf_op jit(solution)/shard_map/ppermute | solution.py:29
  117.0 2.8 %collective-permute-start.35 = (bf16[32,2048]{1,0:T(8,128)(2,1)S(1)}, bf16[32,2048]{1,0:T(8,128)(2,1)S(1)}, u32[]{:S(2)}, u32[]{:S(2)}) collective-permute-start(bf16[32,2048]{1,0:T(8,128)(2,1)S(1)} %get-tuple-element.171), channel_id=1, source_target_pairs={{0,6},{2,4},{4,2},{6,0},{1,7},{3,5},{5,3},{7,1},{8,14},{10,12},{12... | collective-permute-start | bytes 393224 | tf_op jit(solution)/shard_map/ppermute | solution.py:29
  120.0 2.7 %collective-permute-start.32 = (bf16[64,2048]{1,0:T(8,128)(2,1)S(1)}, bf16[64,2048]{1,0:T(8,128)(2,1)S(1)}, u32[]{:S(2)}, u32[]{:S(2)}) collective-permute-start(bf16[64,2048]{1,0:T(8,128)(2,1)S(1)} %combine.4), channel_id=1, source_target_pairs={{0,16},{8,24},{16,0},{24,8},{1,17},{9,25},{17,1},{25,9},{2,18},{10... | collective-permute-start | bytes 786440 | tf_op jit(solution)/shard_map/ppermute | solution.py:29
  123.1 4.8 %collective-permute-start.36 = (bf16[64,2048]{1,0:T(8,128)(2,1)S(1)}, bf16[64,2048]{1,0:T(8,128)(2,1)S(1)}, u32[]{:S(2)}, u32[]{:S(2)}) collective-permute-start(bf16[64,2048]{1,0:T(8,128)(2,1)S(1)} %combine.7), channel_id=1, source_target_pairs={{0,8},{8,0},{16,24},{24,16},{1,9},{9,1},{17,25},{25,17},{2,10},{10... | collective-permute-start | bytes 786440 | tf_op jit(solution)/shard_map/ppermute | solution.py:29
  128.9 3.2 %collective-permute-start.31 = (bf16[32,2048]{1,0:T(8,128)(2,1)S(1)}, bf16[32,2048]{1,0:T(8,128)(2,1)S(1)}, u32[]{:S(2)}, u32[]{:S(2)}) collective-permute-start(bf16[32,2048]{1,0:T(8,128)(2,1)S(1)} %copy-done.31), channel_id=1, source_target_pairs={{0,6},{2,4},{4,2},{6,0},{1,7},{3,5},{5,3},{7,1},{8,14},{10,12},{12... | collective-permute-start | bytes 393224 | tf_op jit(solution)/shard_map/ppermute | solution.py:29
  133.7 1.4 %collective-permute-done.31.refs_3_ = bf16[32,2048]{1,0:T(8,128)(2,1)S(1)} collective-permute-done((bf16[32,2048]{1,0:T(8,128)(2,1)S(1)}, bf16[32,2048]{1,0:T(8,128)(2,1)S(1)}, u32[]{:S(2)}, u32[]{:S(2)}) %collective-permute-start.31) | collective-permute-done | bytes 131104 | tf_op jit(solution)/shard_map/ppermute | solution.py:29
  135.4 1.4 %collective-permute-done.36.refs_3_ = bf16[64,2048]{1,0:T(8,128)(2,1)S(1)} collective-permute-done((bf16[64,2048]{1,0:T(8,128)(2,1)S(1)}, bf16[64,2048]{1,0:T(8,128)(2,1)S(1)}, u32[]{:S(2)}, u32[]{:S(2)}) %collective-permute-start.36) | collective-permute-done | bytes 262176 | tf_op jit(solution)/shard_map/ppermute | solution.py:29
  136.8 2.0 %final.1 = bf16[64,2048]{1,0:T(8,128)(2,1)} custom-call(s32[64,1]{1,0:T(8,128)S(1)} %copy.23.live, bf16[64,2048]{1,0:T(8,128)(2,1)S(1)} %copy-done.13, f32[64,2048]{1,0:T(8,128)S(1)} %copy-done.9, f32[64,2048]{1,0:T(8,128)S(1)} %combine.6.routed, bf16[64,2048]{1,0:T(8,128)(2,1)} %collective-permute-done.21.refs_0_, ...), custom_call_target="tpu_custom_call" | custom-call | flops 1024 | bytes 1024 | tf_op jit(solution)/shard_map/final/pallas_call | solution.py:511
  (143 shorter events, 27.3 us)
Async XLA Ops:
  2.5 13.0 %collective-permute-start.4 = (bf16[704,2048]{1,0:T(8,128)(2,1)}, bf16[704,2048]{1,0:T(8,128)(2,1)S(1)}, u32[]{:S(2)}, u32[]{:S(2)}) collective-permute-start(bf16[704,2048]{1,0:T(8,128)(2,1)} %bitcast.24), channel_id=1, source_target_pairs={{0,1},{1,0},{2,3},{3,2},{4,5},{5,4},{6,7},{7,6},{8,9},{9,8},{10,11... | collective-permute-start | bytes 8650760 | tf_op jit(solution)/shard_map/ppermute | solution.py:29
  2.9 9.7 %collective-permute-start = (bf16[64,2048]{1,0:T(8,128)(2,1)}, bf16[64,2048]{1,0:T(8,128)(2,1)S(1)}, u32[]{:S(2)}, u32[]{:S(2)}) collective-permute-start(bf16[64,2048]{1,0:T(8,128)(2,1)} %bitcast.28), channel_id=1, source_target_pairs={{0,2},{2,0},{1,3},{3,1},{4,6},{6,4},{5,7},{7,5},{8,10},{10,8},{9,1... | collective-permute-start | bytes 786440 | tf_op jit(solution)/shard_map/ppermute | solution.py:29
  15.0 9.4 %collective-permute-start.6 = (bf16[352,2048]{1,0:T(8,128)(2,1)}, bf16[352,2048]{1,0:T(8,128)(2,1)}, u32[]{:S(2)}, u32[]{:S(2)}) collective-permute-start(bf16[352,2048]{1,0:T(8,128)(2,1)} %bitcast.37), channel_id=1, source_target_pairs={{0,1},{1,0},{2,3},{3,2},{4,5},{5,4},{6,7},{7,6},{8,9},{9,8},{10,11... | collective-permute-start | bytes 4325384 | tf_op jit(solution)/shard_map/ppermute | solution.py:29
  15.2 9.3 %collective-permute-start.7 = (bf16[352,2048]{1,0:T(8,128)(2,1)}, bf16[352,2048]{1,0:T(8,128)(2,1)}, u32[]{:S(2)}, u32[]{:S(2)}) collective-permute-start(bf16[352,2048]{1,0:T(8,128)(2,1)} %refs_4_.1), channel_id=1, source_target_pairs={{0,1},{1,0},{2,3},{3,2},{4,5},{5,4},{6,7},{7,6},{8,9},{9,8},{10,11... | collective-permute-start | bytes 4325384 | tf_op jit(solution)/shard_map/ppermute | solution.py:29
  26.0 11.0 %collective-permute-start.9 = (bf16[2048,1408]{1,0:T(8,128)(2,1)}, bf16[2048,1408]{1,0:T(8,128)(2,1)}, u32[]{:S(2)}, u32[]{:S(2)}) collective-permute-start(bf16[2048,1408]{1,0:T(8,128)(2,1)} %bitcast.21), channel_id=1, source_target_pairs={{0,1},{1,0},{2,3},{3,2},{4,5},{5,4},{6,7},{7,6},{8,9},{9,8},{10,11... | collective-permute-start | bytes 17301512 | tf_op jit(solution)/shard_map/ppermute | solution.py:29
  27.3 8.6 %collective-permute-start.8 = (bf16[64,2048]{1,0:T(8,128)(2,1)S(1)}, bf16[64,2048]{1,0:T(8,128)(2,1)S(1)}, u32[]{:S(2)}, u32[]{:S(2)}) collective-permute-start(bf16[64,2048]{1,0:T(8,128)(2,1)S(1)} %add_convert_fusion), channel_id=1, source_target_pairs={{0,2},{2,0},{1,3},{3,1},{4,6},{6,4},{5,7},{7,5},{8,10},{10,8},{9,1... | collective-permute-start | bytes 786440 | tf_op jit(solution)/shard_map/ppermute | solution.py:29
  38.1 23.4 %collective-permute-start.12 = (bf16[64,2176]{1,0:T(8,128)(2,1)S(1)}, bf16[64,2176]{1,0:T(8,128)(2,1)S(1)}, u32[]{:S(2)}, u32[]{:S(2)}) collective-permute-start(bf16[64,2176]{1,0:T(8,128)(2,1)S(1)} %get-tuple-element.120.refs_2_), channel_id=1, source_target_pairs={{0,24},{8,16},{16,8},{24,0},{1,25},{9,17},{17,9},{25,1},{2,26},{10... | collective-permute-start | bytes 835592 | tf_op jit(solution)/shard_map/ppermute | solution.py:29
  43.3 9.3 %collective-permute-start.11 = (bf16[64,2048]{1,0:T(8,128)(2,1)S(1)}, bf16[64,2048]{1,0:T(8,128)(2,1)S(1)}, u32[]{:S(2)}, u32[]{:S(2)}) collective-permute-start(bf16[64,2048]{1,0:T(8,128)(2,1)S(1)} %get-tuple-element.115.refs_0_), channel_id=1, source_target_pairs={{0,2},{2,0},{1,3},{3,1},{4,6},{6,4},{5,7},{7,5},{8,10},{10,8},{9,1... | collective-permute-start | bytes 786440 | tf_op jit(solution)/shard_map/ppermute | solution.py:29
  46.3 22.2 %collective-permute-start.16 = (bf16[64,2176]{1,0:T(8,128)(2,1)S(1)}, bf16[64,2176]{1,0:T(8,128)(2,1)S(1)}, u32[]{:S(2)}, u32[]{:S(2)}) collective-permute-start(bf16[64,2176]{1,0:T(8,128)(2,1)S(1)} %get-tuple-element.120.refs_2_), channel_id=1, source_target_pairs={{0,16},{8,24},{16,0},{24,8},{1,17},{9,25},{17,1},{25,9},{2,18},{10... | collective-permute-start | bytes 835592 | tf_op jit(solution)/shard_map/ppermute | solution.py:29
  47.4 21.1 %collective-permute-start.17 = (bf16[64,2176]{1,0:T(8,128)(2,1)S(1)}, bf16[64,2176]{1,0:T(8,128)(2,1)S(1)}, u32[]{:S(2)}, u32[]{:S(2)}) collective-permute-start(bf16[64,2176]{1,0:T(8,128)(2,1)S(1)} %get-tuple-element.120.refs_2_), channel_id=1, source_target_pairs={{0,8},{8,0},{16,24},{24,16},{1,9},{9,1},{17,25},{25,17},{2,10},{10... | collective-permute-start | bytes 835592 | tf_op jit(solution)/shard_map/ppermute | solution.py:29
  63.2 10.5 %collective-permute-start.13 = (bf16[64,2048]{1,0:T(8,128)(2,1)S(1)}, bf16[64,2048]{1,0:T(8,128)(2,1)S(1)}, u32[]{:S(2)}, u32[]{:S(2)}) collective-permute-start(bf16[64,2048]{1,0:T(8,128)(2,1)S(1)} %get-tuple-element.125), channel_id=1, source_target_pairs={{0,2},{2,0},{4,6},{6,4},{1,3},{3,1},{5,7},{7,5},{8,10},{10,8},{12,... | collective-permute-start | bytes 786440 | tf_op jit(solution)/shard_map/ppermute | solution.py:29
  65.0 14.6 %collective-permute-start.14 = (bf16[64,2048]{1,0:T(8,128)(2,1)S(1)}, bf16[64,2048]{1,0:T(8,128)(2,1)S(1)}, u32[]{:S(2)}, u32[]{:S(2)}) collective-permute-start(bf16[64,2048]{1,0:T(8,128)(2,1)S(1)} %get-tuple-element.126), channel_id=1, source_target_pairs={{0,4},{2,6},{4,0},{6,2},{1,5},{3,7},{5,1},{7,3},{8,12},{10,14},{12... | collective-permute-start | bytes 786440 | tf_op jit(solution)/shard_map/ppermute | solution.py:29
  67.3 14.0 %collective-permute-start.15 = (bf16[64,2048]{1,0:T(8,128)(2,1)S(1)}, bf16[64,2048]{1,0:T(8,128)(2,1)S(1)}, u32[]{:S(2)}, u32[]{:S(2)}) collective-permute-start(bf16[64,2048]{1,0:T(8,128)(2,1)S(1)} %get-tuple-element.127), channel_id=1, source_target_pairs={{0,6},{2,4},{4,2},{6,0},{1,7},{3,5},{5,3},{7,1},{8,14},{10,12},{12... | collective-permute-start | bytes 786440 | tf_op jit(solution)/shard_map/ppermute | solution.py:29
  71.0 21.8 %collective-permute-start.18 = (bf16[64,2048]{1,0:T(8,128)(2,1)}, bf16[64,2048]{1,0:T(8,128)(2,1)S(1)}, u32[]{:S(2)}, u32[]{:S(2)}) collective-permute-start(bf16[64,2048]{1,0:T(8,128)(2,1)} %get-tuple-element.136), channel_id=1, source_target_pairs={{0,2},{2,0},{4,6},{6,4},{1,3},{3,1},{5,7},{7,5},{8,10},{10,8},{12,... | collective-permute-start | bytes 786440 | tf_op jit(solution)/shard_map/ppermute | solution.py:29
  73.7 21.6 %collective-permute-start.19 = (bf16[64,2048]{1,0:T(8,128)(2,1)}, bf16[64,2048]{1,0:T(8,128)(2,1)S(1)}, u32[]{:S(2)}, u32[]{:S(2)}) collective-permute-start(bf16[64,2048]{1,0:T(8,128)(2,1)} %get-tuple-element.137), channel_id=1, source_target_pairs={{0,4},{2,6},{4,0},{6,2},{1,5},{3,7},{5,1},{7,3},{8,12},{10,14},{12... | collective-permute-start | bytes 786440 | tf_op jit(solution)/shard_map/ppermute | solution.py:29
  73.7 22.5 %collective-permute-start.20 = (bf16[64,2048]{1,0:T(8,128)(2,1)}, bf16[64,2048]{1,0:T(8,128)(2,1)S(1)}, u32[]{:S(2)}, u32[]{:S(2)}) collective-permute-start(bf16[64,2048]{1,0:T(8,128)(2,1)} %get-tuple-element.138), channel_id=1, source_target_pairs={{0,6},{2,4},{4,2},{6,0},{1,7},{3,5},{5,3},{7,1},{8,14},{10,12},{12... | collective-permute-start | bytes 786440 | tf_op jit(solution)/shard_map/ppermute | solution.py:29
  79.6 16.5 %collective-permute-start.21 = (bf16[64,2048]{1,0:T(8,128)(2,1)}, bf16[64,2048]{1,0:T(8,128)(2,1)}, u32[]{:S(2)}, u32[]{:S(2)}) collective-permute-start(bf16[64,2048]{1,0:T(8,128)(2,1)} %get-tuple-element.143), channel_id=1, source_target_pairs={{0,2},{2,0},{1,3},{3,1},{4,6},{6,4},{5,7},{7,5},{8,10},{10,8},{9,1... | collective-permute-start | bytes 786440 | tf_op jit(solution)/shard_map/ppermute | solution.py:29
  92.5 18.4 %collective-permute-start.25 = (bf16[32,2048]{1,0:T(8,128)(2,1)}, bf16[32,2048]{1,0:T(8,128)(2,1)S(1)}, u32[]{:S(2)}, u32[]{:S(2)}) collective-permute-start(bf16[32,2048]{1,0:T(8,128)(2,1)} %get-tuple-element.140), channel_id=1, source_target_pairs={{0,2},{2,0},{4,6},{6,4},{1,3},{3,1},{5,7},{7,5},{8,10},{10,8},{12,... | collective-permute-start | bytes 393224 | tf_op jit(solution)/shard_map/ppermute | solution.py:29
  92.9 18.0 %collective-permute-start.26 = (bf16[32,2048]{1,0:T(8,128)(2,1)}, bf16[32,2048]{1,0:T(8,128)(2,1)S(1)}, u32[]{:S(2)}, u32[]{:S(2)}) collective-permute-start(bf16[32,2048]{1,0:T(8,128)(2,1)} %get-tuple-element.141), channel_id=1, source_target_pairs={{0,4},{2,6},{4,0},{6,2},{1,5},{3,7},{5,1},{7,3},{8,12},{10,14},{12... | collective-permute-start | bytes 393224 | tf_op jit(solution)/shard_map/ppermute | solution.py:29
  95.3 15.6 %collective-permute-start.27 = (bf16[32,2048]{1,0:T(8,128)(2,1)}, bf16[32,2048]{1,0:T(8,128)(2,1)S(1)}, u32[]{:S(2)}, u32[]{:S(2)}) collective-permute-start(bf16[32,2048]{1,0:T(8,128)(2,1)} %get-tuple-element.142), channel_id=1, source_target_pairs={{0,6},{2,4},{4,2},{6,0},{1,7},{3,5},{5,3},{7,1},{8,14},{10,12},{12... | collective-permute-start | bytes 393224 | tf_op jit(solution)/shard_map/ppermute | solution.py:29
  107.8 6.4 %collective-permute-start.22 = (bf16[32,2048]{1,0:T(8,128)(2,1)S(1)}, bf16[32,2048]{1,0:T(8,128)(2,1)S(1)}, u32[]{:S(2)}, u32[]{:S(2)}) collective-permute-start(bf16[32,2048]{1,0:T(8,128)(2,1)S(1)} %get-tuple-element.149), channel_id=1, source_target_pairs={{0,2},{2,0},{4,6},{6,4},{1,3},{3,1},{5,7},{7,5},{8,10},{10,8},{12,... | collective-permute-start | bytes 393224 | tf_op jit(solution)/shard_map/ppermute | solution.py:29
  108.5 8.5 %collective-permute-start.23 = (bf16[32,2048]{1,0:T(8,128)(2,1)S(1)}, bf16[32,2048]{1,0:T(8,128)(2,1)S(1)}, u32[]{:S(2)}, u32[]{:S(2)}) collective-permute-start(bf16[32,2048]{1,0:T(8,128)(2,1)S(1)} %get-tuple-element.150), channel_id=1, source_target_pairs={{0,4},{2,6},{4,0},{6,2},{1,5},{3,7},{5,1},{7,3},{8,12},{10,14},{12... | collective-permute-start | bytes 393224 | tf_op jit(solution)/shard_map/ppermute | solution.py:29
  111.1 17.5 %collective-permute-start.28 = (bf16[64,2048]{1,0:T(8,128)(2,1)S(1)}, bf16[64,2048]{1,0:T(8,128)(2,1)S(1)}, u32[]{:S(2)}, u32[]{:S(2)}) collective-permute-start(bf16[64,2048]{1,0:T(8,128)(2,1)S(1)} %combine.5), channel_id=1, source_target_pairs={{0,24},{8,16},{16,8},{24,0},{1,25},{9,17},{17,9},{25,1},{2,26},{10... | collective-permute-start | bytes 786440 | tf_op jit(solution)/shard_map/ppermute | solution.py:29
  111.4 8.4 %collective-permute-start.24 = (bf16[32,2048]{1,0:T(8,128)(2,1)S(1)}, bf16[32,2048]{1,0:T(8,128)(2,1)S(1)}, u32[]{:S(2)}, u32[]{:S(2)}) collective-permute-start(bf16[32,2048]{1,0:T(8,128)(2,1)S(1)} %get-tuple-element.151), channel_id=1, source_target_pairs={{0,6},{2,4},{4,2},{6,0},{1,7},{3,5},{5,3},{7,1},{8,14},{10,12},{12... | collective-permute-start | bytes 393224 | tf_op jit(solution)/shard_map/ppermute | solution.py:29
  112.6 10.1 %collective-permute-start.33 = (bf16[32,2048]{1,0:T(8,128)(2,1)S(1)}, bf16[32,2048]{1,0:T(8,128)(2,1)S(1)}, u32[]{:S(2)}, u32[]{:S(2)}) collective-permute-start(bf16[32,2048]{1,0:T(8,128)(2,1)S(1)} %get-tuple-element.169), channel_id=1, source_target_pairs={{0,2},{2,0},{4,6},{6,4},{1,3},{3,1},{5,7},{7,5},{8,10},{10,8},{12,... | collective-permute-start | bytes 393224 | tf_op jit(solution)/shard_map/ppermute | solution.py:29
  114.2 8.5 %collective-permute-start.34 = (bf16[32,2048]{1,0:T(8,128)(2,1)S(1)}, bf16[32,2048]{1,0:T(8,128)(2,1)S(1)}, u32[]{:S(2)}, u32[]{:S(2)}) collective-permute-start(bf16[32,2048]{1,0:T(8,128)(2,1)S(1)} %get-tuple-element.170), channel_id=1, source_target_pairs={{0,4},{2,6},{4,0},{6,2},{1,5},{3,7},{5,1},{7,3},{8,12},{10,14},{12... | collective-permute-start | bytes 393224 | tf_op jit(solution)/shard_map/ppermute | solution.py:29
  117.0 5.9 %collective-permute-start.35 = (bf16[32,2048]{1,0:T(8,128)(2,1)S(1)}, bf16[32,2048]{1,0:T(8,128)(2,1)S(1)}, u32[]{:S(2)}, u32[]{:S(2)}) collective-permute-start(bf16[32,2048]{1,0:T(8,128)(2,1)S(1)} %get-tuple-element.171), channel_id=1, source_target_pairs={{0,6},{2,4},{4,2},{6,0},{1,7},{3,5},{5,3},{7,1},{8,14},{10,12},{12... | collective-permute-start | bytes 393224 | tf_op jit(solution)/shard_map/ppermute | solution.py:29
  120.0 15.3 %collective-permute-start.32 = (bf16[64,2048]{1,0:T(8,128)(2,1)S(1)}, bf16[64,2048]{1,0:T(8,128)(2,1)S(1)}, u32[]{:S(2)}, u32[]{:S(2)}) collective-permute-start(bf16[64,2048]{1,0:T(8,128)(2,1)S(1)} %combine.4), channel_id=1, source_target_pairs={{0,16},{8,24},{16,0},{24,8},{1,17},{9,25},{17,1},{25,9},{2,18},{10... | collective-permute-start | bytes 786440 | tf_op jit(solution)/shard_map/ppermute | solution.py:29
  123.1 13.7 %collective-permute-start.36 = (bf16[64,2048]{1,0:T(8,128)(2,1)S(1)}, bf16[64,2048]{1,0:T(8,128)(2,1)S(1)}, u32[]{:S(2)}, u32[]{:S(2)}) collective-permute-start(bf16[64,2048]{1,0:T(8,128)(2,1)S(1)} %combine.7), channel_id=1, source_target_pairs={{0,8},{8,0},{16,24},{24,16},{1,9},{9,1},{17,25},{25,17},{2,10},{10... | collective-permute-start | bytes 786440 | tf_op jit(solution)/shard_map/ppermute | solution.py:29
  128.6 5.0 %collective-permute-start.29 = (bf16[32,2048]{1,0:T(8,128)(2,1)S(1)}, bf16[32,2048]{1,0:T(8,128)(2,1)S(1)}, u32[]{:S(2)}, u32[]{:S(2)}) collective-permute-start(bf16[32,2048]{1,0:T(8,128)(2,1)S(1)} %copy-done.33), channel_id=1, source_target_pairs={{0,2},{2,0},{4,6},{6,4},{1,3},{3,1},{5,7},{7,5},{8,10},{10,8},{12,... | collective-permute-start | bytes 393224 | tf_op jit(solution)/shard_map/ppermute | solution.py:29
  128.7 5.0 %collective-permute-start.30 = (bf16[32,2048]{1,0:T(8,128)(2,1)S(1)}, bf16[32,2048]{1,0:T(8,128)(2,1)S(1)}, u32[]{:S(2)}, u32[]{:S(2)}) collective-permute-start(bf16[32,2048]{1,0:T(8,128)(2,1)S(1)} %copy-done.32), channel_id=1, source_target_pairs={{0,4},{2,6},{4,0},{6,2},{1,5},{3,7},{5,1},{7,3},{8,12},{10,14},{12... | collective-permute-start | bytes 393224 | tf_op jit(solution)/shard_map/ppermute | solution.py:29
  128.9 6.2 %collective-permute-start.31 = (bf16[32,2048]{1,0:T(8,128)(2,1)S(1)}, bf16[32,2048]{1,0:T(8,128)(2,1)S(1)}, u32[]{:S(2)}, u32[]{:S(2)}) collective-permute-start(bf16[32,2048]{1,0:T(8,128)(2,1)S(1)} %copy-done.31), channel_id=1, source_target_pairs={{0,6},{2,4},{4,2},{6,0},{1,7},{3,5},{5,3},{7,1},{8,14},{10,12},{12... | collective-permute-start | bytes 393224 | tf_op jit(solution)/shard_map/ppermute | solution.py:29
  (43 other events, 564.1 us)

commit v14 on v11

--- a/solution.py
+++ b/solution.py
@@ -235,23 +235,6 @@
     )(place, lengths, first, second, gain, weight, cosine, sine, reach, cache, outward)
 
 
-def add_kernel(left, right, out):
-    total = left[...].astype(jnp.float32) + right[...].astype(jnp.float32)
-    out[...] = total.astype(out.dtype)
-
-
-def add(left, right, dtype):
-    return pl.pallas_call(
-        add_kernel,
-        in_specs=[in_vmem()] * 2,
-        out_specs=in_vmem(),
-        out_shape=jax.ShapeDtypeStruct(left.shape, dtype),
-        compiler_params=pltpu.CompilerParams(vmem_limit_bytes=16 * 2**20),
-        cost_estimate=SMALL,
-        name="add",
-    )(left, right)
-
-
 def silu(values):
     return values / (1.0 + jnp.exp(-values))
 
@@ -329,7 +312,7 @@
             pltpu.VMEM((rows, width), jnp.bfloat16),
             pltpu.SemaphoreType.DMA((2 * (len(tiles) + 1),)),
         ],
-        compiler_params=pltpu.CompilerParams(vmem_limit_bytes=60 * 2**20),
+        compiler_params=pltpu.CompilerParams(vmem_limit_bytes=40 * 2**20),
         cost_estimate=SMALL,
         name="expert",
     )(*pieces, inner[0], outer[0], inner[1], outer[1])
@@ -609,11 +592,10 @@
             other, middle, late = lax.optimization_barrier((other, middle, late))
             late = partner(late, "c", 1)
         if o:
-            follow = add(own_part, other, jnp.bfloat16)
-            terms[o] = partner(follow, "x", o)
-    own_term = own_part
-    for o in range(1, side):
-        own_term = add(own_term, terms[o], jnp.float32)
+            follow = (own_part + other.astype(jnp.float32)).astype(jnp.bfloat16)
+            crossed = partner(follow, "x", o).astype(jnp.float32)
+            terms[o] = crossed if o == side - 1 else crossed + terms[o + 1]
+    own_term = own_part + terms[1] if side > 1 else own_part
     own_term, late = lax.optimization_barrier((own_term, late))
     others = [other]
     resid, normed, payload = finish(own_rows, own_term, others, ffn_gain[None], routes[0])
@@ -637,11 +619,11 @@
     near_experts = lax.axis_index("z") * plane + (
         lax.axis_index(PLANE) ^ jnp.arange(plane, dtype=jnp.int32)
     )
+    line_rows = [payload] + [partner(payload, "z", k) for k in range(1, line)]
     beside = [partner(normed, "x", o) for o in range(1, side)]
-    calm, beside = lax.optimization_barrier((payload, beside))
-    line_rows = [payload] + [
-        partner(payload if k in GROUPS[0] else calm, "z", k) for k in range(1, line)
-    ]
+
+    shared, beside = shared_terms(normed, beside, shared_weights)
+    line_rows[3], beside = lax.optimization_barrier((line_rows[3], beside))
 
     sent = []
     spread = {}
@@ -651,11 +633,6 @@
         )
         spread.update(zip(ks, spreads))
         sent.append([partner(pieces[o], PLANE, o) for o in range(plane)])
-        if len(sent) == 1:
-            normed, spread[ks[0]] = lax.optimization_barrier((normed, spread[ks[0]]))
-            shared, beside = shared_terms(
-                normed, beside, [gate_turned, up_turned, shared_down, early[0], *middle]
-            )
     parts = [partner(beside[o - 1], "x", o) for o in range(1, side)]
     made = None
     results = {}

time: 138 us -> 134 us (0.971); the launches traced: 135 us -> 134 us
  starting transfers between devices: 46.7 us -> 52.4 us
  Pallas kernels: 52.1 us -> 46.6 us
  waiting for transfers between devices: 22.3 us -> 18.4 us
  other arithmetic: 0.02 us -> 2.22 us
    pallas_call x2, Pallas kernels: 20.7 us -> 14.4 us  [experts(): pl.pallas_call(functools.partial(expert_kernel, plane=plane, count=count,...]
    ppermute x37, starting transfers between devices: 46.7 us -> 52.4 us  [partner(): return lax.ppermute(value, axes, [(i, i ^ offset) for i in range(size)])]
    ppermute x37, waiting for transfers between devices: 22.3 us -> 18.4 us  [partner(): return lax.ppermute(value, axes, [(i, i ^ offset) for i in range(size)])]
    unnamed x80 -> x58, local copies, waits for them, and re-layouts: 11.1 us -> 10.6 us
  transfers between devices with their start and end apart: 37 -> 37, of which waited for: 12 -> 11; matrix products, arithmetic and copies ran while one was open for 2% -> 4% of each run, Pallas kernels for 37% -> 34%
where the time goes in v14:
time: 134 us
  starting transfers between devices  52.4 us (39%)
  Pallas kernels  46.6 us (35%)
  waiting for transfers between devices  18.4 us (14%)
  local copies, waits for them, and re-layouts  12.4 us (9%)
  other arithmetic  2.22 us (2%)
    ppermute x37, starting transfers between devices, partner(): return lax.ppermute(value, axes, [(i, i ^ offset) for i in range(size)])  52.4 us
    ppermute x37, waiting for transfers between devices, partner(): return lax.ppermute(value, axes, [(i, i ^ offset) for i in range(size)])  18.4 us
    pallas_call x2, Pallas kernels, attend(): pl.pallas_call(functools.partial(attend_kernel, offset=offset), in_specs=...  15.9 us
    pallas_call x2, Pallas kernels, experts(): pl.pallas_call(functools.partial(expert_kernel, plane=plane, count=count,...  14.4 us
    unnamed x58, local copies, waits for them, and re-layouts  10.6 us
    pallas_call x1, Pallas kernels, shared_terms(): pl.pallas_call(functools.partial(shared_kernel, side=side), in_specs=[in_...  8.34 us
    pallas_call x2, Pallas kernels, select(): pl.pallas_call(functools.partial(select_kernel, count=count, plane=plane,...  3.8 us
  transfers between devices with their start and end apart: 37, of which 11 were waited for; matrix products, arithmetic and copies ran while one was open for 4% of the time, Pallas kernels for 34%

profile of v14, /device:TPU:0, one launch (start us, length us, event | category | flops | bytes accessed | tf_op | source)
XLA Modules:
  0.0 134.1 jit_solution(9910849420772659181)
XLA Ops:
  1.2 1.4 %collective-permute-done.1.second = bf16[64,2048]{1,0:T(8,128)(2,1)S(1)} collective-permute-done((bf16[64,2048]{1,0:T(8,128)(2,1)}, bf16[64,2048]{1,0:T(8,128)(2,1)S(1)}, u32[]{:S(2)}, u32[]{:S(2)}) %collective-permute-start.1) | collective-permute-done | bytes 262176 | tf_op jit(solution)/shard_map/ppermute | solution.py:29
  2.9 2.6 %collective-permute-start = (bf16[64,2048]{1,0:T(8,128)(2,1)}, bf16[64,2048]{1,0:T(8,128)(2,1)S(1)}, u32[]{:S(2)}, u32[]{:S(2)}) collective-permute-start(bf16[64,2048]{1,0:T(8,128)(2,1)} %bitcast.28), channel_id=1, source_target_pairs={{0,2},{2,0},{1,3},{3,1},{4,6},{6,4},{5,7},{7,5},{8,10},{10,8},{9,1... | collective-permute-start | bytes 786440 | tf_op jit(solution)/shard_map/ppermute | solution.py:29
  7.5 2.0 %prepare.1 = (f32[4,64,64]{2,1,0:T(8,128)S(1)}, f32[4,64,128]{2,1,0:T(8,128)S(1)}, f32[4,64,128]{2,1,0:T(8,128)S(1)}) custom-call(s32[4]{0:T(128)S(1)} %copy-done.14, s32[4,64]{1,0:T(4,128)S(1)} %copy-done.15, f32[1,128]{1,0:T(1,128)S(1)} %copy-done.16), custom_call_target="tpu_custom_call" | custom-call | flops 1024 | bytes 1024 | tf_op jit(solution)/shard_map/prepare/pallas_call | solution.py:68
  12.6 2.5 %collective-permute-done.2.second = bf16[64,2048]{1,0:T(8,128)(2,1)S(1)} collective-permute-done((bf16[64,2048]{1,0:T(8,128)(2,1)S(1)}, bf16[64,2048]{1,0:T(8,128)(2,1)S(1)}, u32[]{:S(2)}, u32[]{:S(2)}) %collective-permute-start.2) | collective-permute-done | bytes 262176 | tf_op jit(solution)/shard_map/ppermute | solution.py:29
  16.7 8.7 %attend.2 = (f32[64,2048]{1,0:T(8,128)}, bf16[64,2048]{1,0:T(8,128)(2,1)}, bf16[64,256]{1,0:T(8,128)(2,1)}, bf16[64,256]{1,0:T(8,128)(2,1)}) custom-call(s32[1]{0:T(128)} %bitcast.2.place, s32[4]{0:T(128)} %lengths.5, bf16[64,2048]{1,0:T(8,128)(2,1)} %copy-done.21, bf16[64,2048]{1,0:T(8,128)(2,1)} %copy-done.22, f32[1,2048]{1,0:T(1,128)} %bitcast.40, ...), custom_call_target="tpu_custom_call" | custom-call | flops 1024 | bytes 1024 | tf_op jit(solution)/shard_map/attend/pallas_call | solution.py:204
  25.6 1.6 %collective-permute-done.5 = bf16[64,2048]{1,0:T(8,128)(2,1)S(1)} collective-permute-done((bf16[64,2048]{1,0:T(8,128)(2,1)}, bf16[64,2048]{1,0:T(8,128)(2,1)S(1)}, u32[]{:S(2)}, u32[]{:S(2)}) %collective-permute-start.5) | collective-permute-done | bytes 262176 | tf_op jit(solution)/shard_map/ppermute | solution.py:29
  28.7 7.2 %attend.3 = (f32[64,2048]{1,0:T(8,128)}, bf16[64,2048]{1,0:T(8,128)(2,1)}, bf16[64,256]{1,0:T(8,128)(2,1)}, bf16[64,256]{1,0:T(8,128)(2,1)}) custom-call(s32[1]{0:T(128)} %bitcast.2.place, s32[4]{0:T(128)} %lengths.5, bf16[64,2048]{1,0:T(8,128)(2,1)} %bitcast.29, bf16[64,2048]{1,0:T(8,128)(2,1)} %copy-done.20, f32[1,2048]{1,0:T(1,128)} %bitcast.41, ...), custom_call_target="tpu_custom_call" | custom-call | flops 1024 | bytes 1024 | tf_op jit(solution)/shard_map/attend/pallas_call | solution.py:204
  39.2 3.8 %collective-permute-start.12 = (bf16[64,2176]{1,0:T(8,128)(2,1)S(1)}, bf16[64,2176]{1,0:T(8,128)(2,1)S(1)}, u32[]{:S(2)}, u32[]{:S(2)}) collective-permute-start(bf16[64,2176]{1,0:T(8,128)(2,1)S(1)} %get-tuple-element.120.refs_2_), channel_id=1, source_target_pairs={{0,24},{8,16},{16,8},{24,0},{1,25},{9,17},{17,9},{25,1},{2,26},{10... | collective-permute-start | bytes 835592 | tf_op jit(solution)/shard_map/ppermute | solution.py:29
  43.1 2.2 %collective-permute-start.11 = (bf16[64,2048]{1,0:T(8,128)(2,1)S(1)}, bf16[64,2048]{1,0:T(8,128)(2,1)}, u32[]{:S(2)}, u32[]{:S(2)}) collective-permute-start(bf16[64,2048]{1,0:T(8,128)(2,1)S(1)} %get-tuple-element.115.refs_0_), channel_id=1, source_target_pairs={{0,2},{2,0},{1,3},{3,1},{4,6},{6,4},{5,7},{7,5},{8,10},{10,8},{9,1... | collective-permute-start | bytes 786440 | tf_op jit(solution)/shard_map/ppermute | solution.py:29
  46.4 5.3 %collective-permute-done.11.refs_1_ = bf16[64,2048]{1,0:T(8,128)(2,1)} collective-permute-done((bf16[64,2048]{1,0:T(8,128)(2,1)S(1)}, bf16[64,2048]{1,0:T(8,128)(2,1)}, u32[]{:S(2)}, u32[]{:S(2)}) %collective-permute-start.11) | collective-permute-done | bytes 262176 | tf_op jit(solution)/shard_map/ppermute | solution.py:29
  51.7 8.3 %shared.1 = (f32[64,2048]{1,0:T(8,128)}, bf16[64,2048]{1,0:T(8,128)(2,1)}) custom-call(bf16[64,2048]{1,0:T(8,128)(2,1)} %copy-done.10, bf16[64,2048]{1,0:T(8,128)(2,1)} %collective-permute-done.11.refs_1_, bf16[352,2048]{1,0:T(8,128)(2,1)} %bitcast.36, bf16[352,2048]{1,0:T(8,128)(2,1)} %bitcast.38, bf16[352,2048]{1,0:T(8,128)(2,1)} %refs_4_.1, ...), custom_call_target="tpu_custom_call" | custom-call | flops 1024 | bytes 1024 | tf_op jit(solution)/shard_map/shared/pallas_call | solution.py:360
  60.1 1.6 %select.2 = (bf16[64,2048]{1,0:T(8,128)(2,1)S(1)}, bf16[64,2048]{1,0:T(8,128)(2,1)S(1)}, bf16[64,2048]{1,0:T(8,128)(2,1)S(1)}, bf16[64,2048]{1,0:T(8,128)(2,1)S(...) custom-call(s32[4]{0:T(128)S(1)} %xor_add_fusion.refs_0_, bf16[2048,16]{1,0:T(8,128)(2,1)S(1)} %copy.21.refs_1_, ...), custom_call_target="tpu_custom_call" | custom-call | flops 1024 | bytes 1024 | tf_op jit(solution)/shard_map/select/pallas_call | solution.py:467
  61.7 1.8 %collective-permute-start.13 = (bf16[64,2048]{1,0:T(8,128)(2,1)S(1)}, bf16[64,2048]{1,0:T(8,128)(2,1)S(1)}, u32[]{:S(2)}, u32[]{:S(2)}) collective-permute-start(bf16[64,2048]{1,0:T(8,128)(2,1)S(1)} %get-tuple-element.125), channel_id=1, source_target_pairs={{0,2},{2,0},{4,6},{6,4},{1,3},{3,1},{5,7},{7,5},{8,10},{10,8},{12,... | collective-permute-start | bytes 786440 | tf_op jit(solution)/shard_map/ppermute | solution.py:29
  63.5 2.5 %collective-permute-start.14 = (bf16[64,2048]{1,0:T(8,128)(2,1)S(1)}, bf16[64,2048]{1,0:T(8,128)(2,1)S(1)}, u32[]{:S(2)}, u32[]{:S(2)}) collective-permute-start(bf16[64,2048]{1,0:T(8,128)(2,1)S(1)} %get-tuple-element.126), channel_id=1, source_target_pairs={{0,4},{2,6},{4,0},{6,2},{1,5},{3,7},{5,1},{7,3},{8,12},{10,14},{12... | collective-permute-start | bytes 786440 | tf_op jit(solution)/shard_map/ppermute | solution.py:29
  67.2 2.2 %select.3 = (bf16[64,2048]{1,0:T(8,128)(2,1)S(1)}, bf16[64,2048]{1,0:T(8,128)(2,1)S(1)}, bf16[64,2048]{1,0:T(8,128)(2,1)S(1)}, bf16[64,2048]{1,0:T(8,128)(2,1)S(...) custom-call(s32[4]{0:T(128)S(1)} %xor_add_fusion.refs_0_, bf16[2048,16]{1,0:T(8,128)(2,1)S(1)} %copy.21.refs_1_, ...), custom_call_target="tpu_custom_call" | custom-call | flops 1024 | bytes 1024 | tf_op jit(solution)/shard_map/select/pallas_call | solution.py:467
  70.0 4.7 %collective-permute-start.19 = (bf16[64,2048]{1,0:T(8,128)(2,1)S(1)}, bf16[64,2048]{1,0:T(8,128)(2,1)S(1)}, u32[]{:S(2)}, u32[]{:S(2)}) collective-permute-start(bf16[64,2048]{1,0:T(8,128)(2,1)S(1)} %get-tuple-element.137), channel_id=1, source_target_pairs={{0,4},{2,6},{4,0},{6,2},{1,5},{3,7},{5,1},{7,3},{8,12},{10,14},{12... | collective-permute-start | bytes 786440 | tf_op jit(solution)/shard_map/ppermute | solution.py:29
  74.8 1.4 %collective-permute-start.20 = (bf16[64,2048]{1,0:T(8,128)(2,1)S(1)}, bf16[64,2048]{1,0:T(8,128)(2,1)S(1)}, u32[]{:S(2)}, u32[]{:S(2)}) collective-permute-start(bf16[64,2048]{1,0:T(8,128)(2,1)S(1)} %get-tuple-element.138), channel_id=1, source_target_pairs={{0,6},{2,4},{4,2},{6,0},{1,7},{3,5},{5,3},{7,1},{8,14},{10,12},{12... | collective-permute-start | bytes 786440 | tf_op jit(solution)/shard_map/ppermute | solution.py:29
  77.0 1.6 %collective-permute-start.21 = (bf16[64,2048]{1,0:T(8,128)(2,1)S(1)}, bf16[64,2048]{1,0:T(8,128)(2,1)S(1)}, u32[]{:S(2)}, u32[]{:S(2)}) collective-permute-start(bf16[64,2048]{1,0:T(8,128)(2,1)S(1)} %copy-done.26), channel_id=1, source_target_pairs={{0,2},{2,0},{1,3},{3,1},{4,6},{6,4},{5,7},{7,5},{8,10},{10,8},{9,1... | collective-permute-start | bytes 786440 | tf_op jit(solution)/shard_map/ppermute | solution.py:29
  79.2 2.6 %copy-done.1 = bf16[1,2048,1408]{2,1,0:T(8,128)(2,1)S(1)} copy-done((bf16[1,2048,1408]{2,1,0:T(8,128)(2,1)S(1)}, bf16[1,2048,1408]{2,1,0:T(8,128)(2,1)}, u32[]{:S(2)}) %copy-start.1) | copy-done | bytes 5767192
  81.8 1.8 %copy-done.4 = bf16[704,2048]{1,0:T(8,128)(2,1)S(1)} copy-done((bf16[704,2048]{1,0:T(8,128)(2,1)S(1)}, bf16[704,2048]{1,0:T(8,128)(2,1)}, u32[]{:S(2)}) %copy-start.4) | copy-done | bytes 2883608
  83.7 7.1 %expert.2 = (bf16[32,2048]{1,0:T(8,128)(2,1)S(1)}, bf16[32,2048]{1,0:T(8,128)(2,1)S(1)}, bf16[32,2048]{1,0:T(8,128)(2,1)S(1)}, bf16[32,2048]{1,0:T(8,128)(2,1)S(...) custom-call(bf16[64,2048]{1,0:T(8,128)(2,1)S(1)} %get-tuple-element., ...), custom_call_target="tpu_custom_call" | custom-call | flops 1024 | bytes 1024 | tf_op jit(solution)/shard_map/expert/pallas_call | solution.py:302
  91.2 1.9 %collective-permute-start.26 = (bf16[32,2048]{1,0:T(8,128)(2,1)S(1)}, bf16[32,2048]{1,0:T(8,128)(2,1)S(1)}, u32[]{:S(2)}, u32[]{:S(2)}) collective-permute-start(bf16[32,2048]{1,0:T(8,128)(2,1)S(1)} %get-tuple-element.141), channel_id=1, source_target_pairs={{0,4},{2,6},{4,0},{6,2},{1,5},{3,7},{5,1},{7,3},{8,12},{10,14},{12... | collective-permute-start | bytes 393224 | tf_op jit(solution)/shard_map/ppermute | solution.py:29
  94.3 7.3 %expert.3 = (bf16[32,2048]{1,0:T(8,128)(2,1)S(1)}, bf16[32,2048]{1,0:T(8,128)(2,1)S(1)}, bf16[32,2048]{1,0:T(8,128)(2,1)S(1)}, bf16[32,2048]{1,0:T(8,128)(2,1)S(...) custom-call(bf16[64,2048]{1,0:T(8,128)(2,1)S(1)} %get-tuple-element., ...), custom_call_target="tpu_custom_call" | custom-call | flops 1024 | bytes 1024 | tf_op jit(solution)/shard_map/expert/pallas_call | solution.py:302
  102.3 2.2 %collective-permute-start.23 = (bf16[32,2048]{1,0:T(8,128)(2,1)S(1)}, bf16[32,2048]{1,0:T(8,128)(2,1)S(1)}, u32[]{:S(2)}, u32[]{:S(2)}) collective-permute-start(bf16[32,2048]{1,0:T(8,128)(2,1)S(1)} %get-tuple-element.150), channel_id=1, source_target_pairs={{0,4},{2,6},{4,0},{6,2},{1,5},{3,7},{5,1},{7,3},{8,12},{10,14},{12... | collective-permute-start | bytes 393224 | tf_op jit(solution)/shard_map/ppermute | solution.py:29
  105.4 1.3 collective-permute-start.24
  108.1 2.4 %collective-permute-start.34 = (bf16[32,2048]{1,0:T(8,128)(2,1)S(1)}, bf16[32,2048]{1,0:T(8,128)(2,1)S(1)}, u32[]{:S(2)}, u32[]{:S(2)}) collective-permute-start(bf16[32,2048]{1,0:T(8,128)(2,1)S(1)} %get-tuple-element.170), channel_id=1, source_target_pairs={{0,4},{2,6},{4,0},{6,2},{1,5},{3,7},{5,1},{7,3},{8,12},{10,14},{12... | collective-permute-start | bytes 393224 | tf_op jit(solution)/shard_map/ppermute | solution.py:29
  111.3 3.5 %collective-permute-start.35 = (bf16[32,2048]{1,0:T(8,128)(2,1)S(1)}, bf16[32,2048]{1,0:T(8,128)(2,1)S(1)}, u32[]{:S(2)}, u32[]{:S(2)}) collective-permute-start(bf16[32,2048]{1,0:T(8,128)(2,1)S(1)} %get-tuple-element.171), channel_id=1, source_target_pairs={{0,6},{2,4},{4,2},{6,0},{1,7},{3,5},{5,3},{7,1},{8,14},{10,12},{12... | collective-permute-start | bytes 393224 | tf_op jit(solution)/shard_map/ppermute | solution.py:29
  115.1 5.6 %collective-permute-start.32 = (bf16[64,2048]{1,0:T(8,128)(2,1)S(1)}, bf16[64,2048]{1,0:T(8,128)(2,1)S(1)}, u32[]{:S(2)}, u32[]{:S(2)}) collective-permute-start(bf16[64,2048]{1,0:T(8,128)(2,1)S(1)} %combine.4), channel_id=1, source_target_pairs={{0,16},{8,24},{16,0},{24,8},{1,17},{9,25},{17,1},{25,9},{2,18},{10... | collective-permute-start | bytes 786440 | tf_op jit(solution)/shard_map/ppermute | solution.py:29
  120.9 2.6 %collective-permute-start.36 = (bf16[64,2048]{1,0:T(8,128)(2,1)S(1)}, bf16[64,2048]{1,0:T(8,128)(2,1)S(1)}, u32[]{:S(2)}, u32[]{:S(2)}) collective-permute-start(bf16[64,2048]{1,0:T(8,128)(2,1)S(1)} %combine.7), channel_id=1, source_target_pairs={{0,8},{8,0},{16,24},{24,16},{1,9},{9,1},{17,25},{25,17},{2,10},{10... | collective-permute-start | bytes 786440 | tf_op jit(solution)/shard_map/ppermute | solution.py:29
  124.2 2.1 %collective-permute-start.29 = (bf16[32,2048]{1,0:T(8,128)(2,1)S(1)}, bf16[32,2048]{1,0:T(8,128)(2,1)S(1)}, u32[]{:S(2)}, u32[]{:S(2)}) collective-permute-start(bf16[32,2048]{1,0:T(8,128)(2,1)S(1)} %copy-done.18), channel_id=1, source_target_pairs={{0,2},{2,0},{4,6},{6,4},{1,3},{3,1},{5,7},{7,5},{8,10},{10,8},{12,... | collective-permute-start | bytes 393224 | tf_op jit(solution)/shard_map/ppermute | solution.py:29
  126.3 1.5 %collective-permute-start.31 = (bf16[32,2048]{1,0:T(8,128)(2,1)S(1)}, bf16[32,2048]{1,0:T(8,128)(2,1)S(1)}, u32[]{:S(2)}, u32[]{:S(2)}) collective-permute-start(bf16[32,2048]{1,0:T(8,128)(2,1)S(1)} %get-tuple-element.160), channel_id=1, source_target_pairs={{0,6},{2,4},{4,2},{6,0},{1,7},{3,5},{5,3},{7,1},{8,14},{10,12},{12... | collective-permute-start | bytes 393224 | tf_op jit(solution)/shard_map/ppermute | solution.py:29
  130.0 2.7 %collective-permute-done.30.refs_2_ = bf16[32,2048]{1,0:T(8,128)(2,1)S(1)} collective-permute-done((bf16[32,2048]{1,0:T(8,128)(2,1)S(1)}, bf16[32,2048]{1,0:T(8,128)(2,1)S(1)}, u32[]{:S(2)}, u32[]{:S(2)}) %collective-permute-start.30) | collective-permute-done | bytes 131104 | tf_op jit(solution)/shard_map/ppermute | solution.py:29
  (123 shorter events, 26.8 us)
Async XLA Ops:
  2.5 13.1 %collective-permute-start.4 = (bf16[704,2048]{1,0:T(8,128)(2,1)}, bf16[704,2048]{1,0:T(8,128)(2,1)S(1)}, u32[]{:S(2)}, u32[]{:S(2)}) collective-permute-start(bf16[704,2048]{1,0:T(8,128)(2,1)} %bitcast.24), channel_id=1, source_target_pairs={{0,1},{1,0},{2,3},{3,2},{4,5},{5,4},{6,7},{7,6},{8,9},{9,8},{10,11... | collective-permute-start | bytes 8650760 | tf_op jit(solution)/shard_map/ppermute | solution.py:29
  2.9 9.7 %collective-permute-start = (bf16[64,2048]{1,0:T(8,128)(2,1)}, bf16[64,2048]{1,0:T(8,128)(2,1)S(1)}, u32[]{:S(2)}, u32[]{:S(2)}) collective-permute-start(bf16[64,2048]{1,0:T(8,128)(2,1)} %bitcast.28), channel_id=1, source_target_pairs={{0,2},{2,0},{1,3},{3,1},{4,6},{6,4},{5,7},{7,5},{8,10},{10,8},{9,1... | collective-permute-start | bytes 786440 | tf_op jit(solution)/shard_map/ppermute | solution.py:29
  15.1 10.6 %collective-permute-start.6 = (bf16[352,2048]{1,0:T(8,128)(2,1)}, bf16[352,2048]{1,0:T(8,128)(2,1)}, u32[]{:S(2)}, u32[]{:S(2)}) collective-permute-start(bf16[352,2048]{1,0:T(8,128)(2,1)} %bitcast.37), channel_id=1, source_target_pairs={{0,1},{1,0},{2,3},{3,2},{4,5},{5,4},{6,7},{7,6},{8,9},{9,8},{10,11... | collective-permute-start | bytes 4325384 | tf_op jit(solution)/shard_map/ppermute | solution.py:29
  15.2 10.4 %collective-permute-start.7 = (bf16[352,2048]{1,0:T(8,128)(2,1)}, bf16[352,2048]{1,0:T(8,128)(2,1)}, u32[]{:S(2)}, u32[]{:S(2)}) collective-permute-start(bf16[352,2048]{1,0:T(8,128)(2,1)} %refs_4_.1), channel_id=1, source_target_pairs={{0,1},{1,0},{2,3},{3,2},{4,5},{5,4},{6,7},{7,6},{8,9},{9,8},{10,11... | collective-permute-start | bytes 4325384 | tf_op jit(solution)/shard_map/ppermute | solution.py:29
  27.2 11.0 %collective-permute-start.9 = (bf16[2048,1408]{1,0:T(8,128)(2,1)}, bf16[2048,1408]{1,0:T(8,128)(2,1)}, u32[]{:S(2)}, u32[]{:S(2)}) collective-permute-start(bf16[2048,1408]{1,0:T(8,128)(2,1)} %bitcast.21), channel_id=1, source_target_pairs={{0,1},{1,0},{2,3},{3,2},{4,5},{5,4},{6,7},{7,6},{8,9},{9,8},{10,11... | collective-permute-start | bytes 17301512 | tf_op jit(solution)/shard_map/ppermute | solution.py:29
  28.5 8.6 %collective-permute-start.8 = (bf16[64,2048]{1,0:T(8,128)(2,1)S(1)}, bf16[64,2048]{1,0:T(8,128)(2,1)S(1)}, u32[]{:S(2)}, u32[]{:S(2)}) collective-permute-start(bf16[64,2048]{1,0:T(8,128)(2,1)S(1)} %add_convert_fusion), channel_id=1, source_target_pairs={{0,2},{2,0},{1,3},{3,1},{4,6},{6,4},{5,7},{7,5},{8,10},{10,8},{9,1... | collective-permute-start | bytes 786440 | tf_op jit(solution)/shard_map/ppermute | solution.py:29
  39.2 20.8 %collective-permute-start.12 = (bf16[64,2176]{1,0:T(8,128)(2,1)S(1)}, bf16[64,2176]{1,0:T(8,128)(2,1)S(1)}, u32[]{:S(2)}, u32[]{:S(2)}) collective-permute-start(bf16[64,2176]{1,0:T(8,128)(2,1)S(1)} %get-tuple-element.120.refs_2_), channel_id=1, source_target_pairs={{0,24},{8,16},{16,8},{24,0},{1,25},{9,17},{17,9},{25,1},{2,26},{10... | collective-permute-start | bytes 835592 | tf_op jit(solution)/shard_map/ppermute | solution.py:29
  43.1 8.6 %collective-permute-start.11 = (bf16[64,2048]{1,0:T(8,128)(2,1)S(1)}, bf16[64,2048]{1,0:T(8,128)(2,1)}, u32[]{:S(2)}, u32[]{:S(2)}) collective-permute-start(bf16[64,2048]{1,0:T(8,128)(2,1)S(1)} %get-tuple-element.115.refs_0_), channel_id=1, source_target_pairs={{0,2},{2,0},{1,3},{3,1},{4,6},{6,4},{5,7},{7,5},{8,10},{10,8},{9,1... | collective-permute-start | bytes 786440 | tf_op jit(solution)/shard_map/ppermute | solution.py:29
  45.3 22.0 %collective-permute-start.16 = (bf16[64,2176]{1,0:T(8,128)(2,1)S(1)}, bf16[64,2176]{1,0:T(8,128)(2,1)}, u32[]{:S(2)}, u32[]{:S(2)}) collective-permute-start(bf16[64,2176]{1,0:T(8,128)(2,1)S(1)} %get-tuple-element.120.refs_2_), channel_id=1, source_target_pairs={{0,16},{8,24},{16,0},{24,8},{1,17},{9,25},{17,1},{25,9},{2,18},{10... | collective-permute-start | bytes 835592 | tf_op jit(solution)/shard_map/ppermute | solution.py:29
  45.3 22.0 %collective-permute-start.17 = (bf16[64,2176]{1,0:T(8,128)(2,1)S(1)}, bf16[64,2176]{1,0:T(8,128)(2,1)}, u32[]{:S(2)}, u32[]{:S(2)}) collective-permute-start(bf16[64,2176]{1,0:T(8,128)(2,1)S(1)} %get-tuple-element.120.refs_2_), channel_id=1, source_target_pairs={{0,8},{8,0},{16,24},{24,16},{1,9},{9,1},{17,25},{25,17},{2,10},{10... | collective-permute-start | bytes 835592 | tf_op jit(solution)/shard_map/ppermute | solution.py:29
  61.7 13.1 %collective-permute-start.13 = (bf16[64,2048]{1,0:T(8,128)(2,1)S(1)}, bf16[64,2048]{1,0:T(8,128)(2,1)S(1)}, u32[]{:S(2)}, u32[]{:S(2)}) collective-permute-start(bf16[64,2048]{1,0:T(8,128)(2,1)S(1)} %get-tuple-element.125), channel_id=1, source_target_pairs={{0,2},{2,0},{4,6},{6,4},{1,3},{3,1},{5,7},{7,5},{8,10},{10,8},{12,... | collective-permute-start | bytes 786440 | tf_op jit(solution)/shard_map/ppermute | solution.py:29
  63.5 13.5 %collective-permute-start.14 = (bf16[64,2048]{1,0:T(8,128)(2,1)S(1)}, bf16[64,2048]{1,0:T(8,128)(2,1)S(1)}, u32[]{:S(2)}, u32[]{:S(2)}) collective-permute-start(bf16[64,2048]{1,0:T(8,128)(2,1)S(1)} %get-tuple-element.126), channel_id=1, source_target_pairs={{0,4},{2,6},{4,0},{6,2},{1,5},{3,7},{5,1},{7,3},{8,12},{10,14},{12... | collective-permute-start | bytes 786440 | tf_op jit(solution)/shard_map/ppermute | solution.py:29
  66.1 13.1 %collective-permute-start.15 = (bf16[64,2048]{1,0:T(8,128)(2,1)S(1)}, bf16[64,2048]{1,0:T(8,128)(2,1)S(1)}, u32[]{:S(2)}, u32[]{:S(2)}) collective-permute-start(bf16[64,2048]{1,0:T(8,128)(2,1)S(1)} %get-tuple-element.127), channel_id=1, source_target_pairs={{0,6},{2,4},{4,2},{6,0},{1,7},{3,5},{5,3},{7,1},{8,14},{10,12},{12... | collective-permute-start | bytes 786440 | tf_op jit(solution)/shard_map/ppermute | solution.py:29
  69.4 21.8 %collective-permute-start.18 = (bf16[64,2048]{1,0:T(8,128)(2,1)S(1)}, bf16[64,2048]{1,0:T(8,128)(2,1)S(1)}, u32[]{:S(2)}, u32[]{:S(2)}) collective-permute-start(bf16[64,2048]{1,0:T(8,128)(2,1)S(1)} %get-tuple-element.136), channel_id=1, source_target_pairs={{0,2},{2,0},{4,6},{6,4},{1,3},{3,1},{5,7},{7,5},{8,10},{10,8},{12,... | collective-permute-start | bytes 786440 | tf_op jit(solution)/shard_map/ppermute | solution.py:29
  70.0 23.1 %collective-permute-start.19 = (bf16[64,2048]{1,0:T(8,128)(2,1)S(1)}, bf16[64,2048]{1,0:T(8,128)(2,1)S(1)}, u32[]{:S(2)}, u32[]{:S(2)}) collective-permute-start(bf16[64,2048]{1,0:T(8,128)(2,1)S(1)} %get-tuple-element.137), channel_id=1, source_target_pairs={{0,4},{2,6},{4,0},{6,2},{1,5},{3,7},{5,1},{7,3},{8,12},{10,14},{12... | collective-permute-start | bytes 786440 | tf_op jit(solution)/shard_map/ppermute | solution.py:29
  74.8 19.5 %collective-permute-start.20 = (bf16[64,2048]{1,0:T(8,128)(2,1)S(1)}, bf16[64,2048]{1,0:T(8,128)(2,1)S(1)}, u32[]{:S(2)}, u32[]{:S(2)}) collective-permute-start(bf16[64,2048]{1,0:T(8,128)(2,1)S(1)} %get-tuple-element.138), channel_id=1, source_target_pairs={{0,6},{2,4},{4,2},{6,0},{1,7},{3,5},{5,3},{7,1},{8,14},{10,12},{12... | collective-permute-start | bytes 786440 | tf_op jit(solution)/shard_map/ppermute | solution.py:29
  77.0 17.3 %collective-permute-start.21 = (bf16[64,2048]{1,0:T(8,128)(2,1)S(1)}, bf16[64,2048]{1,0:T(8,128)(2,1)S(1)}, u32[]{:S(2)}, u32[]{:S(2)}) collective-permute-start(bf16[64,2048]{1,0:T(8,128)(2,1)S(1)} %copy-done.26), channel_id=1, source_target_pairs={{0,2},{2,0},{1,3},{3,1},{4,6},{6,4},{5,7},{7,5},{8,10},{10,8},{9,1... | collective-permute-start | bytes 786440 | tf_op jit(solution)/shard_map/ppermute | solution.py:29
  90.7 13.8 %collective-permute-start.25 = (bf16[32,2048]{1,0:T(8,128)(2,1)S(1)}, bf16[32,2048]{1,0:T(8,128)(2,1)S(1)}, u32[]{:S(2)}, u32[]{:S(2)}) collective-permute-start(bf16[32,2048]{1,0:T(8,128)(2,1)S(1)} %get-tuple-element.140), channel_id=1, source_target_pairs={{0,2},{2,0},{4,6},{6,4},{1,3},{3,1},{5,7},{7,5},{8,10},{10,8},{12,... | collective-permute-start | bytes 393224 | tf_op jit(solution)/shard_map/ppermute | solution.py:29
  91.2 13.3 %collective-permute-start.26 = (bf16[32,2048]{1,0:T(8,128)(2,1)S(1)}, bf16[32,2048]{1,0:T(8,128)(2,1)S(1)}, u32[]{:S(2)}, u32[]{:S(2)}) collective-permute-start(bf16[32,2048]{1,0:T(8,128)(2,1)S(1)} %get-tuple-element.141), channel_id=1, source_target_pairs={{0,4},{2,6},{4,0},{6,2},{1,5},{3,7},{5,1},{7,3},{8,12},{10,14},{12... | collective-permute-start | bytes 393224 | tf_op jit(solution)/shard_map/ppermute | solution.py:29
  93.1 11.4 %collective-permute-start.27 = (bf16[32,2048]{1,0:T(8,128)(2,1)S(1)}, bf16[32,2048]{1,0:T(8,128)(2,1)S(1)}, u32[]{:S(2)}, u32[]{:S(2)}) collective-permute-start(bf16[32,2048]{1,0:T(8,128)(2,1)S(1)} %get-tuple-element.142), channel_id=1, source_target_pairs={{0,6},{2,4},{4,2},{6,0},{1,7},{3,5},{5,3},{7,1},{8,14},{10,12},{12... | collective-permute-start | bytes 393224 | tf_op jit(solution)/shard_map/ppermute | solution.py:29
  101.7 6.4 %collective-permute-start.22 = (bf16[32,2048]{1,0:T(8,128)(2,1)S(1)}, bf16[32,2048]{1,0:T(8,128)(2,1)S(1)}, u32[]{:S(2)}, u32[]{:S(2)}) collective-permute-start(bf16[32,2048]{1,0:T(8,128)(2,1)S(1)} %get-tuple-element.149), channel_id=1, source_target_pairs={{0,2},{2,0},{4,6},{6,4},{1,3},{3,1},{5,7},{7,5},{8,10},{10,8},{12,... | collective-permute-start | bytes 393224 | tf_op jit(solution)/shard_map/ppermute | solution.py:29
  102.3 9.0 %collective-permute-start.23 = (bf16[32,2048]{1,0:T(8,128)(2,1)S(1)}, bf16[32,2048]{1,0:T(8,128)(2,1)S(1)}, u32[]{:S(2)}, u32[]{:S(2)}) collective-permute-start(bf16[32,2048]{1,0:T(8,128)(2,1)S(1)} %get-tuple-element.150), channel_id=1, source_target_pairs={{0,4},{2,6},{4,0},{6,2},{1,5},{3,7},{5,1},{7,3},{8,12},{10,14},{12... | collective-permute-start | bytes 393224 | tf_op jit(solution)/shard_map/ppermute | solution.py:29
  104.8 19.4 %collective-permute-start.28 = (bf16[64,2048]{1,0:T(8,128)(2,1)S(1)}, bf16[64,2048]{1,0:T(8,128)(2,1)S(1)}, u32[]{:S(2)}, u32[]{:S(2)}) collective-permute-start(bf16[64,2048]{1,0:T(8,128)(2,1)S(1)} %combine.5), channel_id=1, source_target_pairs={{0,24},{8,16},{16,8},{24,0},{1,25},{9,17},{17,9},{25,1},{2,26},{10... | collective-permute-start | bytes 786440 | tf_op jit(solution)/shard_map/ppermute | solution.py:29
  105.4 9.5 %collective-permute-start.24 = (bf16[32,2048]{1,0:T(8,128)(2,1)S(1)}, bf16[32,2048]{1,0:T(8,128)(2,1)S(1)}, u32[]{:S(2)}, u32[]{:S(2)}) collective-permute-start(bf16[32,2048]{1,0:T(8,128)(2,1)S(1)} %get-tuple-element.151), channel_id=1, source_target_pairs={{0,6},{2,4},{4,2},{6,0},{1,7},{3,5},{5,3},{7,1},{8,14},{10,12},{12... | collective-permute-start | bytes 393224 | tf_op jit(solution)/shard_map/ppermute | solution.py:29
  106.7 14.0 %collective-permute-start.33 = (bf16[32,2048]{1,0:T(8,128)(2,1)S(1)}, bf16[32,2048]{1,0:T(8,128)(2,1)S(1)}, u32[]{:S(2)}, u32[]{:S(2)}) collective-permute-start(bf16[32,2048]{1,0:T(8,128)(2,1)S(1)} %get-tuple-element.169), channel_id=1, source_target_pairs={{0,2},{2,0},{4,6},{6,4},{1,3},{3,1},{5,7},{7,5},{8,10},{10,8},{12,... | collective-permute-start | bytes 393224 | tf_op jit(solution)/shard_map/ppermute | solution.py:29
  108.1 12.6 %collective-permute-start.34 = (bf16[32,2048]{1,0:T(8,128)(2,1)S(1)}, bf16[32,2048]{1,0:T(8,128)(2,1)S(1)}, u32[]{:S(2)}, u32[]{:S(2)}) collective-permute-start(bf16[32,2048]{1,0:T(8,128)(2,1)S(1)} %get-tuple-element.170), channel_id=1, source_target_pairs={{0,4},{2,6},{4,0},{6,2},{1,5},{3,7},{5,1},{7,3},{8,12},{10,14},{12... | collective-permute-start | bytes 393224 | tf_op jit(solution)/shard_map/ppermute | solution.py:29
  111.3 9.4 %collective-permute-start.35 = (bf16[32,2048]{1,0:T(8,128)(2,1)S(1)}, bf16[32,2048]{1,0:T(8,128)(2,1)S(1)}, u32[]{:S(2)}, u32[]{:S(2)}) collective-permute-start(bf16[32,2048]{1,0:T(8,128)(2,1)S(1)} %get-tuple-element.171), channel_id=1, source_target_pairs={{0,6},{2,4},{4,2},{6,0},{1,7},{3,5},{5,3},{7,1},{8,14},{10,12},{12... | collective-permute-start | bytes 393224 | tf_op jit(solution)/shard_map/ppermute | solution.py:29
  115.1 17.8 %collective-permute-start.32 = (bf16[64,2048]{1,0:T(8,128)(2,1)S(1)}, bf16[64,2048]{1,0:T(8,128)(2,1)S(1)}, u32[]{:S(2)}, u32[]{:S(2)}) collective-permute-start(bf16[64,2048]{1,0:T(8,128)(2,1)S(1)} %combine.4), channel_id=1, source_target_pairs={{0,16},{8,24},{16,0},{24,8},{1,17},{9,25},{17,1},{25,9},{2,18},{10... | collective-permute-start | bytes 786440 | tf_op jit(solution)/shard_map/ppermute | solution.py:29
  120.9 12.0 %collective-permute-start.36 = (bf16[64,2048]{1,0:T(8,128)(2,1)S(1)}, bf16[64,2048]{1,0:T(8,128)(2,1)S(1)}, u32[]{:S(2)}, u32[]{:S(2)}) collective-permute-start(bf16[64,2048]{1,0:T(8,128)(2,1)S(1)} %combine.7), channel_id=1, source_target_pairs={{0,8},{8,0},{16,24},{24,16},{1,9},{9,1},{17,25},{25,17},{2,10},{10... | collective-permute-start | bytes 786440 | tf_op jit(solution)/shard_map/ppermute | solution.py:29
  124.2 5.8 %collective-permute-start.29 = (bf16[32,2048]{1,0:T(8,128)(2,1)S(1)}, bf16[32,2048]{1,0:T(8,128)(2,1)S(1)}, u32[]{:S(2)}, u32[]{:S(2)}) collective-permute-start(bf16[32,2048]{1,0:T(8,128)(2,1)S(1)} %copy-done.18), channel_id=1, source_target_pairs={{0,2},{2,0},{4,6},{6,4},{1,3},{3,1},{5,7},{7,5},{8,10},{10,8},{12,... | collective-permute-start | bytes 393224 | tf_op jit(solution)/shard_map/ppermute | solution.py:29
  126.3 6.4 %collective-permute-start.30 = (bf16[32,2048]{1,0:T(8,128)(2,1)S(1)}, bf16[32,2048]{1,0:T(8,128)(2,1)S(1)}, u32[]{:S(2)}, u32[]{:S(2)}) collective-permute-start(bf16[32,2048]{1,0:T(8,128)(2,1)S(1)} %get-tuple-element.159), channel_id=1, source_target_pairs={{0,4},{2,6},{4,0},{6,2},{1,5},{3,7},{5,1},{7,3},{8,12},{10,14},{12... | collective-permute-start | bytes 393224 | tf_op jit(solution)/shard_map/ppermute | solution.py:29
  126.3 6.4 %collective-permute-start.31 = (bf16[32,2048]{1,0:T(8,128)(2,1)S(1)}, bf16[32,2048]{1,0:T(8,128)(2,1)S(1)}, u32[]{:S(2)}, u32[]{:S(2)}) collective-permute-start(bf16[32,2048]{1,0:T(8,128)(2,1)S(1)} %get-tuple-element.160), channel_id=1, source_target_pairs={{0,6},{2,4},{4,2},{6,0},{1,7},{3,5},{5,3},{7,1},{8,14},{10,12},{12... | collective-permute-start | bytes 393224 | tf_op jit(solution)/shard_map/ppermute | solution.py:29
  (33 other events, 423.2 us)

commit v15 on v14

--- a/solution.py
+++ b/solution.py
@@ -16,6 +16,7 @@
 BACK = ((3, None, None), (2, None, None), (1, 3, None), (0, 2, 3))
 CHUNK = 512
 EXTRA = 128
+LARGE = pl.CostEstimate(flops=23000000000, bytes_accessed=72000000, transcendentals=0)
 SMALL = pl.CostEstimate(flops=1024, bytes_accessed=1024, transcendentals=0)
 ALL = ("z", "y", "x", "c")
 PLANE = ("y", "x")
@@ -460,7 +461,7 @@
             outs[o][i * capacity : (i + 1) * capacity] = chosen[o * capacity : (o + 1) * capacity]
 
 
-def select(near, router, sources, plane, capacity, top_count):
+def select(near, router, sources, plane, capacity, top_count, cost):
     tree = sources[0].shape[0]
     width = router.shape[0]
     count = len(sources)
@@ -473,7 +474,7 @@
         out_shape=[jax.ShapeDtypeStruct((count * capacity, width), jnp.bfloat16)] * plane
         + [jax.ShapeDtypeStruct((tree, plane * capacity), jnp.bfloat16)] * count,
         compiler_params=pltpu.CompilerParams(vmem_limit_bytes=16 * 2**20),
-        cost_estimate=SMALL,
+        cost_estimate=cost,
         name="select",
     )(near, router, *sources)
     return list(made[:plane]), list(made[plane:])
@@ -629,7 +630,13 @@
     spread = {}
     for ks in GROUPS:
         pieces, spreads = select(
-            near_experts, router, [line_rows[k] for k in ks], plane, capacity, top_count
+            near_experts,
+            router,
+            [line_rows[k] for k in ks],
+            plane,
+            capacity,
+            top_count,
+            LARGE if sent else SMALL,
         )
         spread.update(zip(ks, spreads))
         sent.append([partner(pieces[o], PLANE, o) for o in range(plane)])

time: 134 us -> 135 us (level)
  waiting for transfers between devices: 18.4 us -> 27.3 us
  starting transfers between devices: 52.4 us -> 46.7 us
  local copies, waits for them, and re-layouts: 12.4 us -> 9.37 us
    ppermute x37, waiting for transfers between devices: 18.4 us -> 27.3 us  [partner(): return lax.ppermute(value, axes, [(i, i ^ offset) for i in range(size)])]
    ppermute x37, starting transfers between devices: 52.4 us -> 46.7 us  [partner(): return lax.ppermute(value, axes, [(i, i ^ offset) for i in range(size)])]
    unnamed x58 -> x64, local copies, waits for them, and re-layouts: 10.6 us -> 7.56 us
  transfers between devices with their start and end apart: 37 -> 37, of which waited for: 11 -> 12; matrix products, arithmetic and copies ran while one was open for 4% -> 4% of each run, Pallas kernels for 34% -> 34%
where the time goes in v15:
time: 135 us
  Pallas kernels  47.6 us (35%)
  starting transfers between devices  46.7 us (35%)
  waiting for transfers between devices  27.3 us (20%)
  local copies, waits for them, and re-layouts  9.37 us (7%)
  other arithmetic  2.92 us (2%)
    ppermute x37, starting transfers between devices, partner(): return lax.ppermute(value, axes, [(i, i ^ offset) for i in range(size)])  46.7 us
    ppermute x37, waiting for transfers between devices, partner(): return lax.ppermute(value, axes, [(i, i ^ offset) for i in range(size)])  27.3 us
    pallas_call x2, Pallas kernels, attend(): pl.pallas_call(functools.partial(attend_kernel, offset=offset), in_specs=...  14.7 us
    pallas_call x2, Pallas kernels, experts(): pl.pallas_call(functools.partial(expert_kernel, plane=plane, count=count,...  14.6 us
    pallas_call x1, Pallas kernels, shared_terms(): pl.pallas_call(functools.partial(shared_kernel, side=side), in_specs=[in_...  8.21 us
    unnamed x64, local copies, waits for them, and re-layouts  7.56 us
    pallas_call x2, Pallas kernels, select(): pl.pallas_call(functools.partial(select_kernel, count=count, plane=plane,...  5.12 us
  transfers between devices with their start and end apart: 37, of which 12 were waited for; matrix products, arithmetic and copies ran while one was open for 4% of the time, Pallas kernels for 34%

profile of v15, /device:TPU:0, one launch (start us, length us, event | category | flops | bytes accessed | tf_op | source)
XLA Modules:
  0.0 135.2 jit_solution(11023903195988716667)
XLA Ops:
  1.2 1.4 %collective-permute-done.1.second = bf16[64,2048]{1,0:T(8,128)(2,1)S(1)} collective-permute-done((bf16[64,2048]{1,0:T(8,128)(2,1)}, bf16[64,2048]{1,0:T(8,128)(2,1)S(1)}, u32[]{:S(2)}, u32[]{:S(2)}) %collective-permute-start.1) | collective-permute-done | bytes 262176 | tf_op jit(solution)/shard_map/ppermute | solution.py:30
  2.9 2.6 %collective-permute-start = (bf16[64,2048]{1,0:T(8,128)(2,1)}, bf16[64,2048]{1,0:T(8,128)(2,1)S(1)}, u32[]{:S(2)}, u32[]{:S(2)}) collective-permute-start(bf16[64,2048]{1,0:T(8,128)(2,1)} %bitcast.30), channel_id=1, source_target_pairs={{0,2},{2,0},{1,3},{3,1},{4,6},{6,4},{5,7},{7,5},{8,10},{10,8},{9,1... | collective-permute-start | bytes 786440 | tf_op jit(solution)/shard_map/ppermute | solution.py:30
  7.5 2.0 %prepare.1 = (f32[4,64,64]{2,1,0:T(8,128)S(1)}, f32[4,64,128]{2,1,0:T(8,128)S(1)}, f32[4,64,128]{2,1,0:T(8,128)S(1)}) custom-call(s32[4]{0:T(128)S(1)} %copy-done.10, s32[4,64]{1,0:T(4,128)S(1)} %copy-done.11, f32[1,128]{1,0:T(1,128)S(1)} %copy-done.12), custom_call_target="tpu_custom_call" | custom-call | flops 1024 | bytes 1024 | tf_op jit(solution)/shard_map/prepare/pallas_call | solution.py:69
  12.6 2.5 %collective-permute-done.2.second = bf16[64,2048]{1,0:T(8,128)(2,1)S(1)} collective-permute-done((bf16[64,2048]{1,0:T(8,128)(2,1)S(1)}, bf16[64,2048]{1,0:T(8,128)(2,1)S(1)}, u32[]{:S(2)}, u32[]{:S(2)}) %collective-permute-start.2) | collective-permute-done | bytes 262176 | tf_op jit(solution)/shard_map/ppermute | solution.py:30
  16.7 7.5 %attend.2 = (f32[64,2048]{1,0:T(8,128)}, bf16[64,2048]{1,0:T(8,128)(2,1)}, bf16[64,256]{1,0:T(8,128)(2,1)}, bf16[64,256]{1,0:T(8,128)(2,1)}) custom-call(s32[1]{0:T(128)} %bitcast.2.place, s32[4]{0:T(128)} %lengths.5, bf16[64,2048]{1,0:T(8,128)(2,1)} %copy-done.19, bf16[64,2048]{1,0:T(8,128)(2,1)} %copy-done.20, f32[1,2048]{1,0:T(1,128)} %bitcast.42, ...), custom_call_target="tpu_custom_call" | custom-call | flops 1024 | bytes 1024 | tf_op jit(solution)/shard_map/attend/pallas_call | solution.py:205
  24.5 1.6 %collective-permute-done.5 = bf16[64,2048]{1,0:T(8,128)(2,1)S(1)} collective-permute-done((bf16[64,2048]{1,0:T(8,128)(2,1)}, bf16[64,2048]{1,0:T(8,128)(2,1)S(1)}, u32[]{:S(2)}, u32[]{:S(2)}) %collective-permute-start.5) | collective-permute-done | bytes 262176 | tf_op jit(solution)/shard_map/ppermute | solution.py:30
  26.2 1.8 %add_convert_fusion = bf16[64,2048]{1,0:T(8,128)(2,1)} fusion(f32[64,2048]{1,0:T(8,128)} %get-tuple-element.104, bf16[64,2048]{1,0:T(8,128)(2,1)S(1)} %collective-permute-done.5), kind=kLoop, calls=%fused_computation.4 | loop fusion | flops 393216 | bytes 1048576 | tf_op jit(solution)/shard_map/convert_element_type | solution.py:596
  28.6 7.2 %attend.3 = (f32[64,2048]{1,0:T(8,128)}, bf16[64,2048]{1,0:T(8,128)(2,1)}, bf16[64,256]{1,0:T(8,128)(2,1)}, bf16[64,256]{1,0:T(8,128)(2,1)}) custom-call(s32[1]{0:T(128)} %bitcast.2.place, s32[4]{0:T(128)} %lengths.5, bf16[64,2048]{1,0:T(8,128)(2,1)} %bitcast.31, bf16[64,2048]{1,0:T(8,128)(2,1)} %copy-done.18, f32[1,2048]{1,0:T(1,128)} %bitcast.43, ...), custom_call_target="tpu_custom_call" | custom-call | flops 1024 | bytes 1024 | tf_op jit(solution)/shard_map/attend/pallas_call | solution.py:205
  39.7 3.6 %collective-permute-start.12 = (bf16[64,2176]{1,0:T(8,128)(2,1)}, bf16[64,2176]{1,0:T(8,128)(2,1)}, u32[]{:S(2)}, u32[]{:S(2)}) collective-permute-start(bf16[64,2176]{1,0:T(8,128)(2,1)} %get-tuple-element.120.refs_2_), channel_id=1, source_target_pairs={{0,24},{8,16},{16,8},{24,0},{1,25},{9,17},{17,9},{25,1},{2,26},{10... | collective-permute-start | bytes 835592 | tf_op jit(solution)/shard_map/ppermute | solution.py:30
  43.3 3.4 %collective-permute-start.16 = (bf16[64,2176]{1,0:T(8,128)(2,1)}, bf16[64,2176]{1,0:T(8,128)(2,1)}, u32[]{:S(2)}, u32[]{:S(2)}) collective-permute-start(bf16[64,2176]{1,0:T(8,128)(2,1)} %get-tuple-element.120.refs_2_), channel_id=1, source_target_pairs={{0,16},{8,24},{16,0},{24,8},{1,17},{9,25},{17,1},{25,9},{2,18},{10... | collective-permute-start | bytes 835592 | tf_op jit(solution)/shard_map/ppermute | solution.py:30
  47.5 7.8 %collective-permute-done.11.refs_1_ = bf16[64,2048]{1,0:T(8,128)(2,1)} collective-permute-done((bf16[64,2048]{1,0:T(8,128)(2,1)}, bf16[64,2048]{1,0:T(8,128)(2,1)}, u32[]{:S(2)}, u32[]{:S(2)}) %collective-permute-start.11) | collective-permute-done | bytes 262176 | tf_op jit(solution)/shard_map/ppermute | solution.py:30
  55.3 8.2 %shared.1 = (f32[64,2048]{1,0:T(8,128)}, bf16[64,2048]{1,0:T(8,128)(2,1)}) custom-call(bf16[64,2048]{1,0:T(8,128)(2,1)} %get-tuple-element.115.refs_0_, bf16[64,2048]{1,0:T(8,128)(2,1)} %collective-permute-done.11.refs_1_, bf16[352,2048]{1,0:T(8,128)(2,1)} %bitcast.38, bf16[352,2048]{1,0:T(8,128)(2,1)} %bitcast.40, bf16[352,2048]{1,0:T(8,128)(2,1)} %refs_4_.1, ...), custom_call_target="tpu_custom_call" | custom-call | flops 1024 | bytes 1024 | tf_op jit(solution)/shard_map/shared/pallas_call | solution.py:361
  63.6 2.2 %select.2 = (bf16[64,2048]{1,0:T(8,128)(2,1)S(1)}, bf16[64,2048]{1,0:T(8,128)(2,1)S(1)}, bf16[64,2048]{1,0:T(8,128)(2,1)S(1)}, bf16[64,2048]{1,0:T(8,128)(2,1)S(...) custom-call(s32[4]{0:T(128)S(1)} %xor_add_fusion.refs_0_, bf16[2048,16]{1,0:T(8,128)(2,1)S(1)} %copy.21.refs_1_, ...), custom_call_target="tpu_custom_call" | custom-call | flops 1024 | bytes 1024 | tf_op jit(solution)/shard_map/select/pallas_call | solution.py:468
  66.1 1.5 %collective-permute-start.14 = (bf16[64,2048]{1,0:T(8,128)(2,1)S(1)}, bf16[64,2048]{1,0:T(8,128)(2,1)S(1)}, u32[]{:S(2)}, u32[]{:S(2)}) collective-permute-start(bf16[64,2048]{1,0:T(8,128)(2,1)S(1)} %get-tuple-element.126), channel_id=1, source_target_pairs={{0,4},{2,6},{4,0},{6,2},{1,5},{3,7},{5,1},{7,3},{8,12},{10,14},{12... | collective-permute-start | bytes 786440 | tf_op jit(solution)/shard_map/ppermute | solution.py:30
  67.6 1.8 %collective-permute-start.15 = (bf16[64,2048]{1,0:T(8,128)(2,1)S(1)}, bf16[64,2048]{1,0:T(8,128)(2,1)S(1)}, u32[]{:S(2)}, u32[]{:S(2)}) collective-permute-start(bf16[64,2048]{1,0:T(8,128)(2,1)S(1)} %get-tuple-element.127), channel_id=1, source_target_pairs={{0,6},{2,4},{4,2},{6,0},{1,7},{3,5},{5,3},{7,1},{8,14},{10,12},{12... | collective-permute-start | bytes 786440 | tf_op jit(solution)/shard_map/ppermute | solution.py:30
  69.4 3.0 %select.3 = (bf16[64,2048]{1,0:T(8,128)(2,1)S(1)}, bf16[64,2048]{1,0:T(8,128)(2,1)S(1)}, bf16[64,2048]{1,0:T(8,128)(2,1)S(1)}, bf16[64,2048]{1,0:T(8,128)(2,1)S(...) custom-call(s32[4]{0:T(128)S(1)} %xor_add_fusion.refs_0_, bf16[2048,16]{1,0:T(8,128)(2,1)S(1)} %copy.21.refs_1_, ...), custom_call_target="tpu_custom_call" | custom-call | flops 23000000512 | bytes 72000000 | tf_op jit(solution)/shard_map/select/pallas_call | solution.py:468
  72.8 1.5 %collective-permute-start.19 = (bf16[64,2048]{1,0:T(8,128)(2,1)S(1)}, bf16[64,2048]{1,0:T(8,128)(2,1)S(1)}, u32[]{:S(2)}, u32[]{:S(2)}) collective-permute-start(bf16[64,2048]{1,0:T(8,128)(2,1)S(1)} %get-tuple-element.137), channel_id=1, source_target_pairs={{0,4},{2,6},{4,0},{6,2},{1,5},{3,7},{5,1},{7,3},{8,12},{10,14},{12... | collective-permute-start | bytes 786440 | tf_op jit(solution)/shard_map/ppermute | solution.py:30
  76.3 4.1 %collective-permute-start.21 = (bf16[64,2048]{1,0:T(8,128)(2,1)S(1)}, bf16[64,2048]{1,0:T(8,128)(2,1)S(1)}, u32[]{:S(2)}, u32[]{:S(2)}) collective-permute-start(bf16[64,2048]{1,0:T(8,128)(2,1)S(1)} %copy-done.24), channel_id=1, source_target_pairs={{0,2},{2,0},{1,3},{3,1},{4,6},{6,4},{5,7},{7,5},{8,10},{10,8},{9,1... | collective-permute-start | bytes 786440 | tf_op jit(solution)/shard_map/ppermute | solution.py:30
  81.5 7.3 %expert.2 = (bf16[32,2048]{1,0:T(8,128)(2,1)S(1)}, bf16[32,2048]{1,0:T(8,128)(2,1)S(1)}, bf16[32,2048]{1,0:T(8,128)(2,1)S(1)}, bf16[32,2048]{1,0:T(8,128)(2,1)S(...) custom-call(bf16[64,2048]{1,0:T(8,128)(2,1)S(1)} %get-tuple-element., ...), custom_call_target="tpu_custom_call" | custom-call | flops 1024 | bytes 1024 | tf_op jit(solution)/shard_map/expert/pallas_call | solution.py:303
  91.1 2.5 %collective-permute-start.27 = (bf16[32,2048]{1,0:T(8,128)(2,1)S(1)}, bf16[32,2048]{1,0:T(8,128)(2,1)S(1)}, u32[]{:S(2)}, u32[]{:S(2)}) collective-permute-start(bf16[32,2048]{1,0:T(8,128)(2,1)S(1)} %get-tuple-element.142), channel_id=1, source_target_pairs={{0,6},{2,4},{4,2},{6,0},{1,7},{3,5},{5,3},{7,1},{8,14},{10,12},{12... | collective-permute-start | bytes 393224 | tf_op jit(solution)/shard_map/ppermute | solution.py:30
  93.6 3.9 %collective-permute-done.21.refs_0_ = bf16[64,2048]{1,0:T(8,128)(2,1)S(1)} collective-permute-done((bf16[64,2048]{1,0:T(8,128)(2,1)S(1)}, bf16[64,2048]{1,0:T(8,128)(2,1)S(1)}, u32[]{:S(2)}, u32[]{:S(2)}) %collective-permute-start.21) | collective-permute-done | bytes 262176 | tf_op jit(solution)/shard_map/ppermute | solution.py:30
  97.5 7.3 %expert.3 = (bf16[32,2048]{1,0:T(8,128)(2,1)S(1)}, bf16[32,2048]{1,0:T(8,128)(2,1)S(1)}, bf16[32,2048]{1,0:T(8,128)(2,1)S(1)}, bf16[32,2048]{1,0:T(8,128)(2,1)S(...) custom-call(bf16[64,2048]{1,0:T(8,128)(2,1)S(1)} %get-tuple-element., ...), custom_call_target="tpu_custom_call" | custom-call | flops 1024 | bytes 1024 | tf_op jit(solution)/shard_map/expert/pallas_call | solution.py:303
  105.4 1.4 %collective-permute-start.23 = (bf16[32,2048]{1,0:T(8,128)(2,1)S(1)}, bf16[32,2048]{1,0:T(8,128)(2,1)S(1)}, u32[]{:S(2)}, u32[]{:S(2)}) collective-permute-start(bf16[32,2048]{1,0:T(8,128)(2,1)S(1)} %get-tuple-element.150), channel_id=1, source_target_pairs={{0,4},{2,6},{4,0},{6,2},{1,5},{3,7},{5,1},{7,3},{8,12},{10,14},{12... | collective-permute-start | bytes 393224 | tf_op jit(solution)/shard_map/ppermute | solution.py:30
  107.0 1.5 %collective-permute-start.28 = (bf16[64,2048]{1,0:T(8,128)(2,1)S(1)}, bf16[64,2048]{1,0:T(8,128)(2,1)S(1)}, u32[]{:S(2)}, u32[]{:S(2)}) collective-permute-start(bf16[64,2048]{1,0:T(8,128)(2,1)S(1)} %combine.5), channel_id=1, source_target_pairs={{0,24},{8,16},{16,8},{24,0},{1,25},{9,17},{17,9},{25,1},{2,26},{10... | collective-permute-start | bytes 786440 | tf_op jit(solution)/shard_map/ppermute | solution.py:30
  108.5 2.6 %collective-permute-start.24 = (bf16[32,2048]{1,0:T(8,128)(2,1)S(1)}, bf16[32,2048]{1,0:T(8,128)(2,1)S(1)}, u32[]{:S(2)}, u32[]{:S(2)}) collective-permute-start(bf16[32,2048]{1,0:T(8,128)(2,1)S(1)} %get-tuple-element.151), channel_id=1, source_target_pairs={{0,6},{2,4},{4,2},{6,0},{1,7},{3,5},{5,3},{7,1},{8,14},{10,12},{12... | collective-permute-start | bytes 393224 | tf_op jit(solution)/shard_map/ppermute | solution.py:30
  112.8 1.8 %collective-permute-start.35 = (bf16[32,2048]{1,0:T(8,128)(2,1)S(1)}, bf16[32,2048]{1,0:T(8,128)(2,1)S(1)}, u32[]{:S(2)}, u32[]{:S(2)}) collective-permute-start(bf16[32,2048]{1,0:T(8,128)(2,1)S(1)} %get-tuple-element.171), channel_id=1, source_target_pairs={{0,6},{2,4},{4,2},{6,0},{1,7},{3,5},{5,3},{7,1},{8,14},{10,12},{12... | collective-permute-start | bytes 393224 | tf_op jit(solution)/shard_map/ppermute | solution.py:30
  114.9 2.0 %collective-permute-start.32 = (bf16[64,2048]{1,0:T(8,128)(2,1)S(1)}, bf16[64,2048]{1,0:T(8,128)(2,1)S(1)}, u32[]{:S(2)}, u32[]{:S(2)}) collective-permute-start(bf16[64,2048]{1,0:T(8,128)(2,1)S(1)} %combine.4), channel_id=1, source_target_pairs={{0,16},{8,24},{16,0},{24,8},{1,17},{9,25},{17,1},{25,9},{2,18},{10... | collective-permute-start | bytes 786440 | tf_op jit(solution)/shard_map/ppermute | solution.py:30
  116.9 1.9 %collective-permute-done.35.refs_3_ = bf16[32,2048]{1,0:T(8,128)(2,1)S(1)} collective-permute-done((bf16[32,2048]{1,0:T(8,128)(2,1)S(1)}, bf16[32,2048]{1,0:T(8,128)(2,1)S(1)}, u32[]{:S(2)}, u32[]{:S(2)}) %collective-permute-start.35) | collective-permute-done | bytes 131104 | tf_op jit(solution)/shard_map/ppermute | solution.py:30
  118.9 4.2 %collective-permute-start.36 = (bf16[64,2048]{1,0:T(8,128)(2,1)S(1)}, bf16[64,2048]{1,0:T(8,128)(2,1)S(1)}, u32[]{:S(2)}, u32[]{:S(2)}) collective-permute-start(bf16[64,2048]{1,0:T(8,128)(2,1)S(1)} %combine.7), channel_id=1, source_target_pairs={{0,8},{8,0},{16,24},{24,16},{1,9},{9,1},{17,25},{25,17},{2,10},{10... | collective-permute-start | bytes 786440 | tf_op jit(solution)/shard_map/ppermute | solution.py:30
  124.1 3.8 %collective-permute-start.30 = (bf16[32,2048]{1,0:T(8,128)(2,1)S(1)}, bf16[32,2048]{1,0:T(8,128)(2,1)S(1)}, u32[]{:S(2)}, u32[]{:S(2)}) collective-permute-start(bf16[32,2048]{1,0:T(8,128)(2,1)S(1)} %copy-done.14), channel_id=1, source_target_pairs={{0,4},{2,6},{4,0},{6,2},{1,5},{3,7},{5,1},{7,3},{8,12},{10,14},{12... | collective-permute-start | bytes 393224 | tf_op jit(solution)/shard_map/ppermute | solution.py:30
  129.3 2.5 %collective-permute-done.30.refs_2_ = bf16[32,2048]{1,0:T(8,128)(2,1)S(1)} collective-permute-done((bf16[32,2048]{1,0:T(8,128)(2,1)S(1)}, bf16[32,2048]{1,0:T(8,128)(2,1)S(1)}, u32[]{:S(2)}, u32[]{:S(2)}) %collective-permute-start.30) | collective-permute-done | bytes 131104 | tf_op jit(solution)/shard_map/ppermute | solution.py:30
  131.9 1.9 %collective-permute-done.31.refs_3_ = bf16[32,2048]{1,0:T(8,128)(2,1)S(1)} collective-permute-done((bf16[32,2048]{1,0:T(8,128)(2,1)S(1)}, bf16[32,2048]{1,0:T(8,128)(2,1)S(1)}, u32[]{:S(2)}, u32[]{:S(2)}) %collective-permute-start.31) | collective-permute-done | bytes 131104 | tf_op jit(solution)/shard_map/ppermute | solution.py:30
  (130 shorter events, 25.9 us)
Async XLA Ops:
  2.5 13.1 %collective-permute-start.4 = (bf16[704,2048]{1,0:T(8,128)(2,1)}, bf16[704,2048]{1,0:T(8,128)(2,1)S(1)}, u32[]{:S(2)}, u32[]{:S(2)}) collective-permute-start(bf16[704,2048]{1,0:T(8,128)(2,1)} %bitcast.26), channel_id=1, source_target_pairs={{0,1},{1,0},{2,3},{3,2},{4,5},{5,4},{6,7},{7,6},{8,9},{9,8},{10,11... | collective-permute-start | bytes 8650760 | tf_op jit(solution)/shard_map/ppermute | solution.py:30
  2.9 9.7 %collective-permute-start = (bf16[64,2048]{1,0:T(8,128)(2,1)}, bf16[64,2048]{1,0:T(8,128)(2,1)S(1)}, u32[]{:S(2)}, u32[]{:S(2)}) collective-permute-start(bf16[64,2048]{1,0:T(8,128)(2,1)} %bitcast.30), channel_id=1, source_target_pairs={{0,2},{2,0},{1,3},{3,1},{4,6},{6,4},{5,7},{7,5},{8,10},{10,8},{9,1... | collective-permute-start | bytes 786440 | tf_op jit(solution)/shard_map/ppermute | solution.py:30
  15.1 9.4 %collective-permute-start.6 = (bf16[352,2048]{1,0:T(8,128)(2,1)}, bf16[352,2048]{1,0:T(8,128)(2,1)}, u32[]{:S(2)}, u32[]{:S(2)}) collective-permute-start(bf16[352,2048]{1,0:T(8,128)(2,1)} %bitcast.39), channel_id=1, source_target_pairs={{0,1},{1,0},{2,3},{3,2},{4,5},{5,4},{6,7},{7,6},{8,9},{9,8},{10,11... | collective-permute-start | bytes 4325384 | tf_op jit(solution)/shard_map/ppermute | solution.py:30
  15.2 9.2 %collective-permute-start.7 = (bf16[352,2048]{1,0:T(8,128)(2,1)}, bf16[352,2048]{1,0:T(8,128)(2,1)}, u32[]{:S(2)}, u32[]{:S(2)}) collective-permute-start(bf16[352,2048]{1,0:T(8,128)(2,1)} %refs_4_.1), channel_id=1, source_target_pairs={{0,1},{1,0},{2,3},{3,2},{4,5},{5,4},{6,7},{7,6},{8,9},{9,8},{10,11... | collective-permute-start | bytes 4325384 | tf_op jit(solution)/shard_map/ppermute | solution.py:30
  26.1 11.8 %collective-permute-start.9 = (bf16[2048,1408]{1,0:T(8,128)(2,1)}, bf16[2048,1408]{1,0:T(8,128)(2,1)}, u32[]{:S(2)}, u32[]{:S(2)}) collective-permute-start(bf16[2048,1408]{1,0:T(8,128)(2,1)} %bitcast.21), channel_id=1, source_target_pairs={{0,1},{1,0},{2,3},{3,2},{4,5},{5,4},{6,7},{7,6},{8,9},{9,8},{10,11... | collective-permute-start | bytes 17301512 | tf_op jit(solution)/shard_map/ppermute | solution.py:30
  28.0 8.8 %collective-permute-start.8 = (bf16[64,2048]{1,0:T(8,128)(2,1)}, bf16[64,2048]{1,0:T(8,128)(2,1)S(1)}, u32[]{:S(2)}, u32[]{:S(2)}) collective-permute-start(bf16[64,2048]{1,0:T(8,128)(2,1)} %add_convert_fusion), channel_id=1, source_target_pairs={{0,2},{2,0},{1,3},{3,1},{4,6},{6,4},{5,7},{7,5},{8,10},{10,8},{9,1... | collective-permute-start | bytes 786440 | tf_op jit(solution)/shard_map/ppermute | solution.py:30
  39.7 23.9 %collective-permute-start.12 = (bf16[64,2176]{1,0:T(8,128)(2,1)}, bf16[64,2176]{1,0:T(8,128)(2,1)}, u32[]{:S(2)}, u32[]{:S(2)}) collective-permute-start(bf16[64,2176]{1,0:T(8,128)(2,1)} %get-tuple-element.120.refs_2_), channel_id=1, source_target_pairs={{0,24},{8,16},{16,8},{24,0},{1,25},{9,17},{17,9},{25,1},{2,26},{10... | collective-permute-start | bytes 835592 | tf_op jit(solution)/shard_map/ppermute | solution.py:30
  43.3 26.1 %collective-permute-start.16 = (bf16[64,2176]{1,0:T(8,128)(2,1)}, bf16[64,2176]{1,0:T(8,128)(2,1)}, u32[]{:S(2)}, u32[]{:S(2)}) collective-permute-start(bf16[64,2176]{1,0:T(8,128)(2,1)} %get-tuple-element.120.refs_2_), channel_id=1, source_target_pairs={{0,16},{8,24},{16,0},{24,8},{1,17},{9,25},{17,1},{25,9},{2,18},{10... | collective-permute-start | bytes 835592 | tf_op jit(solution)/shard_map/ppermute | solution.py:30
  46.7 22.7 %collective-permute-start.17 = (bf16[64,2176]{1,0:T(8,128)(2,1)}, bf16[64,2176]{1,0:T(8,128)(2,1)}, u32[]{:S(2)}, u32[]{:S(2)}) collective-permute-start(bf16[64,2176]{1,0:T(8,128)(2,1)} %get-tuple-element.120.refs_2_), channel_id=1, source_target_pairs={{0,8},{8,0},{16,24},{24,16},{1,9},{9,1},{17,25},{25,17},{2,10},{10... | collective-permute-start | bytes 835592 | tf_op jit(solution)/shard_map/ppermute | solution.py:30
  47.2 8.1 %collective-permute-start.11 = (bf16[64,2048]{1,0:T(8,128)(2,1)}, bf16[64,2048]{1,0:T(8,128)(2,1)}, u32[]{:S(2)}, u32[]{:S(2)}) collective-permute-start(bf16[64,2048]{1,0:T(8,128)(2,1)} %get-tuple-element.115.refs_0_), channel_id=1, source_target_pairs={{0,2},{2,0},{1,3},{3,1},{4,6},{6,4},{5,7},{7,5},{8,10},{10,8},{9,1... | collective-permute-start | bytes 786440 | tf_op jit(solution)/shard_map/ppermute | solution.py:30
  65.7 9.3 %collective-permute-start.13 = (bf16[64,2048]{1,0:T(8,128)(2,1)S(1)}, bf16[64,2048]{1,0:T(8,128)(2,1)S(1)}, u32[]{:S(2)}, u32[]{:S(2)}) collective-permute-start(bf16[64,2048]{1,0:T(8,128)(2,1)S(1)} %get-tuple-element.125), channel_id=1, source_target_pairs={{0,2},{2,0},{4,6},{6,4},{1,3},{3,1},{5,7},{7,5},{8,10},{10,8},{12,... | collective-permute-start | bytes 786440 | tf_op jit(solution)/shard_map/ppermute | solution.py:30
  66.1 10.2 %collective-permute-start.14 = (bf16[64,2048]{1,0:T(8,128)(2,1)S(1)}, bf16[64,2048]{1,0:T(8,128)(2,1)S(1)}, u32[]{:S(2)}, u32[]{:S(2)}) collective-permute-start(bf16[64,2048]{1,0:T(8,128)(2,1)S(1)} %get-tuple-element.126), channel_id=1, source_target_pairs={{0,4},{2,6},{4,0},{6,2},{1,5},{3,7},{5,1},{7,3},{8,12},{10,14},{12... | collective-permute-start | bytes 786440 | tf_op jit(solution)/shard_map/ppermute | solution.py:30
  67.6 13.9 %collective-permute-start.15 = (bf16[64,2048]{1,0:T(8,128)(2,1)S(1)}, bf16[64,2048]{1,0:T(8,128)(2,1)S(1)}, u32[]{:S(2)}, u32[]{:S(2)}) collective-permute-start(bf16[64,2048]{1,0:T(8,128)(2,1)S(1)} %get-tuple-element.127), channel_id=1, source_target_pairs={{0,6},{2,4},{4,2},{6,0},{1,7},{3,5},{5,3},{7,1},{8,14},{10,12},{12... | collective-permute-start | bytes 786440 | tf_op jit(solution)/shard_map/ppermute | solution.py:30
  72.3 18.2 %collective-permute-start.18 = (bf16[64,2048]{1,0:T(8,128)(2,1)S(1)}, bf16[64,2048]{1,0:T(8,128)(2,1)S(1)}, u32[]{:S(2)}, u32[]{:S(2)}) collective-permute-start(bf16[64,2048]{1,0:T(8,128)(2,1)S(1)} %get-tuple-element.136), channel_id=1, source_target_pairs={{0,2},{2,0},{4,6},{6,4},{1,3},{3,1},{5,7},{7,5},{8,10},{10,8},{12,... | collective-permute-start | bytes 786440 | tf_op jit(solution)/shard_map/ppermute | solution.py:30
  72.8 18.3 %collective-permute-start.19 = (bf16[64,2048]{1,0:T(8,128)(2,1)S(1)}, bf16[64,2048]{1,0:T(8,128)(2,1)S(1)}, u32[]{:S(2)}, u32[]{:S(2)}) collective-permute-start(bf16[64,2048]{1,0:T(8,128)(2,1)S(1)} %get-tuple-element.137), channel_id=1, source_target_pairs={{0,4},{2,6},{4,0},{6,2},{1,5},{3,7},{5,1},{7,3},{8,12},{10,14},{12... | collective-permute-start | bytes 786440 | tf_op jit(solution)/shard_map/ppermute | solution.py:30
  75.0 18.6 %collective-permute-start.20 = (bf16[64,2048]{1,0:T(8,128)(2,1)S(1)}, bf16[64,2048]{1,0:T(8,128)(2,1)S(1)}, u32[]{:S(2)}, u32[]{:S(2)}) collective-permute-start(bf16[64,2048]{1,0:T(8,128)(2,1)S(1)} %get-tuple-element.138), channel_id=1, source_target_pairs={{0,6},{2,4},{4,2},{6,0},{1,7},{3,5},{5,3},{7,1},{8,14},{10,12},{12... | collective-permute-start | bytes 786440 | tf_op jit(solution)/shard_map/ppermute | solution.py:30
  76.3 21.2 %collective-permute-start.21 = (bf16[64,2048]{1,0:T(8,128)(2,1)S(1)}, bf16[64,2048]{1,0:T(8,128)(2,1)S(1)}, u32[]{:S(2)}, u32[]{:S(2)}) collective-permute-start(bf16[64,2048]{1,0:T(8,128)(2,1)S(1)} %copy-done.24), channel_id=1, source_target_pairs={{0,2},{2,0},{1,3},{3,1},{4,6},{6,4},{5,7},{7,5},{8,10},{10,8},{9,1... | collective-permute-start | bytes 786440 | tf_op jit(solution)/shard_map/ppermute | solution.py:30
  90.1 16.6 %collective-permute-start.25 = (bf16[32,2048]{1,0:T(8,128)(2,1)S(1)}, bf16[32,2048]{1,0:T(8,128)(2,1)S(1)}, u32[]{:S(2)}, u32[]{:S(2)}) collective-permute-start(bf16[32,2048]{1,0:T(8,128)(2,1)S(1)} %get-tuple-element.140), channel_id=1, source_target_pairs={{0,2},{2,0},{4,6},{6,4},{1,3},{3,1},{5,7},{7,5},{8,10},{10,8},{12,... | collective-permute-start | bytes 393224 | tf_op jit(solution)/shard_map/ppermute | solution.py:30
  90.5 16.3 %collective-permute-start.26 = (bf16[32,2048]{1,0:T(8,128)(2,1)S(1)}, bf16[32,2048]{1,0:T(8,128)(2,1)S(1)}, u32[]{:S(2)}, u32[]{:S(2)}) collective-permute-start(bf16[32,2048]{1,0:T(8,128)(2,1)S(1)} %get-tuple-element.141), channel_id=1, source_target_pairs={{0,4},{2,6},{4,0},{6,2},{1,5},{3,7},{5,1},{7,3},{8,12},{10,14},{12... | collective-permute-start | bytes 393224 | tf_op jit(solution)/shard_map/ppermute | solution.py:30
  91.1 15.7 %collective-permute-start.27 = (bf16[32,2048]{1,0:T(8,128)(2,1)S(1)}, bf16[32,2048]{1,0:T(8,128)(2,1)S(1)}, u32[]{:S(2)}, u32[]{:S(2)}) collective-permute-start(bf16[32,2048]{1,0:T(8,128)(2,1)S(1)} %get-tuple-element.142), channel_id=1, source_target_pairs={{0,6},{2,4},{4,2},{6,0},{1,7},{3,5},{5,3},{7,1},{8,14},{10,12},{12... | collective-permute-start | bytes 393224 | tf_op jit(solution)/shard_map/ppermute | solution.py:30
  104.9 6.6 %collective-permute-start.22 = (bf16[32,2048]{1,0:T(8,128)(2,1)S(1)}, bf16[32,2048]{1,0:T(8,128)(2,1)S(1)}, u32[]{:S(2)}, u32[]{:S(2)}) collective-permute-start(bf16[32,2048]{1,0:T(8,128)(2,1)S(1)} %get-tuple-element.149), channel_id=1, source_target_pairs={{0,2},{2,0},{4,6},{6,4},{1,3},{3,1},{5,7},{7,5},{8,10},{10,8},{12,... | collective-permute-start | bytes 393224 | tf_op jit(solution)/shard_map/ppermute | solution.py:30
  105.4 7.5 %collective-permute-start.23 = (bf16[32,2048]{1,0:T(8,128)(2,1)S(1)}, bf16[32,2048]{1,0:T(8,128)(2,1)S(1)}, u32[]{:S(2)}, u32[]{:S(2)}) collective-permute-start(bf16[32,2048]{1,0:T(8,128)(2,1)S(1)} %get-tuple-element.150), channel_id=1, source_target_pairs={{0,4},{2,6},{4,0},{6,2},{1,5},{3,7},{5,1},{7,3},{8,12},{10,14},{12... | collective-permute-start | bytes 393224 | tf_op jit(solution)/shard_map/ppermute | solution.py:30
  107.0 16.8 %collective-permute-start.28 = (bf16[64,2048]{1,0:T(8,128)(2,1)S(1)}, bf16[64,2048]{1,0:T(8,128)(2,1)S(1)}, u32[]{:S(2)}, u32[]{:S(2)}) collective-permute-start(bf16[64,2048]{1,0:T(8,128)(2,1)S(1)} %combine.5), channel_id=1, source_target_pairs={{0,24},{8,16},{16,8},{24,0},{1,25},{9,17},{17,9},{25,1},{2,26},{10... | collective-permute-start | bytes 786440 | tf_op jit(solution)/shard_map/ppermute | solution.py:30
  108.5 6.1 %collective-permute-start.24 = (bf16[32,2048]{1,0:T(8,128)(2,1)S(1)}, bf16[32,2048]{1,0:T(8,128)(2,1)S(1)}, u32[]{:S(2)}, u32[]{:S(2)}) collective-permute-start(bf16[32,2048]{1,0:T(8,128)(2,1)S(1)} %get-tuple-element.151), channel_id=1, source_target_pairs={{0,6},{2,4},{4,2},{6,0},{1,7},{3,5},{5,3},{7,1},{8,14},{10,12},{12... | collective-permute-start | bytes 393224 | tf_op jit(solution)/shard_map/ppermute | solution.py:30
  111.1 5.7 %collective-permute-start.33 = (bf16[32,2048]{1,0:T(8,128)(2,1)S(1)}, bf16[32,2048]{1,0:T(8,128)(2,1)S(1)}, u32[]{:S(2)}, u32[]{:S(2)}) collective-permute-start(bf16[32,2048]{1,0:T(8,128)(2,1)S(1)} %get-tuple-element.169), channel_id=1, source_target_pairs={{0,2},{2,0},{4,6},{6,4},{1,3},{3,1},{5,7},{7,5},{8,10},{10,8},{12,... | collective-permute-start | bytes 393224 | tf_op jit(solution)/shard_map/ppermute | solution.py:30
  111.5 5.3 %collective-permute-start.34 = (bf16[32,2048]{1,0:T(8,128)(2,1)S(1)}, bf16[32,2048]{1,0:T(8,128)(2,1)S(1)}, u32[]{:S(2)}, u32[]{:S(2)}) collective-permute-start(bf16[32,2048]{1,0:T(8,128)(2,1)S(1)} %get-tuple-element.170), channel_id=1, source_target_pairs={{0,4},{2,6},{4,0},{6,2},{1,5},{3,7},{5,1},{7,3},{8,12},{10,14},{12... | collective-permute-start | bytes 393224 | tf_op jit(solution)/shard_map/ppermute | solution.py:30
  112.8 5.9 %collective-permute-start.35 = (bf16[32,2048]{1,0:T(8,128)(2,1)S(1)}, bf16[32,2048]{1,0:T(8,128)(2,1)S(1)}, u32[]{:S(2)}, u32[]{:S(2)}) collective-permute-start(bf16[32,2048]{1,0:T(8,128)(2,1)S(1)} %get-tuple-element.171), channel_id=1, source_target_pairs={{0,6},{2,4},{4,2},{6,0},{1,7},{3,5},{5,3},{7,1},{8,14},{10,12},{12... | collective-permute-start | bytes 393224 | tf_op jit(solution)/shard_map/ppermute | solution.py:30
  114.9 19.2 %collective-permute-start.32 = (bf16[64,2048]{1,0:T(8,128)(2,1)S(1)}, bf16[64,2048]{1,0:T(8,128)(2,1)S(1)}, u32[]{:S(2)}, u32[]{:S(2)}) collective-permute-start(bf16[64,2048]{1,0:T(8,128)(2,1)S(1)} %combine.4), channel_id=1, source_target_pairs={{0,16},{8,24},{16,0},{24,8},{1,17},{9,25},{17,1},{25,9},{2,18},{10... | collective-permute-start | bytes 786440 | tf_op jit(solution)/shard_map/ppermute | solution.py:30
  118.9 15.1 %collective-permute-start.36 = (bf16[64,2048]{1,0:T(8,128)(2,1)S(1)}, bf16[64,2048]{1,0:T(8,128)(2,1)S(1)}, u32[]{:S(2)}, u32[]{:S(2)}) collective-permute-start(bf16[64,2048]{1,0:T(8,128)(2,1)S(1)} %combine.7), channel_id=1, source_target_pairs={{0,8},{8,0},{16,24},{24,16},{1,9},{9,1},{17,25},{25,17},{2,10},{10... | collective-permute-start | bytes 786440 | tf_op jit(solution)/shard_map/ppermute | solution.py:30
  123.8 5.5 %collective-permute-start.29 = (bf16[32,2048]{1,0:T(8,128)(2,1)S(1)}, bf16[32,2048]{1,0:T(8,128)(2,1)S(1)}, u32[]{:S(2)}, u32[]{:S(2)}) collective-permute-start(bf16[32,2048]{1,0:T(8,128)(2,1)S(1)} %copy-done.16), channel_id=1, source_target_pairs={{0,2},{2,0},{4,6},{6,4},{1,3},{3,1},{5,7},{7,5},{8,10},{10,8},{12,... | collective-permute-start | bytes 393224 | tf_op jit(solution)/shard_map/ppermute | solution.py:30
  124.1 7.7 %collective-permute-start.30 = (bf16[32,2048]{1,0:T(8,128)(2,1)S(1)}, bf16[32,2048]{1,0:T(8,128)(2,1)S(1)}, u32[]{:S(2)}, u32[]{:S(2)}) collective-permute-start(bf16[32,2048]{1,0:T(8,128)(2,1)S(1)} %copy-done.14), channel_id=1, source_target_pairs={{0,4},{2,6},{4,0},{6,2},{1,5},{3,7},{5,1},{7,3},{8,12},{10,14},{12... | collective-permute-start | bytes 393224 | tf_op jit(solution)/shard_map/ppermute | solution.py:30
  127.9 5.9 %collective-permute-start.31 = (bf16[32,2048]{1,0:T(8,128)(2,1)S(1)}, bf16[32,2048]{1,0:T(8,128)(2,1)S(1)}, u32[]{:S(2)}, u32[]{:S(2)}) collective-permute-start(bf16[32,2048]{1,0:T(8,128)(2,1)S(1)} %get-tuple-element.160), channel_id=1, source_target_pairs={{0,6},{2,4},{4,2},{6,0},{1,7},{3,5},{5,3},{7,1},{8,14},{10,12},{12... | collective-permute-start | bytes 393224 | tf_op jit(solution)/shard_map/ppermute | solution.py:30
  (36 other events, 473.6 us)

commit v16 on v15

--- a/solution.py
+++ b/solution.py
@@ -645,13 +645,15 @@
     results = {}
     for ks, pieces in zip(GROUPS, sent):
         if made is not None:
-            pieces, made, parts = lax.optimization_barrier((pieces, made, parts))
+            pieces, made = lax.optimization_barrier((pieces, made))
         made = experts(pieces, len(ks), inner, outer)
         results.update(zip(ks, made))
     totals = {}
     landed = {}
     for k, after, arrived in BACK:
         pieces = results[k]
+        if k == BACK[1][0]:
+            pieces, parts = lax.optimization_barrier((pieces, parts))
         if after is not None:
             pieces, totals[after] = lax.optimization_barrier((pieces, totals[after]))
         if arrived is not None:

time: 135 us -> 131 us (0.970); the launches traced: 135 us -> 129 us
  waiting for transfers between devices: 27.3 us -> 19.2 us
  starting transfers between devices: 46.7 us -> 48.8 us
    ppermute x37, waiting for transfers between devices: 27.3 us -> 19.2 us  [partner(): return lax.ppermute(value, axes, [(i, i ^ offset) for i in range(size)])]
    ppermute x37, starting transfers between devices: 46.7 us -> 48.8 us  [partner(): return lax.ppermute(value, axes, [(i, i ^ offset) for i in range(size)])]
    unnamed x64 -> x62, local copies, waits for them, and re-layouts: 7.56 us -> 7.51 us
  transfers between devices with their start and end apart: 37 -> 37, of which waited for: 12 -> 10; matrix products, arithmetic and copies ran while one was open for 4% -> 5% of each run, Pallas kernels for 34% -> 34%
where the time goes in v16:
time: 131 us; the launch traced here: 129 us
  starting transfers between devices  48.8 us (37%)
  Pallas kernels  46.5 us (35%)
  waiting for transfers between devices  19.2 us (15%)
  local copies, waits for them, and re-layouts  9.32 us (7%)
  other arithmetic  2.92 us (2%)
    ppermute x37, starting transfers between devices, partner(): return lax.ppermute(value, axes, [(i, i ^ offset) for i in range(size)])  48.8 us
    ppermute x37, waiting for transfers between devices, partner(): return lax.ppermute(value, axes, [(i, i ^ offset) for i in range(size)])  19.2 us
    pallas_call x2, Pallas kernels, experts(): pl.pallas_call(functools.partial(expert_kernel, plane=plane, count=count,...  14.6 us
    pallas_call x2, Pallas kernels, attend(): pl.pallas_call(functools.partial(attend_kernel, offset=offset), in_specs=...  14.3 us
    pallas_call x1, Pallas kernels, shared_terms(): pl.pallas_call(functools.partial(shared_kernel, side=side), in_specs=[in_...  8.22 us
    unnamed x62, local copies, waits for them, and re-layouts  7.51 us
    pallas_call x2, Pallas kernels, select(): pl.pallas_call(functools.partial(select_kernel, count=count, plane=plane,...  4.34 us
  transfers between devices with their start and end apart: 37, of which 10 were waited for; matrix products, arithmetic and copies ran while one was open for 5% of the time, Pallas kernels for 34%

profile of v16, /device:TPU:0, one launch (start us, length us, event | category | flops | bytes accessed | tf_op | source)
XLA Modules:
  0.0 128.7 jit_solution(10036554831920004964)
XLA Ops:
  1.2 1.4 %collective-permute-done.1.second = bf16[64,2048]{1,0:T(8,128)(2,1)S(1)} collective-permute-done((bf16[64,2048]{1,0:T(8,128)(2,1)}, bf16[64,2048]{1,0:T(8,128)(2,1)S(1)}, u32[]{:S(2)}, u32[]{:S(2)}) %collective-permute-start.1) | collective-permute-done | bytes 262176 | tf_op jit(solution)/shard_map/ppermute | solution.py:30
  2.9 2.6 %collective-permute-start = (bf16[64,2048]{1,0:T(8,128)(2,1)}, bf16[64,2048]{1,0:T(8,128)(2,1)S(1)}, u32[]{:S(2)}, u32[]{:S(2)}) collective-permute-start(bf16[64,2048]{1,0:T(8,128)(2,1)} %bitcast.30), channel_id=1, source_target_pairs={{0,2},{2,0},{1,3},{3,1},{4,6},{6,4},{5,7},{7,5},{8,10},{10,8},{9,1... | collective-permute-start | bytes 786440 | tf_op jit(solution)/shard_map/ppermute | solution.py:30
  7.5 2.0 %prepare.1 = (f32[4,64,64]{2,1,0:T(8,128)S(1)}, f32[4,64,128]{2,1,0:T(8,128)S(1)}, f32[4,64,128]{2,1,0:T(8,128)S(1)}) custom-call(s32[4]{0:T(128)S(1)} %copy-done.10, s32[4,64]{1,0:T(4,128)S(1)} %copy-done.11, f32[1,128]{1,0:T(1,128)S(1)} %copy-done.12), custom_call_target="tpu_custom_call" | custom-call | flops 1024 | bytes 1024 | tf_op jit(solution)/shard_map/prepare/pallas_call | solution.py:69
  12.6 2.5 %collective-permute-done.2.second = bf16[64,2048]{1,0:T(8,128)(2,1)S(1)} collective-permute-done((bf16[64,2048]{1,0:T(8,128)(2,1)S(1)}, bf16[64,2048]{1,0:T(8,128)(2,1)S(1)}, u32[]{:S(2)}, u32[]{:S(2)}) %collective-permute-start.2) | collective-permute-done | bytes 262176 | tf_op jit(solution)/shard_map/ppermute | solution.py:30
  16.7 7.1 %attend.2 = (f32[64,2048]{1,0:T(8,128)}, bf16[64,2048]{1,0:T(8,128)(2,1)}, bf16[64,256]{1,0:T(8,128)(2,1)}, bf16[64,256]{1,0:T(8,128)(2,1)}) custom-call(s32[1]{0:T(128)} %bitcast.2.place, s32[4]{0:T(128)} %lengths.5, bf16[64,2048]{1,0:T(8,128)(2,1)} %copy-done.19, bf16[64,2048]{1,0:T(8,128)(2,1)} %copy-done.20, f32[1,2048]{1,0:T(1,128)} %bitcast.42, ...), custom_call_target="tpu_custom_call" | custom-call | flops 1024 | bytes 1024 | tf_op jit(solution)/shard_map/attend/pallas_call | solution.py:205
  24.1 1.6 %collective-permute-done.5 = bf16[64,2048]{1,0:T(8,128)(2,1)S(1)} collective-permute-done((bf16[64,2048]{1,0:T(8,128)(2,1)}, bf16[64,2048]{1,0:T(8,128)(2,1)S(1)}, u32[]{:S(2)}, u32[]{:S(2)}) %collective-permute-start.5) | collective-permute-done | bytes 262176 | tf_op jit(solution)/shard_map/ppermute | solution.py:30
  25.8 1.8 %add_convert_fusion = bf16[64,2048]{1,0:T(8,128)(2,1)} fusion(f32[64,2048]{1,0:T(8,128)} %get-tuple-element.108, bf16[64,2048]{1,0:T(8,128)(2,1)S(1)} %collective-permute-done.5), kind=kLoop, calls=%fused_computation.4 | loop fusion | flops 393216 | bytes 1048576 | tf_op jit(solution)/shard_map/convert_element_type | solution.py:596
  28.5 7.2 %attend.3 = (f32[64,2048]{1,0:T(8,128)}, bf16[64,2048]{1,0:T(8,128)(2,1)}, bf16[64,256]{1,0:T(8,128)(2,1)}, bf16[64,256]{1,0:T(8,128)(2,1)}) custom-call(s32[1]{0:T(128)} %bitcast.2.place, s32[4]{0:T(128)} %lengths.5, bf16[64,2048]{1,0:T(8,128)(2,1)} %bitcast.31, bf16[64,2048]{1,0:T(8,128)(2,1)} %copy-done.18, f32[1,2048]{1,0:T(1,128)} %bitcast.43, ...), custom_call_target="tpu_custom_call" | custom-call | flops 1024 | bytes 1024 | tf_op jit(solution)/shard_map/attend/pallas_call | solution.py:205
  39.3 6.4 %collective-permute-start.12 = (bf16[64,2176]{1,0:T(8,128)(2,1)}, bf16[64,2176]{1,0:T(8,128)(2,1)}, u32[]{:S(2)}, u32[]{:S(2)}) collective-permute-start(bf16[64,2176]{1,0:T(8,128)(2,1)} %get-tuple-element.124.refs_2_), channel_id=1, source_target_pairs={{0,24},{8,16},{16,8},{24,0},{1,25},{9,17},{17,9},{25,1},{2,26},{10... | collective-permute-start | bytes 835592 | tf_op jit(solution)/shard_map/ppermute | solution.py:30
  46.8 7.6 %collective-permute-done.11.refs_1_ = bf16[64,2048]{1,0:T(8,128)(2,1)} collective-permute-done((bf16[64,2048]{1,0:T(8,128)(2,1)}, bf16[64,2048]{1,0:T(8,128)(2,1)}, u32[]{:S(2)}, u32[]{:S(2)}) %collective-permute-start.11) | collective-permute-done | bytes 262176 | tf_op jit(solution)/shard_map/ppermute | solution.py:30
  54.4 8.2 %shared.1 = (f32[64,2048]{1,0:T(8,128)}, bf16[64,2048]{1,0:T(8,128)(2,1)}) custom-call(bf16[64,2048]{1,0:T(8,128)(2,1)} %get-tuple-element.119.refs_0_, bf16[64,2048]{1,0:T(8,128)(2,1)} %collective-permute-done.11.refs_1_, bf16[352,2048]{1,0:T(8,128)(2,1)} %bitcast.38, bf16[352,2048]{1,0:T(8,128)(2,1)} %bitcast.40, bf16[352,2048]{1,0:T(8,128)(2,1)} %refs_4_.1, ...), custom_call_target="tpu_custom_call" | custom-call | flops 1024 | bytes 1024 | tf_op jit(solution)/shard_map/shared/pallas_call | solution.py:361
  62.6 2.2 %select.2 = (bf16[64,2048]{1,0:T(8,128)(2,1)S(1)}, bf16[64,2048]{1,0:T(8,128)(2,1)S(1)}, bf16[64,2048]{1,0:T(8,128)(2,1)S(1)}, bf16[64,2048]{1,0:T(8,128)(2,1)S(...) custom-call(s32[4]{0:T(128)S(1)} %xor_add_fusion.refs_0_, bf16[2048,16]{1,0:T(8,128)(2,1)S(1)} %copy.21.refs_1_, ...), custom_call_target="tpu_custom_call" | custom-call | flops 1024 | bytes 1024 | tf_op jit(solution)/shard_map/select/pallas_call | solution.py:468
  65.1 1.5 %collective-permute-start.14 = (bf16[64,2048]{1,0:T(8,128)(2,1)S(1)}, bf16[64,2048]{1,0:T(8,128)(2,1)S(1)}, u32[]{:S(2)}, u32[]{:S(2)}) collective-permute-start(bf16[64,2048]{1,0:T(8,128)(2,1)S(1)} %get-tuple-element.130), channel_id=1, source_target_pairs={{0,4},{2,6},{4,0},{6,2},{1,5},{3,7},{5,1},{7,3},{8,12},{10,14},{12... | collective-permute-start | bytes 786440 | tf_op jit(solution)/shard_map/ppermute | solution.py:30
  66.6 1.8 %collective-permute-start.15 = (bf16[64,2048]{1,0:T(8,128)(2,1)S(1)}, bf16[64,2048]{1,0:T(8,128)(2,1)S(1)}, u32[]{:S(2)}, u32[]{:S(2)}) collective-permute-start(bf16[64,2048]{1,0:T(8,128)(2,1)S(1)} %get-tuple-element.131), channel_id=1, source_target_pairs={{0,6},{2,4},{4,2},{6,0},{1,7},{3,5},{5,3},{7,1},{8,14},{10,12},{12... | collective-permute-start | bytes 786440 | tf_op jit(solution)/shard_map/ppermute | solution.py:30
  68.4 1.5 %collective-permute-done.16.refs_2_ = bf16[64,2176]{1,0:T(8,128)(2,1)} collective-permute-done((bf16[64,2176]{1,0:T(8,128)(2,1)}, bf16[64,2176]{1,0:T(8,128)(2,1)}, u32[]{:S(2)}, u32[]{:S(2)}) %collective-permute-start.16) | collective-permute-done | bytes 278560 | tf_op jit(solution)/shard_map/ppermute | solution.py:30
  69.9 2.2 %select.3 = (bf16[64,2048]{1,0:T(8,128)(2,1)S(1)}, bf16[64,2048]{1,0:T(8,128)(2,1)S(1)}, bf16[64,2048]{1,0:T(8,128)(2,1)S(1)}, bf16[64,2048]{1,0:T(8,128)(2,1)S(...) custom-call(s32[4]{0:T(128)S(1)} %xor_add_fusion.refs_0_, bf16[2048,16]{1,0:T(8,128)(2,1)S(1)} %copy.21.refs_1_, ...), custom_call_target="tpu_custom_call" | custom-call | flops 23000000512 | bytes 72000000 | tf_op jit(solution)/shard_map/select/pallas_call | solution.py:468
  72.4 2.5 %collective-permute-start.19 = (bf16[64,2048]{1,0:T(8,128)(2,1)S(1)}, bf16[64,2048]{1,0:T(8,128)(2,1)S(1)}, u32[]{:S(2)}, u32[]{:S(2)}) collective-permute-start(bf16[64,2048]{1,0:T(8,128)(2,1)S(1)} %get-tuple-element.141), channel_id=1, source_target_pairs={{0,4},{2,6},{4,0},{6,2},{1,5},{3,7},{5,1},{7,3},{8,12},{10,14},{12... | collective-permute-start | bytes 786440 | tf_op jit(solution)/shard_map/ppermute | solution.py:30
  75.6 3.1 %collective-permute-start.21 = (bf16[64,2048]{1,0:T(8,128)(2,1)S(1)}, bf16[64,2048]{1,0:T(8,128)(2,1)S(1)}, u32[]{:S(2)}, u32[]{:S(2)}) collective-permute-start(bf16[64,2048]{1,0:T(8,128)(2,1)S(1)} %copy-done.24), channel_id=1, source_target_pairs={{0,2},{2,0},{1,3},{3,1},{4,6},{6,4},{5,7},{7,5},{8,10},{10,8},{9,1... | collective-permute-start | bytes 786440 | tf_op jit(solution)/shard_map/ppermute | solution.py:30
  79.4 7.3 %expert.2 = (bf16[32,2048]{1,0:T(8,128)(2,1)S(1)}, bf16[32,2048]{1,0:T(8,128)(2,1)S(1)}, bf16[32,2048]{1,0:T(8,128)(2,1)S(1)}, bf16[32,2048]{1,0:T(8,128)(2,1)S(...) custom-call(bf16[64,2048]{1,0:T(8,128)(2,1)S(1)} %get-tuple-element., ...), custom_call_target="tpu_custom_call" | custom-call | flops 1024 | bytes 1024 | tf_op jit(solution)/shard_map/expert/pallas_call | solution.py:303
  88.8 1.4 %collective-permute-start.26 = (bf16[32,2048]{1,0:T(8,128)(2,1)S(1)}, bf16[32,2048]{1,0:T(8,128)(2,1)S(1)}, u32[]{:S(2)}, u32[]{:S(2)}) collective-permute-start(bf16[32,2048]{1,0:T(8,128)(2,1)S(1)} %get-tuple-element.145), channel_id=1, source_target_pairs={{0,4},{2,6},{4,0},{6,2},{1,5},{3,7},{5,1},{7,3},{8,12},{10,14},{12... | collective-permute-start | bytes 393224 | tf_op jit(solution)/shard_map/ppermute | solution.py:30
  90.1 1.4 %collective-permute-start.27 = (bf16[32,2048]{1,0:T(8,128)(2,1)S(1)}, bf16[32,2048]{1,0:T(8,128)(2,1)S(1)}, u32[]{:S(2)}, u32[]{:S(2)}) collective-permute-start(bf16[32,2048]{1,0:T(8,128)(2,1)S(1)} %get-tuple-element.146), channel_id=1, source_target_pairs={{0,6},{2,4},{4,2},{6,0},{1,7},{3,5},{5,3},{7,1},{8,14},{10,12},{12... | collective-permute-start | bytes 393224 | tf_op jit(solution)/shard_map/ppermute | solution.py:30
  91.5 7.3 %expert.3 = (bf16[32,2048]{1,0:T(8,128)(2,1)S(1)}, bf16[32,2048]{1,0:T(8,128)(2,1)S(1)}, bf16[32,2048]{1,0:T(8,128)(2,1)S(1)}, bf16[32,2048]{1,0:T(8,128)(2,1)S(...) custom-call(bf16[64,2048]{1,0:T(8,128)(2,1)S(1)} %get-tuple-element., ...), custom_call_target="tpu_custom_call" | custom-call | flops 1024 | bytes 1024 | tf_op jit(solution)/shard_map/expert/pallas_call | solution.py:303
  99.7 1.3 %collective-permute-start.23 = (bf16[32,2048]{1,0:T(8,128)(2,1)S(1)}, bf16[32,2048]{1,0:T(8,128)(2,1)S(1)}, u32[]{:S(2)}, u32[]{:S(2)}) collective-permute-start(bf16[32,2048]{1,0:T(8,128)(2,1)S(1)} %get-tuple-element.158), channel_id=1, source_target_pairs={{0,4},{2,6},{4,0},{6,2},{1,5},{3,7},{5,1},{7,3},{8,12},{10,14},{12... | collective-permute-start | bytes 393224 | tf_op jit(solution)/shard_map/ppermute | solution.py:30
  101.3 3.6 %collective-permute-start.28 = (bf16[64,2048]{1,0:T(8,128)(2,1)S(1)}, bf16[64,2048]{1,0:T(8,128)(2,1)S(1)}, u32[]{:S(2)}, u32[]{:S(2)}) collective-permute-start(bf16[64,2048]{1,0:T(8,128)(2,1)S(1)} %combine.5), channel_id=1, source_target_pairs={{0,24},{8,16},{16,8},{24,0},{1,25},{9,17},{17,9},{25,1},{2,26},{10... | collective-permute-start | bytes 786440 | tf_op jit(solution)/shard_map/ppermute | solution.py:30
  106.2 1.6 %collective-permute-start.33 = (bf16[32,2048]{1,0:T(8,128)(2,1)S(1)}, bf16[32,2048]{1,0:T(8,128)(2,1)S(1)}, u32[]{:S(2)}, u32[]{:S(2)}) collective-permute-start(bf16[32,2048]{1,0:T(8,128)(2,1)S(1)} %get-tuple-element.177), channel_id=1, source_target_pairs={{0,2},{2,0},{4,6},{6,4},{1,3},{3,1},{5,7},{7,5},{8,10},{10,8},{12,... | collective-permute-start | bytes 393224 | tf_op jit(solution)/shard_map/ppermute | solution.py:30
  108.4 4.2 %collective-permute-start.35 = (bf16[32,2048]{1,0:T(8,128)(2,1)S(1)}, bf16[32,2048]{1,0:T(8,128)(2,1)S(1)}, u32[]{:S(2)}, u32[]{:S(2)}) collective-permute-start(bf16[32,2048]{1,0:T(8,128)(2,1)S(1)} %get-tuple-element.179), channel_id=1, source_target_pairs={{0,6},{2,4},{4,2},{6,0},{1,7},{3,5},{5,3},{7,1},{8,14},{10,12},{12... | collective-permute-start | bytes 393224 | tf_op jit(solution)/shard_map/ppermute | solution.py:30
  112.8 2.7 %collective-permute-start.32 = (bf16[64,2048]{1,0:T(8,128)(2,1)S(1)}, bf16[64,2048]{1,0:T(8,128)(2,1)S(1)}, u32[]{:S(2)}, u32[]{:S(2)}) collective-permute-start(bf16[64,2048]{1,0:T(8,128)(2,1)S(1)} %combine.4), channel_id=1, source_target_pairs={{0,16},{8,24},{16,0},{24,8},{1,17},{9,25},{17,1},{25,9},{2,18},{10... | collective-permute-start | bytes 786440 | tf_op jit(solution)/shard_map/ppermute | solution.py:30
  115.7 2.0 %collective-permute-start.36 = (bf16[64,2048]{1,0:T(8,128)(2,1)S(1)}, bf16[64,2048]{1,0:T(8,128)(2,1)S(1)}, u32[]{:S(2)}, u32[]{:S(2)}) collective-permute-start(bf16[64,2048]{1,0:T(8,128)(2,1)S(1)} %combine.7), channel_id=1, source_target_pairs={{0,8},{8,0},{16,24},{24,16},{1,9},{9,1},{17,25},{25,17},{2,10},{10... | collective-permute-start | bytes 786440 | tf_op jit(solution)/shard_map/ppermute | solution.py:30
  118.4 1.4 %collective-permute-start.29 = (bf16[32,2048]{1,0:T(8,128)(2,1)S(1)}, bf16[32,2048]{1,0:T(8,128)(2,1)S(1)}, u32[]{:S(2)}, u32[]{:S(2)}) collective-permute-start(bf16[32,2048]{1,0:T(8,128)(2,1)S(1)} %copy-done.16), channel_id=1, source_target_pairs={{0,2},{2,0},{4,6},{6,4},{1,3},{3,1},{5,7},{7,5},{8,10},{10,8},{12,... | collective-permute-start | bytes 393224 | tf_op jit(solution)/shard_map/ppermute | solution.py:30
  119.9 1.5 %collective-permute-start.30 = (bf16[32,2048]{1,0:T(8,128)(2,1)S(1)}, bf16[32,2048]{1,0:T(8,128)(2,1)S(1)}, u32[]{:S(2)}, u32[]{:S(2)}) collective-permute-start(bf16[32,2048]{1,0:T(8,128)(2,1)S(1)} %copy-done.14), channel_id=1, source_target_pairs={{0,4},{2,6},{4,0},{6,2},{1,5},{3,7},{5,1},{7,3},{8,12},{10,14},{12... | collective-permute-start | bytes 393224 | tf_op jit(solution)/shard_map/ppermute | solution.py:30
  121.4 1.4 %collective-permute-start.31 = (bf16[32,2048]{1,0:T(8,128)(2,1)S(1)}, bf16[32,2048]{1,0:T(8,128)(2,1)S(1)}, u32[]{:S(2)}, u32[]{:S(2)}) collective-permute-start(bf16[32,2048]{1,0:T(8,128)(2,1)S(1)} %get-tuple-element.168), channel_id=1, source_target_pairs={{0,6},{2,4},{4,2},{6,0},{1,7},{3,5},{5,3},{7,1},{8,14},{10,12},{12... | collective-permute-start | bytes 393224 | tf_op jit(solution)/shard_map/ppermute | solution.py:30
  124.9 2.4 %collective-permute-done.31.refs_3_ = bf16[32,2048]{1,0:T(8,128)(2,1)S(1)} collective-permute-done((bf16[32,2048]{1,0:T(8,128)(2,1)S(1)}, bf16[32,2048]{1,0:T(8,128)(2,1)S(1)}, u32[]{:S(2)}, u32[]{:S(2)}) %collective-permute-start.31) | collective-permute-done | bytes 131104 | tf_op jit(solution)/shard_map/ppermute | solution.py:30
  (128 shorter events, 25.1 us)
Async XLA Ops:
  2.5 13.0 %collective-permute-start.4 = (bf16[704,2048]{1,0:T(8,128)(2,1)}, bf16[704,2048]{1,0:T(8,128)(2,1)S(1)}, u32[]{:S(2)}, u32[]{:S(2)}) collective-permute-start(bf16[704,2048]{1,0:T(8,128)(2,1)} %bitcast.26), channel_id=1, source_target_pairs={{0,1},{1,0},{2,3},{3,2},{4,5},{5,4},{6,7},{7,6},{8,9},{9,8},{10,11... | collective-permute-start | bytes 8650760 | tf_op jit(solution)/shard_map/ppermute | solution.py:30
  2.9 9.7 %collective-permute-start = (bf16[64,2048]{1,0:T(8,128)(2,1)}, bf16[64,2048]{1,0:T(8,128)(2,1)S(1)}, u32[]{:S(2)}, u32[]{:S(2)}) collective-permute-start(bf16[64,2048]{1,0:T(8,128)(2,1)} %bitcast.30), channel_id=1, source_target_pairs={{0,2},{2,0},{1,3},{3,1},{4,6},{6,4},{5,7},{7,5},{8,10},{10,8},{9,1... | collective-permute-start | bytes 786440 | tf_op jit(solution)/shard_map/ppermute | solution.py:30
  15.1 9.0 %collective-permute-start.6 = (bf16[352,2048]{1,0:T(8,128)(2,1)}, bf16[352,2048]{1,0:T(8,128)(2,1)}, u32[]{:S(2)}, u32[]{:S(2)}) collective-permute-start(bf16[352,2048]{1,0:T(8,128)(2,1)} %bitcast.39), channel_id=1, source_target_pairs={{0,1},{1,0},{2,3},{3,2},{4,5},{5,4},{6,7},{7,6},{8,9},{9,8},{10,11... | collective-permute-start | bytes 4325384 | tf_op jit(solution)/shard_map/ppermute | solution.py:30
  15.2 8.9 %collective-permute-start.7 = (bf16[352,2048]{1,0:T(8,128)(2,1)}, bf16[352,2048]{1,0:T(8,128)(2,1)}, u32[]{:S(2)}, u32[]{:S(2)}) collective-permute-start(bf16[352,2048]{1,0:T(8,128)(2,1)} %refs_4_.1), channel_id=1, source_target_pairs={{0,1},{1,0},{2,3},{3,2},{4,5},{5,4},{6,7},{7,6},{8,9},{9,8},{10,11... | collective-permute-start | bytes 4325384 | tf_op jit(solution)/shard_map/ppermute | solution.py:30
  25.7 11.8 %collective-permute-start.9 = (bf16[2048,1408]{1,0:T(8,128)(2,1)}, bf16[2048,1408]{1,0:T(8,128)(2,1)}, u32[]{:S(2)}, u32[]{:S(2)}) collective-permute-start(bf16[2048,1408]{1,0:T(8,128)(2,1)} %bitcast.21), channel_id=1, source_target_pairs={{0,1},{1,0},{2,3},{3,2},{4,5},{5,4},{6,7},{7,6},{8,9},{9,8},{10,11... | collective-permute-start | bytes 17301512 | tf_op jit(solution)/shard_map/ppermute | solution.py:30
  27.6 8.8 %collective-permute-start.8 = (bf16[64,2048]{1,0:T(8,128)(2,1)}, bf16[64,2048]{1,0:T(8,128)(2,1)S(1)}, u32[]{:S(2)}, u32[]{:S(2)}) collective-permute-start(bf16[64,2048]{1,0:T(8,128)(2,1)} %add_convert_fusion), channel_id=1, source_target_pairs={{0,2},{2,0},{1,3},{3,1},{4,6},{6,4},{5,7},{7,5},{8,10},{10,8},{9,1... | collective-permute-start | bytes 786440 | tf_op jit(solution)/shard_map/ppermute | solution.py:30
  39.3 23.3 %collective-permute-start.12 = (bf16[64,2176]{1,0:T(8,128)(2,1)}, bf16[64,2176]{1,0:T(8,128)(2,1)}, u32[]{:S(2)}, u32[]{:S(2)}) collective-permute-start(bf16[64,2176]{1,0:T(8,128)(2,1)} %get-tuple-element.124.refs_2_), channel_id=1, source_target_pairs={{0,24},{8,16},{16,8},{24,0},{1,25},{9,17},{17,9},{25,1},{2,26},{10... | collective-permute-start | bytes 835592 | tf_op jit(solution)/shard_map/ppermute | solution.py:30
  45.7 24.2 %collective-permute-start.16 = (bf16[64,2176]{1,0:T(8,128)(2,1)}, bf16[64,2176]{1,0:T(8,128)(2,1)}, u32[]{:S(2)}, u32[]{:S(2)}) collective-permute-start(bf16[64,2176]{1,0:T(8,128)(2,1)} %get-tuple-element.124.refs_2_), channel_id=1, source_target_pairs={{0,16},{8,24},{16,0},{24,8},{1,17},{9,25},{17,1},{25,9},{2,18},{10... | collective-permute-start | bytes 835592 | tf_op jit(solution)/shard_map/ppermute | solution.py:30
  45.7 24.2 %collective-permute-start.17 = (bf16[64,2176]{1,0:T(8,128)(2,1)}, bf16[64,2176]{1,0:T(8,128)(2,1)}, u32[]{:S(2)}, u32[]{:S(2)}) collective-permute-start(bf16[64,2176]{1,0:T(8,128)(2,1)} %get-tuple-element.124.refs_2_), channel_id=1, source_target_pairs={{0,8},{8,0},{16,24},{24,16},{1,9},{9,1},{17,25},{25,17},{2,10},{10... | collective-permute-start | bytes 835592 | tf_op jit(solution)/shard_map/ppermute | solution.py:30
  46.3 8.1 %collective-permute-start.11 = (bf16[64,2048]{1,0:T(8,128)(2,1)}, bf16[64,2048]{1,0:T(8,128)(2,1)}, u32[]{:S(2)}, u32[]{:S(2)}) collective-permute-start(bf16[64,2048]{1,0:T(8,128)(2,1)} %get-tuple-element.119.refs_0_), channel_id=1, source_target_pairs={{0,2},{2,0},{1,3},{3,1},{4,6},{6,4},{5,7},{7,5},{8,10},{10,8},{9,1... | collective-permute-start | bytes 786440 | tf_op jit(solution)/shard_map/ppermute | solution.py:30
  64.8 10.1 %collective-permute-start.13 = (bf16[64,2048]{1,0:T(8,128)(2,1)S(1)}, bf16[64,2048]{1,0:T(8,128)(2,1)S(1)}, u32[]{:S(2)}, u32[]{:S(2)}) collective-permute-start(bf16[64,2048]{1,0:T(8,128)(2,1)S(1)} %get-tuple-element.129), channel_id=1, source_target_pairs={{0,2},{2,0},{4,6},{6,4},{1,3},{3,1},{5,7},{7,5},{8,10},{10,8},{12,... | collective-permute-start | bytes 786440 | tf_op jit(solution)/shard_map/ppermute | solution.py:30
  65.1 10.5 %collective-permute-start.14 = (bf16[64,2048]{1,0:T(8,128)(2,1)S(1)}, bf16[64,2048]{1,0:T(8,128)(2,1)S(1)}, u32[]{:S(2)}, u32[]{:S(2)}) collective-permute-start(bf16[64,2048]{1,0:T(8,128)(2,1)S(1)} %get-tuple-element.130), channel_id=1, source_target_pairs={{0,4},{2,6},{4,0},{6,2},{1,5},{3,7},{5,1},{7,3},{8,12},{10,14},{12... | collective-permute-start | bytes 786440 | tf_op jit(solution)/shard_map/ppermute | solution.py:30
  66.6 12.8 %collective-permute-start.15 = (bf16[64,2048]{1,0:T(8,128)(2,1)S(1)}, bf16[64,2048]{1,0:T(8,128)(2,1)S(1)}, u32[]{:S(2)}, u32[]{:S(2)}) collective-permute-start(bf16[64,2048]{1,0:T(8,128)(2,1)S(1)} %get-tuple-element.131), channel_id=1, source_target_pairs={{0,6},{2,4},{4,2},{6,0},{1,7},{3,5},{5,3},{7,1},{8,14},{10,12},{12... | collective-permute-start | bytes 786440 | tf_op jit(solution)/shard_map/ppermute | solution.py:30
  72.0 16.7 %collective-permute-start.18 = (bf16[64,2048]{1,0:T(8,128)(2,1)S(1)}, bf16[64,2048]{1,0:T(8,128)(2,1)S(1)}, u32[]{:S(2)}, u32[]{:S(2)}) collective-permute-start(bf16[64,2048]{1,0:T(8,128)(2,1)S(1)} %get-tuple-element.140), channel_id=1, source_target_pairs={{0,2},{2,0},{4,6},{6,4},{1,3},{3,1},{5,7},{7,5},{8,10},{10,8},{12,... | collective-permute-start | bytes 786440 | tf_op jit(solution)/shard_map/ppermute | solution.py:30
  72.4 17.7 %collective-permute-start.19 = (bf16[64,2048]{1,0:T(8,128)(2,1)S(1)}, bf16[64,2048]{1,0:T(8,128)(2,1)S(1)}, u32[]{:S(2)}, u32[]{:S(2)}) collective-permute-start(bf16[64,2048]{1,0:T(8,128)(2,1)S(1)} %get-tuple-element.141), channel_id=1, source_target_pairs={{0,4},{2,6},{4,0},{6,2},{1,5},{3,7},{5,1},{7,3},{8,12},{10,14},{12... | collective-permute-start | bytes 786440 | tf_op jit(solution)/shard_map/ppermute | solution.py:30
  74.9 16.6 %collective-permute-start.20 = (bf16[64,2048]{1,0:T(8,128)(2,1)S(1)}, bf16[64,2048]{1,0:T(8,128)(2,1)S(1)}, u32[]{:S(2)}, u32[]{:S(2)}) collective-permute-start(bf16[64,2048]{1,0:T(8,128)(2,1)S(1)} %get-tuple-element.142), channel_id=1, source_target_pairs={{0,6},{2,4},{4,2},{6,0},{1,7},{3,5},{5,3},{7,1},{8,14},{10,12},{12... | collective-permute-start | bytes 786440 | tf_op jit(solution)/shard_map/ppermute | solution.py:30
  75.6 23.3 %collective-permute-start.21 = (bf16[64,2048]{1,0:T(8,128)(2,1)S(1)}, bf16[64,2048]{1,0:T(8,128)(2,1)S(1)}, u32[]{:S(2)}, u32[]{:S(2)}) collective-permute-start(bf16[64,2048]{1,0:T(8,128)(2,1)S(1)} %copy-done.24), channel_id=1, source_target_pairs={{0,2},{2,0},{1,3},{3,1},{4,6},{6,4},{5,7},{7,5},{8,10},{10,8},{9,1... | collective-permute-start | bytes 786440 | tf_op jit(solution)/shard_map/ppermute | solution.py:30
  88.0 13.1 %collective-permute-start.25 = (bf16[32,2048]{1,0:T(8,128)(2,1)S(1)}, bf16[32,2048]{1,0:T(8,128)(2,1)S(1)}, u32[]{:S(2)}, u32[]{:S(2)}) collective-permute-start(bf16[32,2048]{1,0:T(8,128)(2,1)S(1)} %get-tuple-element.144), channel_id=1, source_target_pairs={{0,2},{2,0},{4,6},{6,4},{1,3},{3,1},{5,7},{7,5},{8,10},{10,8},{12,... | collective-permute-start | bytes 393224 | tf_op jit(solution)/shard_map/ppermute | solution.py:30
  88.8 12.3 %collective-permute-start.26 = (bf16[32,2048]{1,0:T(8,128)(2,1)S(1)}, bf16[32,2048]{1,0:T(8,128)(2,1)S(1)}, u32[]{:S(2)}, u32[]{:S(2)}) collective-permute-start(bf16[32,2048]{1,0:T(8,128)(2,1)S(1)} %get-tuple-element.145), channel_id=1, source_target_pairs={{0,4},{2,6},{4,0},{6,2},{1,5},{3,7},{5,1},{7,3},{8,12},{10,14},{12... | collective-permute-start | bytes 393224 | tf_op jit(solution)/shard_map/ppermute | solution.py:30
  90.1 11.0 %collective-permute-start.27 = (bf16[32,2048]{1,0:T(8,128)(2,1)S(1)}, bf16[32,2048]{1,0:T(8,128)(2,1)S(1)}, u32[]{:S(2)}, u32[]{:S(2)}) collective-permute-start(bf16[32,2048]{1,0:T(8,128)(2,1)S(1)} %get-tuple-element.146), channel_id=1, source_target_pairs={{0,6},{2,4},{4,2},{6,0},{1,7},{3,5},{5,3},{7,1},{8,14},{10,12},{12... | collective-permute-start | bytes 393224 | tf_op jit(solution)/shard_map/ppermute | solution.py:30
  98.9 8.9 %collective-permute-start.22 = (bf16[32,2048]{1,0:T(8,128)(2,1)S(1)}, bf16[32,2048]{1,0:T(8,128)(2,1)S(1)}, u32[]{:S(2)}, u32[]{:S(2)}) collective-permute-start(bf16[32,2048]{1,0:T(8,128)(2,1)S(1)} %get-tuple-element.157), channel_id=1, source_target_pairs={{0,2},{2,0},{4,6},{6,4},{1,3},{3,1},{5,7},{7,5},{8,10},{10,8},{12,... | collective-permute-start | bytes 393224 | tf_op jit(solution)/shard_map/ppermute | solution.py:30
  99.7 8.7 %collective-permute-start.23 = (bf16[32,2048]{1,0:T(8,128)(2,1)S(1)}, bf16[32,2048]{1,0:T(8,128)(2,1)S(1)}, u32[]{:S(2)}, u32[]{:S(2)}) collective-permute-start(bf16[32,2048]{1,0:T(8,128)(2,1)S(1)} %get-tuple-element.158), channel_id=1, source_target_pairs={{0,4},{2,6},{4,0},{6,2},{1,5},{3,7},{5,1},{7,3},{8,12},{10,14},{12... | collective-permute-start | bytes 393224 | tf_op jit(solution)/shard_map/ppermute | solution.py:30
  101.3 17.1 %collective-permute-start.28 = (bf16[64,2048]{1,0:T(8,128)(2,1)S(1)}, bf16[64,2048]{1,0:T(8,128)(2,1)S(1)}, u32[]{:S(2)}, u32[]{:S(2)}) collective-permute-start(bf16[64,2048]{1,0:T(8,128)(2,1)S(1)} %combine.5), channel_id=1, source_target_pairs={{0,24},{8,16},{16,8},{24,0},{1,25},{9,17},{17,9},{25,1},{2,26},{10... | collective-permute-start | bytes 786440 | tf_op jit(solution)/shard_map/ppermute | solution.py:30
  104.9 7.7 %collective-permute-start.24 = (bf16[32,2048]{1,0:T(8,128)(2,1)S(1)}, bf16[32,2048]{1,0:T(8,128)(2,1)S(1)}, u32[]{:S(2)}, u32[]{:S(2)}) collective-permute-start(bf16[32,2048]{1,0:T(8,128)(2,1)S(1)} %get-tuple-element.159), channel_id=1, source_target_pairs={{0,6},{2,4},{4,2},{6,0},{1,7},{3,5},{5,3},{7,1},{8,14},{10,12},{12... | collective-permute-start | bytes 393224 | tf_op jit(solution)/shard_map/ppermute | solution.py:30
  106.2 9.3 %collective-permute-start.33 = (bf16[32,2048]{1,0:T(8,128)(2,1)S(1)}, bf16[32,2048]{1,0:T(8,128)(2,1)S(1)}, u32[]{:S(2)}, u32[]{:S(2)}) collective-permute-start(bf16[32,2048]{1,0:T(8,128)(2,1)S(1)} %get-tuple-element.177), channel_id=1, source_target_pairs={{0,2},{2,0},{4,6},{6,4},{1,3},{3,1},{5,7},{7,5},{8,10},{10,8},{12,... | collective-permute-start | bytes 393224 | tf_op jit(solution)/shard_map/ppermute | solution.py:30
  107.8 7.7 %collective-permute-start.34 = (bf16[32,2048]{1,0:T(8,128)(2,1)S(1)}, bf16[32,2048]{1,0:T(8,128)(2,1)S(1)}, u32[]{:S(2)}, u32[]{:S(2)}) collective-permute-start(bf16[32,2048]{1,0:T(8,128)(2,1)S(1)} %get-tuple-element.178), channel_id=1, source_target_pairs={{0,4},{2,6},{4,0},{6,2},{1,5},{3,7},{5,1},{7,3},{8,12},{10,14},{12... | collective-permute-start | bytes 393224 | tf_op jit(solution)/shard_map/ppermute | solution.py:30
  108.4 7.1 %collective-permute-start.35 = (bf16[32,2048]{1,0:T(8,128)(2,1)S(1)}, bf16[32,2048]{1,0:T(8,128)(2,1)S(1)}, u32[]{:S(2)}, u32[]{:S(2)}) collective-permute-start(bf16[32,2048]{1,0:T(8,128)(2,1)S(1)} %get-tuple-element.179), channel_id=1, source_target_pairs={{0,6},{2,4},{4,2},{6,0},{1,7},{3,5},{5,3},{7,1},{8,14},{10,12},{12... | collective-permute-start | bytes 393224 | tf_op jit(solution)/shard_map/ppermute | solution.py:30
  112.8 14.7 %collective-permute-start.32 = (bf16[64,2048]{1,0:T(8,128)(2,1)S(1)}, bf16[64,2048]{1,0:T(8,128)(2,1)S(1)}, u32[]{:S(2)}, u32[]{:S(2)}) collective-permute-start(bf16[64,2048]{1,0:T(8,128)(2,1)S(1)} %combine.4), channel_id=1, source_target_pairs={{0,16},{8,24},{16,0},{24,8},{1,17},{9,25},{17,1},{25,9},{2,18},{10... | collective-permute-start | bytes 786440 | tf_op jit(solution)/shard_map/ppermute | solution.py:30
  115.7 11.8 %collective-permute-start.36 = (bf16[64,2048]{1,0:T(8,128)(2,1)S(1)}, bf16[64,2048]{1,0:T(8,128)(2,1)S(1)}, u32[]{:S(2)}, u32[]{:S(2)}) collective-permute-start(bf16[64,2048]{1,0:T(8,128)(2,1)S(1)} %combine.7), channel_id=1, source_target_pairs={{0,8},{8,0},{16,24},{24,16},{1,9},{9,1},{17,25},{25,17},{2,10},{10... | collective-permute-start | bytes 786440 | tf_op jit(solution)/shard_map/ppermute | solution.py:30
  118.4 6.5 %collective-permute-start.29 = (bf16[32,2048]{1,0:T(8,128)(2,1)S(1)}, bf16[32,2048]{1,0:T(8,128)(2,1)S(1)}, u32[]{:S(2)}, u32[]{:S(2)}) collective-permute-start(bf16[32,2048]{1,0:T(8,128)(2,1)S(1)} %copy-done.16), channel_id=1, source_target_pairs={{0,2},{2,0},{4,6},{6,4},{1,3},{3,1},{5,7},{7,5},{8,10},{10,8},{12,... | collective-permute-start | bytes 393224 | tf_op jit(solution)/shard_map/ppermute | solution.py:30
  119.9 5.0 %collective-permute-start.30 = (bf16[32,2048]{1,0:T(8,128)(2,1)S(1)}, bf16[32,2048]{1,0:T(8,128)(2,1)S(1)}, u32[]{:S(2)}, u32[]{:S(2)}) collective-permute-start(bf16[32,2048]{1,0:T(8,128)(2,1)S(1)} %copy-done.14), channel_id=1, source_target_pairs={{0,4},{2,6},{4,0},{6,2},{1,5},{3,7},{5,1},{7,3},{8,12},{10,14},{12... | collective-permute-start | bytes 393224 | tf_op jit(solution)/shard_map/ppermute | solution.py:30
  121.4 5.9 %collective-permute-start.31 = (bf16[32,2048]{1,0:T(8,128)(2,1)S(1)}, bf16[32,2048]{1,0:T(8,128)(2,1)S(1)}, u32[]{:S(2)}, u32[]{:S(2)}) collective-permute-start(bf16[32,2048]{1,0:T(8,128)(2,1)S(1)} %get-tuple-element.168), channel_id=1, source_target_pairs={{0,6},{2,4},{4,2},{6,0},{1,7},{3,5},{5,3},{7,1},{8,14},{10,12},{12... | collective-permute-start | bytes 393224 | tf_op jit(solution)/shard_map/ppermute | solution.py:30
  (35 other events, 444.5 us)

commit v17 on v16

--- a/solution.py
+++ b/solution.py
@@ -230,7 +230,7 @@
             pltpu.VMEM((group_columns, width), jnp.bfloat16),
             pltpu.SemaphoreType.DMA((6,)),
         ],
-        compiler_params=pltpu.CompilerParams(vmem_limit_bytes=60 * 2**20),
+        compiler_params=pltpu.CompilerParams(vmem_limit_bytes=58 * 2**20),
         cost_estimate=SMALL,
         name="attend",
     )(place, lengths, first, second, gain, weight, cosine, sine, reach, cache, outward)

time: 131 us -> 133 us (1.015); the launches traced: 129 us -> 134 us
  waiting for transfers between devices: 19.2 us -> 30 us
  starting transfers between devices: 48.8 us -> 39.6 us
  Pallas kernels: 46.5 us -> 50 us
    ppermute x37, waiting for transfers between devices: 19.2 us -> 30 us  [partner(): return lax.ppermute(value, axes, [(i, i ^ offset) for i in range(size)])]
    ppermute x37, starting transfers between devices: 48.8 us -> 39.6 us  [partner(): return lax.ppermute(value, axes, [(i, i ^ offset) for i in range(size)])]
    pallas_call x2, Pallas kernels: 14.6 us -> 16.8 us  [experts(): pl.pallas_call(functools.partial(expert_kernel, plane=plane, count=count,...]
    unnamed x62 -> x60, local copies, waits for them, and re-layouts: 7.51 us -> 7.54 us
  transfers between devices with their start and end apart: 37 -> 37, of which waited for: 10 -> 14; matrix products, arithmetic and copies ran while one was open for 5% -> 5% of each run, Pallas kernels for 34% -> 36%
where the time goes in v17:
time: 133 us; the launch traced here: 134 us
  Pallas kernels  50 us (38%)
  starting transfers between devices  39.6 us (30%)
  waiting for transfers between devices  30 us (23%)
  local copies, waits for them, and re-layouts  9.35 us (7%)
  other arithmetic  2.98 us (2%)
    ppermute x37, starting transfers between devices, partner(): return lax.ppermute(value, axes, [(i, i ^ offset) for i in range(size)])  39.6 us
    ppermute x37, waiting for transfers between devices, partner(): return lax.ppermute(value, axes, [(i, i ^ offset) for i in range(size)])  30 us
    pallas_call x2, Pallas kernels, experts(): pl.pallas_call(functools.partial(expert_kernel, plane=plane, count=count,...  16.8 us
    pallas_call x2, Pallas kernels, attend(): pl.pallas_call(functools.partial(attend_kernel, offset=offset), in_specs=...  15.6 us
    pallas_call x1, Pallas kernels, shared_terms(): pl.pallas_call(functools.partial(shared_kernel, side=side), in_specs=[in_...  8.21 us
    unnamed x60, local copies, waits for them, and re-layouts  7.54 us
    pallas_call x2, Pallas kernels, select(): pl.pallas_call(functools.partial(select_kernel, count=count, plane=plane,...  4.32 us
  transfers between devices with their start and end apart: 37, of which 14 were waited for; matrix products, arithmetic and copies ran while one was open for 5% of the time, Pallas kernels for 36%

profile of v17, /device:TPU:0, one launch (start us, length us, event | category | flops | bytes accessed | tf_op | source)
XLA Modules:
  0.0 134.0 jit_solution(17187323904886616214)
XLA Ops:
  2.9 2.6 %collective-permute-start = (bf16[64,2048]{1,0:T(8,128)(2,1)}, bf16[64,2048]{1,0:T(8,128)(2,1)}, u32[]{:S(2)}, u32[]{:S(2)}) collective-permute-start(bf16[64,2048]{1,0:T(8,128)(2,1)} %bitcast.25), channel_id=1, source_target_pairs={{0,2},{2,0},{1,3},{3,1},{4,6},{6,4},{5,7},{7,5},{8,10},{10,8},{9,1... | collective-permute-start | bytes 786440 | tf_op jit(solution)/shard_map/ppermute | solution.py:30
  7.5 2.0 %prepare.1 = (f32[4,64,64]{2,1,0:T(8,128)S(1)}, f32[4,64,128]{2,1,0:T(8,128)S(1)}, f32[4,64,128]{2,1,0:T(8,128)S(1)}) custom-call(s32[4]{0:T(128)S(1)} %copy-done.10, s32[4,64]{1,0:T(4,128)S(1)} %copy-done.11, f32[1,128]{1,0:T(1,128)S(1)} %copy-done.12), custom_call_target="tpu_custom_call" | custom-call | flops 1024 | bytes 1024 | tf_op jit(solution)/shard_map/prepare/pallas_call | solution.py:69
  12.7 2.6 %collective-permute-done.2.second = bf16[64,2048]{1,0:T(8,128)(2,1)S(1)} collective-permute-done((bf16[64,2048]{1,0:T(8,128)(2,1)}, bf16[64,2048]{1,0:T(8,128)(2,1)S(1)}, u32[]{:S(2)}, u32[]{:S(2)}) %collective-permute-start.2) | collective-permute-done | bytes 262176 | tf_op jit(solution)/shard_map/ppermute | solution.py:30
  16.9 7.5 %attend.2 = (f32[64,2048]{1,0:T(8,128)}, bf16[64,2048]{1,0:T(8,128)(2,1)}, bf16[64,256]{1,0:T(8,128)(2,1)}, bf16[64,256]{1,0:T(8,128)(2,1)}) custom-call(s32[1]{0:T(128)} %bitcast.2.place, s32[4]{0:T(128)} %lengths.5, bf16[64,2048]{1,0:T(8,128)(2,1)} %collective-permute-done.first, bf16[64,2048]{1,0:T(8,128)(2,1)} %copy-done.21, f32[1,2048]{1,0:T(1,128)} %bitcast.37, ...), custom_call_target="tpu_custom_call" | custom-call | flops 1024 | bytes 1024 | tf_op jit(solution)/shard_map/attend/pallas_call | solution.py:205
  24.6 1.6 %collective-permute-done.5 = bf16[64,2048]{1,0:T(8,128)(2,1)S(1)} collective-permute-done((bf16[64,2048]{1,0:T(8,128)(2,1)}, bf16[64,2048]{1,0:T(8,128)(2,1)S(1)}, u32[]{:S(2)}, u32[]{:S(2)}) %collective-permute-start.5) | collective-permute-done | bytes 262176 | tf_op jit(solution)/shard_map/ppermute | solution.py:30
  26.4 1.8 %add_convert_fusion = bf16[64,2048]{1,0:T(8,128)(2,1)} fusion(f32[64,2048]{1,0:T(8,128)} %get-tuple-element.108, bf16[64,2048]{1,0:T(8,128)(2,1)S(1)} %collective-permute-done.5), kind=kLoop, calls=%fused_computation.4 | loop fusion | flops 393216 | bytes 1048576 | tf_op jit(solution)/shard_map/convert_element_type | solution.py:596
  29.7 8.2 %attend.3 = (f32[64,2048]{1,0:T(8,128)}, bf16[64,2048]{1,0:T(8,128)(2,1)}, bf16[64,256]{1,0:T(8,128)(2,1)}, bf16[64,256]{1,0:T(8,128)(2,1)}) custom-call(s32[1]{0:T(128)} %bitcast.2.place, s32[4]{0:T(128)} %lengths.5, bf16[64,2048]{1,0:T(8,128)(2,1)} %bitcast.26, bf16[64,2048]{1,0:T(8,128)(2,1)} %copy-done.20, f32[1,2048]{1,0:T(1,128)} %bitcast.38, ...), custom_call_target="tpu_custom_call" | custom-call | flops 1024 | bytes 1024 | tf_op jit(solution)/shard_map/attend/pallas_call | solution.py:205
  41.5 4.6 %collective-permute-start.12 = (bf16[64,2176]{1,0:T(8,128)(2,1)}, bf16[64,2176]{1,0:T(8,128)(2,1)}, u32[]{:S(2)}, u32[]{:S(2)}) collective-permute-start(bf16[64,2176]{1,0:T(8,128)(2,1)} %get-tuple-element.124.refs_2_), channel_id=1, source_target_pairs={{0,24},{8,16},{16,8},{24,0},{1,25},{9,17},{17,9},{25,1},{2,26},{10... | collective-permute-start | bytes 835592 | tf_op jit(solution)/shard_map/ppermute | solution.py:30
  46.6 4.0 %collective-permute-start.11 = (bf16[64,2048]{1,0:T(8,128)(2,1)}, bf16[64,2048]{1,0:T(8,128)(2,1)}, u32[]{:S(2)}, u32[]{:S(2)}) collective-permute-start(bf16[64,2048]{1,0:T(8,128)(2,1)} %get-tuple-element.119.refs_0_), channel_id=1, source_target_pairs={{0,2},{2,0},{1,3},{3,1},{4,6},{6,4},{5,7},{7,5},{8,10},{10,8},{9,1... | collective-permute-start | bytes 786440 | tf_op jit(solution)/shard_map/ppermute | solution.py:30
  50.9 6.1 %collective-permute-done.11.refs_1_ = bf16[64,2048]{1,0:T(8,128)(2,1)} collective-permute-done((bf16[64,2048]{1,0:T(8,128)(2,1)}, bf16[64,2048]{1,0:T(8,128)(2,1)}, u32[]{:S(2)}, u32[]{:S(2)}) %collective-permute-start.11) | collective-permute-done | bytes 262176 | tf_op jit(solution)/shard_map/ppermute | solution.py:30
  57.0 8.2 %shared.1 = (f32[64,2048]{1,0:T(8,128)}, bf16[64,2048]{1,0:T(8,128)(2,1)}) custom-call(bf16[64,2048]{1,0:T(8,128)(2,1)} %get-tuple-element.119.refs_0_, bf16[64,2048]{1,0:T(8,128)(2,1)} %collective-permute-done.11.refs_1_, bf16[352,2048]{1,0:T(8,128)(2,1)} %bitcast.33, bf16[352,2048]{1,0:T(8,128)(2,1)} %bitcast.35, bf16[352,2048]{1,0:T(8,128)(2,1)} %refs_4_.1, ...), custom_call_target="tpu_custom_call" | custom-call | flops 1024 | bytes 1024 | tf_op jit(solution)/shard_map/shared/pallas_call | solution.py:361
  65.2 2.2 %select.2 = (bf16[64,2048]{1,0:T(8,128)(2,1)S(1)}, bf16[64,2048]{1,0:T(8,128)(2,1)S(1)}, bf16[64,2048]{1,0:T(8,128)(2,1)S(1)}, bf16[64,2048]{1,0:T(8,128)(2,1)S(...) custom-call(s32[4]{0:T(128)S(1)} %xor_add_fusion.refs_0_, bf16[2048,16]{1,0:T(8,128)(2,1)S(1)} %copy.21.refs_1_, ...), custom_call_target="tpu_custom_call" | custom-call | flops 1024 | bytes 1024 | tf_op jit(solution)/shard_map/select/pallas_call | solution.py:468
  67.4 1.8 %collective-permute-start.13 = (bf16[64,2048]{1,0:T(8,128)(2,1)S(1)}, bf16[64,2048]{1,0:T(8,128)(2,1)S(1)}, u32[]{:S(2)}, u32[]{:S(2)}) collective-permute-start(bf16[64,2048]{1,0:T(8,128)(2,1)S(1)} %get-tuple-element.129), channel_id=1, source_target_pairs={{0,2},{2,0},{4,6},{6,4},{1,3},{3,1},{5,7},{7,5},{8,10},{10,8},{12,... | collective-permute-start | bytes 786440 | tf_op jit(solution)/shard_map/ppermute | solution.py:30
  69.2 1.7 %collective-permute-start.15 = (bf16[64,2048]{1,0:T(8,128)(2,1)S(1)}, bf16[64,2048]{1,0:T(8,128)(2,1)S(1)}, u32[]{:S(2)}, u32[]{:S(2)}) collective-permute-start(bf16[64,2048]{1,0:T(8,128)(2,1)S(1)} %get-tuple-element.131), channel_id=1, source_target_pairs={{0,6},{2,4},{4,2},{6,0},{1,7},{3,5},{5,3},{7,1},{8,14},{10,12},{12... | collective-permute-start | bytes 786440 | tf_op jit(solution)/shard_map/ppermute | solution.py:30
  71.0 2.2 %select.3 = (bf16[64,2048]{1,0:T(8,128)(2,1)S(1)}, bf16[64,2048]{1,0:T(8,128)(2,1)S(1)}, bf16[64,2048]{1,0:T(8,128)(2,1)S(1)}, bf16[64,2048]{1,0:T(8,128)(2,1)S(...) custom-call(s32[4]{0:T(128)S(1)} %xor_add_fusion.refs_0_, bf16[2048,16]{1,0:T(8,128)(2,1)S(1)} %copy.21.refs_1_, ...), custom_call_target="tpu_custom_call" | custom-call | flops 23000000512 | bytes 72000000 | tf_op jit(solution)/shard_map/select/pallas_call | solution.py:468
  73.2 1.8 %collective-permute-start.18 = (bf16[64,2048]{1,0:T(8,128)(2,1)S(1)}, bf16[64,2048]{1,0:T(8,128)(2,1)S(1)}, u32[]{:S(2)}, u32[]{:S(2)}) collective-permute-start(bf16[64,2048]{1,0:T(8,128)(2,1)S(1)} %get-tuple-element.140), channel_id=1, source_target_pairs={{0,2},{2,0},{4,6},{6,4},{1,3},{3,1},{5,7},{7,5},{8,10},{10,8},{12,... | collective-permute-start | bytes 786440 | tf_op jit(solution)/shard_map/ppermute | solution.py:30
  75.0 1.8 %collective-permute-done.13.refs_1_ = bf16[64,2048]{1,0:T(8,128)(2,1)S(1)} collective-permute-done((bf16[64,2048]{1,0:T(8,128)(2,1)S(1)}, bf16[64,2048]{1,0:T(8,128)(2,1)S(1)}, u32[]{:S(2)}, u32[]{:S(2)}) %collective-permute-start.13) | collective-permute-done | bytes 262176 | tf_op jit(solution)/shard_map/ppermute | solution.py:30
  77.5 6.4 %collective-permute-done.14.refs_2_ = bf16[64,2048]{1,0:T(8,128)(2,1)S(1)} collective-permute-done((bf16[64,2048]{1,0:T(8,128)(2,1)S(1)}, bf16[64,2048]{1,0:T(8,128)(2,1)S(1)}, u32[]{:S(2)}, u32[]{:S(2)}) %collective-permute-start.14) | collective-permute-done | bytes 262176 | tf_op jit(solution)/shard_map/ppermute | solution.py:30
  83.9 8.4 %expert.2 = (bf16[32,2048]{1,0:T(8,128)(2,1)S(1)}, bf16[32,2048]{1,0:T(8,128)(2,1)S(1)}, bf16[32,2048]{1,0:T(8,128)(2,1)S(1)}, bf16[32,2048]{1,0:T(8,128)(2,1)S(...) custom-call(bf16[64,2048]{1,0:T(8,128)(2,1)S(1)} %get-tuple-element., ...), custom_call_target="tpu_custom_call" | custom-call | flops 1024 | bytes 1024 | tf_op jit(solution)/shard_map/expert/pallas_call | solution.py:303
  93.6 2.0 %collective-permute-start.25 = (bf16[32,2048]{1,0:T(8,128)(2,1)S(1)}, bf16[32,2048]{1,0:T(8,128)(2,1)S(1)}, u32[]{:S(2)}, u32[]{:S(2)}) collective-permute-start(bf16[32,2048]{1,0:T(8,128)(2,1)S(1)} %get-tuple-element.144), channel_id=1, source_target_pairs={{0,2},{2,0},{4,6},{6,4},{1,3},{3,1},{5,7},{7,5},{8,10},{10,8},{12,... | collective-permute-start | bytes 393224 | tf_op jit(solution)/shard_map/ppermute | solution.py:30
  95.7 1.5 %collective-permute-start.27 = (bf16[32,2048]{1,0:T(8,128)(2,1)S(1)}, bf16[32,2048]{1,0:T(8,128)(2,1)S(1)}, u32[]{:S(2)}, u32[]{:S(2)}) collective-permute-start(bf16[32,2048]{1,0:T(8,128)(2,1)S(1)} %get-tuple-element.146), channel_id=1, source_target_pairs={{0,6},{2,4},{4,2},{6,0},{1,7},{3,5},{5,3},{7,1},{8,14},{10,12},{12... | collective-permute-start | bytes 393224 | tf_op jit(solution)/shard_map/ppermute | solution.py:30
  97.1 8.4 %expert.3 = (bf16[32,2048]{1,0:T(8,128)(2,1)S(1)}, bf16[32,2048]{1,0:T(8,128)(2,1)S(1)}, bf16[32,2048]{1,0:T(8,128)(2,1)S(1)}, bf16[32,2048]{1,0:T(8,128)(2,1)S(...) custom-call(bf16[64,2048]{1,0:T(8,128)(2,1)S(1)} %get-tuple-element., ...), custom_call_target="tpu_custom_call" | custom-call | flops 1024 | bytes 1024 | tf_op jit(solution)/shard_map/expert/pallas_call | solution.py:303
  105.7 2.1 %collective-permute-start.22 = (bf16[32,2048]{1,0:T(8,128)(2,1)S(1)}, bf16[32,2048]{1,0:T(8,128)(2,1)S(1)}, u32[]{:S(2)}, u32[]{:S(2)}) collective-permute-start(bf16[32,2048]{1,0:T(8,128)(2,1)S(1)} %get-tuple-element.157), channel_id=1, source_target_pairs={{0,2},{2,0},{4,6},{6,4},{1,3},{3,1},{5,7},{7,5},{8,10},{10,8},{12,... | collective-permute-start | bytes 393224 | tf_op jit(solution)/shard_map/ppermute | solution.py:30
  108.0 3.9 %collective-permute-start.28 = (bf16[64,2048]{1,0:T(8,128)(2,1)S(1)}, bf16[64,2048]{1,0:T(8,128)(2,1)S(1)}, u32[]{:S(2)}, u32[]{:S(2)}) collective-permute-start(bf16[64,2048]{1,0:T(8,128)(2,1)S(1)} %combine.5), channel_id=1, source_target_pairs={{0,24},{8,16},{16,8},{24,0},{1,25},{9,17},{17,9},{25,1},{2,26},{10... | collective-permute-start | bytes 786440 | tf_op jit(solution)/shard_map/ppermute | solution.py:30
  111.9 1.7 %collective-permute-start.24 = (bf16[32,2048]{1,0:T(8,128)(2,1)S(1)}, bf16[32,2048]{1,0:T(8,128)(2,1)S(1)}, u32[]{:S(2)}, u32[]{:S(2)}) collective-permute-start(bf16[32,2048]{1,0:T(8,128)(2,1)S(1)} %get-tuple-element.159), channel_id=1, source_target_pairs={{0,6},{2,4},{4,2},{6,0},{1,7},{3,5},{5,3},{7,1},{8,14},{10,12},{12... | collective-permute-start | bytes 393224 | tf_op jit(solution)/shard_map/ppermute | solution.py:30
  113.6 1.7 %collective-permute-start.33 = (bf16[32,2048]{1,0:T(8,128)(2,1)S(1)}, bf16[32,2048]{1,0:T(8,128)(2,1)S(1)}, u32[]{:S(2)}, u32[]{:S(2)}) collective-permute-start(bf16[32,2048]{1,0:T(8,128)(2,1)S(1)} %get-tuple-element.177), channel_id=1, source_target_pairs={{0,2},{2,0},{4,6},{6,4},{1,3},{3,1},{5,7},{7,5},{8,10},{10,8},{12,... | collective-permute-start | bytes 393224 | tf_op jit(solution)/shard_map/ppermute | solution.py:30
  115.4 1.7 %collective-permute-start.35 = (bf16[32,2048]{1,0:T(8,128)(2,1)S(1)}, bf16[32,2048]{1,0:T(8,128)(2,1)S(1)}, u32[]{:S(2)}, u32[]{:S(2)}) collective-permute-start(bf16[32,2048]{1,0:T(8,128)(2,1)S(1)} %get-tuple-element.179), channel_id=1, source_target_pairs={{0,6},{2,4},{4,2},{6,0},{1,7},{3,5},{5,3},{7,1},{8,14},{10,12},{12... | collective-permute-start | bytes 393224 | tf_op jit(solution)/shard_map/ppermute | solution.py:30
  117.1 1.5 %collective-permute-done.24.refs_3_ = bf16[32,2048]{1,0:T(8,128)(2,1)S(1)} collective-permute-done((bf16[32,2048]{1,0:T(8,128)(2,1)S(1)}, bf16[32,2048]{1,0:T(8,128)(2,1)S(1)}, u32[]{:S(2)}, u32[]{:S(2)}) %collective-permute-start.24) | collective-permute-done | bytes 131104 | tf_op jit(solution)/shard_map/ppermute | solution.py:30
  118.9 3.4 %collective-permute-done.33.refs_1_ = bf16[32,2048]{1,0:T(8,128)(2,1)S(1)} collective-permute-done((bf16[32,2048]{1,0:T(8,128)(2,1)S(1)}, bf16[32,2048]{1,0:T(8,128)(2,1)S(1)}, u32[]{:S(2)}, u32[]{:S(2)}) %collective-permute-start.33) | collective-permute-done | bytes 131104 | tf_op jit(solution)/shard_map/ppermute | solution.py:30
  122.3 1.5 %collective-permute-done.34.refs_2_ = bf16[32,2048]{1,0:T(8,128)(2,1)S(1)} collective-permute-done((bf16[32,2048]{1,0:T(8,128)(2,1)S(1)}, bf16[32,2048]{1,0:T(8,128)(2,1)S(1)}, u32[]{:S(2)}, u32[]{:S(2)}) %collective-permute-start.34) | collective-permute-done | bytes 131104 | tf_op jit(solution)/shard_map/ppermute | solution.py:30
  126.7 1.7 %collective-permute-start.31 = (bf16[32,2048]{1,0:T(8,128)(2,1)S(1)}, bf16[32,2048]{1,0:T(8,128)(2,1)S(1)}, u32[]{:S(2)}, u32[]{:S(2)}) collective-permute-start(bf16[32,2048]{1,0:T(8,128)(2,1)S(1)} %get-tuple-element.168), channel_id=1, source_target_pairs={{0,6},{2,4},{4,2},{6,0},{1,7},{3,5},{5,3},{7,1},{8,14},{10,12},{12... | collective-permute-start | bytes 393224 | tf_op jit(solution)/shard_map/ppermute | solution.py:30
  130.5 2.0 %collective-permute-done.31.refs_3_ = bf16[32,2048]{1,0:T(8,128)(2,1)S(1)} collective-permute-done((bf16[32,2048]{1,0:T(8,128)(2,1)S(1)}, bf16[32,2048]{1,0:T(8,128)(2,1)S(1)}, u32[]{:S(2)}, u32[]{:S(2)}) %collective-permute-start.31) | collective-permute-done | bytes 131104 | tf_op jit(solution)/shard_map/ppermute | solution.py:30
  (125 shorter events, 24.5 us)
Async XLA Ops:
  2.5 13.3 %collective-permute-start.4 = (bf16[704,2048]{1,0:T(8,128)(2,1)}, bf16[704,2048]{1,0:T(8,128)(2,1)S(1)}, u32[]{:S(2)}, u32[]{:S(2)}) collective-permute-start(bf16[704,2048]{1,0:T(8,128)(2,1)} %bitcast.21), channel_id=1, source_target_pairs={{0,1},{1,0},{2,3},{3,2},{4,5},{5,4},{6,7},{7,6},{8,9},{9,8},{10,11... | collective-permute-start | bytes 8650760 | tf_op jit(solution)/shard_map/ppermute | solution.py:30
  2.9 9.8 %collective-permute-start = (bf16[64,2048]{1,0:T(8,128)(2,1)}, bf16[64,2048]{1,0:T(8,128)(2,1)}, u32[]{:S(2)}, u32[]{:S(2)}) collective-permute-start(bf16[64,2048]{1,0:T(8,128)(2,1)} %bitcast.25), channel_id=1, source_target_pairs={{0,2},{2,0},{1,3},{3,1},{4,6},{6,4},{5,7},{7,5},{8,10},{10,8},{9,1... | collective-permute-start | bytes 786440 | tf_op jit(solution)/shard_map/ppermute | solution.py:30
  15.3 9.3 %collective-permute-start.6 = (bf16[352,2048]{1,0:T(8,128)(2,1)}, bf16[352,2048]{1,0:T(8,128)(2,1)S(1)}, u32[]{:S(2)}, u32[]{:S(2)}) collective-permute-start(bf16[352,2048]{1,0:T(8,128)(2,1)} %bitcast.34), channel_id=1, source_target_pairs={{0,1},{1,0},{2,3},{3,2},{4,5},{5,4},{6,7},{7,6},{8,9},{9,8},{10,11... | collective-permute-start | bytes 4325384 | tf_op jit(solution)/shard_map/ppermute | solution.py:30
  15.4 9.2 %collective-permute-start.7 = (bf16[352,2048]{1,0:T(8,128)(2,1)}, bf16[352,2048]{1,0:T(8,128)(2,1)S(1)}, u32[]{:S(2)}, u32[]{:S(2)}) collective-permute-start(bf16[352,2048]{1,0:T(8,128)(2,1)} %refs_4_.1), channel_id=1, source_target_pairs={{0,1},{1,0},{2,3},{3,2},{4,5},{5,4},{6,7},{7,6},{8,9},{9,8},{10,11... | collective-permute-start | bytes 4325384 | tf_op jit(solution)/shard_map/ppermute | solution.py:30
  26.2 13.0 %collective-permute-start.9 = (bf16[2048,1408]{1,0:T(8,128)(2,1)}, bf16[2048,1408]{1,0:T(8,128)(2,1)}, u32[]{:S(2)}, u32[]{:S(2)}) collective-permute-start(bf16[2048,1408]{1,0:T(8,128)(2,1)} %bitcast.8.refs_4_), channel_id=1, source_target_pairs={{0,1},{1,0},{2,3},{3,2},{4,5},{5,4},{6,7},{7,6},{8,9},{9,8},{10,11... | collective-permute-start | bytes 17301512 | tf_op jit(solution)/shard_map/ppermute | solution.py:30
  28.2 9.9 %collective-permute-start.8 = (bf16[64,2048]{1,0:T(8,128)(2,1)}, bf16[64,2048]{1,0:T(8,128)(2,1)}, u32[]{:S(2)}, u32[]{:S(2)}) collective-permute-start(bf16[64,2048]{1,0:T(8,128)(2,1)} %add_convert_fusion), channel_id=1, source_target_pairs={{0,2},{2,0},{1,3},{3,1},{4,6},{6,4},{5,7},{7,5},{8,10},{10,8},{9,1... | collective-permute-start | bytes 786440 | tf_op jit(solution)/shard_map/ppermute | solution.py:30
  41.5 23.8 %collective-permute-start.12 = (bf16[64,2176]{1,0:T(8,128)(2,1)}, bf16[64,2176]{1,0:T(8,128)(2,1)}, u32[]{:S(2)}, u32[]{:S(2)}) collective-permute-start(bf16[64,2176]{1,0:T(8,128)(2,1)} %get-tuple-element.124.refs_2_), channel_id=1, source_target_pairs={{0,24},{8,16},{16,8},{24,0},{1,25},{9,17},{17,9},{25,1},{2,26},{10... | collective-permute-start | bytes 835592 | tf_op jit(solution)/shard_map/ppermute | solution.py:30
  46.1 25.0 %collective-permute-start.16 = (bf16[64,2176]{1,0:T(8,128)(2,1)}, bf16[64,2176]{1,0:T(8,128)(2,1)}, u32[]{:S(2)}, u32[]{:S(2)}) collective-permute-start(bf16[64,2176]{1,0:T(8,128)(2,1)} %get-tuple-element.124.refs_2_), channel_id=1, source_target_pairs={{0,16},{8,24},{16,0},{24,8},{1,17},{9,25},{17,1},{25,9},{2,18},{10... | collective-permute-start | bytes 835592 | tf_op jit(solution)/shard_map/ppermute | solution.py:30
  46.4 24.6 %collective-permute-start.17 = (bf16[64,2176]{1,0:T(8,128)(2,1)}, bf16[64,2176]{1,0:T(8,128)(2,1)}, u32[]{:S(2)}, u32[]{:S(2)}) collective-permute-start(bf16[64,2176]{1,0:T(8,128)(2,1)} %get-tuple-element.124.refs_2_), channel_id=1, source_target_pairs={{0,8},{8,0},{16,24},{24,16},{1,9},{9,1},{17,25},{25,17},{2,10},{10... | collective-permute-start | bytes 835592 | tf_op jit(solution)/shard_map/ppermute | solution.py:30
  46.6 10.4 %collective-permute-start.11 = (bf16[64,2048]{1,0:T(8,128)(2,1)}, bf16[64,2048]{1,0:T(8,128)(2,1)}, u32[]{:S(2)}, u32[]{:S(2)}) collective-permute-start(bf16[64,2048]{1,0:T(8,128)(2,1)} %get-tuple-element.119.refs_0_), channel_id=1, source_target_pairs={{0,2},{2,0},{1,3},{3,1},{4,6},{6,4},{5,7},{7,5},{8,10},{10,8},{9,1... | collective-permute-start | bytes 786440 | tf_op jit(solution)/shard_map/ppermute | solution.py:30
  67.4 9.3 %collective-permute-start.13 = (bf16[64,2048]{1,0:T(8,128)(2,1)S(1)}, bf16[64,2048]{1,0:T(8,128)(2,1)S(1)}, u32[]{:S(2)}, u32[]{:S(2)}) collective-permute-start(bf16[64,2048]{1,0:T(8,128)(2,1)S(1)} %get-tuple-element.129), channel_id=1, source_target_pairs={{0,2},{2,0},{4,6},{6,4},{1,3},{3,1},{5,7},{7,5},{8,10},{10,8},{12,... | collective-permute-start | bytes 786440 | tf_op jit(solution)/shard_map/ppermute | solution.py:30
  69.2 14.6 %collective-permute-start.14 = (bf16[64,2048]{1,0:T(8,128)(2,1)S(1)}, bf16[64,2048]{1,0:T(8,128)(2,1)S(1)}, u32[]{:S(2)}, u32[]{:S(2)}) collective-permute-start(bf16[64,2048]{1,0:T(8,128)(2,1)S(1)} %get-tuple-element.130), channel_id=1, source_target_pairs={{0,4},{2,6},{4,0},{6,2},{1,5},{3,7},{5,1},{7,3},{8,12},{10,14},{12... | collective-permute-start | bytes 786440 | tf_op jit(solution)/shard_map/ppermute | solution.py:30
  69.2 14.6 %collective-permute-start.15 = (bf16[64,2048]{1,0:T(8,128)(2,1)S(1)}, bf16[64,2048]{1,0:T(8,128)(2,1)S(1)}, u32[]{:S(2)}, u32[]{:S(2)}) collective-permute-start(bf16[64,2048]{1,0:T(8,128)(2,1)S(1)} %get-tuple-element.131), channel_id=1, source_target_pairs={{0,6},{2,4},{4,2},{6,0},{1,7},{3,5},{5,3},{7,1},{8,14},{10,12},{12... | collective-permute-start | bytes 786440 | tf_op jit(solution)/shard_map/ppermute | solution.py:30
  73.2 22.5 %collective-permute-start.18 = (bf16[64,2048]{1,0:T(8,128)(2,1)S(1)}, bf16[64,2048]{1,0:T(8,128)(2,1)S(1)}, u32[]{:S(2)}, u32[]{:S(2)}) collective-permute-start(bf16[64,2048]{1,0:T(8,128)(2,1)S(1)} %get-tuple-element.140), channel_id=1, source_target_pairs={{0,2},{2,0},{4,6},{6,4},{1,3},{3,1},{5,7},{7,5},{8,10},{10,8},{12,... | collective-permute-start | bytes 786440 | tf_op jit(solution)/shard_map/ppermute | solution.py:30
  75.0 20.7 %collective-permute-start.19 = (bf16[64,2048]{1,0:T(8,128)(2,1)S(1)}, bf16[64,2048]{1,0:T(8,128)(2,1)S(1)}, u32[]{:S(2)}, u32[]{:S(2)}) collective-permute-start(bf16[64,2048]{1,0:T(8,128)(2,1)S(1)} %get-tuple-element.141), channel_id=1, source_target_pairs={{0,4},{2,6},{4,0},{6,2},{1,5},{3,7},{5,1},{7,3},{8,12},{10,14},{12... | collective-permute-start | bytes 786440 | tf_op jit(solution)/shard_map/ppermute | solution.py:30
  76.7 20.4 %collective-permute-start.20 = (bf16[64,2048]{1,0:T(8,128)(2,1)S(1)}, bf16[64,2048]{1,0:T(8,128)(2,1)S(1)}, u32[]{:S(2)}, u32[]{:S(2)}) collective-permute-start(bf16[64,2048]{1,0:T(8,128)(2,1)S(1)} %get-tuple-element.142), channel_id=1, source_target_pairs={{0,6},{2,4},{4,2},{6,0},{1,7},{3,5},{5,3},{7,1},{8,14},{10,12},{12... | collective-permute-start | bytes 786440 | tf_op jit(solution)/shard_map/ppermute | solution.py:30
  83.9 21.8 %collective-permute-start.21 = (bf16[64,2048]{1,0:T(8,128)(2,1)S(1)}, bf16[64,2048]{1,0:T(8,128)(2,1)S(1)}, u32[]{:S(2)}, u32[]{:S(2)}) collective-permute-start(bf16[64,2048]{1,0:T(8,128)(2,1)S(1)} %copy-done.25), channel_id=1, source_target_pairs={{0,2},{2,0},{1,3},{3,1},{4,6},{6,4},{5,7},{7,5},{8,10},{10,8},{9,1... | collective-permute-start | bytes 786440 | tf_op jit(solution)/shard_map/ppermute | solution.py:30
  93.6 14.2 %collective-permute-start.25 = (bf16[32,2048]{1,0:T(8,128)(2,1)S(1)}, bf16[32,2048]{1,0:T(8,128)(2,1)S(1)}, u32[]{:S(2)}, u32[]{:S(2)}) collective-permute-start(bf16[32,2048]{1,0:T(8,128)(2,1)S(1)} %get-tuple-element.144), channel_id=1, source_target_pairs={{0,2},{2,0},{4,6},{6,4},{1,3},{3,1},{5,7},{7,5},{8,10},{10,8},{12,... | collective-permute-start | bytes 393224 | tf_op jit(solution)/shard_map/ppermute | solution.py:30
  95.6 12.2 %collective-permute-start.26 = (bf16[32,2048]{1,0:T(8,128)(2,1)S(1)}, bf16[32,2048]{1,0:T(8,128)(2,1)S(1)}, u32[]{:S(2)}, u32[]{:S(2)}) collective-permute-start(bf16[32,2048]{1,0:T(8,128)(2,1)S(1)} %get-tuple-element.145), channel_id=1, source_target_pairs={{0,4},{2,6},{4,0},{6,2},{1,5},{3,7},{5,1},{7,3},{8,12},{10,14},{12... | collective-permute-start | bytes 393224 | tf_op jit(solution)/shard_map/ppermute | solution.py:30
  95.7 12.2 %collective-permute-start.27 = (bf16[32,2048]{1,0:T(8,128)(2,1)S(1)}, bf16[32,2048]{1,0:T(8,128)(2,1)S(1)}, u32[]{:S(2)}, u32[]{:S(2)}) collective-permute-start(bf16[32,2048]{1,0:T(8,128)(2,1)S(1)} %get-tuple-element.146), channel_id=1, source_target_pairs={{0,6},{2,4},{4,2},{6,0},{1,7},{3,5},{5,3},{7,1},{8,14},{10,12},{12... | collective-permute-start | bytes 393224 | tf_op jit(solution)/shard_map/ppermute | solution.py:30
  105.7 9.7 %collective-permute-start.22 = (bf16[32,2048]{1,0:T(8,128)(2,1)S(1)}, bf16[32,2048]{1,0:T(8,128)(2,1)S(1)}, u32[]{:S(2)}, u32[]{:S(2)}) collective-permute-start(bf16[32,2048]{1,0:T(8,128)(2,1)S(1)} %get-tuple-element.157), channel_id=1, source_target_pairs={{0,2},{2,0},{4,6},{6,4},{1,3},{3,1},{5,7},{7,5},{8,10},{10,8},{12,... | collective-permute-start | bytes 393224 | tf_op jit(solution)/shard_map/ppermute | solution.py:30
  107.7 7.7 %collective-permute-start.23 = (bf16[32,2048]{1,0:T(8,128)(2,1)S(1)}, bf16[32,2048]{1,0:T(8,128)(2,1)S(1)}, u32[]{:S(2)}, u32[]{:S(2)}) collective-permute-start(bf16[32,2048]{1,0:T(8,128)(2,1)S(1)} %get-tuple-element.158), channel_id=1, source_target_pairs={{0,4},{2,6},{4,0},{6,2},{1,5},{3,7},{5,1},{7,3},{8,12},{10,14},{12... | collective-permute-start | bytes 393224 | tf_op jit(solution)/shard_map/ppermute | solution.py:30
  108.0 16.8 %collective-permute-start.28 = (bf16[64,2048]{1,0:T(8,128)(2,1)S(1)}, bf16[64,2048]{1,0:T(8,128)(2,1)S(1)}, u32[]{:S(2)}, u32[]{:S(2)}) collective-permute-start(bf16[64,2048]{1,0:T(8,128)(2,1)S(1)} %combine.5), channel_id=1, source_target_pairs={{0,24},{8,16},{16,8},{24,0},{1,25},{9,17},{17,9},{25,1},{2,26},{10... | collective-permute-start | bytes 786440 | tf_op jit(solution)/shard_map/ppermute | solution.py:30
  111.9 6.7 %collective-permute-start.24 = (bf16[32,2048]{1,0:T(8,128)(2,1)S(1)}, bf16[32,2048]{1,0:T(8,128)(2,1)S(1)}, u32[]{:S(2)}, u32[]{:S(2)}) collective-permute-start(bf16[32,2048]{1,0:T(8,128)(2,1)S(1)} %get-tuple-element.159), channel_id=1, source_target_pairs={{0,6},{2,4},{4,2},{6,0},{1,7},{3,5},{5,3},{7,1},{8,14},{10,12},{12... | collective-permute-start | bytes 393224 | tf_op jit(solution)/shard_map/ppermute | solution.py:30
  113.6 8.7 %collective-permute-start.33 = (bf16[32,2048]{1,0:T(8,128)(2,1)S(1)}, bf16[32,2048]{1,0:T(8,128)(2,1)S(1)}, u32[]{:S(2)}, u32[]{:S(2)}) collective-permute-start(bf16[32,2048]{1,0:T(8,128)(2,1)S(1)} %get-tuple-element.177), channel_id=1, source_target_pairs={{0,2},{2,0},{4,6},{6,4},{1,3},{3,1},{5,7},{7,5},{8,10},{10,8},{12,... | collective-permute-start | bytes 393224 | tf_op jit(solution)/shard_map/ppermute | solution.py:30
  115.3 8.5 %collective-permute-start.34 = (bf16[32,2048]{1,0:T(8,128)(2,1)S(1)}, bf16[32,2048]{1,0:T(8,128)(2,1)S(1)}, u32[]{:S(2)}, u32[]{:S(2)}) collective-permute-start(bf16[32,2048]{1,0:T(8,128)(2,1)S(1)} %get-tuple-element.178), channel_id=1, source_target_pairs={{0,4},{2,6},{4,0},{6,2},{1,5},{3,7},{5,1},{7,3},{8,12},{10,14},{12... | collective-permute-start | bytes 393224 | tf_op jit(solution)/shard_map/ppermute | solution.py:30
  115.4 8.4 %collective-permute-start.35 = (bf16[32,2048]{1,0:T(8,128)(2,1)S(1)}, bf16[32,2048]{1,0:T(8,128)(2,1)S(1)}, u32[]{:S(2)}, u32[]{:S(2)}) collective-permute-start(bf16[32,2048]{1,0:T(8,128)(2,1)S(1)} %get-tuple-element.179), channel_id=1, source_target_pairs={{0,6},{2,4},{4,2},{6,0},{1,7},{3,5},{5,3},{7,1},{8,14},{10,12},{12... | collective-permute-start | bytes 393224 | tf_op jit(solution)/shard_map/ppermute | solution.py:30
  118.8 14.0 %collective-permute-start.32 = (bf16[64,2048]{1,0:T(8,128)(2,1)S(1)}, bf16[64,2048]{1,0:T(8,128)(2,1)S(1)}, u32[]{:S(2)}, u32[]{:S(2)}) collective-permute-start(bf16[64,2048]{1,0:T(8,128)(2,1)S(1)} %combine.4), channel_id=1, source_target_pairs={{0,16},{8,24},{16,0},{24,8},{1,17},{9,25},{17,1},{25,9},{2,18},{10... | collective-permute-start | bytes 786440 | tf_op jit(solution)/shard_map/ppermute | solution.py:30
  124.0 8.8 %collective-permute-start.36 = (bf16[64,2048]{1,0:T(8,128)(2,1)S(1)}, bf16[64,2048]{1,0:T(8,128)(2,1)S(1)}, u32[]{:S(2)}, u32[]{:S(2)}) collective-permute-start(bf16[64,2048]{1,0:T(8,128)(2,1)S(1)} %combine.7), channel_id=1, source_target_pairs={{0,8},{8,0},{16,24},{24,16},{1,9},{9,1},{17,25},{25,17},{2,10},{10... | collective-permute-start | bytes 786440 | tf_op jit(solution)/shard_map/ppermute | solution.py:30
  124.8 5.7 %collective-permute-start.29 = (bf16[32,2048]{1,0:T(8,128)(2,1)S(1)}, bf16[32,2048]{1,0:T(8,128)(2,1)S(1)}, u32[]{:S(2)}, u32[]{:S(2)}) collective-permute-start(bf16[32,2048]{1,0:T(8,128)(2,1)S(1)} %copy-done.16), channel_id=1, source_target_pairs={{0,2},{2,0},{4,6},{6,4},{1,3},{3,1},{5,7},{7,5},{8,10},{10,8},{12,... | collective-permute-start | bytes 393224 | tf_op jit(solution)/shard_map/ppermute | solution.py:30
  125.6 5.0 %collective-permute-start.30 = (bf16[32,2048]{1,0:T(8,128)(2,1)S(1)}, bf16[32,2048]{1,0:T(8,128)(2,1)S(1)}, u32[]{:S(2)}, u32[]{:S(2)}) collective-permute-start(bf16[32,2048]{1,0:T(8,128)(2,1)S(1)} %copy-done.14), channel_id=1, source_target_pairs={{0,4},{2,6},{4,0},{6,2},{1,5},{3,7},{5,1},{7,3},{8,12},{10,14},{12... | collective-permute-start | bytes 393224 | tf_op jit(solution)/shard_map/ppermute | solution.py:30
  126.7 5.9 %collective-permute-start.31 = (bf16[32,2048]{1,0:T(8,128)(2,1)S(1)}, bf16[32,2048]{1,0:T(8,128)(2,1)S(1)}, u32[]{:S(2)}, u32[]{:S(2)}) collective-permute-start(bf16[32,2048]{1,0:T(8,128)(2,1)S(1)} %get-tuple-element.168), channel_id=1, source_target_pairs={{0,6},{2,4},{4,2},{6,0},{1,7},{3,5},{5,3},{7,1},{8,14},{10,12},{12... | collective-permute-start | bytes 393224 | tf_op jit(solution)/shard_map/ppermute | solution.py:30
  (34 other events, 434.2 us)
